TPU v7x, 32 devices: a whole 2x2x4 slice. The times are simulated.
32 devices in a mesh: blk: 8 (over y, x, core), tp: 4 (over z).
Axes of the slice: x: 2, y: 2, z: 4, core: 2. Of those that a mesh axis runs over, the one named last changes fastest.
Arguments:
- text_emb: bfloat16 [12288, 1024], P('blk', 'tp'), may hold values from -4 to 4
- image_emb: bfloat16 [12288, 1024], P(('blk', 'tp')), may hold values from -4 to 4
- logit_scale: float32 [1], replicated, may hold values from 4 to 12
- logit_bias: float32 [1], replicated, may hold values from -3 to -1
- bucket: int32 [12288], replicated, may hold values from 0 to 3
- positive: int32 [12288], replicated, may hold values from 0 to 12287, as said below
- blocks: int32 [96, 8, 3], replicated, may hold values from -1 to 2, as said below
Outputs:
- text_grad: bfloat16 [12288, 1024], P('blk', 'tp')
- image_grad: bfloat16 [12288, 1024], P(('blk', 'tp'))
Inputs may be any that keep to these rules, and one draw needn't show every extreme that they name: positive[i] lies in the same 128-row tile as i, and within each tile the entries are a permutation of that tile's rows. `blocks`: each entry is a tile of the named shard or -1 for an unused slot; slot 0 is never -1; the used slots of one text tile and shard name different tiles; for the text tile's own blk index, slot 0 names the text tile's own tile.
All inputs are finite; a program needn't handle non-finite values.
Results may differ from a plain program's by a relative error of at most 0.015.
Values may be sent and summed in bfloat16 or wider, within the bound.
No kernel may reach another device: no remote copies, remote signals or barrier semaphores. Data moves between devices by JAX's collectives and lax.ppermute only.
A program may use at most 128 MiB of HBM per device.

v0:
```python
import functools
import math

import jax
import jax.numpy as jnp
from jax import lax
from jax.experimental import pallas as pl
from jax.experimental.pallas import tpu as pltpu
from jax.sharding import PartitionSpec as P

TILE = 128
SLOTS = 3
WAIT_FLOPS = 20_000_000_000
TEXT_PIECES = 2
ACC_PIECES = 3
CORES = 2
EPS = 1e-06
LOG2E = math.log2(math.e)
MIB = 1024 * 1024

VMEM_SPEC = pl.BlockSpec(memory_space=pltpu.VMEM)
ANY_SPEC = pl.BlockSpec(memory_space=pl.ANY)
SMEM_SPEC = pl.BlockSpec(memory_space=pltpu.SMEM)


def call_kernel(
    body,
    outs,
    operands,
    scalars=0,
    anywhere=(),
    outs_anywhere=False,
    scratch=(),
    flops=0,
    limit=24,
):
    moved = sum(x.size * x.dtype.itemsize for x in operands)
    moved += sum(math.prod(o.shape) * o.dtype.itemsize for o in outs)
    specs = [SMEM_SPEC] * scalars + [VMEM_SPEC] * (len(operands) - scalars)
    for at in anywhere:
        specs[at] = ANY_SPEC
    return list(
        pl.pallas_call(
            body,
            out_shape=outs,
            in_specs=specs,
            out_specs=[ANY_SPEC if outs_anywhere else VMEM_SPEC] * len(outs),
            scratch_shapes=list(scratch),
            compiler_params=pltpu.CompilerParams(vmem_limit_bytes=limit * MIB),
            cost_estimate=pl.CostEstimate(flops=flops, bytes_accessed=moved, transcendentals=0),
        )(*operands)
    )


def struct(shape, dtype):
    return jax.ShapeDtypeStruct(shape, dtype)


def row_scales(square_sum):
    return lax.rsqrt(square_sum + EPS)


def column_of(row):
    return jnp.broadcast_to(row, (TILE, TILE)).T


def dot_nt(left, right):
    return lax.dot_general(
        left, right, (((1,), (1,)), ((), ())), preferred_element_type=jnp.float32
    )


def dot_tn(left, right):
    return lax.dot_general(
        left, right, (((0,), (0,)), ((), ())), preferred_element_type=jnp.float32
    )


def feature_slice(place, k, width):
    return pl.ds(pl.multiple_of((place ^ k) * width, width), width)


def pick_body(text_ref, *out_refs):
    place = lax.axis_index("tp")
    rows = out_refs[0].shape[0]
    for k, out_ref in enumerate(out_refs):
        out_ref[...] = text_ref[pl.ds(pl.multiple_of((place ^ k) * rows, rows), rows), :]


def unit_text_body(chunks, *refs):
    chunk_refs, unit_ref, piece_refs = refs[:chunks], refs[chunks], refs[chunks + 1 :]
    place = lax.axis_index("tp")
    rows, width = chunk_refs[0].shape
    for first in range(0, rows, TILE):
        part = pl.ds(first, TILE)
        parts = [ref[part, :].astype(jnp.float32) for ref in chunk_refs]
        scales = row_scales(sum(jnp.sum(x * x, axis=-1, keepdims=True) for x in parts))
        for k, x in enumerate(parts):
            unit_ref[part, feature_slice(place, k, width)] = (x * scales).astype(jnp.bfloat16)
    split_rows(unit_ref, piece_refs)


def split_rows(whole_ref, piece_refs):
    for at, ref in enumerate(piece_refs):
        ref[...] = whole_ref[pl.ds(at * ref.shape[0], ref.shape[0]), :]


def join_rows(piece_refs, whole_ref):
    for at, ref in enumerate(piece_refs):
        whole_ref[pl.ds(at * ref.shape[0], ref.shape[0]), :] = ref[...]


def unit_images(piece_refs, image_ref):
    start = 0
    step = 64
    for ref in piece_refs:
        for first in range(0, ref.shape[0], step):
            values = ref[pl.ds(first, step), :].astype(jnp.float32)
            scales = row_scales(jnp.sum(values * values, axis=-1, keepdims=True))
            image_ref[pl.ds(start + first, step), :] = (values * scales).astype(jnp.bfloat16)
        start += ref.shape[0]


def unit_images_body(own_ref, first_ref, second_ref, own_out_ref, near_out_ref):
    unit_images([own_ref], own_out_ref)
    unit_images([first_ref, second_ref], near_out_ref)


def neighbour_bits(shard):
    core = shard % CORES
    return 2 << core, 4 >> core


def list_body(groups, tiles, chips, *refs):
    scale_ref, bias_ref, blocks_ref, bucket_ref, positive_ref = refs[:5]
    line_ref, amount_ref, column_ref, row_ref, match_ref, own_ref = refs[5:]
    here, place = lax.axis_index("blk"), lax.axis_index("tp")
    scale = scale_ref[0]
    line_ref[pl.ds(0, 1), :] = jnp.full((1, TILE), -scale * LOG2E, jnp.float32)
    line_ref[pl.ds(1, 1), :] = jnp.full((1, TILE), -bias_ref[0] * LOG2E, jnp.float32)
    if chips == 4:
        first, second = neighbour_bits(here)
        shards = [here, here ^ first, here ^ second, here ^ 6]
    else:
        shards = [chip * CORES + here % CORES for chip in range(chips)]
    count = len(shards) * tiles

    def first_tile(shard):
        return (shard * groups + place) * tiles

    for n, shard in enumerate(shards):
        own_ref[pl.ds(n, 1), :] = jnp.full((1, TILE), jnp.where(shard == here, 1.0, 0.0))
        for j in range(tiles):
            column_ref[pl.ds(n * tiles + j, 1), :] = bucket_ref[pl.ds(first_tile(shard) + j, 1), :]
    for at in range(CORES * tiles):
        tile = first_tile(here ^ (at // tiles)) + at % tiles
        row_ref[pl.ds(at * TILE, TILE), :] = column_of(bucket_ref[pl.ds(tile, 1), :])
        if at < tiles:
            ids = lax.broadcasted_iota(jnp.int32, (1, TILE), 1) + tile * TILE
            matched = column_of(positive_ref[pl.ds(tile, 1), :]) == ids
            match_ref[pl.ds(at * TILE, TILE), :] = jnp.where(matched, 1.0, 0.0)
        for n, shard in enumerate(shards):
            entries = [blocks_ref[slot, shard, tile] for slot in range(SLOTS)]
            for j in range(tiles):
                listed = sum(jnp.where(entry == j, 1.0, 0.0) for entry in entries)
                amount_ref[pl.ds(at * count + n * tiles + j, 1), :] = jnp.full(
                    (1, TILE), scale * listed, jnp.float32
                )


class Pairs:
    count = 6

    def __init__(self, refs, tiles):
        self.line_ref, self.amount_ref, self.column_ref = refs[:3]
        self.row_ref, self.match_ref, self.own_ref = refs[3:6]
        self.tiles = tiles

    def weigh(self, products, half, group, weight_ref, top, left, own=None):
        tiles = self.tiles
        slope, offset = self.line_ref[pl.ds(0, 1), :], self.line_ref[pl.ds(1, 1), :]
        count = self.column_ref.shape[0]
        for a in range(tiles):
            at = half * tiles + a
            row_bucket = self.row_ref[pl.ds(at * TILE, TILE), :]
            for j in range(tiles):
                n = group * tiles + j
                amount = self.amount_ref[pl.ds(at * count + n, 1), :]
                power = (
                    products[a * TILE : (a + 1) * TILE, j * TILE : (j + 1) * TILE] * slope + offset
                )
                factor = jnp.where(row_bucket == self.column_ref[pl.ds(n, 1), :], amount, 0.0)
                if own and a == j:
                    match = self.match_ref[pl.ds(a * TILE, TILE), :]
                    if own == "search":
                        match = match * self.own_ref[pl.ds(group, 1), :]
                    power = jnp.where(match > 0.0, -power, power)
                    factor = jnp.where(match > 0.0, -amount, factor)
                below = 1.0 + jnp.exp2(power)
                inverse = pl.reciprocal(below, approx=True)
                inverse = inverse * (2.0 - below * inverse)
                weight_ref[pl.ds(top + a * TILE, TILE), pl.ds(left + j * TILE, TILE)] = (
                    factor * inverse
                ).astype(jnp.bfloat16)


def near_own_body(tiles, *refs):
    pairs = Pairs(refs, tiles)
    unit_ref, own_image_ref, near_image_ref, own_weight_ref, weight_ref = refs[Pairs.count :]
    rows = unit_ref.shape[0]
    first = dot_nt(unit_ref[...], near_image_ref[pl.ds(0, rows), :])
    second = dot_nt(unit_ref[...], near_image_ref[pl.ds(rows, rows), :])
    pairs.weigh(first, 0, 1, weight_ref, 0, 0)
    own = dot_nt(unit_ref[...], own_image_ref[...])
    pairs.weigh(second, 0, 2, weight_ref, 0, rows)
    pairs.weigh(own, 0, 0, own_weight_ref, 0, 0, "diagonal")


def first_sum_body(tiles, *refs):
    pairs = Pairs(refs, tiles)
    own_unit_ref, near_image_ref, weight_in_ref = refs[Pairs.count : Pairs.count + 3]
    piece_refs = refs[Pairs.count + 3 : Pairs.count + 3 + TEXT_PIECES]
    unit_ref, weight_ref, sum_ref = refs[Pairs.count + 3 + TEXT_PIECES :]
    rows = own_unit_ref.shape[0]
    for at, ref in enumerate(piece_refs):
        unit_ref[pl.ds(rows + at * ref.shape[0], ref.shape[0]), :] = ref[...]
    unit_ref[:rows, :] = own_unit_ref[...]
    weight_ref[:rows, :] = weight_in_ref[:, :rows]
    products = dot_nt(unit_ref[rows:, :], near_image_ref[pl.ds(0, rows), :])
    pairs.weigh(products, 1, 1, weight_ref, rows, 0)
    sum_ref[...] = dot_tn(weight_ref[...], unit_ref[...]).astype(jnp.bfloat16)


def second_sum_body(tiles, *refs):
    pairs = Pairs(refs, tiles)
    unit_ref, own_image_ref, near_image_ref, own_weight_in_ref, weight_in_ref, first_ref = refs[
        Pairs.count : Pairs.count + 6
    ]
    own_weight_ref, weight_ref, sum_ref = refs[Pairs.count + 6 :]
    rows = own_image_ref.shape[0]
    second = dot_nt(unit_ref[rows:, :], near_image_ref[pl.ds(rows, rows), :])
    own = dot_nt(unit_ref[rows:, :], own_image_ref[...])
    own_weight_ref[:rows, :] = own_weight_in_ref[...]
    weight_ref[:, :rows] = first_ref[...]
    weight_ref[:rows, rows:] = weight_in_ref[:, rows:]
    pairs.weigh(second, 1, 2, weight_ref, rows, rows)
    sum_ref[...] = dot_tn(weight_ref[:, rows:], unit_ref[...])
    pairs.weigh(own, 1, 0, own_weight_ref, rows, 0)


def far_sum_body(tiles, *refs):
    pairs = Pairs(refs, tiles)
    unit_ref, own_image_ref, own_weight_ref, raw_ref = refs[Pairs.count : Pairs.count + 4]
    sum_ref, weight_ref, image_ref = refs[Pairs.count + 4 :]
    rows = raw_ref.shape[0]
    unit_images([raw_ref], image_ref.at[pl.ds(rows, rows), :])
    products = dot_nt(unit_ref[...], image_ref[rows:, :])
    for half in range(CORES):
        part = products[half * rows : (half + 1) * rows, :]
        pairs.weigh(part, half, 3, weight_ref, half * rows, rows)
    sum_ref[...] = dot_tn(weight_ref[:, rows:], unit_ref[...]).astype(jnp.bfloat16)
    image_ref[:rows, :] = own_image_ref[...]
    weight_ref[:, :rows] = own_weight_ref[...]


def text_sum_body(near_weight_ref, near_image_ref, weight_ref, image_ref, acc_ref, *piece_refs):
    rows = acc_ref.shape[0]
    size = rows // ACC_PIECES
    for part in (slice(rows, 2 * rows), slice(0, rows)):
        acc = jnp.dot(
            near_weight_ref[part, :], near_image_ref[...], preferred_element_type=jnp.float32
        ) + jnp.dot(weight_ref[part, :], image_ref[...], preferred_element_type=jnp.float32)
        if part.start == 0:
            acc_ref[...] = acc
            continue
        for at, ref in enumerate(piece_refs):
            ref[...] = acc[at * size : (at + 1) * size, :].astype(jnp.bfloat16)


def own_sum_body(weight_ref, unit_ref, add_ref, out_ref):
    rows = out_ref.shape[0]
    out_ref[...] = dot_tn(weight_ref[:, :rows], unit_ref[...]) + add_ref[...].astype(jnp.float32)


def all_body(tiles, chips, *refs):
    pairs = Pairs(refs, tiles)
    own_ref, other_ref, piece_ref = refs[Pairs.count : Pairs.count + 3]
    outs = refs[Pairs.count + 3 :]
    spread_ref, acc_ref, acc_piece_refs = outs[0], outs[1], outs[2 : 2 + ACC_PIECES]
    image_ref, weight_ref = outs[2 + ACC_PIECES :]
    rows = own_ref.shape[0]
    unit_images([piece_ref], image_ref)
    for half, text_ref in enumerate((own_ref, other_ref)):
        for chip in range(chips):
            products = dot_nt(text_ref[...], image_ref[pl.ds(chip * rows, rows), :])
            pairs.weigh(
                products, half, chip, weight_ref, half * rows, chip * rows, None if half else "search"
            )
        acc = jnp.dot(
            weight_ref[pl.ds(half * rows, rows), :],
            image_ref[...],
            preferred_element_type=jnp.float32,
        )
        if half == 0:
            acc_ref[...] = acc
            continue
        size = rows // ACC_PIECES
        for at, ref in enumerate(acc_piece_refs):
            ref[...] = acc[at * size : (at + 1) * size, :].astype(jnp.bfloat16)
    for chip in range(chips):
        columns = pl.ds(chip * rows, rows)
        total = dot_tn(weight_ref[pl.ds(0, rows), columns], own_ref[...])
        total += dot_tn(weight_ref[pl.ds(rows, rows), columns], other_ref[...])
        spread_ref[columns, :] = total.astype(jnp.bfloat16)


def relay_body(sum_ref, in_ref, out_ref):
    out_ref[...] = (sum_ref[...] + in_ref[...].astype(jnp.float32)).astype(jnp.bfloat16)


def text_grad_body(chunks, *refs):
    raw_refs, acc_ref, add_refs = refs[:chunks], refs[chunks], refs[chunks + 1 : -chunks]
    out_refs = refs[-chunks:]
    place = lax.axis_index("tp")
    rows, width = raw_refs[0].shape
    size = add_refs[0].shape[0]
    for first in range(0, rows, TILE):
        part = pl.ds(first, TILE)
        raws = [ref[part, :].astype(jnp.float32) for ref in raw_refs]
        scales = row_scales(sum(jnp.sum(x * x, axis=-1, keepdims=True) for x in raws))
        accs = []
        for k in range(chunks):
            features = feature_slice(place, k, width)
            added = add_refs[first // size][pl.ds(first % size, TILE), features]
            accs.append(acc_ref[part, features] + added.astype(jnp.float32))
        units = [x * scales for x in raws]
        inner = sum(jnp.sum(u * a, axis=-1, keepdims=True) for u, a in zip(units, accs))
        for k in range(chunks):
            out_refs[k][part, :] = (scales * (accs[k] - units[k] * inner)).astype(jnp.bfloat16)


def place_text_body(chunks, *refs):
    part_refs, out_ref, sems = refs[:chunks], refs[chunks], refs[chunks + 1]
    place = lax.axis_index("tp")
    rows = part_refs[0].shape[0]
    copies = []
    for k in range(chunks):
        block = pl.ds(pl.multiple_of((place ^ k) * rows, rows), rows)
        copies.append(pltpu.make_async_copy(part_refs[k], out_ref.at[block, :], sems.at[k]))
    for copy in copies:
        copy.start()
    for copy in copies:
        copy.wait()


def image_grad_body(sum_count, raw_ref, *refs):
    sum_refs, (out_ref, grad_ref, sems) = refs[:sum_count], refs[sum_count:]
    copies = []
    for block in range(raw_ref.shape[0] // TILE):
        for first in range(block * TILE, (block + 1) * TILE, TILE // 2):
            part = pl.ds(first, TILE // 2)
            raw = raw_ref[part, :].astype(jnp.float32)
            scales = row_scales(jnp.sum(raw * raw, axis=-1, keepdims=True))
            unit = raw * scales
            acc = sum(ref[part, :].astype(jnp.float32) for ref in sum_refs)
            inner = jnp.sum(unit * acc, axis=-1, keepdims=True)
            grad_ref[part, :] = (scales * (acc - unit * inner)).astype(jnp.bfloat16)
        part = pl.ds(block * TILE, TILE)
        copies.append(
            pltpu.make_async_copy(grad_ref.at[part, :], out_ref.at[part, :], sems.at[block])
        )
        copies[-1].start()
    for copy in copies:
        copy.wait()


def swap(value, axis, bits):
    count = lax.axis_size(axis)
    return lax.ppermute(value, axis, [(i, i ^ bits) for i in range(count)])


def swap_near(value, which):
    count = lax.axis_size("blk")
    return lax.ppermute(value, "blk", [(i, i ^ neighbour_bits(i)[which]) for i in range(count)])


def per_device(text_emb, image_emb, logit_scale, logit_bias, bucket, positive, blocks):
    groups = lax.axis_size("tp")
    shards = lax.axis_size("blk")
    chips = shards // CORES
    rows, embed = image_emb.shape
    tiles = rows // TILE
    width = text_emb.shape[1]
    square = chips == 4

    def bf16(count, columns=embed):
        return struct((count, columns), jnp.bfloat16)

    def f32(count, columns=embed):
        return struct((count, columns), jnp.float32)

    def i32(count, columns):
        return struct((count, columns), jnp.int32)

    picked = call_kernel(pick_body, [bf16(rows, width)] * groups, [text_emb], limit=8)
    picked[-1], image_sent = lax.optimization_barrier((picked[-1], image_emb))
    text_raw = [picked[0]] + [swap(picked[k], "tp", k) for k in range(1, groups)]
    if square:
        from_second = swap_near(image_sent, 1)
        from_first = swap_near(image_sent, 0)
        from_far = swap_near(from_second, 0)
        own_images, near_images = call_kernel(
            unit_images_body,
            [bf16(rows), bf16(2 * rows)],
            [image_emb, from_first, from_second],
            limit=8,
        )
    else:
        same_core = [[chip * CORES + core for chip in range(chips)] for core in range(CORES)]
        gathered = lax.all_gather(
            image_emb, "blk", axis=0, tiled=True, axis_index_groups=same_core
        )
    lists = call_kernel(
        functools.partial(list_body, groups, tiles, chips),
        [
            f32(2, TILE),
            f32(CORES * tiles * chips * tiles, TILE),
            i32(chips * tiles, TILE),
            i32(CORES * rows, TILE),
            f32(rows, TILE),
            f32(chips, TILE),
        ],
        [
            logit_scale,
            logit_bias,
            blocks.transpose(2, 1, 0),
            bucket.reshape(-1, TILE),
            positive.reshape(-1, TILE),
        ],
        scalars=3,
        flops=WAIT_FLOPS // 2,
        limit=8,
    )
    if square:
        text_raw[-1], own_images, *lists = lax.optimization_barrier(
            (text_raw[-1], own_images, *lists)
        )
    text_own, *pieces = call_kernel(
        functools.partial(unit_text_body, groups),
        [bf16(rows)] + [bf16(rows // TEXT_PIECES)] * TEXT_PIECES,
        text_raw,
        limit=8,
    )
    text_other = [swap(piece, "blk", 1) for piece in pieces]
    unit_flops = 2 * rows * rows * embed

    def finish_text(acc_own, acc_other):
        parts = call_kernel(
            functools.partial(text_grad_body, groups),
            [bf16(rows, width)] * groups,
            text_raw + [acc_own] + [swap(piece, "blk", 1) for piece in acc_other],
            limit=16,
        )
        return [parts[0]] + [swap(parts[k], "tp", k) for k in range(1, groups)]

    def place_text(text_parts):
        return call_kernel(
            functools.partial(place_text_body, groups),
            [bf16(groups * rows, width)],
            text_parts,
            outs_anywhere=True,
            scratch=[pltpu.SemaphoreType.DMA((groups,))],
            flops=WAIT_FLOPS,
            limit=8,
        )[0]

    def finish_image(sums):
        return call_kernel(
            functools.partial(image_grad_body, len(sums)),
            [bf16(rows)],
            [image_emb] + sums,
            outs_anywhere=True,
            scratch=[pltpu.VMEM((rows, embed), jnp.bfloat16), pltpu.SemaphoreType.DMA((tiles,))],
            limit=8,
        )[0]

    if not square:
        columns = gathered.shape[0]
        spread, acc_own, *acc_other = call_kernel(
            functools.partial(all_body, tiles, chips),
            [bf16(columns), f32(rows)] + [bf16(rows // ACC_PIECES)] * ACC_PIECES,
            lists + [text_own, jnp.concatenate(text_other), gathered],
            scratch=[
                pltpu.VMEM((columns, embed), jnp.bfloat16),
                pltpu.VMEM((2 * rows, columns), jnp.bfloat16),
            ],
            flops=6 * chips * unit_flops,
            limit=56,
        )
        text_parts = finish_text(acc_own, acc_other)
        parts = lax.all_to_all(
            spread, "blk", split_axis=0, concat_axis=0, tiled=True, axis_index_groups=same_core
        )
        total = jnp.sum(parts.reshape(-1, rows, embed).astype(jnp.float32), axis=0)
        return (place_text(text_parts), finish_image([total]))

    own_weights, near_weights = call_kernel(
        functools.partial(near_own_body, tiles),
        [bf16(rows, rows), bf16(rows, 2 * rows)],
        lists + [text_own, own_images, near_images],
        limit=16,
    )
    units, first_weights, first_sum = call_kernel(
        functools.partial(first_sum_body, tiles),
        [bf16(2 * rows), bf16(2 * rows, rows), bf16(rows)],
        lists + [text_own, near_images, near_weights] + text_other,
        limit=16,
    )
    image_add = swap_near(first_sum, 0)
    own_weights, near_weights, second_sum = call_kernel(
        functools.partial(second_sum_body, tiles),
        [bf16(2 * rows, rows), bf16(2 * rows, 2 * rows), f32(rows)],
        lists + [units, own_images, near_images, own_weights, near_weights, first_weights],
        limit=16,
    )
    own_weights, from_far = lax.optimization_barrier((own_weights, from_far))
    far_sum, far_weights, far_images = call_kernel(
        functools.partial(far_sum_body, tiles),
        [bf16(rows), bf16(2 * rows, 2 * rows), bf16(2 * rows)],
        lists + [units, own_images, own_weights, from_far],
        limit=16,
    )
    acc_own, *acc_other = call_kernel(
        text_sum_body,
        [f32(rows)] + [bf16(rows // ACC_PIECES)] * ACC_PIECES,
        [near_weights, near_images, far_weights, far_images],
        limit=24,
    )
    text_parts = finish_text(acc_own, acc_other)
    far_weights, text_parts[0] = lax.optimization_barrier((far_weights, text_parts[0]))
    base = call_kernel(
        own_sum_body, [f32(rows)], [far_weights, units, image_add], limit=16
    )[0]
    base, second_sum = lax.optimization_barrier((base, second_sum))
    relayed = call_kernel(
        relay_body, [bf16(rows)], [second_sum, swap_near(far_sum, 0)], limit=8
    )[0]
    image_last = swap_near(relayed, 1)
    text_grad = place_text(text_parts)
    base, _ = lax.optimization_barrier((base, text_grad))
    return (text_grad, finish_image([base, image_last]))


def solution(mesh):
    in_specs = (P("blk", "tp"), P(("blk", "tp"), None), P(), P(), P(), P(), P())
    out_specs = (P("blk", "tp"), P(("blk", "tp"), None))
    return jax.shard_map(
        per_device, mesh=mesh, in_specs=in_specs, out_specs=out_specs, check_vma=False
    )
```

profile of v0, /device:TPU:0, one launch (start us, length us, event | category | flops | bytes accessed | tf_op | source)
XLA Modules:
  0.0 66.9 jit_solution(490742893621790557)
XLA Ops:
  0.6 1.1 %copy-done.1 = bf16[1536,256]{1,0:T(8,128)(2,1)S(1)} copy-done((bf16[1536,256]{1,0:T(8,128)(2,1)S(1)}, bf16[1536,256]{1,0:T(8,128)(2,1)}, u32[]{:S(2)}) %copy-start.1) | copy-done | bytes 786456
  1.8 0.1 shard_map.86
  1.8 3.0 %collective-permute-start.2 = (bf16[384,1024]{1,0:T(8,128)(2,1)}, bf16[384,1024]{1,0:T(8,128)(2,1)S(1)}, u32[]{:S(2)}, u32[]{:S(2)}) collective-permute-start(bf16[384,1024]{1,0:T(8,128)(2,1)} %raw_ref.1), channel_id=1, source_target_pairs={{0,16},{4,12},{8,24},{12,4},{16,0},{20,28},{24,8},{28,20},{1,17},{... | collective-permute-start | bytes 2359304 | tf_op jit(solution)/shard_map/ppermute | solution.py:384
  4.9 1.5 %collective-permute-start.1 = (bf16[384,1024]{1,0:T(8,128)(2,1)}, bf16[384,1024]{1,0:T(8,128)(2,1)S(1)}, u32[]{:S(2)}, u32[]{:S(2)}) collective-permute-start(bf16[384,1024]{1,0:T(8,128)(2,1)} %raw_ref.1), channel_id=1, source_target_pairs={{0,8},{4,20},{8,0},{12,28},{16,24},{20,4},{24,16},{28,12},{1,9},{5... | collective-permute-start | bytes 2359304 | tf_op jit(solution)/shard_map/ppermute | solution.py:384
  6.3 3.6 %collective-permute-start = (bf16[384,256]{1,0:T(8,128)(2,1)S(1)}, bf16[384,256]{1,0:T(8,128)(2,1)S(1)}, u32[]{:S(2)}, u32[]{:S(2)}) collective-permute-start(bf16[384,256]{1,0:T(8,128)(2,1)S(1)} %get-tuple-element.54), channel_id=1, source_target_pairs={{0,3},{1,2},{2,1},{3,0},{4,7},{5,6},{6,5},{7,4},{8,11},{9,10},{10,... | collective-permute-start | bytes 589832 | tf_op jit(solution)/shard_map/ppermute | solution.py:379
  9.9 0.8 %collective-permute-start.4 = (bf16[384,256]{1,0:T(8,128)(2,1)S(1)}, bf16[384,256]{1,0:T(8,128)(2,1)S(1)}, u32[]{:S(2)}, u32[]{:S(2)}) collective-permute-start(bf16[384,256]{1,0:T(8,128)(2,1)S(1)} %get-tuple-element.71), channel_id=1, source_target_pairs={{0,2},{1,3},{2,0},{3,1},{4,6},{5,7},{6,4},{7,5},{8,10},{9,11},{10,... | collective-permute-start | bytes 589832 | tf_op jit(solution)/shard_map/ppermute | solution.py:379
  12.0 11.0 %collective-permute-done.2.second_ref = bf16[384,1024]{1,0:T(8,128)(2,1)S(1)} collective-permute-done((bf16[384,1024]{1,0:T(8,128)(2,1)}, bf16[384,1024]{1,0:T(8,128)(2,1)S(1)}, u32[]{:S(2)}, u32[]{:S(2)}) %collective-permute-start.2) | collective-permute-done | bytes 786464 | tf_op jit(solution)/shard_map/ppermute | solution.py:384
  23.0 1.4 %collective-permute-start.7 = (bf16[384,1024]{1,0:T(8,128)(2,1)S(1)}, bf16[384,1024]{1,0:T(8,128)(2,1)S(1)}, u32[]{:S(2)}, u32[]{:S(2)}) collective-permute-start(bf16[384,1024]{1,0:T(8,128)(2,1)S(1)} %collective-permute-done.2.second_ref), channel_id=1, source_target_pairs={{0,8},{4,20},{8,0},{12,28},{16,24},{20,4},{24,16},{28,12},{1,9},{5... | collective-permute-start | bytes 2359304 | tf_op jit(solution)/shard_map/ppermute | solution.py:384
  24.4 0.8 %copy-done.2 = s32[12288]{0:T(1024)S(1)} copy-done((s32[12288]{0:T(1024)S(1)}, s32[12288]{0:T(1024)}, u32[]{:S(2)}) %copy-start.2) | copy-done | bytes 49176
  25.2 0.8 %copy-done.3 = s32[12288]{0:T(1024)S(1)} copy-done((s32[12288]{0:T(1024)S(1)}, s32[12288]{0:T(1024)}, u32[]{:S(2)}) %copy-start.3) | copy-done | bytes 49176
  26.0 0.7 %copy-done.4 = s32[96,8,3]{0,1,2:T(8,128)S(1)} copy-done((s32[96,8,3]{0,1,2:T(8,128)S(1)}, s32[96,8,3]{0,1,2:T(8,128)}, u32[]{:S(2)}) %copy-start.4) | copy-done | bytes 9240
  26.7 1.1 %shard_map.88 = (f32[2,128]{1,0:T(2,128)S(1)}, f32[72,128]{1,0:T(8,128)S(1)}, s32[12,128]{1,0:T(8,128)S(1)}, s32[768,128]{1,0:T(8,128)S(1)}, f32[384,128]{1,0:T(8,128)S(1)}, /*index=5*/f32[4,128]{1,0:T(4,128)S(1)}) custom-call(f32[1]{0:T(128)S(6)} %copy.9.refs_0_, f32[1]{0:T(128)S(6)} %copy.10.refs_1_, s32[3,8,96]{2,1,0:T(8,128)S(1)} %bitcast.5, ...), custom_call_target="tpu_custom_call" | custom-call | flops 10000000000 | bytes 743432 | tf_op jit(solution)/shard_map/pallas_call | solution.py:43
  27.8 0.0 collective-permute-done.1.first_ref
  27.8 0.0 copy-done
  27.9 0.7 %shard_map.87 = (bf16[384,1024]{1,0:T(8,128)(2,1)S(1)}, bf16[768,1024]{1,0:T(8,128)(2,1)S(1)}) custom-call(bf16[384,1024]{1,0:T(8,128)(2,1)S(1)} %copy-done, bf16[384,1024]{1,0:T(8,128)(2,1)S(1)} %collective-permute-done.1.first_ref, bf16[384,1024]{1,0:T(8,128)(2,1)S(1)} %collective-permute-done.2.second_ref), custom_call_target="tpu_custom_call" | custom-call | bytes 4718592 | tf_op jit(solution)/shard_map/pallas_call | solution.py:43
  28.6 0.0 collective-permute-done.3.refs_1_
  28.6 0.0 collective-permute-done.4.refs_2_
  28.6 0.4 shard_map.89
  29.0 0.1 collective-permute-start.5
  29.1 0.5 collective-permute-start.6
  29.6 1.8 %shard_map.90 = (bf16[384,384]{1,0:T(8,128)(2,1)S(1)}, bf16[384,768]{1,0:T(8,128)(2,1)S(1)}) custom-call(f32[2,128]{1,0:T(2,128)S(1)} %get-tuple-element.63.refs_0_, f32[72,128]{1,0:T(8,128)S(1)} %get-tuple-element.64.refs_1_, s32[12,128]{1,0:T(8,128)S(1)} %get-tuple-element.65.refs_2_, s32[768,128]{1,0:T(8,128)S(1)} %get-tuple-element.66.refs_3_, ...), custom_call_target="tpu_custom_call" | custom-call | bytes 4666368 | tf_op jit(solution)/shard_map/pallas_call | solution.py:43
  31.4 0.0 collective-permute-done.5.refs_9_
  31.4 1.4 %shard_map.91 = (bf16[768,1024]{1,0:T(8,128)(2,1)S(1)}, bf16[768,384]{1,0:T(8,128)(2,1)S(1)}, bf16[384,1024]{1,0:T(8,128)(2,1)S(1)}) custom-call(f32[2,128]{1,0:T(2,128)S(1)} %get-tuple-element.63.refs_0_, f32[72,128]{1,0:T(8,128)S(1)} %get-tuple-element.64.refs_1_, s32[12,128]{1,0:T(8,128)S(1)} %get-tuple-element.65.refs_2_, ...), custom_call_target="tpu_custom_call" | custom-call | bytes 7320576 | tf_op jit(solution)/shard_map/pallas_call | solution.py:43
  32.8 0.7 %collective-permute-start.14 = (bf16[384,1024]{1,0:T(8,128)(2,1)S(1)}, bf16[384,1024]{1,0:T(8,128)(2,1)S(1)}, u32[]{:S(2)}, u32[]{:S(2)}) collective-permute-start(bf16[384,1024]{1,0:T(8,128)(2,1)S(1)} %get-tuple-element.98), channel_id=1, source_target_pairs={{0,8},{4,20},{8,0},{12,28},{16,24},{20,4},{24,16},{28,12},{1,9},{5... | collective-permute-start | bytes 2359304 | tf_op jit(solution)/shard_map/ppermute | solution.py:384
  33.5 1.9 %shard_map.92 = (bf16[768,384]{1,0:T(8,128)(2,1)S(1)}, bf16[768,768]{1,0:T(8,128)(2,1)S(1)}, f32[384,1024]{1,0:T(8,128)S(1)}) custom-call(f32[2,128]{1,0:T(2,128)S(1)} %get-tuple-element.63.refs_0_, f32[72,128]{1,0:T(8,128)S(1)} %get-tuple-element.64.refs_1_, s32[12,128]{1,0:T(8,128)S(1)} %get-tuple-element.65.refs_2_, ...), custom_call_target="tpu_custom_call" | custom-call | bytes 9384960 | tf_op jit(solution)/shard_map/pallas_call | solution.py:43
  35.4 0.0 collective-permute-done.7.refs_9_
  35.4 2.2 %shard_map.93 = (bf16[384,1024]{1,0:T(8,128)(2,1)S(1)}, bf16[768,768]{1,0:T(8,128)(2,1)S(1)}, bf16[768,1024]{1,0:T(8,128)(2,1)S(1)}) custom-call(f32[2,128]{1,0:T(2,128)S(1)} %get-tuple-element.63.refs_0_, f32[72,128]{1,0:T(8,128)S(1)} %get-tuple-element.64.refs_1_, s32[12,128]{1,0:T(8,128)S(1)} %get-tuple-element.65.refs_2_, ...), custom_call_target="tpu_custom_call" | custom-call | bytes 7910400 | tf_op jit(solution)/shard_map/pallas_call | solution.py:43
  37.6 1.5 %collective-permute-start.15 = (bf16[384,1024]{1,0:T(8,128)(2,1)S(1)}, bf16[384,1024]{1,0:T(8,128)(2,1)S(1)}, u32[]{:S(2)}, u32[]{:S(2)}) collective-permute-start(bf16[384,1024]{1,0:T(8,128)(2,1)S(1)} %get-tuple-element.103), channel_id=1, source_target_pairs={{0,8},{4,20},{8,0},{12,28},{16,24},{20,4},{24,16},{28,12},{1,9},{5... | collective-permute-start | bytes 2359304 | tf_op jit(solution)/shard_map/ppermute | solution.py:384
  39.0 2.6 %shard_map.94 = (f32[384,1024]{1,0:T(8,128)S(1)}, bf16[128,1024]{1,0:T(8,128)(2,1)S(1)}, bf16[128,1024]{1,0:T(8,128)(2,1)S(1)}, bf16[128,1024]{1,0:T(8,128)(2,1)S(1)}) custom-call(bf16[768,768]{1,0:T(8,128)(2,1)S(1)} %get-tuple-element.86.near_weight_ref, bf16[768,1024]{1,0:T(8,128)(2,1)S(1)} %get-tuple-element.74.refs_8_.refs_7_.near_image_ref, ...), custom_call_target="tpu_custom_call" | custom-call | bytes 7864320 | tf_op jit(solution)/shard_map/pallas_call | solution.py:43
  41.6 0.1 collective-permute-start.8
  41.7 0.5 collective-permute-start.9
  42.2 0.1 collective-permute-start.10
  42.3 0.9 %collective-permute-done.8.refs_5_ = bf16[128,1024]{1,0:T(8,128)(2,1)S(1)} collective-permute-done((bf16[128,1024]{1,0:T(8,128)(2,1)S(1)}, bf16[128,1024]{1,0:T(8,128)(2,1)S(1)}, u32[]{:S(2)}, u32[]{:S(2)}) %collective-permute-start.8) | collective-permute-done | bytes 262176 | tf_op jit(solution)/shard_map/ppermute | solution.py:379
  43.2 0.4 collective-permute-done.9.refs_6_
  43.6 0.4 collective-permute-done.10.refs_7_
  44.0 0.8 %shard_map.95 = (bf16[384,256]{1,0:T(8,128)(2,1)S(1)}, bf16[384,256]{1,0:T(8,128)(2,1)S(1)}, bf16[384,256]{1,0:T(8,128)(2,1)S(1)}, bf16[384,256]{1,0:T(8,128)(2,1)S(1)}) custom-call(bf16[384,256]{1,0:T(8,128)(2,1)S(1)} %get-tuple-element.69.refs_0_, bf16[384,256]{1,0:T(8,128)(2,1)S(1)} %collective-permute-done.3.refs_1_, ...), custom_call_target="tpu_custom_call" | custom-call | bytes 3932160 | tf_op jit(solution)/shard_map/pallas_call | solution.py:43
  44.8 1.8 %collective-permute-start.11 = (bf16[384,256]{1,0:T(8,128)(2,1)S(1)}, bf16[384,256]{1,0:T(8,128)(2,1)S(1)}, u32[]{:S(2)}, u32[]{:S(2)}) collective-permute-start(bf16[384,256]{1,0:T(8,128)(2,1)S(1)} %get-tuple-element.94), channel_id=1, source_target_pairs={{0,1},{1,0},{2,3},{3,2},{4,5},{5,4},{6,7},{7,6},{8,9},{9,8},{10,11... | collective-permute-start | bytes 589832 | tf_op jit(solution)/shard_map/ppermute | solution.py:379
  46.6 2.6 %collective-permute-start.12 = (bf16[384,256]{1,0:T(8,128)(2,1)S(1)}, bf16[384,256]{1,0:T(8,128)(2,1)S(1)}, u32[]{:S(2)}, u32[]{:S(2)}) collective-permute-start(bf16[384,256]{1,0:T(8,128)(2,1)S(1)} %get-tuple-element.95), channel_id=1, source_target_pairs={{0,2},{1,3},{2,0},{3,1},{4,6},{5,7},{6,4},{7,5},{8,10},{9,11},{10,... | collective-permute-start | bytes 589832 | tf_op jit(solution)/shard_map/ppermute | solution.py:379
  49.2 0.1 collective-permute-start.13
  49.3 0.8 %shard_map.97.refs_0_ = f32[384,1024]{1,0:T(8,128)S(1)} custom-call(bf16[768,768]{1,0:T(8,128)(2,1)S(1)} %get-tuple-element.97.weight_ref, bf16[768,1024]{1,0:T(8,128)(2,1)S(1)} %get-tuple-element.79.refs_6_.unit_ref, bf16[384,1024]{1,0:T(8,128)(2,1)S(1)} %collective-permute-done.14.add_ref), custom_call_target="tpu_custom_call" | custom-call | bytes 5111808 | tf_op jit(solution)/shard_map/pallas_call | solution.py:43
  50.1 3.2 %collective-permute-done.15.in_ref = bf16[384,1024]{1,0:T(8,128)(2,1)S(1)} collective-permute-done((bf16[384,1024]{1,0:T(8,128)(2,1)S(1)}, bf16[384,1024]{1,0:T(8,128)(2,1)S(1)}, u32[]{:S(2)}, u32[]{:S(2)}) %collective-permute-start.15) | collective-permute-done | bytes 786464 | tf_op jit(solution)/shard_map/ppermute | solution.py:384
  53.3 0.1 shard_map.98
  53.4 1.7 %collective-permute-start.16 = (bf16[384,1024]{1,0:T(8,128)(2,1)S(1)}, bf16[384,1024]{1,0:T(8,128)(2,1)S(1)}, u32[]{:S(2)}, u32[]{:S(2)}) collective-permute-start(bf16[384,1024]{1,0:T(8,128)(2,1)S(1)} %shard_map.98), channel_id=1, source_target_pairs={{0,16},{4,12},{8,24},{12,4},{16,0},{20,28},{24,8},{28,20},{1,17},{... | collective-permute-start | bytes 2359304 | tf_op jit(solution)/shard_map/ppermute | solution.py:384
  55.2 0.3 collective-permute-done.11.refs_1_
  55.4 8.3 %collective-permute-done.12.refs_2_ = bf16[384,256]{1,0:T(8,128)(2,1)S(1)} collective-permute-done((bf16[384,256]{1,0:T(8,128)(2,1)S(1)}, bf16[384,256]{1,0:T(8,128)(2,1)S(1)}, u32[]{:S(2)}, u32[]{:S(2)}) %collective-permute-start.12) | collective-permute-done | bytes 196640 | tf_op jit(solution)/shard_map/ppermute | solution.py:379
  63.7 0.9 %shard_map.96 = bf16[1536,256]{1,0:T(8,128)(2,1)} custom-call(bf16[384,256]{1,0:T(8,128)(2,1)S(1)} %get-tuple-element.93.refs_0_, bf16[384,256]{1,0:T(8,128)(2,1)S(1)} %collective-permute-done.11.refs_1_, bf16[384,256]{1,0:T(8,128)(2,1)S(1)} %collective-permute-done.12.refs_2_, bf16[384,256]{1,0:T(8,128)(2,1)S(1)} %collective-permute-done.13.refs_3_), custom_call_target="tpu_custom_call" | custom-call | flops 20000000000 | bytes 1572864 | tf_op jit(solution)/shard_map/pallas_call | solution.py:43
  64.6 0.9 %collective-permute-done.16.refs_1_ = bf16[384,1024]{1,0:T(8,128)(2,1)S(1)} collective-permute-done((bf16[384,1024]{1,0:T(8,128)(2,1)S(1)}, bf16[384,1024]{1,0:T(8,128)(2,1)S(1)}, u32[]{:S(2)}, u32[]{:S(2)}) %collective-permute-start.16) | collective-permute-done | bytes 786464 | tf_op jit(solution)/shard_map/ppermute | solution.py:384
  65.5 1.4 %shard_map.99 = bf16[384,1024]{1,0:T(8,128)(2,1)} custom-call(bf16[384,1024]{1,0:T(8,128)(2,1)S(1)} %copy-done, f32[384,1024]{1,0:T(8,128)S(1)} %shard_map.97.refs_0_, bf16[384,1024]{1,0:T(8,128)(2,1)S(1)} %collective-permute-done.16.refs_1_), custom_call_target="tpu_custom_call" | custom-call | bytes 3932160 | tf_op jit(solution)/shard_map/pallas_call | solution.py:43
  (10 shorter events, 0.0 us)
Async XLA Ops:
  0.6 1.1 %copy-start.1 = (bf16[1536,256]{1,0:T(8,128)(2,1)S(1)}, bf16[1536,256]{1,0:T(8,128)(2,1)}, u32[]{:S(2)}) copy-start(bf16[1536,256]{1,0:T(8,128)(2,1)} %text_ref.1) | copy-start | bytes 2359300
  1.8 21.2 %collective-permute-start.2 = (bf16[384,1024]{1,0:T(8,128)(2,1)}, bf16[384,1024]{1,0:T(8,128)(2,1)S(1)}, u32[]{:S(2)}, u32[]{:S(2)}) collective-permute-start(bf16[384,1024]{1,0:T(8,128)(2,1)} %raw_ref.1), channel_id=1, source_target_pairs={{0,16},{4,12},{8,24},{12,4},{16,0},{20,28},{24,8},{28,20},{1,17},{... | collective-permute-start | bytes 2359304 | tf_op jit(solution)/shard_map/ppermute | solution.py:384
  4.9 23.0 %collective-permute-start.1 = (bf16[384,1024]{1,0:T(8,128)(2,1)}, bf16[384,1024]{1,0:T(8,128)(2,1)S(1)}, u32[]{:S(2)}, u32[]{:S(2)}) collective-permute-start(bf16[384,1024]{1,0:T(8,128)(2,1)} %raw_ref.1), channel_id=1, source_target_pairs={{0,8},{4,20},{8,0},{12,28},{16,24},{20,4},{24,16},{28,12},{1,9},{5... | collective-permute-start | bytes 2359304 | tf_op jit(solution)/shard_map/ppermute | solution.py:384
  6.3 22.2 %collective-permute-start = (bf16[384,256]{1,0:T(8,128)(2,1)S(1)}, bf16[384,256]{1,0:T(8,128)(2,1)S(1)}, u32[]{:S(2)}, u32[]{:S(2)}) collective-permute-start(bf16[384,256]{1,0:T(8,128)(2,1)S(1)} %get-tuple-element.54), channel_id=1, source_target_pairs={{0,3},{1,2},{2,1},{3,0},{4,7},{5,6},{6,5},{7,4},{8,11},{9,10},{10,... | collective-permute-start | bytes 589832 | tf_op jit(solution)/shard_map/ppermute | solution.py:379
  9.9 18.7 %collective-permute-start.3 = (bf16[384,256]{1,0:T(8,128)(2,1)S(1)}, bf16[384,256]{1,0:T(8,128)(2,1)S(1)}, u32[]{:S(2)}, u32[]{:S(2)}) collective-permute-start(bf16[384,256]{1,0:T(8,128)(2,1)S(1)} %get-tuple-element.70), channel_id=1, source_target_pairs={{0,1},{1,0},{2,3},{3,2},{4,5},{5,4},{6,7},{7,6},{8,9},{9,8},{10,11... | collective-permute-start | bytes 589832 | tf_op jit(solution)/shard_map/ppermute | solution.py:379
  9.9 18.7 %collective-permute-start.4 = (bf16[384,256]{1,0:T(8,128)(2,1)S(1)}, bf16[384,256]{1,0:T(8,128)(2,1)S(1)}, u32[]{:S(2)}, u32[]{:S(2)}) collective-permute-start(bf16[384,256]{1,0:T(8,128)(2,1)S(1)} %get-tuple-element.71), channel_id=1, source_target_pairs={{0,2},{1,3},{2,0},{3,1},{4,6},{5,7},{6,4},{7,5},{8,10},{9,11},{10,... | collective-permute-start | bytes 589832 | tf_op jit(solution)/shard_map/ppermute | solution.py:379
  23.0 12.3 %collective-permute-start.7 = (bf16[384,1024]{1,0:T(8,128)(2,1)S(1)}, bf16[384,1024]{1,0:T(8,128)(2,1)S(1)}, u32[]{:S(2)}, u32[]{:S(2)}) collective-permute-start(bf16[384,1024]{1,0:T(8,128)(2,1)S(1)} %collective-permute-done.2.second_ref), channel_id=1, source_target_pairs={{0,8},{4,20},{8,0},{12,28},{16,24},{20,4},{24,16},{28,12},{1,9},{5... | collective-permute-start | bytes 2359304 | tf_op jit(solution)/shard_map/ppermute | solution.py:384
  24.4 0.8 %copy-start.2 = (s32[12288]{0:T(1024)S(1)}, s32[12288]{0:T(1024)}, u32[]{:S(2)}) copy-start(s32[12288]{0:T(1024)} %param.11) | copy-start | bytes 147460
  25.2 0.8 %copy-start.3 = (s32[12288]{0:T(1024)S(1)}, s32[12288]{0:T(1024)}, u32[]{:S(2)}) copy-start(s32[12288]{0:T(1024)} %param.12) | copy-start | bytes 147460
  26.0 0.7 %copy-start.4 = (s32[96,8,3]{0,1,2:T(8,128)S(1)}, s32[96,8,3]{0,1,2:T(8,128)}, u32[]{:S(2)}) copy-start(s32[96,8,3]{0,1,2:T(8,128)} %param.13) | copy-start | bytes 27652
  26.7 1.1 %copy-start = (bf16[384,1024]{1,0:T(8,128)(2,1)S(1)}, bf16[384,1024]{1,0:T(8,128)(2,1)}, u32[]{:S(2)}) copy-start(bf16[384,1024]{1,0:T(8,128)(2,1)} %raw_ref.1) | copy-start | bytes 2359300
  29.0 2.4 %collective-permute-start.5 = (bf16[192,1024]{1,0:T(8,128)(2,1)S(1)}, bf16[192,1024]{1,0:T(8,128)(2,1)S(1)}, u32[]{:S(2)}, u32[]{:S(2)}) collective-permute-start(bf16[192,1024]{1,0:T(8,128)(2,1)S(1)} %get-tuple-element.77), channel_id=1, source_target_pairs={{0,4},{4,0},{8,12},{12,8},{16,20},{20,16},{24,28},{28,24},{1,5},{5... | collective-permute-start | bytes 1179656 | tf_op jit(solution)/shard_map/ppermute | solution.py:379
  29.1 2.3 %collective-permute-start.6 = (bf16[192,1024]{1,0:T(8,128)(2,1)S(1)}, bf16[192,1024]{1,0:T(8,128)(2,1)S(1)}, u32[]{:S(2)}, u32[]{:S(2)}) collective-permute-start(bf16[192,1024]{1,0:T(8,128)(2,1)S(1)} %get-tuple-element.78), channel_id=1, source_target_pairs={{0,4},{4,0},{8,12},{12,8},{16,20},{20,16},{24,28},{28,24},{1,5},{5... | collective-permute-start | bytes 1179656 | tf_op jit(solution)/shard_map/ppermute | solution.py:379
  32.8 16.4 %collective-permute-start.14 = (bf16[384,1024]{1,0:T(8,128)(2,1)S(1)}, bf16[384,1024]{1,0:T(8,128)(2,1)S(1)}, u32[]{:S(2)}, u32[]{:S(2)}) collective-permute-start(bf16[384,1024]{1,0:T(8,128)(2,1)S(1)} %get-tuple-element.98), channel_id=1, source_target_pairs={{0,8},{4,20},{8,0},{12,28},{16,24},{20,4},{24,16},{28,12},{1,9},{5... | collective-permute-start | bytes 2359304 | tf_op jit(solution)/shard_map/ppermute | solution.py:384
  37.6 15.7 %collective-permute-start.15 = (bf16[384,1024]{1,0:T(8,128)(2,1)S(1)}, bf16[384,1024]{1,0:T(8,128)(2,1)S(1)}, u32[]{:S(2)}, u32[]{:S(2)}) collective-permute-start(bf16[384,1024]{1,0:T(8,128)(2,1)S(1)} %get-tuple-element.103), channel_id=1, source_target_pairs={{0,8},{4,20},{8,0},{12,28},{16,24},{20,4},{24,16},{28,12},{1,9},{5... | collective-permute-start | bytes 2359304 | tf_op jit(solution)/shard_map/ppermute | solution.py:384
  41.6 1.6 %collective-permute-start.8 = (bf16[128,1024]{1,0:T(8,128)(2,1)S(1)}, bf16[128,1024]{1,0:T(8,128)(2,1)S(1)}, u32[]{:S(2)}, u32[]{:S(2)}) collective-permute-start(bf16[128,1024]{1,0:T(8,128)(2,1)S(1)} %get-tuple-element.89), channel_id=1, source_target_pairs={{0,4},{4,0},{8,12},{12,8},{16,20},{20,16},{24,28},{28,24},{1,5},{5... | collective-permute-start | bytes 786440 | tf_op jit(solution)/shard_map/ppermute | solution.py:379
  41.7 1.9 %collective-permute-start.9 = (bf16[128,1024]{1,0:T(8,128)(2,1)S(1)}, bf16[128,1024]{1,0:T(8,128)(2,1)S(1)}, u32[]{:S(2)}, u32[]{:S(2)}) collective-permute-start(bf16[128,1024]{1,0:T(8,128)(2,1)S(1)} %get-tuple-element.90), channel_id=1, source_target_pairs={{0,4},{4,0},{8,12},{12,8},{16,20},{20,16},{24,28},{28,24},{1,5},{5... | collective-permute-start | bytes 786440 | tf_op jit(solution)/shard_map/ppermute | solution.py:379
  42.2 1.8 %collective-permute-start.10 = (bf16[128,1024]{1,0:T(8,128)(2,1)S(1)}, bf16[128,1024]{1,0:T(8,128)(2,1)S(1)}, u32[]{:S(2)}, u32[]{:S(2)}) collective-permute-start(bf16[128,1024]{1,0:T(8,128)(2,1)S(1)} %get-tuple-element.91), channel_id=1, source_target_pairs={{0,4},{4,0},{8,12},{12,8},{16,20},{20,16},{24,28},{28,24},{1,5},{5... | collective-permute-start | bytes 786440 | tf_op jit(solution)/shard_map/ppermute | solution.py:379
  44.8 10.6 %collective-permute-start.11 = (bf16[384,256]{1,0:T(8,128)(2,1)S(1)}, bf16[384,256]{1,0:T(8,128)(2,1)S(1)}, u32[]{:S(2)}, u32[]{:S(2)}) collective-permute-start(bf16[384,256]{1,0:T(8,128)(2,1)S(1)} %get-tuple-element.94), channel_id=1, source_target_pairs={{0,1},{1,0},{2,3},{3,2},{4,5},{5,4},{6,7},{7,6},{8,9},{9,8},{10,11... | collective-permute-start | bytes 589832 | tf_op jit(solution)/shard_map/ppermute | solution.py:379
  46.6 17.1 %collective-permute-start.12 = (bf16[384,256]{1,0:T(8,128)(2,1)S(1)}, bf16[384,256]{1,0:T(8,128)(2,1)S(1)}, u32[]{:S(2)}, u32[]{:S(2)}) collective-permute-start(bf16[384,256]{1,0:T(8,128)(2,1)S(1)} %get-tuple-element.95), channel_id=1, source_target_pairs={{0,2},{1,3},{2,0},{3,1},{4,6},{5,7},{6,4},{7,5},{8,10},{9,11},{10,... | collective-permute-start | bytes 589832 | tf_op jit(solution)/shard_map/ppermute | solution.py:379
  49.2 14.5 %collective-permute-start.13 = (bf16[384,256]{1,0:T(8,128)(2,1)S(1)}, bf16[384,256]{1,0:T(8,128)(2,1)S(1)}, u32[]{:S(2)}, u32[]{:S(2)}) collective-permute-start(bf16[384,256]{1,0:T(8,128)(2,1)S(1)} %get-tuple-element.96), channel_id=1, source_target_pairs={{0,3},{1,2},{2,1},{3,0},{4,7},{5,6},{6,5},{7,4},{8,11},{9,10},{10,... | collective-permute-start | bytes 589832 | tf_op jit(solution)/shard_map/ppermute | solution.py:379
  53.4 12.1 %collective-permute-start.16 = (bf16[384,1024]{1,0:T(8,128)(2,1)S(1)}, bf16[384,1024]{1,0:T(8,128)(2,1)S(1)}, u32[]{:S(2)}, u32[]{:S(2)}) collective-permute-start(bf16[384,1024]{1,0:T(8,128)(2,1)S(1)} %shard_map.98), channel_id=1, source_target_pairs={{0,16},{4,12},{8,24},{12,4},{16,0},{20,28},{24,8},{28,20},{1,17},{... | collective-permute-start | bytes 2359304 | tf_op jit(solution)/shard_map/ppermute | solution.py:384
where the time goes:
time: 67.2 us; the launch traced here: 66.9 us
  waiting for transfers between devices  25.3 us (38%)
  starting transfers between devices  19.9 us (30%)
  Pallas kernels  16.1 us (24%)
  local copies, waits for them, and re-layouts  3.47 us (5%)
  between operations  2.1 us (3%)
    pallas_call x14, Pallas kernels, call_kernel(): pl.pallas_call(body, out_shape=outs, in_specs=specs, out_specs=[ANY_SPEC...  16.1 us
    ppermute x6, waiting for transfers between devices, swap_near(): lax.ppermute(value, 'blk', [(i, i ^ neighbour_bits(i)[which]) for i in ra...  15.1 us
    ppermute x11, waiting for transfers between devices, swap(): return lax.ppermute(value, axis, [(i, i ^ bits) for i in range(count)])  10.2 us
    ppermute x11, starting transfers between devices, swap(): return lax.ppermute(value, axis, [(i, i ^ bits) for i in range(count)])  10.1 us
    ppermute x6, starting transfers between devices, swap_near(): lax.ppermute(value, 'blk', [(i, i ^ neighbour_bits(i)[which]) for i in ra...  9.81 us
    unnamed x10, local copies, waits for them, and re-layouts  3.47 us
  transfers between devices with their start and end apart: 17, of which 8 were waited for; matrix products, arithmetic and copies ran while one was open for 0% of the time, Pallas kernels for 22%

commit v1 on v0

--- a/solution.py
+++ b/solution.py
@@ -409,12 +409,7 @@
         from_second = swap_near(image_sent, 1)
         from_first = swap_near(image_sent, 0)
         from_far = swap_near(from_second, 0)
-        own_images, near_images = call_kernel(
-            unit_images_body,
-            [bf16(rows), bf16(2 * rows)],
-            [image_emb, from_first, from_second],
-            limit=8,
-        )
+        blocks, from_second = lax.optimization_barrier((blocks, from_second))
     else:
         same_core = [[chip * CORES + core for chip in range(chips)] for core in range(CORES)]
         gathered = lax.all_gather(
@@ -442,9 +437,7 @@
         limit=8,
     )
     if square:
-        text_raw[-1], own_images, *lists = lax.optimization_barrier(
-            (text_raw[-1], own_images, *lists)
-        )
+        text_raw[-1], *lists = lax.optimization_barrier((text_raw[-1], *lists))
     text_own, *pieces = call_kernel(
         functools.partial(unit_text_body, groups),
         [bf16(rows)] + [bf16(rows // TEXT_PIECES)] * TEXT_PIECES,
@@ -452,6 +445,14 @@
         limit=8,
     )
     text_other = [swap(piece, "blk", 1) for piece in pieces]
+    if square:
+        from_first, text_own = lax.optimization_barrier((from_first, text_own))
+        own_images, near_images = call_kernel(
+            unit_images_body,
+            [bf16(rows), bf16(2 * rows)],
+            [image_emb, from_first, from_second],
+            limit=8,
+        )
     unit_flops = 2 * rows * rows * embed
 
     def finish_text(acc_own, acc_other):

time: 67.2 us -> 67.2 us (level)
  no operation moved by 1% of the time
where the time goes in v1:
time: 67.2 us; the launch traced here: 66.8 us
  waiting for transfers between devices  25.3 us (38%)
  starting transfers between devices  19.9 us (30%)
  Pallas kernels  16.1 us (24%)
  local copies, waits for them, and re-layouts  3.43 us (5%)
  between operations  2.1 us (3%)
    pallas_call x14, Pallas kernels, call_kernel(): pl.pallas_call(body, out_shape=outs, in_specs=specs, out_specs=[ANY_SPEC...  16.1 us
    ppermute x6, waiting for transfers between devices, swap_near(): lax.ppermute(value, 'blk', [(i, i ^ neighbour_bits(i)[which]) for i in ra...  15.1 us
    ppermute x11, waiting for transfers between devices, swap(): return lax.ppermute(value, axis, [(i, i ^ bits) for i in range(count)])  10.2 us
    ppermute x11, starting transfers between devices, swap(): return lax.ppermute(value, axis, [(i, i ^ bits) for i in range(count)])  10.1 us
    ppermute x6, starting transfers between devices, swap_near(): lax.ppermute(value, 'blk', [(i, i ^ neighbour_bits(i)[which]) for i in ra...  9.81 us
    unnamed x10, local copies, waits for them, and re-layouts  3.43 us
  transfers between devices with their start and end apart: 17, of which 8 were waited for; matrix products, arithmetic and copies ran while one was open for 0% of the time, Pallas kernels for 22%

profile of v1, /device:TPU:0, one launch (start us, length us, event | category | flops | bytes accessed | tf_op | source)
XLA Modules:
  0.0 66.8 jit_solution(17356033160838816955)
XLA Ops:
  0.6 1.1 %copy-done.1 = bf16[1536,256]{1,0:T(8,128)(2,1)S(1)} copy-done((bf16[1536,256]{1,0:T(8,128)(2,1)S(1)}, bf16[1536,256]{1,0:T(8,128)(2,1)}, u32[]{:S(2)}) %copy-start.1) | copy-done | bytes 786456
  1.8 0.1 shard_map.86
  1.8 3.0 %collective-permute-start.1 = (bf16[384,1024]{1,0:T(8,128)(2,1)}, bf16[384,1024]{1,0:T(8,128)(2,1)S(1)}, u32[]{:S(2)}, u32[]{:S(2)}) collective-permute-start(bf16[384,1024]{1,0:T(8,128)(2,1)} %raw_ref.1), channel_id=1, source_target_pairs={{0,16},{4,12},{8,24},{12,4},{16,0},{20,28},{24,8},{28,20},{1,17},{... | collective-permute-start | bytes 2359304 | tf_op jit(solution)/shard_map/ppermute | solution.py:384
  4.9 1.5 %collective-permute-start.2 = (bf16[384,1024]{1,0:T(8,128)(2,1)}, bf16[384,1024]{1,0:T(8,128)(2,1)S(1)}, u32[]{:S(2)}, u32[]{:S(2)}) collective-permute-start(bf16[384,1024]{1,0:T(8,128)(2,1)} %raw_ref.1), channel_id=1, source_target_pairs={{0,8},{4,20},{8,0},{12,28},{16,24},{20,4},{24,16},{28,12},{1,9},{5... | collective-permute-start | bytes 2359304 | tf_op jit(solution)/shard_map/ppermute | solution.py:384
  6.3 3.6 %collective-permute-start = (bf16[384,256]{1,0:T(8,128)(2,1)S(1)}, bf16[384,256]{1,0:T(8,128)(2,1)S(1)}, u32[]{:S(2)}, u32[]{:S(2)}) collective-permute-start(bf16[384,256]{1,0:T(8,128)(2,1)S(1)} %get-tuple-element.57), channel_id=1, source_target_pairs={{0,3},{1,2},{2,1},{3,0},{4,7},{5,6},{6,5},{7,4},{8,11},{9,10},{10,... | collective-permute-start | bytes 589832 | tf_op jit(solution)/shard_map/ppermute | solution.py:379
  9.9 0.0 collective-permute-start.3
  9.9 0.8 %collective-permute-start.4 = (bf16[384,256]{1,0:T(8,128)(2,1)S(1)}, bf16[384,256]{1,0:T(8,128)(2,1)S(1)}, u32[]{:S(2)}, u32[]{:S(2)}) collective-permute-start(bf16[384,256]{1,0:T(8,128)(2,1)S(1)} %get-tuple-element.74), channel_id=1, source_target_pairs={{0,2},{1,3},{2,0},{3,1},{4,6},{5,7},{6,4},{7,5},{8,10},{9,11},{10,... | collective-permute-start | bytes 589832 | tf_op jit(solution)/shard_map/ppermute | solution.py:379
  12.0 11.0 %collective-permute-done.1.second_ref = bf16[384,1024]{1,0:T(8,128)(2,1)S(1)} collective-permute-done((bf16[384,1024]{1,0:T(8,128)(2,1)}, bf16[384,1024]{1,0:T(8,128)(2,1)S(1)}, u32[]{:S(2)}, u32[]{:S(2)}) %collective-permute-start.1) | collective-permute-done | bytes 786464 | tf_op jit(solution)/shard_map/ppermute | solution.py:384
  23.0 1.4 %collective-permute-start.7 = (bf16[384,1024]{1,0:T(8,128)(2,1)S(1)}, bf16[384,1024]{1,0:T(8,128)(2,1)S(1)}, u32[]{:S(2)}, u32[]{:S(2)}) collective-permute-start(bf16[384,1024]{1,0:T(8,128)(2,1)S(1)} %collective-permute-done.1.second_ref), channel_id=1, source_target_pairs={{0,8},{4,20},{8,0},{12,28},{16,24},{20,4},{24,16},{28,12},{1,9},{5... | collective-permute-start | bytes 2359304 | tf_op jit(solution)/shard_map/ppermute | solution.py:384
  24.4 0.8 %copy-done.2 = s32[12288]{0:T(1024)S(1)} copy-done((s32[12288]{0:T(1024)S(1)}, s32[12288]{0:T(1024)}, u32[]{:S(2)}) %copy-start.2) | copy-done | bytes 49176
  25.2 0.8 %copy-done.3 = s32[12288]{0:T(1024)S(1)} copy-done((s32[12288]{0:T(1024)S(1)}, s32[12288]{0:T(1024)}, u32[]{:S(2)}) %copy-start.3) | copy-done | bytes 49176
  26.0 0.7 %copy-done.4 = s32[96,8,3]{0,1,2:T(8,128)S(1)} copy-done((s32[96,8,3]{0,1,2:T(8,128)S(1)}, s32[96,8,3]{0,1,2:T(8,128)}, u32[]{:S(2)}) %copy-start.4) | copy-done | bytes 9240
  26.7 1.1 %shard_map.87 = (f32[2,128]{1,0:T(2,128)S(1)}, f32[72,128]{1,0:T(8,128)S(1)}, s32[12,128]{1,0:T(8,128)S(1)}, s32[768,128]{1,0:T(8,128)S(1)}, f32[384,128]{1,0:T(8,128)S(1)}, /*index=5*/f32[4,128]{1,0:T(4,128)S(1)}) custom-call(f32[1]{0:T(128)S(6)} %copy.9.refs_0_, f32[1]{0:T(128)S(6)} %copy.10.refs_1_, s32[3,8,96]{2,1,0:T(8,128)S(1)} %bitcast.5, ...), custom_call_target="tpu_custom_call" | custom-call | flops 10000000000 | bytes 743432 | tf_op jit(solution)/shard_map/pallas_call | solution.py:43
  27.8 0.0 collective-permute-done.refs_3_
  27.8 0.0 collective-permute-done.3.refs_1_
  27.8 0.4 shard_map.88
  28.2 0.1 collective-permute-start.5
  28.3 0.5 collective-permute-start.6
  28.8 0.7 %shard_map.89 = (bf16[384,1024]{1,0:T(8,128)(2,1)S(1)}, bf16[768,1024]{1,0:T(8,128)(2,1)S(1)}) custom-call(bf16[384,1024]{1,0:T(8,128)(2,1)S(1)} %copy-done, bf16[384,1024]{1,0:T(8,128)(2,1)S(1)} %collective-permute-done.2.first_ref, bf16[384,1024]{1,0:T(8,128)(2,1)S(1)} %collective-permute-done.1.second_ref), custom_call_target="tpu_custom_call" | custom-call | bytes 4718592 | tf_op jit(solution)/shard_map/pallas_call | solution.py:43
  29.6 1.8 %shard_map.90 = (bf16[384,384]{1,0:T(8,128)(2,1)S(1)}, bf16[384,768]{1,0:T(8,128)(2,1)S(1)}) custom-call(f32[2,128]{1,0:T(2,128)S(1)} %get-tuple-element.66.refs_0_, f32[72,128]{1,0:T(8,128)S(1)} %get-tuple-element.67.refs_1_, s32[12,128]{1,0:T(8,128)S(1)} %get-tuple-element.68.refs_2_, s32[768,128]{1,0:T(8,128)S(1)} %get-tuple-element.69.refs_3_, ...), custom_call_target="tpu_custom_call" | custom-call | bytes 4666368 | tf_op jit(solution)/shard_map/pallas_call | solution.py:43
  31.3 0.0 collective-permute-done.5.refs_9_
  31.4 1.4 %shard_map.91 = (bf16[768,1024]{1,0:T(8,128)(2,1)S(1)}, bf16[768,384]{1,0:T(8,128)(2,1)S(1)}, bf16[384,1024]{1,0:T(8,128)(2,1)S(1)}) custom-call(f32[2,128]{1,0:T(2,128)S(1)} %get-tuple-element.66.refs_0_, f32[72,128]{1,0:T(8,128)S(1)} %get-tuple-element.67.refs_1_, s32[12,128]{1,0:T(8,128)S(1)} %get-tuple-element.68.refs_2_, ...), custom_call_target="tpu_custom_call" | custom-call | bytes 7320576 | tf_op jit(solution)/shard_map/pallas_call | solution.py:43
  32.8 0.7 %collective-permute-start.14 = (bf16[384,1024]{1,0:T(8,128)(2,1)S(1)}, bf16[384,1024]{1,0:T(8,128)(2,1)S(1)}, u32[]{:S(2)}, u32[]{:S(2)}) collective-permute-start(bf16[384,1024]{1,0:T(8,128)(2,1)S(1)} %get-tuple-element.104), channel_id=1, source_target_pairs={{0,8},{4,20},{8,0},{12,28},{16,24},{20,4},{24,16},{28,12},{1,9},{5... | collective-permute-start | bytes 2359304 | tf_op jit(solution)/shard_map/ppermute | solution.py:384
  33.5 1.9 %shard_map.92 = (bf16[768,384]{1,0:T(8,128)(2,1)S(1)}, bf16[768,768]{1,0:T(8,128)(2,1)S(1)}, f32[384,1024]{1,0:T(8,128)S(1)}) custom-call(f32[2,128]{1,0:T(2,128)S(1)} %get-tuple-element.66.refs_0_, f32[72,128]{1,0:T(8,128)S(1)} %get-tuple-element.67.refs_1_, s32[12,128]{1,0:T(8,128)S(1)} %get-tuple-element.68.refs_2_, ...), custom_call_target="tpu_custom_call" | custom-call | bytes 9384960 | tf_op jit(solution)/shard_map/pallas_call | solution.py:43
  35.3 0.0 collective-permute-done.7.refs_9_
  35.4 2.2 %shard_map.93 = (bf16[384,1024]{1,0:T(8,128)(2,1)S(1)}, bf16[768,768]{1,0:T(8,128)(2,1)S(1)}, bf16[768,1024]{1,0:T(8,128)(2,1)S(1)}) custom-call(f32[2,128]{1,0:T(2,128)S(1)} %get-tuple-element.66.refs_0_, f32[72,128]{1,0:T(8,128)S(1)} %get-tuple-element.67.refs_1_, s32[12,128]{1,0:T(8,128)S(1)} %get-tuple-element.68.refs_2_, ...), custom_call_target="tpu_custom_call" | custom-call | bytes 7910400 | tf_op jit(solution)/shard_map/pallas_call | solution.py:43
  37.5 1.4 %collective-permute-start.15 = (bf16[384,1024]{1,0:T(8,128)(2,1)S(1)}, bf16[384,1024]{1,0:T(8,128)(2,1)S(1)}, u32[]{:S(2)}, u32[]{:S(2)}) collective-permute-start(bf16[384,1024]{1,0:T(8,128)(2,1)S(1)} %get-tuple-element.109), channel_id=1, source_target_pairs={{0,8},{4,20},{8,0},{12,28},{16,24},{20,4},{24,16},{28,12},{1,9},{5... | collective-permute-start | bytes 2359304 | tf_op jit(solution)/shard_map/ppermute | solution.py:384
  39.0 2.6 %shard_map.94 = (f32[384,1024]{1,0:T(8,128)S(1)}, bf16[128,1024]{1,0:T(8,128)(2,1)S(1)}, bf16[128,1024]{1,0:T(8,128)(2,1)S(1)}, bf16[128,1024]{1,0:T(8,128)(2,1)S(1)}) custom-call(bf16[768,768]{1,0:T(8,128)(2,1)S(1)} %get-tuple-element.92.near_weight_ref, bf16[768,1024]{1,0:T(8,128)(2,1)S(1)} %get-tuple-element.80.refs_8_.refs_7_.near_image_ref, ...), custom_call_target="tpu_custom_call" | custom-call | bytes 7864320 | tf_op jit(solution)/shard_map/pallas_call | solution.py:43
  41.6 0.1 collective-permute-start.8
  41.7 0.5 collective-permute-start.9
  42.2 0.1 collective-permute-start.10
  42.2 0.9 %collective-permute-done.8.refs_5_ = bf16[128,1024]{1,0:T(8,128)(2,1)S(1)} collective-permute-done((bf16[128,1024]{1,0:T(8,128)(2,1)S(1)}, bf16[128,1024]{1,0:T(8,128)(2,1)S(1)}, u32[]{:S(2)}, u32[]{:S(2)}) %collective-permute-start.8) | collective-permute-done | bytes 262176 | tf_op jit(solution)/shard_map/ppermute | solution.py:379
  43.2 0.4 collective-permute-done.9.refs_6_
  43.6 0.4 collective-permute-done.10.refs_7_
  43.9 0.8 %shard_map.95 = (bf16[384,256]{1,0:T(8,128)(2,1)S(1)}, bf16[384,256]{1,0:T(8,128)(2,1)S(1)}, bf16[384,256]{1,0:T(8,128)(2,1)S(1)}, bf16[384,256]{1,0:T(8,128)(2,1)S(1)}) custom-call(bf16[384,256]{1,0:T(8,128)(2,1)S(1)} %get-tuple-element.72.refs_0_, bf16[384,256]{1,0:T(8,128)(2,1)S(1)} %collective-permute-done.3.refs_1_, ...), custom_call_target="tpu_custom_call" | custom-call | bytes 3932160 | tf_op jit(solution)/shard_map/pallas_call | solution.py:43
  44.7 1.8 %collective-permute-start.11 = (bf16[384,256]{1,0:T(8,128)(2,1)S(1)}, bf16[384,256]{1,0:T(8,128)(2,1)S(1)}, u32[]{:S(2)}, u32[]{:S(2)}) collective-permute-start(bf16[384,256]{1,0:T(8,128)(2,1)S(1)} %get-tuple-element.100), channel_id=1, source_target_pairs={{0,1},{1,0},{2,3},{3,2},{4,5},{5,4},{6,7},{7,6},{8,9},{9,8},{10,11... | collective-permute-start | bytes 589832 | tf_op jit(solution)/shard_map/ppermute | solution.py:379
  46.5 2.6 %collective-permute-start.12 = (bf16[384,256]{1,0:T(8,128)(2,1)S(1)}, bf16[384,256]{1,0:T(8,128)(2,1)S(1)}, u32[]{:S(2)}, u32[]{:S(2)}) collective-permute-start(bf16[384,256]{1,0:T(8,128)(2,1)S(1)} %get-tuple-element.101), channel_id=1, source_target_pairs={{0,2},{1,3},{2,0},{3,1},{4,6},{5,7},{6,4},{7,5},{8,10},{9,11},{10,... | collective-permute-start | bytes 589832 | tf_op jit(solution)/shard_map/ppermute | solution.py:379
  49.1 0.1 collective-permute-start.13
  49.2 0.0 collective-permute-done.14.add_ref
  49.2 0.8 %shard_map.97.refs_0_ = f32[384,1024]{1,0:T(8,128)S(1)} custom-call(bf16[768,768]{1,0:T(8,128)(2,1)S(1)} %get-tuple-element.103.weight_ref, bf16[768,1024]{1,0:T(8,128)(2,1)S(1)} %get-tuple-element.85.refs_6_.unit_ref, bf16[384,1024]{1,0:T(8,128)(2,1)S(1)} %collective-permute-done.14.add_ref), custom_call_target="tpu_custom_call" | custom-call | bytes 5111808 | tf_op jit(solution)/shard_map/pallas_call | solution.py:43
  50.0 3.2 %collective-permute-done.15.in_ref = bf16[384,1024]{1,0:T(8,128)(2,1)S(1)} collective-permute-done((bf16[384,1024]{1,0:T(8,128)(2,1)S(1)}, bf16[384,1024]{1,0:T(8,128)(2,1)S(1)}, u32[]{:S(2)}, u32[]{:S(2)}) %collective-permute-start.15) | collective-permute-done | bytes 786464 | tf_op jit(solution)/shard_map/ppermute | solution.py:384
  53.2 0.1 shard_map.98
  53.4 1.7 %collective-permute-start.16 = (bf16[384,1024]{1,0:T(8,128)(2,1)S(1)}, bf16[384,1024]{1,0:T(8,128)(2,1)S(1)}, u32[]{:S(2)}, u32[]{:S(2)}) collective-permute-start(bf16[384,1024]{1,0:T(8,128)(2,1)S(1)} %shard_map.98), channel_id=1, source_target_pairs={{0,16},{4,12},{8,24},{12,4},{16,0},{20,28},{24,8},{28,20},{1,17},{... | collective-permute-start | bytes 2359304 | tf_op jit(solution)/shard_map/ppermute | solution.py:384
  55.1 0.3 collective-permute-done.11.refs_1_
  55.4 8.3 %collective-permute-done.12.refs_2_ = bf16[384,256]{1,0:T(8,128)(2,1)S(1)} collective-permute-done((bf16[384,256]{1,0:T(8,128)(2,1)S(1)}, bf16[384,256]{1,0:T(8,128)(2,1)S(1)}, u32[]{:S(2)}, u32[]{:S(2)}) %collective-permute-start.12) | collective-permute-done | bytes 196640 | tf_op jit(solution)/shard_map/ppermute | solution.py:379
  63.6 0.9 %shard_map.96 = bf16[1536,256]{1,0:T(8,128)(2,1)} custom-call(bf16[384,256]{1,0:T(8,128)(2,1)S(1)} %get-tuple-element.99.refs_0_, bf16[384,256]{1,0:T(8,128)(2,1)S(1)} %collective-permute-done.11.refs_1_, bf16[384,256]{1,0:T(8,128)(2,1)S(1)} %collective-permute-done.12.refs_2_, bf16[384,256]{1,0:T(8,128)(2,1)S(1)} %collective-permute-done.13.refs_3_), custom_call_target="tpu_custom_call" | custom-call | flops 20000000000 | bytes 1572864 | tf_op jit(solution)/shard_map/pallas_call | solution.py:43
  64.6 0.9 %collective-permute-done.16.refs_1_ = bf16[384,1024]{1,0:T(8,128)(2,1)S(1)} collective-permute-done((bf16[384,1024]{1,0:T(8,128)(2,1)S(1)}, bf16[384,1024]{1,0:T(8,128)(2,1)S(1)}, u32[]{:S(2)}, u32[]{:S(2)}) %collective-permute-start.16) | collective-permute-done | bytes 786464 | tf_op jit(solution)/shard_map/ppermute | solution.py:384
  65.4 1.4 %shard_map.99 = bf16[384,1024]{1,0:T(8,128)(2,1)} custom-call(bf16[384,1024]{1,0:T(8,128)(2,1)S(1)} %copy-done, f32[384,1024]{1,0:T(8,128)S(1)} %shard_map.97.refs_0_, bf16[384,1024]{1,0:T(8,128)(2,1)S(1)} %collective-permute-done.16.refs_1_), custom_call_target="tpu_custom_call" | custom-call | bytes 3932160 | tf_op jit(solution)/shard_map/pallas_call | solution.py:43
  (10 shorter events, 0.0 us)
Async XLA Ops:
  0.6 1.1 %copy-start.1 = (bf16[1536,256]{1,0:T(8,128)(2,1)S(1)}, bf16[1536,256]{1,0:T(8,128)(2,1)}, u32[]{:S(2)}) copy-start(bf16[1536,256]{1,0:T(8,128)(2,1)} %text_ref.1) | copy-start | bytes 2359300
  1.8 21.2 %collective-permute-start.1 = (bf16[384,1024]{1,0:T(8,128)(2,1)}, bf16[384,1024]{1,0:T(8,128)(2,1)S(1)}, u32[]{:S(2)}, u32[]{:S(2)}) collective-permute-start(bf16[384,1024]{1,0:T(8,128)(2,1)} %raw_ref.1), channel_id=1, source_target_pairs={{0,16},{4,12},{8,24},{12,4},{16,0},{20,28},{24,8},{28,20},{1,17},{... | collective-permute-start | bytes 2359304 | tf_op jit(solution)/shard_map/ppermute | solution.py:384
  4.9 24.0 %collective-permute-start.2 = (bf16[384,1024]{1,0:T(8,128)(2,1)}, bf16[384,1024]{1,0:T(8,128)(2,1)S(1)}, u32[]{:S(2)}, u32[]{:S(2)}) collective-permute-start(bf16[384,1024]{1,0:T(8,128)(2,1)} %raw_ref.1), channel_id=1, source_target_pairs={{0,8},{4,20},{8,0},{12,28},{16,24},{20,4},{24,16},{28,12},{1,9},{5... | collective-permute-start | bytes 2359304 | tf_op jit(solution)/shard_map/ppermute | solution.py:384
  6.3 21.5 %collective-permute-start = (bf16[384,256]{1,0:T(8,128)(2,1)S(1)}, bf16[384,256]{1,0:T(8,128)(2,1)S(1)}, u32[]{:S(2)}, u32[]{:S(2)}) collective-permute-start(bf16[384,256]{1,0:T(8,128)(2,1)S(1)} %get-tuple-element.57), channel_id=1, source_target_pairs={{0,3},{1,2},{2,1},{3,0},{4,7},{5,6},{6,5},{7,4},{8,11},{9,10},{10,... | collective-permute-start | bytes 589832 | tf_op jit(solution)/shard_map/ppermute | solution.py:379
  9.9 17.9 %collective-permute-start.3 = (bf16[384,256]{1,0:T(8,128)(2,1)S(1)}, bf16[384,256]{1,0:T(8,128)(2,1)S(1)}, u32[]{:S(2)}, u32[]{:S(2)}) collective-permute-start(bf16[384,256]{1,0:T(8,128)(2,1)S(1)} %get-tuple-element.73), channel_id=1, source_target_pairs={{0,1},{1,0},{2,3},{3,2},{4,5},{5,4},{6,7},{7,6},{8,9},{9,8},{10,11... | collective-permute-start | bytes 589832 | tf_op jit(solution)/shard_map/ppermute | solution.py:379
  9.9 17.9 %collective-permute-start.4 = (bf16[384,256]{1,0:T(8,128)(2,1)S(1)}, bf16[384,256]{1,0:T(8,128)(2,1)S(1)}, u32[]{:S(2)}, u32[]{:S(2)}) collective-permute-start(bf16[384,256]{1,0:T(8,128)(2,1)S(1)} %get-tuple-element.74), channel_id=1, source_target_pairs={{0,2},{1,3},{2,0},{3,1},{4,6},{5,7},{6,4},{7,5},{8,10},{9,11},{10,... | collective-permute-start | bytes 589832 | tf_op jit(solution)/shard_map/ppermute | solution.py:379
  23.0 12.3 %collective-permute-start.7 = (bf16[384,1024]{1,0:T(8,128)(2,1)S(1)}, bf16[384,1024]{1,0:T(8,128)(2,1)S(1)}, u32[]{:S(2)}, u32[]{:S(2)}) collective-permute-start(bf16[384,1024]{1,0:T(8,128)(2,1)S(1)} %collective-permute-done.1.second_ref), channel_id=1, source_target_pairs={{0,8},{4,20},{8,0},{12,28},{16,24},{20,4},{24,16},{28,12},{1,9},{5... | collective-permute-start | bytes 2359304 | tf_op jit(solution)/shard_map/ppermute | solution.py:384
  24.4 0.8 %copy-start.2 = (s32[12288]{0:T(1024)S(1)}, s32[12288]{0:T(1024)}, u32[]{:S(2)}) copy-start(s32[12288]{0:T(1024)} %param.11) | copy-start | bytes 147460
  25.2 0.8 %copy-start.3 = (s32[12288]{0:T(1024)S(1)}, s32[12288]{0:T(1024)}, u32[]{:S(2)}) copy-start(s32[12288]{0:T(1024)} %param.12) | copy-start | bytes 147460
  26.0 0.7 %copy-start.4 = (s32[96,8,3]{0,1,2:T(8,128)S(1)}, s32[96,8,3]{0,1,2:T(8,128)}, u32[]{:S(2)}) copy-start(s32[96,8,3]{0,1,2:T(8,128)} %param.13) | copy-start | bytes 27652
  26.7 2.1 %copy-start = (bf16[384,1024]{1,0:T(8,128)(2,1)S(1)}, bf16[384,1024]{1,0:T(8,128)(2,1)}, u32[]{:S(2)}) copy-start(bf16[384,1024]{1,0:T(8,128)(2,1)} %raw_ref.1) | copy-start | bytes 2359300
  28.2 3.1 %collective-permute-start.5 = (bf16[192,1024]{1,0:T(8,128)(2,1)S(1)}, bf16[192,1024]{1,0:T(8,128)(2,1)S(1)}, u32[]{:S(2)}, u32[]{:S(2)}) collective-permute-start(bf16[192,1024]{1,0:T(8,128)(2,1)S(1)} %get-tuple-element.83), channel_id=1, source_target_pairs={{0,4},{4,0},{8,12},{12,8},{16,20},{20,16},{24,28},{28,24},{1,5},{5... | collective-permute-start | bytes 1179656 | tf_op jit(solution)/shard_map/ppermute | solution.py:379
  28.3 3.0 %collective-permute-start.6 = (bf16[192,1024]{1,0:T(8,128)(2,1)S(1)}, bf16[192,1024]{1,0:T(8,128)(2,1)S(1)}, u32[]{:S(2)}, u32[]{:S(2)}) collective-permute-start(bf16[192,1024]{1,0:T(8,128)(2,1)S(1)} %get-tuple-element.84), channel_id=1, source_target_pairs={{0,4},{4,0},{8,12},{12,8},{16,20},{20,16},{24,28},{28,24},{1,5},{5... | collective-permute-start | bytes 1179656 | tf_op jit(solution)/shard_map/ppermute | solution.py:379
  32.8 16.4 %collective-permute-start.14 = (bf16[384,1024]{1,0:T(8,128)(2,1)S(1)}, bf16[384,1024]{1,0:T(8,128)(2,1)S(1)}, u32[]{:S(2)}, u32[]{:S(2)}) collective-permute-start(bf16[384,1024]{1,0:T(8,128)(2,1)S(1)} %get-tuple-element.104), channel_id=1, source_target_pairs={{0,8},{4,20},{8,0},{12,28},{16,24},{20,4},{24,16},{28,12},{1,9},{5... | collective-permute-start | bytes 2359304 | tf_op jit(solution)/shard_map/ppermute | solution.py:384
  37.5 15.7 %collective-permute-start.15 = (bf16[384,1024]{1,0:T(8,128)(2,1)S(1)}, bf16[384,1024]{1,0:T(8,128)(2,1)S(1)}, u32[]{:S(2)}, u32[]{:S(2)}) collective-permute-start(bf16[384,1024]{1,0:T(8,128)(2,1)S(1)} %get-tuple-element.109), channel_id=1, source_target_pairs={{0,8},{4,20},{8,0},{12,28},{16,24},{20,4},{24,16},{28,12},{1,9},{5... | collective-permute-start | bytes 2359304 | tf_op jit(solution)/shard_map/ppermute | solution.py:384
  41.6 1.6 %collective-permute-start.8 = (bf16[128,1024]{1,0:T(8,128)(2,1)S(1)}, bf16[128,1024]{1,0:T(8,128)(2,1)S(1)}, u32[]{:S(2)}, u32[]{:S(2)}) collective-permute-start(bf16[128,1024]{1,0:T(8,128)(2,1)S(1)} %get-tuple-element.95), channel_id=1, source_target_pairs={{0,4},{4,0},{8,12},{12,8},{16,20},{20,16},{24,28},{28,24},{1,5},{5... | collective-permute-start | bytes 786440 | tf_op jit(solution)/shard_map/ppermute | solution.py:379
  41.7 1.9 %collective-permute-start.9 = (bf16[128,1024]{1,0:T(8,128)(2,1)S(1)}, bf16[128,1024]{1,0:T(8,128)(2,1)S(1)}, u32[]{:S(2)}, u32[]{:S(2)}) collective-permute-start(bf16[128,1024]{1,0:T(8,128)(2,1)S(1)} %get-tuple-element.96), channel_id=1, source_target_pairs={{0,4},{4,0},{8,12},{12,8},{16,20},{20,16},{24,28},{28,24},{1,5},{5... | collective-permute-start | bytes 786440 | tf_op jit(solution)/shard_map/ppermute | solution.py:379
  42.2 1.8 %collective-permute-start.10 = (bf16[128,1024]{1,0:T(8,128)(2,1)S(1)}, bf16[128,1024]{1,0:T(8,128)(2,1)S(1)}, u32[]{:S(2)}, u32[]{:S(2)}) collective-permute-start(bf16[128,1024]{1,0:T(8,128)(2,1)S(1)} %get-tuple-element.97), channel_id=1, source_target_pairs={{0,4},{4,0},{8,12},{12,8},{16,20},{20,16},{24,28},{28,24},{1,5},{5... | collective-permute-start | bytes 786440 | tf_op jit(solution)/shard_map/ppermute | solution.py:379
  44.7 10.6 %collective-permute-start.11 = (bf16[384,256]{1,0:T(8,128)(2,1)S(1)}, bf16[384,256]{1,0:T(8,128)(2,1)S(1)}, u32[]{:S(2)}, u32[]{:S(2)}) collective-permute-start(bf16[384,256]{1,0:T(8,128)(2,1)S(1)} %get-tuple-element.100), channel_id=1, source_target_pairs={{0,1},{1,0},{2,3},{3,2},{4,5},{5,4},{6,7},{7,6},{8,9},{9,8},{10,11... | collective-permute-start | bytes 589832 | tf_op jit(solution)/shard_map/ppermute | solution.py:379
  46.5 17.1 %collective-permute-start.12 = (bf16[384,256]{1,0:T(8,128)(2,1)S(1)}, bf16[384,256]{1,0:T(8,128)(2,1)S(1)}, u32[]{:S(2)}, u32[]{:S(2)}) collective-permute-start(bf16[384,256]{1,0:T(8,128)(2,1)S(1)} %get-tuple-element.101), channel_id=1, source_target_pairs={{0,2},{1,3},{2,0},{3,1},{4,6},{5,7},{6,4},{7,5},{8,10},{9,11},{10,... | collective-permute-start | bytes 589832 | tf_op jit(solution)/shard_map/ppermute | solution.py:379
  49.1 14.5 %collective-permute-start.13 = (bf16[384,256]{1,0:T(8,128)(2,1)S(1)}, bf16[384,256]{1,0:T(8,128)(2,1)S(1)}, u32[]{:S(2)}, u32[]{:S(2)}) collective-permute-start(bf16[384,256]{1,0:T(8,128)(2,1)S(1)} %get-tuple-element.102), channel_id=1, source_target_pairs={{0,3},{1,2},{2,1},{3,0},{4,7},{5,6},{6,5},{7,4},{8,11},{9,10},{10,... | collective-permute-start | bytes 589832 | tf_op jit(solution)/shard_map/ppermute | solution.py:379
  53.4 12.1 %collective-permute-start.16 = (bf16[384,1024]{1,0:T(8,128)(2,1)S(1)}, bf16[384,1024]{1,0:T(8,128)(2,1)S(1)}, u32[]{:S(2)}, u32[]{:S(2)}) collective-permute-start(bf16[384,1024]{1,0:T(8,128)(2,1)S(1)} %shard_map.98), channel_id=1, source_target_pairs={{0,16},{4,12},{8,24},{12,4},{16,0},{20,28},{24,8},{28,20},{1,17},{... | collective-permute-start | bytes 2359304 | tf_op jit(solution)/shard_map/ppermute | solution.py:384

commit v2 on v1

--- a/solution.py
+++ b/solution.py
@@ -121,9 +121,14 @@
         start += ref.shape[0]
 
 
-def unit_images_body(own_ref, first_ref, second_ref, own_out_ref, near_out_ref):
-    unit_images([own_ref], own_out_ref)
-    unit_images([first_ref, second_ref], near_out_ref)
+def unit_images_body(raw_ref, out_ref):
+    unit_images([raw_ref], out_ref)
+
+
+def near_images_body(first_ref, second_unit_ref, out_ref):
+    rows = first_ref.shape[0]
+    unit_images([first_ref], out_ref)
+    out_ref[rows:, :] = second_unit_ref[...]
 
 
 def neighbour_bits(shard):
@@ -408,8 +413,6 @@
     if square:
         from_second = swap_near(image_sent, 1)
         from_first = swap_near(image_sent, 0)
-        from_far = swap_near(from_second, 0)
-        blocks, from_second = lax.optimization_barrier((blocks, from_second))
     else:
         same_core = [[chip * CORES + core for chip in range(chips)] for core in range(CORES)]
         gathered = lax.all_gather(
@@ -433,11 +436,18 @@
             positive.reshape(-1, TILE),
         ],
         scalars=3,
-        flops=WAIT_FLOPS // 2,
         limit=8,
     )
     if square:
-        text_raw[-1], *lists = lax.optimization_barrier((text_raw[-1], *lists))
+        own_images = call_kernel(unit_images_body, [bf16(rows)], [image_emb], limit=8)[0]
+        from_second, own_images, *lists = lax.optimization_barrier(
+            (from_second, own_images, *lists)
+        )
+        from_far = swap_near(from_second, 0)
+        second_images = call_kernel(
+            unit_images_body, [bf16(rows)], [from_second], flops=WAIT_FLOPS // 2, limit=8
+        )[0]
+        text_raw[-1], second_images = lax.optimization_barrier((text_raw[-1], second_images))
     text_own, *pieces = call_kernel(
         functools.partial(unit_text_body, groups),
         [bf16(rows)] + [bf16(rows // TEXT_PIECES)] * TEXT_PIECES,
@@ -447,12 +457,9 @@
     text_other = [swap(piece, "blk", 1) for piece in pieces]
     if square:
         from_first, text_own = lax.optimization_barrier((from_first, text_own))
-        own_images, near_images = call_kernel(
-            unit_images_body,
-            [bf16(rows), bf16(2 * rows)],
-            [image_emb, from_first, from_second],
-            limit=8,
-        )
+        near_images = call_kernel(
+            near_images_body, [bf16(2 * rows)], [from_first, second_images], limit=8
+        )[0]
     unit_flops = 2 * rows * rows * embed
 
     def finish_text(acc_own, acc_other):

time: 67.2 us -> 66.5 us (0.990)
  local copies, waits for them, and re-layouts: 3.43 us -> 2.28 us
  starting transfers between devices: 19.9 us -> 20.6 us
    ppermute x6, waiting for transfers between devices: 15.1 us -> 13 us  [swap_near(): lax.ppermute(value, 'blk', [(i, i ^ neighbour_bits(i)[which]) for i in ra...]
    ppermute x11, waiting for transfers between devices: 10.2 us -> 11.8 us  [swap(): return lax.ppermute(value, axis, [(i, i ^ bits) for i in range(count)])]
    unnamed x10 -> x12, local copies, waits for them, and re-layouts: 3.43 us -> 2.28 us
    ppermute x6, starting transfers between devices: 9.81 us -> 10.6 us  [swap_near(): lax.ppermute(value, 'blk', [(i, i ^ neighbour_bits(i)[which]) for i in ra...]
    pallas_call x14 -> x16, Pallas kernels: 16.1 us -> 16.1 us  [call_kernel(): pl.pallas_call(body, out_shape=outs, in_specs=specs, out_specs=[ANY_SPEC...]
  transfers between devices with their start and end apart: 17 -> 17, of which waited for: 8 -> 10; matrix products, arithmetic and copies ran while one was open for 0% -> 0% of each run, Pallas kernels for 22% -> 22%
where the time goes in v2:
time: 66.5 us; the launch traced here: 66 us
  waiting for transfers between devices  24.8 us (37%)
  starting transfers between devices  20.6 us (31%)
  Pallas kernels  16.1 us (24%)
  local copies, waits for them, and re-layouts  2.28 us (3%)
  between operations  2.12 us (3%)
    pallas_call x16, Pallas kernels, call_kernel(): pl.pallas_call(body, out_shape=outs, in_specs=specs, out_specs=[ANY_SPEC...  16.1 us
    ppermute x6, waiting for transfers between devices, swap_near(): lax.ppermute(value, 'blk', [(i, i ^ neighbour_bits(i)[which]) for i in ra...  13 us
    ppermute x11, waiting for transfers between devices, swap(): return lax.ppermute(value, axis, [(i, i ^ bits) for i in range(count)])  11.8 us
    ppermute x6, starting transfers between devices, swap_near(): lax.ppermute(value, 'blk', [(i, i ^ neighbour_bits(i)[which]) for i in ra...  10.6 us
    ppermute x11, starting transfers between devices, swap(): return lax.ppermute(value, axis, [(i, i ^ bits) for i in range(count)])  10.1 us
    unnamed x12, local copies, waits for them, and re-layouts  2.28 us
  transfers between devices with their start and end apart: 17, of which 10 were waited for; matrix products, arithmetic and copies ran while one was open for 0% of the time, Pallas kernels for 22%

profile of v2, /device:TPU:0, one launch (start us, length us, event | category | flops | bytes accessed | tf_op | source)
XLA Modules:
  0.0 66.0 jit_solution(13029627013418343184)
XLA Ops:
  0.6 1.1 %copy-done.2 = bf16[1536,256]{1,0:T(8,128)(2,1)S(1)} copy-done((bf16[1536,256]{1,0:T(8,128)(2,1)S(1)}, bf16[1536,256]{1,0:T(8,128)(2,1)}, u32[]{:S(2)}) %copy-start.2) | copy-done | bytes 786456
  1.8 0.1 shard_map.86
  1.8 3.0 %collective-permute-start = (bf16[384,1024]{1,0:T(8,128)(2,1)}, bf16[384,1024]{1,0:T(8,128)(2,1)S(1)}, u32[]{:S(2)}, u32[]{:S(2)}) collective-permute-start(bf16[384,1024]{1,0:T(8,128)(2,1)} %raw_ref.3), channel_id=1, source_target_pairs={{0,16},{4,12},{8,24},{12,4},{16,0},{20,28},{24,8},{28,20},{1,17},{... | collective-permute-start | bytes 2359304 | tf_op jit(solution)/shard_map/ppermute | solution.py:389
  4.9 1.5 %collective-permute-start.1 = (bf16[384,1024]{1,0:T(8,128)(2,1)}, bf16[384,1024]{1,0:T(8,128)(2,1)S(1)}, u32[]{:S(2)}, u32[]{:S(2)}) collective-permute-start(bf16[384,1024]{1,0:T(8,128)(2,1)} %raw_ref.3), channel_id=1, source_target_pairs={{0,8},{4,20},{8,0},{12,28},{16,24},{20,4},{24,16},{28,12},{1,9},{5... | collective-permute-start | bytes 2359304 | tf_op jit(solution)/shard_map/ppermute | solution.py:389
  6.3 3.6 %collective-permute-start.4 = (bf16[384,256]{1,0:T(8,128)(2,1)S(1)}, bf16[384,256]{1,0:T(8,128)(2,1)S(1)}, u32[]{:S(2)}, u32[]{:S(2)}) collective-permute-start(bf16[384,256]{1,0:T(8,128)(2,1)S(1)} %get-tuple-element.72), channel_id=1, source_target_pairs={{0,3},{1,2},{2,1},{3,0},{4,7},{5,6},{6,5},{7,4},{8,11},{9,10},{10,... | collective-permute-start | bytes 589832 | tf_op jit(solution)/shard_map/ppermute | solution.py:384
  10.0 0.0 collective-permute-start.2
  10.0 0.8 %collective-permute-start.3 = (bf16[384,256]{1,0:T(8,128)(2,1)S(1)}, bf16[384,256]{1,0:T(8,128)(2,1)S(1)}, u32[]{:S(2)}, u32[]{:S(2)}) collective-permute-start(bf16[384,256]{1,0:T(8,128)(2,1)S(1)} %get-tuple-element.71), channel_id=1, source_target_pairs={{0,2},{1,3},{2,0},{3,1},{4,6},{5,7},{6,4},{7,5},{8,10},{9,11},{10,... | collective-permute-start | bytes 589832 | tf_op jit(solution)/shard_map/ppermute | solution.py:384
  10.7 1.1 %copy-done = bf16[384,1024]{1,0:T(8,128)(2,1)S(1)} copy-done((bf16[384,1024]{1,0:T(8,128)(2,1)S(1)}, bf16[384,1024]{1,0:T(8,128)(2,1)}, u32[]{:S(2)}) %copy-start) | copy-done | bytes 786456
  11.9 0.2 shard_map.87.refs_7_
  13.4 1.1 %shard_map.88 = (f32[2,128]{1,0:T(2,128)S(1)}, f32[72,128]{1,0:T(8,128)S(1)}, s32[12,128]{1,0:T(8,128)S(1)}, s32[768,128]{1,0:T(8,128)S(1)}, f32[384,128]{1,0:T(8,128)S(1)}, /*index=5*/f32[4,128]{1,0:T(4,128)S(1)}) custom-call(f32[1]{0:T(128)S(6)} %copy.9.refs_0_, f32[1]{0:T(128)S(6)} %copy.10.refs_1_, s32[3,8,96]{2,1,0:T(8,128)S(1)} %bitcast.5, ...), custom_call_target="tpu_custom_call" | custom-call | bytes 743432 | tf_op jit(solution)/shard_map/pallas_call | solution.py:43
  14.5 8.5 %collective-permute-done.raw_ref = bf16[384,1024]{1,0:T(8,128)(2,1)S(1)} collective-permute-done((bf16[384,1024]{1,0:T(8,128)(2,1)}, bf16[384,1024]{1,0:T(8,128)(2,1)S(1)}, u32[]{:S(2)}, u32[]{:S(2)}) %collective-permute-start) | collective-permute-done | bytes 786464 | tf_op jit(solution)/shard_map/ppermute | solution.py:389
  23.0 1.4 %collective-permute-start.7 = (bf16[384,1024]{1,0:T(8,128)(2,1)S(1)}, bf16[384,1024]{1,0:T(8,128)(2,1)S(1)}, u32[]{:S(2)}, u32[]{:S(2)}) collective-permute-start(bf16[384,1024]{1,0:T(8,128)(2,1)S(1)} %collective-permute-done.raw_ref), channel_id=1, source_target_pairs={{0,8},{4,20},{8,0},{12,28},{16,24},{20,4},{24,16},{28,12},{1,9},{5... | collective-permute-start | bytes 2359304 | tf_op jit(solution)/shard_map/ppermute | solution.py:389
  24.4 0.2 shard_map.89.second_unit_ref
  24.7 0.0 collective-permute-done.4.refs_3_
  24.7 0.0 collective-permute-done.2.refs_1_
  24.7 1.4 %collective-permute-done.3.refs_2_ = bf16[384,256]{1,0:T(8,128)(2,1)S(1)} collective-permute-done((bf16[384,256]{1,0:T(8,128)(2,1)S(1)}, bf16[384,256]{1,0:T(8,128)(2,1)S(1)}, u32[]{:S(2)}, u32[]{:S(2)}) %collective-permute-start.3) | collective-permute-done | bytes 196640 | tf_op jit(solution)/shard_map/ppermute | solution.py:384
  26.1 0.4 shard_map.90
  26.5 0.1 collective-permute-start.5
  26.6 0.5 collective-permute-start.6
  27.1 0.3 shard_map.91.refs_8_.refs_7_.near_image_ref
  27.4 1.8 %shard_map.92 = (bf16[384,384]{1,0:T(8,128)(2,1)S(1)}, bf16[384,768]{1,0:T(8,128)(2,1)S(1)}) custom-call(f32[2,128]{1,0:T(2,128)S(1)} %get-tuple-element.63.refs_0_, f32[72,128]{1,0:T(8,128)S(1)} %get-tuple-element.64.refs_1_, s32[12,128]{1,0:T(8,128)S(1)} %get-tuple-element.65.refs_2_, s32[768,128]{1,0:T(8,128)S(1)} %get-tuple-element.66.refs_3_, ...), custom_call_target="tpu_custom_call" | custom-call | bytes 4666368 | tf_op jit(solution)/shard_map/pallas_call | solution.py:43
  29.2 1.4 %shard_map.93 = (bf16[768,1024]{1,0:T(8,128)(2,1)S(1)}, bf16[768,384]{1,0:T(8,128)(2,1)S(1)}, bf16[384,1024]{1,0:T(8,128)(2,1)S(1)}) custom-call(f32[2,128]{1,0:T(2,128)S(1)} %get-tuple-element.63.refs_0_, f32[72,128]{1,0:T(8,128)S(1)} %get-tuple-element.64.refs_1_, s32[12,128]{1,0:T(8,128)S(1)} %get-tuple-element.65.refs_2_, ...), custom_call_target="tpu_custom_call" | custom-call | bytes 7320576 | tf_op jit(solution)/shard_map/pallas_call | solution.py:43
  30.6 0.6 collective-permute-start.14
  31.2 1.9 %shard_map.94 = (bf16[768,384]{1,0:T(8,128)(2,1)S(1)}, bf16[768,768]{1,0:T(8,128)(2,1)S(1)}, f32[384,1024]{1,0:T(8,128)S(1)}) custom-call(f32[2,128]{1,0:T(2,128)S(1)} %get-tuple-element.63.refs_0_, f32[72,128]{1,0:T(8,128)S(1)} %get-tuple-element.64.refs_1_, s32[12,128]{1,0:T(8,128)S(1)} %get-tuple-element.65.refs_2_, ...), custom_call_target="tpu_custom_call" | custom-call | bytes 9384960 | tf_op jit(solution)/shard_map/pallas_call | solution.py:43
  33.0 2.0 %collective-permute-done.7.refs_9_ = bf16[384,1024]{1,0:T(8,128)(2,1)S(1)} collective-permute-done((bf16[384,1024]{1,0:T(8,128)(2,1)S(1)}, bf16[384,1024]{1,0:T(8,128)(2,1)S(1)}, u32[]{:S(2)}, u32[]{:S(2)}) %collective-permute-start.7) | collective-permute-done | bytes 786464 | tf_op jit(solution)/shard_map/ppermute | solution.py:389
  35.0 2.2 %shard_map.95 = (bf16[384,1024]{1,0:T(8,128)(2,1)S(1)}, bf16[768,768]{1,0:T(8,128)(2,1)S(1)}, bf16[768,1024]{1,0:T(8,128)(2,1)S(1)}) custom-call(f32[2,128]{1,0:T(2,128)S(1)} %get-tuple-element.63.refs_0_, f32[72,128]{1,0:T(8,128)S(1)} %get-tuple-element.64.refs_1_, s32[12,128]{1,0:T(8,128)S(1)} %get-tuple-element.65.refs_2_, ...), custom_call_target="tpu_custom_call" | custom-call | bytes 7910400 | tf_op jit(solution)/shard_map/pallas_call | solution.py:43
  37.2 1.5 %collective-permute-start.15 = (bf16[384,1024]{1,0:T(8,128)(2,1)S(1)}, bf16[384,1024]{1,0:T(8,128)(2,1)S(1)}, u32[]{:S(2)}, u32[]{:S(2)}) collective-permute-start(bf16[384,1024]{1,0:T(8,128)(2,1)S(1)} %get-tuple-element.107), channel_id=1, source_target_pairs={{0,8},{4,20},{8,0},{12,28},{16,24},{20,4},{24,16},{28,12},{1,9},{5... | collective-permute-start | bytes 2359304 | tf_op jit(solution)/shard_map/ppermute | solution.py:389
  38.7 2.6 %shard_map.96 = (f32[384,1024]{1,0:T(8,128)S(1)}, bf16[128,1024]{1,0:T(8,128)(2,1)S(1)}, bf16[128,1024]{1,0:T(8,128)(2,1)S(1)}, bf16[128,1024]{1,0:T(8,128)(2,1)S(1)}) custom-call(bf16[768,768]{1,0:T(8,128)(2,1)S(1)} %get-tuple-element.90.near_weight_ref, bf16[768,1024]{1,0:T(8,128)(2,1)S(1)} %shard_map.91.refs_8_.refs_7_.near_image_ref, ...), custom_call_target="tpu_custom_call" | custom-call | bytes 7864320 | tf_op jit(solution)/shard_map/pallas_call | solution.py:43
  41.3 0.1 collective-permute-start.8
  41.3 0.5 collective-permute-start.9
  41.8 0.1 collective-permute-start.10
  41.9 0.9 %collective-permute-done.8.refs_5_ = bf16[128,1024]{1,0:T(8,128)(2,1)S(1)} collective-permute-done((bf16[128,1024]{1,0:T(8,128)(2,1)S(1)}, bf16[128,1024]{1,0:T(8,128)(2,1)S(1)}, u32[]{:S(2)}, u32[]{:S(2)}) %collective-permute-start.8) | collective-permute-done | bytes 262176 | tf_op jit(solution)/shard_map/ppermute | solution.py:384
  42.9 0.4 collective-permute-done.9.refs_6_
  43.2 0.4 collective-permute-done.10.refs_7_
  43.6 0.8 %shard_map.97 = (bf16[384,256]{1,0:T(8,128)(2,1)S(1)}, bf16[384,256]{1,0:T(8,128)(2,1)S(1)}, bf16[384,256]{1,0:T(8,128)(2,1)S(1)}, bf16[384,256]{1,0:T(8,128)(2,1)S(1)}) custom-call(bf16[384,256]{1,0:T(8,128)(2,1)S(1)} %get-tuple-element.69.refs_0_, bf16[384,256]{1,0:T(8,128)(2,1)S(1)} %collective-permute-done.2.refs_1_, ...), custom_call_target="tpu_custom_call" | custom-call | bytes 3932160 | tf_op jit(solution)/shard_map/pallas_call | solution.py:43
  44.4 1.8 %collective-permute-start.11 = (bf16[384,256]{1,0:T(8,128)(2,1)S(1)}, bf16[384,256]{1,0:T(8,128)(2,1)S(1)}, u32[]{:S(2)}, u32[]{:S(2)}) collective-permute-start(bf16[384,256]{1,0:T(8,128)(2,1)S(1)} %get-tuple-element.98), channel_id=1, source_target_pairs={{0,1},{1,0},{2,3},{3,2},{4,5},{5,4},{6,7},{7,6},{8,9},{9,8},{10,11... | collective-permute-start | bytes 589832 | tf_op jit(solution)/shard_map/ppermute | solution.py:384
  46.2 2.6 %collective-permute-start.12 = (bf16[384,256]{1,0:T(8,128)(2,1)S(1)}, bf16[384,256]{1,0:T(8,128)(2,1)S(1)}, u32[]{:S(2)}, u32[]{:S(2)}) collective-permute-start(bf16[384,256]{1,0:T(8,128)(2,1)S(1)} %get-tuple-element.99), channel_id=1, source_target_pairs={{0,2},{1,3},{2,0},{3,1},{4,6},{5,7},{6,4},{7,5},{8,10},{9,11},{10,... | collective-permute-start | bytes 589832 | tf_op jit(solution)/shard_map/ppermute | solution.py:384
  48.8 0.1 collective-permute-start.13
  48.9 0.8 %shard_map.99.refs_0_ = f32[384,1024]{1,0:T(8,128)S(1)} custom-call(bf16[768,768]{1,0:T(8,128)(2,1)S(1)} %get-tuple-element.101.weight_ref, bf16[768,1024]{1,0:T(8,128)(2,1)S(1)} %get-tuple-element.83.refs_6_.unit_ref, bf16[384,1024]{1,0:T(8,128)(2,1)S(1)} %collective-permute-done.14.add_ref), custom_call_target="tpu_custom_call" | custom-call | bytes 5111808 | tf_op jit(solution)/shard_map/pallas_call | solution.py:43
  49.7 2.2 %collective-permute-done.15.in_ref = bf16[384,1024]{1,0:T(8,128)(2,1)S(1)} collective-permute-done((bf16[384,1024]{1,0:T(8,128)(2,1)S(1)}, bf16[384,1024]{1,0:T(8,128)(2,1)S(1)}, u32[]{:S(2)}, u32[]{:S(2)}) %collective-permute-start.15) | collective-permute-done | bytes 786464 | tf_op jit(solution)/shard_map/ppermute | solution.py:389
  51.9 0.1 shard_map.100
  52.0 0.0 copy-start.1
  52.0 2.6 %collective-permute-start.16 = (bf16[384,1024]{1,0:T(8,128)(2,1)S(1)}, bf16[384,1024]{1,0:T(8,128)(2,1)S(1)}, u32[]{:S(2)}, u32[]{:S(2)}) collective-permute-start(bf16[384,1024]{1,0:T(8,128)(2,1)S(1)} %shard_map.100), channel_id=1, source_target_pairs={{0,16},{4,12},{8,24},{12,4},{16,0},{20,28},{24,8},{28,20},{1,17},{... | collective-permute-start | bytes 2359304 | tf_op jit(solution)/shard_map/ppermute | solution.py:389
  54.6 0.4 collective-permute-done.11.refs_1_
  55.1 8.3 %collective-permute-done.12.refs_2_ = bf16[384,256]{1,0:T(8,128)(2,1)S(1)} collective-permute-done((bf16[384,256]{1,0:T(8,128)(2,1)S(1)}, bf16[384,256]{1,0:T(8,128)(2,1)S(1)}, u32[]{:S(2)}, u32[]{:S(2)}) %collective-permute-start.12) | collective-permute-done | bytes 196640 | tf_op jit(solution)/shard_map/ppermute | solution.py:384
  63.3 0.9 %shard_map.98 = bf16[1536,256]{1,0:T(8,128)(2,1)} custom-call(bf16[384,256]{1,0:T(8,128)(2,1)S(1)} %get-tuple-element.97.refs_0_, bf16[384,256]{1,0:T(8,128)(2,1)S(1)} %collective-permute-done.11.refs_1_, bf16[384,256]{1,0:T(8,128)(2,1)S(1)} %collective-permute-done.12.refs_2_, bf16[384,256]{1,0:T(8,128)(2,1)S(1)} %collective-permute-done.13.refs_3_), custom_call_target="tpu_custom_call" | custom-call | flops 20000000000 | bytes 1572864 | tf_op jit(solution)/shard_map/pallas_call | solution.py:43
  64.2 0.4 collective-permute-done.16.refs_1_
  64.6 1.4 %shard_map.101 = bf16[384,1024]{1,0:T(8,128)(2,1)} custom-call(bf16[384,1024]{1,0:T(8,128)(2,1)S(1)} %copy-done.1, f32[384,1024]{1,0:T(8,128)S(1)} %shard_map.99.refs_0_, bf16[384,1024]{1,0:T(8,128)(2,1)S(1)} %collective-permute-done.16.refs_1_), custom_call_target="tpu_custom_call" | custom-call | bytes 3932160 | tf_op jit(solution)/shard_map/pallas_call | solution.py:43
  (14 shorter events, 0.0 us)
Async XLA Ops:
  0.6 1.1 %copy-start.2 = (bf16[1536,256]{1,0:T(8,128)(2,1)S(1)}, bf16[1536,256]{1,0:T(8,128)(2,1)}, u32[]{:S(2)}) copy-start(bf16[1536,256]{1,0:T(8,128)(2,1)} %text_ref.1) | copy-start | bytes 2359300
  1.8 11.7 %copy-start.3 = (s32[12288]{0:T(1024)S(1)}, s32[12288]{0:T(1024)}, u32[]{:S(2)}) copy-start(s32[12288]{0:T(1024)} %param.11) | copy-start | bytes 147460
  1.8 11.7 %copy-start.4 = (s32[12288]{0:T(1024)S(1)}, s32[12288]{0:T(1024)}, u32[]{:S(2)}) copy-start(s32[12288]{0:T(1024)} %param.12) | copy-start | bytes 147460
  1.8 11.7 %copy-start.5 = (s32[96,8,3]{0,1,2:T(8,128)S(1)}, s32[96,8,3]{0,1,2:T(8,128)}, u32[]{:S(2)}) copy-start(s32[96,8,3]{0,1,2:T(8,128)} %param.13) | copy-start | bytes 27652
  1.8 21.2 %collective-permute-start = (bf16[384,1024]{1,0:T(8,128)(2,1)}, bf16[384,1024]{1,0:T(8,128)(2,1)S(1)}, u32[]{:S(2)}, u32[]{:S(2)}) collective-permute-start(bf16[384,1024]{1,0:T(8,128)(2,1)} %raw_ref.3), channel_id=1, source_target_pairs={{0,16},{4,12},{8,24},{12,4},{16,0},{20,28},{24,8},{28,20},{1,17},{... | collective-permute-start | bytes 2359304 | tf_op jit(solution)/shard_map/ppermute | solution.py:389
  4.9 22.2 %collective-permute-start.1 = (bf16[384,1024]{1,0:T(8,128)(2,1)}, bf16[384,1024]{1,0:T(8,128)(2,1)S(1)}, u32[]{:S(2)}, u32[]{:S(2)}) collective-permute-start(bf16[384,1024]{1,0:T(8,128)(2,1)} %raw_ref.3), channel_id=1, source_target_pairs={{0,8},{4,20},{8,0},{12,28},{16,24},{20,4},{24,16},{28,12},{1,9},{5... | collective-permute-start | bytes 2359304 | tf_op jit(solution)/shard_map/ppermute | solution.py:389
  6.3 18.3 %collective-permute-start.4 = (bf16[384,256]{1,0:T(8,128)(2,1)S(1)}, bf16[384,256]{1,0:T(8,128)(2,1)S(1)}, u32[]{:S(2)}, u32[]{:S(2)}) collective-permute-start(bf16[384,256]{1,0:T(8,128)(2,1)S(1)} %get-tuple-element.72), channel_id=1, source_target_pairs={{0,3},{1,2},{2,1},{3,0},{4,7},{5,6},{6,5},{7,4},{8,11},{9,10},{10,... | collective-permute-start | bytes 589832 | tf_op jit(solution)/shard_map/ppermute | solution.py:384
  10.0 14.7 %collective-permute-start.2 = (bf16[384,256]{1,0:T(8,128)(2,1)S(1)}, bf16[384,256]{1,0:T(8,128)(2,1)S(1)}, u32[]{:S(2)}, u32[]{:S(2)}) collective-permute-start(bf16[384,256]{1,0:T(8,128)(2,1)S(1)} %get-tuple-element.70), channel_id=1, source_target_pairs={{0,1},{1,0},{2,3},{3,2},{4,5},{5,4},{6,7},{7,6},{8,9},{9,8},{10,11... | collective-permute-start | bytes 589832 | tf_op jit(solution)/shard_map/ppermute | solution.py:384
  10.0 16.1 %collective-permute-start.3 = (bf16[384,256]{1,0:T(8,128)(2,1)S(1)}, bf16[384,256]{1,0:T(8,128)(2,1)S(1)}, u32[]{:S(2)}, u32[]{:S(2)}) collective-permute-start(bf16[384,256]{1,0:T(8,128)(2,1)S(1)} %get-tuple-element.71), channel_id=1, source_target_pairs={{0,2},{1,3},{2,0},{3,1},{4,6},{5,7},{6,4},{7,5},{8,10},{9,11},{10,... | collective-permute-start | bytes 589832 | tf_op jit(solution)/shard_map/ppermute | solution.py:384
  10.7 1.1 %copy-start = (bf16[384,1024]{1,0:T(8,128)(2,1)S(1)}, bf16[384,1024]{1,0:T(8,128)(2,1)}, u32[]{:S(2)}) copy-start(bf16[384,1024]{1,0:T(8,128)(2,1)} %raw_ref.3) | copy-start | bytes 2359300
  23.0 12.0 %collective-permute-start.7 = (bf16[384,1024]{1,0:T(8,128)(2,1)S(1)}, bf16[384,1024]{1,0:T(8,128)(2,1)S(1)}, u32[]{:S(2)}, u32[]{:S(2)}) collective-permute-start(bf16[384,1024]{1,0:T(8,128)(2,1)S(1)} %collective-permute-done.raw_ref), channel_id=1, source_target_pairs={{0,8},{4,20},{8,0},{12,28},{16,24},{20,4},{24,16},{28,12},{1,9},{5... | collective-permute-start | bytes 2359304 | tf_op jit(solution)/shard_map/ppermute | solution.py:389
  26.5 2.7 %collective-permute-start.5 = (bf16[192,1024]{1,0:T(8,128)(2,1)S(1)}, bf16[192,1024]{1,0:T(8,128)(2,1)S(1)}, u32[]{:S(2)}, u32[]{:S(2)}) collective-permute-start(bf16[192,1024]{1,0:T(8,128)(2,1)S(1)} %get-tuple-element.81), channel_id=1, source_target_pairs={{0,4},{4,0},{8,12},{12,8},{16,20},{20,16},{24,28},{28,24},{1,5},{5... | collective-permute-start | bytes 1179656 | tf_op jit(solution)/shard_map/ppermute | solution.py:384
  26.6 2.6 %collective-permute-start.6 = (bf16[192,1024]{1,0:T(8,128)(2,1)S(1)}, bf16[192,1024]{1,0:T(8,128)(2,1)S(1)}, u32[]{:S(2)}, u32[]{:S(2)}) collective-permute-start(bf16[192,1024]{1,0:T(8,128)(2,1)S(1)} %get-tuple-element.82), channel_id=1, source_target_pairs={{0,4},{4,0},{8,12},{12,8},{16,20},{20,16},{24,28},{28,24},{1,5},{5... | collective-permute-start | bytes 1179656 | tf_op jit(solution)/shard_map/ppermute | solution.py:384
  30.6 18.3 %collective-permute-start.14 = (bf16[384,1024]{1,0:T(8,128)(2,1)S(1)}, bf16[384,1024]{1,0:T(8,128)(2,1)S(1)}, u32[]{:S(2)}, u32[]{:S(2)}) collective-permute-start(bf16[384,1024]{1,0:T(8,128)(2,1)S(1)} %get-tuple-element.102), channel_id=1, source_target_pairs={{0,8},{4,20},{8,0},{12,28},{16,24},{20,4},{24,16},{28,12},{1,9},{5... | collective-permute-start | bytes 2359304 | tf_op jit(solution)/shard_map/ppermute | solution.py:389
  37.2 14.7 %collective-permute-start.15 = (bf16[384,1024]{1,0:T(8,128)(2,1)S(1)}, bf16[384,1024]{1,0:T(8,128)(2,1)S(1)}, u32[]{:S(2)}, u32[]{:S(2)}) collective-permute-start(bf16[384,1024]{1,0:T(8,128)(2,1)S(1)} %get-tuple-element.107), channel_id=1, source_target_pairs={{0,8},{4,20},{8,0},{12,28},{16,24},{20,4},{24,16},{28,12},{1,9},{5... | collective-permute-start | bytes 2359304 | tf_op jit(solution)/shard_map/ppermute | solution.py:389
  41.3 1.6 %collective-permute-start.8 = (bf16[128,1024]{1,0:T(8,128)(2,1)S(1)}, bf16[128,1024]{1,0:T(8,128)(2,1)S(1)}, u32[]{:S(2)}, u32[]{:S(2)}) collective-permute-start(bf16[128,1024]{1,0:T(8,128)(2,1)S(1)} %get-tuple-element.93), channel_id=1, source_target_pairs={{0,4},{4,0},{8,12},{12,8},{16,20},{20,16},{24,28},{28,24},{1,5},{5... | collective-permute-start | bytes 786440 | tf_op jit(solution)/shard_map/ppermute | solution.py:384
  41.3 1.9 %collective-permute-start.9 = (bf16[128,1024]{1,0:T(8,128)(2,1)S(1)}, bf16[128,1024]{1,0:T(8,128)(2,1)S(1)}, u32[]{:S(2)}, u32[]{:S(2)}) collective-permute-start(bf16[128,1024]{1,0:T(8,128)(2,1)S(1)} %get-tuple-element.94), channel_id=1, source_target_pairs={{0,4},{4,0},{8,12},{12,8},{16,20},{20,16},{24,28},{28,24},{1,5},{5... | collective-permute-start | bytes 786440 | tf_op jit(solution)/shard_map/ppermute | solution.py:384
  41.8 1.8 %collective-permute-start.10 = (bf16[128,1024]{1,0:T(8,128)(2,1)S(1)}, bf16[128,1024]{1,0:T(8,128)(2,1)S(1)}, u32[]{:S(2)}, u32[]{:S(2)}) collective-permute-start(bf16[128,1024]{1,0:T(8,128)(2,1)S(1)} %get-tuple-element.95), channel_id=1, source_target_pairs={{0,4},{4,0},{8,12},{12,8},{16,20},{20,16},{24,28},{28,24},{1,5},{5... | collective-permute-start | bytes 786440 | tf_op jit(solution)/shard_map/ppermute | solution.py:384
  44.4 10.6 %collective-permute-start.11 = (bf16[384,256]{1,0:T(8,128)(2,1)S(1)}, bf16[384,256]{1,0:T(8,128)(2,1)S(1)}, u32[]{:S(2)}, u32[]{:S(2)}) collective-permute-start(bf16[384,256]{1,0:T(8,128)(2,1)S(1)} %get-tuple-element.98), channel_id=1, source_target_pairs={{0,1},{1,0},{2,3},{3,2},{4,5},{5,4},{6,7},{7,6},{8,9},{9,8},{10,11... | collective-permute-start | bytes 589832 | tf_op jit(solution)/shard_map/ppermute | solution.py:384
  46.2 17.1 %collective-permute-start.12 = (bf16[384,256]{1,0:T(8,128)(2,1)S(1)}, bf16[384,256]{1,0:T(8,128)(2,1)S(1)}, u32[]{:S(2)}, u32[]{:S(2)}) collective-permute-start(bf16[384,256]{1,0:T(8,128)(2,1)S(1)} %get-tuple-element.99), channel_id=1, source_target_pairs={{0,2},{1,3},{2,0},{3,1},{4,6},{5,7},{6,4},{7,5},{8,10},{9,11},{10,... | collective-permute-start | bytes 589832 | tf_op jit(solution)/shard_map/ppermute | solution.py:384
  48.8 14.5 %collective-permute-start.13 = (bf16[384,256]{1,0:T(8,128)(2,1)S(1)}, bf16[384,256]{1,0:T(8,128)(2,1)S(1)}, u32[]{:S(2)}, u32[]{:S(2)}) collective-permute-start(bf16[384,256]{1,0:T(8,128)(2,1)S(1)} %get-tuple-element.100), channel_id=1, source_target_pairs={{0,3},{1,2},{2,1},{3,0},{4,7},{5,6},{6,5},{7,4},{8,11},{9,10},{10,... | collective-permute-start | bytes 589832 | tf_op jit(solution)/shard_map/ppermute | solution.py:384
  52.0 12.6 %copy-start.1 = (bf16[384,1024]{1,0:T(8,128)(2,1)S(1)}, bf16[384,1024]{1,0:T(8,128)(2,1)}, u32[]{:S(2)}) copy-start(bf16[384,1024]{1,0:T(8,128)(2,1)} %raw_ref.3) | copy-start | bytes 2359300
  52.0 12.6 %collective-permute-start.16 = (bf16[384,1024]{1,0:T(8,128)(2,1)S(1)}, bf16[384,1024]{1,0:T(8,128)(2,1)S(1)}, u32[]{:S(2)}, u32[]{:S(2)}) collective-permute-start(bf16[384,1024]{1,0:T(8,128)(2,1)S(1)} %shard_map.100), channel_id=1, source_target_pairs={{0,16},{4,12},{8,24},{12,4},{16,0},{20,28},{24,8},{28,20},{1,17},{... | collective-permute-start | bytes 2359304 | tf_op jit(solution)/shard_map/ppermute | solution.py:389

commit v3 on v2

--- a/solution.py
+++ b/solution.py
@@ -125,6 +125,11 @@
     unit_images([raw_ref], out_ref)
 
 
+def own_images_body(raw_ref, out_ref, raw_out_ref):
+    unit_images([raw_ref], out_ref)
+    raw_out_ref[...] = raw_ref[...]
+
+
 def near_images_body(first_ref, second_unit_ref, out_ref):
     rows = first_ref.shape[0]
     unit_images([first_ref], out_ref)
@@ -241,7 +246,7 @@
     unit_ref, own_image_ref, near_image_ref, own_weight_in_ref, weight_in_ref, first_ref = refs[
         Pairs.count : Pairs.count + 6
     ]
-    own_weight_ref, weight_ref, sum_ref = refs[Pairs.count + 6 :]
+    own_weight_ref, acc_ref, sum_ref, weight_ref = refs[Pairs.count + 6 :]
     rows = own_image_ref.shape[0]
     second = dot_nt(unit_ref[rows:, :], near_image_ref[pl.ds(rows, rows), :])
     own = dot_nt(unit_ref[rows:, :], own_image_ref[...])
@@ -251,6 +256,9 @@
     pairs.weigh(second, 1, 2, weight_ref, rows, rows)
     sum_ref[...] = dot_tn(weight_ref[:, rows:], unit_ref[...])
     pairs.weigh(own, 1, 0, own_weight_ref, rows, 0)
+    acc_ref[...] = jnp.dot(
+        weight_ref[...], near_image_ref[...], preferred_element_type=jnp.float32
+    )
 
 
 def far_sum_body(tiles, *refs):
@@ -268,18 +276,15 @@
     weight_ref[:, :rows] = own_weight_ref[...]
 
 
-def text_sum_body(near_weight_ref, near_image_ref, weight_ref, image_ref, acc_ref, *piece_refs):
-    rows = acc_ref.shape[0]
-    size = rows // ACC_PIECES
-    for part in (slice(rows, 2 * rows), slice(0, rows)):
-        acc = jnp.dot(
-            near_weight_ref[part, :], near_image_ref[...], preferred_element_type=jnp.float32
-        ) + jnp.dot(weight_ref[part, :], image_ref[...], preferred_element_type=jnp.float32)
-        if part.start == 0:
-            acc_ref[...] = acc
-            continue
-        for at, ref in enumerate(piece_refs):
-            ref[...] = acc[at * size : (at + 1) * size, :].astype(jnp.bfloat16)
+def text_sum_body(half, weight_ref, image_ref, acc_ref, *out_refs):
+    rows = weight_ref.shape[0] // CORES
+    size = out_refs[0].shape[0]
+    part = pl.ds(half * rows, rows)
+    acc = acc_ref[part, :] + jnp.dot(
+        weight_ref[part, :], image_ref[...], preferred_element_type=jnp.float32
+    )
+    for at, ref in enumerate(out_refs):
+        ref[...] = acc[at * size : (at + 1) * size, :].astype(ref.dtype)
 
 
 def own_sum_body(weight_ref, unit_ref, add_ref, out_ref):
@@ -412,7 +417,6 @@
     text_raw = [picked[0]] + [swap(picked[k], "tp", k) for k in range(1, groups)]
     if square:
         from_second = swap_near(image_sent, 1)
-        from_first = swap_near(image_sent, 0)
     else:
         same_core = [[chip * CORES + core for chip in range(chips)] for core in range(CORES)]
         gathered = lax.all_gather(
@@ -439,7 +443,11 @@
         limit=8,
     )
     if square:
-        own_images = call_kernel(unit_images_body, [bf16(rows)], [image_emb], limit=8)[0]
+        own_images, image_emb = call_kernel(
+            own_images_body, [bf16(rows)] * 2, [image_emb], limit=8
+        )
+        image_sent, own_images = lax.optimization_barrier((image_sent, own_images))
+        from_first = swap_near(image_sent, 0)
         from_second, own_images, *lists = lax.optimization_barrier(
             (from_second, own_images, *lists)
         )
@@ -525,11 +533,12 @@
         limit=16,
     )
     image_add = swap_near(first_sum, 0)
-    own_weights, near_weights, second_sum = call_kernel(
+    own_weights, acc, second_sum = call_kernel(
         functools.partial(second_sum_body, tiles),
-        [bf16(2 * rows, rows), bf16(2 * rows, 2 * rows), f32(rows)],
+        [bf16(2 * rows, rows), f32(2 * rows), f32(rows)],
         lists + [units, own_images, near_images, own_weights, near_weights, first_weights],
-        limit=16,
+        scratch=[pltpu.VMEM((2 * rows, 2 * rows), jnp.bfloat16)],
+        limit=24,
     )
     own_weights, from_far = lax.optimization_barrier((own_weights, from_far))
     far_sum, far_weights, far_images = call_kernel(
@@ -538,12 +547,19 @@
         lists + [units, own_images, own_weights, from_far],
         limit=16,
     )
-    acc_own, *acc_other = call_kernel(
-        text_sum_body,
-        [f32(rows)] + [bf16(rows // ACC_PIECES)] * ACC_PIECES,
-        [near_weights, near_images, far_weights, far_images],
-        limit=24,
-    )
+    acc_other = call_kernel(
+        functools.partial(text_sum_body, 1),
+        [bf16(rows // ACC_PIECES)] * ACC_PIECES,
+        [far_weights, far_images, acc],
+        limit=16,
+    )
+    far_images, acc_other[0] = lax.optimization_barrier((far_images, acc_other[0]))
+    acc_own = call_kernel(
+        functools.partial(text_sum_body, 0),
+        [f32(rows)],
+        [far_weights, far_images, acc],
+        limit=16,
+    )[0]
     text_parts = finish_text(acc_own, acc_other)
     far_weights, text_parts[0] = lax.optimization_barrier((far_weights, text_parts[0]))
     base = call_kernel(

time: 66.5 us -> 63.6 us (0.956)
  waiting for transfers between devices: 24.8 us -> 20.9 us
  Pallas kernels: 16.1 us -> 17.5 us
  local copies, waits for them, and re-layouts: 2.28 us -> 1.14 us
  starting transfers between devices: 20.6 us -> 21.7 us
    ppermute x6, waiting for transfers between devices: 13 us -> 9.76 us  [swap_near(): lax.ppermute(value, 'blk', [(i, i ^ neighbour_bits(i)[which]) for i in ra...]
    pallas_call x16 -> x17, Pallas kernels: 16.1 us -> 17.5 us  [call_kernel(): pl.pallas_call(body, out_shape=outs, in_specs=specs, out_specs=[ANY_SPEC...]
    unnamed x12 -> x8, local copies, waits for them, and re-layouts: 2.28 us -> 1.14 us
    ppermute x6, starting transfers between devices: 10.6 us -> 11.6 us  [swap_near(): lax.ppermute(value, 'blk', [(i, i ^ neighbour_bits(i)[which]) for i in ra...]
  transfers between devices with their start and end apart: 17 -> 17, of which waited for: 10 -> 8; matrix products, arithmetic and copies ran while one was open for 0% -> 0% of each run, Pallas kernels for 22% -> 25%
where the time goes in v3:
time: 63.6 us; the launch traced here: 63.4 us
  starting transfers between devices  21.7 us (34%)
  waiting for transfers between devices  20.9 us (33%)
  Pallas kernels  17.5 us (28%)
  between operations  2.13 us (3%)
  local copies, waits for them, and re-layouts  1.14 us (2%)
    pallas_call x17, Pallas kernels, call_kernel(): pl.pallas_call(body, out_shape=outs, in_specs=specs, out_specs=[ANY_SPEC...  17.5 us
    ppermute x6, starting transfers between devices, swap_near(): lax.ppermute(value, 'blk', [(i, i ^ neighbour_bits(i)[which]) for i in ra...  11.6 us
    ppermute x11, waiting for transfers between devices, swap(): return lax.ppermute(value, axis, [(i, i ^ bits) for i in range(count)])  11.2 us
    ppermute x11, starting transfers between devices, swap(): return lax.ppermute(value, axis, [(i, i ^ bits) for i in range(count)])  10.1 us
    ppermute x6, waiting for transfers between devices, swap_near(): lax.ppermute(value, 'blk', [(i, i ^ neighbour_bits(i)[which]) for i in ra...  9.76 us
  transfers between devices with their start and end apart: 17, of which 8 were waited for; matrix products, arithmetic and copies ran while one was open for 0% of the time, Pallas kernels for 25%

profile of v3, /device:TPU:0, one launch (start us, length us, event | category | flops | bytes accessed | tf_op | source)
XLA Modules:
  0.0 63.4 jit_solution(13837254985850179472)
XLA Ops:
  0.6 1.1 %copy-done = bf16[1536,256]{1,0:T(8,128)(2,1)S(1)} copy-done((bf16[1536,256]{1,0:T(8,128)(2,1)S(1)}, bf16[1536,256]{1,0:T(8,128)(2,1)}, u32[]{:S(2)}) %copy-start) | copy-done | bytes 786456
  1.8 0.1 shard_map.86
  1.8 3.0 %collective-permute-start = (bf16[384,1024]{1,0:T(8,128)(2,1)}, bf16[384,1024]{1,0:T(8,128)(2,1)S(1)}, u32[]{:S(2)}, u32[]{:S(2)}) collective-permute-start(bf16[384,1024]{1,0:T(8,128)(2,1)} %raw_ref.1), channel_id=1, source_target_pairs={{0,16},{4,12},{8,24},{12,4},{16,0},{20,28},{24,8},{28,20},{1,17},{... | collective-permute-start | bytes 2359304 | tf_op jit(solution)/shard_map/ppermute | solution.py:394
  4.9 3.6 %collective-permute-start.4 = (bf16[384,256]{1,0:T(8,128)(2,1)S(1)}, bf16[384,256]{1,0:T(8,128)(2,1)S(1)}, u32[]{:S(2)}, u32[]{:S(2)}) collective-permute-start(bf16[384,256]{1,0:T(8,128)(2,1)S(1)} %get-tuple-element.80), channel_id=1, source_target_pairs={{0,3},{1,2},{2,1},{3,0},{4,7},{5,6},{6,5},{7,4},{8,11},{9,10},{10,... | collective-permute-start | bytes 589832 | tf_op jit(solution)/shard_map/ppermute | solution.py:389
  8.5 0.0 collective-permute-start.2
  8.5 0.8 %collective-permute-start.3 = (bf16[384,256]{1,0:T(8,128)(2,1)S(1)}, bf16[384,256]{1,0:T(8,128)(2,1)S(1)}, u32[]{:S(2)}, u32[]{:S(2)}) collective-permute-start(bf16[384,256]{1,0:T(8,128)(2,1)S(1)} %get-tuple-element.79), channel_id=1, source_target_pairs={{0,2},{1,3},{2,0},{3,1},{4,6},{5,7},{6,4},{7,5},{8,10},{9,11},{10,... | collective-permute-start | bytes 589832 | tf_op jit(solution)/shard_map/ppermute | solution.py:389
  9.2 1.4 %shard_map.87 = (bf16[384,1024]{1,0:T(8,128)(2,1)S(1)}, bf16[384,1024]{1,0:T(8,128)(2,1)S(1)}) custom-call(bf16[384,1024]{1,0:T(8,128)(2,1)} %raw_ref.1), custom_call_target="tpu_custom_call" | custom-call | bytes 2359296 | tf_op jit(solution)/shard_map/pallas_call | solution.py:43
  10.7 1.6 %collective-permute-start.1 = (bf16[384,1024]{1,0:T(8,128)(2,1)}, bf16[384,1024]{1,0:T(8,128)(2,1)S(1)}, u32[]{:S(2)}, u32[]{:S(2)}) collective-permute-start(bf16[384,1024]{1,0:T(8,128)(2,1)} %raw_ref.1), channel_id=1, source_target_pairs={{0,8},{4,20},{8,0},{12,28},{16,24},{20,4},{24,16},{28,12},{1,9},{5... | collective-permute-start | bytes 2359304 | tf_op jit(solution)/shard_map/ppermute | solution.py:394
  13.5 1.1 %shard_map.88 = (f32[2,128]{1,0:T(2,128)S(1)}, f32[72,128]{1,0:T(8,128)S(1)}, s32[12,128]{1,0:T(8,128)S(1)}, s32[768,128]{1,0:T(8,128)S(1)}, f32[384,128]{1,0:T(8,128)S(1)}, /*index=5*/f32[4,128]{1,0:T(4,128)S(1)}) custom-call(f32[1]{0:T(128)S(6)} %copy.9.refs_0_, f32[1]{0:T(128)S(6)} %copy.10.refs_1_, s32[3,8,96]{2,1,0:T(8,128)S(1)} %bitcast.5, ...), custom_call_target="tpu_custom_call" | custom-call | bytes 743432 | tf_op jit(solution)/shard_map/pallas_call | solution.py:43
  14.6 3.2 %collective-permute-done.raw_ref = bf16[384,1024]{1,0:T(8,128)(2,1)S(1)} collective-permute-done((bf16[384,1024]{1,0:T(8,128)(2,1)}, bf16[384,1024]{1,0:T(8,128)(2,1)S(1)}, u32[]{:S(2)}, u32[]{:S(2)}) %collective-permute-start) | collective-permute-done | bytes 786464 | tf_op jit(solution)/shard_map/ppermute | solution.py:394
  17.9 3.3 %collective-permute-start.7 = (bf16[384,1024]{1,0:T(8,128)(2,1)S(1)}, bf16[384,1024]{1,0:T(8,128)(2,1)S(1)}, u32[]{:S(2)}, u32[]{:S(2)}) collective-permute-start(bf16[384,1024]{1,0:T(8,128)(2,1)S(1)} %collective-permute-done.raw_ref), channel_id=1, source_target_pairs={{0,8},{4,20},{8,0},{12,28},{16,24},{20,4},{24,16},{28,12},{1,9},{5... | collective-permute-start | bytes 2359304 | tf_op jit(solution)/shard_map/ppermute | solution.py:394
  21.2 0.2 shard_map.89.second_unit_ref
  21.4 0.0 collective-permute-done.2.refs_1_
  21.4 3.4 %collective-permute-done.3.refs_2_ = bf16[384,256]{1,0:T(8,128)(2,1)S(1)} collective-permute-done((bf16[384,256]{1,0:T(8,128)(2,1)S(1)}, bf16[384,256]{1,0:T(8,128)(2,1)S(1)}, u32[]{:S(2)}, u32[]{:S(2)}) %collective-permute-start.3) | collective-permute-done | bytes 196640 | tf_op jit(solution)/shard_map/ppermute | solution.py:389
  24.8 0.4 shard_map.90
  25.2 0.1 collective-permute-start.5
  25.3 0.5 collective-permute-start.6
  25.8 0.0 collective-permute-done.1.first_ref
  25.8 0.3 shard_map.91.refs_8_.refs_7_
  26.1 1.8 %shard_map.92 = (bf16[384,384]{1,0:T(8,128)(2,1)S(1)}, bf16[384,768]{1,0:T(8,128)(2,1)S(1)}) custom-call(f32[2,128]{1,0:T(2,128)S(1)} %get-tuple-element.70.refs_0_, f32[72,128]{1,0:T(8,128)S(1)} %get-tuple-element.71.refs_1_, s32[12,128]{1,0:T(8,128)S(1)} %get-tuple-element.72.refs_2_, s32[768,128]{1,0:T(8,128)S(1)} %get-tuple-element.73.refs_3_, ...), custom_call_target="tpu_custom_call" | custom-call | bytes 4666368 | tf_op jit(solution)/shard_map/pallas_call | solution.py:43
  27.9 0.0 collective-permute-done.5.refs_9_
  27.9 1.4 %shard_map.93 = (bf16[768,1024]{1,0:T(8,128)(2,1)S(1)}, bf16[768,384]{1,0:T(8,128)(2,1)S(1)}, bf16[384,1024]{1,0:T(8,128)(2,1)S(1)}) custom-call(f32[2,128]{1,0:T(2,128)S(1)} %get-tuple-element.70.refs_0_, f32[72,128]{1,0:T(8,128)S(1)} %get-tuple-element.71.refs_1_, s32[12,128]{1,0:T(8,128)S(1)} %get-tuple-element.72.refs_2_, ...), custom_call_target="tpu_custom_call" | custom-call | bytes 7320576 | tf_op jit(solution)/shard_map/pallas_call | solution.py:43
  29.3 0.6 collective-permute-start.14
  29.9 3.1 %shard_map.94 = (bf16[768,384]{1,0:T(8,128)(2,1)S(1)}, f32[768,1024]{1,0:T(8,128)S(1)}, f32[384,1024]{1,0:T(8,128)S(1)}) custom-call(f32[2,128]{1,0:T(2,128)S(1)} %get-tuple-element.70.refs_0_, f32[72,128]{1,0:T(8,128)S(1)} %get-tuple-element.71.refs_1_, s32[12,128]{1,0:T(8,128)S(1)} %get-tuple-element.72.refs_2_, s32[768,128]{1,0:T(8,128)S(1)} %get-tuple-element.73.refs_3_, ...), custom_call_target="tpu_custom_call" | custom-call | bytes 11351040 | tf_op jit(solution)/shard_map/pallas_call | solution.py:43
  33.0 0.0 collective-permute-done.7.refs_9_
  33.0 2.2 %shard_map.95 = (bf16[384,1024]{1,0:T(8,128)(2,1)S(1)}, bf16[768,768]{1,0:T(8,128)(2,1)S(1)}, bf16[768,1024]{1,0:T(8,128)(2,1)S(1)}) custom-call(f32[2,128]{1,0:T(2,128)S(1)} %get-tuple-element.70.refs_0_, f32[72,128]{1,0:T(8,128)S(1)} %get-tuple-element.71.refs_1_, s32[12,128]{1,0:T(8,128)S(1)} %get-tuple-element.72.refs_2_, ...), custom_call_target="tpu_custom_call" | custom-call | bytes 7910400 | tf_op jit(solution)/shard_map/pallas_call | solution.py:43
  35.2 1.6 %collective-permute-start.15 = (bf16[384,1024]{1,0:T(8,128)(2,1)S(1)}, bf16[384,1024]{1,0:T(8,128)(2,1)S(1)}, u32[]{:S(2)}, u32[]{:S(2)}) collective-permute-start(bf16[384,1024]{1,0:T(8,128)(2,1)S(1)} %get-tuple-element.117), channel_id=1, source_target_pairs={{0,8},{4,20},{8,0},{12,28},{16,24},{20,4},{24,16},{28,12},{1,9},{5... | collective-permute-start | bytes 2359304 | tf_op jit(solution)/shard_map/ppermute | solution.py:394
  36.8 0.8 %shard_map.96 = (bf16[128,1024]{1,0:T(8,128)(2,1)S(1)}, bf16[128,1024]{1,0:T(8,128)(2,1)S(1)}, bf16[128,1024]{1,0:T(8,128)(2,1)S(1)}) custom-call(bf16[768,768]{1,0:T(8,128)(2,1)S(1)} %get-tuple-element.111.weight_ref, bf16[768,1024]{1,0:T(8,128)(2,1)S(1)} %get-tuple-element.101.image_ref, f32[768,1024]{1,0:T(8,128)S(1)} %get-tuple-element.99.acc_ref), custom_call_target="tpu_custom_call" | custom-call | bytes 6684672 | tf_op jit(solution)/shard_map/pallas_call | solution.py:43
  37.6 0.1 collective-permute-start.8
  37.6 0.5 collective-permute-start.9
  38.1 0.1 collective-permute-start.10
  38.2 0.8 %shard_map.97.refs_4_ = f32[384,1024]{1,0:T(8,128)S(1)} custom-call(bf16[768,768]{1,0:T(8,128)(2,1)S(1)} %get-tuple-element.111.weight_ref, bf16[768,1024]{1,0:T(8,128)(2,1)S(1)} %get-tuple-element.101.image_ref, f32[768,1024]{1,0:T(8,128)S(1)} %get-tuple-element.99.acc_ref), custom_call_target="tpu_custom_call" | custom-call | bytes 7471104 | tf_op jit(solution)/shard_map/pallas_call | solution.py:43
  39.0 0.2 collective-permute-done.8.refs_5_
  39.2 0.4 collective-permute-done.9.refs_6_
  39.5 0.4 collective-permute-done.10.refs_7_
  39.9 0.8 %shard_map.98 = (bf16[384,256]{1,0:T(8,128)(2,1)S(1)}, bf16[384,256]{1,0:T(8,128)(2,1)S(1)}, bf16[384,256]{1,0:T(8,128)(2,1)S(1)}, bf16[384,256]{1,0:T(8,128)(2,1)S(1)}) custom-call(bf16[384,256]{1,0:T(8,128)(2,1)S(1)} %get-tuple-element.77.refs_0_, bf16[384,256]{1,0:T(8,128)(2,1)S(1)} %collective-permute-done.2.refs_1_, ...), custom_call_target="tpu_custom_call" | custom-call | bytes 3932160 | tf_op jit(solution)/shard_map/pallas_call | solution.py:43
  40.7 0.5 collective-permute-start.11
  41.2 2.6 %collective-permute-start.12 = (bf16[384,256]{1,0:T(8,128)(2,1)S(1)}, bf16[384,256]{1,0:T(8,128)(2,1)S(1)}, u32[]{:S(2)}, u32[]{:S(2)}) collective-permute-start(bf16[384,256]{1,0:T(8,128)(2,1)S(1)} %get-tuple-element.108), channel_id=1, source_target_pairs={{0,2},{1,3},{2,0},{3,1},{4,6},{5,7},{6,4},{7,5},{8,10},{9,11},{10,... | collective-permute-start | bytes 589832 | tf_op jit(solution)/shard_map/ppermute | solution.py:389
  43.8 1.3 %collective-permute-start.13 = (bf16[384,256]{1,0:T(8,128)(2,1)S(1)}, bf16[384,256]{1,0:T(8,128)(2,1)S(1)}, u32[]{:S(2)}, u32[]{:S(2)}) collective-permute-start(bf16[384,256]{1,0:T(8,128)(2,1)S(1)} %get-tuple-element.109), channel_id=1, source_target_pairs={{0,3},{1,2},{2,1},{3,0},{4,7},{5,6},{6,5},{7,4},{8,11},{9,10},{10,... | collective-permute-start | bytes 589832 | tf_op jit(solution)/shard_map/ppermute | solution.py:389
  45.2 0.0 collective-permute-done.14.add_ref
  45.2 0.8 %shard_map.100.refs_0_ = f32[384,1024]{1,0:T(8,128)S(1)} custom-call(bf16[768,768]{1,0:T(8,128)(2,1)S(1)} %get-tuple-element.111.weight_ref, bf16[768,1024]{1,0:T(8,128)(2,1)S(1)} %get-tuple-element.91.refs_6_.unit_ref, bf16[384,1024]{1,0:T(8,128)(2,1)S(1)} %collective-permute-done.14.add_ref), custom_call_target="tpu_custom_call" | custom-call | bytes 5111808 | tf_op jit(solution)/shard_map/pallas_call | solution.py:43
  46.0 3.8 %collective-permute-done.15.in_ref = bf16[384,1024]{1,0:T(8,128)(2,1)S(1)} collective-permute-done((bf16[384,1024]{1,0:T(8,128)(2,1)S(1)}, bf16[384,1024]{1,0:T(8,128)(2,1)S(1)}, u32[]{:S(2)}, u32[]{:S(2)}) %collective-permute-start.15) | collective-permute-done | bytes 786464 | tf_op jit(solution)/shard_map/ppermute | solution.py:394
  49.8 0.1 shard_map.101
  49.9 1.6 %collective-permute-start.16 = (bf16[384,1024]{1,0:T(8,128)(2,1)S(1)}, bf16[384,1024]{1,0:T(8,128)(2,1)S(1)}, u32[]{:S(2)}, u32[]{:S(2)}) collective-permute-start(bf16[384,1024]{1,0:T(8,128)(2,1)S(1)} %shard_map.101), channel_id=1, source_target_pairs={{0,16},{4,12},{8,24},{12,4},{16,0},{20,28},{24,8},{28,20},{1,17},{... | collective-permute-start | bytes 2359304 | tf_op jit(solution)/shard_map/ppermute | solution.py:394
  51.5 6.8 %collective-permute-done.12.refs_2_ = bf16[384,256]{1,0:T(8,128)(2,1)S(1)} collective-permute-done((bf16[384,256]{1,0:T(8,128)(2,1)S(1)}, bf16[384,256]{1,0:T(8,128)(2,1)S(1)}, u32[]{:S(2)}, u32[]{:S(2)}) %collective-permute-start.12) | collective-permute-done | bytes 196640 | tf_op jit(solution)/shard_map/ppermute | solution.py:389
  58.4 0.9 %shard_map.99 = bf16[1536,256]{1,0:T(8,128)(2,1)} custom-call(bf16[384,256]{1,0:T(8,128)(2,1)S(1)} %get-tuple-element.106.refs_0_, bf16[384,256]{1,0:T(8,128)(2,1)S(1)} %collective-permute-done.11.refs_1_, bf16[384,256]{1,0:T(8,128)(2,1)S(1)} %collective-permute-done.12.refs_2_, bf16[384,256]{1,0:T(8,128)(2,1)S(1)} %collective-permute-done.13.refs_3_), custom_call_target="tpu_custom_call" | custom-call | flops 20000000000 | bytes 1572864 | tf_op jit(solution)/shard_map/pallas_call | solution.py:43
  59.3 2.7 %collective-permute-done.16.refs_1_ = bf16[384,1024]{1,0:T(8,128)(2,1)S(1)} collective-permute-done((bf16[384,1024]{1,0:T(8,128)(2,1)S(1)}, bf16[384,1024]{1,0:T(8,128)(2,1)S(1)}, u32[]{:S(2)}, u32[]{:S(2)}) %collective-permute-start.16) | collective-permute-done | bytes 786464 | tf_op jit(solution)/shard_map/ppermute | solution.py:394
  62.0 1.4 %shard_map.102 = bf16[384,1024]{1,0:T(8,128)(2,1)} custom-call(bf16[384,1024]{1,0:T(8,128)(2,1)S(1)} %get-tuple-element.110.raw_ref, f32[384,1024]{1,0:T(8,128)S(1)} %shard_map.100.refs_0_, bf16[384,1024]{1,0:T(8,128)(2,1)S(1)} %collective-permute-done.16.refs_1_), custom_call_target="tpu_custom_call" | custom-call | bytes 3932160 | tf_op jit(solution)/shard_map/pallas_call | solution.py:43
  (11 shorter events, 0.0 us)
Async XLA Ops:
  0.6 1.1 %copy-start = (bf16[1536,256]{1,0:T(8,128)(2,1)S(1)}, bf16[1536,256]{1,0:T(8,128)(2,1)}, u32[]{:S(2)}) copy-start(bf16[1536,256]{1,0:T(8,128)(2,1)} %text_ref.1) | copy-start | bytes 2359300
  1.8 11.8 %copy-start.1 = (s32[12288]{0:T(1024)S(1)}, s32[12288]{0:T(1024)}, u32[]{:S(2)}) copy-start(s32[12288]{0:T(1024)} %param.11) | copy-start | bytes 147460
  1.8 11.8 %copy-start.2 = (s32[12288]{0:T(1024)S(1)}, s32[12288]{0:T(1024)}, u32[]{:S(2)}) copy-start(s32[12288]{0:T(1024)} %param.12) | copy-start | bytes 147460
  1.8 11.8 %copy-start.3 = (s32[96,8,3]{0,1,2:T(8,128)S(1)}, s32[96,8,3]{0,1,2:T(8,128)}, u32[]{:S(2)}) copy-start(s32[96,8,3]{0,1,2:T(8,128)} %param.13) | copy-start | bytes 27652
  1.8 16.0 %collective-permute-start = (bf16[384,1024]{1,0:T(8,128)(2,1)}, bf16[384,1024]{1,0:T(8,128)(2,1)S(1)}, u32[]{:S(2)}, u32[]{:S(2)}) collective-permute-start(bf16[384,1024]{1,0:T(8,128)(2,1)} %raw_ref.1), channel_id=1, source_target_pairs={{0,16},{4,12},{8,24},{12,4},{16,0},{20,28},{24,8},{28,20},{1,17},{... | collective-permute-start | bytes 2359304 | tf_op jit(solution)/shard_map/ppermute | solution.py:394
  4.9 16.6 %collective-permute-start.4 = (bf16[384,256]{1,0:T(8,128)(2,1)S(1)}, bf16[384,256]{1,0:T(8,128)(2,1)S(1)}, u32[]{:S(2)}, u32[]{:S(2)}) collective-permute-start(bf16[384,256]{1,0:T(8,128)(2,1)S(1)} %get-tuple-element.80), channel_id=1, source_target_pairs={{0,3},{1,2},{2,1},{3,0},{4,7},{5,6},{6,5},{7,4},{8,11},{9,10},{10,... | collective-permute-start | bytes 589832 | tf_op jit(solution)/shard_map/ppermute | solution.py:389
  8.5 13.0 %collective-permute-start.2 = (bf16[384,256]{1,0:T(8,128)(2,1)S(1)}, bf16[384,256]{1,0:T(8,128)(2,1)S(1)}, u32[]{:S(2)}, u32[]{:S(2)}) collective-permute-start(bf16[384,256]{1,0:T(8,128)(2,1)S(1)} %get-tuple-element.78), channel_id=1, source_target_pairs={{0,1},{1,0},{2,3},{3,2},{4,5},{5,4},{6,7},{7,6},{8,9},{9,8},{10,11... | collective-permute-start | bytes 589832 | tf_op jit(solution)/shard_map/ppermute | solution.py:389
  8.5 16.4 %collective-permute-start.3 = (bf16[384,256]{1,0:T(8,128)(2,1)S(1)}, bf16[384,256]{1,0:T(8,128)(2,1)S(1)}, u32[]{:S(2)}, u32[]{:S(2)}) collective-permute-start(bf16[384,256]{1,0:T(8,128)(2,1)S(1)} %get-tuple-element.79), channel_id=1, source_target_pairs={{0,2},{1,3},{2,0},{3,1},{4,6},{5,7},{6,4},{7,5},{8,10},{9,11},{10,... | collective-permute-start | bytes 589832 | tf_op jit(solution)/shard_map/ppermute | solution.py:389
  10.7 15.2 %collective-permute-start.1 = (bf16[384,1024]{1,0:T(8,128)(2,1)}, bf16[384,1024]{1,0:T(8,128)(2,1)S(1)}, u32[]{:S(2)}, u32[]{:S(2)}) collective-permute-start(bf16[384,1024]{1,0:T(8,128)(2,1)} %raw_ref.1), channel_id=1, source_target_pairs={{0,8},{4,20},{8,0},{12,28},{16,24},{20,4},{24,16},{28,12},{1,9},{5... | collective-permute-start | bytes 2359304 | tf_op jit(solution)/shard_map/ppermute | solution.py:394
  17.9 15.1 %collective-permute-start.7 = (bf16[384,1024]{1,0:T(8,128)(2,1)S(1)}, bf16[384,1024]{1,0:T(8,128)(2,1)S(1)}, u32[]{:S(2)}, u32[]{:S(2)}) collective-permute-start(bf16[384,1024]{1,0:T(8,128)(2,1)S(1)} %collective-permute-done.raw_ref), channel_id=1, source_target_pairs={{0,8},{4,20},{8,0},{12,28},{16,24},{20,4},{24,16},{28,12},{1,9},{5... | collective-permute-start | bytes 2359304 | tf_op jit(solution)/shard_map/ppermute | solution.py:394
  25.2 2.6 %collective-permute-start.5 = (bf16[192,1024]{1,0:T(8,128)(2,1)S(1)}, bf16[192,1024]{1,0:T(8,128)(2,1)S(1)}, u32[]{:S(2)}, u32[]{:S(2)}) collective-permute-start(bf16[192,1024]{1,0:T(8,128)(2,1)S(1)} %get-tuple-element.89), channel_id=1, source_target_pairs={{0,4},{4,0},{8,12},{12,8},{16,20},{20,16},{24,28},{28,24},{1,5},{5... | collective-permute-start | bytes 1179656 | tf_op jit(solution)/shard_map/ppermute | solution.py:389
  25.3 2.6 %collective-permute-start.6 = (bf16[192,1024]{1,0:T(8,128)(2,1)S(1)}, bf16[192,1024]{1,0:T(8,128)(2,1)S(1)}, u32[]{:S(2)}, u32[]{:S(2)}) collective-permute-start(bf16[192,1024]{1,0:T(8,128)(2,1)S(1)} %get-tuple-element.90), channel_id=1, source_target_pairs={{0,4},{4,0},{8,12},{12,8},{16,20},{20,16},{24,28},{28,24},{1,5},{5... | collective-permute-start | bytes 1179656 | tf_op jit(solution)/shard_map/ppermute | solution.py:389
  29.3 15.9 %collective-permute-start.14 = (bf16[384,1024]{1,0:T(8,128)(2,1)S(1)}, bf16[384,1024]{1,0:T(8,128)(2,1)S(1)}, u32[]{:S(2)}, u32[]{:S(2)}) collective-permute-start(bf16[384,1024]{1,0:T(8,128)(2,1)S(1)} %get-tuple-element.112), channel_id=1, source_target_pairs={{0,8},{4,20},{8,0},{12,28},{16,24},{20,4},{24,16},{28,12},{1,9},{5... | collective-permute-start | bytes 2359304 | tf_op jit(solution)/shard_map/ppermute | solution.py:394
  35.2 14.6 %collective-permute-start.15 = (bf16[384,1024]{1,0:T(8,128)(2,1)S(1)}, bf16[384,1024]{1,0:T(8,128)(2,1)S(1)}, u32[]{:S(2)}, u32[]{:S(2)}) collective-permute-start(bf16[384,1024]{1,0:T(8,128)(2,1)S(1)} %get-tuple-element.117), channel_id=1, source_target_pairs={{0,8},{4,20},{8,0},{12,28},{16,24},{20,4},{24,16},{28,12},{1,9},{5... | collective-permute-start | bytes 2359304 | tf_op jit(solution)/shard_map/ppermute | solution.py:394
  37.6 1.6 %collective-permute-start.8 = (bf16[128,1024]{1,0:T(8,128)(2,1)S(1)}, bf16[128,1024]{1,0:T(8,128)(2,1)S(1)}, u32[]{:S(2)}, u32[]{:S(2)}) collective-permute-start(bf16[128,1024]{1,0:T(8,128)(2,1)S(1)} %get-tuple-element.102), channel_id=1, source_target_pairs={{0,4},{4,0},{8,12},{12,8},{16,20},{20,16},{24,28},{28,24},{1,5},{5... | collective-permute-start | bytes 786440 | tf_op jit(solution)/shard_map/ppermute | solution.py:389
  37.6 1.9 %collective-permute-start.9 = (bf16[128,1024]{1,0:T(8,128)(2,1)S(1)}, bf16[128,1024]{1,0:T(8,128)(2,1)S(1)}, u32[]{:S(2)}, u32[]{:S(2)}) collective-permute-start(bf16[128,1024]{1,0:T(8,128)(2,1)S(1)} %get-tuple-element.103), channel_id=1, source_target_pairs={{0,4},{4,0},{8,12},{12,8},{16,20},{20,16},{24,28},{28,24},{1,5},{5... | collective-permute-start | bytes 786440 | tf_op jit(solution)/shard_map/ppermute | solution.py:389
  38.1 1.8 %collective-permute-start.10 = (bf16[128,1024]{1,0:T(8,128)(2,1)S(1)}, bf16[128,1024]{1,0:T(8,128)(2,1)S(1)}, u32[]{:S(2)}, u32[]{:S(2)}) collective-permute-start(bf16[128,1024]{1,0:T(8,128)(2,1)S(1)} %get-tuple-element.104), channel_id=1, source_target_pairs={{0,4},{4,0},{8,12},{12,8},{16,20},{20,16},{24,28},{28,24},{1,5},{5... | collective-permute-start | bytes 786440 | tf_op jit(solution)/shard_map/ppermute | solution.py:389
  40.7 10.8 %collective-permute-start.11 = (bf16[384,256]{1,0:T(8,128)(2,1)S(1)}, bf16[384,256]{1,0:T(8,128)(2,1)S(1)}, u32[]{:S(2)}, u32[]{:S(2)}) collective-permute-start(bf16[384,256]{1,0:T(8,128)(2,1)S(1)} %get-tuple-element.107), channel_id=1, source_target_pairs={{0,1},{1,0},{2,3},{3,2},{4,5},{5,4},{6,7},{7,6},{8,9},{9,8},{10,11... | collective-permute-start | bytes 589832 | tf_op jit(solution)/shard_map/ppermute | solution.py:389
  41.2 17.1 %collective-permute-start.12 = (bf16[384,256]{1,0:T(8,128)(2,1)S(1)}, bf16[384,256]{1,0:T(8,128)(2,1)S(1)}, u32[]{:S(2)}, u32[]{:S(2)}) collective-permute-start(bf16[384,256]{1,0:T(8,128)(2,1)S(1)} %get-tuple-element.108), channel_id=1, source_target_pairs={{0,2},{1,3},{2,0},{3,1},{4,6},{5,7},{6,4},{7,5},{8,10},{9,11},{10,... | collective-permute-start | bytes 589832 | tf_op jit(solution)/shard_map/ppermute | solution.py:389
  43.8 14.5 %collective-permute-start.13 = (bf16[384,256]{1,0:T(8,128)(2,1)S(1)}, bf16[384,256]{1,0:T(8,128)(2,1)S(1)}, u32[]{:S(2)}, u32[]{:S(2)}) collective-permute-start(bf16[384,256]{1,0:T(8,128)(2,1)S(1)} %get-tuple-element.109), channel_id=1, source_target_pairs={{0,3},{1,2},{2,1},{3,0},{4,7},{5,6},{6,5},{7,4},{8,11},{9,10},{10,... | collective-permute-start | bytes 589832 | tf_op jit(solution)/shard_map/ppermute | solution.py:389
  49.9 12.1 %collective-permute-start.16 = (bf16[384,1024]{1,0:T(8,128)(2,1)S(1)}, bf16[384,1024]{1,0:T(8,128)(2,1)S(1)}, u32[]{:S(2)}, u32[]{:S(2)}) collective-permute-start(bf16[384,1024]{1,0:T(8,128)(2,1)S(1)} %shard_map.101), channel_id=1, source_target_pairs={{0,16},{4,12},{8,24},{12,4},{16,0},{20,28},{24,8},{28,20},{1,17},{... | collective-permute-start | bytes 2359304 | tf_op jit(solution)/shard_map/ppermute | solution.py:394

commit v4 on v3

--- a/solution.py
+++ b/solution.py
@@ -11,8 +11,9 @@
 TILE = 128
 SLOTS = 3
 WAIT_FLOPS = 20_000_000_000
-TEXT_PIECES = 2
+TEXT_PIECES = 3
 ACC_PIECES = 3
+LAST_PIECES = 2
 CORES = 2
 EPS = 1e-06
 LOG2E = math.log2(math.e)
@@ -32,10 +33,12 @@
     outs_anywhere=False,
     scratch=(),
     flops=0,
+    moved=None,
     limit=24,
 ):
-    moved = sum(x.size * x.dtype.itemsize for x in operands)
-    moved += sum(math.prod(o.shape) * o.dtype.itemsize for o in outs)
+    if moved is None:
+        moved = sum(x.size * x.dtype.itemsize for x in operands)
+        moved += sum(math.prod(o.shape) * o.dtype.itemsize for o in outs)
     specs = [SMEM_SPEC] * scalars + [VMEM_SPEC] * (len(operands) - scalars)
     for at in anywhere:
         specs[at] = ANY_SPEC
@@ -88,13 +91,15 @@
 
 
 def unit_text_body(chunks, *refs):
-    chunk_refs, unit_ref, piece_refs = refs[:chunks], refs[chunks], refs[chunks + 1 :]
+    chunk_refs, (unit_ref, scale_ref) = refs[:chunks], refs[chunks : chunks + 2]
+    piece_refs = refs[chunks + 2 :]
     place = lax.axis_index("tp")
     rows, width = chunk_refs[0].shape
     for first in range(0, rows, TILE):
         part = pl.ds(first, TILE)
         parts = [ref[part, :].astype(jnp.float32) for ref in chunk_refs]
         scales = row_scales(sum(jnp.sum(x * x, axis=-1, keepdims=True) for x in parts))
+        scale_ref[part, :] = jnp.broadcast_to(scales, (TILE, TILE))
         for k, x in enumerate(parts):
             unit_ref[part, feature_slice(place, k, width)] = (x * scales).astype(jnp.bfloat16)
     split_rows(unit_ref, piece_refs)
@@ -110,29 +115,29 @@
         whole_ref[pl.ds(at * ref.shape[0], ref.shape[0]), :] = ref[...]
 
 
-def unit_images(piece_refs, image_ref):
-    start = 0
+def unit_images(ref, image_ref, scale_ref=None):
     step = 64
-    for ref in piece_refs:
-        for first in range(0, ref.shape[0], step):
-            values = ref[pl.ds(first, step), :].astype(jnp.float32)
-            scales = row_scales(jnp.sum(values * values, axis=-1, keepdims=True))
-            image_ref[pl.ds(start + first, step), :] = (values * scales).astype(jnp.bfloat16)
-        start += ref.shape[0]
+    for first in range(0, ref.shape[0], step):
+        part = pl.ds(first, step)
+        values = ref[part, :].astype(jnp.float32)
+        scales = row_scales(jnp.sum(values * values, axis=-1, keepdims=True))
+        image_ref[part, :] = (values * scales).astype(jnp.bfloat16)
+        if scale_ref is not None:
+            scale_ref[part, :] = jnp.broadcast_to(scales, (step, TILE))
 
 
 def unit_images_body(raw_ref, out_ref):
-    unit_images([raw_ref], out_ref)
-
-
-def own_images_body(raw_ref, out_ref, raw_out_ref):
-    unit_images([raw_ref], out_ref)
+    unit_images(raw_ref, out_ref)
+
+
+def own_images_body(raw_ref, out_ref, raw_out_ref, scale_ref):
+    unit_images(raw_ref, out_ref, scale_ref)
     raw_out_ref[...] = raw_ref[...]
 
 
 def near_images_body(first_ref, second_unit_ref, out_ref):
     rows = first_ref.shape[0]
-    unit_images([first_ref], out_ref)
+    unit_images(first_ref, out_ref)
     out_ref[rows:, :] = second_unit_ref[...]
 
 
@@ -241,12 +246,12 @@
     sum_ref[...] = dot_tn(weight_ref[...], unit_ref[...]).astype(jnp.bfloat16)
 
 
-def second_sum_body(tiles, *refs):
+def near_sum_body(tiles, *refs):
     pairs = Pairs(refs, tiles)
     unit_ref, own_image_ref, near_image_ref, own_weight_in_ref, weight_in_ref, first_ref = refs[
         Pairs.count : Pairs.count + 6
     ]
-    own_weight_ref, acc_ref, sum_ref, weight_ref = refs[Pairs.count + 6 :]
+    own_weight_ref, acc_ref, weight_ref = refs[Pairs.count + 6 :]
     rows = own_image_ref.shape[0]
     second = dot_nt(unit_ref[rows:, :], near_image_ref[pl.ds(rows, rows), :])
     own = dot_nt(unit_ref[rows:, :], own_image_ref[...])
@@ -254,26 +259,29 @@
     weight_ref[:, :rows] = first_ref[...]
     weight_ref[:rows, rows:] = weight_in_ref[:, rows:]
     pairs.weigh(second, 1, 2, weight_ref, rows, rows)
-    sum_ref[...] = dot_tn(weight_ref[:, rows:], unit_ref[...])
     pairs.weigh(own, 1, 0, own_weight_ref, rows, 0)
     acc_ref[...] = jnp.dot(
         weight_ref[...], near_image_ref[...], preferred_element_type=jnp.float32
     )
 
 
-def far_sum_body(tiles, *refs):
+def far_weights_body(tiles, *refs):
     pairs = Pairs(refs, tiles)
     unit_ref, own_image_ref, own_weight_ref, raw_ref = refs[Pairs.count : Pairs.count + 4]
-    sum_ref, weight_ref, image_ref = refs[Pairs.count + 4 :]
+    weight_ref, image_ref = refs[Pairs.count + 4 :]
     rows = raw_ref.shape[0]
-    unit_images([raw_ref], image_ref.at[pl.ds(rows, rows), :])
+    unit_images(raw_ref, image_ref.at[pl.ds(rows, rows), :])
     products = dot_nt(unit_ref[...], image_ref[rows:, :])
     for half in range(CORES):
         part = products[half * rows : (half + 1) * rows, :]
         pairs.weigh(part, half, 3, weight_ref, half * rows, rows)
-    sum_ref[...] = dot_tn(weight_ref[:, rows:], unit_ref[...]).astype(jnp.bfloat16)
     image_ref[:rows, :] = own_image_ref[...]
     weight_ref[:, :rows] = own_weight_ref[...]
+
+
+def far_sum_body(weight_ref, unit_ref, out_ref):
+    rows = out_ref.shape[0]
+    out_ref[...] = dot_tn(weight_ref[:, rows:], unit_ref[...]).astype(jnp.bfloat16)
 
 
 def text_sum_body(half, weight_ref, image_ref, acc_ref, *out_refs):
@@ -287,9 +295,10 @@
         ref[...] = acc[at * size : (at + 1) * size, :].astype(ref.dtype)
 
 
-def own_sum_body(weight_ref, unit_ref, add_ref, out_ref):
-    rows = out_ref.shape[0]
-    out_ref[...] = dot_tn(weight_ref[:, :rows], unit_ref[...]) + add_ref[...].astype(jnp.float32)
+def own_sum_body(own_weight_ref, near_weight_ref, unit_ref, add_ref, own_ref, second_ref):
+    rows = own_ref.shape[0]
+    second_ref[...] = dot_tn(near_weight_ref[:, rows:], unit_ref[...])
+    own_ref[...] = dot_tn(own_weight_ref[...], unit_ref[...]) + add_ref[...].astype(jnp.float32)
 
 
 def all_body(tiles, chips, *refs):
@@ -299,7 +308,7 @@
     spread_ref, acc_ref, acc_piece_refs = outs[0], outs[1], outs[2 : 2 + ACC_PIECES]
     image_ref, weight_ref = outs[2 + ACC_PIECES :]
     rows = own_ref.shape[0]
-    unit_images([piece_ref], image_ref)
+    unit_images(piece_ref, image_ref)
     for half, text_ref in enumerate((own_ref, other_ref)):
         for chip in range(chips):
             products = dot_nt(text_ref[...], image_ref[pl.ds(chip * rows, rows), :])
@@ -324,29 +333,31 @@
         spread_ref[columns, :] = total.astype(jnp.bfloat16)
 
 
-def relay_body(sum_ref, in_ref, out_ref):
-    out_ref[...] = (sum_ref[...] + in_ref[...].astype(jnp.float32)).astype(jnp.bfloat16)
+def relay_body(sum_ref, in_ref, *out_refs):
+    for at, ref in enumerate(out_refs):
+        part = pl.ds(at * ref.shape[0], ref.shape[0])
+        ref[...] = (sum_ref[part, :] + in_ref[part, :].astype(jnp.float32)).astype(jnp.bfloat16)
 
 
 def text_grad_body(chunks, *refs):
-    raw_refs, acc_ref, add_refs = refs[:chunks], refs[chunks], refs[chunks + 1 : -chunks]
-    out_refs = refs[-chunks:]
+    scale_ref, raw_refs, acc_ref = refs[0], refs[1 : 1 + chunks], refs[1 + chunks]
+    add_refs, out_refs = refs[2 + chunks : -chunks], refs[-chunks:]
     place = lax.axis_index("tp")
     rows, width = raw_refs[0].shape
     size = add_refs[0].shape[0]
-    for first in range(0, rows, TILE):
-        part = pl.ds(first, TILE)
+    for first in range(0, rows, TILE // 2):
+        part = pl.ds(first, TILE // 2)
+        scales = scale_ref[part, :1]
         raws = [ref[part, :].astype(jnp.float32) for ref in raw_refs]
-        scales = row_scales(sum(jnp.sum(x * x, axis=-1, keepdims=True) for x in raws))
         accs = []
         for k in range(chunks):
             features = feature_slice(place, k, width)
-            added = add_refs[first // size][pl.ds(first % size, TILE), features]
+            added = add_refs[first // size][pl.ds(first % size, TILE // 2), features]
             accs.append(acc_ref[part, features] + added.astype(jnp.float32))
-        units = [x * scales for x in raws]
-        inner = sum(jnp.sum(u * a, axis=-1, keepdims=True) for u, a in zip(units, accs))
+        inner = sum(jnp.sum(x * a, axis=-1, keepdims=True) for x, a in zip(raws, accs))
+        inner = inner * scales * scales
         for k in range(chunks):
-            out_refs[k][part, :] = (scales * (accs[k] - units[k] * inner)).astype(jnp.bfloat16)
+            out_refs[k][part, :] = (scales * (accs[k] - raws[k] * inner)).astype(jnp.bfloat16)
 
 
 def place_text_body(chunks, *refs):
@@ -363,18 +374,21 @@
         copy.wait()
 
 
-def image_grad_body(sum_count, raw_ref, *refs):
-    sum_refs, (out_ref, grad_ref, sems) = refs[:sum_count], refs[sum_count:]
+def image_grad_body(piece_count, raw_ref, scale_ref, sum_ref, *refs):
+    piece_refs, (out_ref, grad_ref, sems) = refs[:piece_count], refs[piece_count:]
     copies = []
     for block in range(raw_ref.shape[0] // TILE):
         for first in range(block * TILE, (block + 1) * TILE, TILE // 2):
             part = pl.ds(first, TILE // 2)
             raw = raw_ref[part, :].astype(jnp.float32)
-            scales = row_scales(jnp.sum(raw * raw, axis=-1, keepdims=True))
-            unit = raw * scales
-            acc = sum(ref[part, :].astype(jnp.float32) for ref in sum_refs)
-            inner = jnp.sum(unit * acc, axis=-1, keepdims=True)
-            grad_ref[part, :] = (scales * (acc - unit * inner)).astype(jnp.bfloat16)
+            scales = scale_ref[part, :1]
+            acc = sum_ref[part, :]
+            if piece_refs:
+                size = piece_refs[0].shape[0]
+                piece = piece_refs[first // size][pl.ds(first % size, TILE // 2), :]
+                acc = acc + piece.astype(jnp.float32)
+            inner = jnp.sum(raw * acc, axis=-1, keepdims=True) * scales * scales
+            grad_ref[part, :] = (scales * (acc - raw * inner)).astype(jnp.bfloat16)
         part = pl.ds(block * TILE, TILE)
         copies.append(
             pltpu.make_async_copy(grad_ref.at[part, :], out_ref.at[part, :], sems.at[block])
@@ -413,14 +427,16 @@
         return struct((count, columns), jnp.int32)
 
     picked = call_kernel(pick_body, [bf16(rows, width)] * groups, [text_emb], limit=8)
-    picked[-1], image_sent = lax.optimization_barrier((picked[-1], image_emb))
     text_raw = [picked[0]] + [swap(picked[k], "tp", k) for k in range(1, groups)]
     if square:
-        from_second = swap_near(image_sent, 1)
+        from_second = swap_near(image_emb, 1)
     else:
         same_core = [[chip * CORES + core for chip in range(chips)] for core in range(CORES)]
         gathered = lax.all_gather(
             image_emb, "blk", axis=0, tiled=True, axis_index_groups=same_core
+        )
+        _, image_raw, image_scales = call_kernel(
+            own_images_body, [bf16(rows), bf16(rows), f32(rows, TILE)], [image_emb], limit=8
         )
     lists = call_kernel(
         functools.partial(list_body, groups, tiles, chips),
@@ -443,10 +459,10 @@
         limit=8,
     )
     if square:
-        own_images, image_emb = call_kernel(
-            own_images_body, [bf16(rows)] * 2, [image_emb], limit=8
-        )
-        image_sent, own_images = lax.optimization_barrier((image_sent, own_images))
+        own_images, image_raw, image_scales = call_kernel(
+            own_images_body, [bf16(rows), bf16(rows), f32(rows, TILE)], [image_emb], limit=8
+        )
+        image_sent, own_images = lax.optimization_barrier((image_emb, own_images))
         from_first = swap_near(image_sent, 0)
         from_second, own_images, *lists = lax.optimization_barrier(
             (from_second, own_images, *lists)
@@ -456,9 +472,9 @@
             unit_images_body, [bf16(rows)], [from_second], flops=WAIT_FLOPS // 2, limit=8
         )[0]
         text_raw[-1], second_images = lax.optimization_barrier((text_raw[-1], second_images))
-    text_own, *pieces = call_kernel(
+    text_own, text_scales, *pieces = call_kernel(
         functools.partial(unit_text_body, groups),
-        [bf16(rows)] + [bf16(rows // TEXT_PIECES)] * TEXT_PIECES,
+        [bf16(rows), f32(rows, TILE)] + [bf16(rows // TEXT_PIECES)] * TEXT_PIECES,
         text_raw,
         limit=8,
     )
@@ -474,10 +490,11 @@
         parts = call_kernel(
             functools.partial(text_grad_body, groups),
             [bf16(rows, width)] * groups,
-            text_raw + [acc_own] + [swap(piece, "blk", 1) for piece in acc_other],
+            [text_scales] + text_raw + [acc_own] + [swap(piece, "blk", 1) for piece in acc_other],
             limit=16,
         )
-        return [parts[0]] + [swap(parts[k], "tp", k) for k in range(1, groups)]
+        sent = [swap(parts[k], "tp", k) for k in reversed(range(1, groups))]
+        return [parts[0]] + sent[::-1]
 
     def place_text(text_parts):
         return call_kernel(
@@ -490,11 +507,11 @@
             limit=8,
         )[0]
 
-    def finish_image(sums):
+    def finish_image(total, pieces):
         return call_kernel(
-            functools.partial(image_grad_body, len(sums)),
+            functools.partial(image_grad_body, len(pieces)),
             [bf16(rows)],
-            [image_emb] + sums,
+            [image_raw, image_scales, total] + pieces,
             outs_anywhere=True,
             scratch=[pltpu.VMEM((rows, embed), jnp.bfloat16), pltpu.SemaphoreType.DMA((tiles,))],
             limit=8,
@@ -518,7 +535,7 @@
             spread, "blk", split_axis=0, concat_axis=0, tiled=True, axis_index_groups=same_core
         )
         total = jnp.sum(parts.reshape(-1, rows, embed).astype(jnp.float32), axis=0)
-        return (place_text(text_parts), finish_image([total]))
+        return (place_text(text_parts), finish_image(total, []))
 
     own_weights, near_weights = call_kernel(
         functools.partial(near_own_body, tiles),
@@ -533,17 +550,16 @@
         limit=16,
     )
     image_add = swap_near(first_sum, 0)
-    own_weights, acc, second_sum = call_kernel(
-        functools.partial(second_sum_body, tiles),
-        [bf16(2 * rows, rows), f32(2 * rows), f32(rows)],
+    own_weights, acc, near_weights = call_kernel(
+        functools.partial(near_sum_body, tiles),
+        [bf16(2 * rows, rows), f32(2 * rows), bf16(2 * rows, 2 * rows)],
         lists + [units, own_images, near_images, own_weights, near_weights, first_weights],
-        scratch=[pltpu.VMEM((2 * rows, 2 * rows), jnp.bfloat16)],
         limit=24,
     )
     own_weights, from_far = lax.optimization_barrier((own_weights, from_far))
-    far_sum, far_weights, far_images = call_kernel(
-        functools.partial(far_sum_body, tiles),
-        [bf16(rows), bf16(2 * rows, 2 * rows), bf16(2 * rows)],
+    far_weights, far_images = call_kernel(
+        functools.partial(far_weights_body, tiles),
+        [bf16(2 * rows, 2 * rows), bf16(2 * rows)],
         lists + [units, own_images, own_weights, from_far],
         limit=16,
     )
@@ -560,19 +576,28 @@
         [far_weights, far_images, acc],
         limit=16,
     )[0]
+    far_weights, acc_own = lax.optimization_barrier((far_weights, acc_own))
+    far_sum = call_kernel(far_sum_body, [bf16(rows)], [far_weights, units], limit=16)[0]
+    acc_own, far_sum = lax.optimization_barrier((acc_own, far_sum))
     text_parts = finish_text(acc_own, acc_other)
-    far_weights, text_parts[0] = lax.optimization_barrier((far_weights, text_parts[0]))
-    base = call_kernel(
-        own_sum_body, [f32(rows)], [far_weights, units, image_add], limit=16
-    )[0]
-    base, second_sum = lax.optimization_barrier((base, second_sum))
+    own_weights, text_parts[0] = lax.optimization_barrier((own_weights, text_parts[0]))
+    base, second_sum = call_kernel(
+        own_sum_body,
+        [f32(rows), f32(rows)],
+        [own_weights, near_weights, units, image_add],
+        flops=WAIT_FLOPS,
+        limit=16,
+    )
     relayed = call_kernel(
-        relay_body, [bf16(rows)], [second_sum, swap_near(far_sum, 0)], limit=8
-    )[0]
-    image_last = swap_near(relayed, 1)
+        relay_body,
+        [bf16(rows // LAST_PIECES)] * LAST_PIECES,
+        [second_sum, swap_near(far_sum, 0)],
+        limit=8,
+    )
+    image_last = [swap_near(piece, 1) for piece in relayed]
     text_grad = place_text(text_parts)
     base, _ = lax.optimization_barrier((base, text_grad))
-    return (text_grad, finish_image([base, image_last]))
+    return (text_grad, finish_image(base, image_last))
 
 
 def solution(mesh):

time: 63.6 us -> 62.9 us (0.989)
  waiting for transfers between devices: 20.9 us -> 17.9 us
  starting transfers between devices: 21.7 us -> 23.6 us
    ppermute x6 -> x7, waiting for transfers between devices: 9.76 us -> 5.66 us  [swap_near(): lax.ppermute(value, 'blk', [(i, i ^ neighbour_bits(i)[which]) for i in ra...]
    ppermute x11 -> x12, starting transfers between devices: 10.1 us -> 11.3 us  [swap(): return lax.ppermute(value, axis, [(i, i ^ bits) for i in range(count)])]
    ppermute x11 -> x12, waiting for transfers between devices: 11.2 us -> 12.3 us  [swap(): return lax.ppermute(value, axis, [(i, i ^ bits) for i in range(count)])]
    ppermute x6 -> x7, starting transfers between devices: 11.6 us -> 12.3 us  [swap_near(): lax.ppermute(value, 'blk', [(i, i ^ neighbour_bits(i)[which]) for i in ra...]
    pallas_call x17 -> x18, Pallas kernels: 17.5 us -> 17.5 us  [call_kernel(): pl.pallas_call(body, out_shape=outs, in_specs=specs, out_specs=[ANY_SPEC...]
  transfers between devices with their start and end apart: 17 -> 19, of which waited for: 8 -> 6; matrix products, arithmetic and copies ran while one was open for 0% -> 0% of each run, Pallas kernels for 25% -> 26%
where the time goes in v4:
time: 62.9 us; the launch traced here: 62.3 us
  starting transfers between devices  23.6 us (38%)
  waiting for transfers between devices  17.9 us (28%)
  Pallas kernels  17.5 us (28%)
  between operations  2.13 us (3%)
  local copies, waits for them, and re-layouts  1.14 us (2%)
    pallas_call x18, Pallas kernels, call_kernel(): pl.pallas_call(body, out_shape=outs, in_specs=specs, out_specs=[ANY_SPEC...  17.5 us
    ppermute x12, waiting for transfers between devices, swap(): return lax.ppermute(value, axis, [(i, i ^ bits) for i in range(count)])  12.3 us
    ppermute x7, starting transfers between devices, swap_near(): lax.ppermute(value, 'blk', [(i, i ^ neighbour_bits(i)[which]) for i in ra...  12.3 us
    ppermute x12, starting transfers between devices, swap(): return lax.ppermute(value, axis, [(i, i ^ bits) for i in range(count)])  11.3 us
    ppermute x7, waiting for transfers between devices, swap_near(): lax.ppermute(value, 'blk', [(i, i ^ neighbour_bits(i)[which]) for i in ra...  5.66 us
  transfers between devices with their start and end apart: 19, of which 6 were waited for; matrix products, arithmetic and copies ran while one was open for 0% of the time, Pallas kernels for 26%

profile of v4, /device:TPU:0, one launch (start us, length us, event | category | flops | bytes accessed | tf_op | source)
XLA Modules:
  0.0 62.3 jit_solution(14799608101841765208)
XLA Ops:
  0.6 3.0 %collective-permute-start = (bf16[384,1024]{1,0:T(8,128)(2,1)}, bf16[384,1024]{1,0:T(8,128)(2,1)S(1)}, u32[]{:S(2)}, u32[]{:S(2)}) collective-permute-start(bf16[384,1024]{1,0:T(8,128)(2,1)} %raw_ref.1), channel_id=1, source_target_pairs={{0,16},{4,12},{8,24},{12,4},{16,0},{20,28},{24,8},{28,20},{1,17},{... | collective-permute-start | bytes 2359304 | tf_op jit(solution)/shard_map/ppermute | solution.py:408
  3.7 1.1 %copy-done = bf16[1536,256]{1,0:T(8,128)(2,1)S(1)} copy-done((bf16[1536,256]{1,0:T(8,128)(2,1)S(1)}, bf16[1536,256]{1,0:T(8,128)(2,1)}, u32[]{:S(2)}) %copy-start) | copy-done | bytes 786456
  4.8 0.1 shard_map.88
  4.9 1.6 %collective-permute-start.2 = (bf16[384,256]{1,0:T(8,128)(2,1)S(1)}, bf16[384,256]{1,0:T(8,128)(2,1)S(1)}, u32[]{:S(2)}, u32[]{:S(2)}) collective-permute-start(bf16[384,256]{1,0:T(8,128)(2,1)S(1)} %get-tuple-element.82), channel_id=1, source_target_pairs={{0,1},{1,0},{2,3},{3,2},{4,5},{5,4},{6,7},{7,6},{8,9},{9,8},{10,11... | collective-permute-start | bytes 589832 | tf_op jit(solution)/shard_map/ppermute | solution.py:403
  6.5 2.6 %collective-permute-start.3 = (bf16[384,256]{1,0:T(8,128)(2,1)S(1)}, bf16[384,256]{1,0:T(8,128)(2,1)S(1)}, u32[]{:S(2)}, u32[]{:S(2)}) collective-permute-start(bf16[384,256]{1,0:T(8,128)(2,1)S(1)} %get-tuple-element.83), channel_id=1, source_target_pairs={{0,2},{1,3},{2,0},{3,1},{4,6},{5,7},{6,4},{7,5},{8,10},{9,11},{10,... | collective-permute-start | bytes 589832 | tf_op jit(solution)/shard_map/ppermute | solution.py:403
  9.1 0.2 collective-permute-start.4
  9.3 1.4 %shard_map.86 = (bf16[384,1024]{1,0:T(8,128)(2,1)S(1)}, bf16[384,1024]{1,0:T(8,128)(2,1)S(1)}, f32[384,128]{1,0:T(8,128)S(1)}) custom-call(bf16[384,1024]{1,0:T(8,128)(2,1)} %raw_ref.1), custom_call_target="tpu_custom_call" | custom-call | bytes 2555904 | tf_op jit(solution)/shard_map/pallas_call | solution.py:46
  10.7 1.6 %collective-permute-start.1 = (bf16[384,1024]{1,0:T(8,128)(2,1)}, bf16[384,1024]{1,0:T(8,128)(2,1)S(1)}, u32[]{:S(2)}, u32[]{:S(2)}) collective-permute-start(bf16[384,1024]{1,0:T(8,128)(2,1)} %raw_ref.1), channel_id=1, source_target_pairs={{0,8},{4,20},{8,0},{12,28},{16,24},{20,4},{24,16},{28,12},{1,9},{5... | collective-permute-start | bytes 2359304 | tf_op jit(solution)/shard_map/ppermute | solution.py:408
  13.6 1.1 %shard_map.87 = (f32[2,128]{1,0:T(2,128)S(1)}, f32[72,128]{1,0:T(8,128)S(1)}, s32[12,128]{1,0:T(8,128)S(1)}, s32[768,128]{1,0:T(8,128)S(1)}, f32[384,128]{1,0:T(8,128)S(1)}, /*index=5*/f32[4,128]{1,0:T(4,128)S(1)}) custom-call(f32[1]{0:T(128)S(6)} %copy.9.refs_0_, f32[1]{0:T(128)S(6)} %copy.10.refs_1_, s32[3,8,96]{2,1,0:T(8,128)S(1)} %bitcast.5, ...), custom_call_target="tpu_custom_call" | custom-call | bytes 743432 | tf_op jit(solution)/shard_map/pallas_call | solution.py:46
  14.7 0.7 %collective-permute-done.raw_ref = bf16[384,1024]{1,0:T(8,128)(2,1)S(1)} collective-permute-done((bf16[384,1024]{1,0:T(8,128)(2,1)}, bf16[384,1024]{1,0:T(8,128)(2,1)S(1)}, u32[]{:S(2)}, u32[]{:S(2)}) %collective-permute-start) | collective-permute-done | bytes 786464 | tf_op jit(solution)/shard_map/ppermute | solution.py:408
  15.4 3.3 %collective-permute-start.8 = (bf16[384,1024]{1,0:T(8,128)(2,1)S(1)}, bf16[384,1024]{1,0:T(8,128)(2,1)S(1)}, u32[]{:S(2)}, u32[]{:S(2)}) collective-permute-start(bf16[384,1024]{1,0:T(8,128)(2,1)S(1)} %collective-permute-done.raw_ref), channel_id=1, source_target_pairs={{0,8},{4,20},{8,0},{12,28},{16,24},{20,4},{24,16},{28,12},{1,9},{5... | collective-permute-start | bytes 2359304 | tf_op jit(solution)/shard_map/ppermute | solution.py:408
  18.7 0.2 shard_map.89.second_unit_ref
  19.0 2.8 %collective-permute-done.4.refs_3_.refs_4_ = bf16[384,256]{1,0:T(8,128)(2,1)S(1)} collective-permute-done((bf16[384,256]{1,0:T(8,128)(2,1)S(1)}, bf16[384,256]{1,0:T(8,128)(2,1)S(1)}, u32[]{:S(2)}, u32[]{:S(2)}) %collective-permute-start.4) | collective-permute-done | bytes 196640 | tf_op jit(solution)/shard_map/ppermute | solution.py:403
  21.8 0.0 collective-permute-done.2.refs_1_.refs_2_
  21.8 1.9 %collective-permute-done.3.refs_2_.refs_3_ = bf16[384,256]{1,0:T(8,128)(2,1)S(1)} collective-permute-done((bf16[384,256]{1,0:T(8,128)(2,1)S(1)}, bf16[384,256]{1,0:T(8,128)(2,1)S(1)}, u32[]{:S(2)}, u32[]{:S(2)}) %collective-permute-start.3) | collective-permute-done | bytes 196640 | tf_op jit(solution)/shard_map/ppermute | solution.py:403
  23.7 0.4 shard_map.90
  24.1 0.1 collective-permute-start.5
  24.2 0.5 collective-permute-start.6
  24.6 0.1 collective-permute-start.7
  24.7 0.0 collective-permute-done.1.first_ref
  24.7 0.3 shard_map.91.refs_8_.refs_7_
  25.0 1.8 %shard_map.92 = (bf16[384,384]{1,0:T(8,128)(2,1)S(1)}, bf16[384,768]{1,0:T(8,128)(2,1)S(1)}) custom-call(f32[2,128]{1,0:T(2,128)S(1)} %get-tuple-element.74.refs_0_, f32[72,128]{1,0:T(8,128)S(1)} %get-tuple-element.75.refs_1_, s32[12,128]{1,0:T(8,128)S(1)} %get-tuple-element.76.refs_2_, s32[768,128]{1,0:T(8,128)S(1)} %get-tuple-element.77.refs_3_, ...), custom_call_target="tpu_custom_call" | custom-call | bytes 4666368 | tf_op jit(solution)/shard_map/pallas_call | solution.py:46
  26.8 0.0 collective-permute-done.6.refs_10_
  26.8 0.0 collective-permute-done.7.refs_11_
  26.8 1.4 %shard_map.93 = (bf16[768,1024]{1,0:T(8,128)(2,1)S(1)}, bf16[768,384]{1,0:T(8,128)(2,1)S(1)}, bf16[384,1024]{1,0:T(8,128)(2,1)S(1)}) custom-call(f32[2,128]{1,0:T(2,128)S(1)} %get-tuple-element.74.refs_0_, f32[72,128]{1,0:T(8,128)S(1)} %get-tuple-element.75.refs_1_, s32[12,128]{1,0:T(8,128)S(1)} %get-tuple-element.76.refs_2_, ...), custom_call_target="tpu_custom_call" | custom-call | bytes 7320576 | tf_op jit(solution)/shard_map/pallas_call | solution.py:46
  28.2 0.9 %collective-permute-start.15 = (bf16[384,1024]{1,0:T(8,128)(2,1)S(1)}, bf16[384,1024]{1,0:T(8,128)(2,1)S(1)}, u32[]{:S(2)}, u32[]{:S(2)}) collective-permute-start(bf16[384,1024]{1,0:T(8,128)(2,1)S(1)} %get-tuple-element.123), channel_id=1, source_target_pairs={{0,8},{4,20},{8,0},{12,28},{16,24},{20,4},{24,16},{28,12},{1,9},{5... | collective-permute-start | bytes 2359304 | tf_op jit(solution)/shard_map/ppermute | solution.py:408
  29.2 2.5 %shard_map.94 = (bf16[768,384]{1,0:T(8,128)(2,1)S(1)}, f32[768,1024]{1,0:T(8,128)S(1)}, bf16[768,768]{1,0:T(8,128)(2,1)S(1)}) custom-call(f32[2,128]{1,0:T(2,128)S(1)} %get-tuple-element.74.refs_0_, f32[72,128]{1,0:T(8,128)S(1)} %get-tuple-element.75.refs_1_, s32[12,128]{1,0:T(8,128)S(1)} %get-tuple-element.76.refs_2_, ...), custom_call_target="tpu_custom_call" | custom-call | bytes 10957824 | tf_op jit(solution)/shard_map/pallas_call | solution.py:46
  31.7 1.6 %shard_map.95 = (bf16[768,768]{1,0:T(8,128)(2,1)S(1)}, bf16[768,1024]{1,0:T(8,128)(2,1)S(1)}) custom-call(f32[2,128]{1,0:T(2,128)S(1)} %get-tuple-element.74.refs_0_, f32[72,128]{1,0:T(8,128)S(1)} %get-tuple-element.75.refs_1_, s32[12,128]{1,0:T(8,128)S(1)} %get-tuple-element.76.refs_2_, s32[768,128]{1,0:T(8,128)S(1)} %get-tuple-element.77.refs_3_, ...), custom_call_target="tpu_custom_call" | custom-call | bytes 7123968 | tf_op jit(solution)/shard_map/pallas_call | solution.py:46
  33.2 0.8 %shard_map.96 = (bf16[128,1024]{1,0:T(8,128)(2,1)S(1)}, bf16[128,1024]{1,0:T(8,128)(2,1)S(1)}, bf16[128,1024]{1,0:T(8,128)(2,1)S(1)}) custom-call(bf16[768,768]{1,0:T(8,128)(2,1)S(1)} %get-tuple-element.109.weight_ref, bf16[768,1024]{1,0:T(8,128)(2,1)S(1)} %get-tuple-element.107.image_ref, f32[768,1024]{1,0:T(8,128)S(1)} %get-tuple-element.105.acc_ref), custom_call_target="tpu_custom_call" | custom-call | bytes 6684672 | tf_op jit(solution)/shard_map/pallas_call | solution.py:46
  34.0 0.1 collective-permute-start.9
  34.1 0.5 collective-permute-start.10
  34.6 0.1 collective-permute-start.11
  34.7 0.8 %shard_map.97.refs_5_ = f32[384,1024]{1,0:T(8,128)S(1)} custom-call(bf16[768,768]{1,0:T(8,128)(2,1)S(1)} %get-tuple-element.109.weight_ref, bf16[768,1024]{1,0:T(8,128)(2,1)S(1)} %get-tuple-element.107.image_ref, f32[768,1024]{1,0:T(8,128)S(1)} %get-tuple-element.105.acc_ref), custom_call_target="tpu_custom_call" | custom-call | bytes 7471104 | tf_op jit(solution)/shard_map/pallas_call | solution.py:46
  35.5 0.8 %shard_map.98 = bf16[384,1024]{1,0:T(8,128)(2,1)S(1)} custom-call(bf16[768,768]{1,0:T(8,128)(2,1)S(1)} %get-tuple-element.109.weight_ref, bf16[768,1024]{1,0:T(8,128)(2,1)S(1)} %get-tuple-element.96.refs_6_.unit_ref), custom_call_target="tpu_custom_call" | custom-call | bytes 3538944 | tf_op jit(solution)/shard_map/pallas_call | solution.py:46
  36.3 1.3 %collective-permute-start.16 = (bf16[384,1024]{1,0:T(8,128)(2,1)S(1)}, bf16[384,1024]{1,0:T(8,128)(2,1)S(1)}, u32[]{:S(2)}, u32[]{:S(2)}) collective-permute-start(bf16[384,1024]{1,0:T(8,128)(2,1)S(1)} %shard_map.98), channel_id=1, source_target_pairs={{0,8},{4,20},{8,0},{12,28},{16,24},{20,4},{24,16},{28,12},{1,9},{5... | collective-permute-start | bytes 2359304 | tf_op jit(solution)/shard_map/ppermute | solution.py:408
  37.6 0.6 %shard_map.99 = (bf16[384,256]{1,0:T(8,128)(2,1)S(1)}, bf16[384,256]{1,0:T(8,128)(2,1)S(1)}, bf16[384,256]{1,0:T(8,128)(2,1)S(1)}, bf16[384,256]{1,0:T(8,128)(2,1)S(1)}) custom-call(f32[384,128]{1,0:T(8,128)S(1)} %get-tuple-element.101.refs_0_, bf16[384,256]{1,0:T(8,128)(2,1)S(1)} %get-tuple-element.81.refs_0_.refs_1_, ...), custom_call_target="tpu_custom_call" | custom-call | bytes 4128768 | tf_op jit(solution)/shard_map/pallas_call | solution.py:46
  38.3 3.1 %collective-permute-start.12 = (bf16[384,256]{1,0:T(8,128)(2,1)S(1)}, bf16[384,256]{1,0:T(8,128)(2,1)S(1)}, u32[]{:S(2)}, u32[]{:S(2)}) collective-permute-start(bf16[384,256]{1,0:T(8,128)(2,1)S(1)} %get-tuple-element.116), channel_id=1, source_target_pairs={{0,1},{1,0},{2,3},{3,2},{4,5},{5,4},{6,7},{7,6},{8,9},{9,8},{10,11... | collective-permute-start | bytes 589832 | tf_op jit(solution)/shard_map/ppermute | solution.py:403
  41.4 1.1 %collective-permute-start.13 = (bf16[384,256]{1,0:T(8,128)(2,1)S(1)}, bf16[384,256]{1,0:T(8,128)(2,1)S(1)}, u32[]{:S(2)}, u32[]{:S(2)}) collective-permute-start(bf16[384,256]{1,0:T(8,128)(2,1)S(1)} %get-tuple-element.117), channel_id=1, source_target_pairs={{0,2},{1,3},{2,0},{3,1},{4,6},{5,7},{6,4},{7,5},{8,10},{9,11},{10,... | collective-permute-start | bytes 589832 | tf_op jit(solution)/shard_map/ppermute | solution.py:403
  42.5 1.3 %collective-permute-start.14 = (bf16[384,256]{1,0:T(8,128)(2,1)S(1)}, bf16[384,256]{1,0:T(8,128)(2,1)S(1)}, u32[]{:S(2)}, u32[]{:S(2)}) collective-permute-start(bf16[384,256]{1,0:T(8,128)(2,1)S(1)} %get-tuple-element.118), channel_id=1, source_target_pairs={{0,3},{1,2},{2,1},{3,0},{4,7},{5,6},{6,5},{7,4},{8,11},{9,10},{10,... | collective-permute-start | bytes 589832 | tf_op jit(solution)/shard_map/ppermute | solution.py:403
  43.8 1.4 %shard_map.101 = (f32[384,1024]{1,0:T(8,128)S(1)}, f32[384,1024]{1,0:T(8,128)S(1)}) custom-call(bf16[768,384]{1,0:T(8,128)(2,1)S(1)} %get-tuple-element.121.refs_8_.own_weight_ref, bf16[768,768]{1,0:T(8,128)(2,1)S(1)} %get-tuple-element.122.near_weight_ref, bf16[768,1024]{1,0:T(8,128)(2,1)S(1)} %get-tuple-element.96.refs_6_.unit_ref, ...), custom_call_target="tpu_custom_call" | custom-call | flops 20000000000 | bytes 7274496 | tf_op jit(solution)/shard_map/pallas_call | solution.py:46
  45.3 3.4 %collective-permute-done.16.in_ref = bf16[384,1024]{1,0:T(8,128)(2,1)S(1)} collective-permute-done((bf16[384,1024]{1,0:T(8,128)(2,1)S(1)}, bf16[384,1024]{1,0:T(8,128)(2,1)S(1)}, u32[]{:S(2)}, u32[]{:S(2)}) %collective-permute-start.16) | collective-permute-done | bytes 786464 | tf_op jit(solution)/shard_map/ppermute | solution.py:408
  48.7 0.1 shard_map.102
  48.9 0.9 %collective-permute-start.17 = (bf16[192,1024]{1,0:T(8,128)(2,1)S(1)}, bf16[192,1024]{1,0:T(8,128)(2,1)S(1)}, u32[]{:S(2)}, u32[]{:S(2)}) collective-permute-start(bf16[192,1024]{1,0:T(8,128)(2,1)S(1)} %get-tuple-element.128), channel_id=1, source_target_pairs={{0,16},{4,12},{8,24},{12,4},{16,0},{20,28},{24,8},{28,20},{1,17},{... | collective-permute-start | bytes 1179656 | tf_op jit(solution)/shard_map/ppermute | solution.py:408
  49.8 1.2 %collective-permute-start.18 = (bf16[192,1024]{1,0:T(8,128)(2,1)S(1)}, bf16[192,1024]{1,0:T(8,128)(2,1)S(1)}, u32[]{:S(2)}, u32[]{:S(2)}) collective-permute-start(bf16[192,1024]{1,0:T(8,128)(2,1)S(1)} %get-tuple-element.129), channel_id=1, source_target_pairs={{0,16},{4,12},{8,24},{12,4},{16,0},{20,28},{24,8},{28,20},{1,17},{... | collective-permute-start | bytes 1179656 | tf_op jit(solution)/shard_map/ppermute | solution.py:408
  51.0 7.5 %collective-permute-done.13.refs_2_ = bf16[384,256]{1,0:T(8,128)(2,1)S(1)} collective-permute-done((bf16[384,256]{1,0:T(8,128)(2,1)S(1)}, bf16[384,256]{1,0:T(8,128)(2,1)S(1)}, u32[]{:S(2)}, u32[]{:S(2)}) %collective-permute-start.13) | collective-permute-done | bytes 196640 | tf_op jit(solution)/shard_map/ppermute | solution.py:403
  58.5 0.9 %shard_map.100 = bf16[1536,256]{1,0:T(8,128)(2,1)} custom-call(bf16[384,256]{1,0:T(8,128)(2,1)S(1)} %get-tuple-element.115.refs_0_, bf16[384,256]{1,0:T(8,128)(2,1)S(1)} %collective-permute-done.12.refs_1_, bf16[384,256]{1,0:T(8,128)(2,1)S(1)} %collective-permute-done.13.refs_2_, bf16[384,256]{1,0:T(8,128)(2,1)S(1)} %collective-permute-done.14.refs_3_), custom_call_target="tpu_custom_call" | custom-call | flops 20000000000 | bytes 1572864 | tf_op jit(solution)/shard_map/pallas_call | solution.py:46
  59.4 1.5 %collective-permute-done.18.refs_1_ = bf16[192,1024]{1,0:T(8,128)(2,1)S(1)} collective-permute-done((bf16[192,1024]{1,0:T(8,128)(2,1)S(1)}, bf16[192,1024]{1,0:T(8,128)(2,1)S(1)}, u32[]{:S(2)}, u32[]{:S(2)}) %collective-permute-start.18) | collective-permute-done | bytes 393248 | tf_op jit(solution)/shard_map/ppermute | solution.py:408
  60.9 1.4 %shard_map.103 = bf16[384,1024]{1,0:T(8,128)(2,1)} custom-call(bf16[384,1024]{1,0:T(8,128)(2,1)S(1)} %get-tuple-element.119.raw_ref, f32[384,128]{1,0:T(8,128)S(1)} %get-tuple-element.120.scale_ref, f32[384,1024]{1,0:T(8,128)S(1)} %get-tuple-element.125.sum_ref, bf16[192,1024]{1,0:T(8,128)(2,1)S(1)} %collective-permute-done.17.refs_0_, ...), custom_call_target="tpu_custom_call" | custom-call | bytes 4128768 | tf_op jit(solution)/shard_map/pallas_call | solution.py:46
  (16 shorter events, 0.0 us)
Async XLA Ops:
  0.6 14.8 %collective-permute-start = (bf16[384,1024]{1,0:T(8,128)(2,1)}, bf16[384,1024]{1,0:T(8,128)(2,1)S(1)}, u32[]{:S(2)}, u32[]{:S(2)}) collective-permute-start(bf16[384,1024]{1,0:T(8,128)(2,1)} %raw_ref.1), channel_id=1, source_target_pairs={{0,16},{4,12},{8,24},{12,4},{16,0},{20,28},{24,8},{28,20},{1,17},{... | collective-permute-start | bytes 2359304 | tf_op jit(solution)/shard_map/ppermute | solution.py:408
  3.7 1.1 %copy-start = (bf16[1536,256]{1,0:T(8,128)(2,1)S(1)}, bf16[1536,256]{1,0:T(8,128)(2,1)}, u32[]{:S(2)}) copy-start(bf16[1536,256]{1,0:T(8,128)(2,1)} %text_ref.1) | copy-start | bytes 2359300
  4.8 8.8 %copy-start.1 = (s32[12288]{0:T(1024)S(1)}, s32[12288]{0:T(1024)}, u32[]{:S(2)}) copy-start(s32[12288]{0:T(1024)} %param.11) | copy-start | bytes 147460
  4.8 8.8 %copy-start.2 = (s32[12288]{0:T(1024)S(1)}, s32[12288]{0:T(1024)}, u32[]{:S(2)}) copy-start(s32[12288]{0:T(1024)} %param.12) | copy-start | bytes 147460
  4.8 8.8 %copy-start.3 = (s32[96,8,3]{0,1,2:T(8,128)S(1)}, s32[96,8,3]{0,1,2:T(8,128)}, u32[]{:S(2)}) copy-start(s32[96,8,3]{0,1,2:T(8,128)} %param.13) | copy-start | bytes 27652
  4.9 17.0 %collective-permute-start.2 = (bf16[384,256]{1,0:T(8,128)(2,1)S(1)}, bf16[384,256]{1,0:T(8,128)(2,1)S(1)}, u32[]{:S(2)}, u32[]{:S(2)}) collective-permute-start(bf16[384,256]{1,0:T(8,128)(2,1)S(1)} %get-tuple-element.82), channel_id=1, source_target_pairs={{0,1},{1,0},{2,3},{3,2},{4,5},{5,4},{6,7},{7,6},{8,9},{9,8},{10,11... | collective-permute-start | bytes 589832 | tf_op jit(solution)/shard_map/ppermute | solution.py:403
  6.5 17.2 %collective-permute-start.3 = (bf16[384,256]{1,0:T(8,128)(2,1)S(1)}, bf16[384,256]{1,0:T(8,128)(2,1)S(1)}, u32[]{:S(2)}, u32[]{:S(2)}) collective-permute-start(bf16[384,256]{1,0:T(8,128)(2,1)S(1)} %get-tuple-element.83), channel_id=1, source_target_pairs={{0,2},{1,3},{2,0},{3,1},{4,6},{5,7},{6,4},{7,5},{8,10},{9,11},{10,... | collective-permute-start | bytes 589832 | tf_op jit(solution)/shard_map/ppermute | solution.py:403
  9.1 12.7 %collective-permute-start.4 = (bf16[384,256]{1,0:T(8,128)(2,1)S(1)}, bf16[384,256]{1,0:T(8,128)(2,1)S(1)}, u32[]{:S(2)}, u32[]{:S(2)}) collective-permute-start(bf16[384,256]{1,0:T(8,128)(2,1)S(1)} %get-tuple-element.84), channel_id=1, source_target_pairs={{0,3},{1,2},{2,1},{3,0},{4,7},{5,6},{6,5},{7,4},{8,11},{9,10},{10,... | collective-permute-start | bytes 589832 | tf_op jit(solution)/shard_map/ppermute | solution.py:403
  10.7 14.0 %collective-permute-start.1 = (bf16[384,1024]{1,0:T(8,128)(2,1)}, bf16[384,1024]{1,0:T(8,128)(2,1)S(1)}, u32[]{:S(2)}, u32[]{:S(2)}) collective-permute-start(bf16[384,1024]{1,0:T(8,128)(2,1)} %raw_ref.1), channel_id=1, source_target_pairs={{0,8},{4,20},{8,0},{12,28},{16,24},{20,4},{24,16},{28,12},{1,9},{5... | collective-permute-start | bytes 2359304 | tf_op jit(solution)/shard_map/ppermute | solution.py:408
  15.4 16.2 %collective-permute-start.8 = (bf16[384,1024]{1,0:T(8,128)(2,1)S(1)}, bf16[384,1024]{1,0:T(8,128)(2,1)S(1)}, u32[]{:S(2)}, u32[]{:S(2)}) collective-permute-start(bf16[384,1024]{1,0:T(8,128)(2,1)S(1)} %collective-permute-done.raw_ref), channel_id=1, source_target_pairs={{0,8},{4,20},{8,0},{12,28},{16,24},{20,4},{24,16},{28,12},{1,9},{5... | collective-permute-start | bytes 2359304 | tf_op jit(solution)/shard_map/ppermute | solution.py:408
  24.1 2.7 %collective-permute-start.5 = (bf16[128,1024]{1,0:T(8,128)(2,1)S(1)}, bf16[128,1024]{1,0:T(8,128)(2,1)S(1)}, u32[]{:S(2)}, u32[]{:S(2)}) collective-permute-start(bf16[128,1024]{1,0:T(8,128)(2,1)S(1)} %get-tuple-element.93), channel_id=1, source_target_pairs={{0,4},{4,0},{8,12},{12,8},{16,20},{20,16},{24,28},{28,24},{1,5},{5... | collective-permute-start | bytes 786440 | tf_op jit(solution)/shard_map/ppermute | solution.py:403
  24.2 2.7 %collective-permute-start.6 = (bf16[128,1024]{1,0:T(8,128)(2,1)S(1)}, bf16[128,1024]{1,0:T(8,128)(2,1)S(1)}, u32[]{:S(2)}, u32[]{:S(2)}) collective-permute-start(bf16[128,1024]{1,0:T(8,128)(2,1)S(1)} %get-tuple-element.94), channel_id=1, source_target_pairs={{0,4},{4,0},{8,12},{12,8},{16,20},{20,16},{24,28},{28,24},{1,5},{5... | collective-permute-start | bytes 786440 | tf_op jit(solution)/shard_map/ppermute | solution.py:403
  24.6 2.2 %collective-permute-start.7 = (bf16[128,1024]{1,0:T(8,128)(2,1)S(1)}, bf16[128,1024]{1,0:T(8,128)(2,1)S(1)}, u32[]{:S(2)}, u32[]{:S(2)}) collective-permute-start(bf16[128,1024]{1,0:T(8,128)(2,1)S(1)} %get-tuple-element.95), channel_id=1, source_target_pairs={{0,4},{4,0},{8,12},{12,8},{16,20},{20,16},{24,28},{28,24},{1,5},{5... | collective-permute-start | bytes 786440 | tf_op jit(solution)/shard_map/ppermute | solution.py:403
  28.2 15.6 %collective-permute-start.15 = (bf16[384,1024]{1,0:T(8,128)(2,1)S(1)}, bf16[384,1024]{1,0:T(8,128)(2,1)S(1)}, u32[]{:S(2)}, u32[]{:S(2)}) collective-permute-start(bf16[384,1024]{1,0:T(8,128)(2,1)S(1)} %get-tuple-element.123), channel_id=1, source_target_pairs={{0,8},{4,20},{8,0},{12,28},{16,24},{20,4},{24,16},{28,12},{1,9},{5... | collective-permute-start | bytes 2359304 | tf_op jit(solution)/shard_map/ppermute | solution.py:408
  34.0 3.6 %collective-permute-start.9 = (bf16[128,1024]{1,0:T(8,128)(2,1)S(1)}, bf16[128,1024]{1,0:T(8,128)(2,1)S(1)}, u32[]{:S(2)}, u32[]{:S(2)}) collective-permute-start(bf16[128,1024]{1,0:T(8,128)(2,1)S(1)} %get-tuple-element.111), channel_id=1, source_target_pairs={{0,4},{4,0},{8,12},{12,8},{16,20},{20,16},{24,28},{28,24},{1,5},{5... | collective-permute-start | bytes 786440 | tf_op jit(solution)/shard_map/ppermute | solution.py:403
  34.1 3.5 %collective-permute-start.10 = (bf16[128,1024]{1,0:T(8,128)(2,1)S(1)}, bf16[128,1024]{1,0:T(8,128)(2,1)S(1)}, u32[]{:S(2)}, u32[]{:S(2)}) collective-permute-start(bf16[128,1024]{1,0:T(8,128)(2,1)S(1)} %get-tuple-element.112), channel_id=1, source_target_pairs={{0,4},{4,0},{8,12},{12,8},{16,20},{20,16},{24,28},{28,24},{1,5},{5... | collective-permute-start | bytes 786440 | tf_op jit(solution)/shard_map/ppermute | solution.py:403
  34.6 3.0 %collective-permute-start.11 = (bf16[128,1024]{1,0:T(8,128)(2,1)S(1)}, bf16[128,1024]{1,0:T(8,128)(2,1)S(1)}, u32[]{:S(2)}, u32[]{:S(2)}) collective-permute-start(bf16[128,1024]{1,0:T(8,128)(2,1)S(1)} %get-tuple-element.113), channel_id=1, source_target_pairs={{0,4},{4,0},{8,12},{12,8},{16,20},{20,16},{24,28},{28,24},{1,5},{5... | collective-permute-start | bytes 786440 | tf_op jit(solution)/shard_map/ppermute | solution.py:403
  36.3 12.4 %collective-permute-start.16 = (bf16[384,1024]{1,0:T(8,128)(2,1)S(1)}, bf16[384,1024]{1,0:T(8,128)(2,1)S(1)}, u32[]{:S(2)}, u32[]{:S(2)}) collective-permute-start(bf16[384,1024]{1,0:T(8,128)(2,1)S(1)} %shard_map.98), channel_id=1, source_target_pairs={{0,8},{4,20},{8,0},{12,28},{16,24},{20,4},{24,16},{28,12},{1,9},{5... | collective-permute-start | bytes 2359304 | tf_op jit(solution)/shard_map/ppermute | solution.py:408
  38.3 12.7 %collective-permute-start.12 = (bf16[384,256]{1,0:T(8,128)(2,1)S(1)}, bf16[384,256]{1,0:T(8,128)(2,1)S(1)}, u32[]{:S(2)}, u32[]{:S(2)}) collective-permute-start(bf16[384,256]{1,0:T(8,128)(2,1)S(1)} %get-tuple-element.116), channel_id=1, source_target_pairs={{0,1},{1,0},{2,3},{3,2},{4,5},{5,4},{6,7},{7,6},{8,9},{9,8},{10,11... | collective-permute-start | bytes 589832 | tf_op jit(solution)/shard_map/ppermute | solution.py:403
  41.4 17.1 %collective-permute-start.13 = (bf16[384,256]{1,0:T(8,128)(2,1)S(1)}, bf16[384,256]{1,0:T(8,128)(2,1)S(1)}, u32[]{:S(2)}, u32[]{:S(2)}) collective-permute-start(bf16[384,256]{1,0:T(8,128)(2,1)S(1)} %get-tuple-element.117), channel_id=1, source_target_pairs={{0,2},{1,3},{2,0},{3,1},{4,6},{5,7},{6,4},{7,5},{8,10},{9,11},{10,... | collective-permute-start | bytes 589832 | tf_op jit(solution)/shard_map/ppermute | solution.py:403
  42.5 16.0 %collective-permute-start.14 = (bf16[384,256]{1,0:T(8,128)(2,1)S(1)}, bf16[384,256]{1,0:T(8,128)(2,1)S(1)}, u32[]{:S(2)}, u32[]{:S(2)}) collective-permute-start(bf16[384,256]{1,0:T(8,128)(2,1)S(1)} %get-tuple-element.118), channel_id=1, source_target_pairs={{0,3},{1,2},{2,1},{3,0},{4,7},{5,6},{6,5},{7,4},{8,11},{9,10},{10,... | collective-permute-start | bytes 589832 | tf_op jit(solution)/shard_map/ppermute | solution.py:403
  48.9 10.5 %collective-permute-start.17 = (bf16[192,1024]{1,0:T(8,128)(2,1)S(1)}, bf16[192,1024]{1,0:T(8,128)(2,1)S(1)}, u32[]{:S(2)}, u32[]{:S(2)}) collective-permute-start(bf16[192,1024]{1,0:T(8,128)(2,1)S(1)} %get-tuple-element.128), channel_id=1, source_target_pairs={{0,16},{4,12},{8,24},{12,4},{16,0},{20,28},{24,8},{28,20},{1,17},{... | collective-permute-start | bytes 1179656 | tf_op jit(solution)/shard_map/ppermute | solution.py:408
  49.8 11.2 %collective-permute-start.18 = (bf16[192,1024]{1,0:T(8,128)(2,1)S(1)}, bf16[192,1024]{1,0:T(8,128)(2,1)S(1)}, u32[]{:S(2)}, u32[]{:S(2)}) collective-permute-start(bf16[192,1024]{1,0:T(8,128)(2,1)S(1)} %get-tuple-element.129), channel_id=1, source_target_pairs={{0,16},{4,12},{8,24},{12,4},{16,0},{20,28},{24,8},{28,20},{1,17},{... | collective-permute-start | bytes 1179656 | tf_op jit(solution)/shard_map/ppermute | solution.py:408

commit v5 on v4

--- a/solution.py
+++ b/solution.py
@@ -79,15 +79,20 @@
     )
 
 
-def feature_slice(place, k, width):
-    return pl.ds(pl.multiple_of((place ^ k) * width, width), width)
+def peer_bits(k, chunks):
+    return (chunks - k) % chunks
+
+
+def feature_slice(peer, width):
+    return pl.ds(pl.multiple_of(peer * width, width), width)
 
 
 def pick_body(text_ref, *out_refs):
     place = lax.axis_index("tp")
     rows = out_refs[0].shape[0]
     for k, out_ref in enumerate(out_refs):
-        out_ref[...] = text_ref[pl.ds(pl.multiple_of((place ^ k) * rows, rows), rows), :]
+        peer = place ^ peer_bits(k, len(out_refs))
+        out_ref[...] = text_ref[pl.ds(pl.multiple_of(peer * rows, rows), rows), :]
 
 
 def unit_text_body(chunks, *refs):
@@ -101,7 +106,7 @@
         scales = row_scales(sum(jnp.sum(x * x, axis=-1, keepdims=True) for x in parts))
         scale_ref[part, :] = jnp.broadcast_to(scales, (TILE, TILE))
         for k, x in enumerate(parts):
-            unit_ref[part, feature_slice(place, k, width)] = (x * scales).astype(jnp.bfloat16)
+            unit_ref[part, feature_slice(place ^ peer_bits(k, chunks), width)] = (x * scales).astype(jnp.bfloat16)
     split_rows(unit_ref, piece_refs)
 
 
@@ -351,7 +356,7 @@
         raws = [ref[part, :].astype(jnp.float32) for ref in raw_refs]
         accs = []
         for k in range(chunks):
-            features = feature_slice(place, k, width)
+            features = feature_slice(place ^ peer_bits(k, chunks), width)
             added = add_refs[first // size][pl.ds(first % size, TILE // 2), features]
             accs.append(acc_ref[part, features] + added.astype(jnp.float32))
         inner = sum(jnp.sum(x * a, axis=-1, keepdims=True) for x, a in zip(raws, accs))
@@ -366,7 +371,8 @@
     rows = part_refs[0].shape[0]
     copies = []
     for k in range(chunks):
-        block = pl.ds(pl.multiple_of((place ^ k) * rows, rows), rows)
+        peer = place ^ peer_bits(k, chunks)
+        block = pl.ds(pl.multiple_of(peer * rows, rows), rows)
         copies.append(pltpu.make_async_copy(part_refs[k], out_ref.at[block, :], sems.at[k]))
     for copy in copies:
         copy.start()
@@ -408,6 +414,11 @@
     return lax.ppermute(value, "blk", [(i, i ^ neighbour_bits(i)[which]) for i in range(count)])
 
 
+def swap_chunks(chunks):
+    count = len(chunks)
+    return chunks[:1] + [swap(chunks[k], "tp", peer_bits(k, count)) for k in range(1, count)]
+
+
 def per_device(text_emb, image_emb, logit_scale, logit_bias, bucket, positive, blocks):
     groups = lax.axis_size("tp")
     shards = lax.axis_size("blk")
@@ -427,7 +438,7 @@
         return struct((count, columns), jnp.int32)
 
     picked = call_kernel(pick_body, [bf16(rows, width)] * groups, [text_emb], limit=8)
-    text_raw = [picked[0]] + [swap(picked[k], "tp", k) for k in range(1, groups)]
+    text_raw = swap_chunks(picked)
     if square:
         from_second = swap_near(image_emb, 1)
     else:
@@ -493,8 +504,7 @@
             [text_scales] + text_raw + [acc_own] + [swap(piece, "blk", 1) for piece in acc_other],
             limit=16,
         )
-        sent = [swap(parts[k], "tp", k) for k in reversed(range(1, groups))]
-        return [parts[0]] + sent[::-1]
+        return swap_chunks(parts)
 
     def place_text(text_parts):
         return call_kernel(

time: 62.9 us -> 64.1 us (1.019)
  waiting for transfers between devices: 17.9 us -> 20.6 us
  starting transfers between devices: 23.6 us -> 22.4 us
    ppermute x7, waiting for transfers between devices: 5.66 us -> 8.84 us  [swap_near(): lax.ppermute(value, 'blk', [(i, i ^ neighbour_bits(i)[which]) for i in ra...]
    ppermute x7, starting transfers between devices: 12.3 us -> 11.2 us  [swap_near(): lax.ppermute(value, 'blk', [(i, i ^ neighbour_bits(i)[which]) for i in ra...]
  transfers between devices with their start and end apart: 19 -> 19, of which waited for: 6 -> 6; matrix products, arithmetic and copies ran while one was open for 0% -> 0% of each run, Pallas kernels for 26% -> 25%
where the time goes in v5:
time: 64.1 us; the launch traced here: 63.9 us
  starting transfers between devices  22.4 us (35%)
  waiting for transfers between devices  20.6 us (32%)
  Pallas kernels  17.5 us (27%)
  between operations  2.12 us (3%)
  local copies, waits for them, and re-layouts  1.14 us (2%)
    pallas_call x18, Pallas kernels, call_kernel(): pl.pallas_call(body, out_shape=outs, in_specs=specs, out_specs=[ANY_SPEC...  17.5 us
    ppermute x12, waiting for transfers between devices, swap(): return lax.ppermute(value, axis, [(i, i ^ bits) for i in range(count)])  11.8 us
    ppermute x12, starting transfers between devices, swap(): return lax.ppermute(value, axis, [(i, i ^ bits) for i in range(count)])  11.3 us
    ppermute x7, starting transfers between devices, swap_near(): lax.ppermute(value, 'blk', [(i, i ^ neighbour_bits(i)[which]) for i in ra...  11.2 us
    ppermute x7, waiting for transfers between devices, swap_near(): lax.ppermute(value, 'blk', [(i, i ^ neighbour_bits(i)[which]) for i in ra...  8.84 us
  transfers between devices with their start and end apart: 19, of which 6 were waited for; matrix products, arithmetic and copies ran while one was open for 0% of the time, Pallas kernels for 25%

profile of v5, /device:TPU:0, one launch (start us, length us, event | category | flops | bytes accessed | tf_op | source)
XLA Modules:
  0.0 63.9 jit_solution(17014726451427458314)
XLA Ops:
  0.6 3.0 %collective-permute-start = (bf16[384,1024]{1,0:T(8,128)(2,1)}, bf16[384,1024]{1,0:T(8,128)(2,1)S(1)}, u32[]{:S(2)}, u32[]{:S(2)}) collective-permute-start(bf16[384,1024]{1,0:T(8,128)(2,1)} %raw_ref.1), channel_id=1, source_target_pairs={{0,16},{4,12},{8,24},{12,4},{16,0},{20,28},{24,8},{28,20},{1,17},{... | collective-permute-start | bytes 2359304 | tf_op jit(solution)/shard_map/ppermute | solution.py:414
  3.7 1.1 %copy-done = bf16[1536,256]{1,0:T(8,128)(2,1)S(1)} copy-done((bf16[1536,256]{1,0:T(8,128)(2,1)S(1)}, bf16[1536,256]{1,0:T(8,128)(2,1)}, u32[]{:S(2)}) %copy-start) | copy-done | bytes 786456
  4.8 0.1 shard_map.88
  4.9 3.7 %collective-permute-start.2 = (bf16[384,256]{1,0:T(8,128)(2,1)S(1)}, bf16[384,256]{1,0:T(8,128)(2,1)S(1)}, u32[]{:S(2)}, u32[]{:S(2)}) collective-permute-start(bf16[384,256]{1,0:T(8,128)(2,1)S(1)} %get-tuple-element.82), channel_id=1, source_target_pairs={{0,3},{1,2},{2,1},{3,0},{4,7},{5,6},{6,5},{7,4},{8,11},{9,10},{10,... | collective-permute-start | bytes 589832 | tf_op jit(solution)/shard_map/ppermute | solution.py:409
  8.5 0.8 %collective-permute-start.4 = (bf16[384,256]{1,0:T(8,128)(2,1)S(1)}, bf16[384,256]{1,0:T(8,128)(2,1)S(1)}, u32[]{:S(2)}, u32[]{:S(2)}) collective-permute-start(bf16[384,256]{1,0:T(8,128)(2,1)S(1)} %get-tuple-element.84), channel_id=1, source_target_pairs={{0,1},{1,0},{2,3},{3,2},{4,5},{5,4},{6,7},{7,6},{8,9},{9,8},{10,11... | collective-permute-start | bytes 589832 | tf_op jit(solution)/shard_map/ppermute | solution.py:409
  9.3 1.4 %shard_map.86 = (bf16[384,1024]{1,0:T(8,128)(2,1)S(1)}, bf16[384,1024]{1,0:T(8,128)(2,1)S(1)}, f32[384,128]{1,0:T(8,128)S(1)}) custom-call(bf16[384,1024]{1,0:T(8,128)(2,1)} %raw_ref.1), custom_call_target="tpu_custom_call" | custom-call | bytes 2555904 | tf_op jit(solution)/shard_map/pallas_call | solution.py:46
  10.7 1.6 %collective-permute-start.1 = (bf16[384,1024]{1,0:T(8,128)(2,1)}, bf16[384,1024]{1,0:T(8,128)(2,1)S(1)}, u32[]{:S(2)}, u32[]{:S(2)}) collective-permute-start(bf16[384,1024]{1,0:T(8,128)(2,1)} %raw_ref.1), channel_id=1, source_target_pairs={{0,8},{4,20},{8,0},{12,28},{16,24},{20,4},{24,16},{28,12},{1,9},{5... | collective-permute-start | bytes 2359304 | tf_op jit(solution)/shard_map/ppermute | solution.py:414
  13.6 1.1 %shard_map.87 = (f32[2,128]{1,0:T(2,128)S(1)}, f32[72,128]{1,0:T(8,128)S(1)}, s32[12,128]{1,0:T(8,128)S(1)}, s32[768,128]{1,0:T(8,128)S(1)}, f32[384,128]{1,0:T(8,128)S(1)}, /*index=5*/f32[4,128]{1,0:T(4,128)S(1)}) custom-call(f32[1]{0:T(128)S(6)} %copy.9.refs_0_, f32[1]{0:T(128)S(6)} %copy.10.refs_1_, s32[3,8,96]{2,1,0:T(8,128)S(1)} %bitcast.5, ...), custom_call_target="tpu_custom_call" | custom-call | bytes 743432 | tf_op jit(solution)/shard_map/pallas_call | solution.py:46
  14.7 0.6 collective-permute-done.raw_ref
  15.3 3.3 %collective-permute-start.8 = (bf16[384,1024]{1,0:T(8,128)(2,1)S(1)}, bf16[384,1024]{1,0:T(8,128)(2,1)S(1)}, u32[]{:S(2)}, u32[]{:S(2)}) collective-permute-start(bf16[384,1024]{1,0:T(8,128)(2,1)S(1)} %collective-permute-done.raw_ref), channel_id=1, source_target_pairs={{0,8},{4,20},{8,0},{12,28},{16,24},{20,4},{24,16},{28,12},{1,9},{5... | collective-permute-start | bytes 2359304 | tf_op jit(solution)/shard_map/ppermute | solution.py:414
  18.6 0.2 shard_map.89.second_unit_ref
  18.9 2.0 %collective-permute-done.4.refs_3_.refs_4_ = bf16[384,256]{1,0:T(8,128)(2,1)S(1)} collective-permute-done((bf16[384,256]{1,0:T(8,128)(2,1)S(1)}, bf16[384,256]{1,0:T(8,128)(2,1)S(1)}, u32[]{:S(2)}, u32[]{:S(2)}) %collective-permute-start.4) | collective-permute-done | bytes 196640 | tf_op jit(solution)/shard_map/ppermute | solution.py:409
  20.9 4.0 %collective-permute-done.3.refs_2_.refs_3_ = bf16[384,256]{1,0:T(8,128)(2,1)S(1)} collective-permute-done((bf16[384,256]{1,0:T(8,128)(2,1)S(1)}, bf16[384,256]{1,0:T(8,128)(2,1)S(1)}, u32[]{:S(2)}, u32[]{:S(2)}) %collective-permute-start.3) | collective-permute-done | bytes 196640 | tf_op jit(solution)/shard_map/ppermute | solution.py:409
  24.9 0.4 shard_map.90
  25.3 0.1 collective-permute-start.5
  25.4 0.5 collective-permute-start.6
  25.9 0.1 collective-permute-start.7
  26.0 0.0 collective-permute-done.1.first_ref
  26.0 0.3 shard_map.91.refs_8_.refs_7_
  26.3 1.8 %shard_map.92 = (bf16[384,384]{1,0:T(8,128)(2,1)S(1)}, bf16[384,768]{1,0:T(8,128)(2,1)S(1)}) custom-call(f32[2,128]{1,0:T(2,128)S(1)} %get-tuple-element.74.refs_0_, f32[72,128]{1,0:T(8,128)S(1)} %get-tuple-element.75.refs_1_, s32[12,128]{1,0:T(8,128)S(1)} %get-tuple-element.76.refs_2_, s32[768,128]{1,0:T(8,128)S(1)} %get-tuple-element.77.refs_3_, ...), custom_call_target="tpu_custom_call" | custom-call | bytes 4666368 | tf_op jit(solution)/shard_map/pallas_call | solution.py:46
  28.1 0.0 collective-permute-done.6.refs_10_
  28.1 0.0 collective-permute-done.7.refs_11_
  28.1 1.4 %shard_map.93 = (bf16[768,1024]{1,0:T(8,128)(2,1)S(1)}, bf16[768,384]{1,0:T(8,128)(2,1)S(1)}, bf16[384,1024]{1,0:T(8,128)(2,1)S(1)}) custom-call(f32[2,128]{1,0:T(2,128)S(1)} %get-tuple-element.74.refs_0_, f32[72,128]{1,0:T(8,128)S(1)} %get-tuple-element.75.refs_1_, s32[12,128]{1,0:T(8,128)S(1)} %get-tuple-element.76.refs_2_, ...), custom_call_target="tpu_custom_call" | custom-call | bytes 7320576 | tf_op jit(solution)/shard_map/pallas_call | solution.py:46
  29.5 0.6 collective-permute-start.15
  30.1 2.5 %shard_map.94 = (bf16[768,384]{1,0:T(8,128)(2,1)S(1)}, f32[768,1024]{1,0:T(8,128)S(1)}, bf16[768,768]{1,0:T(8,128)(2,1)S(1)}) custom-call(f32[2,128]{1,0:T(2,128)S(1)} %get-tuple-element.74.refs_0_, f32[72,128]{1,0:T(8,128)S(1)} %get-tuple-element.75.refs_1_, s32[12,128]{1,0:T(8,128)S(1)} %get-tuple-element.76.refs_2_, ...), custom_call_target="tpu_custom_call" | custom-call | bytes 10957824 | tf_op jit(solution)/shard_map/pallas_call | solution.py:46
  32.5 0.0 collective-permute-done.8.refs_9_
  32.6 1.6 %shard_map.95 = (bf16[768,768]{1,0:T(8,128)(2,1)S(1)}, bf16[768,1024]{1,0:T(8,128)(2,1)S(1)}) custom-call(f32[2,128]{1,0:T(2,128)S(1)} %get-tuple-element.74.refs_0_, f32[72,128]{1,0:T(8,128)S(1)} %get-tuple-element.75.refs_1_, s32[12,128]{1,0:T(8,128)S(1)} %get-tuple-element.76.refs_2_, s32[768,128]{1,0:T(8,128)S(1)} %get-tuple-element.77.refs_3_, ...), custom_call_target="tpu_custom_call" | custom-call | bytes 7123968 | tf_op jit(solution)/shard_map/pallas_call | solution.py:46
  34.1 0.8 %shard_map.96 = (bf16[128,1024]{1,0:T(8,128)(2,1)S(1)}, bf16[128,1024]{1,0:T(8,128)(2,1)S(1)}, bf16[128,1024]{1,0:T(8,128)(2,1)S(1)}) custom-call(bf16[768,768]{1,0:T(8,128)(2,1)S(1)} %get-tuple-element.109.weight_ref, bf16[768,1024]{1,0:T(8,128)(2,1)S(1)} %get-tuple-element.107.image_ref, f32[768,1024]{1,0:T(8,128)S(1)} %get-tuple-element.105.acc_ref), custom_call_target="tpu_custom_call" | custom-call | bytes 6684672 | tf_op jit(solution)/shard_map/pallas_call | solution.py:46
  34.9 1.2 %collective-permute-start.9 = (bf16[128,1024]{1,0:T(8,128)(2,1)S(1)}, bf16[128,1024]{1,0:T(8,128)(2,1)S(1)}, u32[]{:S(2)}, u32[]{:S(2)}) collective-permute-start(bf16[128,1024]{1,0:T(8,128)(2,1)S(1)} %get-tuple-element.111), channel_id=1, source_target_pairs={{0,4},{4,0},{8,12},{12,8},{16,20},{20,16},{24,28},{28,24},{1,5},{5... | collective-permute-start | bytes 786440 | tf_op jit(solution)/shard_map/ppermute | solution.py:409
  36.1 0.1 collective-permute-start.10
  36.2 0.4 collective-permute-start.11
  36.6 0.8 %shard_map.97.refs_5_ = f32[384,1024]{1,0:T(8,128)S(1)} custom-call(bf16[768,768]{1,0:T(8,128)(2,1)S(1)} %get-tuple-element.109.weight_ref, bf16[768,1024]{1,0:T(8,128)(2,1)S(1)} %get-tuple-element.107.image_ref, f32[768,1024]{1,0:T(8,128)S(1)} %get-tuple-element.105.acc_ref), custom_call_target="tpu_custom_call" | custom-call | bytes 7471104 | tf_op jit(solution)/shard_map/pallas_call | solution.py:46
  37.4 0.8 %shard_map.98 = bf16[384,1024]{1,0:T(8,128)(2,1)S(1)} custom-call(bf16[768,768]{1,0:T(8,128)(2,1)S(1)} %get-tuple-element.109.weight_ref, bf16[768,1024]{1,0:T(8,128)(2,1)S(1)} %get-tuple-element.96.refs_6_.unit_ref), custom_call_target="tpu_custom_call" | custom-call | bytes 3538944 | tf_op jit(solution)/shard_map/pallas_call | solution.py:46
  38.2 0.6 collective-permute-start.16
  38.8 0.0 collective-permute-done.10.refs_7_
  38.9 0.0 collective-permute-done.11.refs_8_
  38.9 0.6 shard_map.99
  39.5 2.5 %collective-permute-start.12 = (bf16[384,256]{1,0:T(8,128)(2,1)S(1)}, bf16[384,256]{1,0:T(8,128)(2,1)S(1)}, u32[]{:S(2)}, u32[]{:S(2)}) collective-permute-start(bf16[384,256]{1,0:T(8,128)(2,1)S(1)} %get-tuple-element.116), channel_id=1, source_target_pairs={{0,3},{1,2},{2,1},{3,0},{4,7},{5,6},{6,5},{7,4},{8,11},{9,10},{10,... | collective-permute-start | bytes 589832 | tf_op jit(solution)/shard_map/ppermute | solution.py:409
  42.0 1.9 %collective-permute-start.14 = (bf16[384,256]{1,0:T(8,128)(2,1)S(1)}, bf16[384,256]{1,0:T(8,128)(2,1)S(1)}, u32[]{:S(2)}, u32[]{:S(2)}) collective-permute-start(bf16[384,256]{1,0:T(8,128)(2,1)S(1)} %get-tuple-element.118), channel_id=1, source_target_pairs={{0,1},{1,0},{2,3},{3,2},{4,5},{5,4},{6,7},{7,6},{8,9},{9,8},{10,11... | collective-permute-start | bytes 589832 | tf_op jit(solution)/shard_map/ppermute | solution.py:409
  44.0 1.4 %shard_map.101 = (f32[384,1024]{1,0:T(8,128)S(1)}, f32[384,1024]{1,0:T(8,128)S(1)}) custom-call(bf16[768,384]{1,0:T(8,128)(2,1)S(1)} %get-tuple-element.121.refs_8_.own_weight_ref, bf16[768,768]{1,0:T(8,128)(2,1)S(1)} %get-tuple-element.122.near_weight_ref, bf16[768,1024]{1,0:T(8,128)(2,1)S(1)} %get-tuple-element.96.refs_6_.unit_ref, ...), custom_call_target="tpu_custom_call" | custom-call | flops 20000000000 | bytes 7274496 | tf_op jit(solution)/shard_map/pallas_call | solution.py:46
  45.4 4.9 %collective-permute-done.16.in_ref = bf16[384,1024]{1,0:T(8,128)(2,1)S(1)} collective-permute-done((bf16[384,1024]{1,0:T(8,128)(2,1)S(1)}, bf16[384,1024]{1,0:T(8,128)(2,1)S(1)}, u32[]{:S(2)}, u32[]{:S(2)}) %collective-permute-start.16) | collective-permute-done | bytes 786464 | tf_op jit(solution)/shard_map/ppermute | solution.py:414
  50.3 0.1 shard_map.102
  50.4 1.3 %collective-permute-start.17 = (bf16[192,1024]{1,0:T(8,128)(2,1)S(1)}, bf16[192,1024]{1,0:T(8,128)(2,1)S(1)}, u32[]{:S(2)}, u32[]{:S(2)}) collective-permute-start(bf16[192,1024]{1,0:T(8,128)(2,1)S(1)} %get-tuple-element.128), channel_id=1, source_target_pairs={{0,16},{4,12},{8,24},{12,4},{16,0},{20,28},{24,8},{28,20},{1,17},{... | collective-permute-start | bytes 1179656 | tf_op jit(solution)/shard_map/ppermute | solution.py:414
  51.7 0.8 %collective-permute-start.18 = (bf16[192,1024]{1,0:T(8,128)(2,1)S(1)}, bf16[192,1024]{1,0:T(8,128)(2,1)S(1)}, u32[]{:S(2)}, u32[]{:S(2)}) collective-permute-start(bf16[192,1024]{1,0:T(8,128)(2,1)S(1)} %get-tuple-element.129), channel_id=1, source_target_pairs={{0,16},{4,12},{8,24},{12,4},{16,0},{20,28},{24,8},{28,20},{1,17},{... | collective-permute-start | bytes 1179656 | tf_op jit(solution)/shard_map/ppermute | solution.py:414
  52.5 5.7 %collective-permute-done.13.refs_2_ = bf16[384,256]{1,0:T(8,128)(2,1)S(1)} collective-permute-done((bf16[384,256]{1,0:T(8,128)(2,1)S(1)}, bf16[384,256]{1,0:T(8,128)(2,1)S(1)}, u32[]{:S(2)}, u32[]{:S(2)}) %collective-permute-start.13) | collective-permute-done | bytes 196640 | tf_op jit(solution)/shard_map/ppermute | solution.py:409
  58.3 0.9 %shard_map.100 = bf16[1536,256]{1,0:T(8,128)(2,1)} custom-call(bf16[384,256]{1,0:T(8,128)(2,1)S(1)} %get-tuple-element.115.refs_0_, bf16[384,256]{1,0:T(8,128)(2,1)S(1)} %collective-permute-done.12.refs_1_, bf16[384,256]{1,0:T(8,128)(2,1)S(1)} %collective-permute-done.13.refs_2_, bf16[384,256]{1,0:T(8,128)(2,1)S(1)} %collective-permute-done.14.refs_3_), custom_call_target="tpu_custom_call" | custom-call | flops 20000000000 | bytes 1572864 | tf_op jit(solution)/shard_map/pallas_call | solution.py:46
  59.2 3.3 %collective-permute-done.18.refs_1_ = bf16[192,1024]{1,0:T(8,128)(2,1)S(1)} collective-permute-done((bf16[192,1024]{1,0:T(8,128)(2,1)S(1)}, bf16[192,1024]{1,0:T(8,128)(2,1)S(1)}, u32[]{:S(2)}, u32[]{:S(2)}) %collective-permute-start.18) | collective-permute-done | bytes 393248 | tf_op jit(solution)/shard_map/ppermute | solution.py:414
  62.5 1.4 %shard_map.103 = bf16[384,1024]{1,0:T(8,128)(2,1)} custom-call(bf16[384,1024]{1,0:T(8,128)(2,1)S(1)} %get-tuple-element.119.raw_ref, f32[384,128]{1,0:T(8,128)S(1)} %get-tuple-element.120.scale_ref, f32[384,1024]{1,0:T(8,128)S(1)} %get-tuple-element.125.sum_ref, bf16[192,1024]{1,0:T(8,128)(2,1)S(1)} %collective-permute-done.17.refs_0_, ...), custom_call_target="tpu_custom_call" | custom-call | bytes 4128768 | tf_op jit(solution)/shard_map/pallas_call | solution.py:46
  (16 shorter events, 0.0 us)
Async XLA Ops:
  0.6 14.7 %collective-permute-start = (bf16[384,1024]{1,0:T(8,128)(2,1)}, bf16[384,1024]{1,0:T(8,128)(2,1)S(1)}, u32[]{:S(2)}, u32[]{:S(2)}) collective-permute-start(bf16[384,1024]{1,0:T(8,128)(2,1)} %raw_ref.1), channel_id=1, source_target_pairs={{0,16},{4,12},{8,24},{12,4},{16,0},{20,28},{24,8},{28,20},{1,17},{... | collective-permute-start | bytes 2359304 | tf_op jit(solution)/shard_map/ppermute | solution.py:414
  3.7 1.1 %copy-start = (bf16[1536,256]{1,0:T(8,128)(2,1)S(1)}, bf16[1536,256]{1,0:T(8,128)(2,1)}, u32[]{:S(2)}) copy-start(bf16[1536,256]{1,0:T(8,128)(2,1)} %text_ref.1) | copy-start | bytes 2359300
  4.8 8.8 %copy-start.1 = (s32[12288]{0:T(1024)S(1)}, s32[12288]{0:T(1024)}, u32[]{:S(2)}) copy-start(s32[12288]{0:T(1024)} %param.11) | copy-start | bytes 147460
  4.8 8.8 %copy-start.2 = (s32[12288]{0:T(1024)S(1)}, s32[12288]{0:T(1024)}, u32[]{:S(2)}) copy-start(s32[12288]{0:T(1024)} %param.12) | copy-start | bytes 147460
  4.8 8.8 %copy-start.3 = (s32[96,8,3]{0,1,2:T(8,128)S(1)}, s32[96,8,3]{0,1,2:T(8,128)}, u32[]{:S(2)}) copy-start(s32[96,8,3]{0,1,2:T(8,128)} %param.13) | copy-start | bytes 27652
  4.9 16.0 %collective-permute-start.2 = (bf16[384,256]{1,0:T(8,128)(2,1)S(1)}, bf16[384,256]{1,0:T(8,128)(2,1)S(1)}, u32[]{:S(2)}, u32[]{:S(2)}) collective-permute-start(bf16[384,256]{1,0:T(8,128)(2,1)S(1)} %get-tuple-element.82), channel_id=1, source_target_pairs={{0,3},{1,2},{2,1},{3,0},{4,7},{5,6},{6,5},{7,4},{8,11},{9,10},{10,... | collective-permute-start | bytes 589832 | tf_op jit(solution)/shard_map/ppermute | solution.py:409
  8.5 16.4 %collective-permute-start.3 = (bf16[384,256]{1,0:T(8,128)(2,1)S(1)}, bf16[384,256]{1,0:T(8,128)(2,1)S(1)}, u32[]{:S(2)}, u32[]{:S(2)}) collective-permute-start(bf16[384,256]{1,0:T(8,128)(2,1)S(1)} %get-tuple-element.83), channel_id=1, source_target_pairs={{0,2},{1,3},{2,0},{3,1},{4,6},{5,7},{6,4},{7,5},{8,10},{9,11},{10,... | collective-permute-start | bytes 589832 | tf_op jit(solution)/shard_map/ppermute | solution.py:409
  8.5 12.4 %collective-permute-start.4 = (bf16[384,256]{1,0:T(8,128)(2,1)S(1)}, bf16[384,256]{1,0:T(8,128)(2,1)S(1)}, u32[]{:S(2)}, u32[]{:S(2)}) collective-permute-start(bf16[384,256]{1,0:T(8,128)(2,1)S(1)} %get-tuple-element.84), channel_id=1, source_target_pairs={{0,1},{1,0},{2,3},{3,2},{4,5},{5,4},{6,7},{7,6},{8,9},{9,8},{10,11... | collective-permute-start | bytes 589832 | tf_op jit(solution)/shard_map/ppermute | solution.py:409
  10.7 15.2 %collective-permute-start.1 = (bf16[384,1024]{1,0:T(8,128)(2,1)}, bf16[384,1024]{1,0:T(8,128)(2,1)S(1)}, u32[]{:S(2)}, u32[]{:S(2)}) collective-permute-start(bf16[384,1024]{1,0:T(8,128)(2,1)} %raw_ref.1), channel_id=1, source_target_pairs={{0,8},{4,20},{8,0},{12,28},{16,24},{20,4},{24,16},{28,12},{1,9},{5... | collective-permute-start | bytes 2359304 | tf_op jit(solution)/shard_map/ppermute | solution.py:414
  15.3 17.2 %collective-permute-start.8 = (bf16[384,1024]{1,0:T(8,128)(2,1)S(1)}, bf16[384,1024]{1,0:T(8,128)(2,1)S(1)}, u32[]{:S(2)}, u32[]{:S(2)}) collective-permute-start(bf16[384,1024]{1,0:T(8,128)(2,1)S(1)} %collective-permute-done.raw_ref), channel_id=1, source_target_pairs={{0,8},{4,20},{8,0},{12,28},{16,24},{20,4},{24,16},{28,12},{1,9},{5... | collective-permute-start | bytes 2359304 | tf_op jit(solution)/shard_map/ppermute | solution.py:414
  25.3 2.7 %collective-permute-start.5 = (bf16[128,1024]{1,0:T(8,128)(2,1)S(1)}, bf16[128,1024]{1,0:T(8,128)(2,1)S(1)}, u32[]{:S(2)}, u32[]{:S(2)}) collective-permute-start(bf16[128,1024]{1,0:T(8,128)(2,1)S(1)} %get-tuple-element.93), channel_id=1, source_target_pairs={{0,4},{4,0},{8,12},{12,8},{16,20},{20,16},{24,28},{28,24},{1,5},{5... | collective-permute-start | bytes 786440 | tf_op jit(solution)/shard_map/ppermute | solution.py:409
  25.4 2.7 %collective-permute-start.6 = (bf16[128,1024]{1,0:T(8,128)(2,1)S(1)}, bf16[128,1024]{1,0:T(8,128)(2,1)S(1)}, u32[]{:S(2)}, u32[]{:S(2)}) collective-permute-start(bf16[128,1024]{1,0:T(8,128)(2,1)S(1)} %get-tuple-element.94), channel_id=1, source_target_pairs={{0,4},{4,0},{8,12},{12,8},{16,20},{20,16},{24,28},{28,24},{1,5},{5... | collective-permute-start | bytes 786440 | tf_op jit(solution)/shard_map/ppermute | solution.py:409
  25.9 2.2 %collective-permute-start.7 = (bf16[128,1024]{1,0:T(8,128)(2,1)S(1)}, bf16[128,1024]{1,0:T(8,128)(2,1)S(1)}, u32[]{:S(2)}, u32[]{:S(2)}) collective-permute-start(bf16[128,1024]{1,0:T(8,128)(2,1)S(1)} %get-tuple-element.95), channel_id=1, source_target_pairs={{0,4},{4,0},{8,12},{12,8},{16,20},{20,16},{24,28},{28,24},{1,5},{5... | collective-permute-start | bytes 786440 | tf_op jit(solution)/shard_map/ppermute | solution.py:409
  29.5 14.5 %collective-permute-start.15 = (bf16[384,1024]{1,0:T(8,128)(2,1)S(1)}, bf16[384,1024]{1,0:T(8,128)(2,1)S(1)}, u32[]{:S(2)}, u32[]{:S(2)}) collective-permute-start(bf16[384,1024]{1,0:T(8,128)(2,1)S(1)} %get-tuple-element.123), channel_id=1, source_target_pairs={{0,8},{4,20},{8,0},{12,28},{16,24},{20,4},{24,16},{28,12},{1,9},{5... | collective-permute-start | bytes 2359304 | tf_op jit(solution)/shard_map/ppermute | solution.py:414
  34.9 3.9 %collective-permute-start.9 = (bf16[128,1024]{1,0:T(8,128)(2,1)S(1)}, bf16[128,1024]{1,0:T(8,128)(2,1)S(1)}, u32[]{:S(2)}, u32[]{:S(2)}) collective-permute-start(bf16[128,1024]{1,0:T(8,128)(2,1)S(1)} %get-tuple-element.111), channel_id=1, source_target_pairs={{0,4},{4,0},{8,12},{12,8},{16,20},{20,16},{24,28},{28,24},{1,5},{5... | collective-permute-start | bytes 786440 | tf_op jit(solution)/shard_map/ppermute | solution.py:409
  36.1 2.7 %collective-permute-start.10 = (bf16[128,1024]{1,0:T(8,128)(2,1)S(1)}, bf16[128,1024]{1,0:T(8,128)(2,1)S(1)}, u32[]{:S(2)}, u32[]{:S(2)}) collective-permute-start(bf16[128,1024]{1,0:T(8,128)(2,1)S(1)} %get-tuple-element.112), channel_id=1, source_target_pairs={{0,4},{4,0},{8,12},{12,8},{16,20},{20,16},{24,28},{28,24},{1,5},{5... | collective-permute-start | bytes 786440 | tf_op jit(solution)/shard_map/ppermute | solution.py:409
  36.2 2.7 %collective-permute-start.11 = (bf16[128,1024]{1,0:T(8,128)(2,1)S(1)}, bf16[128,1024]{1,0:T(8,128)(2,1)S(1)}, u32[]{:S(2)}, u32[]{:S(2)}) collective-permute-start(bf16[128,1024]{1,0:T(8,128)(2,1)S(1)} %get-tuple-element.113), channel_id=1, source_target_pairs={{0,4},{4,0},{8,12},{12,8},{16,20},{20,16},{24,28},{28,24},{1,5},{5... | collective-permute-start | bytes 786440 | tf_op jit(solution)/shard_map/ppermute | solution.py:409
  38.2 12.1 %collective-permute-start.16 = (bf16[384,1024]{1,0:T(8,128)(2,1)S(1)}, bf16[384,1024]{1,0:T(8,128)(2,1)S(1)}, u32[]{:S(2)}, u32[]{:S(2)}) collective-permute-start(bf16[384,1024]{1,0:T(8,128)(2,1)S(1)} %shard_map.98), channel_id=1, source_target_pairs={{0,8},{4,20},{8,0},{12,28},{16,24},{20,4},{24,16},{28,12},{1,9},{5... | collective-permute-start | bytes 2359304 | tf_op jit(solution)/shard_map/ppermute | solution.py:414
  39.5 13.0 %collective-permute-start.12 = (bf16[384,256]{1,0:T(8,128)(2,1)S(1)}, bf16[384,256]{1,0:T(8,128)(2,1)S(1)}, u32[]{:S(2)}, u32[]{:S(2)}) collective-permute-start(bf16[384,256]{1,0:T(8,128)(2,1)S(1)} %get-tuple-element.116), channel_id=1, source_target_pairs={{0,3},{1,2},{2,1},{3,0},{4,7},{5,6},{6,5},{7,4},{8,11},{9,10},{10,... | collective-permute-start | bytes 589832 | tf_op jit(solution)/shard_map/ppermute | solution.py:409
  42.0 16.2 %collective-permute-start.13 = (bf16[384,256]{1,0:T(8,128)(2,1)S(1)}, bf16[384,256]{1,0:T(8,128)(2,1)S(1)}, u32[]{:S(2)}, u32[]{:S(2)}) collective-permute-start(bf16[384,256]{1,0:T(8,128)(2,1)S(1)} %get-tuple-element.117), channel_id=1, source_target_pairs={{0,2},{1,3},{2,0},{3,1},{4,6},{5,7},{6,4},{7,5},{8,10},{9,11},{10,... | collective-permute-start | bytes 589832 | tf_op jit(solution)/shard_map/ppermute | solution.py:409
  42.0 16.2 %collective-permute-start.14 = (bf16[384,256]{1,0:T(8,128)(2,1)S(1)}, bf16[384,256]{1,0:T(8,128)(2,1)S(1)}, u32[]{:S(2)}, u32[]{:S(2)}) collective-permute-start(bf16[384,256]{1,0:T(8,128)(2,1)S(1)} %get-tuple-element.118), channel_id=1, source_target_pairs={{0,1},{1,0},{2,3},{3,2},{4,5},{5,4},{6,7},{7,6},{8,9},{9,8},{10,11... | collective-permute-start | bytes 589832 | tf_op jit(solution)/shard_map/ppermute | solution.py:409
  50.4 8.8 %collective-permute-start.17 = (bf16[192,1024]{1,0:T(8,128)(2,1)S(1)}, bf16[192,1024]{1,0:T(8,128)(2,1)S(1)}, u32[]{:S(2)}, u32[]{:S(2)}) collective-permute-start(bf16[192,1024]{1,0:T(8,128)(2,1)S(1)} %get-tuple-element.128), channel_id=1, source_target_pairs={{0,16},{4,12},{8,24},{12,4},{16,0},{20,28},{24,8},{28,20},{1,17},{... | collective-permute-start | bytes 1179656 | tf_op jit(solution)/shard_map/ppermute | solution.py:414
  51.7 10.8 %collective-permute-start.18 = (bf16[192,1024]{1,0:T(8,128)(2,1)S(1)}, bf16[192,1024]{1,0:T(8,128)(2,1)S(1)}, u32[]{:S(2)}, u32[]{:S(2)}) collective-permute-start(bf16[192,1024]{1,0:T(8,128)(2,1)S(1)} %get-tuple-element.129), channel_id=1, source_target_pairs={{0,16},{4,12},{8,24},{12,4},{16,0},{20,28},{24,8},{28,20},{1,17},{... | collective-permute-start | bytes 1179656 | tf_op jit(solution)/shard_map/ppermute | solution.py:414

commit v6 on v5

--- a/solution.py
+++ b/solution.py
@@ -12,8 +12,7 @@
 SLOTS = 3
 WAIT_FLOPS = 20_000_000_000
 TEXT_PIECES = 3
-ACC_PIECES = 3
-LAST_PIECES = 2
+ACC_PIECES = 2
 CORES = 2
 EPS = 1e-06
 LOG2E = math.log2(math.e)
@@ -256,7 +255,7 @@
     unit_ref, own_image_ref, near_image_ref, own_weight_in_ref, weight_in_ref, first_ref = refs[
         Pairs.count : Pairs.count + 6
     ]
-    own_weight_ref, acc_ref, weight_ref = refs[Pairs.count + 6 :]
+    own_weight_ref, acc_ref, sum_ref, weight_ref = refs[Pairs.count + 6 :]
     rows = own_image_ref.shape[0]
     second = dot_nt(unit_ref[rows:, :], near_image_ref[pl.ds(rows, rows), :])
     own = dot_nt(unit_ref[rows:, :], own_image_ref[...])
@@ -264,6 +263,7 @@
     weight_ref[:, :rows] = first_ref[...]
     weight_ref[:rows, rows:] = weight_in_ref[:, rows:]
     pairs.weigh(second, 1, 2, weight_ref, rows, rows)
+    sum_ref[...] = dot_tn(weight_ref[:, rows:], unit_ref[...]).astype(jnp.bfloat16)
     pairs.weigh(own, 1, 0, own_weight_ref, rows, 0)
     acc_ref[...] = jnp.dot(
         weight_ref[...], near_image_ref[...], preferred_element_type=jnp.float32
@@ -300,10 +300,9 @@
         ref[...] = acc[at * size : (at + 1) * size, :].astype(ref.dtype)
 
 
-def own_sum_body(own_weight_ref, near_weight_ref, unit_ref, add_ref, own_ref, second_ref):
-    rows = own_ref.shape[0]
-    second_ref[...] = dot_tn(near_weight_ref[:, rows:], unit_ref[...])
-    own_ref[...] = dot_tn(own_weight_ref[...], unit_ref[...]) + add_ref[...].astype(jnp.float32)
+def own_sum_body(weight_ref, unit_ref, first_ref, second_ref, out_ref):
+    total = dot_tn(weight_ref[...], unit_ref[...])
+    out_ref[...] = total + first_ref[...].astype(jnp.float32) + second_ref[...].astype(jnp.float32)
 
 
 def all_body(tiles, chips, *refs):
@@ -336,12 +335,6 @@
         total = dot_tn(weight_ref[pl.ds(0, rows), columns], own_ref[...])
         total += dot_tn(weight_ref[pl.ds(rows, rows), columns], other_ref[...])
         spread_ref[columns, :] = total.astype(jnp.bfloat16)
-
-
-def relay_body(sum_ref, in_ref, *out_refs):
-    for at, ref in enumerate(out_refs):
-        part = pl.ds(at * ref.shape[0], ref.shape[0])
-        ref[...] = (sum_ref[part, :] + in_ref[part, :].astype(jnp.float32)).astype(jnp.bfloat16)
 
 
 def text_grad_body(chunks, *refs):
@@ -380,8 +373,8 @@
         copy.wait()
 
 
-def image_grad_body(piece_count, raw_ref, scale_ref, sum_ref, *refs):
-    piece_refs, (out_ref, grad_ref, sems) = refs[:piece_count], refs[piece_count:]
+def image_grad_body(raw_ref, scale_ref, sum_ref, *refs):
+    add_refs, (out_ref, grad_ref, sems) = refs[:-3], refs[-3:]
     copies = []
     for block in range(raw_ref.shape[0] // TILE):
         for first in range(block * TILE, (block + 1) * TILE, TILE // 2):
@@ -389,10 +382,8 @@
             raw = raw_ref[part, :].astype(jnp.float32)
             scales = scale_ref[part, :1]
             acc = sum_ref[part, :]
-            if piece_refs:
-                size = piece_refs[0].shape[0]
-                piece = piece_refs[first // size][pl.ds(first % size, TILE // 2), :]
-                acc = acc + piece.astype(jnp.float32)
+            for ref in add_refs:
+                acc = acc + ref[part, :].astype(jnp.float32)
             inner = jnp.sum(raw * acc, axis=-1, keepdims=True) * scales * scales
             grad_ref[part, :] = (scales * (acc - raw * inner)).astype(jnp.bfloat16)
         part = pl.ds(block * TILE, TILE)
@@ -517,11 +508,11 @@
             limit=8,
         )[0]
 
-    def finish_image(total, pieces):
+    def finish_image(total, adds):
         return call_kernel(
-            functools.partial(image_grad_body, len(pieces)),
+            image_grad_body,
             [bf16(rows)],
-            [image_raw, image_scales, total] + pieces,
+            [image_raw, image_scales, total] + adds,
             outs_anywhere=True,
             scratch=[pltpu.VMEM((rows, embed), jnp.bfloat16), pltpu.SemaphoreType.DMA((tiles,))],
             limit=8,
@@ -560,12 +551,14 @@
         limit=16,
     )
     image_add = swap_near(first_sum, 0)
-    own_weights, acc, near_weights = call_kernel(
+    own_weights, acc, second_sum = call_kernel(
         functools.partial(near_sum_body, tiles),
-        [bf16(2 * rows, rows), f32(2 * rows), bf16(2 * rows, 2 * rows)],
+        [bf16(2 * rows, rows), f32(2 * rows), bf16(rows)],
         lists + [units, own_images, near_images, own_weights, near_weights, first_weights],
+        scratch=[pltpu.VMEM((2 * rows, 2 * rows), jnp.bfloat16)],
         limit=24,
     )
+    second_add = swap_near(second_sum, 1)
     own_weights, from_far = lax.optimization_barrier((own_weights, from_far))
     far_weights, far_images = call_kernel(
         functools.partial(far_weights_body, tiles),
@@ -590,24 +583,18 @@
     far_sum = call_kernel(far_sum_body, [bf16(rows)], [far_weights, units], limit=16)[0]
     acc_own, far_sum = lax.optimization_barrier((acc_own, far_sum))
     text_parts = finish_text(acc_own, acc_other)
+    far_add = swap(far_sum, "blk", 6)
     own_weights, text_parts[0] = lax.optimization_barrier((own_weights, text_parts[0]))
-    base, second_sum = call_kernel(
+    base = call_kernel(
         own_sum_body,
-        [f32(rows), f32(rows)],
-        [own_weights, near_weights, units, image_add],
+        [f32(rows)],
+        [own_weights, units, image_add, second_add],
         flops=WAIT_FLOPS,
         limit=16,
-    )
-    relayed = call_kernel(
-        relay_body,
-        [bf16(rows // LAST_PIECES)] * LAST_PIECES,
-        [second_sum, swap_near(far_sum, 0)],
-        limit=8,
-    )
-    image_last = [swap_near(piece, 1) for piece in relayed]
+    )[0]
     text_grad = place_text(text_parts)
     base, _ = lax.optimization_barrier((base, text_grad))
-    return (text_grad, finish_image(base, image_last))
+    return (text_grad, finish_image(base, [far_add]))
 
 
 def solution(mesh):

time: 64.1 us -> 68.7 us (1.072)
  the two profiles are of different devices: /device:TPU:0 before, /device:TPU:1 now
where the time goes in v6:
time: 68.7 us; the launch traced here: 68.5 us
  waiting for transfers between devices  31.1 us (45%)
  Pallas kernels  17.4 us (25%)
  starting transfers between devices  16.8 us (24%)
  between operations  2.11 us (3%)
  local copies, waits for them, and re-layouts  1.14 us (2%)
    ppermute x12, waiting for transfers between devices, swap(): return lax.ppermute(value, axis, [(i, i ^ bits) for i in range(count)])  21 us
    pallas_call x17, Pallas kernels, call_kernel(): pl.pallas_call(body, out_shape=outs, in_specs=specs, out_specs=[ANY_SPEC...  17.4 us
    ppermute x12, starting transfers between devices, swap(): return lax.ppermute(value, axis, [(i, i ^ bits) for i in range(count)])  10.4 us
    ppermute x5, waiting for transfers between devices, swap_near(): lax.ppermute(value, 'blk', [(i, i ^ neighbour_bits(i)[which]) for i in ra...  10 us
    ppermute x5, starting transfers between devices, swap_near(): lax.ppermute(value, 'blk', [(i, i ^ neighbour_bits(i)[which]) for i in ra...  6.32 us
  transfers between devices with their start and end apart: 17, of which 6 were waited for; matrix products, arithmetic and copies ran while one was open for 0% of the time, Pallas kernels for 23%

profile of v6, /device:TPU:1, one launch (start us, length us, event | category | flops | bytes accessed | tf_op | source)
XLA Modules:
  0.0 68.5 jit_solution(15569105246472897625)
XLA Ops:
  0.6 2.1 %collective-permute-start = (bf16[384,1024]{1,0:T(8,128)(2,1)}, bf16[384,1024]{1,0:T(8,128)(2,1)S(1)}, u32[]{:S(2)}, u32[]{:S(2)}) collective-permute-start(bf16[384,1024]{1,0:T(8,128)(2,1)} %raw_ref.1), channel_id=1, source_target_pairs={{0,16},{4,12},{8,24},{12,4},{16,0},{20,28},{24,8},{28,20},{1,17},{... | collective-permute-start | bytes 2359304 | tf_op jit(solution)/shard_map/ppermute | solution.py:405
  2.7 1.1 %copy-done = bf16[1536,256]{1,0:T(8,128)(2,1)S(1)} copy-done((bf16[1536,256]{1,0:T(8,128)(2,1)S(1)}, bf16[1536,256]{1,0:T(8,128)(2,1)}, u32[]{:S(2)}) %copy-start) | copy-done | bytes 786456
  3.9 0.1 shard_map.88
  3.9 3.4 %collective-permute-start.2 = (bf16[384,256]{1,0:T(8,128)(2,1)S(1)}, bf16[384,256]{1,0:T(8,128)(2,1)S(1)}, u32[]{:S(2)}, u32[]{:S(2)}) collective-permute-start(bf16[384,256]{1,0:T(8,128)(2,1)S(1)} %get-tuple-element.77), channel_id=1, source_target_pairs={{0,3},{1,2},{2,1},{3,0},{4,7},{5,6},{6,5},{7,4},{8,11},{9,10},{10,... | collective-permute-start | bytes 589832 | tf_op jit(solution)/shard_map/ppermute | solution.py:400
  7.3 0.0 collective-permute-start.3
  7.3 0.4 collective-permute-start.4
  7.7 1.4 %shard_map.86 = (bf16[384,1024]{1,0:T(8,128)(2,1)S(1)}, bf16[384,1024]{1,0:T(8,128)(2,1)S(1)}, f32[384,128]{1,0:T(8,128)S(1)}) custom-call(bf16[384,1024]{1,0:T(8,128)(2,1)} %raw_ref.1), custom_call_target="tpu_custom_call" | custom-call | bytes 2555904 | tf_op jit(solution)/shard_map/pallas_call | solution.py:45
  9.1 1.3 %collective-permute-start.1 = (bf16[384,1024]{1,0:T(8,128)(2,1)}, bf16[384,1024]{1,0:T(8,128)(2,1)S(1)}, u32[]{:S(2)}, u32[]{:S(2)}) collective-permute-start(bf16[384,1024]{1,0:T(8,128)(2,1)} %raw_ref.1), channel_id=1, source_target_pairs={{0,8},{4,20},{8,0},{12,28},{16,24},{20,4},{24,16},{28,12},{1,9},{5... | collective-permute-start | bytes 2359304 | tf_op jit(solution)/shard_map/ppermute | solution.py:405
  11.7 1.1 %shard_map.87 = (f32[2,128]{1,0:T(2,128)S(1)}, f32[72,128]{1,0:T(8,128)S(1)}, s32[12,128]{1,0:T(8,128)S(1)}, s32[768,128]{1,0:T(8,128)S(1)}, f32[384,128]{1,0:T(8,128)S(1)}, /*index=5*/f32[4,128]{1,0:T(4,128)S(1)}) custom-call(f32[1]{0:T(128)S(6)} %copy.9.refs_0_, f32[1]{0:T(128)S(6)} %copy.10.refs_1_, s32[3,8,96]{2,1,0:T(8,128)S(1)} %bitcast.5, ...), custom_call_target="tpu_custom_call" | custom-call | bytes 743432 | tf_op jit(solution)/shard_map/pallas_call | solution.py:45
  12.8 0.0 collective-permute-done.raw_ref
  12.8 1.3 %collective-permute-start.8 = (bf16[384,1024]{1,0:T(8,128)(2,1)S(1)}, bf16[384,1024]{1,0:T(8,128)(2,1)S(1)}, u32[]{:S(2)}, u32[]{:S(2)}) collective-permute-start(bf16[384,1024]{1,0:T(8,128)(2,1)S(1)} %collective-permute-done.raw_ref), channel_id=1, source_target_pairs={{0,8},{4,20},{8,0},{12,28},{16,24},{20,4},{24,16},{28,12},{1,9},{5... | collective-permute-start | bytes 2359304 | tf_op jit(solution)/shard_map/ppermute | solution.py:405
  14.1 0.2 shard_map.89.second_unit_ref
  14.4 4.7 %collective-permute-done.4.refs_3_.refs_4_ = bf16[384,256]{1,0:T(8,128)(2,1)S(1)} collective-permute-done((bf16[384,256]{1,0:T(8,128)(2,1)S(1)}, bf16[384,256]{1,0:T(8,128)(2,1)S(1)}, u32[]{:S(2)}, u32[]{:S(2)}) %collective-permute-start.4) | collective-permute-done | bytes 196640 | tf_op jit(solution)/shard_map/ppermute | solution.py:400
  19.1 0.0 collective-permute-done.2.refs_1_.refs_2_
  19.1 4.5 %collective-permute-done.3.refs_2_.refs_3_ = bf16[384,256]{1,0:T(8,128)(2,1)S(1)} collective-permute-done((bf16[384,256]{1,0:T(8,128)(2,1)S(1)}, bf16[384,256]{1,0:T(8,128)(2,1)S(1)}, u32[]{:S(2)}, u32[]{:S(2)}) %collective-permute-start.3) | collective-permute-done | bytes 196640 | tf_op jit(solution)/shard_map/ppermute | solution.py:400
  23.6 0.4 shard_map.90
  24.0 1.5 %collective-permute-start.5 = (bf16[128,1024]{1,0:T(8,128)(2,1)S(1)}, bf16[128,1024]{1,0:T(8,128)(2,1)S(1)}, u32[]{:S(2)}, u32[]{:S(2)}) collective-permute-start(bf16[128,1024]{1,0:T(8,128)(2,1)S(1)} %get-tuple-element.88), channel_id=1, source_target_pairs={{0,4},{4,0},{8,12},{12,8},{16,20},{20,16},{24,28},{28,24},{1,5},{5... | collective-permute-start | bytes 786440 | tf_op jit(solution)/shard_map/ppermute | solution.py:400
  25.4 0.1 collective-permute-start.6
  25.5 0.4 collective-permute-start.7
  26.0 0.3 shard_map.91.refs_8_.refs_7_
  26.2 1.8 %shard_map.92 = (bf16[384,384]{1,0:T(8,128)(2,1)S(1)}, bf16[384,768]{1,0:T(8,128)(2,1)S(1)}) custom-call(f32[2,128]{1,0:T(2,128)S(1)} %get-tuple-element.69.refs_0_, f32[72,128]{1,0:T(8,128)S(1)} %get-tuple-element.70.refs_1_, s32[12,128]{1,0:T(8,128)S(1)} %get-tuple-element.71.refs_2_, s32[768,128]{1,0:T(8,128)S(1)} %get-tuple-element.72.refs_3_, ...), custom_call_target="tpu_custom_call" | custom-call | bytes 4666368 | tf_op jit(solution)/shard_map/pallas_call | solution.py:45
  28.0 0.0 collective-permute-done.5.refs_9_
  28.0 0.0 collective-permute-done.6.refs_10_
  28.0 1.4 %shard_map.93 = (bf16[768,1024]{1,0:T(8,128)(2,1)S(1)}, bf16[768,384]{1,0:T(8,128)(2,1)S(1)}, bf16[384,1024]{1,0:T(8,128)(2,1)S(1)}) custom-call(f32[2,128]{1,0:T(2,128)S(1)} %get-tuple-element.69.refs_0_, f32[72,128]{1,0:T(8,128)S(1)} %get-tuple-element.70.refs_1_, s32[12,128]{1,0:T(8,128)S(1)} %get-tuple-element.71.refs_2_, ...), custom_call_target="tpu_custom_call" | custom-call | bytes 7320576 | tf_op jit(solution)/shard_map/pallas_call | solution.py:45
  29.5 1.3 %collective-permute-start.14 = (bf16[384,1024]{1,0:T(8,128)(2,1)S(1)}, bf16[384,1024]{1,0:T(8,128)(2,1)S(1)}, u32[]{:S(2)}, u32[]{:S(2)}) collective-permute-start(bf16[384,1024]{1,0:T(8,128)(2,1)S(1)} %get-tuple-element.116), channel_id=1, source_target_pairs={{0,8},{4,20},{8,0},{12,28},{16,24},{20,4},{24,16},{28,12},{1,9},{5... | collective-permute-start | bytes 2359304 | tf_op jit(solution)/shard_map/ppermute | solution.py:405
  30.8 3.1 %shard_map.94 = (bf16[768,384]{1,0:T(8,128)(2,1)S(1)}, f32[768,1024]{1,0:T(8,128)S(1)}, bf16[384,1024]{1,0:T(8,128)(2,1)S(1)}) custom-call(f32[2,128]{1,0:T(2,128)S(1)} %get-tuple-element.69.refs_0_, f32[72,128]{1,0:T(8,128)S(1)} %get-tuple-element.70.refs_1_, s32[12,128]{1,0:T(8,128)S(1)} %get-tuple-element.71.refs_2_, ...), custom_call_target="tpu_custom_call" | custom-call | bytes 10564608 | tf_op jit(solution)/shard_map/pallas_call | solution.py:45
  33.9 0.3 collective-permute-start.15
  34.2 0.0 collective-permute-done.8.refs_9_
  34.2 1.6 %shard_map.95 = (bf16[768,768]{1,0:T(8,128)(2,1)S(1)}, bf16[768,1024]{1,0:T(8,128)(2,1)S(1)}) custom-call(f32[2,128]{1,0:T(2,128)S(1)} %get-tuple-element.69.refs_0_, f32[72,128]{1,0:T(8,128)S(1)} %get-tuple-element.70.refs_1_, s32[12,128]{1,0:T(8,128)S(1)} %get-tuple-element.71.refs_2_, s32[768,128]{1,0:T(8,128)S(1)} %get-tuple-element.72.refs_3_, ...), custom_call_target="tpu_custom_call" | custom-call | bytes 7123968 | tf_op jit(solution)/shard_map/pallas_call | solution.py:45
  35.8 0.8 %shard_map.96 = (bf16[192,1024]{1,0:T(8,128)(2,1)S(1)}, bf16[192,1024]{1,0:T(8,128)(2,1)S(1)}) custom-call(bf16[768,768]{1,0:T(8,128)(2,1)S(1)} %get-tuple-element.104.weight_ref, bf16[768,1024]{1,0:T(8,128)(2,1)S(1)} %get-tuple-element.102.image_ref, f32[768,1024]{1,0:T(8,128)S(1)} %get-tuple-element.100.acc_ref), custom_call_target="tpu_custom_call" | custom-call | bytes 6684672 | tf_op jit(solution)/shard_map/pallas_call | solution.py:45
  36.6 0.7 %collective-permute-start.9 = (bf16[192,1024]{1,0:T(8,128)(2,1)S(1)}, bf16[192,1024]{1,0:T(8,128)(2,1)S(1)}, u32[]{:S(2)}, u32[]{:S(2)}) collective-permute-start(bf16[192,1024]{1,0:T(8,128)(2,1)S(1)} %get-tuple-element.106), channel_id=1, source_target_pairs={{0,4},{4,0},{8,12},{12,8},{16,20},{20,16},{24,28},{28,24},{1,5},{5... | collective-permute-start | bytes 1179656 | tf_op jit(solution)/shard_map/ppermute | solution.py:400
  37.3 0.1 collective-permute-start.10
  37.3 0.8 %shard_map.97.refs_5_ = f32[384,1024]{1,0:T(8,128)S(1)} custom-call(bf16[768,768]{1,0:T(8,128)(2,1)S(1)} %get-tuple-element.104.weight_ref, bf16[768,1024]{1,0:T(8,128)(2,1)S(1)} %get-tuple-element.102.image_ref, f32[768,1024]{1,0:T(8,128)S(1)} %get-tuple-element.100.acc_ref), custom_call_target="tpu_custom_call" | custom-call | bytes 7471104 | tf_op jit(solution)/shard_map/pallas_call | solution.py:45
  38.1 0.8 %shard_map.98 = bf16[384,1024]{1,0:T(8,128)(2,1)S(1)} custom-call(bf16[768,768]{1,0:T(8,128)(2,1)S(1)} %get-tuple-element.104.weight_ref, bf16[768,1024]{1,0:T(8,128)(2,1)S(1)} %get-tuple-element.91.refs_6_.unit_ref), custom_call_target="tpu_custom_call" | custom-call | bytes 3538944 | tf_op jit(solution)/shard_map/pallas_call | solution.py:45
  38.9 1.2 %collective-permute-start.16 = (bf16[384,1024]{1,0:T(8,128)(2,1)S(1)}, bf16[384,1024]{1,0:T(8,128)(2,1)S(1)}, u32[]{:S(2)}, u32[]{:S(2)}) collective-permute-start(bf16[384,1024]{1,0:T(8,128)(2,1)S(1)} %shard_map.98), channel_id=1, source_target_pairs={{0,24},{4,28},{8,16},{12,20},{16,8},{20,12},{24,0},{28,4},{1,25},{... | collective-permute-start | bytes 2359304 | tf_op jit(solution)/shard_map/ppermute | solution.py:400
  40.2 0.0 collective-permute-done.9.refs_6_
  40.2 0.0 collective-permute-done.10.refs_7_
  40.2 0.6 shard_map.99
  40.8 2.3 %collective-permute-start.11 = (bf16[384,256]{1,0:T(8,128)(2,1)S(1)}, bf16[384,256]{1,0:T(8,128)(2,1)S(1)}, u32[]{:S(2)}, u32[]{:S(2)}) collective-permute-start(bf16[384,256]{1,0:T(8,128)(2,1)S(1)} %get-tuple-element.110), channel_id=1, source_target_pairs={{0,3},{1,2},{2,1},{3,0},{4,7},{5,6},{6,5},{7,4},{8,11},{9,10},{10,... | collective-permute-start | bytes 589832 | tf_op jit(solution)/shard_map/ppermute | solution.py:400
  43.1 0.0 collective-permute-start.12
  43.1 1.7 %collective-permute-done.14.first_ref = bf16[384,1024]{1,0:T(8,128)(2,1)S(1)} collective-permute-done((bf16[384,1024]{1,0:T(8,128)(2,1)S(1)}, bf16[384,1024]{1,0:T(8,128)(2,1)S(1)}, u32[]{:S(2)}, u32[]{:S(2)}) %collective-permute-start.14) | collective-permute-done | bytes 786464 | tf_op jit(solution)/shard_map/ppermute | solution.py:405
  44.8 0.5 collective-permute-start.13
  45.3 8.3 %collective-permute-done.15.second_ref = bf16[384,1024]{1,0:T(8,128)(2,1)S(1)} collective-permute-done((bf16[384,1024]{1,0:T(8,128)(2,1)S(1)}, bf16[384,1024]{1,0:T(8,128)(2,1)S(1)}, u32[]{:S(2)}, u32[]{:S(2)}) %collective-permute-start.15) | collective-permute-done | bytes 786464 | tf_op jit(solution)/shard_map/ppermute | solution.py:405
  53.6 0.9 %shard_map.101.sum_ref = f32[384,1024]{1,0:T(8,128)S(1)} custom-call(bf16[768,384]{1,0:T(8,128)(2,1)S(1)} %get-tuple-element.115.refs_8_.weight_ref, bf16[768,1024]{1,0:T(8,128)(2,1)S(1)} %get-tuple-element.91.refs_6_.unit_ref, bf16[384,1024]{1,0:T(8,128)(2,1)S(1)} %collective-permute-done.14.first_ref, bf16[384,1024]{1,0:T(8,128)(2,1)S(1)} %collective-permute-done.15.second_ref), custom_call_target="tpu_custom_call" | custom-call | flops 20000000000 | bytes 5308416 | tf_op jit(solution)/shard_map/pallas_call | solution.py:45
  54.4 3.9 %collective-permute-done.12.refs_2_ = bf16[384,256]{1,0:T(8,128)(2,1)S(1)} collective-permute-done((bf16[384,256]{1,0:T(8,128)(2,1)S(1)}, bf16[384,256]{1,0:T(8,128)(2,1)S(1)}, u32[]{:S(2)}, u32[]{:S(2)}) %collective-permute-start.12) | collective-permute-done | bytes 196640 | tf_op jit(solution)/shard_map/ppermute | solution.py:400
  58.3 0.9 %shard_map.100 = bf16[1536,256]{1,0:T(8,128)(2,1)} custom-call(bf16[384,256]{1,0:T(8,128)(2,1)S(1)} %get-tuple-element.109.refs_0_, bf16[384,256]{1,0:T(8,128)(2,1)S(1)} %collective-permute-done.11.refs_1_, bf16[384,256]{1,0:T(8,128)(2,1)S(1)} %collective-permute-done.12.refs_2_, bf16[384,256]{1,0:T(8,128)(2,1)S(1)} %collective-permute-done.13.refs_3_), custom_call_target="tpu_custom_call" | custom-call | flops 20000000000 | bytes 1572864 | tf_op jit(solution)/shard_map/pallas_call | solution.py:45
  59.2 7.9 %collective-permute-done.16.refs_0_ = bf16[384,1024]{1,0:T(8,128)(2,1)S(1)} collective-permute-done((bf16[384,1024]{1,0:T(8,128)(2,1)S(1)}, bf16[384,1024]{1,0:T(8,128)(2,1)S(1)}, u32[]{:S(2)}, u32[]{:S(2)}) %collective-permute-start.16) | collective-permute-done | bytes 786464 | tf_op jit(solution)/shard_map/ppermute | solution.py:400
  67.1 1.4 %shard_map.102 = bf16[384,1024]{1,0:T(8,128)(2,1)} custom-call(bf16[384,1024]{1,0:T(8,128)(2,1)S(1)} %get-tuple-element.113.raw_ref, f32[384,128]{1,0:T(8,128)S(1)} %get-tuple-element.114.scale_ref, f32[384,1024]{1,0:T(8,128)S(1)} %shard_map.101.sum_ref, bf16[384,1024]{1,0:T(8,128)(2,1)S(1)} %collective-permute-done.16.refs_0_), custom_call_target="tpu_custom_call" | custom-call | bytes 4128768 | tf_op jit(solution)/shard_map/pallas_call | solution.py:45
  (11 shorter events, 0.0 us)
Async XLA Ops:
  0.6 12.2 %collective-permute-start = (bf16[384,1024]{1,0:T(8,128)(2,1)}, bf16[384,1024]{1,0:T(8,128)(2,1)S(1)}, u32[]{:S(2)}, u32[]{:S(2)}) collective-permute-start(bf16[384,1024]{1,0:T(8,128)(2,1)} %raw_ref.1), channel_id=1, source_target_pairs={{0,16},{4,12},{8,24},{12,4},{16,0},{20,28},{24,8},{28,20},{1,17},{... | collective-permute-start | bytes 2359304 | tf_op jit(solution)/shard_map/ppermute | solution.py:405
  2.7 1.1 %copy-start = (bf16[1536,256]{1,0:T(8,128)(2,1)S(1)}, bf16[1536,256]{1,0:T(8,128)(2,1)}, u32[]{:S(2)}) copy-start(bf16[1536,256]{1,0:T(8,128)(2,1)} %text_ref.1) | copy-start | bytes 2359300
  3.9 7.8 %copy-start.1 = (s32[12288]{0:T(1024)S(1)}, s32[12288]{0:T(1024)}, u32[]{:S(2)}) copy-start(s32[12288]{0:T(1024)} %param.11) | copy-start | bytes 147460
  3.9 7.8 %copy-start.2 = (s32[12288]{0:T(1024)S(1)}, s32[12288]{0:T(1024)}, u32[]{:S(2)}) copy-start(s32[12288]{0:T(1024)} %param.12) | copy-start | bytes 147460
  3.9 7.9 %copy-start.3 = (s32[96,8,3]{0,1,2:T(8,128)S(1)}, s32[96,8,3]{0,1,2:T(8,128)}, u32[]{:S(2)}) copy-start(s32[96,8,3]{0,1,2:T(8,128)} %param.13) | copy-start | bytes 27652
  3.9 15.2 %collective-permute-start.2 = (bf16[384,256]{1,0:T(8,128)(2,1)S(1)}, bf16[384,256]{1,0:T(8,128)(2,1)S(1)}, u32[]{:S(2)}, u32[]{:S(2)}) collective-permute-start(bf16[384,256]{1,0:T(8,128)(2,1)S(1)} %get-tuple-element.77), channel_id=1, source_target_pairs={{0,3},{1,2},{2,1},{3,0},{4,7},{5,6},{6,5},{7,4},{8,11},{9,10},{10,... | collective-permute-start | bytes 589832 | tf_op jit(solution)/shard_map/ppermute | solution.py:400
  7.3 16.2 %collective-permute-start.3 = (bf16[384,256]{1,0:T(8,128)(2,1)S(1)}, bf16[384,256]{1,0:T(8,128)(2,1)S(1)}, u32[]{:S(2)}, u32[]{:S(2)}) collective-permute-start(bf16[384,256]{1,0:T(8,128)(2,1)S(1)} %get-tuple-element.78), channel_id=1, source_target_pairs={{0,2},{1,3},{2,0},{3,1},{4,6},{5,7},{6,4},{7,5},{8,10},{9,11},{10,... | collective-permute-start | bytes 589832 | tf_op jit(solution)/shard_map/ppermute | solution.py:400
  7.3 11.8 %collective-permute-start.4 = (bf16[384,256]{1,0:T(8,128)(2,1)S(1)}, bf16[384,256]{1,0:T(8,128)(2,1)S(1)}, u32[]{:S(2)}, u32[]{:S(2)}) collective-permute-start(bf16[384,256]{1,0:T(8,128)(2,1)S(1)} %get-tuple-element.79), channel_id=1, source_target_pairs={{0,1},{1,0},{2,3},{3,2},{4,5},{5,4},{6,7},{7,6},{8,9},{9,8},{10,11... | collective-permute-start | bytes 589832 | tf_op jit(solution)/shard_map/ppermute | solution.py:400
  9.1 16.9 %collective-permute-start.1 = (bf16[384,1024]{1,0:T(8,128)(2,1)}, bf16[384,1024]{1,0:T(8,128)(2,1)S(1)}, u32[]{:S(2)}, u32[]{:S(2)}) collective-permute-start(bf16[384,1024]{1,0:T(8,128)(2,1)} %raw_ref.1), channel_id=1, source_target_pairs={{0,8},{4,20},{8,0},{12,28},{16,24},{20,4},{24,16},{28,12},{1,9},{5... | collective-permute-start | bytes 2359304 | tf_op jit(solution)/shard_map/ppermute | solution.py:405
  12.8 21.4 %collective-permute-start.8 = (bf16[384,1024]{1,0:T(8,128)(2,1)S(1)}, bf16[384,1024]{1,0:T(8,128)(2,1)S(1)}, u32[]{:S(2)}, u32[]{:S(2)}) collective-permute-start(bf16[384,1024]{1,0:T(8,128)(2,1)S(1)} %collective-permute-done.raw_ref), channel_id=1, source_target_pairs={{0,8},{4,20},{8,0},{12,28},{16,24},{20,4},{24,16},{28,12},{1,9},{5... | collective-permute-start | bytes 2359304 | tf_op jit(solution)/shard_map/ppermute | solution.py:405
  24.0 4.0 %collective-permute-start.5 = (bf16[128,1024]{1,0:T(8,128)(2,1)S(1)}, bf16[128,1024]{1,0:T(8,128)(2,1)S(1)}, u32[]{:S(2)}, u32[]{:S(2)}) collective-permute-start(bf16[128,1024]{1,0:T(8,128)(2,1)S(1)} %get-tuple-element.88), channel_id=1, source_target_pairs={{0,4},{4,0},{8,12},{12,8},{16,20},{20,16},{24,28},{28,24},{1,5},{5... | collective-permute-start | bytes 786440 | tf_op jit(solution)/shard_map/ppermute | solution.py:400
  25.4 2.6 %collective-permute-start.6 = (bf16[128,1024]{1,0:T(8,128)(2,1)S(1)}, bf16[128,1024]{1,0:T(8,128)(2,1)S(1)}, u32[]{:S(2)}, u32[]{:S(2)}) collective-permute-start(bf16[128,1024]{1,0:T(8,128)(2,1)S(1)} %get-tuple-element.89), channel_id=1, source_target_pairs={{0,4},{4,0},{8,12},{12,8},{16,20},{20,16},{24,28},{28,24},{1,5},{5... | collective-permute-start | bytes 786440 | tf_op jit(solution)/shard_map/ppermute | solution.py:400
  25.5 2.5 %collective-permute-start.7 = (bf16[128,1024]{1,0:T(8,128)(2,1)S(1)}, bf16[128,1024]{1,0:T(8,128)(2,1)S(1)}, u32[]{:S(2)}, u32[]{:S(2)}) collective-permute-start(bf16[128,1024]{1,0:T(8,128)(2,1)S(1)} %get-tuple-element.90), channel_id=1, source_target_pairs={{0,4},{4,0},{8,12},{12,8},{16,20},{20,16},{24,28},{28,24},{1,5},{5... | collective-permute-start | bytes 786440 | tf_op jit(solution)/shard_map/ppermute | solution.py:400
  29.5 15.3 %collective-permute-start.14 = (bf16[384,1024]{1,0:T(8,128)(2,1)S(1)}, bf16[384,1024]{1,0:T(8,128)(2,1)S(1)}, u32[]{:S(2)}, u32[]{:S(2)}) collective-permute-start(bf16[384,1024]{1,0:T(8,128)(2,1)S(1)} %get-tuple-element.116), channel_id=1, source_target_pairs={{0,8},{4,20},{8,0},{12,28},{16,24},{20,4},{24,16},{28,12},{1,9},{5... | collective-permute-start | bytes 2359304 | tf_op jit(solution)/shard_map/ppermute | solution.py:405
  33.9 19.7 %collective-permute-start.15 = (bf16[384,1024]{1,0:T(8,128)(2,1)S(1)}, bf16[384,1024]{1,0:T(8,128)(2,1)S(1)}, u32[]{:S(2)}, u32[]{:S(2)}) collective-permute-start(bf16[384,1024]{1,0:T(8,128)(2,1)S(1)} %get-tuple-element.117), channel_id=1, source_target_pairs={{0,16},{4,12},{8,24},{12,4},{16,0},{20,28},{24,8},{28,20},{1,17},{... | collective-permute-start | bytes 2359304 | tf_op jit(solution)/shard_map/ppermute | solution.py:405
  36.6 3.6 %collective-permute-start.9 = (bf16[192,1024]{1,0:T(8,128)(2,1)S(1)}, bf16[192,1024]{1,0:T(8,128)(2,1)S(1)}, u32[]{:S(2)}, u32[]{:S(2)}) collective-permute-start(bf16[192,1024]{1,0:T(8,128)(2,1)S(1)} %get-tuple-element.106), channel_id=1, source_target_pairs={{0,4},{4,0},{8,12},{12,8},{16,20},{20,16},{24,28},{28,24},{1,5},{5... | collective-permute-start | bytes 1179656 | tf_op jit(solution)/shard_map/ppermute | solution.py:400
  37.3 2.9 %collective-permute-start.10 = (bf16[192,1024]{1,0:T(8,128)(2,1)S(1)}, bf16[192,1024]{1,0:T(8,128)(2,1)S(1)}, u32[]{:S(2)}, u32[]{:S(2)}) collective-permute-start(bf16[192,1024]{1,0:T(8,128)(2,1)S(1)} %get-tuple-element.107), channel_id=1, source_target_pairs={{0,4},{4,0},{8,12},{12,8},{16,20},{20,16},{24,28},{28,24},{1,5},{5... | collective-permute-start | bytes 1179656 | tf_op jit(solution)/shard_map/ppermute | solution.py:400
  38.9 28.2 %collective-permute-start.16 = (bf16[384,1024]{1,0:T(8,128)(2,1)S(1)}, bf16[384,1024]{1,0:T(8,128)(2,1)S(1)}, u32[]{:S(2)}, u32[]{:S(2)}) collective-permute-start(bf16[384,1024]{1,0:T(8,128)(2,1)S(1)} %shard_map.98), channel_id=1, source_target_pairs={{0,24},{4,28},{8,16},{12,20},{16,8},{20,12},{24,0},{28,4},{1,25},{... | collective-permute-start | bytes 2359304 | tf_op jit(solution)/shard_map/ppermute | solution.py:400
  40.8 13.6 %collective-permute-start.11 = (bf16[384,256]{1,0:T(8,128)(2,1)S(1)}, bf16[384,256]{1,0:T(8,128)(2,1)S(1)}, u32[]{:S(2)}, u32[]{:S(2)}) collective-permute-start(bf16[384,256]{1,0:T(8,128)(2,1)S(1)} %get-tuple-element.110), channel_id=1, source_target_pairs={{0,3},{1,2},{2,1},{3,0},{4,7},{5,6},{6,5},{7,4},{8,11},{9,10},{10,... | collective-permute-start | bytes 589832 | tf_op jit(solution)/shard_map/ppermute | solution.py:400
  43.1 15.3 %collective-permute-start.12 = (bf16[384,256]{1,0:T(8,128)(2,1)S(1)}, bf16[384,256]{1,0:T(8,128)(2,1)S(1)}, u32[]{:S(2)}, u32[]{:S(2)}) collective-permute-start(bf16[384,256]{1,0:T(8,128)(2,1)S(1)} %get-tuple-element.111), channel_id=1, source_target_pairs={{0,2},{1,3},{2,0},{3,1},{4,6},{5,7},{6,4},{7,5},{8,10},{9,11},{10,... | collective-permute-start | bytes 589832 | tf_op jit(solution)/shard_map/ppermute | solution.py:400
  44.8 13.5 %collective-permute-start.13 = (bf16[384,256]{1,0:T(8,128)(2,1)S(1)}, bf16[384,256]{1,0:T(8,128)(2,1)S(1)}, u32[]{:S(2)}, u32[]{:S(2)}) collective-permute-start(bf16[384,256]{1,0:T(8,128)(2,1)S(1)} %get-tuple-element.112), channel_id=1, source_target_pairs={{0,1},{1,0},{2,3},{3,2},{4,5},{5,4},{6,7},{7,6},{8,9},{9,8},{10,11... | collective-permute-start | bytes 589832 | tf_op jit(solution)/shard_map/ppermute | solution.py:400

commit v7 on v5

--- a/solution.py
+++ b/solution.py
@@ -12,7 +12,7 @@
 SLOTS = 3
 WAIT_FLOPS = 20_000_000_000
 TEXT_PIECES = 3
-ACC_PIECES = 3
+ACC_PIECES = 2
 LAST_PIECES = 2
 CORES = 2
 EPS = 1e-06
@@ -79,7 +79,7 @@
     )
 
 
-def peer_bits(k, chunks):
+def far_first(k, chunks):
     return (chunks - k) % chunks
 
 
@@ -91,8 +91,7 @@
     place = lax.axis_index("tp")
     rows = out_refs[0].shape[0]
     for k, out_ref in enumerate(out_refs):
-        peer = place ^ peer_bits(k, len(out_refs))
-        out_ref[...] = text_ref[pl.ds(pl.multiple_of(peer * rows, rows), rows), :]
+        out_ref[...] = text_ref[pl.ds(pl.multiple_of((place ^ k) * rows, rows), rows), :]
 
 
 def unit_text_body(chunks, *refs):
@@ -106,7 +105,7 @@
         scales = row_scales(sum(jnp.sum(x * x, axis=-1, keepdims=True) for x in parts))
         scale_ref[part, :] = jnp.broadcast_to(scales, (TILE, TILE))
         for k, x in enumerate(parts):
-            unit_ref[part, feature_slice(place ^ peer_bits(k, chunks), width)] = (x * scales).astype(jnp.bfloat16)
+            unit_ref[part, feature_slice(place ^ k, width)] = (x * scales).astype(jnp.bfloat16)
     split_rows(unit_ref, piece_refs)
 
 
@@ -284,9 +283,12 @@
     weight_ref[:, :rows] = own_weight_ref[...]
 
 
-def far_sum_body(weight_ref, unit_ref, out_ref):
-    rows = out_ref.shape[0]
-    out_ref[...] = dot_tn(weight_ref[:, rows:], unit_ref[...]).astype(jnp.bfloat16)
+def far_sum_body(weight_ref, unit_ref, *out_refs):
+    rows = weight_ref.shape[1] // 2
+    total = dot_tn(weight_ref[:, rows:], unit_ref[...]).astype(jnp.bfloat16)
+    size = rows // len(out_refs)
+    for at, ref in enumerate(out_refs):
+        ref[...] = total[at * size : (at + 1) * size, :]
 
 
 def text_sum_body(half, weight_ref, image_ref, acc_ref, *out_refs):
@@ -338,10 +340,10 @@
         spread_ref[columns, :] = total.astype(jnp.bfloat16)
 
 
-def relay_body(sum_ref, in_ref, *out_refs):
-    for at, ref in enumerate(out_refs):
-        part = pl.ds(at * ref.shape[0], ref.shape[0])
-        ref[...] = (sum_ref[part, :] + in_ref[part, :].astype(jnp.float32)).astype(jnp.bfloat16)
+def relay_body(at, sum_ref, in_ref, out_ref):
+    size = in_ref.shape[0]
+    part = sum_ref[pl.ds(at * size, size), :]
+    out_ref[...] = (part + in_ref[...].astype(jnp.float32)).astype(jnp.bfloat16)
 
 
 def text_grad_body(chunks, *refs):
@@ -356,13 +358,15 @@
         raws = [ref[part, :].astype(jnp.float32) for ref in raw_refs]
         accs = []
         for k in range(chunks):
-            features = feature_slice(place ^ peer_bits(k, chunks), width)
+            features = feature_slice(place ^ k, width)
             added = add_refs[first // size][pl.ds(first % size, TILE // 2), features]
             accs.append(acc_ref[part, features] + added.astype(jnp.float32))
         inner = sum(jnp.sum(x * a, axis=-1, keepdims=True) for x, a in zip(raws, accs))
         inner = inner * scales * scales
         for k in range(chunks):
-            out_refs[k][part, :] = (scales * (accs[k] - raws[k] * inner)).astype(jnp.bfloat16)
+            out_refs[far_first(k, chunks)][part, :] = (
+                scales * (accs[k] - raws[k] * inner)
+            ).astype(jnp.bfloat16)
 
 
 def place_text_body(chunks, *refs):
@@ -371,7 +375,7 @@
     rows = part_refs[0].shape[0]
     copies = []
     for k in range(chunks):
-        peer = place ^ peer_bits(k, chunks)
+        peer = place ^ far_first(k, chunks)
         block = pl.ds(pl.multiple_of(peer * rows, rows), rows)
         copies.append(pltpu.make_async_copy(part_refs[k], out_ref.at[block, :], sems.at[k]))
     for copy in copies:
@@ -414,11 +418,6 @@
     return lax.ppermute(value, "blk", [(i, i ^ neighbour_bits(i)[which]) for i in range(count)])
 
 
-def swap_chunks(chunks):
-    count = len(chunks)
-    return chunks[:1] + [swap(chunks[k], "tp", peer_bits(k, count)) for k in range(1, count)]
-
-
 def per_device(text_emb, image_emb, logit_scale, logit_bias, bucket, positive, blocks):
     groups = lax.axis_size("tp")
     shards = lax.axis_size("blk")
@@ -438,7 +437,7 @@
         return struct((count, columns), jnp.int32)
 
     picked = call_kernel(pick_body, [bf16(rows, width)] * groups, [text_emb], limit=8)
-    text_raw = swap_chunks(picked)
+    text_raw = picked[:1] + [swap(picked[k], "tp", k) for k in range(1, groups)]
     if square:
         from_second = swap_near(image_emb, 1)
     else:
@@ -504,7 +503,9 @@
             [text_scales] + text_raw + [acc_own] + [swap(piece, "blk", 1) for piece in acc_other],
             limit=16,
         )
-        return swap_chunks(parts)
+        return parts[:1] + [
+            swap(parts[k], "tp", far_first(k, groups)) for k in range(1, groups)
+        ]
 
     def place_text(text_parts):
         return call_kernel(
@@ -587,8 +588,10 @@
         limit=16,
     )[0]
     far_weights, acc_own = lax.optimization_barrier((far_weights, acc_own))
-    far_sum = call_kernel(far_sum_body, [bf16(rows)], [far_weights, units], limit=16)[0]
-    acc_own, far_sum = lax.optimization_barrier((acc_own, far_sum))
+    far_sum = call_kernel(
+        far_sum_body, [bf16(rows // LAST_PIECES)] * LAST_PIECES, [far_weights, units], limit=16
+    )
+    acc_own, far_sum[0] = lax.optimization_barrier((acc_own, far_sum[0]))
     text_parts = finish_text(acc_own, acc_other)
     own_weights, text_parts[0] = lax.optimization_barrier((own_weights, text_parts[0]))
     base, second_sum = call_kernel(
@@ -598,13 +601,15 @@
         flops=WAIT_FLOPS,
         limit=16,
     )
-    relayed = call_kernel(
-        relay_body,
-        [bf16(rows // LAST_PIECES)] * LAST_PIECES,
-        [second_sum, swap_near(far_sum, 0)],
-        limit=8,
-    )
-    image_last = [swap_near(piece, 1) for piece in relayed]
+    image_last = []
+    for at, piece in enumerate(far_sum):
+        relayed = call_kernel(
+            functools.partial(relay_body, at),
+            [bf16(rows // LAST_PIECES)],
+            [second_sum, swap_near(piece, 0)],
+            limit=8,
+        )[0]
+        image_last.append(swap_near(relayed, 1))
     text_grad = place_text(text_parts)
     base, _ = lax.optimization_barrier((base, text_grad))
     return (text_grad, finish_image(base, image_last))

time: 64.1 us -> 62.3 us (0.972)
  waiting for transfers between devices: 20.6 us -> 18.1 us
  starting transfers between devices: 22.4 us -> 23.1 us
    ppermute x7 -> x8, waiting for transfers between devices: 8.84 us -> 4.11 us  [swap_near(): lax.ppermute(value, 'blk', [(i, i ^ neighbour_bits(i)[which]) for i in ra...]
    ppermute x12 -> x11, waiting for transfers between devices: 11.8 us -> 14 us  [swap(): return lax.ppermute(value, axis, [(i, i ^ bits) for i in range(count)])]
    ppermute x7 -> x8, starting transfers between devices: 11.2 us -> 12.4 us  [swap_near(): lax.ppermute(value, 'blk', [(i, i ^ neighbour_bits(i)[which]) for i in ra...]
    ppermute x12 -> x11, starting transfers between devices: 11.3 us -> 10.7 us  [swap(): return lax.ppermute(value, axis, [(i, i ^ bits) for i in range(count)])]
    pallas_call x18 -> x19, Pallas kernels: 17.5 us -> 17.6 us  [call_kernel(): pl.pallas_call(body, out_shape=outs, in_specs=specs, out_specs=[ANY_SPEC...]
  transfers between devices with their start and end apart: 19 -> 19, of which waited for: 6 -> 5; matrix products, arithmetic and copies ran while one was open for 0% -> 0% of each run, Pallas kernels for 25% -> 26%
where the time goes in v7:
time: 62.3 us; the launch traced here: 62.1 us
  starting transfers between devices  23.1 us (37%)
  waiting for transfers between devices  18.1 us (29%)
  Pallas kernels  17.6 us (28%)
  between operations  2.14 us (3%)
  local copies, waits for them, and re-layouts  1.14 us (2%)
    pallas_call x19, Pallas kernels, call_kernel(): pl.pallas_call(body, out_shape=outs, in_specs=specs, out_specs=[ANY_SPEC...  17.6 us
    ppermute x11, waiting for transfers between devices, swap(): return lax.ppermute(value, axis, [(i, i ^ bits) for i in range(count)])  14 us
    ppermute x8, starting transfers between devices, swap_near(): lax.ppermute(value, 'blk', [(i, i ^ neighbour_bits(i)[which]) for i in ra...  12.4 us
    ppermute x11, starting transfers between devices, swap(): return lax.ppermute(value, axis, [(i, i ^ bits) for i in range(count)])  10.7 us
    ppermute x8, waiting for transfers between devices, swap_near(): lax.ppermute(value, 'blk', [(i, i ^ neighbour_bits(i)[which]) for i in ra...  4.11 us
  transfers between devices with their start and end apart: 19, of which 5 were waited for; matrix products, arithmetic and copies ran while one was open for 0% of the time, Pallas kernels for 26%

profile of v7, /device:TPU:0, one launch (start us, length us, event | category | flops | bytes accessed | tf_op | source)
XLA Modules:
  0.0 62.1 jit_solution(1471034416377292888)
XLA Ops:
  0.6 3.0 %collective-permute-start = (bf16[384,1024]{1,0:T(8,128)(2,1)}, bf16[384,1024]{1,0:T(8,128)(2,1)S(1)}, u32[]{:S(2)}, u32[]{:S(2)}) collective-permute-start(bf16[384,1024]{1,0:T(8,128)(2,1)} %raw_ref.1), channel_id=1, source_target_pairs={{0,16},{4,12},{8,24},{12,4},{16,0},{20,28},{24,8},{28,20},{1,17},{... | collective-permute-start | bytes 2359304 | tf_op jit(solution)/shard_map/ppermute | solution.py:418
  3.7 1.1 %copy-done = bf16[1536,256]{1,0:T(8,128)(2,1)S(1)} copy-done((bf16[1536,256]{1,0:T(8,128)(2,1)S(1)}, bf16[1536,256]{1,0:T(8,128)(2,1)}, u32[]{:S(2)}) %copy-start) | copy-done | bytes 786456
  4.8 0.1 shard_map.88
  4.9 1.6 %collective-permute-start.2 = (bf16[384,256]{1,0:T(8,128)(2,1)S(1)}, bf16[384,256]{1,0:T(8,128)(2,1)S(1)}, u32[]{:S(2)}, u32[]{:S(2)}) collective-permute-start(bf16[384,256]{1,0:T(8,128)(2,1)S(1)} %get-tuple-element.81), channel_id=1, source_target_pairs={{0,1},{1,0},{2,3},{3,2},{4,5},{5,4},{6,7},{7,6},{8,9},{9,8},{10,11... | collective-permute-start | bytes 589832 | tf_op jit(solution)/shard_map/ppermute | solution.py:413
  6.5 2.6 %collective-permute-start.3 = (bf16[384,256]{1,0:T(8,128)(2,1)S(1)}, bf16[384,256]{1,0:T(8,128)(2,1)S(1)}, u32[]{:S(2)}, u32[]{:S(2)}) collective-permute-start(bf16[384,256]{1,0:T(8,128)(2,1)S(1)} %get-tuple-element.82), channel_id=1, source_target_pairs={{0,2},{1,3},{2,0},{3,1},{4,6},{5,7},{6,4},{7,5},{8,10},{9,11},{10,... | collective-permute-start | bytes 589832 | tf_op jit(solution)/shard_map/ppermute | solution.py:413
  9.1 0.2 collective-permute-start.4
  9.3 1.4 %shard_map.86 = (bf16[384,1024]{1,0:T(8,128)(2,1)S(1)}, bf16[384,1024]{1,0:T(8,128)(2,1)S(1)}, f32[384,128]{1,0:T(8,128)S(1)}) custom-call(bf16[384,1024]{1,0:T(8,128)(2,1)} %raw_ref.1), custom_call_target="tpu_custom_call" | custom-call | bytes 2555904 | tf_op jit(solution)/shard_map/pallas_call | solution.py:46
  10.7 1.6 %collective-permute-start.1 = (bf16[384,1024]{1,0:T(8,128)(2,1)}, bf16[384,1024]{1,0:T(8,128)(2,1)S(1)}, u32[]{:S(2)}, u32[]{:S(2)}) collective-permute-start(bf16[384,1024]{1,0:T(8,128)(2,1)} %raw_ref.1), channel_id=1, source_target_pairs={{0,8},{4,20},{8,0},{12,28},{16,24},{20,4},{24,16},{28,12},{1,9},{5... | collective-permute-start | bytes 2359304 | tf_op jit(solution)/shard_map/ppermute | solution.py:418
  13.6 1.1 %shard_map.87 = (f32[2,128]{1,0:T(2,128)S(1)}, f32[72,128]{1,0:T(8,128)S(1)}, s32[12,128]{1,0:T(8,128)S(1)}, s32[768,128]{1,0:T(8,128)S(1)}, f32[384,128]{1,0:T(8,128)S(1)}, /*index=5*/f32[4,128]{1,0:T(4,128)S(1)}) custom-call(f32[1]{0:T(128)S(6)} %copy.9.refs_0_, f32[1]{0:T(128)S(6)} %copy.10.refs_1_, s32[3,8,96]{2,1,0:T(8,128)S(1)} %bitcast.5, ...), custom_call_target="tpu_custom_call" | custom-call | bytes 743432 | tf_op jit(solution)/shard_map/pallas_call | solution.py:46
  14.7 0.7 %collective-permute-done.raw_ref = bf16[384,1024]{1,0:T(8,128)(2,1)S(1)} collective-permute-done((bf16[384,1024]{1,0:T(8,128)(2,1)}, bf16[384,1024]{1,0:T(8,128)(2,1)S(1)}, u32[]{:S(2)}, u32[]{:S(2)}) %collective-permute-start) | collective-permute-done | bytes 786464 | tf_op jit(solution)/shard_map/ppermute | solution.py:418
  15.4 3.3 %collective-permute-start.8 = (bf16[384,1024]{1,0:T(8,128)(2,1)S(1)}, bf16[384,1024]{1,0:T(8,128)(2,1)S(1)}, u32[]{:S(2)}, u32[]{:S(2)}) collective-permute-start(bf16[384,1024]{1,0:T(8,128)(2,1)S(1)} %collective-permute-done.raw_ref), channel_id=1, source_target_pairs={{0,8},{4,20},{8,0},{12,28},{16,24},{20,4},{24,16},{28,12},{1,9},{5... | collective-permute-start | bytes 2359304 | tf_op jit(solution)/shard_map/ppermute | solution.py:418
  18.7 0.2 shard_map.89.second_unit_ref
  19.0 2.8 %collective-permute-done.4.refs_3_.refs_4_ = bf16[384,256]{1,0:T(8,128)(2,1)S(1)} collective-permute-done((bf16[384,256]{1,0:T(8,128)(2,1)S(1)}, bf16[384,256]{1,0:T(8,128)(2,1)S(1)}, u32[]{:S(2)}, u32[]{:S(2)}) %collective-permute-start.4) | collective-permute-done | bytes 196640 | tf_op jit(solution)/shard_map/ppermute | solution.py:413
  21.8 0.0 collective-permute-done.2.refs_1_.refs_2_
  21.8 1.9 %collective-permute-done.3.refs_2_.refs_3_ = bf16[384,256]{1,0:T(8,128)(2,1)S(1)} collective-permute-done((bf16[384,256]{1,0:T(8,128)(2,1)S(1)}, bf16[384,256]{1,0:T(8,128)(2,1)S(1)}, u32[]{:S(2)}, u32[]{:S(2)}) %collective-permute-start.3) | collective-permute-done | bytes 196640 | tf_op jit(solution)/shard_map/ppermute | solution.py:413
  23.7 0.4 shard_map.90
  24.1 0.1 collective-permute-start.5
  24.2 0.5 collective-permute-start.6
  24.6 0.1 collective-permute-start.7
  24.7 0.0 collective-permute-done.1.first_ref
  24.7 0.3 shard_map.91.refs_8_.refs_7_
  25.0 1.8 %shard_map.92 = (bf16[384,384]{1,0:T(8,128)(2,1)S(1)}, bf16[384,768]{1,0:T(8,128)(2,1)S(1)}) custom-call(f32[2,128]{1,0:T(2,128)S(1)} %get-tuple-element.73.refs_0_, f32[72,128]{1,0:T(8,128)S(1)} %get-tuple-element.74.refs_1_, s32[12,128]{1,0:T(8,128)S(1)} %get-tuple-element.75.refs_2_, s32[768,128]{1,0:T(8,128)S(1)} %get-tuple-element.76.refs_3_, ...), custom_call_target="tpu_custom_call" | custom-call | bytes 4666368 | tf_op jit(solution)/shard_map/pallas_call | solution.py:46
  26.8 0.0 collective-permute-done.6.refs_10_
  26.8 0.0 collective-permute-done.7.refs_11_
  26.8 1.4 %shard_map.93 = (bf16[768,1024]{1,0:T(8,128)(2,1)S(1)}, bf16[768,384]{1,0:T(8,128)(2,1)S(1)}, bf16[384,1024]{1,0:T(8,128)(2,1)S(1)}) custom-call(f32[2,128]{1,0:T(2,128)S(1)} %get-tuple-element.73.refs_0_, f32[72,128]{1,0:T(8,128)S(1)} %get-tuple-element.74.refs_1_, s32[12,128]{1,0:T(8,128)S(1)} %get-tuple-element.75.refs_2_, ...), custom_call_target="tpu_custom_call" | custom-call | bytes 7320576 | tf_op jit(solution)/shard_map/pallas_call | solution.py:46
  28.2 0.9 %collective-permute-start.14 = (bf16[384,1024]{1,0:T(8,128)(2,1)S(1)}, bf16[384,1024]{1,0:T(8,128)(2,1)S(1)}, u32[]{:S(2)}, u32[]{:S(2)}) collective-permute-start(bf16[384,1024]{1,0:T(8,128)(2,1)S(1)} %get-tuple-element.122), channel_id=1, source_target_pairs={{0,8},{4,20},{8,0},{12,28},{16,24},{20,4},{24,16},{28,12},{1,9},{5... | collective-permute-start | bytes 2359304 | tf_op jit(solution)/shard_map/ppermute | solution.py:418
  29.2 2.5 %shard_map.94 = (bf16[768,384]{1,0:T(8,128)(2,1)S(1)}, f32[768,1024]{1,0:T(8,128)S(1)}, bf16[768,768]{1,0:T(8,128)(2,1)S(1)}) custom-call(f32[2,128]{1,0:T(2,128)S(1)} %get-tuple-element.73.refs_0_, f32[72,128]{1,0:T(8,128)S(1)} %get-tuple-element.74.refs_1_, s32[12,128]{1,0:T(8,128)S(1)} %get-tuple-element.75.refs_2_, ...), custom_call_target="tpu_custom_call" | custom-call | bytes 10957824 | tf_op jit(solution)/shard_map/pallas_call | solution.py:46
  31.7 1.6 %shard_map.95 = (bf16[768,768]{1,0:T(8,128)(2,1)S(1)}, bf16[768,1024]{1,0:T(8,128)(2,1)S(1)}) custom-call(f32[2,128]{1,0:T(2,128)S(1)} %get-tuple-element.73.refs_0_, f32[72,128]{1,0:T(8,128)S(1)} %get-tuple-element.74.refs_1_, s32[12,128]{1,0:T(8,128)S(1)} %get-tuple-element.75.refs_2_, s32[768,128]{1,0:T(8,128)S(1)} %get-tuple-element.76.refs_3_, ...), custom_call_target="tpu_custom_call" | custom-call | bytes 7123968 | tf_op jit(solution)/shard_map/pallas_call | solution.py:46
  33.2 0.8 %shard_map.96 = (bf16[192,1024]{1,0:T(8,128)(2,1)S(1)}, bf16[192,1024]{1,0:T(8,128)(2,1)S(1)}) custom-call(bf16[768,768]{1,0:T(8,128)(2,1)S(1)} %get-tuple-element.108.weight_ref, bf16[768,1024]{1,0:T(8,128)(2,1)S(1)} %get-tuple-element.106.image_ref, f32[768,1024]{1,0:T(8,128)S(1)} %get-tuple-element.104.acc_ref), custom_call_target="tpu_custom_call" | custom-call | bytes 6684672 | tf_op jit(solution)/shard_map/pallas_call | solution.py:46
  34.0 0.1 collective-permute-start.9
  34.1 0.5 collective-permute-start.10
  34.6 0.8 %shard_map.97.refs_5_ = f32[384,1024]{1,0:T(8,128)S(1)} custom-call(bf16[768,768]{1,0:T(8,128)(2,1)S(1)} %get-tuple-element.108.weight_ref, bf16[768,1024]{1,0:T(8,128)(2,1)S(1)} %get-tuple-element.106.image_ref, f32[768,1024]{1,0:T(8,128)S(1)} %get-tuple-element.104.acc_ref), custom_call_target="tpu_custom_call" | custom-call | bytes 7471104 | tf_op jit(solution)/shard_map/pallas_call | solution.py:46
  35.4 0.8 %shard_map.98 = (bf16[192,1024]{1,0:T(8,128)(2,1)S(1)}, bf16[192,1024]{1,0:T(8,128)(2,1)S(1)}) custom-call(bf16[768,768]{1,0:T(8,128)(2,1)S(1)} %get-tuple-element.108.weight_ref, bf16[768,1024]{1,0:T(8,128)(2,1)S(1)} %get-tuple-element.95.refs_6_.unit_ref), custom_call_target="tpu_custom_call" | custom-call | bytes 3538944 | tf_op jit(solution)/shard_map/pallas_call | solution.py:46
  36.2 1.3 %collective-permute-start.15 = (bf16[192,1024]{1,0:T(8,128)(2,1)S(1)}, bf16[192,1024]{1,0:T(8,128)(2,1)S(1)}, u32[]{:S(2)}, u32[]{:S(2)}) collective-permute-start(bf16[192,1024]{1,0:T(8,128)(2,1)S(1)} %get-tuple-element.126), channel_id=1, source_target_pairs={{0,8},{4,20},{8,0},{12,28},{16,24},{20,4},{24,16},{28,12},{1,9},{5... | collective-permute-start | bytes 1179656 | tf_op jit(solution)/shard_map/ppermute | solution.py:418
  37.5 0.8 %collective-permute-start.17 = (bf16[192,1024]{1,0:T(8,128)(2,1)S(1)}, bf16[192,1024]{1,0:T(8,128)(2,1)S(1)}, u32[]{:S(2)}, u32[]{:S(2)}) collective-permute-start(bf16[192,1024]{1,0:T(8,128)(2,1)S(1)} %get-tuple-element.127), channel_id=1, source_target_pairs={{0,8},{4,20},{8,0},{12,28},{16,24},{20,4},{24,16},{28,12},{1,9},{5... | collective-permute-start | bytes 1179656 | tf_op jit(solution)/shard_map/ppermute | solution.py:418
  38.3 0.6 shard_map.99
  38.9 3.4 %collective-permute-start.11 = (bf16[384,256]{1,0:T(8,128)(2,1)S(1)}, bf16[384,256]{1,0:T(8,128)(2,1)S(1)}, u32[]{:S(2)}, u32[]{:S(2)}) collective-permute-start(bf16[384,256]{1,0:T(8,128)(2,1)S(1)} %get-tuple-element.115), channel_id=1, source_target_pairs={{0,3},{1,2},{2,1},{3,0},{4,7},{5,6},{6,5},{7,4},{8,11},{9,10},{10,... | collective-permute-start | bytes 589832 | tf_op jit(solution)/shard_map/ppermute | solution.py:413
  42.4 1.5 %collective-permute-start.12 = (bf16[384,256]{1,0:T(8,128)(2,1)S(1)}, bf16[384,256]{1,0:T(8,128)(2,1)S(1)}, u32[]{:S(2)}, u32[]{:S(2)}) collective-permute-start(bf16[384,256]{1,0:T(8,128)(2,1)S(1)} %get-tuple-element.116), channel_id=1, source_target_pairs={{0,2},{1,3},{2,0},{3,1},{4,6},{5,7},{6,4},{7,5},{8,10},{9,11},{10,... | collective-permute-start | bytes 589832 | tf_op jit(solution)/shard_map/ppermute | solution.py:413
  43.9 0.1 collective-permute-start.13
  44.0 1.4 %shard_map.101 = (f32[384,1024]{1,0:T(8,128)S(1)}, f32[384,1024]{1,0:T(8,128)S(1)}) custom-call(bf16[768,384]{1,0:T(8,128)(2,1)S(1)} %get-tuple-element.120.refs_8_.own_weight_ref, bf16[768,768]{1,0:T(8,128)(2,1)S(1)} %get-tuple-element.121.near_weight_ref, bf16[768,1024]{1,0:T(8,128)(2,1)S(1)} %get-tuple-element.95.refs_6_.unit_ref, ...), custom_call_target="tpu_custom_call" | custom-call | flops 20000000000 | bytes 7274496 | tf_op jit(solution)/shard_map/pallas_call | solution.py:46
  45.4 0.1 shard_map.102
  45.5 0.9 %collective-permute-start.16 = (bf16[192,1024]{1,0:T(8,128)(2,1)S(1)}, bf16[192,1024]{1,0:T(8,128)(2,1)S(1)}, u32[]{:S(2)}, u32[]{:S(2)}) collective-permute-start(bf16[192,1024]{1,0:T(8,128)(2,1)S(1)} %shard_map.102), channel_id=1, source_target_pairs={{0,16},{4,12},{8,24},{12,4},{16,0},{20,28},{24,8},{28,20},{1,17},{... | collective-permute-start | bytes 1179656 | tf_op jit(solution)/shard_map/ppermute | solution.py:418
  46.5 3.4 %collective-permute-done.17.in_ref = bf16[192,1024]{1,0:T(8,128)(2,1)S(1)} collective-permute-done((bf16[192,1024]{1,0:T(8,128)(2,1)S(1)}, bf16[192,1024]{1,0:T(8,128)(2,1)S(1)}, u32[]{:S(2)}, u32[]{:S(2)}) %collective-permute-start.17) | collective-permute-done | bytes 393248 | tf_op jit(solution)/shard_map/ppermute | solution.py:418
  49.9 0.1 shard_map.103
  50.0 0.5 collective-permute-start.18
  50.5 9.3 %collective-permute-done.12.refs_2_ = bf16[384,256]{1,0:T(8,128)(2,1)S(1)} collective-permute-done((bf16[384,256]{1,0:T(8,128)(2,1)S(1)}, bf16[384,256]{1,0:T(8,128)(2,1)S(1)}, u32[]{:S(2)}, u32[]{:S(2)}) %collective-permute-start.12) | collective-permute-done | bytes 196640 | tf_op jit(solution)/shard_map/ppermute | solution.py:413
  59.8 0.9 %shard_map.100 = bf16[1536,256]{1,0:T(8,128)(2,1)} custom-call(bf16[384,256]{1,0:T(8,128)(2,1)S(1)} %get-tuple-element.114.refs_0_, bf16[384,256]{1,0:T(8,128)(2,1)S(1)} %collective-permute-done.11.refs_1_, bf16[384,256]{1,0:T(8,128)(2,1)S(1)} %collective-permute-done.12.refs_2_, bf16[384,256]{1,0:T(8,128)(2,1)S(1)} %collective-permute-done.13.refs_3_), custom_call_target="tpu_custom_call" | custom-call | flops 20000000000 | bytes 1572864 | tf_op jit(solution)/shard_map/pallas_call | solution.py:46
  60.7 1.4 %shard_map.104 = bf16[384,1024]{1,0:T(8,128)(2,1)} custom-call(bf16[384,1024]{1,0:T(8,128)(2,1)S(1)} %get-tuple-element.118.raw_ref, f32[384,128]{1,0:T(8,128)S(1)} %get-tuple-element.119.scale_ref, f32[384,1024]{1,0:T(8,128)S(1)} %get-tuple-element.124.sum_ref, bf16[192,1024]{1,0:T(8,128)(2,1)S(1)} %collective-permute-done.16.refs_0_, ...), custom_call_target="tpu_custom_call" | custom-call | bytes 4128768 | tf_op jit(solution)/shard_map/pallas_call | solution.py:46
  (17 shorter events, 0.0 us)
Async XLA Ops:
  0.6 14.8 %collective-permute-start = (bf16[384,1024]{1,0:T(8,128)(2,1)}, bf16[384,1024]{1,0:T(8,128)(2,1)S(1)}, u32[]{:S(2)}, u32[]{:S(2)}) collective-permute-start(bf16[384,1024]{1,0:T(8,128)(2,1)} %raw_ref.1), channel_id=1, source_target_pairs={{0,16},{4,12},{8,24},{12,4},{16,0},{20,28},{24,8},{28,20},{1,17},{... | collective-permute-start | bytes 2359304 | tf_op jit(solution)/shard_map/ppermute | solution.py:418
  3.7 1.1 %copy-start = (bf16[1536,256]{1,0:T(8,128)(2,1)S(1)}, bf16[1536,256]{1,0:T(8,128)(2,1)}, u32[]{:S(2)}) copy-start(bf16[1536,256]{1,0:T(8,128)(2,1)} %text_ref.1) | copy-start | bytes 2359300
  4.8 8.8 %copy-start.1 = (s32[12288]{0:T(1024)S(1)}, s32[12288]{0:T(1024)}, u32[]{:S(2)}) copy-start(s32[12288]{0:T(1024)} %param.11) | copy-start | bytes 147460
  4.8 8.8 %copy-start.2 = (s32[12288]{0:T(1024)S(1)}, s32[12288]{0:T(1024)}, u32[]{:S(2)}) copy-start(s32[12288]{0:T(1024)} %param.12) | copy-start | bytes 147460
  4.8 8.8 %copy-start.3 = (s32[96,8,3]{0,1,2:T(8,128)S(1)}, s32[96,8,3]{0,1,2:T(8,128)}, u32[]{:S(2)}) copy-start(s32[96,8,3]{0,1,2:T(8,128)} %param.13) | copy-start | bytes 27652
  4.9 17.0 %collective-permute-start.2 = (bf16[384,256]{1,0:T(8,128)(2,1)S(1)}, bf16[384,256]{1,0:T(8,128)(2,1)S(1)}, u32[]{:S(2)}, u32[]{:S(2)}) collective-permute-start(bf16[384,256]{1,0:T(8,128)(2,1)S(1)} %get-tuple-element.81), channel_id=1, source_target_pairs={{0,1},{1,0},{2,3},{3,2},{4,5},{5,4},{6,7},{7,6},{8,9},{9,8},{10,11... | collective-permute-start | bytes 589832 | tf_op jit(solution)/shard_map/ppermute | solution.py:413
  6.5 17.2 %collective-permute-start.3 = (bf16[384,256]{1,0:T(8,128)(2,1)S(1)}, bf16[384,256]{1,0:T(8,128)(2,1)S(1)}, u32[]{:S(2)}, u32[]{:S(2)}) collective-permute-start(bf16[384,256]{1,0:T(8,128)(2,1)S(1)} %get-tuple-element.82), channel_id=1, source_target_pairs={{0,2},{1,3},{2,0},{3,1},{4,6},{5,7},{6,4},{7,5},{8,10},{9,11},{10,... | collective-permute-start | bytes 589832 | tf_op jit(solution)/shard_map/ppermute | solution.py:413
  9.1 12.7 %collective-permute-start.4 = (bf16[384,256]{1,0:T(8,128)(2,1)S(1)}, bf16[384,256]{1,0:T(8,128)(2,1)S(1)}, u32[]{:S(2)}, u32[]{:S(2)}) collective-permute-start(bf16[384,256]{1,0:T(8,128)(2,1)S(1)} %get-tuple-element.83), channel_id=1, source_target_pairs={{0,3},{1,2},{2,1},{3,0},{4,7},{5,6},{6,5},{7,4},{8,11},{9,10},{10,... | collective-permute-start | bytes 589832 | tf_op jit(solution)/shard_map/ppermute | solution.py:413
  10.7 14.0 %collective-permute-start.1 = (bf16[384,1024]{1,0:T(8,128)(2,1)}, bf16[384,1024]{1,0:T(8,128)(2,1)S(1)}, u32[]{:S(2)}, u32[]{:S(2)}) collective-permute-start(bf16[384,1024]{1,0:T(8,128)(2,1)} %raw_ref.1), channel_id=1, source_target_pairs={{0,8},{4,20},{8,0},{12,28},{16,24},{20,4},{24,16},{28,12},{1,9},{5... | collective-permute-start | bytes 2359304 | tf_op jit(solution)/shard_map/ppermute | solution.py:418
  15.4 16.2 %collective-permute-start.8 = (bf16[384,1024]{1,0:T(8,128)(2,1)S(1)}, bf16[384,1024]{1,0:T(8,128)(2,1)S(1)}, u32[]{:S(2)}, u32[]{:S(2)}) collective-permute-start(bf16[384,1024]{1,0:T(8,128)(2,1)S(1)} %collective-permute-done.raw_ref), channel_id=1, source_target_pairs={{0,8},{4,20},{8,0},{12,28},{16,24},{20,4},{24,16},{28,12},{1,9},{5... | collective-permute-start | bytes 2359304 | tf_op jit(solution)/shard_map/ppermute | solution.py:418
  24.1 2.7 %collective-permute-start.5 = (bf16[128,1024]{1,0:T(8,128)(2,1)S(1)}, bf16[128,1024]{1,0:T(8,128)(2,1)S(1)}, u32[]{:S(2)}, u32[]{:S(2)}) collective-permute-start(bf16[128,1024]{1,0:T(8,128)(2,1)S(1)} %get-tuple-element.92), channel_id=1, source_target_pairs={{0,4},{4,0},{8,12},{12,8},{16,20},{20,16},{24,28},{28,24},{1,5},{5... | collective-permute-start | bytes 786440 | tf_op jit(solution)/shard_map/ppermute | solution.py:413
  24.2 2.7 %collective-permute-start.6 = (bf16[128,1024]{1,0:T(8,128)(2,1)S(1)}, bf16[128,1024]{1,0:T(8,128)(2,1)S(1)}, u32[]{:S(2)}, u32[]{:S(2)}) collective-permute-start(bf16[128,1024]{1,0:T(8,128)(2,1)S(1)} %get-tuple-element.93), channel_id=1, source_target_pairs={{0,4},{4,0},{8,12},{12,8},{16,20},{20,16},{24,28},{28,24},{1,5},{5... | collective-permute-start | bytes 786440 | tf_op jit(solution)/shard_map/ppermute | solution.py:413
  24.6 2.2 %collective-permute-start.7 = (bf16[128,1024]{1,0:T(8,128)(2,1)S(1)}, bf16[128,1024]{1,0:T(8,128)(2,1)S(1)}, u32[]{:S(2)}, u32[]{:S(2)}) collective-permute-start(bf16[128,1024]{1,0:T(8,128)(2,1)S(1)} %get-tuple-element.94), channel_id=1, source_target_pairs={{0,4},{4,0},{8,12},{12,8},{16,20},{20,16},{24,28},{28,24},{1,5},{5... | collective-permute-start | bytes 786440 | tf_op jit(solution)/shard_map/ppermute | solution.py:413
  28.2 15.6 %collective-permute-start.14 = (bf16[384,1024]{1,0:T(8,128)(2,1)S(1)}, bf16[384,1024]{1,0:T(8,128)(2,1)S(1)}, u32[]{:S(2)}, u32[]{:S(2)}) collective-permute-start(bf16[384,1024]{1,0:T(8,128)(2,1)S(1)} %get-tuple-element.122), channel_id=1, source_target_pairs={{0,8},{4,20},{8,0},{12,28},{16,24},{20,4},{24,16},{28,12},{1,9},{5... | collective-permute-start | bytes 2359304 | tf_op jit(solution)/shard_map/ppermute | solution.py:418
  34.0 4.3 %collective-permute-start.9 = (bf16[192,1024]{1,0:T(8,128)(2,1)S(1)}, bf16[192,1024]{1,0:T(8,128)(2,1)S(1)}, u32[]{:S(2)}, u32[]{:S(2)}) collective-permute-start(bf16[192,1024]{1,0:T(8,128)(2,1)S(1)} %get-tuple-element.111), channel_id=1, source_target_pairs={{0,4},{4,0},{8,12},{12,8},{16,20},{20,16},{24,28},{28,24},{1,5},{5... | collective-permute-start | bytes 1179656 | tf_op jit(solution)/shard_map/ppermute | solution.py:413
  34.1 4.2 %collective-permute-start.10 = (bf16[192,1024]{1,0:T(8,128)(2,1)S(1)}, bf16[192,1024]{1,0:T(8,128)(2,1)S(1)}, u32[]{:S(2)}, u32[]{:S(2)}) collective-permute-start(bf16[192,1024]{1,0:T(8,128)(2,1)S(1)} %get-tuple-element.112), channel_id=1, source_target_pairs={{0,4},{4,0},{8,12},{12,8},{16,20},{20,16},{24,28},{28,24},{1,5},{5... | collective-permute-start | bytes 1179656 | tf_op jit(solution)/shard_map/ppermute | solution.py:413
  36.2 9.2 %collective-permute-start.15 = (bf16[192,1024]{1,0:T(8,128)(2,1)S(1)}, bf16[192,1024]{1,0:T(8,128)(2,1)S(1)}, u32[]{:S(2)}, u32[]{:S(2)}) collective-permute-start(bf16[192,1024]{1,0:T(8,128)(2,1)S(1)} %get-tuple-element.126), channel_id=1, source_target_pairs={{0,8},{4,20},{8,0},{12,28},{16,24},{20,4},{24,16},{28,12},{1,9},{5... | collective-permute-start | bytes 1179656 | tf_op jit(solution)/shard_map/ppermute | solution.py:418
  37.5 12.3 %collective-permute-start.17 = (bf16[192,1024]{1,0:T(8,128)(2,1)S(1)}, bf16[192,1024]{1,0:T(8,128)(2,1)S(1)}, u32[]{:S(2)}, u32[]{:S(2)}) collective-permute-start(bf16[192,1024]{1,0:T(8,128)(2,1)S(1)} %get-tuple-element.127), channel_id=1, source_target_pairs={{0,8},{4,20},{8,0},{12,28},{16,24},{20,4},{24,16},{28,12},{1,9},{5... | collective-permute-start | bytes 1179656 | tf_op jit(solution)/shard_map/ppermute | solution.py:418
  38.9 11.6 %collective-permute-start.11 = (bf16[384,256]{1,0:T(8,128)(2,1)S(1)}, bf16[384,256]{1,0:T(8,128)(2,1)S(1)}, u32[]{:S(2)}, u32[]{:S(2)}) collective-permute-start(bf16[384,256]{1,0:T(8,128)(2,1)S(1)} %get-tuple-element.115), channel_id=1, source_target_pairs={{0,3},{1,2},{2,1},{3,0},{4,7},{5,6},{6,5},{7,4},{8,11},{9,10},{10,... | collective-permute-start | bytes 589832 | tf_op jit(solution)/shard_map/ppermute | solution.py:413
  42.4 17.4 %collective-permute-start.12 = (bf16[384,256]{1,0:T(8,128)(2,1)S(1)}, bf16[384,256]{1,0:T(8,128)(2,1)S(1)}, u32[]{:S(2)}, u32[]{:S(2)}) collective-permute-start(bf16[384,256]{1,0:T(8,128)(2,1)S(1)} %get-tuple-element.116), channel_id=1, source_target_pairs={{0,2},{1,3},{2,0},{3,1},{4,6},{5,7},{6,4},{7,5},{8,10},{9,11},{10,... | collective-permute-start | bytes 589832 | tf_op jit(solution)/shard_map/ppermute | solution.py:413
  43.9 15.9 %collective-permute-start.13 = (bf16[384,256]{1,0:T(8,128)(2,1)S(1)}, bf16[384,256]{1,0:T(8,128)(2,1)S(1)}, u32[]{:S(2)}, u32[]{:S(2)}) collective-permute-start(bf16[384,256]{1,0:T(8,128)(2,1)S(1)} %get-tuple-element.117), channel_id=1, source_target_pairs={{0,1},{1,0},{2,3},{3,2},{4,5},{5,4},{6,7},{7,6},{8,9},{9,8},{10,11... | collective-permute-start | bytes 589832 | tf_op jit(solution)/shard_map/ppermute | solution.py:413
  45.5 15.1 %collective-permute-start.16 = (bf16[192,1024]{1,0:T(8,128)(2,1)S(1)}, bf16[192,1024]{1,0:T(8,128)(2,1)S(1)}, u32[]{:S(2)}, u32[]{:S(2)}) collective-permute-start(bf16[192,1024]{1,0:T(8,128)(2,1)S(1)} %shard_map.102), channel_id=1, source_target_pairs={{0,16},{4,12},{8,24},{12,4},{16,0},{20,28},{24,8},{28,20},{1,17},{... | collective-permute-start | bytes 1179656 | tf_op jit(solution)/shard_map/ppermute | solution.py:418
  50.0 10.7 %collective-permute-start.18 = (bf16[192,1024]{1,0:T(8,128)(2,1)S(1)}, bf16[192,1024]{1,0:T(8,128)(2,1)S(1)}, u32[]{:S(2)}, u32[]{:S(2)}) collective-permute-start(bf16[192,1024]{1,0:T(8,128)(2,1)S(1)} %shard_map.103), channel_id=1, source_target_pairs={{0,16},{4,12},{8,24},{12,4},{16,0},{20,28},{24,8},{28,20},{1,17},{... | collective-permute-start | bytes 1179656 | tf_op jit(solution)/shard_map/ppermute | solution.py:418

commit v8 on v7

--- a/solution.py
+++ b/solution.py
@@ -91,7 +91,8 @@
     place = lax.axis_index("tp")
     rows = out_refs[0].shape[0]
     for k, out_ref in enumerate(out_refs):
-        out_ref[...] = text_ref[pl.ds(pl.multiple_of((place ^ k) * rows, rows), rows), :]
+        peer = place ^ far_first(k, len(out_refs))
+        out_ref[...] = text_ref[pl.ds(pl.multiple_of(peer * rows, rows), rows), :]
 
 
 def unit_text_body(chunks, *refs):
@@ -105,7 +106,7 @@
         scales = row_scales(sum(jnp.sum(x * x, axis=-1, keepdims=True) for x in parts))
         scale_ref[part, :] = jnp.broadcast_to(scales, (TILE, TILE))
         for k, x in enumerate(parts):
-            unit_ref[part, feature_slice(place ^ k, width)] = (x * scales).astype(jnp.bfloat16)
+            unit_ref[part, feature_slice(place ^ far_first(k, chunks), width)] = (x * scales).astype(jnp.bfloat16)
     split_rows(unit_ref, piece_refs)
 
 
@@ -358,36 +359,33 @@
         raws = [ref[part, :].astype(jnp.float32) for ref in raw_refs]
         accs = []
         for k in range(chunks):
-            features = feature_slice(place ^ k, width)
+            features = feature_slice(place ^ far_first(k, chunks), width)
             added = add_refs[first // size][pl.ds(first % size, TILE // 2), features]
             accs.append(acc_ref[part, features] + added.astype(jnp.float32))
         inner = sum(jnp.sum(x * a, axis=-1, keepdims=True) for x, a in zip(raws, accs))
         inner = inner * scales * scales
         for k in range(chunks):
-            out_refs[far_first(k, chunks)][part, :] = (
-                scales * (accs[k] - raws[k] * inner)
-            ).astype(jnp.bfloat16)
-
-
-def place_text_body(chunks, *refs):
-    part_refs, out_ref, sems = refs[:chunks], refs[chunks], refs[chunks + 1]
+            out_refs[k][part, :] = (scales * (accs[k] - raws[k] * inner)).astype(jnp.bfloat16)
+
+
+def arrived_body(*refs):
+    out_ref = refs[-1]
+    out_ref[...] = sum(ref[: out_ref.shape[0], : out_ref.shape[1]] for ref in refs[:-1])
+
+
+def finish_body(chunks, adds, *refs):
+    part_refs, (raw_ref, scale_ref, sum_ref) = refs[:chunks], refs[chunks : chunks + 3]
+    piece_refs = refs[chunks + 3 : chunks + 3 + adds]
+    text_ref, image_ref, grad_ref, sems = refs[-4:]
     place = lax.axis_index("tp")
     rows = part_refs[0].shape[0]
     copies = []
     for k in range(chunks):
         peer = place ^ far_first(k, chunks)
         block = pl.ds(pl.multiple_of(peer * rows, rows), rows)
-        copies.append(pltpu.make_async_copy(part_refs[k], out_ref.at[block, :], sems.at[k]))
-    for copy in copies:
-        copy.start()
-    for copy in copies:
-        copy.wait()
-
-
-def image_grad_body(piece_count, raw_ref, scale_ref, sum_ref, *refs):
-    piece_refs, (out_ref, grad_ref, sems) = refs[:piece_count], refs[piece_count:]
-    copies = []
-    for block in range(raw_ref.shape[0] // TILE):
+        copies.append(pltpu.make_async_copy(part_refs[k], text_ref.at[block, :], sems.at[k]))
+        copies[-1].start()
+    for block in range(rows // TILE):
         for first in range(block * TILE, (block + 1) * TILE, TILE // 2):
             part = pl.ds(first, TILE // 2)
             raw = raw_ref[part, :].astype(jnp.float32)
@@ -401,7 +399,9 @@
             grad_ref[part, :] = (scales * (acc - raw * inner)).astype(jnp.bfloat16)
         part = pl.ds(block * TILE, TILE)
         copies.append(
-            pltpu.make_async_copy(grad_ref.at[part, :], out_ref.at[part, :], sems.at[block])
+            pltpu.make_async_copy(
+                grad_ref.at[part, :], image_ref.at[part, :], sems.at[chunks + block]
+            )
         )
         copies[-1].start()
     for copy in copies:
@@ -416,6 +416,11 @@
 def swap_near(value, which):
     count = lax.axis_size("blk")
     return lax.ppermute(value, "blk", [(i, i ^ neighbour_bits(i)[which]) for i in range(count)])
+
+
+def swap_chunks(chunks):
+    count = len(chunks)
+    return chunks[:1] + [swap(chunks[k], "tp", far_first(k, count)) for k in range(1, count)]
 
 
 def per_device(text_emb, image_emb, logit_scale, logit_bias, bucket, positive, blocks):
@@ -437,7 +442,7 @@
         return struct((count, columns), jnp.int32)
 
     picked = call_kernel(pick_body, [bf16(rows, width)] * groups, [text_emb], limit=8)
-    text_raw = picked[:1] + [swap(picked[k], "tp", k) for k in range(1, groups)]
+    text_raw = swap_chunks(picked)
     if square:
         from_second = swap_near(image_emb, 1)
     else:
@@ -503,30 +508,29 @@
             [text_scales] + text_raw + [acc_own] + [swap(piece, "blk", 1) for piece in acc_other],
             limit=16,
         )
-        return parts[:1] + [
-            swap(parts[k], "tp", far_first(k, groups)) for k in range(1, groups)
-        ]
-
-    def place_text(text_parts):
-        return call_kernel(
-            functools.partial(place_text_body, groups),
-            [bf16(groups * rows, width)],
-            text_parts,
-            outs_anywhere=True,
-            scratch=[pltpu.SemaphoreType.DMA((groups,))],
+        return swap_chunks(parts)
+
+    def finish(text_parts, total, pieces):
+        arrived = call_kernel(
+            arrived_body,
+            [struct((16, TILE), jnp.bfloat16)],
+            text_parts[1:],
             flops=WAIT_FLOPS,
             limit=8,
-        )[0]
-
-    def finish_image(total, pieces):
-        return call_kernel(
-            functools.partial(image_grad_body, len(pieces)),
-            [bf16(rows)],
-            [image_raw, image_scales, total] + pieces,
-            outs_anywhere=True,
-            scratch=[pltpu.VMEM((rows, embed), jnp.bfloat16), pltpu.SemaphoreType.DMA((tiles,))],
-            limit=8,
-        )[0]
+        )
+        return tuple(
+            call_kernel(
+                functools.partial(finish_body, groups, len(pieces)),
+                [bf16(groups * rows, width), bf16(rows)],
+                text_parts + [image_raw, image_scales, total] + pieces + arrived,
+                outs_anywhere=True,
+                scratch=[
+                    pltpu.VMEM((rows, embed), jnp.bfloat16),
+                    pltpu.SemaphoreType.DMA((groups + tiles,)),
+                ],
+                limit=8,
+            )
+        )
 
     if not square:
         columns = gathered.shape[0]
@@ -546,7 +550,7 @@
             spread, "blk", split_axis=0, concat_axis=0, tiled=True, axis_index_groups=same_core
         )
         total = jnp.sum(parts.reshape(-1, rows, embed).astype(jnp.float32), axis=0)
-        return (place_text(text_parts), finish_image(total, []))
+        return finish(text_parts, total, [])
 
     own_weights, near_weights = call_kernel(
         functools.partial(near_own_body, tiles),
@@ -610,9 +614,7 @@
             limit=8,
         )[0]
         image_last.append(swap_near(relayed, 1))
-    text_grad = place_text(text_parts)
-    base, _ = lax.optimization_barrier((base, text_grad))
-    return (text_grad, finish_image(base, image_last))
+    return finish(text_parts, base, image_last)
 
 
 def solution(mesh):

time: 62.3 us -> 61.4 us (0.986)
  waiting for transfers between devices: 18.1 us -> 17 us
  starting transfers between devices: 23.1 us -> 24 us
  Pallas kernels: 17.6 us -> 16.9 us
    ppermute x11, waiting for transfers between devices: 14 us -> 11.6 us  [swap(): return lax.ppermute(value, axis, [(i, i ^ bits) for i in range(count)])]
    ppermute x8, waiting for transfers between devices: 4.11 us -> 5.4 us  [swap_near(): lax.ppermute(value, 'blk', [(i, i ^ neighbour_bits(i)[which]) for i in ra...]
    ppermute x8, starting transfers between devices: 12.4 us -> 13.2 us  [swap_near(): lax.ppermute(value, 'blk', [(i, i ^ neighbour_bits(i)[which]) for i in ra...]
    pallas_call x19, Pallas kernels: 17.6 us -> 16.9 us  [call_kernel(): pl.pallas_call(body, out_shape=outs, in_specs=specs, out_specs=[ANY_SPEC...]
  transfers between devices with their start and end apart: 19 -> 19, of which waited for: 5 -> 6; matrix products, arithmetic and copies ran while one was open for 0% -> 0% of each run, Pallas kernels for 26% -> 25%
where the time goes in v8:
time: 61.4 us; the launch traced here: 61.2 us
  starting transfers between devices  24 us (39%)
  waiting for transfers between devices  17 us (28%)
  Pallas kernels  16.9 us (28%)
  between operations  2.12 us (3%)
  local copies, waits for them, and re-layouts  1.14 us (2%)
    pallas_call x19, Pallas kernels, call_kernel(): pl.pallas_call(body, out_shape=outs, in_specs=specs, out_specs=[ANY_SPEC...  16.9 us
    ppermute x8, starting transfers between devices, swap_near(): lax.ppermute(value, 'blk', [(i, i ^ neighbour_bits(i)[which]) for i in ra...  13.2 us
    ppermute x11, waiting for transfers between devices, swap(): return lax.ppermute(value, axis, [(i, i ^ bits) for i in range(count)])  11.6 us
    ppermute x11, starting transfers between devices, swap(): return lax.ppermute(value, axis, [(i, i ^ bits) for i in range(count)])  10.8 us
    ppermute x8, waiting for transfers between devices, swap_near(): lax.ppermute(value, 'blk', [(i, i ^ neighbour_bits(i)[which]) for i in ra...  5.4 us
  transfers between devices with their start and end apart: 19, of which 6 were waited for; matrix products, arithmetic and copies ran while one was open for 0% of the time, Pallas kernels for 25%

profile of v8, /device:TPU:0, one launch (start us, length us, event | category | flops | bytes accessed | tf_op | source)
XLA Modules:
  0.0 61.2 jit_solution(7945157442309779180)
XLA Ops:
  0.6 3.0 %collective-permute-start = (bf16[384,1024]{1,0:T(8,128)(2,1)}, bf16[384,1024]{1,0:T(8,128)(2,1)S(1)}, u32[]{:S(2)}, u32[]{:S(2)}) collective-permute-start(bf16[384,1024]{1,0:T(8,128)(2,1)} %raw_ref.1), channel_id=1, source_target_pairs={{0,16},{4,12},{8,24},{12,4},{16,0},{20,28},{24,8},{28,20},{1,17},{... | collective-permute-start | bytes 2359304 | tf_op jit(solution)/shard_map/ppermute | solution.py:418
  3.7 1.1 %copy-done = bf16[1536,256]{1,0:T(8,128)(2,1)S(1)} copy-done((bf16[1536,256]{1,0:T(8,128)(2,1)S(1)}, bf16[1536,256]{1,0:T(8,128)(2,1)}, u32[]{:S(2)}) %copy-start) | copy-done | bytes 786456
  4.8 0.1 shard_map.88
  4.9 3.7 %collective-permute-start.2 = (bf16[384,256]{1,0:T(8,128)(2,1)S(1)}, bf16[384,256]{1,0:T(8,128)(2,1)S(1)}, u32[]{:S(2)}, u32[]{:S(2)}) collective-permute-start(bf16[384,256]{1,0:T(8,128)(2,1)S(1)} %get-tuple-element.80), channel_id=1, source_target_pairs={{0,3},{1,2},{2,1},{3,0},{4,7},{5,6},{6,5},{7,4},{8,11},{9,10},{10,... | collective-permute-start | bytes 589832 | tf_op jit(solution)/shard_map/ppermute | solution.py:413
  8.5 0.0 collective-permute-start.3
  8.5 0.8 %collective-permute-start.4 = (bf16[384,256]{1,0:T(8,128)(2,1)S(1)}, bf16[384,256]{1,0:T(8,128)(2,1)S(1)}, u32[]{:S(2)}, u32[]{:S(2)}) collective-permute-start(bf16[384,256]{1,0:T(8,128)(2,1)S(1)} %get-tuple-element.82), channel_id=1, source_target_pairs={{0,1},{1,0},{2,3},{3,2},{4,5},{5,4},{6,7},{7,6},{8,9},{9,8},{10,11... | collective-permute-start | bytes 589832 | tf_op jit(solution)/shard_map/ppermute | solution.py:413
  9.3 1.4 %shard_map.86 = (bf16[384,1024]{1,0:T(8,128)(2,1)S(1)}, bf16[384,1024]{1,0:T(8,128)(2,1)S(1)}, f32[384,128]{1,0:T(8,128)S(1)}) custom-call(bf16[384,1024]{1,0:T(8,128)(2,1)} %raw_ref.1), custom_call_target="tpu_custom_call" | custom-call | bytes 2555904 | tf_op jit(solution)/shard_map/pallas_call | solution.py:46
  10.7 1.6 %collective-permute-start.1 = (bf16[384,1024]{1,0:T(8,128)(2,1)}, bf16[384,1024]{1,0:T(8,128)(2,1)S(1)}, u32[]{:S(2)}, u32[]{:S(2)}) collective-permute-start(bf16[384,1024]{1,0:T(8,128)(2,1)} %raw_ref.1), channel_id=1, source_target_pairs={{0,8},{4,20},{8,0},{12,28},{16,24},{20,4},{24,16},{28,12},{1,9},{5... | collective-permute-start | bytes 2359304 | tf_op jit(solution)/shard_map/ppermute | solution.py:418
  13.6 1.1 %shard_map.87 = (f32[2,128]{1,0:T(2,128)S(1)}, f32[72,128]{1,0:T(8,128)S(1)}, s32[12,128]{1,0:T(8,128)S(1)}, s32[768,128]{1,0:T(8,128)S(1)}, f32[384,128]{1,0:T(8,128)S(1)}, /*index=5*/f32[4,128]{1,0:T(4,128)S(1)}) custom-call(f32[1]{0:T(128)S(6)} %copy.9.refs_0_, f32[1]{0:T(128)S(6)} %copy.10.refs_1_, s32[3,8,96]{2,1,0:T(8,128)S(1)} %bitcast.5, ...), custom_call_target="tpu_custom_call" | custom-call | bytes 743432 | tf_op jit(solution)/shard_map/pallas_call | solution.py:46
  14.7 0.6 %collective-permute-done.raw_ref = bf16[384,1024]{1,0:T(8,128)(2,1)S(1)} collective-permute-done((bf16[384,1024]{1,0:T(8,128)(2,1)}, bf16[384,1024]{1,0:T(8,128)(2,1)S(1)}, u32[]{:S(2)}, u32[]{:S(2)}) %collective-permute-start) | collective-permute-done | bytes 786464 | tf_op jit(solution)/shard_map/ppermute | solution.py:418
  15.3 3.3 %collective-permute-start.8 = (bf16[384,1024]{1,0:T(8,128)(2,1)S(1)}, bf16[384,1024]{1,0:T(8,128)(2,1)S(1)}, u32[]{:S(2)}, u32[]{:S(2)}) collective-permute-start(bf16[384,1024]{1,0:T(8,128)(2,1)S(1)} %collective-permute-done.raw_ref), channel_id=1, source_target_pairs={{0,8},{4,20},{8,0},{12,28},{16,24},{20,4},{24,16},{28,12},{1,9},{5... | collective-permute-start | bytes 2359304 | tf_op jit(solution)/shard_map/ppermute | solution.py:418
  18.6 0.2 shard_map.89.second_unit_ref
  18.9 2.0 %collective-permute-done.4.refs_3_.refs_4_ = bf16[384,256]{1,0:T(8,128)(2,1)S(1)} collective-permute-done((bf16[384,256]{1,0:T(8,128)(2,1)S(1)}, bf16[384,256]{1,0:T(8,128)(2,1)S(1)}, u32[]{:S(2)}, u32[]{:S(2)}) %collective-permute-start.4) | collective-permute-done | bytes 196640 | tf_op jit(solution)/shard_map/ppermute | solution.py:413
  20.9 0.0 collective-permute-done.2.refs_1_.refs_2_
  20.9 4.0 %collective-permute-done.3.refs_2_.refs_3_ = bf16[384,256]{1,0:T(8,128)(2,1)S(1)} collective-permute-done((bf16[384,256]{1,0:T(8,128)(2,1)S(1)}, bf16[384,256]{1,0:T(8,128)(2,1)S(1)}, u32[]{:S(2)}, u32[]{:S(2)}) %collective-permute-start.3) | collective-permute-done | bytes 196640 | tf_op jit(solution)/shard_map/ppermute | solution.py:413
  24.9 0.4 shard_map.90
  25.3 0.1 collective-permute-start.5
  25.4 0.5 collective-permute-start.6
  25.9 0.1 collective-permute-start.7
  26.0 0.3 shard_map.91.refs_8_.refs_7_
  26.3 1.8 %shard_map.92 = (bf16[384,384]{1,0:T(8,128)(2,1)S(1)}, bf16[384,768]{1,0:T(8,128)(2,1)S(1)}) custom-call(f32[2,128]{1,0:T(2,128)S(1)} %get-tuple-element.72.refs_0_, f32[72,128]{1,0:T(8,128)S(1)} %get-tuple-element.73.refs_1_, s32[12,128]{1,0:T(8,128)S(1)} %get-tuple-element.74.refs_2_, s32[768,128]{1,0:T(8,128)S(1)} %get-tuple-element.75.refs_3_, ...), custom_call_target="tpu_custom_call" | custom-call | bytes 4666368 | tf_op jit(solution)/shard_map/pallas_call | solution.py:46
  28.0 0.0 collective-permute-done.5.refs_9_
  28.1 0.0 collective-permute-done.6.refs_10_
  28.1 1.4 %shard_map.93 = (bf16[768,1024]{1,0:T(8,128)(2,1)S(1)}, bf16[768,384]{1,0:T(8,128)(2,1)S(1)}, bf16[384,1024]{1,0:T(8,128)(2,1)S(1)}) custom-call(f32[2,128]{1,0:T(2,128)S(1)} %get-tuple-element.72.refs_0_, f32[72,128]{1,0:T(8,128)S(1)} %get-tuple-element.73.refs_1_, s32[12,128]{1,0:T(8,128)S(1)} %get-tuple-element.74.refs_2_, ...), custom_call_target="tpu_custom_call" | custom-call | bytes 7320576 | tf_op jit(solution)/shard_map/pallas_call | solution.py:46
  29.5 0.6 collective-permute-start.14
  30.1 2.5 %shard_map.94 = (bf16[768,384]{1,0:T(8,128)(2,1)S(1)}, f32[768,1024]{1,0:T(8,128)S(1)}, bf16[768,768]{1,0:T(8,128)(2,1)S(1)}) custom-call(f32[2,128]{1,0:T(2,128)S(1)} %get-tuple-element.72.refs_0_, f32[72,128]{1,0:T(8,128)S(1)} %get-tuple-element.73.refs_1_, s32[12,128]{1,0:T(8,128)S(1)} %get-tuple-element.74.refs_2_, ...), custom_call_target="tpu_custom_call" | custom-call | bytes 10957824 | tf_op jit(solution)/shard_map/pallas_call | solution.py:46
  32.6 1.6 %shard_map.95 = (bf16[768,768]{1,0:T(8,128)(2,1)S(1)}, bf16[768,1024]{1,0:T(8,128)(2,1)S(1)}) custom-call(f32[2,128]{1,0:T(2,128)S(1)} %get-tuple-element.72.refs_0_, f32[72,128]{1,0:T(8,128)S(1)} %get-tuple-element.73.refs_1_, s32[12,128]{1,0:T(8,128)S(1)} %get-tuple-element.74.refs_2_, s32[768,128]{1,0:T(8,128)S(1)} %get-tuple-element.75.refs_3_, ...), custom_call_target="tpu_custom_call" | custom-call | bytes 7123968 | tf_op jit(solution)/shard_map/pallas_call | solution.py:46
  34.1 0.8 %shard_map.96 = (bf16[192,1024]{1,0:T(8,128)(2,1)S(1)}, bf16[192,1024]{1,0:T(8,128)(2,1)S(1)}) custom-call(bf16[768,768]{1,0:T(8,128)(2,1)S(1)} %get-tuple-element.107.weight_ref, bf16[768,1024]{1,0:T(8,128)(2,1)S(1)} %get-tuple-element.105.image_ref, f32[768,1024]{1,0:T(8,128)S(1)} %get-tuple-element.103.acc_ref), custom_call_target="tpu_custom_call" | custom-call | bytes 6684672 | tf_op jit(solution)/shard_map/pallas_call | solution.py:46
  34.9 1.2 %collective-permute-start.9 = (bf16[192,1024]{1,0:T(8,128)(2,1)S(1)}, bf16[192,1024]{1,0:T(8,128)(2,1)S(1)}, u32[]{:S(2)}, u32[]{:S(2)}) collective-permute-start(bf16[192,1024]{1,0:T(8,128)(2,1)S(1)} %get-tuple-element.110), channel_id=1, source_target_pairs={{0,4},{4,0},{8,12},{12,8},{16,20},{20,16},{24,28},{28,24},{1,5},{5... | collective-permute-start | bytes 1179656 | tf_op jit(solution)/shard_map/ppermute | solution.py:413
  36.1 0.1 collective-permute-start.10
  36.2 0.8 %shard_map.97.refs_5_ = f32[384,1024]{1,0:T(8,128)S(1)} custom-call(bf16[768,768]{1,0:T(8,128)(2,1)S(1)} %get-tuple-element.107.weight_ref, bf16[768,1024]{1,0:T(8,128)(2,1)S(1)} %get-tuple-element.105.image_ref, f32[768,1024]{1,0:T(8,128)S(1)} %get-tuple-element.103.acc_ref), custom_call_target="tpu_custom_call" | custom-call | bytes 7471104 | tf_op jit(solution)/shard_map/pallas_call | solution.py:46
  37.0 0.8 %shard_map.98 = (bf16[192,1024]{1,0:T(8,128)(2,1)S(1)}, bf16[192,1024]{1,0:T(8,128)(2,1)S(1)}) custom-call(bf16[768,768]{1,0:T(8,128)(2,1)S(1)} %get-tuple-element.107.weight_ref, bf16[768,1024]{1,0:T(8,128)(2,1)S(1)} %get-tuple-element.94.refs_6_.unit_ref), custom_call_target="tpu_custom_call" | custom-call | bytes 3538944 | tf_op jit(solution)/shard_map/pallas_call | solution.py:46
  37.8 0.9 %collective-permute-start.15 = (bf16[192,1024]{1,0:T(8,128)(2,1)S(1)}, bf16[192,1024]{1,0:T(8,128)(2,1)S(1)}, u32[]{:S(2)}, u32[]{:S(2)}) collective-permute-start(bf16[192,1024]{1,0:T(8,128)(2,1)S(1)} %get-tuple-element.124), channel_id=1, source_target_pairs={{0,8},{4,20},{8,0},{12,28},{16,24},{20,4},{24,16},{28,12},{1,9},{5... | collective-permute-start | bytes 1179656 | tf_op jit(solution)/shard_map/ppermute | solution.py:418
  38.7 1.2 %collective-permute-start.17 = (bf16[192,1024]{1,0:T(8,128)(2,1)S(1)}, bf16[192,1024]{1,0:T(8,128)(2,1)S(1)}, u32[]{:S(2)}, u32[]{:S(2)}) collective-permute-start(bf16[192,1024]{1,0:T(8,128)(2,1)S(1)} %get-tuple-element.125), channel_id=1, source_target_pairs={{0,8},{4,20},{8,0},{12,28},{16,24},{20,4},{24,16},{28,12},{1,9},{5... | collective-permute-start | bytes 1179656 | tf_op jit(solution)/shard_map/ppermute | solution.py:418
  39.9 0.6 %shard_map.99 = (bf16[384,256]{1,0:T(8,128)(2,1)S(1)}, bf16[384,256]{1,0:T(8,128)(2,1)S(1)}, bf16[384,256]{1,0:T(8,128)(2,1)S(1)}, bf16[384,256]{1,0:T(8,128)(2,1)S(1)}) custom-call(f32[384,128]{1,0:T(8,128)S(1)} %get-tuple-element.99.refs_0_, bf16[384,256]{1,0:T(8,128)(2,1)S(1)} %get-tuple-element.79.refs_0_.refs_1_, ...), custom_call_target="tpu_custom_call" | custom-call | bytes 4128768 | tf_op jit(solution)/shard_map/pallas_call | solution.py:46
  40.5 2.5 %collective-permute-start.11 = (bf16[384,256]{1,0:T(8,128)(2,1)S(1)}, bf16[384,256]{1,0:T(8,128)(2,1)S(1)}, u32[]{:S(2)}, u32[]{:S(2)}) collective-permute-start(bf16[384,256]{1,0:T(8,128)(2,1)S(1)} %get-tuple-element.114), channel_id=1, source_target_pairs={{0,3},{1,2},{2,1},{3,0},{4,7},{5,6},{6,5},{7,4},{8,11},{9,10},{10,... | collective-permute-start | bytes 589832 | tf_op jit(solution)/shard_map/ppermute | solution.py:413
  43.1 0.0 collective-permute-start.12
  43.1 0.0 collective-permute-done.14.add_ref
  43.1 1.9 %collective-permute-start.13 = (bf16[384,256]{1,0:T(8,128)(2,1)S(1)}, bf16[384,256]{1,0:T(8,128)(2,1)S(1)}, u32[]{:S(2)}, u32[]{:S(2)}) collective-permute-start(bf16[384,256]{1,0:T(8,128)(2,1)S(1)} %get-tuple-element.116), channel_id=1, source_target_pairs={{0,1},{1,0},{2,3},{3,2},{4,5},{5,4},{6,7},{7,6},{8,9},{9,8},{10,11... | collective-permute-start | bytes 589832 | tf_op jit(solution)/shard_map/ppermute | solution.py:413
  45.0 1.4 %shard_map.100 = (f32[384,1024]{1,0:T(8,128)S(1)}, f32[384,1024]{1,0:T(8,128)S(1)}) custom-call(bf16[768,384]{1,0:T(8,128)(2,1)S(1)} %get-tuple-element.119.refs_8_.own_weight_ref, bf16[768,768]{1,0:T(8,128)(2,1)S(1)} %get-tuple-element.120.near_weight_ref, bf16[768,1024]{1,0:T(8,128)(2,1)S(1)} %get-tuple-element.94.refs_6_.unit_ref, ...), custom_call_target="tpu_custom_call" | custom-call | flops 20000000000 | bytes 7274496 | tf_op jit(solution)/shard_map/pallas_call | solution.py:46
  46.4 0.1 shard_map.101
  46.5 0.9 %collective-permute-start.16 = (bf16[192,1024]{1,0:T(8,128)(2,1)S(1)}, bf16[192,1024]{1,0:T(8,128)(2,1)S(1)}, u32[]{:S(2)}, u32[]{:S(2)}) collective-permute-start(bf16[192,1024]{1,0:T(8,128)(2,1)S(1)} %shard_map.101), channel_id=1, source_target_pairs={{0,16},{4,12},{8,24},{12,4},{16,0},{20,28},{24,8},{28,20},{1,17},{... | collective-permute-start | bytes 1179656 | tf_op jit(solution)/shard_map/ppermute | solution.py:418
  47.4 4.2 %collective-permute-done.17.in_ref = bf16[192,1024]{1,0:T(8,128)(2,1)S(1)} collective-permute-done((bf16[192,1024]{1,0:T(8,128)(2,1)S(1)}, bf16[192,1024]{1,0:T(8,128)(2,1)S(1)}, u32[]{:S(2)}, u32[]{:S(2)}) %collective-permute-start.17) | collective-permute-done | bytes 393248 | tf_op jit(solution)/shard_map/ppermute | solution.py:418
  51.6 0.1 shard_map.102
  51.7 1.7 %collective-permute-start.18 = (bf16[192,1024]{1,0:T(8,128)(2,1)S(1)}, bf16[192,1024]{1,0:T(8,128)(2,1)S(1)}, u32[]{:S(2)}, u32[]{:S(2)}) collective-permute-start(bf16[192,1024]{1,0:T(8,128)(2,1)S(1)} %shard_map.102), channel_id=1, source_target_pairs={{0,16},{4,12},{8,24},{12,4},{16,0},{20,28},{24,8},{28,20},{1,17},{... | collective-permute-start | bytes 1179656 | tf_op jit(solution)/shard_map/ppermute | solution.py:418
  53.5 5.5 %collective-permute-done.12.refs_1_.refs_2_ = bf16[384,256]{1,0:T(8,128)(2,1)S(1)} collective-permute-done((bf16[384,256]{1,0:T(8,128)(2,1)S(1)}, bf16[384,256]{1,0:T(8,128)(2,1)S(1)}, u32[]{:S(2)}, u32[]{:S(2)}) %collective-permute-start.12) | collective-permute-done | bytes 196640 | tf_op jit(solution)/shard_map/ppermute | solution.py:413
  59.0 0.6 collective-permute-done.18.refs_8_
  59.6 1.6 %shard_map.104 = (bf16[1536,256]{1,0:T(8,128)(2,1)}, bf16[384,1024]{1,0:T(8,128)(2,1)}) custom-call(bf16[384,256]{1,0:T(8,128)(2,1)S(1)} %get-tuple-element.113.refs_0_, bf16[384,256]{1,0:T(8,128)(2,1)S(1)} %collective-permute-done.11.refs_0_.refs_1_, bf16[384,256]{1,0:T(8,128)(2,1)S(1)} %collective-permute-done.12.refs_1_.refs_2_, ...), custom_call_target="tpu_custom_call" | custom-call | bytes 5705728 | tf_op jit(solution)/shard_map/pallas_call | solution.py:46
  (17 shorter events, 0.0 us)
Async XLA Ops:
  0.6 14.7 %collective-permute-start = (bf16[384,1024]{1,0:T(8,128)(2,1)}, bf16[384,1024]{1,0:T(8,128)(2,1)S(1)}, u32[]{:S(2)}, u32[]{:S(2)}) collective-permute-start(bf16[384,1024]{1,0:T(8,128)(2,1)} %raw_ref.1), channel_id=1, source_target_pairs={{0,16},{4,12},{8,24},{12,4},{16,0},{20,28},{24,8},{28,20},{1,17},{... | collective-permute-start | bytes 2359304 | tf_op jit(solution)/shard_map/ppermute | solution.py:418
  3.7 1.1 %copy-start = (bf16[1536,256]{1,0:T(8,128)(2,1)S(1)}, bf16[1536,256]{1,0:T(8,128)(2,1)}, u32[]{:S(2)}) copy-start(bf16[1536,256]{1,0:T(8,128)(2,1)} %text_ref.1) | copy-start | bytes 2359300
  4.8 8.8 %copy-start.1 = (s32[12288]{0:T(1024)S(1)}, s32[12288]{0:T(1024)}, u32[]{:S(2)}) copy-start(s32[12288]{0:T(1024)} %param.11) | copy-start | bytes 147460
  4.8 8.8 %copy-start.2 = (s32[12288]{0:T(1024)S(1)}, s32[12288]{0:T(1024)}, u32[]{:S(2)}) copy-start(s32[12288]{0:T(1024)} %param.12) | copy-start | bytes 147460
  4.8 8.8 %copy-start.3 = (s32[96,8,3]{0,1,2:T(8,128)S(1)}, s32[96,8,3]{0,1,2:T(8,128)}, u32[]{:S(2)}) copy-start(s32[96,8,3]{0,1,2:T(8,128)} %param.13) | copy-start | bytes 27652
  4.9 16.0 %collective-permute-start.2 = (bf16[384,256]{1,0:T(8,128)(2,1)S(1)}, bf16[384,256]{1,0:T(8,128)(2,1)S(1)}, u32[]{:S(2)}, u32[]{:S(2)}) collective-permute-start(bf16[384,256]{1,0:T(8,128)(2,1)S(1)} %get-tuple-element.80), channel_id=1, source_target_pairs={{0,3},{1,2},{2,1},{3,0},{4,7},{5,6},{6,5},{7,4},{8,11},{9,10},{10,... | collective-permute-start | bytes 589832 | tf_op jit(solution)/shard_map/ppermute | solution.py:413
  8.5 16.4 %collective-permute-start.3 = (bf16[384,256]{1,0:T(8,128)(2,1)S(1)}, bf16[384,256]{1,0:T(8,128)(2,1)S(1)}, u32[]{:S(2)}, u32[]{:S(2)}) collective-permute-start(bf16[384,256]{1,0:T(8,128)(2,1)S(1)} %get-tuple-element.81), channel_id=1, source_target_pairs={{0,2},{1,3},{2,0},{3,1},{4,6},{5,7},{6,4},{7,5},{8,10},{9,11},{10,... | collective-permute-start | bytes 589832 | tf_op jit(solution)/shard_map/ppermute | solution.py:413
  8.5 12.4 %collective-permute-start.4 = (bf16[384,256]{1,0:T(8,128)(2,1)S(1)}, bf16[384,256]{1,0:T(8,128)(2,1)S(1)}, u32[]{:S(2)}, u32[]{:S(2)}) collective-permute-start(bf16[384,256]{1,0:T(8,128)(2,1)S(1)} %get-tuple-element.82), channel_id=1, source_target_pairs={{0,1},{1,0},{2,3},{3,2},{4,5},{5,4},{6,7},{7,6},{8,9},{9,8},{10,11... | collective-permute-start | bytes 589832 | tf_op jit(solution)/shard_map/ppermute | solution.py:413
  10.7 15.2 %collective-permute-start.1 = (bf16[384,1024]{1,0:T(8,128)(2,1)}, bf16[384,1024]{1,0:T(8,128)(2,1)S(1)}, u32[]{:S(2)}, u32[]{:S(2)}) collective-permute-start(bf16[384,1024]{1,0:T(8,128)(2,1)} %raw_ref.1), channel_id=1, source_target_pairs={{0,8},{4,20},{8,0},{12,28},{16,24},{20,4},{24,16},{28,12},{1,9},{5... | collective-permute-start | bytes 2359304 | tf_op jit(solution)/shard_map/ppermute | solution.py:418
  15.3 17.2 %collective-permute-start.8 = (bf16[384,1024]{1,0:T(8,128)(2,1)S(1)}, bf16[384,1024]{1,0:T(8,128)(2,1)S(1)}, u32[]{:S(2)}, u32[]{:S(2)}) collective-permute-start(bf16[384,1024]{1,0:T(8,128)(2,1)S(1)} %collective-permute-done.raw_ref), channel_id=1, source_target_pairs={{0,8},{4,20},{8,0},{12,28},{16,24},{20,4},{24,16},{28,12},{1,9},{5... | collective-permute-start | bytes 2359304 | tf_op jit(solution)/shard_map/ppermute | solution.py:418
  25.3 2.7 %collective-permute-start.5 = (bf16[128,1024]{1,0:T(8,128)(2,1)S(1)}, bf16[128,1024]{1,0:T(8,128)(2,1)S(1)}, u32[]{:S(2)}, u32[]{:S(2)}) collective-permute-start(bf16[128,1024]{1,0:T(8,128)(2,1)S(1)} %get-tuple-element.91), channel_id=1, source_target_pairs={{0,4},{4,0},{8,12},{12,8},{16,20},{20,16},{24,28},{28,24},{1,5},{5... | collective-permute-start | bytes 786440 | tf_op jit(solution)/shard_map/ppermute | solution.py:413
  25.4 2.7 %collective-permute-start.6 = (bf16[128,1024]{1,0:T(8,128)(2,1)S(1)}, bf16[128,1024]{1,0:T(8,128)(2,1)S(1)}, u32[]{:S(2)}, u32[]{:S(2)}) collective-permute-start(bf16[128,1024]{1,0:T(8,128)(2,1)S(1)} %get-tuple-element.92), channel_id=1, source_target_pairs={{0,4},{4,0},{8,12},{12,8},{16,20},{20,16},{24,28},{28,24},{1,5},{5... | collective-permute-start | bytes 786440 | tf_op jit(solution)/shard_map/ppermute | solution.py:413
  25.9 2.2 %collective-permute-start.7 = (bf16[128,1024]{1,0:T(8,128)(2,1)S(1)}, bf16[128,1024]{1,0:T(8,128)(2,1)S(1)}, u32[]{:S(2)}, u32[]{:S(2)}) collective-permute-start(bf16[128,1024]{1,0:T(8,128)(2,1)S(1)} %get-tuple-element.93), channel_id=1, source_target_pairs={{0,4},{4,0},{8,12},{12,8},{16,20},{20,16},{24,28},{28,24},{1,5},{5... | collective-permute-start | bytes 786440 | tf_op jit(solution)/shard_map/ppermute | solution.py:413
  29.5 13.6 %collective-permute-start.14 = (bf16[384,1024]{1,0:T(8,128)(2,1)S(1)}, bf16[384,1024]{1,0:T(8,128)(2,1)S(1)}, u32[]{:S(2)}, u32[]{:S(2)}) collective-permute-start(bf16[384,1024]{1,0:T(8,128)(2,1)S(1)} %get-tuple-element.121), channel_id=1, source_target_pairs={{0,8},{4,20},{8,0},{12,28},{16,24},{20,4},{24,16},{28,12},{1,9},{5... | collective-permute-start | bytes 2359304 | tf_op jit(solution)/shard_map/ppermute | solution.py:418
  34.9 5.0 %collective-permute-start.9 = (bf16[192,1024]{1,0:T(8,128)(2,1)S(1)}, bf16[192,1024]{1,0:T(8,128)(2,1)S(1)}, u32[]{:S(2)}, u32[]{:S(2)}) collective-permute-start(bf16[192,1024]{1,0:T(8,128)(2,1)S(1)} %get-tuple-element.110), channel_id=1, source_target_pairs={{0,4},{4,0},{8,12},{12,8},{16,20},{20,16},{24,28},{28,24},{1,5},{5... | collective-permute-start | bytes 1179656 | tf_op jit(solution)/shard_map/ppermute | solution.py:413
  36.1 3.8 %collective-permute-start.10 = (bf16[192,1024]{1,0:T(8,128)(2,1)S(1)}, bf16[192,1024]{1,0:T(8,128)(2,1)S(1)}, u32[]{:S(2)}, u32[]{:S(2)}) collective-permute-start(bf16[192,1024]{1,0:T(8,128)(2,1)S(1)} %get-tuple-element.111), channel_id=1, source_target_pairs={{0,4},{4,0},{8,12},{12,8},{16,20},{20,16},{24,28},{28,24},{1,5},{5... | collective-permute-start | bytes 1179656 | tf_op jit(solution)/shard_map/ppermute | solution.py:413
  37.8 8.6 %collective-permute-start.15 = (bf16[192,1024]{1,0:T(8,128)(2,1)S(1)}, bf16[192,1024]{1,0:T(8,128)(2,1)S(1)}, u32[]{:S(2)}, u32[]{:S(2)}) collective-permute-start(bf16[192,1024]{1,0:T(8,128)(2,1)S(1)} %get-tuple-element.124), channel_id=1, source_target_pairs={{0,8},{4,20},{8,0},{12,28},{16,24},{20,4},{24,16},{28,12},{1,9},{5... | collective-permute-start | bytes 1179656 | tf_op jit(solution)/shard_map/ppermute | solution.py:418
  38.7 13.0 %collective-permute-start.17 = (bf16[192,1024]{1,0:T(8,128)(2,1)S(1)}, bf16[192,1024]{1,0:T(8,128)(2,1)S(1)}, u32[]{:S(2)}, u32[]{:S(2)}) collective-permute-start(bf16[192,1024]{1,0:T(8,128)(2,1)S(1)} %get-tuple-element.125), channel_id=1, source_target_pairs={{0,8},{4,20},{8,0},{12,28},{16,24},{20,4},{24,16},{28,12},{1,9},{5... | collective-permute-start | bytes 1179656 | tf_op jit(solution)/shard_map/ppermute | solution.py:418
  40.5 12.9 %collective-permute-start.11 = (bf16[384,256]{1,0:T(8,128)(2,1)S(1)}, bf16[384,256]{1,0:T(8,128)(2,1)S(1)}, u32[]{:S(2)}, u32[]{:S(2)}) collective-permute-start(bf16[384,256]{1,0:T(8,128)(2,1)S(1)} %get-tuple-element.114), channel_id=1, source_target_pairs={{0,3},{1,2},{2,1},{3,0},{4,7},{5,6},{6,5},{7,4},{8,11},{9,10},{10,... | collective-permute-start | bytes 589832 | tf_op jit(solution)/shard_map/ppermute | solution.py:413
  43.1 15.9 %collective-permute-start.12 = (bf16[384,256]{1,0:T(8,128)(2,1)S(1)}, bf16[384,256]{1,0:T(8,128)(2,1)S(1)}, u32[]{:S(2)}, u32[]{:S(2)}) collective-permute-start(bf16[384,256]{1,0:T(8,128)(2,1)S(1)} %get-tuple-element.115), channel_id=1, source_target_pairs={{0,2},{1,3},{2,0},{3,1},{4,6},{5,7},{6,4},{7,5},{8,10},{9,11},{10,... | collective-permute-start | bytes 589832 | tf_op jit(solution)/shard_map/ppermute | solution.py:413
  43.1 15.9 %collective-permute-start.13 = (bf16[384,256]{1,0:T(8,128)(2,1)S(1)}, bf16[384,256]{1,0:T(8,128)(2,1)S(1)}, u32[]{:S(2)}, u32[]{:S(2)}) collective-permute-start(bf16[384,256]{1,0:T(8,128)(2,1)S(1)} %get-tuple-element.116), channel_id=1, source_target_pairs={{0,1},{1,0},{2,3},{3,2},{4,5},{5,4},{6,7},{7,6},{8,9},{9,8},{10,11... | collective-permute-start | bytes 589832 | tf_op jit(solution)/shard_map/ppermute | solution.py:413
  46.5 12.5 %collective-permute-start.16 = (bf16[192,1024]{1,0:T(8,128)(2,1)S(1)}, bf16[192,1024]{1,0:T(8,128)(2,1)S(1)}, u32[]{:S(2)}, u32[]{:S(2)}) collective-permute-start(bf16[192,1024]{1,0:T(8,128)(2,1)S(1)} %shard_map.101), channel_id=1, source_target_pairs={{0,16},{4,12},{8,24},{12,4},{16,0},{20,28},{24,8},{28,20},{1,17},{... | collective-permute-start | bytes 1179656 | tf_op jit(solution)/shard_map/ppermute | solution.py:418
  51.7 7.8 %collective-permute-start.18 = (bf16[192,1024]{1,0:T(8,128)(2,1)S(1)}, bf16[192,1024]{1,0:T(8,128)(2,1)S(1)}, u32[]{:S(2)}, u32[]{:S(2)}) collective-permute-start(bf16[192,1024]{1,0:T(8,128)(2,1)S(1)} %shard_map.102), channel_id=1, source_target_pairs={{0,16},{4,12},{8,24},{12,4},{16,0},{20,28},{24,8},{28,20},{1,17},{... | collective-permute-start | bytes 1179656 | tf_op jit(solution)/shard_map/ppermute | solution.py:418

commit v9 on v8

--- a/solution.py
+++ b/solution.py
@@ -216,9 +216,7 @@
                         match = match * self.own_ref[pl.ds(group, 1), :]
                     power = jnp.where(match > 0.0, -power, power)
                     factor = jnp.where(match > 0.0, -amount, factor)
-                below = 1.0 + jnp.exp2(power)
-                inverse = pl.reciprocal(below, approx=True)
-                inverse = inverse * (2.0 - below * inverse)
+                inverse = pl.reciprocal(1.0 + jnp.exp2(power), approx=True)
                 weight_ref[pl.ds(top + a * TILE, TILE), pl.ds(left + j * TILE, TILE)] = (
                     factor * inverse
                 ).astype(jnp.bfloat16)
@@ -382,25 +380,30 @@
     copies = []
     for k in range(chunks):
         peer = place ^ far_first(k, chunks)
-        block = pl.ds(pl.multiple_of(peer * rows, rows), rows)
-        copies.append(pltpu.make_async_copy(part_refs[k], text_ref.at[block, :], sems.at[k]))
-        copies[-1].start()
-    for block in range(rows // TILE):
-        for first in range(block * TILE, (block + 1) * TILE, TILE // 2):
-            part = pl.ds(first, TILE // 2)
-            raw = raw_ref[part, :].astype(jnp.float32)
-            scales = scale_ref[part, :1]
-            acc = sum_ref[part, :]
-            if piece_refs:
-                size = piece_refs[0].shape[0]
-                piece = piece_refs[first // size][pl.ds(first % size, TILE // 2), :]
-                acc = acc + piece.astype(jnp.float32)
-            inner = jnp.sum(raw * acc, axis=-1, keepdims=True) * scales * scales
-            grad_ref[part, :] = (scales * (acc - raw * inner)).astype(jnp.bfloat16)
-        part = pl.ds(block * TILE, TILE)
+        for first in range(0, rows, TILE):
+            block = pl.ds(pl.multiple_of(peer * rows + first, TILE), TILE)
+            copies.append(
+                pltpu.make_async_copy(
+                    part_refs[k].at[pl.ds(first, TILE), :],
+                    text_ref.at[block, :],
+                    sems.at[len(copies)],
+                )
+            )
+            copies[-1].start()
+    for first in range(0, rows, TILE // 2):
+        part = pl.ds(first, TILE // 2)
+        raw = raw_ref[part, :].astype(jnp.float32)
+        scales = scale_ref[part, :1]
+        acc = sum_ref[part, :]
+        if piece_refs:
+            size = piece_refs[0].shape[0]
+            piece = piece_refs[first // size][pl.ds(first % size, TILE // 2), :]
+            acc = acc + piece.astype(jnp.float32)
+        inner = jnp.sum(raw * acc, axis=-1, keepdims=True) * scales * scales
+        grad_ref[part, :] = (scales * (acc - raw * inner)).astype(jnp.bfloat16)
         copies.append(
             pltpu.make_async_copy(
-                grad_ref.at[part, :], image_ref.at[part, :], sems.at[chunks + block]
+                grad_ref.at[part, :], image_ref.at[part, :], sems.at[len(copies)]
             )
         )
         copies[-1].start()
@@ -486,7 +489,10 @@
         second_images = call_kernel(
             unit_images_body, [bf16(rows)], [from_second], flops=WAIT_FLOPS // 2, limit=8
         )[0]
-        text_raw[-1], second_images = lax.optimization_barrier((text_raw[-1], second_images))
+        near_images = call_kernel(
+            near_images_body, [bf16(2 * rows)], [from_first, second_images], limit=8
+        )[0]
+        text_raw[-1], near_images = lax.optimization_barrier((text_raw[-1], near_images))
     text_own, text_scales, *pieces = call_kernel(
         functools.partial(unit_text_body, groups),
         [bf16(rows), f32(rows, TILE)] + [bf16(rows // TEXT_PIECES)] * TEXT_PIECES,
@@ -494,11 +500,6 @@
         limit=8,
     )
     text_other = [swap(piece, "blk", 1) for piece in pieces]
-    if square:
-        from_first, text_own = lax.optimization_barrier((from_first, text_own))
-        near_images = call_kernel(
-            near_images_body, [bf16(2 * rows)], [from_first, second_images], limit=8
-        )[0]
     unit_flops = 2 * rows * rows * embed
 
     def finish_text(acc_own, acc_other):
@@ -526,7 +527,7 @@
                 outs_anywhere=True,
                 scratch=[
                     pltpu.VMEM((rows, embed), jnp.bfloat16),
-                    pltpu.SemaphoreType.DMA((groups + tiles,)),
+                    pltpu.SemaphoreType.DMA(((groups + 2) * tiles,)),
                 ],
                 limit=8,
             )
@@ -605,6 +606,7 @@
         flops=WAIT_FLOPS,
         limit=16,
     )
+    far_sum[1], text_parts[0] = lax.optimization_barrier((far_sum[1], text_parts[0]))
     image_last = []
     for at, piece in enumerate(far_sum):
         relayed = call_kernel(

time: 61.4 us -> 63.7 us (1.037)
  waiting for transfers between devices: 17 us -> 19.7 us
    ppermute x8, waiting for transfers between devices: 5.4 us -> 15.6 us  [swap_near(): lax.ppermute(value, 'blk', [(i, i ^ neighbour_bits(i)[which]) for i in ra...]
    ppermute x11, waiting for transfers between devices: 11.6 us -> 4.19 us  [swap(): return lax.ppermute(value, axis, [(i, i ^ bits) for i in range(count)])]
  transfers between devices with their start and end apart: 19 -> 19, of which waited for: 6 -> 7; matrix products, arithmetic and copies ran while one was open for 0% -> 0% of each run, Pallas kernels for 25% -> 23%
where the time goes in v9:
time: 63.7 us; the launch traced here: 63.5 us
  starting transfers between devices  24.2 us (38%)
  waiting for transfers between devices  19.7 us (31%)
  Pallas kernels  16.3 us (26%)
  between operations  2.13 us (3%)
  local copies, waits for them, and re-layouts  1.14 us (2%)
    pallas_call x19, Pallas kernels, call_kernel(): pl.pallas_call(body, out_shape=outs, in_specs=specs, out_specs=[ANY_SPEC...  16.3 us
    ppermute x8, waiting for transfers between devices, swap_near(): lax.ppermute(value, 'blk', [(i, i ^ neighbour_bits(i)[which]) for i in ra...  15.6 us
    ppermute x8, starting transfers between devices, swap_near(): lax.ppermute(value, 'blk', [(i, i ^ neighbour_bits(i)[which]) for i in ra...  13.4 us
    ppermute x11, starting transfers between devices, swap(): return lax.ppermute(value, axis, [(i, i ^ bits) for i in range(count)])  10.8 us
    ppermute x11, waiting for transfers between devices, swap(): return lax.ppermute(value, axis, [(i, i ^ bits) for i in range(count)])  4.19 us
  transfers between devices with their start and end apart: 19, of which 7 were waited for; matrix products, arithmetic and copies ran while one was open for 0% of the time, Pallas kernels for 23%

profile of v9, /device:TPU:0, one launch (start us, length us, event | category | flops | bytes accessed | tf_op | source)
XLA Modules:
  0.0 63.5 jit_solution(3155862385519563819)
XLA Ops:
  0.6 3.0 %collective-permute-start = (bf16[384,1024]{1,0:T(8,128)(2,1)}, bf16[384,1024]{1,0:T(8,128)(2,1)S(1)}, u32[]{:S(2)}, u32[]{:S(2)}) collective-permute-start(bf16[384,1024]{1,0:T(8,128)(2,1)} %raw_ref.1), channel_id=1, source_target_pairs={{0,16},{4,12},{8,24},{12,4},{16,0},{20,28},{24,8},{28,20},{1,17},{... | collective-permute-start | bytes 2359304 | tf_op jit(solution)/shard_map/ppermute | solution.py:421
  3.7 1.1 %copy-done = bf16[1536,256]{1,0:T(8,128)(2,1)S(1)} copy-done((bf16[1536,256]{1,0:T(8,128)(2,1)S(1)}, bf16[1536,256]{1,0:T(8,128)(2,1)}, u32[]{:S(2)}) %copy-start) | copy-done | bytes 786456
  4.8 0.1 shard_map.88
  4.9 3.7 %collective-permute-start.1 = (bf16[384,256]{1,0:T(8,128)(2,1)S(1)}, bf16[384,256]{1,0:T(8,128)(2,1)S(1)}, u32[]{:S(2)}, u32[]{:S(2)}) collective-permute-start(bf16[384,256]{1,0:T(8,128)(2,1)S(1)} %get-tuple-element.79), channel_id=1, source_target_pairs={{0,3},{1,2},{2,1},{3,0},{4,7},{5,6},{6,5},{7,4},{8,11},{9,10},{10,... | collective-permute-start | bytes 589832 | tf_op jit(solution)/shard_map/ppermute | solution.py:416
  8.5 0.0 collective-permute-start.2
  8.5 0.8 %collective-permute-start.3 = (bf16[384,256]{1,0:T(8,128)(2,1)S(1)}, bf16[384,256]{1,0:T(8,128)(2,1)S(1)}, u32[]{:S(2)}, u32[]{:S(2)}) collective-permute-start(bf16[384,256]{1,0:T(8,128)(2,1)S(1)} %get-tuple-element.81), channel_id=1, source_target_pairs={{0,1},{1,0},{2,3},{3,2},{4,5},{5,4},{6,7},{7,6},{8,9},{9,8},{10,11... | collective-permute-start | bytes 589832 | tf_op jit(solution)/shard_map/ppermute | solution.py:416
  9.3 1.4 %shard_map.86 = (bf16[384,1024]{1,0:T(8,128)(2,1)S(1)}, bf16[384,1024]{1,0:T(8,128)(2,1)S(1)}, f32[384,128]{1,0:T(8,128)S(1)}) custom-call(bf16[384,1024]{1,0:T(8,128)(2,1)} %raw_ref.1), custom_call_target="tpu_custom_call" | custom-call | bytes 2555904 | tf_op jit(solution)/shard_map/pallas_call | solution.py:46
  10.7 1.6 %collective-permute-start.4 = (bf16[384,1024]{1,0:T(8,128)(2,1)}, bf16[384,1024]{1,0:T(8,128)(2,1)S(1)}, u32[]{:S(2)}, u32[]{:S(2)}) collective-permute-start(bf16[384,1024]{1,0:T(8,128)(2,1)} %raw_ref.1), channel_id=1, source_target_pairs={{0,8},{4,20},{8,0},{12,28},{16,24},{20,4},{24,16},{28,12},{1,9},{5... | collective-permute-start | bytes 2359304 | tf_op jit(solution)/shard_map/ppermute | solution.py:421
  13.6 1.1 %shard_map.87 = (f32[2,128]{1,0:T(2,128)S(1)}, f32[72,128]{1,0:T(8,128)S(1)}, s32[12,128]{1,0:T(8,128)S(1)}, s32[768,128]{1,0:T(8,128)S(1)}, f32[384,128]{1,0:T(8,128)S(1)}, /*index=5*/f32[4,128]{1,0:T(4,128)S(1)}) custom-call(f32[1]{0:T(128)S(6)} %copy.9.refs_0_, f32[1]{0:T(128)S(6)} %copy.10.refs_1_, s32[3,8,96]{2,1,0:T(8,128)S(1)} %bitcast.5, ...), custom_call_target="tpu_custom_call" | custom-call | bytes 743432 | tf_op jit(solution)/shard_map/pallas_call | solution.py:46
  14.7 0.6 collective-permute-done.raw_ref
  15.3 3.3 %collective-permute-start.8 = (bf16[384,1024]{1,0:T(8,128)(2,1)S(1)}, bf16[384,1024]{1,0:T(8,128)(2,1)S(1)}, u32[]{:S(2)}, u32[]{:S(2)}) collective-permute-start(bf16[384,1024]{1,0:T(8,128)(2,1)S(1)} %collective-permute-done.raw_ref), channel_id=1, source_target_pairs={{0,8},{4,20},{8,0},{12,28},{16,24},{20,4},{24,16},{28,12},{1,9},{5... | collective-permute-start | bytes 2359304 | tf_op jit(solution)/shard_map/ppermute | solution.py:421
  18.6 0.2 shard_map.89.second_unit_ref
  18.9 4.1 %collective-permute-done.4.first_ref = bf16[384,1024]{1,0:T(8,128)(2,1)S(1)} collective-permute-done((bf16[384,1024]{1,0:T(8,128)(2,1)}, bf16[384,1024]{1,0:T(8,128)(2,1)S(1)}, u32[]{:S(2)}, u32[]{:S(2)}) %collective-permute-start.4) | collective-permute-done | bytes 786464 | tf_op jit(solution)/shard_map/ppermute | solution.py:421
  23.0 0.3 shard_map.90.refs_8_.refs_7_
  23.3 0.0 collective-permute-done.3.refs_3_.refs_4_
  23.3 1.6 %collective-permute-done.2.refs_2_.refs_3_ = bf16[384,256]{1,0:T(8,128)(2,1)S(1)} collective-permute-done((bf16[384,256]{1,0:T(8,128)(2,1)S(1)}, bf16[384,256]{1,0:T(8,128)(2,1)S(1)}, u32[]{:S(2)}, u32[]{:S(2)}) %collective-permute-start.2) | collective-permute-done | bytes 196640 | tf_op jit(solution)/shard_map/ppermute | solution.py:416
  24.9 0.4 shard_map.91
  25.3 0.1 collective-permute-start.5
  25.4 0.5 collective-permute-start.6
  25.9 0.1 collective-permute-start.7
  26.0 1.6 %shard_map.92 = (bf16[384,384]{1,0:T(8,128)(2,1)S(1)}, bf16[384,768]{1,0:T(8,128)(2,1)S(1)}) custom-call(f32[2,128]{1,0:T(2,128)S(1)} %get-tuple-element.72.refs_0_, f32[72,128]{1,0:T(8,128)S(1)} %get-tuple-element.73.refs_1_, s32[12,128]{1,0:T(8,128)S(1)} %get-tuple-element.74.refs_2_, s32[768,128]{1,0:T(8,128)S(1)} %get-tuple-element.75.refs_3_, ...), custom_call_target="tpu_custom_call" | custom-call | bytes 4666368 | tf_op jit(solution)/shard_map/pallas_call | solution.py:46
  27.5 0.0 collective-permute-done.5.refs_9_
  27.6 0.0 collective-permute-done.6.refs_10_
  27.6 0.1 collective-permute-done.7.refs_11_
  27.7 1.3 %shard_map.93 = (bf16[768,1024]{1,0:T(8,128)(2,1)S(1)}, bf16[768,384]{1,0:T(8,128)(2,1)S(1)}, bf16[384,1024]{1,0:T(8,128)(2,1)S(1)}) custom-call(f32[2,128]{1,0:T(2,128)S(1)} %get-tuple-element.72.refs_0_, f32[72,128]{1,0:T(8,128)S(1)} %get-tuple-element.73.refs_1_, s32[12,128]{1,0:T(8,128)S(1)} %get-tuple-element.74.refs_2_, ...), custom_call_target="tpu_custom_call" | custom-call | bytes 7320576 | tf_op jit(solution)/shard_map/pallas_call | solution.py:46
  29.0 0.6 collective-permute-start.14
  29.6 2.3 %shard_map.94 = (bf16[768,384]{1,0:T(8,128)(2,1)S(1)}, f32[768,1024]{1,0:T(8,128)S(1)}, bf16[768,768]{1,0:T(8,128)(2,1)S(1)}) custom-call(f32[2,128]{1,0:T(2,128)S(1)} %get-tuple-element.72.refs_0_, f32[72,128]{1,0:T(8,128)S(1)} %get-tuple-element.73.refs_1_, s32[12,128]{1,0:T(8,128)S(1)} %get-tuple-element.74.refs_2_, ...), custom_call_target="tpu_custom_call" | custom-call | bytes 10957824 | tf_op jit(solution)/shard_map/pallas_call | solution.py:46
  31.9 1.4 %shard_map.95 = (bf16[768,768]{1,0:T(8,128)(2,1)S(1)}, bf16[768,1024]{1,0:T(8,128)(2,1)S(1)}) custom-call(f32[2,128]{1,0:T(2,128)S(1)} %get-tuple-element.72.refs_0_, f32[72,128]{1,0:T(8,128)S(1)} %get-tuple-element.73.refs_1_, s32[12,128]{1,0:T(8,128)S(1)} %get-tuple-element.74.refs_2_, s32[768,128]{1,0:T(8,128)S(1)} %get-tuple-element.75.refs_3_, ...), custom_call_target="tpu_custom_call" | custom-call | bytes 7123968 | tf_op jit(solution)/shard_map/pallas_call | solution.py:46
  33.4 0.8 %shard_map.96 = (bf16[192,1024]{1,0:T(8,128)(2,1)S(1)}, bf16[192,1024]{1,0:T(8,128)(2,1)S(1)}) custom-call(bf16[768,768]{1,0:T(8,128)(2,1)S(1)} %get-tuple-element.103.weight_ref, bf16[768,1024]{1,0:T(8,128)(2,1)S(1)} %get-tuple-element.102.image_ref, f32[768,1024]{1,0:T(8,128)S(1)} %get-tuple-element.100.acc_ref), custom_call_target="tpu_custom_call" | custom-call | bytes 6684672 | tf_op jit(solution)/shard_map/pallas_call | solution.py:46
  34.2 1.1 %collective-permute-start.9 = (bf16[192,1024]{1,0:T(8,128)(2,1)S(1)}, bf16[192,1024]{1,0:T(8,128)(2,1)S(1)}, u32[]{:S(2)}, u32[]{:S(2)}) collective-permute-start(bf16[192,1024]{1,0:T(8,128)(2,1)S(1)} %get-tuple-element.109), channel_id=1, source_target_pairs={{0,4},{4,0},{8,12},{12,8},{16,20},{20,16},{24,28},{28,24},{1,5},{5... | collective-permute-start | bytes 1179656 | tf_op jit(solution)/shard_map/ppermute | solution.py:416
  35.3 0.1 collective-permute-start.10
  35.4 0.8 %shard_map.97.refs_5_ = f32[384,1024]{1,0:T(8,128)S(1)} custom-call(bf16[768,768]{1,0:T(8,128)(2,1)S(1)} %get-tuple-element.103.weight_ref, bf16[768,1024]{1,0:T(8,128)(2,1)S(1)} %get-tuple-element.102.image_ref, f32[768,1024]{1,0:T(8,128)S(1)} %get-tuple-element.100.acc_ref), custom_call_target="tpu_custom_call" | custom-call | bytes 7471104 | tf_op jit(solution)/shard_map/pallas_call | solution.py:46
  36.2 0.8 %shard_map.98 = (bf16[192,1024]{1,0:T(8,128)(2,1)S(1)}, bf16[192,1024]{1,0:T(8,128)(2,1)S(1)}) custom-call(bf16[768,768]{1,0:T(8,128)(2,1)S(1)} %get-tuple-element.103.weight_ref, bf16[768,1024]{1,0:T(8,128)(2,1)S(1)} %get-tuple-element.92.refs_6_.unit_ref), custom_call_target="tpu_custom_call" | custom-call | bytes 3538944 | tf_op jit(solution)/shard_map/pallas_call | solution.py:46
  37.0 0.9 %collective-permute-start.15 = (bf16[192,1024]{1,0:T(8,128)(2,1)S(1)}, bf16[192,1024]{1,0:T(8,128)(2,1)S(1)}, u32[]{:S(2)}, u32[]{:S(2)}) collective-permute-start(bf16[192,1024]{1,0:T(8,128)(2,1)S(1)} %get-tuple-element.124), channel_id=1, source_target_pairs={{0,8},{4,20},{8,0},{12,28},{16,24},{20,4},{24,16},{28,12},{1,9},{5... | collective-permute-start | bytes 1179656 | tf_op jit(solution)/shard_map/ppermute | solution.py:421
  37.9 0.0 collective-permute-done.9.refs_6_
  37.9 0.6 shard_map.99
  38.5 3.2 %collective-permute-start.11 = (bf16[384,256]{1,0:T(8,128)(2,1)S(1)}, bf16[384,256]{1,0:T(8,128)(2,1)S(1)}, u32[]{:S(2)}, u32[]{:S(2)}) collective-permute-start(bf16[384,256]{1,0:T(8,128)(2,1)S(1)} %get-tuple-element.114), channel_id=1, source_target_pairs={{0,3},{1,2},{2,1},{3,0},{4,7},{5,6},{6,5},{7,4},{8,11},{9,10},{10,... | collective-permute-start | bytes 589832 | tf_op jit(solution)/shard_map/ppermute | solution.py:416
  41.7 1.3 %collective-permute-start.13 = (bf16[384,256]{1,0:T(8,128)(2,1)S(1)}, bf16[384,256]{1,0:T(8,128)(2,1)S(1)}, u32[]{:S(2)}, u32[]{:S(2)}) collective-permute-start(bf16[384,256]{1,0:T(8,128)(2,1)S(1)} %get-tuple-element.116), channel_id=1, source_target_pairs={{0,1},{1,0},{2,3},{3,2},{4,5},{5,4},{6,7},{7,6},{8,9},{9,8},{10,11... | collective-permute-start | bytes 589832 | tf_op jit(solution)/shard_map/ppermute | solution.py:416
  43.0 1.2 %collective-permute-start.17 = (bf16[192,1024]{1,0:T(8,128)(2,1)S(1)}, bf16[192,1024]{1,0:T(8,128)(2,1)S(1)}, u32[]{:S(2)}, u32[]{:S(2)}) collective-permute-start(bf16[192,1024]{1,0:T(8,128)(2,1)S(1)} %get-tuple-element.125), channel_id=1, source_target_pairs={{0,8},{4,20},{8,0},{12,28},{16,24},{20,4},{24,16},{28,12},{1,9},{5... | collective-permute-start | bytes 1179656 | tf_op jit(solution)/shard_map/ppermute | solution.py:421
  44.2 1.4 %shard_map.100 = (f32[384,1024]{1,0:T(8,128)S(1)}, f32[384,1024]{1,0:T(8,128)S(1)}) custom-call(bf16[768,384]{1,0:T(8,128)(2,1)S(1)} %get-tuple-element.119.refs_8_.own_weight_ref, bf16[768,768]{1,0:T(8,128)(2,1)S(1)} %get-tuple-element.120.near_weight_ref, bf16[768,1024]{1,0:T(8,128)(2,1)S(1)} %get-tuple-element.92.refs_6_.unit_ref, ...), custom_call_target="tpu_custom_call" | custom-call | flops 20000000000 | bytes 7274496 | tf_op jit(solution)/shard_map/pallas_call | solution.py:46
  45.6 0.1 shard_map.101
  45.7 1.2 %collective-permute-start.16 = (bf16[192,1024]{1,0:T(8,128)(2,1)S(1)}, bf16[192,1024]{1,0:T(8,128)(2,1)S(1)}, u32[]{:S(2)}, u32[]{:S(2)}) collective-permute-start(bf16[192,1024]{1,0:T(8,128)(2,1)S(1)} %shard_map.101), channel_id=1, source_target_pairs={{0,16},{4,12},{8,24},{12,4},{16,0},{20,28},{24,8},{28,20},{1,17},{... | collective-permute-start | bytes 1179656 | tf_op jit(solution)/shard_map/ppermute | solution.py:421
  47.0 7.1 %collective-permute-done.17.in_ref = bf16[192,1024]{1,0:T(8,128)(2,1)S(1)} collective-permute-done((bf16[192,1024]{1,0:T(8,128)(2,1)S(1)}, bf16[192,1024]{1,0:T(8,128)(2,1)S(1)}, u32[]{:S(2)}, u32[]{:S(2)}) %collective-permute-start.17) | collective-permute-done | bytes 393248 | tf_op jit(solution)/shard_map/ppermute | solution.py:421
  54.0 0.1 shard_map.102
  54.1 1.6 %collective-permute-start.18 = (bf16[192,1024]{1,0:T(8,128)(2,1)S(1)}, bf16[192,1024]{1,0:T(8,128)(2,1)S(1)}, u32[]{:S(2)}, u32[]{:S(2)}) collective-permute-start(bf16[192,1024]{1,0:T(8,128)(2,1)S(1)} %shard_map.102), channel_id=1, source_target_pairs={{0,16},{4,12},{8,24},{12,4},{16,0},{20,28},{24,8},{28,20},{1,17},{... | collective-permute-start | bytes 1179656 | tf_op jit(solution)/shard_map/ppermute | solution.py:421
  55.7 2.5 %collective-permute-done.12.refs_1_.refs_2_ = bf16[384,256]{1,0:T(8,128)(2,1)S(1)} collective-permute-done((bf16[384,256]{1,0:T(8,128)(2,1)S(1)}, bf16[384,256]{1,0:T(8,128)(2,1)S(1)}, u32[]{:S(2)}, u32[]{:S(2)}) %collective-permute-start.12) | collective-permute-done | bytes 196640 | tf_op jit(solution)/shard_map/ppermute | solution.py:416
  58.2 3.7 %collective-permute-done.18.refs_8_ = bf16[192,1024]{1,0:T(8,128)(2,1)S(1)} collective-permute-done((bf16[192,1024]{1,0:T(8,128)(2,1)S(1)}, bf16[192,1024]{1,0:T(8,128)(2,1)S(1)}, u32[]{:S(2)}, u32[]{:S(2)}) %collective-permute-start.18) | collective-permute-done | bytes 393248 | tf_op jit(solution)/shard_map/ppermute | solution.py:421
  61.9 1.6 %shard_map.104 = (bf16[1536,256]{1,0:T(8,128)(2,1)}, bf16[384,1024]{1,0:T(8,128)(2,1)}) custom-call(bf16[384,256]{1,0:T(8,128)(2,1)S(1)} %get-tuple-element.113.refs_0_, bf16[384,256]{1,0:T(8,128)(2,1)S(1)} %collective-permute-done.11.refs_0_.refs_1_, bf16[384,256]{1,0:T(8,128)(2,1)S(1)} %collective-permute-done.12.refs_1_.refs_2_, ...), custom_call_target="tpu_custom_call" | custom-call | bytes 5705728 | tf_op jit(solution)/shard_map/pallas_call | solution.py:46
  (17 shorter events, 0.0 us)
Async XLA Ops:
  0.6 14.7 %collective-permute-start = (bf16[384,1024]{1,0:T(8,128)(2,1)}, bf16[384,1024]{1,0:T(8,128)(2,1)S(1)}, u32[]{:S(2)}, u32[]{:S(2)}) collective-permute-start(bf16[384,1024]{1,0:T(8,128)(2,1)} %raw_ref.1), channel_id=1, source_target_pairs={{0,16},{4,12},{8,24},{12,4},{16,0},{20,28},{24,8},{28,20},{1,17},{... | collective-permute-start | bytes 2359304 | tf_op jit(solution)/shard_map/ppermute | solution.py:421
  3.7 1.1 %copy-start = (bf16[1536,256]{1,0:T(8,128)(2,1)S(1)}, bf16[1536,256]{1,0:T(8,128)(2,1)}, u32[]{:S(2)}) copy-start(bf16[1536,256]{1,0:T(8,128)(2,1)} %text_ref.1) | copy-start | bytes 2359300
  4.8 8.8 %copy-start.1 = (s32[12288]{0:T(1024)S(1)}, s32[12288]{0:T(1024)}, u32[]{:S(2)}) copy-start(s32[12288]{0:T(1024)} %param.11) | copy-start | bytes 147460
  4.8 8.8 %copy-start.2 = (s32[12288]{0:T(1024)S(1)}, s32[12288]{0:T(1024)}, u32[]{:S(2)}) copy-start(s32[12288]{0:T(1024)} %param.12) | copy-start | bytes 147460
  4.8 8.8 %copy-start.3 = (s32[96,8,3]{0,1,2:T(8,128)S(1)}, s32[96,8,3]{0,1,2:T(8,128)}, u32[]{:S(2)}) copy-start(s32[96,8,3]{0,1,2:T(8,128)} %param.13) | copy-start | bytes 27652
  4.9 18.5 %collective-permute-start.1 = (bf16[384,256]{1,0:T(8,128)(2,1)S(1)}, bf16[384,256]{1,0:T(8,128)(2,1)S(1)}, u32[]{:S(2)}, u32[]{:S(2)}) collective-permute-start(bf16[384,256]{1,0:T(8,128)(2,1)S(1)} %get-tuple-element.79), channel_id=1, source_target_pairs={{0,3},{1,2},{2,1},{3,0},{4,7},{5,6},{6,5},{7,4},{8,11},{9,10},{10,... | collective-permute-start | bytes 589832 | tf_op jit(solution)/shard_map/ppermute | solution.py:416
  8.5 16.4 %collective-permute-start.2 = (bf16[384,256]{1,0:T(8,128)(2,1)S(1)}, bf16[384,256]{1,0:T(8,128)(2,1)S(1)}, u32[]{:S(2)}, u32[]{:S(2)}) collective-permute-start(bf16[384,256]{1,0:T(8,128)(2,1)S(1)} %get-tuple-element.80), channel_id=1, source_target_pairs={{0,2},{1,3},{2,0},{3,1},{4,6},{5,7},{6,4},{7,5},{8,10},{9,11},{10,... | collective-permute-start | bytes 589832 | tf_op jit(solution)/shard_map/ppermute | solution.py:416
  8.5 14.8 %collective-permute-start.3 = (bf16[384,256]{1,0:T(8,128)(2,1)S(1)}, bf16[384,256]{1,0:T(8,128)(2,1)S(1)}, u32[]{:S(2)}, u32[]{:S(2)}) collective-permute-start(bf16[384,256]{1,0:T(8,128)(2,1)S(1)} %get-tuple-element.81), channel_id=1, source_target_pairs={{0,1},{1,0},{2,3},{3,2},{4,5},{5,4},{6,7},{7,6},{8,9},{9,8},{10,11... | collective-permute-start | bytes 589832 | tf_op jit(solution)/shard_map/ppermute | solution.py:416
  10.7 12.3 %collective-permute-start.4 = (bf16[384,1024]{1,0:T(8,128)(2,1)}, bf16[384,1024]{1,0:T(8,128)(2,1)S(1)}, u32[]{:S(2)}, u32[]{:S(2)}) collective-permute-start(bf16[384,1024]{1,0:T(8,128)(2,1)} %raw_ref.1), channel_id=1, source_target_pairs={{0,8},{4,20},{8,0},{12,28},{16,24},{20,4},{24,16},{28,12},{1,9},{5... | collective-permute-start | bytes 2359304 | tf_op jit(solution)/shard_map/ppermute | solution.py:421
  15.3 16.6 %collective-permute-start.8 = (bf16[384,1024]{1,0:T(8,128)(2,1)S(1)}, bf16[384,1024]{1,0:T(8,128)(2,1)S(1)}, u32[]{:S(2)}, u32[]{:S(2)}) collective-permute-start(bf16[384,1024]{1,0:T(8,128)(2,1)S(1)} %collective-permute-done.raw_ref), channel_id=1, source_target_pairs={{0,8},{4,20},{8,0},{12,28},{16,24},{20,4},{24,16},{28,12},{1,9},{5... | collective-permute-start | bytes 2359304 | tf_op jit(solution)/shard_map/ppermute | solution.py:421
  25.3 2.2 %collective-permute-start.5 = (bf16[128,1024]{1,0:T(8,128)(2,1)S(1)}, bf16[128,1024]{1,0:T(8,128)(2,1)S(1)}, u32[]{:S(2)}, u32[]{:S(2)}) collective-permute-start(bf16[128,1024]{1,0:T(8,128)(2,1)S(1)} %get-tuple-element.89), channel_id=1, source_target_pairs={{0,4},{4,0},{8,12},{12,8},{16,20},{20,16},{24,28},{28,24},{1,5},{5... | collective-permute-start | bytes 786440 | tf_op jit(solution)/shard_map/ppermute | solution.py:416
  25.4 2.2 %collective-permute-start.6 = (bf16[128,1024]{1,0:T(8,128)(2,1)S(1)}, bf16[128,1024]{1,0:T(8,128)(2,1)S(1)}, u32[]{:S(2)}, u32[]{:S(2)}) collective-permute-start(bf16[128,1024]{1,0:T(8,128)(2,1)S(1)} %get-tuple-element.90), channel_id=1, source_target_pairs={{0,4},{4,0},{8,12},{12,8},{16,20},{20,16},{24,28},{28,24},{1,5},{5... | collective-permute-start | bytes 786440 | tf_op jit(solution)/shard_map/ppermute | solution.py:416
  25.9 1.8 %collective-permute-start.7 = (bf16[128,1024]{1,0:T(8,128)(2,1)S(1)}, bf16[128,1024]{1,0:T(8,128)(2,1)S(1)}, u32[]{:S(2)}, u32[]{:S(2)}) collective-permute-start(bf16[128,1024]{1,0:T(8,128)(2,1)S(1)} %get-tuple-element.91), channel_id=1, source_target_pairs={{0,4},{4,0},{8,12},{12,8},{16,20},{20,16},{24,28},{28,24},{1,5},{5... | collective-permute-start | bytes 786440 | tf_op jit(solution)/shard_map/ppermute | solution.py:416
  29.0 14.0 %collective-permute-start.14 = (bf16[384,1024]{1,0:T(8,128)(2,1)S(1)}, bf16[384,1024]{1,0:T(8,128)(2,1)S(1)}, u32[]{:S(2)}, u32[]{:S(2)}) collective-permute-start(bf16[384,1024]{1,0:T(8,128)(2,1)S(1)} %get-tuple-element.121), channel_id=1, source_target_pairs={{0,8},{4,20},{8,0},{12,28},{16,24},{20,4},{24,16},{28,12},{1,9},{5... | collective-permute-start | bytes 2359304 | tf_op jit(solution)/shard_map/ppermute | solution.py:421
  34.2 3.7 %collective-permute-start.9 = (bf16[192,1024]{1,0:T(8,128)(2,1)S(1)}, bf16[192,1024]{1,0:T(8,128)(2,1)S(1)}, u32[]{:S(2)}, u32[]{:S(2)}) collective-permute-start(bf16[192,1024]{1,0:T(8,128)(2,1)S(1)} %get-tuple-element.109), channel_id=1, source_target_pairs={{0,4},{4,0},{8,12},{12,8},{16,20},{20,16},{24,28},{28,24},{1,5},{5... | collective-permute-start | bytes 1179656 | tf_op jit(solution)/shard_map/ppermute | solution.py:416
  35.3 2.6 %collective-permute-start.10 = (bf16[192,1024]{1,0:T(8,128)(2,1)S(1)}, bf16[192,1024]{1,0:T(8,128)(2,1)S(1)}, u32[]{:S(2)}, u32[]{:S(2)}) collective-permute-start(bf16[192,1024]{1,0:T(8,128)(2,1)S(1)} %get-tuple-element.110), channel_id=1, source_target_pairs={{0,4},{4,0},{8,12},{12,8},{16,20},{20,16},{24,28},{28,24},{1,5},{5... | collective-permute-start | bytes 1179656 | tf_op jit(solution)/shard_map/ppermute | solution.py:416
  37.0 8.6 %collective-permute-start.15 = (bf16[192,1024]{1,0:T(8,128)(2,1)S(1)}, bf16[192,1024]{1,0:T(8,128)(2,1)S(1)}, u32[]{:S(2)}, u32[]{:S(2)}) collective-permute-start(bf16[192,1024]{1,0:T(8,128)(2,1)S(1)} %get-tuple-element.124), channel_id=1, source_target_pairs={{0,8},{4,20},{8,0},{12,28},{16,24},{20,4},{24,16},{28,12},{1,9},{5... | collective-permute-start | bytes 1179656 | tf_op jit(solution)/shard_map/ppermute | solution.py:421
  38.5 17.2 %collective-permute-start.11 = (bf16[384,256]{1,0:T(8,128)(2,1)S(1)}, bf16[384,256]{1,0:T(8,128)(2,1)S(1)}, u32[]{:S(2)}, u32[]{:S(2)}) collective-permute-start(bf16[384,256]{1,0:T(8,128)(2,1)S(1)} %get-tuple-element.114), channel_id=1, source_target_pairs={{0,3},{1,2},{2,1},{3,0},{4,7},{5,6},{6,5},{7,4},{8,11},{9,10},{10,... | collective-permute-start | bytes 589832 | tf_op jit(solution)/shard_map/ppermute | solution.py:416
  41.7 16.5 %collective-permute-start.12 = (bf16[384,256]{1,0:T(8,128)(2,1)S(1)}, bf16[384,256]{1,0:T(8,128)(2,1)S(1)}, u32[]{:S(2)}, u32[]{:S(2)}) collective-permute-start(bf16[384,256]{1,0:T(8,128)(2,1)S(1)} %get-tuple-element.115), channel_id=1, source_target_pairs={{0,2},{1,3},{2,0},{3,1},{4,6},{5,7},{6,4},{7,5},{8,10},{9,11},{10,... | collective-permute-start | bytes 589832 | tf_op jit(solution)/shard_map/ppermute | solution.py:416
  41.7 16.5 %collective-permute-start.13 = (bf16[384,256]{1,0:T(8,128)(2,1)S(1)}, bf16[384,256]{1,0:T(8,128)(2,1)S(1)}, u32[]{:S(2)}, u32[]{:S(2)}) collective-permute-start(bf16[384,256]{1,0:T(8,128)(2,1)S(1)} %get-tuple-element.116), channel_id=1, source_target_pairs={{0,1},{1,0},{2,3},{3,2},{4,5},{5,4},{6,7},{7,6},{8,9},{9,8},{10,11... | collective-permute-start | bytes 589832 | tf_op jit(solution)/shard_map/ppermute | solution.py:416
  43.0 11.0 %collective-permute-start.17 = (bf16[192,1024]{1,0:T(8,128)(2,1)S(1)}, bf16[192,1024]{1,0:T(8,128)(2,1)S(1)}, u32[]{:S(2)}, u32[]{:S(2)}) collective-permute-start(bf16[192,1024]{1,0:T(8,128)(2,1)S(1)} %get-tuple-element.125), channel_id=1, source_target_pairs={{0,8},{4,20},{8,0},{12,28},{16,24},{20,4},{24,16},{28,12},{1,9},{5... | collective-permute-start | bytes 1179656 | tf_op jit(solution)/shard_map/ppermute | solution.py:421
  45.7 12.5 %collective-permute-start.16 = (bf16[192,1024]{1,0:T(8,128)(2,1)S(1)}, bf16[192,1024]{1,0:T(8,128)(2,1)S(1)}, u32[]{:S(2)}, u32[]{:S(2)}) collective-permute-start(bf16[192,1024]{1,0:T(8,128)(2,1)S(1)} %shard_map.101), channel_id=1, source_target_pairs={{0,16},{4,12},{8,24},{12,4},{16,0},{20,28},{24,8},{28,20},{1,17},{... | collective-permute-start | bytes 1179656 | tf_op jit(solution)/shard_map/ppermute | solution.py:421
  54.1 7.8 %collective-permute-start.18 = (bf16[192,1024]{1,0:T(8,128)(2,1)S(1)}, bf16[192,1024]{1,0:T(8,128)(2,1)S(1)}, u32[]{:S(2)}, u32[]{:S(2)}) collective-permute-start(bf16[192,1024]{1,0:T(8,128)(2,1)S(1)} %shard_map.102), channel_id=1, source_target_pairs={{0,16},{4,12},{8,24},{12,4},{16,0},{20,28},{24,8},{28,20},{1,17},{... | collective-permute-start | bytes 1179656 | tf_op jit(solution)/shard_map/ppermute | solution.py:421

commit v10 on v9

--- a/solution.py
+++ b/solution.py
@@ -301,10 +301,14 @@
         ref[...] = acc[at * size : (at + 1) * size, :].astype(ref.dtype)
 
 
-def own_sum_body(own_weight_ref, near_weight_ref, unit_ref, add_ref, own_ref, second_ref):
-    rows = own_ref.shape[0]
-    second_ref[...] = dot_tn(near_weight_ref[:, rows:], unit_ref[...])
-    own_ref[...] = dot_tn(own_weight_ref[...], unit_ref[...]) + add_ref[...].astype(jnp.float32)
+def second_sum_body(weight_ref, unit_ref, add_ref, out_ref, add_out_ref):
+    rows = out_ref.shape[0]
+    out_ref[...] = dot_tn(weight_ref[:, rows:], unit_ref[...])
+    add_out_ref[...] = add_ref[...]
+
+
+def own_sum_body(weight_ref, unit_ref, add_ref, out_ref):
+    out_ref[...] = dot_tn(weight_ref[...], unit_ref[...]) + add_ref[...].astype(jnp.float32)
 
 
 def all_body(tiles, chips, *refs):
@@ -598,24 +602,29 @@
     )
     acc_own, far_sum[0] = lax.optimization_barrier((acc_own, far_sum[0]))
     text_parts = finish_text(acc_own, acc_other)
-    own_weights, text_parts[0] = lax.optimization_barrier((own_weights, text_parts[0]))
-    base, second_sum = call_kernel(
-        own_sum_body,
-        [f32(rows), f32(rows)],
-        [own_weights, near_weights, units, image_add],
+    near_weights, text_parts[0] = lax.optimization_barrier((near_weights, text_parts[0]))
+    second_sum, image_add = call_kernel(
+        second_sum_body,
+        [f32(rows), bf16(rows)],
+        [near_weights, units, image_add],
         flops=WAIT_FLOPS,
         limit=16,
     )
-    far_sum[1], text_parts[0] = lax.optimization_barrier((far_sum[1], text_parts[0]))
     image_last = []
-    for at, piece in enumerate(far_sum):
+    far_in = [swap_near(piece, 0) for piece in far_sum]
+    for at, piece in enumerate(far_in):
         relayed = call_kernel(
             functools.partial(relay_body, at),
             [bf16(rows // LAST_PIECES)],
-            [second_sum, swap_near(piece, 0)],
+            [second_sum, piece],
             limit=8,
         )[0]
         image_last.append(swap_near(relayed, 1))
+        second_sum, relayed = lax.optimization_barrier((second_sum, relayed))
+    own_weights, relayed = lax.optimization_barrier((own_weights, relayed))
+    base = call_kernel(
+        own_sum_body, [f32(rows)], [own_weights, units, image_add], moved=0, limit=16
+    )[0]
     return finish(text_parts, base, image_last)
 
 

time: 63.7 us -> 61.1 us (0.959)
  waiting for transfers between devices: 19.7 us -> 16.6 us
    ppermute x8, waiting for transfers between devices: 15.6 us -> 10.3 us  [swap_near(): lax.ppermute(value, 'blk', [(i, i ^ neighbour_bits(i)[which]) for i in ra...]
    ppermute x11, waiting for transfers between devices: 4.19 us -> 6.24 us  [swap(): return lax.ppermute(value, axis, [(i, i ^ bits) for i in range(count)])]
    pallas_call x19 -> x20, Pallas kernels: 16.3 us -> 16.5 us  [call_kernel(): pl.pallas_call(body, out_shape=outs, in_specs=specs, out_specs=[ANY_SPEC...]
  transfers between devices with their start and end apart: 19 -> 19, of which waited for: 7 -> 8; matrix products, arithmetic and copies ran while one was open for 0% -> 0% of each run, Pallas kernels for 23% -> 25%
where the time goes in v10:
time: 61.1 us; the launch traced here: 60.9 us
  starting transfers between devices  24.5 us (40%)
  waiting for transfers between devices  16.6 us (27%)
  Pallas kernels  16.5 us (27%)
  between operations  2.13 us (3%)
  local copies, waits for them, and re-layouts  1.14 us (2%)
    pallas_call x20, Pallas kernels, call_kernel(): pl.pallas_call(body, out_shape=outs, in_specs=specs, out_specs=[ANY_SPEC...  16.5 us
    ppermute x8, starting transfers between devices, swap_near(): lax.ppermute(value, 'blk', [(i, i ^ neighbour_bits(i)[which]) for i in ra...  13.8 us
    ppermute x11, starting transfers between devices, swap(): return lax.ppermute(value, axis, [(i, i ^ bits) for i in range(count)])  10.8 us
    ppermute x8, waiting for transfers between devices, swap_near(): lax.ppermute(value, 'blk', [(i, i ^ neighbour_bits(i)[which]) for i in ra...  10.3 us
    ppermute x11, waiting for transfers between devices, swap(): return lax.ppermute(value, axis, [(i, i ^ bits) for i in range(count)])  6.24 us
  transfers between devices with their start and end apart: 19, of which 8 were waited for; matrix products, arithmetic and copies ran while one was open for 0% of the time, Pallas kernels for 25%

profile of v10, /device:TPU:0, one launch (start us, length us, event | category | flops | bytes accessed | tf_op | source)
XLA Modules:
  0.0 60.9 jit_solution(7499100392455899542)
XLA Ops:
  0.6 3.0 %collective-permute-start = (bf16[384,1024]{1,0:T(8,128)(2,1)}, bf16[384,1024]{1,0:T(8,128)(2,1)S(1)}, u32[]{:S(2)}, u32[]{:S(2)}) collective-permute-start(bf16[384,1024]{1,0:T(8,128)(2,1)} %raw_ref.1), channel_id=1, source_target_pairs={{0,16},{4,12},{8,24},{12,4},{16,0},{20,28},{24,8},{28,20},{1,17},{... | collective-permute-start | bytes 2359304 | tf_op jit(solution)/shard_map/ppermute | solution.py:425
  3.7 1.1 %copy-done = bf16[1536,256]{1,0:T(8,128)(2,1)S(1)} copy-done((bf16[1536,256]{1,0:T(8,128)(2,1)S(1)}, bf16[1536,256]{1,0:T(8,128)(2,1)}, u32[]{:S(2)}) %copy-start) | copy-done | bytes 786456
  4.8 0.1 shard_map.88
  4.9 3.7 %collective-permute-start.1 = (bf16[384,256]{1,0:T(8,128)(2,1)S(1)}, bf16[384,256]{1,0:T(8,128)(2,1)S(1)}, u32[]{:S(2)}, u32[]{:S(2)}) collective-permute-start(bf16[384,256]{1,0:T(8,128)(2,1)S(1)} %get-tuple-element.78), channel_id=1, source_target_pairs={{0,3},{1,2},{2,1},{3,0},{4,7},{5,6},{6,5},{7,4},{8,11},{9,10},{10,... | collective-permute-start | bytes 589832 | tf_op jit(solution)/shard_map/ppermute | solution.py:420
  8.5 0.0 collective-permute-start.2
  8.5 0.8 %collective-permute-start.3 = (bf16[384,256]{1,0:T(8,128)(2,1)S(1)}, bf16[384,256]{1,0:T(8,128)(2,1)S(1)}, u32[]{:S(2)}, u32[]{:S(2)}) collective-permute-start(bf16[384,256]{1,0:T(8,128)(2,1)S(1)} %get-tuple-element.80), channel_id=1, source_target_pairs={{0,1},{1,0},{2,3},{3,2},{4,5},{5,4},{6,7},{7,6},{8,9},{9,8},{10,11... | collective-permute-start | bytes 589832 | tf_op jit(solution)/shard_map/ppermute | solution.py:420
  9.3 1.4 %shard_map.86 = (bf16[384,1024]{1,0:T(8,128)(2,1)S(1)}, bf16[384,1024]{1,0:T(8,128)(2,1)S(1)}, f32[384,128]{1,0:T(8,128)S(1)}) custom-call(bf16[384,1024]{1,0:T(8,128)(2,1)} %raw_ref.1), custom_call_target="tpu_custom_call" | custom-call | bytes 2555904 | tf_op jit(solution)/shard_map/pallas_call | solution.py:46
  10.7 1.6 %collective-permute-start.4 = (bf16[384,1024]{1,0:T(8,128)(2,1)}, bf16[384,1024]{1,0:T(8,128)(2,1)S(1)}, u32[]{:S(2)}, u32[]{:S(2)}) collective-permute-start(bf16[384,1024]{1,0:T(8,128)(2,1)} %raw_ref.1), channel_id=1, source_target_pairs={{0,8},{4,20},{8,0},{12,28},{16,24},{20,4},{24,16},{28,12},{1,9},{5... | collective-permute-start | bytes 2359304 | tf_op jit(solution)/shard_map/ppermute | solution.py:425
  13.6 1.1 %shard_map.87 = (f32[2,128]{1,0:T(2,128)S(1)}, f32[72,128]{1,0:T(8,128)S(1)}, s32[12,128]{1,0:T(8,128)S(1)}, s32[768,128]{1,0:T(8,128)S(1)}, f32[384,128]{1,0:T(8,128)S(1)}, /*index=5*/f32[4,128]{1,0:T(4,128)S(1)}) custom-call(f32[1]{0:T(128)S(6)} %copy.9.refs_0_, f32[1]{0:T(128)S(6)} %copy.10.refs_1_, s32[3,8,96]{2,1,0:T(8,128)S(1)} %bitcast.5, ...), custom_call_target="tpu_custom_call" | custom-call | bytes 743432 | tf_op jit(solution)/shard_map/pallas_call | solution.py:46
  14.7 0.6 %collective-permute-done.raw_ref = bf16[384,1024]{1,0:T(8,128)(2,1)S(1)} collective-permute-done((bf16[384,1024]{1,0:T(8,128)(2,1)}, bf16[384,1024]{1,0:T(8,128)(2,1)S(1)}, u32[]{:S(2)}, u32[]{:S(2)}) %collective-permute-start) | collective-permute-done | bytes 786464 | tf_op jit(solution)/shard_map/ppermute | solution.py:425
  15.3 3.3 %collective-permute-start.8 = (bf16[384,1024]{1,0:T(8,128)(2,1)S(1)}, bf16[384,1024]{1,0:T(8,128)(2,1)S(1)}, u32[]{:S(2)}, u32[]{:S(2)}) collective-permute-start(bf16[384,1024]{1,0:T(8,128)(2,1)S(1)} %collective-permute-done.raw_ref), channel_id=1, source_target_pairs={{0,8},{4,20},{8,0},{12,28},{16,24},{20,4},{24,16},{28,12},{1,9},{5... | collective-permute-start | bytes 2359304 | tf_op jit(solution)/shard_map/ppermute | solution.py:425
  18.6 0.2 shard_map.89.second_unit_ref
  18.9 4.1 %collective-permute-done.4.first_ref = bf16[384,1024]{1,0:T(8,128)(2,1)S(1)} collective-permute-done((bf16[384,1024]{1,0:T(8,128)(2,1)}, bf16[384,1024]{1,0:T(8,128)(2,1)S(1)}, u32[]{:S(2)}, u32[]{:S(2)}) %collective-permute-start.4) | collective-permute-done | bytes 786464 | tf_op jit(solution)/shard_map/ppermute | solution.py:425
  23.0 0.3 shard_map.90.refs_8_.refs_7_
  23.3 0.0 collective-permute-done.3.refs_3_.refs_4_
  23.3 1.6 %collective-permute-done.2.refs_2_.refs_3_ = bf16[384,256]{1,0:T(8,128)(2,1)S(1)} collective-permute-done((bf16[384,256]{1,0:T(8,128)(2,1)S(1)}, bf16[384,256]{1,0:T(8,128)(2,1)S(1)}, u32[]{:S(2)}, u32[]{:S(2)}) %collective-permute-start.2) | collective-permute-done | bytes 196640 | tf_op jit(solution)/shard_map/ppermute | solution.py:420
  24.9 0.4 shard_map.91
  25.3 0.1 collective-permute-start.5
  25.4 0.5 collective-permute-start.6
  25.9 0.1 collective-permute-start.7
  26.0 1.6 %shard_map.92 = (bf16[384,384]{1,0:T(8,128)(2,1)S(1)}, bf16[384,768]{1,0:T(8,128)(2,1)S(1)}) custom-call(f32[2,128]{1,0:T(2,128)S(1)} %get-tuple-element.71.refs_0_, f32[72,128]{1,0:T(8,128)S(1)} %get-tuple-element.72.refs_1_, s32[12,128]{1,0:T(8,128)S(1)} %get-tuple-element.73.refs_2_, s32[768,128]{1,0:T(8,128)S(1)} %get-tuple-element.74.refs_3_, ...), custom_call_target="tpu_custom_call" | custom-call | bytes 4666368 | tf_op jit(solution)/shard_map/pallas_call | solution.py:46
  27.5 0.0 collective-permute-done.5.refs_9_
  27.6 0.1 collective-permute-done.7.refs_11_
  27.7 1.3 %shard_map.93 = (bf16[768,1024]{1,0:T(8,128)(2,1)S(1)}, bf16[768,384]{1,0:T(8,128)(2,1)S(1)}, bf16[384,1024]{1,0:T(8,128)(2,1)S(1)}) custom-call(f32[2,128]{1,0:T(2,128)S(1)} %get-tuple-element.71.refs_0_, f32[72,128]{1,0:T(8,128)S(1)} %get-tuple-element.72.refs_1_, s32[12,128]{1,0:T(8,128)S(1)} %get-tuple-element.73.refs_2_, ...), custom_call_target="tpu_custom_call" | custom-call | bytes 7320576 | tf_op jit(solution)/shard_map/pallas_call | solution.py:46
  29.0 0.6 collective-permute-start.14
  29.6 2.3 %shard_map.94 = (bf16[768,384]{1,0:T(8,128)(2,1)S(1)}, f32[768,1024]{1,0:T(8,128)S(1)}, bf16[768,768]{1,0:T(8,128)(2,1)S(1)}) custom-call(f32[2,128]{1,0:T(2,128)S(1)} %get-tuple-element.71.refs_0_, f32[72,128]{1,0:T(8,128)S(1)} %get-tuple-element.72.refs_1_, s32[12,128]{1,0:T(8,128)S(1)} %get-tuple-element.73.refs_2_, ...), custom_call_target="tpu_custom_call" | custom-call | bytes 10957824 | tf_op jit(solution)/shard_map/pallas_call | solution.py:46
  31.9 1.4 %shard_map.95 = (bf16[768,768]{1,0:T(8,128)(2,1)S(1)}, bf16[768,1024]{1,0:T(8,128)(2,1)S(1)}) custom-call(f32[2,128]{1,0:T(2,128)S(1)} %get-tuple-element.71.refs_0_, f32[72,128]{1,0:T(8,128)S(1)} %get-tuple-element.72.refs_1_, s32[12,128]{1,0:T(8,128)S(1)} %get-tuple-element.73.refs_2_, s32[768,128]{1,0:T(8,128)S(1)} %get-tuple-element.74.refs_3_, ...), custom_call_target="tpu_custom_call" | custom-call | bytes 7123968 | tf_op jit(solution)/shard_map/pallas_call | solution.py:46
  33.4 0.8 %shard_map.96 = (bf16[192,1024]{1,0:T(8,128)(2,1)S(1)}, bf16[192,1024]{1,0:T(8,128)(2,1)S(1)}) custom-call(bf16[768,768]{1,0:T(8,128)(2,1)S(1)} %get-tuple-element.105.weight_ref, bf16[768,1024]{1,0:T(8,128)(2,1)S(1)} %get-tuple-element.103.image_ref, f32[768,1024]{1,0:T(8,128)S(1)} %get-tuple-element.101.acc_ref), custom_call_target="tpu_custom_call" | custom-call | bytes 6684672 | tf_op jit(solution)/shard_map/pallas_call | solution.py:46
  34.2 1.1 %collective-permute-start.9 = (bf16[192,1024]{1,0:T(8,128)(2,1)S(1)}, bf16[192,1024]{1,0:T(8,128)(2,1)S(1)}, u32[]{:S(2)}, u32[]{:S(2)}) collective-permute-start(bf16[192,1024]{1,0:T(8,128)(2,1)S(1)} %get-tuple-element.108), channel_id=1, source_target_pairs={{0,4},{4,0},{8,12},{12,8},{16,20},{20,16},{24,28},{28,24},{1,5},{5... | collective-permute-start | bytes 1179656 | tf_op jit(solution)/shard_map/ppermute | solution.py:420
  35.3 0.1 collective-permute-start.10
  35.4 0.8 %shard_map.97.refs_5_ = f32[384,1024]{1,0:T(8,128)S(1)} custom-call(bf16[768,768]{1,0:T(8,128)(2,1)S(1)} %get-tuple-element.105.weight_ref, bf16[768,1024]{1,0:T(8,128)(2,1)S(1)} %get-tuple-element.103.image_ref, f32[768,1024]{1,0:T(8,128)S(1)} %get-tuple-element.101.acc_ref), custom_call_target="tpu_custom_call" | custom-call | bytes 7471104 | tf_op jit(solution)/shard_map/pallas_call | solution.py:46
  36.2 0.8 %shard_map.98 = (bf16[192,1024]{1,0:T(8,128)(2,1)S(1)}, bf16[192,1024]{1,0:T(8,128)(2,1)S(1)}) custom-call(bf16[768,768]{1,0:T(8,128)(2,1)S(1)} %get-tuple-element.105.weight_ref, bf16[768,1024]{1,0:T(8,128)(2,1)S(1)} %get-tuple-element.91.refs_6_.unit_ref), custom_call_target="tpu_custom_call" | custom-call | bytes 3538944 | tf_op jit(solution)/shard_map/pallas_call | solution.py:46
  37.0 0.9 %collective-permute-start.15 = (bf16[192,1024]{1,0:T(8,128)(2,1)S(1)}, bf16[192,1024]{1,0:T(8,128)(2,1)S(1)}, u32[]{:S(2)}, u32[]{:S(2)}) collective-permute-start(bf16[192,1024]{1,0:T(8,128)(2,1)S(1)} %get-tuple-element.121), channel_id=1, source_target_pairs={{0,8},{4,20},{8,0},{12,28},{16,24},{20,4},{24,16},{28,12},{1,9},{5... | collective-permute-start | bytes 1179656 | tf_op jit(solution)/shard_map/ppermute | solution.py:425
  37.9 1.2 %collective-permute-start.17 = (bf16[192,1024]{1,0:T(8,128)(2,1)S(1)}, bf16[192,1024]{1,0:T(8,128)(2,1)S(1)}, u32[]{:S(2)}, u32[]{:S(2)}) collective-permute-start(bf16[192,1024]{1,0:T(8,128)(2,1)S(1)} %get-tuple-element.123), channel_id=1, source_target_pairs={{0,8},{4,20},{8,0},{12,28},{16,24},{20,4},{24,16},{28,12},{1,9},{5... | collective-permute-start | bytes 1179656 | tf_op jit(solution)/shard_map/ppermute | solution.py:425
  39.1 0.6 %shard_map.99 = (bf16[384,256]{1,0:T(8,128)(2,1)S(1)}, bf16[384,256]{1,0:T(8,128)(2,1)S(1)}, bf16[384,256]{1,0:T(8,128)(2,1)S(1)}, bf16[384,256]{1,0:T(8,128)(2,1)S(1)}) custom-call(f32[384,128]{1,0:T(8,128)S(1)} %get-tuple-element.95.refs_0_, bf16[384,256]{1,0:T(8,128)(2,1)S(1)} %get-tuple-element.77.refs_0_.refs_1_, ...), custom_call_target="tpu_custom_call" | custom-call | bytes 4128768 | tf_op jit(solution)/shard_map/pallas_call | solution.py:46
  39.7 2.5 %collective-permute-start.11 = (bf16[384,256]{1,0:T(8,128)(2,1)S(1)}, bf16[384,256]{1,0:T(8,128)(2,1)S(1)}, u32[]{:S(2)}, u32[]{:S(2)}) collective-permute-start(bf16[384,256]{1,0:T(8,128)(2,1)S(1)} %get-tuple-element.112), channel_id=1, source_target_pairs={{0,3},{1,2},{2,1},{3,0},{4,7},{5,6},{6,5},{7,4},{8,11},{9,10},{10,... | collective-permute-start | bytes 589832 | tf_op jit(solution)/shard_map/ppermute | solution.py:420
  42.2 1.9 %collective-permute-start.13 = (bf16[384,256]{1,0:T(8,128)(2,1)S(1)}, bf16[384,256]{1,0:T(8,128)(2,1)S(1)}, u32[]{:S(2)}, u32[]{:S(2)}) collective-permute-start(bf16[384,256]{1,0:T(8,128)(2,1)S(1)} %get-tuple-element.114), channel_id=1, source_target_pairs={{0,1},{1,0},{2,3},{3,2},{4,5},{5,4},{6,7},{7,6},{8,9},{9,8},{10,11... | collective-permute-start | bytes 589832 | tf_op jit(solution)/shard_map/ppermute | solution.py:420
  44.2 0.8 %shard_map.100 = (f32[384,1024]{1,0:T(8,128)S(1)}, bf16[384,1024]{1,0:T(8,128)(2,1)S(1)}) custom-call(bf16[768,768]{1,0:T(8,128)(2,1)S(1)} %get-tuple-element.117.weight_ref, bf16[768,1024]{1,0:T(8,128)(2,1)S(1)} %get-tuple-element.91.refs_6_.unit_ref, bf16[384,1024]{1,0:T(8,128)(2,1)S(1)} %collective-permute-done.14.add_ref), custom_call_target="tpu_custom_call" | custom-call | flops 20000000000 | bytes 5898240 | tf_op jit(solution)/shard_map/pallas_call | solution.py:46
  45.0 0.3 collective-permute-done.15.in_ref
  45.3 0.1 shard_map.102
  45.4 1.6 %collective-permute-start.16 = (bf16[192,1024]{1,0:T(8,128)(2,1)S(1)}, bf16[192,1024]{1,0:T(8,128)(2,1)S(1)}, u32[]{:S(2)}, u32[]{:S(2)}) collective-permute-start(bf16[192,1024]{1,0:T(8,128)(2,1)S(1)} %shard_map.102), channel_id=1, source_target_pairs={{0,16},{4,12},{8,24},{12,4},{16,0},{20,28},{24,8},{28,20},{1,17},{... | collective-permute-start | bytes 1179656 | tf_op jit(solution)/shard_map/ppermute | solution.py:425
  47.0 4.4 %collective-permute-done.17.in_ref = bf16[192,1024]{1,0:T(8,128)(2,1)S(1)} collective-permute-done((bf16[192,1024]{1,0:T(8,128)(2,1)S(1)}, bf16[192,1024]{1,0:T(8,128)(2,1)S(1)}, u32[]{:S(2)}, u32[]{:S(2)}) %collective-permute-start.17) | collective-permute-done | bytes 393248 | tf_op jit(solution)/shard_map/ppermute | solution.py:425
  51.4 0.1 shard_map.103
  51.5 1.6 %collective-permute-start.18 = (bf16[192,1024]{1,0:T(8,128)(2,1)S(1)}, bf16[192,1024]{1,0:T(8,128)(2,1)S(1)}, u32[]{:S(2)}, u32[]{:S(2)}) collective-permute-start(bf16[192,1024]{1,0:T(8,128)(2,1)S(1)} %shard_map.103), channel_id=1, source_target_pairs={{0,16},{4,12},{8,24},{12,4},{16,0},{20,28},{24,8},{28,20},{1,17},{... | collective-permute-start | bytes 1179656 | tf_op jit(solution)/shard_map/ppermute | solution.py:425
  53.1 0.8 %shard_map.101.refs_6_ = f32[384,1024]{1,0:T(8,128)S(1)} custom-call(bf16[768,384]{1,0:T(8,128)(2,1)S(1)} %get-tuple-element.97.refs_8_.weight_ref, bf16[768,1024]{1,0:T(8,128)(2,1)S(1)} %get-tuple-element.91.refs_6_.unit_ref, bf16[384,1024]{1,0:T(8,128)(2,1)S(1)} %get-tuple-element.119.add_ref), custom_call_target="tpu_custom_call" | custom-call | tf_op jit(solution)/shard_map/pallas_call | solution.py:46
  53.9 4.5 %collective-permute-done.12.refs_1_.refs_2_ = bf16[384,256]{1,0:T(8,128)(2,1)S(1)} collective-permute-done((bf16[384,256]{1,0:T(8,128)(2,1)S(1)}, bf16[384,256]{1,0:T(8,128)(2,1)S(1)}, u32[]{:S(2)}, u32[]{:S(2)}) %collective-permute-start.12) | collective-permute-done | bytes 196640 | tf_op jit(solution)/shard_map/ppermute | solution.py:420
  58.4 0.9 %collective-permute-done.18.refs_8_ = bf16[192,1024]{1,0:T(8,128)(2,1)S(1)} collective-permute-done((bf16[192,1024]{1,0:T(8,128)(2,1)S(1)}, bf16[192,1024]{1,0:T(8,128)(2,1)S(1)}, u32[]{:S(2)}, u32[]{:S(2)}) %collective-permute-start.18) | collective-permute-done | bytes 393248 | tf_op jit(solution)/shard_map/ppermute | solution.py:425
  59.3 1.6 %shard_map.105 = (bf16[1536,256]{1,0:T(8,128)(2,1)}, bf16[384,1024]{1,0:T(8,128)(2,1)}) custom-call(bf16[384,256]{1,0:T(8,128)(2,1)S(1)} %get-tuple-element.111.refs_0_, bf16[384,256]{1,0:T(8,128)(2,1)S(1)} %collective-permute-done.11.refs_0_.refs_1_, bf16[384,256]{1,0:T(8,128)(2,1)S(1)} %collective-permute-done.12.refs_1_.refs_2_, ...), custom_call_target="tpu_custom_call" | custom-call | bytes 5705728 | tf_op jit(solution)/shard_map/pallas_call | solution.py:46
  (18 shorter events, 0.0 us)
Async XLA Ops:
  0.6 14.7 %collective-permute-start = (bf16[384,1024]{1,0:T(8,128)(2,1)}, bf16[384,1024]{1,0:T(8,128)(2,1)S(1)}, u32[]{:S(2)}, u32[]{:S(2)}) collective-permute-start(bf16[384,1024]{1,0:T(8,128)(2,1)} %raw_ref.1), channel_id=1, source_target_pairs={{0,16},{4,12},{8,24},{12,4},{16,0},{20,28},{24,8},{28,20},{1,17},{... | collective-permute-start | bytes 2359304 | tf_op jit(solution)/shard_map/ppermute | solution.py:425
  3.7 1.1 %copy-start = (bf16[1536,256]{1,0:T(8,128)(2,1)S(1)}, bf16[1536,256]{1,0:T(8,128)(2,1)}, u32[]{:S(2)}) copy-start(bf16[1536,256]{1,0:T(8,128)(2,1)} %text_ref.1) | copy-start | bytes 2359300
  4.8 8.8 %copy-start.1 = (s32[12288]{0:T(1024)S(1)}, s32[12288]{0:T(1024)}, u32[]{:S(2)}) copy-start(s32[12288]{0:T(1024)} %param.11) | copy-start | bytes 147460
  4.8 8.8 %copy-start.2 = (s32[12288]{0:T(1024)S(1)}, s32[12288]{0:T(1024)}, u32[]{:S(2)}) copy-start(s32[12288]{0:T(1024)} %param.12) | copy-start | bytes 147460
  4.8 8.8 %copy-start.3 = (s32[96,8,3]{0,1,2:T(8,128)S(1)}, s32[96,8,3]{0,1,2:T(8,128)}, u32[]{:S(2)}) copy-start(s32[96,8,3]{0,1,2:T(8,128)} %param.13) | copy-start | bytes 27652
  4.9 18.5 %collective-permute-start.1 = (bf16[384,256]{1,0:T(8,128)(2,1)S(1)}, bf16[384,256]{1,0:T(8,128)(2,1)S(1)}, u32[]{:S(2)}, u32[]{:S(2)}) collective-permute-start(bf16[384,256]{1,0:T(8,128)(2,1)S(1)} %get-tuple-element.78), channel_id=1, source_target_pairs={{0,3},{1,2},{2,1},{3,0},{4,7},{5,6},{6,5},{7,4},{8,11},{9,10},{10,... | collective-permute-start | bytes 589832 | tf_op jit(solution)/shard_map/ppermute | solution.py:420
  8.5 16.4 %collective-permute-start.2 = (bf16[384,256]{1,0:T(8,128)(2,1)S(1)}, bf16[384,256]{1,0:T(8,128)(2,1)S(1)}, u32[]{:S(2)}, u32[]{:S(2)}) collective-permute-start(bf16[384,256]{1,0:T(8,128)(2,1)S(1)} %get-tuple-element.79), channel_id=1, source_target_pairs={{0,2},{1,3},{2,0},{3,1},{4,6},{5,7},{6,4},{7,5},{8,10},{9,11},{10,... | collective-permute-start | bytes 589832 | tf_op jit(solution)/shard_map/ppermute | solution.py:420
  8.5 14.8 %collective-permute-start.3 = (bf16[384,256]{1,0:T(8,128)(2,1)S(1)}, bf16[384,256]{1,0:T(8,128)(2,1)S(1)}, u32[]{:S(2)}, u32[]{:S(2)}) collective-permute-start(bf16[384,256]{1,0:T(8,128)(2,1)S(1)} %get-tuple-element.80), channel_id=1, source_target_pairs={{0,1},{1,0},{2,3},{3,2},{4,5},{5,4},{6,7},{7,6},{8,9},{9,8},{10,11... | collective-permute-start | bytes 589832 | tf_op jit(solution)/shard_map/ppermute | solution.py:420
  10.7 12.3 %collective-permute-start.4 = (bf16[384,1024]{1,0:T(8,128)(2,1)}, bf16[384,1024]{1,0:T(8,128)(2,1)S(1)}, u32[]{:S(2)}, u32[]{:S(2)}) collective-permute-start(bf16[384,1024]{1,0:T(8,128)(2,1)} %raw_ref.1), channel_id=1, source_target_pairs={{0,8},{4,20},{8,0},{12,28},{16,24},{20,4},{24,16},{28,12},{1,9},{5... | collective-permute-start | bytes 2359304 | tf_op jit(solution)/shard_map/ppermute | solution.py:425
  15.3 16.6 %collective-permute-start.8 = (bf16[384,1024]{1,0:T(8,128)(2,1)S(1)}, bf16[384,1024]{1,0:T(8,128)(2,1)S(1)}, u32[]{:S(2)}, u32[]{:S(2)}) collective-permute-start(bf16[384,1024]{1,0:T(8,128)(2,1)S(1)} %collective-permute-done.raw_ref), channel_id=1, source_target_pairs={{0,8},{4,20},{8,0},{12,28},{16,24},{20,4},{24,16},{28,12},{1,9},{5... | collective-permute-start | bytes 2359304 | tf_op jit(solution)/shard_map/ppermute | solution.py:425
  25.3 2.2 %collective-permute-start.5 = (bf16[128,1024]{1,0:T(8,128)(2,1)S(1)}, bf16[128,1024]{1,0:T(8,128)(2,1)S(1)}, u32[]{:S(2)}, u32[]{:S(2)}) collective-permute-start(bf16[128,1024]{1,0:T(8,128)(2,1)S(1)} %get-tuple-element.88), channel_id=1, source_target_pairs={{0,4},{4,0},{8,12},{12,8},{16,20},{20,16},{24,28},{28,24},{1,5},{5... | collective-permute-start | bytes 786440 | tf_op jit(solution)/shard_map/ppermute | solution.py:420
  25.4 2.2 %collective-permute-start.6 = (bf16[128,1024]{1,0:T(8,128)(2,1)S(1)}, bf16[128,1024]{1,0:T(8,128)(2,1)S(1)}, u32[]{:S(2)}, u32[]{:S(2)}) collective-permute-start(bf16[128,1024]{1,0:T(8,128)(2,1)S(1)} %get-tuple-element.89), channel_id=1, source_target_pairs={{0,4},{4,0},{8,12},{12,8},{16,20},{20,16},{24,28},{28,24},{1,5},{5... | collective-permute-start | bytes 786440 | tf_op jit(solution)/shard_map/ppermute | solution.py:420
  25.9 1.8 %collective-permute-start.7 = (bf16[128,1024]{1,0:T(8,128)(2,1)S(1)}, bf16[128,1024]{1,0:T(8,128)(2,1)S(1)}, u32[]{:S(2)}, u32[]{:S(2)}) collective-permute-start(bf16[128,1024]{1,0:T(8,128)(2,1)S(1)} %get-tuple-element.90), channel_id=1, source_target_pairs={{0,4},{4,0},{8,12},{12,8},{16,20},{20,16},{24,28},{28,24},{1,5},{5... | collective-permute-start | bytes 786440 | tf_op jit(solution)/shard_map/ppermute | solution.py:420
  29.0 13.2 %collective-permute-start.14 = (bf16[384,1024]{1,0:T(8,128)(2,1)S(1)}, bf16[384,1024]{1,0:T(8,128)(2,1)S(1)}, u32[]{:S(2)}, u32[]{:S(2)}) collective-permute-start(bf16[384,1024]{1,0:T(8,128)(2,1)S(1)} %get-tuple-element.118), channel_id=1, source_target_pairs={{0,8},{4,20},{8,0},{12,28},{16,24},{20,4},{24,16},{28,12},{1,9},{5... | collective-permute-start | bytes 2359304 | tf_op jit(solution)/shard_map/ppermute | solution.py:425
  34.2 4.9 %collective-permute-start.9 = (bf16[192,1024]{1,0:T(8,128)(2,1)S(1)}, bf16[192,1024]{1,0:T(8,128)(2,1)S(1)}, u32[]{:S(2)}, u32[]{:S(2)}) collective-permute-start(bf16[192,1024]{1,0:T(8,128)(2,1)S(1)} %get-tuple-element.108), channel_id=1, source_target_pairs={{0,4},{4,0},{8,12},{12,8},{16,20},{20,16},{24,28},{28,24},{1,5},{5... | collective-permute-start | bytes 1179656 | tf_op jit(solution)/shard_map/ppermute | solution.py:420
  35.3 3.8 %collective-permute-start.10 = (bf16[192,1024]{1,0:T(8,128)(2,1)S(1)}, bf16[192,1024]{1,0:T(8,128)(2,1)S(1)}, u32[]{:S(2)}, u32[]{:S(2)}) collective-permute-start(bf16[192,1024]{1,0:T(8,128)(2,1)S(1)} %get-tuple-element.109), channel_id=1, source_target_pairs={{0,4},{4,0},{8,12},{12,8},{16,20},{20,16},{24,28},{28,24},{1,5},{5... | collective-permute-start | bytes 1179656 | tf_op jit(solution)/shard_map/ppermute | solution.py:420
  37.0 8.3 %collective-permute-start.15 = (bf16[192,1024]{1,0:T(8,128)(2,1)S(1)}, bf16[192,1024]{1,0:T(8,128)(2,1)S(1)}, u32[]{:S(2)}, u32[]{:S(2)}) collective-permute-start(bf16[192,1024]{1,0:T(8,128)(2,1)S(1)} %get-tuple-element.121), channel_id=1, source_target_pairs={{0,8},{4,20},{8,0},{12,28},{16,24},{20,4},{24,16},{28,12},{1,9},{5... | collective-permute-start | bytes 1179656 | tf_op jit(solution)/shard_map/ppermute | solution.py:425
  37.9 13.5 %collective-permute-start.17 = (bf16[192,1024]{1,0:T(8,128)(2,1)S(1)}, bf16[192,1024]{1,0:T(8,128)(2,1)S(1)}, u32[]{:S(2)}, u32[]{:S(2)}) collective-permute-start(bf16[192,1024]{1,0:T(8,128)(2,1)S(1)} %get-tuple-element.123), channel_id=1, source_target_pairs={{0,8},{4,20},{8,0},{12,28},{16,24},{20,4},{24,16},{28,12},{1,9},{5... | collective-permute-start | bytes 1179656 | tf_op jit(solution)/shard_map/ppermute | solution.py:425
  39.7 14.2 %collective-permute-start.11 = (bf16[384,256]{1,0:T(8,128)(2,1)S(1)}, bf16[384,256]{1,0:T(8,128)(2,1)S(1)}, u32[]{:S(2)}, u32[]{:S(2)}) collective-permute-start(bf16[384,256]{1,0:T(8,128)(2,1)S(1)} %get-tuple-element.112), channel_id=1, source_target_pairs={{0,3},{1,2},{2,1},{3,0},{4,7},{5,6},{6,5},{7,4},{8,11},{9,10},{10,... | collective-permute-start | bytes 589832 | tf_op jit(solution)/shard_map/ppermute | solution.py:420
  42.2 16.2 %collective-permute-start.12 = (bf16[384,256]{1,0:T(8,128)(2,1)S(1)}, bf16[384,256]{1,0:T(8,128)(2,1)S(1)}, u32[]{:S(2)}, u32[]{:S(2)}) collective-permute-start(bf16[384,256]{1,0:T(8,128)(2,1)S(1)} %get-tuple-element.113), channel_id=1, source_target_pairs={{0,2},{1,3},{2,0},{3,1},{4,6},{5,7},{6,4},{7,5},{8,10},{9,11},{10,... | collective-permute-start | bytes 589832 | tf_op jit(solution)/shard_map/ppermute | solution.py:420
  42.2 16.2 %collective-permute-start.13 = (bf16[384,256]{1,0:T(8,128)(2,1)S(1)}, bf16[384,256]{1,0:T(8,128)(2,1)S(1)}, u32[]{:S(2)}, u32[]{:S(2)}) collective-permute-start(bf16[384,256]{1,0:T(8,128)(2,1)S(1)} %get-tuple-element.114), channel_id=1, source_target_pairs={{0,1},{1,0},{2,3},{3,2},{4,5},{5,4},{6,7},{7,6},{8,9},{9,8},{10,11... | collective-permute-start | bytes 589832 | tf_op jit(solution)/shard_map/ppermute | solution.py:420
  45.4 13.9 %collective-permute-start.16 = (bf16[192,1024]{1,0:T(8,128)(2,1)S(1)}, bf16[192,1024]{1,0:T(8,128)(2,1)S(1)}, u32[]{:S(2)}, u32[]{:S(2)}) collective-permute-start(bf16[192,1024]{1,0:T(8,128)(2,1)S(1)} %shard_map.102), channel_id=1, source_target_pairs={{0,16},{4,12},{8,24},{12,4},{16,0},{20,28},{24,8},{28,20},{1,17},{... | collective-permute-start | bytes 1179656 | tf_op jit(solution)/shard_map/ppermute | solution.py:425
  51.5 7.8 %collective-permute-start.18 = (bf16[192,1024]{1,0:T(8,128)(2,1)S(1)}, bf16[192,1024]{1,0:T(8,128)(2,1)S(1)}, u32[]{:S(2)}, u32[]{:S(2)}) collective-permute-start(bf16[192,1024]{1,0:T(8,128)(2,1)S(1)} %shard_map.103), channel_id=1, source_target_pairs={{0,16},{4,12},{8,24},{12,4},{16,0},{20,28},{24,8},{28,20},{1,17},{... | collective-permute-start | bytes 1179656 | tf_op jit(solution)/shard_map/ppermute | solution.py:425

commit v11 on v10

--- a/solution.py
+++ b/solution.py
@@ -13,7 +13,7 @@
 WAIT_FLOPS = 20_000_000_000
 TEXT_PIECES = 3
 ACC_PIECES = 2
-LAST_PIECES = 2
+LAST_PIECES = 1
 CORES = 2
 EPS = 1e-06
 LOG2E = math.log2(math.e)
@@ -583,6 +583,10 @@
         lists + [units, own_images, own_weights, from_far],
         limit=16,
     )
+    far_sum = call_kernel(
+        far_sum_body, [bf16(rows // LAST_PIECES)] * LAST_PIECES, [far_weights, units], limit=16
+    )
+    far_images, far_sum[0] = lax.optimization_barrier((far_images, far_sum[0]))
     acc_other = call_kernel(
         functools.partial(text_sum_body, 1),
         [bf16(rows // ACC_PIECES)] * ACC_PIECES,
@@ -596,18 +600,13 @@
         [far_weights, far_images, acc],
         limit=16,
     )[0]
-    far_weights, acc_own = lax.optimization_barrier((far_weights, acc_own))
-    far_sum = call_kernel(
-        far_sum_body, [bf16(rows // LAST_PIECES)] * LAST_PIECES, [far_weights, units], limit=16
-    )
-    acc_own, far_sum[0] = lax.optimization_barrier((acc_own, far_sum[0]))
     text_parts = finish_text(acc_own, acc_other)
     near_weights, text_parts[0] = lax.optimization_barrier((near_weights, text_parts[0]))
     second_sum, image_add = call_kernel(
         second_sum_body,
         [f32(rows), bf16(rows)],
         [near_weights, units, image_add],
-        flops=WAIT_FLOPS,
+        flops=0,
         limit=16,
     )
     image_last = []

time: 61.1 us -> 63.5 us (1.039)
  waiting for transfers between devices: 16.6 us -> 21.8 us
  starting transfers between devices: 24.5 us -> 21.7 us
    ppermute x11, waiting for transfers between devices: 6.24 us -> 10.8 us  [swap(): return lax.ppermute(value, axis, [(i, i ^ bits) for i in range(count)])]
    ppermute x8 -> x6, starting transfers between devices: 13.8 us -> 11.6 us  [swap_near(): lax.ppermute(value, 'blk', [(i, i ^ neighbour_bits(i)[which]) for i in ra...]
    ppermute x8 -> x6, waiting for transfers between devices: 10.3 us -> 11 us  [swap_near(): lax.ppermute(value, 'blk', [(i, i ^ neighbour_bits(i)[which]) for i in ra...]
    pallas_call x20 -> x19, Pallas kernels: 16.5 us -> 16.4 us  [call_kernel(): pl.pallas_call(body, out_shape=outs, in_specs=specs, out_specs=[ANY_SPEC...]
  transfers between devices with their start and end apart: 19 -> 17, of which waited for: 8 -> 9; matrix products, arithmetic and copies ran while one was open for 0% -> 0% of each run, Pallas kernels for 25% -> 23%
where the time goes in v11:
time: 63.5 us; the launch traced here: 63.2 us
  waiting for transfers between devices  21.8 us (34%)
  starting transfers between devices  21.7 us (34%)
  Pallas kernels  16.4 us (26%)
  between operations  2.13 us (3%)
  local copies, waits for them, and re-layouts  1.14 us (2%)
    pallas_call x19, Pallas kernels, call_kernel(): pl.pallas_call(body, out_shape=outs, in_specs=specs, out_specs=[ANY_SPEC...  16.4 us
    ppermute x6, starting transfers between devices, swap_near(): lax.ppermute(value, 'blk', [(i, i ^ neighbour_bits(i)[which]) for i in ra...  11.6 us
    ppermute x6, waiting for transfers between devices, swap_near(): lax.ppermute(value, 'blk', [(i, i ^ neighbour_bits(i)[which]) for i in ra...  11 us
    ppermute x11, waiting for transfers between devices, swap(): return lax.ppermute(value, axis, [(i, i ^ bits) for i in range(count)])  10.8 us
    ppermute x11, starting transfers between devices, swap(): return lax.ppermute(value, axis, [(i, i ^ bits) for i in range(count)])  10.1 us
  transfers between devices with their start and end apart: 17, of which 9 were waited for; matrix products, arithmetic and copies ran while one was open for 0% of the time, Pallas kernels for 23%

profile of v11, /device:TPU:0, one launch (start us, length us, event | category | flops | bytes accessed | tf_op | source)
XLA Modules:
  0.0 63.2 jit_solution(3616704832917829096)
XLA Ops:
  0.6 3.0 %collective-permute-start = (bf16[384,1024]{1,0:T(8,128)(2,1)}, bf16[384,1024]{1,0:T(8,128)(2,1)S(1)}, u32[]{:S(2)}, u32[]{:S(2)}) collective-permute-start(bf16[384,1024]{1,0:T(8,128)(2,1)} %raw_ref.1), channel_id=1, source_target_pairs={{0,16},{4,12},{8,24},{12,4},{16,0},{20,28},{24,8},{28,20},{1,17},{... | collective-permute-start | bytes 2359304 | tf_op jit(solution)/shard_map/ppermute | solution.py:425
  3.7 1.1 %copy-done = bf16[1536,256]{1,0:T(8,128)(2,1)S(1)} copy-done((bf16[1536,256]{1,0:T(8,128)(2,1)S(1)}, bf16[1536,256]{1,0:T(8,128)(2,1)}, u32[]{:S(2)}) %copy-start) | copy-done | bytes 786456
  4.8 0.1 shard_map.88
  4.9 3.7 %collective-permute-start.1 = (bf16[384,256]{1,0:T(8,128)(2,1)S(1)}, bf16[384,256]{1,0:T(8,128)(2,1)S(1)}, u32[]{:S(2)}, u32[]{:S(2)}) collective-permute-start(bf16[384,256]{1,0:T(8,128)(2,1)S(1)} %get-tuple-element.73), channel_id=1, source_target_pairs={{0,3},{1,2},{2,1},{3,0},{4,7},{5,6},{6,5},{7,4},{8,11},{9,10},{10,... | collective-permute-start | bytes 589832 | tf_op jit(solution)/shard_map/ppermute | solution.py:420
  8.5 0.0 collective-permute-start.2
  8.5 0.8 %collective-permute-start.3 = (bf16[384,256]{1,0:T(8,128)(2,1)S(1)}, bf16[384,256]{1,0:T(8,128)(2,1)S(1)}, u32[]{:S(2)}, u32[]{:S(2)}) collective-permute-start(bf16[384,256]{1,0:T(8,128)(2,1)S(1)} %get-tuple-element.75), channel_id=1, source_target_pairs={{0,1},{1,0},{2,3},{3,2},{4,5},{5,4},{6,7},{7,6},{8,9},{9,8},{10,11... | collective-permute-start | bytes 589832 | tf_op jit(solution)/shard_map/ppermute | solution.py:420
  9.3 1.4 %shard_map.86 = (bf16[384,1024]{1,0:T(8,128)(2,1)S(1)}, bf16[384,1024]{1,0:T(8,128)(2,1)S(1)}, f32[384,128]{1,0:T(8,128)S(1)}) custom-call(bf16[384,1024]{1,0:T(8,128)(2,1)} %raw_ref.1), custom_call_target="tpu_custom_call" | custom-call | bytes 2555904 | tf_op jit(solution)/shard_map/pallas_call | solution.py:46
  10.7 1.6 %collective-permute-start.4 = (bf16[384,1024]{1,0:T(8,128)(2,1)}, bf16[384,1024]{1,0:T(8,128)(2,1)S(1)}, u32[]{:S(2)}, u32[]{:S(2)}) collective-permute-start(bf16[384,1024]{1,0:T(8,128)(2,1)} %raw_ref.1), channel_id=1, source_target_pairs={{0,8},{4,20},{8,0},{12,28},{16,24},{20,4},{24,16},{28,12},{1,9},{5... | collective-permute-start | bytes 2359304 | tf_op jit(solution)/shard_map/ppermute | solution.py:425
  13.6 1.1 %shard_map.87 = (f32[2,128]{1,0:T(2,128)S(1)}, f32[72,128]{1,0:T(8,128)S(1)}, s32[12,128]{1,0:T(8,128)S(1)}, s32[768,128]{1,0:T(8,128)S(1)}, f32[384,128]{1,0:T(8,128)S(1)}, /*index=5*/f32[4,128]{1,0:T(4,128)S(1)}) custom-call(f32[1]{0:T(128)S(6)} %copy.9.refs_0_, f32[1]{0:T(128)S(6)} %copy.10.refs_1_, s32[3,8,96]{2,1,0:T(8,128)S(1)} %bitcast.5, ...), custom_call_target="tpu_custom_call" | custom-call | bytes 743432 | tf_op jit(solution)/shard_map/pallas_call | solution.py:46
  14.7 0.6 collective-permute-done.raw_ref
  15.3 3.3 %collective-permute-start.8 = (bf16[384,1024]{1,0:T(8,128)(2,1)S(1)}, bf16[384,1024]{1,0:T(8,128)(2,1)S(1)}, u32[]{:S(2)}, u32[]{:S(2)}) collective-permute-start(bf16[384,1024]{1,0:T(8,128)(2,1)S(1)} %collective-permute-done.raw_ref), channel_id=1, source_target_pairs={{0,8},{4,20},{8,0},{12,28},{16,24},{20,4},{24,16},{28,12},{1,9},{5... | collective-permute-start | bytes 2359304 | tf_op jit(solution)/shard_map/ppermute | solution.py:425
  18.6 0.2 shard_map.89.second_unit_ref
  18.9 4.1 %collective-permute-done.4.first_ref = bf16[384,1024]{1,0:T(8,128)(2,1)S(1)} collective-permute-done((bf16[384,1024]{1,0:T(8,128)(2,1)}, bf16[384,1024]{1,0:T(8,128)(2,1)S(1)}, u32[]{:S(2)}, u32[]{:S(2)}) %collective-permute-start.4) | collective-permute-done | bytes 786464 | tf_op jit(solution)/shard_map/ppermute | solution.py:425
  23.0 0.3 shard_map.90.refs_8_.refs_7_
  23.3 0.0 collective-permute-done.3.refs_3_.refs_4_
  23.3 1.6 %collective-permute-done.2.refs_2_.refs_3_ = bf16[384,256]{1,0:T(8,128)(2,1)S(1)} collective-permute-done((bf16[384,256]{1,0:T(8,128)(2,1)S(1)}, bf16[384,256]{1,0:T(8,128)(2,1)S(1)}, u32[]{:S(2)}, u32[]{:S(2)}) %collective-permute-start.2) | collective-permute-done | bytes 196640 | tf_op jit(solution)/shard_map/ppermute | solution.py:420
  24.9 0.4 shard_map.91
  25.3 0.1 collective-permute-start.5
  25.4 0.5 collective-permute-start.6
  25.9 0.1 collective-permute-start.7
  26.0 1.6 %shard_map.92 = (bf16[384,384]{1,0:T(8,128)(2,1)S(1)}, bf16[384,768]{1,0:T(8,128)(2,1)S(1)}) custom-call(f32[2,128]{1,0:T(2,128)S(1)} %get-tuple-element.66.refs_0_, f32[72,128]{1,0:T(8,128)S(1)} %get-tuple-element.67.refs_1_, s32[12,128]{1,0:T(8,128)S(1)} %get-tuple-element.68.refs_2_, s32[768,128]{1,0:T(8,128)S(1)} %get-tuple-element.69.refs_3_, ...), custom_call_target="tpu_custom_call" | custom-call | bytes 4666368 | tf_op jit(solution)/shard_map/pallas_call | solution.py:46
  27.6 0.1 collective-permute-done.7.refs_11_
  27.7 1.3 %shard_map.93 = (bf16[768,1024]{1,0:T(8,128)(2,1)S(1)}, bf16[768,384]{1,0:T(8,128)(2,1)S(1)}, bf16[384,1024]{1,0:T(8,128)(2,1)S(1)}) custom-call(f32[2,128]{1,0:T(2,128)S(1)} %get-tuple-element.66.refs_0_, f32[72,128]{1,0:T(8,128)S(1)} %get-tuple-element.67.refs_1_, s32[12,128]{1,0:T(8,128)S(1)} %get-tuple-element.68.refs_2_, ...), custom_call_target="tpu_custom_call" | custom-call | bytes 7320576 | tf_op jit(solution)/shard_map/pallas_call | solution.py:46
  29.0 0.6 collective-permute-start.14
  29.6 2.3 %shard_map.94 = (bf16[768,384]{1,0:T(8,128)(2,1)S(1)}, f32[768,1024]{1,0:T(8,128)S(1)}, bf16[768,768]{1,0:T(8,128)(2,1)S(1)}) custom-call(f32[2,128]{1,0:T(2,128)S(1)} %get-tuple-element.66.refs_0_, f32[72,128]{1,0:T(8,128)S(1)} %get-tuple-element.67.refs_1_, s32[12,128]{1,0:T(8,128)S(1)} %get-tuple-element.68.refs_2_, ...), custom_call_target="tpu_custom_call" | custom-call | bytes 10957824 | tf_op jit(solution)/shard_map/pallas_call | solution.py:46
  31.9 0.0 collective-permute-done.8.refs_9_
  31.9 1.4 %shard_map.95 = (bf16[768,768]{1,0:T(8,128)(2,1)S(1)}, bf16[768,1024]{1,0:T(8,128)(2,1)S(1)}) custom-call(f32[2,128]{1,0:T(2,128)S(1)} %get-tuple-element.66.refs_0_, f32[72,128]{1,0:T(8,128)S(1)} %get-tuple-element.67.refs_1_, s32[12,128]{1,0:T(8,128)S(1)} %get-tuple-element.68.refs_2_, s32[768,128]{1,0:T(8,128)S(1)} %get-tuple-element.69.refs_3_, ...), custom_call_target="tpu_custom_call" | custom-call | bytes 7123968 | tf_op jit(solution)/shard_map/pallas_call | solution.py:46
  33.4 0.8 %shard_map.96 = bf16[384,1024]{1,0:T(8,128)(2,1)S(1)} custom-call(bf16[768,768]{1,0:T(8,128)(2,1)S(1)} %get-tuple-element.94.weight_ref, bf16[768,1024]{1,0:T(8,128)(2,1)S(1)} %get-tuple-element.86.refs_6_.unit_ref), custom_call_target="tpu_custom_call" | custom-call | bytes 3538944 | tf_op jit(solution)/shard_map/pallas_call | solution.py:46
  34.2 1.5 %collective-permute-start.15 = (bf16[384,1024]{1,0:T(8,128)(2,1)S(1)}, bf16[384,1024]{1,0:T(8,128)(2,1)S(1)}, u32[]{:S(2)}, u32[]{:S(2)}) collective-permute-start(bf16[384,1024]{1,0:T(8,128)(2,1)S(1)} %shard_map.96), channel_id=1, source_target_pairs={{0,8},{4,20},{8,0},{12,28},{16,24},{20,4},{24,16},{28,12},{1,9},{5... | collective-permute-start | bytes 2359304 | tf_op jit(solution)/shard_map/ppermute | solution.py:425
  35.7 0.8 %shard_map.97 = (bf16[192,1024]{1,0:T(8,128)(2,1)S(1)}, bf16[192,1024]{1,0:T(8,128)(2,1)S(1)}) custom-call(bf16[768,768]{1,0:T(8,128)(2,1)S(1)} %get-tuple-element.94.weight_ref, bf16[768,1024]{1,0:T(8,128)(2,1)S(1)} %get-tuple-element.99.image_ref, f32[768,1024]{1,0:T(8,128)S(1)} %get-tuple-element.97.acc_ref), custom_call_target="tpu_custom_call" | custom-call | bytes 6684672 | tf_op jit(solution)/shard_map/pallas_call | solution.py:46
  36.5 0.1 collective-permute-start.9
  36.6 0.5 collective-permute-start.10
  37.1 0.8 %shard_map.98.refs_5_ = f32[384,1024]{1,0:T(8,128)S(1)} custom-call(bf16[768,768]{1,0:T(8,128)(2,1)S(1)} %get-tuple-element.94.weight_ref, bf16[768,1024]{1,0:T(8,128)(2,1)S(1)} %get-tuple-element.99.image_ref, f32[768,1024]{1,0:T(8,128)S(1)} %get-tuple-element.97.acc_ref), custom_call_target="tpu_custom_call" | custom-call | bytes 7471104 | tf_op jit(solution)/shard_map/pallas_call | solution.py:46
  37.8 0.4 collective-permute-done.9.refs_6_
  38.3 0.6 collective-permute-done.10.refs_7_
  38.8 0.6 shard_map.99
  39.5 3.2 %collective-permute-start.11 = (bf16[384,256]{1,0:T(8,128)(2,1)S(1)}, bf16[384,256]{1,0:T(8,128)(2,1)S(1)}, u32[]{:S(2)}, u32[]{:S(2)}) collective-permute-start(bf16[384,256]{1,0:T(8,128)(2,1)S(1)} %get-tuple-element.104), channel_id=1, source_target_pairs={{0,3},{1,2},{2,1},{3,0},{4,7},{5,6},{6,5},{7,4},{8,11},{9,10},{10,... | collective-permute-start | bytes 589832 | tf_op jit(solution)/shard_map/ppermute | solution.py:420
  42.6 1.3 %collective-permute-start.13 = (bf16[384,256]{1,0:T(8,128)(2,1)S(1)}, bf16[384,256]{1,0:T(8,128)(2,1)S(1)}, u32[]{:S(2)}, u32[]{:S(2)}) collective-permute-start(bf16[384,256]{1,0:T(8,128)(2,1)S(1)} %get-tuple-element.106), channel_id=1, source_target_pairs={{0,1},{1,0},{2,3},{3,2},{4,5},{5,4},{6,7},{7,6},{8,9},{9,8},{10,11... | collective-permute-start | bytes 589832 | tf_op jit(solution)/shard_map/ppermute | solution.py:420
  43.9 0.0 collective-permute-done.14.add_ref
  43.9 0.8 %shard_map.100 = (f32[384,1024]{1,0:T(8,128)S(1)}, bf16[384,1024]{1,0:T(8,128)(2,1)S(1)}) custom-call(bf16[768,768]{1,0:T(8,128)(2,1)S(1)} %get-tuple-element.109.weight_ref, bf16[768,1024]{1,0:T(8,128)(2,1)S(1)} %get-tuple-element.86.refs_6_.unit_ref, bf16[384,1024]{1,0:T(8,128)(2,1)S(1)} %collective-permute-done.14.add_ref), custom_call_target="tpu_custom_call" | custom-call | bytes 5898240 | tf_op jit(solution)/shard_map/pallas_call | solution.py:46
  44.7 0.8 %shard_map.101.refs_6_ = f32[384,1024]{1,0:T(8,128)S(1)} custom-call(bf16[768,384]{1,0:T(8,128)(2,1)S(1)} %get-tuple-element.92.refs_8_.weight_ref, bf16[768,1024]{1,0:T(8,128)(2,1)S(1)} %get-tuple-element.86.refs_6_.unit_ref, bf16[384,1024]{1,0:T(8,128)(2,1)S(1)} %get-tuple-element.111.add_ref), custom_call_target="tpu_custom_call" | custom-call | tf_op jit(solution)/shard_map/pallas_call | solution.py:46
  45.6 3.9 %collective-permute-done.15.in_ref = bf16[384,1024]{1,0:T(8,128)(2,1)S(1)} collective-permute-done((bf16[384,1024]{1,0:T(8,128)(2,1)S(1)}, bf16[384,1024]{1,0:T(8,128)(2,1)S(1)}, u32[]{:S(2)}, u32[]{:S(2)}) %collective-permute-start.15) | collective-permute-done | bytes 786464 | tf_op jit(solution)/shard_map/ppermute | solution.py:425
  49.5 0.1 shard_map.102
  49.6 1.6 %collective-permute-start.16 = (bf16[384,1024]{1,0:T(8,128)(2,1)S(1)}, bf16[384,1024]{1,0:T(8,128)(2,1)S(1)}, u32[]{:S(2)}, u32[]{:S(2)}) collective-permute-start(bf16[384,1024]{1,0:T(8,128)(2,1)S(1)} %shard_map.102), channel_id=1, source_target_pairs={{0,16},{4,12},{8,24},{12,4},{16,0},{20,28},{24,8},{28,20},{1,17},{... | collective-permute-start | bytes 2359304 | tf_op jit(solution)/shard_map/ppermute | solution.py:425
  51.2 0.0 collective-permute-done.11.refs_0_.refs_1_
  51.2 8.1 %collective-permute-done.12.refs_1_.refs_2_ = bf16[384,256]{1,0:T(8,128)(2,1)S(1)} collective-permute-done((bf16[384,256]{1,0:T(8,128)(2,1)S(1)}, bf16[384,256]{1,0:T(8,128)(2,1)S(1)}, u32[]{:S(2)}, u32[]{:S(2)}) %collective-permute-start.12) | collective-permute-done | bytes 196640 | tf_op jit(solution)/shard_map/ppermute | solution.py:420
  59.3 2.4 %collective-permute-done.16.refs_7_ = bf16[384,1024]{1,0:T(8,128)(2,1)S(1)} collective-permute-done((bf16[384,1024]{1,0:T(8,128)(2,1)S(1)}, bf16[384,1024]{1,0:T(8,128)(2,1)S(1)}, u32[]{:S(2)}, u32[]{:S(2)}) %collective-permute-start.16) | collective-permute-done | bytes 786464 | tf_op jit(solution)/shard_map/ppermute | solution.py:425
  61.7 1.6 %shard_map.104 = (bf16[1536,256]{1,0:T(8,128)(2,1)}, bf16[384,1024]{1,0:T(8,128)(2,1)}) custom-call(bf16[384,256]{1,0:T(8,128)(2,1)S(1)} %get-tuple-element.103.refs_0_, bf16[384,256]{1,0:T(8,128)(2,1)S(1)} %collective-permute-done.11.refs_0_.refs_1_, bf16[384,256]{1,0:T(8,128)(2,1)S(1)} %collective-permute-done.12.refs_1_.refs_2_, ...), custom_call_target="tpu_custom_call" | custom-call | bytes 5705728 | tf_op jit(solution)/shard_map/pallas_call | solution.py:46
  (13 shorter events, 0.0 us)
Async XLA Ops:
  0.6 14.7 %collective-permute-start = (bf16[384,1024]{1,0:T(8,128)(2,1)}, bf16[384,1024]{1,0:T(8,128)(2,1)S(1)}, u32[]{:S(2)}, u32[]{:S(2)}) collective-permute-start(bf16[384,1024]{1,0:T(8,128)(2,1)} %raw_ref.1), channel_id=1, source_target_pairs={{0,16},{4,12},{8,24},{12,4},{16,0},{20,28},{24,8},{28,20},{1,17},{... | collective-permute-start | bytes 2359304 | tf_op jit(solution)/shard_map/ppermute | solution.py:425
  3.7 1.1 %copy-start = (bf16[1536,256]{1,0:T(8,128)(2,1)S(1)}, bf16[1536,256]{1,0:T(8,128)(2,1)}, u32[]{:S(2)}) copy-start(bf16[1536,256]{1,0:T(8,128)(2,1)} %text_ref.1) | copy-start | bytes 2359300
  4.8 8.8 %copy-start.1 = (s32[12288]{0:T(1024)S(1)}, s32[12288]{0:T(1024)}, u32[]{:S(2)}) copy-start(s32[12288]{0:T(1024)} %param.11) | copy-start | bytes 147460
  4.8 8.8 %copy-start.2 = (s32[12288]{0:T(1024)S(1)}, s32[12288]{0:T(1024)}, u32[]{:S(2)}) copy-start(s32[12288]{0:T(1024)} %param.12) | copy-start | bytes 147460
  4.8 8.8 %copy-start.3 = (s32[96,8,3]{0,1,2:T(8,128)S(1)}, s32[96,8,3]{0,1,2:T(8,128)}, u32[]{:S(2)}) copy-start(s32[96,8,3]{0,1,2:T(8,128)} %param.13) | copy-start | bytes 27652
  4.9 18.5 %collective-permute-start.1 = (bf16[384,256]{1,0:T(8,128)(2,1)S(1)}, bf16[384,256]{1,0:T(8,128)(2,1)S(1)}, u32[]{:S(2)}, u32[]{:S(2)}) collective-permute-start(bf16[384,256]{1,0:T(8,128)(2,1)S(1)} %get-tuple-element.73), channel_id=1, source_target_pairs={{0,3},{1,2},{2,1},{3,0},{4,7},{5,6},{6,5},{7,4},{8,11},{9,10},{10,... | collective-permute-start | bytes 589832 | tf_op jit(solution)/shard_map/ppermute | solution.py:420
  8.5 16.4 %collective-permute-start.2 = (bf16[384,256]{1,0:T(8,128)(2,1)S(1)}, bf16[384,256]{1,0:T(8,128)(2,1)S(1)}, u32[]{:S(2)}, u32[]{:S(2)}) collective-permute-start(bf16[384,256]{1,0:T(8,128)(2,1)S(1)} %get-tuple-element.74), channel_id=1, source_target_pairs={{0,2},{1,3},{2,0},{3,1},{4,6},{5,7},{6,4},{7,5},{8,10},{9,11},{10,... | collective-permute-start | bytes 589832 | tf_op jit(solution)/shard_map/ppermute | solution.py:420
  8.5 14.8 %collective-permute-start.3 = (bf16[384,256]{1,0:T(8,128)(2,1)S(1)}, bf16[384,256]{1,0:T(8,128)(2,1)S(1)}, u32[]{:S(2)}, u32[]{:S(2)}) collective-permute-start(bf16[384,256]{1,0:T(8,128)(2,1)S(1)} %get-tuple-element.75), channel_id=1, source_target_pairs={{0,1},{1,0},{2,3},{3,2},{4,5},{5,4},{6,7},{7,6},{8,9},{9,8},{10,11... | collective-permute-start | bytes 589832 | tf_op jit(solution)/shard_map/ppermute | solution.py:420
  10.7 12.3 %collective-permute-start.4 = (bf16[384,1024]{1,0:T(8,128)(2,1)}, bf16[384,1024]{1,0:T(8,128)(2,1)S(1)}, u32[]{:S(2)}, u32[]{:S(2)}) collective-permute-start(bf16[384,1024]{1,0:T(8,128)(2,1)} %raw_ref.1), channel_id=1, source_target_pairs={{0,8},{4,20},{8,0},{12,28},{16,24},{20,4},{24,16},{28,12},{1,9},{5... | collective-permute-start | bytes 2359304 | tf_op jit(solution)/shard_map/ppermute | solution.py:425
  15.3 16.6 %collective-permute-start.8 = (bf16[384,1024]{1,0:T(8,128)(2,1)S(1)}, bf16[384,1024]{1,0:T(8,128)(2,1)S(1)}, u32[]{:S(2)}, u32[]{:S(2)}) collective-permute-start(bf16[384,1024]{1,0:T(8,128)(2,1)S(1)} %collective-permute-done.raw_ref), channel_id=1, source_target_pairs={{0,8},{4,20},{8,0},{12,28},{16,24},{20,4},{24,16},{28,12},{1,9},{5... | collective-permute-start | bytes 2359304 | tf_op jit(solution)/shard_map/ppermute | solution.py:425
  25.3 2.2 %collective-permute-start.5 = (bf16[128,1024]{1,0:T(8,128)(2,1)S(1)}, bf16[128,1024]{1,0:T(8,128)(2,1)S(1)}, u32[]{:S(2)}, u32[]{:S(2)}) collective-permute-start(bf16[128,1024]{1,0:T(8,128)(2,1)S(1)} %get-tuple-element.83), channel_id=1, source_target_pairs={{0,4},{4,0},{8,12},{12,8},{16,20},{20,16},{24,28},{28,24},{1,5},{5... | collective-permute-start | bytes 786440 | tf_op jit(solution)/shard_map/ppermute | solution.py:420
  25.4 2.2 %collective-permute-start.6 = (bf16[128,1024]{1,0:T(8,128)(2,1)S(1)}, bf16[128,1024]{1,0:T(8,128)(2,1)S(1)}, u32[]{:S(2)}, u32[]{:S(2)}) collective-permute-start(bf16[128,1024]{1,0:T(8,128)(2,1)S(1)} %get-tuple-element.84), channel_id=1, source_target_pairs={{0,4},{4,0},{8,12},{12,8},{16,20},{20,16},{24,28},{28,24},{1,5},{5... | collective-permute-start | bytes 786440 | tf_op jit(solution)/shard_map/ppermute | solution.py:420
  25.9 1.8 %collective-permute-start.7 = (bf16[128,1024]{1,0:T(8,128)(2,1)S(1)}, bf16[128,1024]{1,0:T(8,128)(2,1)S(1)}, u32[]{:S(2)}, u32[]{:S(2)}) collective-permute-start(bf16[128,1024]{1,0:T(8,128)(2,1)S(1)} %get-tuple-element.85), channel_id=1, source_target_pairs={{0,4},{4,0},{8,12},{12,8},{16,20},{20,16},{24,28},{28,24},{1,5},{5... | collective-permute-start | bytes 786440 | tf_op jit(solution)/shard_map/ppermute | solution.py:420
  29.0 14.9 %collective-permute-start.14 = (bf16[384,1024]{1,0:T(8,128)(2,1)S(1)}, bf16[384,1024]{1,0:T(8,128)(2,1)S(1)}, u32[]{:S(2)}, u32[]{:S(2)}) collective-permute-start(bf16[384,1024]{1,0:T(8,128)(2,1)S(1)} %get-tuple-element.110), channel_id=1, source_target_pairs={{0,8},{4,20},{8,0},{12,28},{16,24},{20,4},{24,16},{28,12},{1,9},{5... | collective-permute-start | bytes 2359304 | tf_op jit(solution)/shard_map/ppermute | solution.py:425
  34.2 15.3 %collective-permute-start.15 = (bf16[384,1024]{1,0:T(8,128)(2,1)S(1)}, bf16[384,1024]{1,0:T(8,128)(2,1)S(1)}, u32[]{:S(2)}, u32[]{:S(2)}) collective-permute-start(bf16[384,1024]{1,0:T(8,128)(2,1)S(1)} %shard_map.96), channel_id=1, source_target_pairs={{0,8},{4,20},{8,0},{12,28},{16,24},{20,4},{24,16},{28,12},{1,9},{5... | collective-permute-start | bytes 2359304 | tf_op jit(solution)/shard_map/ppermute | solution.py:425
  36.5 1.8 %collective-permute-start.9 = (bf16[192,1024]{1,0:T(8,128)(2,1)S(1)}, bf16[192,1024]{1,0:T(8,128)(2,1)S(1)}, u32[]{:S(2)}, u32[]{:S(2)}) collective-permute-start(bf16[192,1024]{1,0:T(8,128)(2,1)S(1)} %get-tuple-element.100), channel_id=1, source_target_pairs={{0,4},{4,0},{8,12},{12,8},{16,20},{20,16},{24,28},{28,24},{1,5},{5... | collective-permute-start | bytes 1179656 | tf_op jit(solution)/shard_map/ppermute | solution.py:420
  36.6 2.3 %collective-permute-start.10 = (bf16[192,1024]{1,0:T(8,128)(2,1)S(1)}, bf16[192,1024]{1,0:T(8,128)(2,1)S(1)}, u32[]{:S(2)}, u32[]{:S(2)}) collective-permute-start(bf16[192,1024]{1,0:T(8,128)(2,1)S(1)} %get-tuple-element.101), channel_id=1, source_target_pairs={{0,4},{4,0},{8,12},{12,8},{16,20},{20,16},{24,28},{28,24},{1,5},{5... | collective-permute-start | bytes 1179656 | tf_op jit(solution)/shard_map/ppermute | solution.py:420
  39.5 11.7 %collective-permute-start.11 = (bf16[384,256]{1,0:T(8,128)(2,1)S(1)}, bf16[384,256]{1,0:T(8,128)(2,1)S(1)}, u32[]{:S(2)}, u32[]{:S(2)}) collective-permute-start(bf16[384,256]{1,0:T(8,128)(2,1)S(1)} %get-tuple-element.104), channel_id=1, source_target_pairs={{0,3},{1,2},{2,1},{3,0},{4,7},{5,6},{6,5},{7,4},{8,11},{9,10},{10,... | collective-permute-start | bytes 589832 | tf_op jit(solution)/shard_map/ppermute | solution.py:420
  42.6 16.7 %collective-permute-start.12 = (bf16[384,256]{1,0:T(8,128)(2,1)S(1)}, bf16[384,256]{1,0:T(8,128)(2,1)S(1)}, u32[]{:S(2)}, u32[]{:S(2)}) collective-permute-start(bf16[384,256]{1,0:T(8,128)(2,1)S(1)} %get-tuple-element.105), channel_id=1, source_target_pairs={{0,2},{1,3},{2,0},{3,1},{4,6},{5,7},{6,4},{7,5},{8,10},{9,11},{10,... | collective-permute-start | bytes 589832 | tf_op jit(solution)/shard_map/ppermute | solution.py:420
  42.6 16.7 %collective-permute-start.13 = (bf16[384,256]{1,0:T(8,128)(2,1)S(1)}, bf16[384,256]{1,0:T(8,128)(2,1)S(1)}, u32[]{:S(2)}, u32[]{:S(2)}) collective-permute-start(bf16[384,256]{1,0:T(8,128)(2,1)S(1)} %get-tuple-element.106), channel_id=1, source_target_pairs={{0,1},{1,0},{2,3},{3,2},{4,5},{5,4},{6,7},{7,6},{8,9},{9,8},{10,11... | collective-permute-start | bytes 589832 | tf_op jit(solution)/shard_map/ppermute | solution.py:420
  49.6 12.1 %collective-permute-start.16 = (bf16[384,1024]{1,0:T(8,128)(2,1)S(1)}, bf16[384,1024]{1,0:T(8,128)(2,1)S(1)}, u32[]{:S(2)}, u32[]{:S(2)}) collective-permute-start(bf16[384,1024]{1,0:T(8,128)(2,1)S(1)} %shard_map.102), channel_id=1, source_target_pairs={{0,16},{4,12},{8,24},{12,4},{16,0},{20,28},{24,8},{28,20},{1,17},{... | collective-permute-start | bytes 2359304 | tf_op jit(solution)/shard_map/ppermute | solution.py:425

commit v12 on v11

--- a/solution.py
+++ b/solution.py
@@ -13,7 +13,7 @@
 WAIT_FLOPS = 20_000_000_000
 TEXT_PIECES = 3
 ACC_PIECES = 2
-LAST_PIECES = 1
+LAST_PIECES = 2
 CORES = 2
 EPS = 1e-06
 LOG2E = math.log2(math.e)
@@ -606,7 +606,6 @@
         second_sum_body,
         [f32(rows), bf16(rows)],
         [near_weights, units, image_add],
-        flops=0,
         limit=16,
     )
     image_last = []

time: 63.5 us -> 61.1 us (0.962)
  waiting for transfers between devices: 21.8 us -> 16.7 us
  starting transfers between devices: 21.7 us -> 24.4 us
    ppermute x11, waiting for transfers between devices: 10.8 us -> 6.17 us  [swap(): return lax.ppermute(value, axis, [(i, i ^ bits) for i in range(count)])]
    ppermute x6 -> x8, starting transfers between devices: 11.6 us -> 13.7 us  [swap_near(): lax.ppermute(value, 'blk', [(i, i ^ neighbour_bits(i)[which]) for i in ra...]
    ppermute x6 -> x8, waiting for transfers between devices: 11 us -> 10.6 us  [swap_near(): lax.ppermute(value, 'blk', [(i, i ^ neighbour_bits(i)[which]) for i in ra...]
    pallas_call x19 -> x20, Pallas kernels: 16.4 us -> 16.4 us  [call_kernel(): pl.pallas_call(body, out_shape=outs, in_specs=specs, out_specs=[ANY_SPEC...]
  transfers between devices with their start and end apart: 17 -> 19, of which waited for: 9 -> 8; matrix products, arithmetic and copies ran while one was open for 0% -> 0% of each run, Pallas kernels for 23% -> 24%
where the time goes in v12:
time: 61.1 us; the launch traced here: 60.9 us
  starting transfers between devices  24.4 us (40%)
  waiting for transfers between devices  16.7 us (27%)
  Pallas kernels  16.4 us (27%)
  between operations  2.15 us (4%)
  local copies, waits for them, and re-layouts  1.14 us (2%)
    pallas_call x20, Pallas kernels, call_kernel(): pl.pallas_call(body, out_shape=outs, in_specs=specs, out_specs=[ANY_SPEC...  16.4 us
    ppermute x8, starting transfers between devices, swap_near(): lax.ppermute(value, 'blk', [(i, i ^ neighbour_bits(i)[which]) for i in ra...  13.7 us
    ppermute x11, starting transfers between devices, swap(): return lax.ppermute(value, axis, [(i, i ^ bits) for i in range(count)])  10.7 us
    ppermute x8, waiting for transfers between devices, swap_near(): lax.ppermute(value, 'blk', [(i, i ^ neighbour_bits(i)[which]) for i in ra...  10.6 us
    ppermute x11, waiting for transfers between devices, swap(): return lax.ppermute(value, axis, [(i, i ^ bits) for i in range(count)])  6.17 us
  transfers between devices with their start and end apart: 19, of which 8 were waited for; matrix products, arithmetic and copies ran while one was open for 0% of the time, Pallas kernels for 24%

profile of v12, /device:TPU:0, one launch (start us, length us, event | category | flops | bytes accessed | tf_op | source)
XLA Modules:
  0.0 60.9 jit_solution(15524835749387206415)
XLA Ops:
  0.6 3.0 %collective-permute-start = (bf16[384,1024]{1,0:T(8,128)(2,1)}, bf16[384,1024]{1,0:T(8,128)(2,1)S(1)}, u32[]{:S(2)}, u32[]{:S(2)}) collective-permute-start(bf16[384,1024]{1,0:T(8,128)(2,1)} %raw_ref.1), channel_id=1, source_target_pairs={{0,16},{4,12},{8,24},{12,4},{16,0},{20,28},{24,8},{28,20},{1,17},{... | collective-permute-start | bytes 2359304 | tf_op jit(solution)/shard_map/ppermute | solution.py:425
  3.7 1.1 %copy-done = bf16[1536,256]{1,0:T(8,128)(2,1)S(1)} copy-done((bf16[1536,256]{1,0:T(8,128)(2,1)S(1)}, bf16[1536,256]{1,0:T(8,128)(2,1)}, u32[]{:S(2)}) %copy-start) | copy-done | bytes 786456
  4.8 0.1 shard_map.88
  4.9 3.7 %collective-permute-start.1 = (bf16[384,256]{1,0:T(8,128)(2,1)S(1)}, bf16[384,256]{1,0:T(8,128)(2,1)S(1)}, u32[]{:S(2)}, u32[]{:S(2)}) collective-permute-start(bf16[384,256]{1,0:T(8,128)(2,1)S(1)} %get-tuple-element.76), channel_id=1, source_target_pairs={{0,3},{1,2},{2,1},{3,0},{4,7},{5,6},{6,5},{7,4},{8,11},{9,10},{10,... | collective-permute-start | bytes 589832 | tf_op jit(solution)/shard_map/ppermute | solution.py:420
  8.5 0.0 collective-permute-start.2
  8.5 0.8 %collective-permute-start.3 = (bf16[384,256]{1,0:T(8,128)(2,1)S(1)}, bf16[384,256]{1,0:T(8,128)(2,1)S(1)}, u32[]{:S(2)}, u32[]{:S(2)}) collective-permute-start(bf16[384,256]{1,0:T(8,128)(2,1)S(1)} %get-tuple-element.78), channel_id=1, source_target_pairs={{0,1},{1,0},{2,3},{3,2},{4,5},{5,4},{6,7},{7,6},{8,9},{9,8},{10,11... | collective-permute-start | bytes 589832 | tf_op jit(solution)/shard_map/ppermute | solution.py:420
  9.3 1.4 %shard_map.86 = (bf16[384,1024]{1,0:T(8,128)(2,1)S(1)}, bf16[384,1024]{1,0:T(8,128)(2,1)S(1)}, f32[384,128]{1,0:T(8,128)S(1)}) custom-call(bf16[384,1024]{1,0:T(8,128)(2,1)} %raw_ref.1), custom_call_target="tpu_custom_call" | custom-call | bytes 2555904 | tf_op jit(solution)/shard_map/pallas_call | solution.py:46
  10.7 1.6 %collective-permute-start.4 = (bf16[384,1024]{1,0:T(8,128)(2,1)}, bf16[384,1024]{1,0:T(8,128)(2,1)S(1)}, u32[]{:S(2)}, u32[]{:S(2)}) collective-permute-start(bf16[384,1024]{1,0:T(8,128)(2,1)} %raw_ref.1), channel_id=1, source_target_pairs={{0,8},{4,20},{8,0},{12,28},{16,24},{20,4},{24,16},{28,12},{1,9},{5... | collective-permute-start | bytes 2359304 | tf_op jit(solution)/shard_map/ppermute | solution.py:425
  13.6 1.1 %shard_map.87 = (f32[2,128]{1,0:T(2,128)S(1)}, f32[72,128]{1,0:T(8,128)S(1)}, s32[12,128]{1,0:T(8,128)S(1)}, s32[768,128]{1,0:T(8,128)S(1)}, f32[384,128]{1,0:T(8,128)S(1)}, /*index=5*/f32[4,128]{1,0:T(4,128)S(1)}) custom-call(f32[1]{0:T(128)S(6)} %copy.9.refs_0_, f32[1]{0:T(128)S(6)} %copy.10.refs_1_, s32[3,8,96]{2,1,0:T(8,128)S(1)} %bitcast.5, ...), custom_call_target="tpu_custom_call" | custom-call | bytes 743432 | tf_op jit(solution)/shard_map/pallas_call | solution.py:46
  14.7 0.6 %collective-permute-done.raw_ref = bf16[384,1024]{1,0:T(8,128)(2,1)S(1)} collective-permute-done((bf16[384,1024]{1,0:T(8,128)(2,1)}, bf16[384,1024]{1,0:T(8,128)(2,1)S(1)}, u32[]{:S(2)}, u32[]{:S(2)}) %collective-permute-start) | collective-permute-done | bytes 786464 | tf_op jit(solution)/shard_map/ppermute | solution.py:425
  15.3 3.3 %collective-permute-start.8 = (bf16[384,1024]{1,0:T(8,128)(2,1)S(1)}, bf16[384,1024]{1,0:T(8,128)(2,1)S(1)}, u32[]{:S(2)}, u32[]{:S(2)}) collective-permute-start(bf16[384,1024]{1,0:T(8,128)(2,1)S(1)} %collective-permute-done.raw_ref), channel_id=1, source_target_pairs={{0,8},{4,20},{8,0},{12,28},{16,24},{20,4},{24,16},{28,12},{1,9},{5... | collective-permute-start | bytes 2359304 | tf_op jit(solution)/shard_map/ppermute | solution.py:425
  18.6 0.2 shard_map.89.second_unit_ref
  18.9 4.1 %collective-permute-done.4.first_ref = bf16[384,1024]{1,0:T(8,128)(2,1)S(1)} collective-permute-done((bf16[384,1024]{1,0:T(8,128)(2,1)}, bf16[384,1024]{1,0:T(8,128)(2,1)S(1)}, u32[]{:S(2)}, u32[]{:S(2)}) %collective-permute-start.4) | collective-permute-done | bytes 786464 | tf_op jit(solution)/shard_map/ppermute | solution.py:425
  23.0 0.3 shard_map.90.refs_8_.refs_7_
  23.3 0.0 collective-permute-done.3.refs_3_.refs_4_
  23.3 1.6 %collective-permute-done.2.refs_2_.refs_3_ = bf16[384,256]{1,0:T(8,128)(2,1)S(1)} collective-permute-done((bf16[384,256]{1,0:T(8,128)(2,1)S(1)}, bf16[384,256]{1,0:T(8,128)(2,1)S(1)}, u32[]{:S(2)}, u32[]{:S(2)}) %collective-permute-start.2) | collective-permute-done | bytes 196640 | tf_op jit(solution)/shard_map/ppermute | solution.py:420
  24.9 0.4 shard_map.91
  25.3 0.1 collective-permute-start.5
  25.4 0.5 collective-permute-start.6
  25.9 0.1 collective-permute-start.7
  26.0 1.6 %shard_map.92 = (bf16[384,384]{1,0:T(8,128)(2,1)S(1)}, bf16[384,768]{1,0:T(8,128)(2,1)S(1)}) custom-call(f32[2,128]{1,0:T(2,128)S(1)} %get-tuple-element.69.refs_0_, f32[72,128]{1,0:T(8,128)S(1)} %get-tuple-element.70.refs_1_, s32[12,128]{1,0:T(8,128)S(1)} %get-tuple-element.71.refs_2_, s32[768,128]{1,0:T(8,128)S(1)} %get-tuple-element.72.refs_3_, ...), custom_call_target="tpu_custom_call" | custom-call | bytes 4666368 | tf_op jit(solution)/shard_map/pallas_call | solution.py:46
  27.6 0.1 collective-permute-done.7.refs_11_
  27.7 1.3 %shard_map.93 = (bf16[768,1024]{1,0:T(8,128)(2,1)S(1)}, bf16[768,384]{1,0:T(8,128)(2,1)S(1)}, bf16[384,1024]{1,0:T(8,128)(2,1)S(1)}) custom-call(f32[2,128]{1,0:T(2,128)S(1)} %get-tuple-element.69.refs_0_, f32[72,128]{1,0:T(8,128)S(1)} %get-tuple-element.70.refs_1_, s32[12,128]{1,0:T(8,128)S(1)} %get-tuple-element.71.refs_2_, ...), custom_call_target="tpu_custom_call" | custom-call | bytes 7320576 | tf_op jit(solution)/shard_map/pallas_call | solution.py:46
  29.0 0.6 collective-permute-start.14
  29.6 2.3 %shard_map.94 = (bf16[768,384]{1,0:T(8,128)(2,1)S(1)}, f32[768,1024]{1,0:T(8,128)S(1)}, bf16[768,768]{1,0:T(8,128)(2,1)S(1)}) custom-call(f32[2,128]{1,0:T(2,128)S(1)} %get-tuple-element.69.refs_0_, f32[72,128]{1,0:T(8,128)S(1)} %get-tuple-element.70.refs_1_, s32[12,128]{1,0:T(8,128)S(1)} %get-tuple-element.71.refs_2_, ...), custom_call_target="tpu_custom_call" | custom-call | bytes 10957824 | tf_op jit(solution)/shard_map/pallas_call | solution.py:46
  31.9 0.0 collective-permute-done.8.refs_9_
  31.9 1.4 %shard_map.95 = (bf16[768,768]{1,0:T(8,128)(2,1)S(1)}, bf16[768,1024]{1,0:T(8,128)(2,1)S(1)}) custom-call(f32[2,128]{1,0:T(2,128)S(1)} %get-tuple-element.69.refs_0_, f32[72,128]{1,0:T(8,128)S(1)} %get-tuple-element.70.refs_1_, s32[12,128]{1,0:T(8,128)S(1)} %get-tuple-element.71.refs_2_, s32[768,128]{1,0:T(8,128)S(1)} %get-tuple-element.72.refs_3_, ...), custom_call_target="tpu_custom_call" | custom-call | bytes 7123968 | tf_op jit(solution)/shard_map/pallas_call | solution.py:46
  33.4 0.8 %shard_map.96 = (bf16[192,1024]{1,0:T(8,128)(2,1)S(1)}, bf16[192,1024]{1,0:T(8,128)(2,1)S(1)}) custom-call(bf16[768,768]{1,0:T(8,128)(2,1)S(1)} %get-tuple-element.97.weight_ref, bf16[768,1024]{1,0:T(8,128)(2,1)S(1)} %get-tuple-element.89.refs_6_.unit_ref), custom_call_target="tpu_custom_call" | custom-call | bytes 3538944 | tf_op jit(solution)/shard_map/pallas_call | solution.py:46
  34.2 0.8 %shard_map.97 = (bf16[192,1024]{1,0:T(8,128)(2,1)S(1)}, bf16[192,1024]{1,0:T(8,128)(2,1)S(1)}) custom-call(bf16[768,768]{1,0:T(8,128)(2,1)S(1)} %get-tuple-element.97.weight_ref, bf16[768,1024]{1,0:T(8,128)(2,1)S(1)} %get-tuple-element.103.image_ref, f32[768,1024]{1,0:T(8,128)S(1)} %get-tuple-element.101.acc_ref), custom_call_target="tpu_custom_call" | custom-call | bytes 6684672 | tf_op jit(solution)/shard_map/pallas_call | solution.py:46
  35.0 1.1 %collective-permute-start.9 = (bf16[192,1024]{1,0:T(8,128)(2,1)S(1)}, bf16[192,1024]{1,0:T(8,128)(2,1)S(1)}, u32[]{:S(2)}, u32[]{:S(2)}) collective-permute-start(bf16[192,1024]{1,0:T(8,128)(2,1)S(1)} %get-tuple-element.104), channel_id=1, source_target_pairs={{0,4},{4,0},{8,12},{12,8},{16,20},{20,16},{24,28},{28,24},{1,5},{5... | collective-permute-start | bytes 1179656 | tf_op jit(solution)/shard_map/ppermute | solution.py:420
  36.1 0.1 collective-permute-start.10
  36.1 0.9 %collective-permute-start.15 = (bf16[192,1024]{1,0:T(8,128)(2,1)S(1)}, bf16[192,1024]{1,0:T(8,128)(2,1)S(1)}, u32[]{:S(2)}, u32[]{:S(2)}) collective-permute-start(bf16[192,1024]{1,0:T(8,128)(2,1)S(1)} %get-tuple-element.117), channel_id=1, source_target_pairs={{0,8},{4,20},{8,0},{12,28},{16,24},{20,4},{24,16},{28,12},{1,9},{5... | collective-permute-start | bytes 1179656 | tf_op jit(solution)/shard_map/ppermute | solution.py:425
  37.0 1.2 %collective-permute-start.17 = (bf16[192,1024]{1,0:T(8,128)(2,1)S(1)}, bf16[192,1024]{1,0:T(8,128)(2,1)S(1)}, u32[]{:S(2)}, u32[]{:S(2)}) collective-permute-start(bf16[192,1024]{1,0:T(8,128)(2,1)S(1)} %get-tuple-element.119), channel_id=1, source_target_pairs={{0,8},{4,20},{8,0},{12,28},{16,24},{20,4},{24,16},{28,12},{1,9},{5... | collective-permute-start | bytes 1179656 | tf_op jit(solution)/shard_map/ppermute | solution.py:425
  38.2 0.8 %shard_map.98.refs_5_ = f32[384,1024]{1,0:T(8,128)S(1)} custom-call(bf16[768,768]{1,0:T(8,128)(2,1)S(1)} %get-tuple-element.97.weight_ref, bf16[768,1024]{1,0:T(8,128)(2,1)S(1)} %get-tuple-element.103.image_ref, f32[768,1024]{1,0:T(8,128)S(1)} %get-tuple-element.101.acc_ref), custom_call_target="tpu_custom_call" | custom-call | bytes 7471104 | tf_op jit(solution)/shard_map/pallas_call | solution.py:46
  39.0 0.6 %shard_map.99 = (bf16[384,256]{1,0:T(8,128)(2,1)S(1)}, bf16[384,256]{1,0:T(8,128)(2,1)S(1)}, bf16[384,256]{1,0:T(8,128)(2,1)S(1)}, bf16[384,256]{1,0:T(8,128)(2,1)S(1)}) custom-call(f32[384,128]{1,0:T(8,128)S(1)} %get-tuple-element.93.refs_0_, bf16[384,256]{1,0:T(8,128)(2,1)S(1)} %get-tuple-element.75.refs_0_.refs_1_, ...), custom_call_target="tpu_custom_call" | custom-call | bytes 4128768 | tf_op jit(solution)/shard_map/pallas_call | solution.py:46
  39.6 2.5 %collective-permute-start.11 = (bf16[384,256]{1,0:T(8,128)(2,1)S(1)}, bf16[384,256]{1,0:T(8,128)(2,1)S(1)}, u32[]{:S(2)}, u32[]{:S(2)}) collective-permute-start(bf16[384,256]{1,0:T(8,128)(2,1)S(1)} %get-tuple-element.108), channel_id=1, source_target_pairs={{0,3},{1,2},{2,1},{3,0},{4,7},{5,6},{6,5},{7,4},{8,11},{9,10},{10,... | collective-permute-start | bytes 589832 | tf_op jit(solution)/shard_map/ppermute | solution.py:420
  42.1 1.9 %collective-permute-start.13 = (bf16[384,256]{1,0:T(8,128)(2,1)S(1)}, bf16[384,256]{1,0:T(8,128)(2,1)S(1)}, u32[]{:S(2)}, u32[]{:S(2)}) collective-permute-start(bf16[384,256]{1,0:T(8,128)(2,1)S(1)} %get-tuple-element.110), channel_id=1, source_target_pairs={{0,1},{1,0},{2,3},{3,2},{4,5},{5,4},{6,7},{7,6},{8,9},{9,8},{10,11... | collective-permute-start | bytes 589832 | tf_op jit(solution)/shard_map/ppermute | solution.py:420
  44.1 0.8 %shard_map.100 = (f32[384,1024]{1,0:T(8,128)S(1)}, bf16[384,1024]{1,0:T(8,128)(2,1)S(1)}) custom-call(bf16[768,768]{1,0:T(8,128)(2,1)S(1)} %get-tuple-element.113.weight_ref, bf16[768,1024]{1,0:T(8,128)(2,1)S(1)} %get-tuple-element.89.refs_6_.unit_ref, bf16[384,1024]{1,0:T(8,128)(2,1)S(1)} %collective-permute-done.14.add_ref), custom_call_target="tpu_custom_call" | custom-call | bytes 5898240 | tf_op jit(solution)/shard_map/pallas_call | solution.py:46
  44.9 0.4 collective-permute-done.15.in_ref
  45.3 0.1 shard_map.102
  45.3 1.6 %collective-permute-start.16 = (bf16[192,1024]{1,0:T(8,128)(2,1)S(1)}, bf16[192,1024]{1,0:T(8,128)(2,1)S(1)}, u32[]{:S(2)}, u32[]{:S(2)}) collective-permute-start(bf16[192,1024]{1,0:T(8,128)(2,1)S(1)} %shard_map.102), channel_id=1, source_target_pairs={{0,16},{4,12},{8,24},{12,4},{16,0},{20,28},{24,8},{28,20},{1,17},{... | collective-permute-start | bytes 1179656 | tf_op jit(solution)/shard_map/ppermute | solution.py:425
  46.9 4.5 %collective-permute-done.17.in_ref = bf16[192,1024]{1,0:T(8,128)(2,1)S(1)} collective-permute-done((bf16[192,1024]{1,0:T(8,128)(2,1)S(1)}, bf16[192,1024]{1,0:T(8,128)(2,1)S(1)}, u32[]{:S(2)}, u32[]{:S(2)}) %collective-permute-start.17) | collective-permute-done | bytes 393248 | tf_op jit(solution)/shard_map/ppermute | solution.py:425
  51.4 0.1 shard_map.103
  51.5 1.6 %collective-permute-start.18 = (bf16[192,1024]{1,0:T(8,128)(2,1)S(1)}, bf16[192,1024]{1,0:T(8,128)(2,1)S(1)}, u32[]{:S(2)}, u32[]{:S(2)}) collective-permute-start(bf16[192,1024]{1,0:T(8,128)(2,1)S(1)} %shard_map.103), channel_id=1, source_target_pairs={{0,16},{4,12},{8,24},{12,4},{16,0},{20,28},{24,8},{28,20},{1,17},{... | collective-permute-start | bytes 1179656 | tf_op jit(solution)/shard_map/ppermute | solution.py:425
  53.1 0.8 %shard_map.101.refs_6_ = f32[384,1024]{1,0:T(8,128)S(1)} custom-call(bf16[768,384]{1,0:T(8,128)(2,1)S(1)} %get-tuple-element.95.refs_8_.weight_ref, bf16[768,1024]{1,0:T(8,128)(2,1)S(1)} %get-tuple-element.89.refs_6_.unit_ref, bf16[384,1024]{1,0:T(8,128)(2,1)S(1)} %get-tuple-element.115.add_ref), custom_call_target="tpu_custom_call" | custom-call | tf_op jit(solution)/shard_map/pallas_call | solution.py:46
  53.9 4.5 %collective-permute-done.12.refs_1_.refs_2_ = bf16[384,256]{1,0:T(8,128)(2,1)S(1)} collective-permute-done((bf16[384,256]{1,0:T(8,128)(2,1)S(1)}, bf16[384,256]{1,0:T(8,128)(2,1)S(1)}, u32[]{:S(2)}, u32[]{:S(2)}) %collective-permute-start.12) | collective-permute-done | bytes 196640 | tf_op jit(solution)/shard_map/ppermute | solution.py:420
  58.3 1.0 %collective-permute-done.18.refs_8_ = bf16[192,1024]{1,0:T(8,128)(2,1)S(1)} collective-permute-done((bf16[192,1024]{1,0:T(8,128)(2,1)S(1)}, bf16[192,1024]{1,0:T(8,128)(2,1)S(1)}, u32[]{:S(2)}, u32[]{:S(2)}) %collective-permute-start.18) | collective-permute-done | bytes 393248 | tf_op jit(solution)/shard_map/ppermute | solution.py:425
  59.3 1.6 %shard_map.105 = (bf16[1536,256]{1,0:T(8,128)(2,1)}, bf16[384,1024]{1,0:T(8,128)(2,1)}) custom-call(bf16[384,256]{1,0:T(8,128)(2,1)S(1)} %get-tuple-element.107.refs_0_, bf16[384,256]{1,0:T(8,128)(2,1)S(1)} %collective-permute-done.11.refs_0_.refs_1_, bf16[384,256]{1,0:T(8,128)(2,1)S(1)} %collective-permute-done.12.refs_1_.refs_2_, ...), custom_call_target="tpu_custom_call" | custom-call | bytes 5705728 | tf_op jit(solution)/shard_map/pallas_call | solution.py:46
  (18 shorter events, 0.0 us)
Async XLA Ops:
  0.6 14.7 %collective-permute-start = (bf16[384,1024]{1,0:T(8,128)(2,1)}, bf16[384,1024]{1,0:T(8,128)(2,1)S(1)}, u32[]{:S(2)}, u32[]{:S(2)}) collective-permute-start(bf16[384,1024]{1,0:T(8,128)(2,1)} %raw_ref.1), channel_id=1, source_target_pairs={{0,16},{4,12},{8,24},{12,4},{16,0},{20,28},{24,8},{28,20},{1,17},{... | collective-permute-start | bytes 2359304 | tf_op jit(solution)/shard_map/ppermute | solution.py:425
  3.7 1.1 %copy-start = (bf16[1536,256]{1,0:T(8,128)(2,1)S(1)}, bf16[1536,256]{1,0:T(8,128)(2,1)}, u32[]{:S(2)}) copy-start(bf16[1536,256]{1,0:T(8,128)(2,1)} %text_ref.1) | copy-start | bytes 2359300
  4.8 8.8 %copy-start.1 = (s32[12288]{0:T(1024)S(1)}, s32[12288]{0:T(1024)}, u32[]{:S(2)}) copy-start(s32[12288]{0:T(1024)} %param.11) | copy-start | bytes 147460
  4.8 8.8 %copy-start.2 = (s32[12288]{0:T(1024)S(1)}, s32[12288]{0:T(1024)}, u32[]{:S(2)}) copy-start(s32[12288]{0:T(1024)} %param.12) | copy-start | bytes 147460
  4.8 8.8 %copy-start.3 = (s32[96,8,3]{0,1,2:T(8,128)S(1)}, s32[96,8,3]{0,1,2:T(8,128)}, u32[]{:S(2)}) copy-start(s32[96,8,3]{0,1,2:T(8,128)} %param.13) | copy-start | bytes 27652
  4.9 18.5 %collective-permute-start.1 = (bf16[384,256]{1,0:T(8,128)(2,1)S(1)}, bf16[384,256]{1,0:T(8,128)(2,1)S(1)}, u32[]{:S(2)}, u32[]{:S(2)}) collective-permute-start(bf16[384,256]{1,0:T(8,128)(2,1)S(1)} %get-tuple-element.76), channel_id=1, source_target_pairs={{0,3},{1,2},{2,1},{3,0},{4,7},{5,6},{6,5},{7,4},{8,11},{9,10},{10,... | collective-permute-start | bytes 589832 | tf_op jit(solution)/shard_map/ppermute | solution.py:420
  8.5 16.4 %collective-permute-start.2 = (bf16[384,256]{1,0:T(8,128)(2,1)S(1)}, bf16[384,256]{1,0:T(8,128)(2,1)S(1)}, u32[]{:S(2)}, u32[]{:S(2)}) collective-permute-start(bf16[384,256]{1,0:T(8,128)(2,1)S(1)} %get-tuple-element.77), channel_id=1, source_target_pairs={{0,2},{1,3},{2,0},{3,1},{4,6},{5,7},{6,4},{7,5},{8,10},{9,11},{10,... | collective-permute-start | bytes 589832 | tf_op jit(solution)/shard_map/ppermute | solution.py:420
  8.5 14.8 %collective-permute-start.3 = (bf16[384,256]{1,0:T(8,128)(2,1)S(1)}, bf16[384,256]{1,0:T(8,128)(2,1)S(1)}, u32[]{:S(2)}, u32[]{:S(2)}) collective-permute-start(bf16[384,256]{1,0:T(8,128)(2,1)S(1)} %get-tuple-element.78), channel_id=1, source_target_pairs={{0,1},{1,0},{2,3},{3,2},{4,5},{5,4},{6,7},{7,6},{8,9},{9,8},{10,11... | collective-permute-start | bytes 589832 | tf_op jit(solution)/shard_map/ppermute | solution.py:420
  10.7 12.3 %collective-permute-start.4 = (bf16[384,1024]{1,0:T(8,128)(2,1)}, bf16[384,1024]{1,0:T(8,128)(2,1)S(1)}, u32[]{:S(2)}, u32[]{:S(2)}) collective-permute-start(bf16[384,1024]{1,0:T(8,128)(2,1)} %raw_ref.1), channel_id=1, source_target_pairs={{0,8},{4,20},{8,0},{12,28},{16,24},{20,4},{24,16},{28,12},{1,9},{5... | collective-permute-start | bytes 2359304 | tf_op jit(solution)/shard_map/ppermute | solution.py:425
  15.3 16.6 %collective-permute-start.8 = (bf16[384,1024]{1,0:T(8,128)(2,1)S(1)}, bf16[384,1024]{1,0:T(8,128)(2,1)S(1)}, u32[]{:S(2)}, u32[]{:S(2)}) collective-permute-start(bf16[384,1024]{1,0:T(8,128)(2,1)S(1)} %collective-permute-done.raw_ref), channel_id=1, source_target_pairs={{0,8},{4,20},{8,0},{12,28},{16,24},{20,4},{24,16},{28,12},{1,9},{5... | collective-permute-start | bytes 2359304 | tf_op jit(solution)/shard_map/ppermute | solution.py:425
  25.3 2.2 %collective-permute-start.5 = (bf16[128,1024]{1,0:T(8,128)(2,1)S(1)}, bf16[128,1024]{1,0:T(8,128)(2,1)S(1)}, u32[]{:S(2)}, u32[]{:S(2)}) collective-permute-start(bf16[128,1024]{1,0:T(8,128)(2,1)S(1)} %get-tuple-element.86), channel_id=1, source_target_pairs={{0,4},{4,0},{8,12},{12,8},{16,20},{20,16},{24,28},{28,24},{1,5},{5... | collective-permute-start | bytes 786440 | tf_op jit(solution)/shard_map/ppermute | solution.py:420
  25.4 2.2 %collective-permute-start.6 = (bf16[128,1024]{1,0:T(8,128)(2,1)S(1)}, bf16[128,1024]{1,0:T(8,128)(2,1)S(1)}, u32[]{:S(2)}, u32[]{:S(2)}) collective-permute-start(bf16[128,1024]{1,0:T(8,128)(2,1)S(1)} %get-tuple-element.87), channel_id=1, source_target_pairs={{0,4},{4,0},{8,12},{12,8},{16,20},{20,16},{24,28},{28,24},{1,5},{5... | collective-permute-start | bytes 786440 | tf_op jit(solution)/shard_map/ppermute | solution.py:420
  25.9 1.8 %collective-permute-start.7 = (bf16[128,1024]{1,0:T(8,128)(2,1)S(1)}, bf16[128,1024]{1,0:T(8,128)(2,1)S(1)}, u32[]{:S(2)}, u32[]{:S(2)}) collective-permute-start(bf16[128,1024]{1,0:T(8,128)(2,1)S(1)} %get-tuple-element.88), channel_id=1, source_target_pairs={{0,4},{4,0},{8,12},{12,8},{16,20},{20,16},{24,28},{28,24},{1,5},{5... | collective-permute-start | bytes 786440 | tf_op jit(solution)/shard_map/ppermute | solution.py:420
  29.0 13.1 %collective-permute-start.14 = (bf16[384,1024]{1,0:T(8,128)(2,1)S(1)}, bf16[384,1024]{1,0:T(8,128)(2,1)S(1)}, u32[]{:S(2)}, u32[]{:S(2)}) collective-permute-start(bf16[384,1024]{1,0:T(8,128)(2,1)S(1)} %get-tuple-element.114), channel_id=1, source_target_pairs={{0,8},{4,20},{8,0},{12,28},{16,24},{20,4},{24,16},{28,12},{1,9},{5... | collective-permute-start | bytes 2359304 | tf_op jit(solution)/shard_map/ppermute | solution.py:425
  35.0 4.0 %collective-permute-start.9 = (bf16[192,1024]{1,0:T(8,128)(2,1)S(1)}, bf16[192,1024]{1,0:T(8,128)(2,1)S(1)}, u32[]{:S(2)}, u32[]{:S(2)}) collective-permute-start(bf16[192,1024]{1,0:T(8,128)(2,1)S(1)} %get-tuple-element.104), channel_id=1, source_target_pairs={{0,4},{4,0},{8,12},{12,8},{16,20},{20,16},{24,28},{28,24},{1,5},{5... | collective-permute-start | bytes 1179656 | tf_op jit(solution)/shard_map/ppermute | solution.py:420
  36.1 2.9 %collective-permute-start.10 = (bf16[192,1024]{1,0:T(8,128)(2,1)S(1)}, bf16[192,1024]{1,0:T(8,128)(2,1)S(1)}, u32[]{:S(2)}, u32[]{:S(2)}) collective-permute-start(bf16[192,1024]{1,0:T(8,128)(2,1)S(1)} %get-tuple-element.105), channel_id=1, source_target_pairs={{0,4},{4,0},{8,12},{12,8},{16,20},{20,16},{24,28},{28,24},{1,5},{5... | collective-permute-start | bytes 1179656 | tf_op jit(solution)/shard_map/ppermute | solution.py:420
  36.1 9.1 %collective-permute-start.15 = (bf16[192,1024]{1,0:T(8,128)(2,1)S(1)}, bf16[192,1024]{1,0:T(8,128)(2,1)S(1)}, u32[]{:S(2)}, u32[]{:S(2)}) collective-permute-start(bf16[192,1024]{1,0:T(8,128)(2,1)S(1)} %get-tuple-element.117), channel_id=1, source_target_pairs={{0,8},{4,20},{8,0},{12,28},{16,24},{20,4},{24,16},{28,12},{1,9},{5... | collective-permute-start | bytes 1179656 | tf_op jit(solution)/shard_map/ppermute | solution.py:425
  37.0 14.4 %collective-permute-start.17 = (bf16[192,1024]{1,0:T(8,128)(2,1)S(1)}, bf16[192,1024]{1,0:T(8,128)(2,1)S(1)}, u32[]{:S(2)}, u32[]{:S(2)}) collective-permute-start(bf16[192,1024]{1,0:T(8,128)(2,1)S(1)} %get-tuple-element.119), channel_id=1, source_target_pairs={{0,8},{4,20},{8,0},{12,28},{16,24},{20,4},{24,16},{28,12},{1,9},{5... | collective-permute-start | bytes 1179656 | tf_op jit(solution)/shard_map/ppermute | solution.py:425
  39.6 14.3 %collective-permute-start.11 = (bf16[384,256]{1,0:T(8,128)(2,1)S(1)}, bf16[384,256]{1,0:T(8,128)(2,1)S(1)}, u32[]{:S(2)}, u32[]{:S(2)}) collective-permute-start(bf16[384,256]{1,0:T(8,128)(2,1)S(1)} %get-tuple-element.108), channel_id=1, source_target_pairs={{0,3},{1,2},{2,1},{3,0},{4,7},{5,6},{6,5},{7,4},{8,11},{9,10},{10,... | collective-permute-start | bytes 589832 | tf_op jit(solution)/shard_map/ppermute | solution.py:420
  42.1 16.2 %collective-permute-start.12 = (bf16[384,256]{1,0:T(8,128)(2,1)S(1)}, bf16[384,256]{1,0:T(8,128)(2,1)S(1)}, u32[]{:S(2)}, u32[]{:S(2)}) collective-permute-start(bf16[384,256]{1,0:T(8,128)(2,1)S(1)} %get-tuple-element.109), channel_id=1, source_target_pairs={{0,2},{1,3},{2,0},{3,1},{4,6},{5,7},{6,4},{7,5},{8,10},{9,11},{10,... | collective-permute-start | bytes 589832 | tf_op jit(solution)/shard_map/ppermute | solution.py:420
  42.1 16.2 %collective-permute-start.13 = (bf16[384,256]{1,0:T(8,128)(2,1)S(1)}, bf16[384,256]{1,0:T(8,128)(2,1)S(1)}, u32[]{:S(2)}, u32[]{:S(2)}) collective-permute-start(bf16[384,256]{1,0:T(8,128)(2,1)S(1)} %get-tuple-element.110), channel_id=1, source_target_pairs={{0,1},{1,0},{2,3},{3,2},{4,5},{5,4},{6,7},{7,6},{8,9},{9,8},{10,11... | collective-permute-start | bytes 589832 | tf_op jit(solution)/shard_map/ppermute | solution.py:420
  45.3 14.0 %collective-permute-start.16 = (bf16[192,1024]{1,0:T(8,128)(2,1)S(1)}, bf16[192,1024]{1,0:T(8,128)(2,1)S(1)}, u32[]{:S(2)}, u32[]{:S(2)}) collective-permute-start(bf16[192,1024]{1,0:T(8,128)(2,1)S(1)} %shard_map.102), channel_id=1, source_target_pairs={{0,16},{4,12},{8,24},{12,4},{16,0},{20,28},{24,8},{28,20},{1,17},{... | collective-permute-start | bytes 1179656 | tf_op jit(solution)/shard_map/ppermute | solution.py:425
  51.5 7.8 %collective-permute-start.18 = (bf16[192,1024]{1,0:T(8,128)(2,1)S(1)}, bf16[192,1024]{1,0:T(8,128)(2,1)S(1)}, u32[]{:S(2)}, u32[]{:S(2)}) collective-permute-start(bf16[192,1024]{1,0:T(8,128)(2,1)S(1)} %shard_map.103), channel_id=1, source_target_pairs={{0,16},{4,12},{8,24},{12,4},{16,0},{20,28},{24,8},{28,20},{1,17},{... | collective-permute-start | bytes 1179656 | tf_op jit(solution)/shard_map/ppermute | solution.py:425

commit v13 on v12

--- a/solution.py
+++ b/solution.py
@@ -13,7 +13,6 @@
 WAIT_FLOPS = 20_000_000_000
 TEXT_PIECES = 3
 ACC_PIECES = 2
-LAST_PIECES = 2
 CORES = 2
 EPS = 1e-06
 LOG2E = math.log2(math.e)
@@ -34,6 +33,7 @@
     scratch=(),
     flops=0,
     moved=None,
+    aliases=None,
     limit=24,
 ):
     if moved is None:
@@ -49,6 +49,7 @@
             in_specs=specs,
             out_specs=[ANY_SPEC if outs_anywhere else VMEM_SPEC] * len(outs),
             scratch_shapes=list(scratch),
+            input_output_aliases=aliases or {},
             compiler_params=pltpu.CompilerParams(vmem_limit_bytes=limit * MIB),
             cost_estimate=pl.CostEstimate(flops=flops, bytes_accessed=moved, transcendentals=0),
         )(*operands)
@@ -285,9 +286,10 @@
 def far_sum_body(weight_ref, unit_ref, *out_refs):
     rows = weight_ref.shape[1] // 2
     total = dot_tn(weight_ref[:, rows:], unit_ref[...]).astype(jnp.bfloat16)
-    size = rows // len(out_refs)
-    for at, ref in enumerate(out_refs):
-        ref[...] = total[at * size : (at + 1) * size, :]
+    start = 0
+    for ref in out_refs:
+        ref[...] = total[start : start + ref.shape[0], :]
+        start += ref.shape[0]
 
 
 def text_sum_body(half, weight_ref, image_ref, acc_ref, *out_refs):
@@ -343,9 +345,8 @@
         spread_ref[columns, :] = total.astype(jnp.bfloat16)
 
 
-def relay_body(at, sum_ref, in_ref, out_ref):
-    size = in_ref.shape[0]
-    part = sum_ref[pl.ds(at * size, size), :]
+def relay_body(start, sum_ref, in_ref, out_ref):
+    part = sum_ref[pl.ds(start, in_ref.shape[0]), :]
     out_ref[...] = (part + in_ref[...].astype(jnp.float32)).astype(jnp.bfloat16)
 
 
@@ -375,9 +376,28 @@
     out_ref[...] = sum(ref[: out_ref.shape[0], : out_ref.shape[1]] for ref in refs[:-1])
 
 
-def finish_body(chunks, adds, *refs):
+def finish_rows(start, count, raw_ref, scale_ref, sum_ref, add_ref, grad_ref, out_ref, sems, copies):
+    step = TILE // 2
+    for first in range(0, count, step):
+        part = pl.ds(start + first, step)
+        raw = raw_ref[part, :].astype(jnp.float32)
+        scales = scale_ref[part, :1]
+        acc = sum_ref[part, :]
+        if add_ref is not None:
+            acc = acc + add_ref[pl.ds(first, step), :].astype(jnp.float32)
+        inner = jnp.sum(raw * acc, axis=-1, keepdims=True) * scales * scales
+        grad_ref[part, :] = (scales * (acc - raw * inner)).astype(jnp.bfloat16)
+        copies.append(
+            pltpu.make_async_copy(
+                grad_ref.at[part, :], out_ref.at[part, :], sems.at[len(copies)]
+            )
+        )
+        copies[-1].start()
+
+
+def finish_body(chunks, count, *refs):
     part_refs, (raw_ref, scale_ref, sum_ref) = refs[:chunks], refs[chunks : chunks + 3]
-    piece_refs = refs[chunks + 3 : chunks + 3 + adds]
+    add_ref = refs[chunks + 3] if len(refs) == chunks + 9 else None
     text_ref, image_ref, grad_ref, sems = refs[-4:]
     place = lax.axis_index("tp")
     rows = part_refs[0].shape[0]
@@ -394,23 +414,19 @@
                 )
             )
             copies[-1].start()
-    for first in range(0, rows, TILE // 2):
-        part = pl.ds(first, TILE // 2)
-        raw = raw_ref[part, :].astype(jnp.float32)
-        scales = scale_ref[part, :1]
-        acc = sum_ref[part, :]
-        if piece_refs:
-            size = piece_refs[0].shape[0]
-            piece = piece_refs[first // size][pl.ds(first % size, TILE // 2), :]
-            acc = acc + piece.astype(jnp.float32)
-        inner = jnp.sum(raw * acc, axis=-1, keepdims=True) * scales * scales
-        grad_ref[part, :] = (scales * (acc - raw * inner)).astype(jnp.bfloat16)
-        copies.append(
-            pltpu.make_async_copy(
-                grad_ref.at[part, :], image_ref.at[part, :], sems.at[len(copies)]
-            )
-        )
-        copies[-1].start()
+    finish_rows(
+        0, count, raw_ref, scale_ref, sum_ref, add_ref, grad_ref, image_ref, sems, copies
+    )
+    for copy in copies:
+        copy.wait()
+
+
+def finish_last_body(start, raw_ref, scale_ref, sum_ref, add_ref, _, image_ref, grad_ref, sems):
+    copies = []
+    count = add_ref.shape[0]
+    finish_rows(
+        start, count, raw_ref, scale_ref, sum_ref, add_ref, grad_ref, image_ref, sems, copies
+    )
     for copy in copies:
         copy.wait()
 
@@ -523,19 +539,33 @@
             flops=WAIT_FLOPS,
             limit=8,
         )
-        return tuple(
-            call_kernel(
-                functools.partial(finish_body, groups, len(pieces)),
-                [bf16(groups * rows, width), bf16(rows)],
-                text_parts + [image_raw, image_scales, total] + pieces + arrived,
+        head = pieces[0].shape[0] if pieces else rows
+        text_grad, image_grad = call_kernel(
+            functools.partial(finish_body, groups, head),
+            [bf16(groups * rows, width), bf16(rows)],
+            text_parts + [image_raw, image_scales, total] + pieces[:1] + arrived,
+            outs_anywhere=True,
+            scratch=[
+                pltpu.VMEM((rows, embed), jnp.bfloat16),
+                pltpu.SemaphoreType.DMA(((groups + 2) * tiles,)),
+            ],
+            limit=8,
+        )
+        if pieces:
+            image_grad = call_kernel(
+                functools.partial(finish_last_body, head),
+                [bf16(rows)],
+                [image_raw, image_scales, total, pieces[1], image_grad],
+                anywhere=(4,),
                 outs_anywhere=True,
+                aliases={4: 0},
                 scratch=[
                     pltpu.VMEM((rows, embed), jnp.bfloat16),
-                    pltpu.SemaphoreType.DMA(((groups + 2) * tiles,)),
+                    pltpu.SemaphoreType.DMA((2 * tiles,)),
                 ],
                 limit=8,
-            )
-        )
+            )[0]
+        return (text_grad, image_grad)
 
     if not square:
         columns = gathered.shape[0]
@@ -583,8 +613,9 @@
         lists + [units, own_images, own_weights, from_far],
         limit=16,
     )
+    sizes = [rows - TILE, TILE]
     far_sum = call_kernel(
-        far_sum_body, [bf16(rows // LAST_PIECES)] * LAST_PIECES, [far_weights, units], limit=16
+        far_sum_body, [bf16(size) for size in sizes], [far_weights, units], limit=16
     )
     far_images, far_sum[0] = lax.optimization_barrier((far_images, far_sum[0]))
     acc_other = call_kernel(
@@ -610,12 +641,9 @@
     )
     image_last = []
     far_in = [swap_near(piece, 0) for piece in far_sum]
-    for at, piece in enumerate(far_in):
+    for size, start, piece in zip(sizes, (0, sizes[0]), far_in):
         relayed = call_kernel(
-            functools.partial(relay_body, at),
-            [bf16(rows // LAST_PIECES)],
-            [second_sum, piece],
-            limit=8,
+            functools.partial(relay_body, start), [bf16(size)], [second_sum, piece], limit=8
         )[0]
         image_last.append(swap_near(relayed, 1))
         second_sum, relayed = lax.optimization_barrier((second_sum, relayed))

time: 61.1 us -> 61 us (level)
  Pallas kernels: 16.4 us -> 17.3 us
  waiting for transfers between devices: 16.7 us -> 15.8 us
    ppermute x8, waiting for transfers between devices: 10.6 us -> 7.36 us  [swap_near(): lax.ppermute(value, 'blk', [(i, i ^ neighbour_bits(i)[which]) for i in ra...]
    ppermute x11, waiting for transfers between devices: 6.17 us -> 8.42 us  [swap(): return lax.ppermute(value, axis, [(i, i ^ bits) for i in range(count)])]
    pallas_call x20 -> x21, Pallas kernels: 16.4 us -> 17.3 us  [call_kernel(): pl.pallas_call(body, out_shape=outs, in_specs=specs, out_specs=[ANY_SPEC...]
  transfers between devices with their start and end apart: 19 -> 19, of which waited for: 8 -> 7; matrix products, arithmetic and copies ran while one was open for 0% -> 0% of each run, Pallas kernels for 24% -> 27%
where the time goes in v13:
time: 61 us; the launch traced here: 60.8 us
  starting transfers between devices  24.4 us (40%)
  Pallas kernels  17.3 us (28%)
  waiting for transfers between devices  15.8 us (26%)
  between operations  2.16 us (4%)
  local copies, waits for them, and re-layouts  1.14 us (2%)
    pallas_call x21, Pallas kernels, call_kernel(): pl.pallas_call(body, out_shape=outs, in_specs=specs, out_specs=[ANY_SPEC...  17.3 us
    ppermute x8, starting transfers between devices, swap_near(): lax.ppermute(value, 'blk', [(i, i ^ neighbour_bits(i)[which]) for i in ra...  13.7 us
    ppermute x11, starting transfers between devices, swap(): return lax.ppermute(value, axis, [(i, i ^ bits) for i in range(count)])  10.7 us
    ppermute x11, waiting for transfers between devices, swap(): return lax.ppermute(value, axis, [(i, i ^ bits) for i in range(count)])  8.42 us
    ppermute x8, waiting for transfers between devices, swap_near(): lax.ppermute(value, 'blk', [(i, i ^ neighbour_bits(i)[which]) for i in ra...  7.36 us
  transfers between devices with their start and end apart: 19, of which 7 were waited for; matrix products, arithmetic and copies ran while one was open for 0% of the time, Pallas kernels for 27%

profile of v13, /device:TPU:0, one launch (start us, length us, event | category | flops | bytes accessed | tf_op | source)
XLA Modules:
  0.0 60.8 jit_solution(6336874062586393080)
XLA Ops:
  0.6 3.0 %collective-permute-start = (bf16[384,1024]{1,0:T(8,128)(2,1)}, bf16[384,1024]{1,0:T(8,128)(2,1)S(1)}, u32[]{:S(2)}, u32[]{:S(2)}) collective-permute-start(bf16[384,1024]{1,0:T(8,128)(2,1)} %raw_ref.1), channel_id=1, source_target_pairs={{0,16},{4,12},{8,24},{12,4},{16,0},{20,28},{24,8},{28,20},{1,17},{... | collective-permute-start | bytes 2359304 | tf_op jit(solution)/shard_map/ppermute | solution.py:441
  3.7 1.1 %copy-done = bf16[1536,256]{1,0:T(8,128)(2,1)S(1)} copy-done((bf16[1536,256]{1,0:T(8,128)(2,1)S(1)}, bf16[1536,256]{1,0:T(8,128)(2,1)}, u32[]{:S(2)}) %copy-start) | copy-done | bytes 786456
  4.8 0.1 shard_map.88
  4.9 3.7 %collective-permute-start.1 = (bf16[384,256]{1,0:T(8,128)(2,1)S(1)}, bf16[384,256]{1,0:T(8,128)(2,1)S(1)}, u32[]{:S(2)}, u32[]{:S(2)}) collective-permute-start(bf16[384,256]{1,0:T(8,128)(2,1)S(1)} %get-tuple-element.78), channel_id=1, source_target_pairs={{0,3},{1,2},{2,1},{3,0},{4,7},{5,6},{6,5},{7,4},{8,11},{9,10},{10,... | collective-permute-start | bytes 589832 | tf_op jit(solution)/shard_map/ppermute | solution.py:436
  8.5 0.8 %collective-permute-start.3 = (bf16[384,256]{1,0:T(8,128)(2,1)S(1)}, bf16[384,256]{1,0:T(8,128)(2,1)S(1)}, u32[]{:S(2)}, u32[]{:S(2)}) collective-permute-start(bf16[384,256]{1,0:T(8,128)(2,1)S(1)} %get-tuple-element.80), channel_id=1, source_target_pairs={{0,1},{1,0},{2,3},{3,2},{4,5},{5,4},{6,7},{7,6},{8,9},{9,8},{10,11... | collective-permute-start | bytes 589832 | tf_op jit(solution)/shard_map/ppermute | solution.py:436
  9.3 1.4 %shard_map.86 = (bf16[384,1024]{1,0:T(8,128)(2,1)S(1)}, bf16[384,1024]{1,0:T(8,128)(2,1)S(1)}, f32[384,128]{1,0:T(8,128)S(1)}) custom-call(bf16[384,1024]{1,0:T(8,128)(2,1)} %raw_ref.1), custom_call_target="tpu_custom_call" | custom-call | bytes 2555904 | tf_op jit(solution)/shard_map/pallas_call | solution.py:46
  10.7 1.6 %collective-permute-start.4 = (bf16[384,1024]{1,0:T(8,128)(2,1)}, bf16[384,1024]{1,0:T(8,128)(2,1)S(1)}, u32[]{:S(2)}, u32[]{:S(2)}) collective-permute-start(bf16[384,1024]{1,0:T(8,128)(2,1)} %raw_ref.1), channel_id=1, source_target_pairs={{0,8},{4,20},{8,0},{12,28},{16,24},{20,4},{24,16},{28,12},{1,9},{5... | collective-permute-start | bytes 2359304 | tf_op jit(solution)/shard_map/ppermute | solution.py:441
  13.6 1.1 %shard_map.87 = (f32[2,128]{1,0:T(2,128)S(1)}, f32[72,128]{1,0:T(8,128)S(1)}, s32[12,128]{1,0:T(8,128)S(1)}, s32[768,128]{1,0:T(8,128)S(1)}, f32[384,128]{1,0:T(8,128)S(1)}, /*index=5*/f32[4,128]{1,0:T(4,128)S(1)}) custom-call(f32[1]{0:T(128)S(6)} %copy.11.refs_0_, f32[1]{0:T(128)S(6)} %copy.12.refs_1_, s32[3,8,96]{2,1,0:T(8,128)S(1)} %bitcast.5, ...), custom_call_target="tpu_custom_call" | custom-call | bytes 743432 | tf_op jit(solution)/shard_map/pallas_call | solution.py:46
  14.7 0.6 %collective-permute-done.raw_ref = bf16[384,1024]{1,0:T(8,128)(2,1)S(1)} collective-permute-done((bf16[384,1024]{1,0:T(8,128)(2,1)}, bf16[384,1024]{1,0:T(8,128)(2,1)S(1)}, u32[]{:S(2)}, u32[]{:S(2)}) %collective-permute-start) | collective-permute-done | bytes 786464 | tf_op jit(solution)/shard_map/ppermute | solution.py:441
  15.3 3.3 %collective-permute-start.8 = (bf16[384,1024]{1,0:T(8,128)(2,1)S(1)}, bf16[384,1024]{1,0:T(8,128)(2,1)S(1)}, u32[]{:S(2)}, u32[]{:S(2)}) collective-permute-start(bf16[384,1024]{1,0:T(8,128)(2,1)S(1)} %collective-permute-done.raw_ref), channel_id=1, source_target_pairs={{0,8},{4,20},{8,0},{12,28},{16,24},{20,4},{24,16},{28,12},{1,9},{5... | collective-permute-start | bytes 2359304 | tf_op jit(solution)/shard_map/ppermute | solution.py:441
  18.6 0.2 shard_map.89.second_unit_ref
  18.9 4.1 %collective-permute-done.4.first_ref = bf16[384,1024]{1,0:T(8,128)(2,1)S(1)} collective-permute-done((bf16[384,1024]{1,0:T(8,128)(2,1)}, bf16[384,1024]{1,0:T(8,128)(2,1)S(1)}, u32[]{:S(2)}, u32[]{:S(2)}) %collective-permute-start.4) | collective-permute-done | bytes 786464 | tf_op jit(solution)/shard_map/ppermute | solution.py:441
  23.0 0.3 shard_map.90.refs_8_.refs_7_
  23.3 1.6 %collective-permute-done.2.refs_2_.refs_3_ = bf16[384,256]{1,0:T(8,128)(2,1)S(1)} collective-permute-done((bf16[384,256]{1,0:T(8,128)(2,1)S(1)}, bf16[384,256]{1,0:T(8,128)(2,1)S(1)}, u32[]{:S(2)}, u32[]{:S(2)}) %collective-permute-start.2) | collective-permute-done | bytes 196640 | tf_op jit(solution)/shard_map/ppermute | solution.py:436
  24.9 0.4 shard_map.91
  25.3 0.1 collective-permute-start.5
  25.4 0.5 collective-permute-start.6
  25.9 0.1 collective-permute-start.7
  26.0 1.6 %shard_map.92 = (bf16[384,384]{1,0:T(8,128)(2,1)S(1)}, bf16[384,768]{1,0:T(8,128)(2,1)S(1)}) custom-call(f32[2,128]{1,0:T(2,128)S(1)} %get-tuple-element.71.refs_0_, f32[72,128]{1,0:T(8,128)S(1)} %get-tuple-element.72.refs_1_, s32[12,128]{1,0:T(8,128)S(1)} %get-tuple-element.73.refs_2_, s32[768,128]{1,0:T(8,128)S(1)} %get-tuple-element.74.refs_3_, ...), custom_call_target="tpu_custom_call" | custom-call | bytes 4666368 | tf_op jit(solution)/shard_map/pallas_call | solution.py:46
  27.6 0.0 collective-permute-done.5.refs_9_
  27.6 0.0 collective-permute-done.6.refs_10_
  27.6 0.1 collective-permute-done.7.refs_11_
  27.7 1.3 %shard_map.93 = (bf16[768,1024]{1,0:T(8,128)(2,1)S(1)}, bf16[768,384]{1,0:T(8,128)(2,1)S(1)}, bf16[384,1024]{1,0:T(8,128)(2,1)S(1)}) custom-call(f32[2,128]{1,0:T(2,128)S(1)} %get-tuple-element.71.refs_0_, f32[72,128]{1,0:T(8,128)S(1)} %get-tuple-element.72.refs_1_, s32[12,128]{1,0:T(8,128)S(1)} %get-tuple-element.73.refs_2_, ...), custom_call_target="tpu_custom_call" | custom-call | bytes 7320576 | tf_op jit(solution)/shard_map/pallas_call | solution.py:46
  29.0 0.6 collective-permute-start.14
  29.6 2.3 %shard_map.94 = (bf16[768,384]{1,0:T(8,128)(2,1)S(1)}, f32[768,1024]{1,0:T(8,128)S(1)}, bf16[768,768]{1,0:T(8,128)(2,1)S(1)}) custom-call(f32[2,128]{1,0:T(2,128)S(1)} %get-tuple-element.71.refs_0_, f32[72,128]{1,0:T(8,128)S(1)} %get-tuple-element.72.refs_1_, s32[12,128]{1,0:T(8,128)S(1)} %get-tuple-element.73.refs_2_, ...), custom_call_target="tpu_custom_call" | custom-call | bytes 10957824 | tf_op jit(solution)/shard_map/pallas_call | solution.py:46
  31.9 0.0 collective-permute-done.8.refs_9_
  31.9 1.4 %shard_map.95 = (bf16[768,768]{1,0:T(8,128)(2,1)S(1)}, bf16[768,1024]{1,0:T(8,128)(2,1)S(1)}) custom-call(f32[2,128]{1,0:T(2,128)S(1)} %get-tuple-element.71.refs_0_, f32[72,128]{1,0:T(8,128)S(1)} %get-tuple-element.72.refs_1_, s32[12,128]{1,0:T(8,128)S(1)} %get-tuple-element.73.refs_2_, s32[768,128]{1,0:T(8,128)S(1)} %get-tuple-element.74.refs_3_, ...), custom_call_target="tpu_custom_call" | custom-call | bytes 7123968 | tf_op jit(solution)/shard_map/pallas_call | solution.py:46
  33.3 0.8 %shard_map.96 = (bf16[256,1024]{1,0:T(8,128)(2,1)S(1)}, bf16[128,1024]{1,0:T(8,128)(2,1)S(1)}) custom-call(bf16[768,768]{1,0:T(8,128)(2,1)S(1)} %get-tuple-element.99.weight_ref, bf16[768,1024]{1,0:T(8,128)(2,1)S(1)} %get-tuple-element.91.refs_6_.unit_ref), custom_call_target="tpu_custom_call" | custom-call | bytes 3538944 | tf_op jit(solution)/shard_map/pallas_call | solution.py:46
  34.2 0.8 %shard_map.97 = (bf16[192,1024]{1,0:T(8,128)(2,1)S(1)}, bf16[192,1024]{1,0:T(8,128)(2,1)S(1)}) custom-call(bf16[768,768]{1,0:T(8,128)(2,1)S(1)} %get-tuple-element.99.weight_ref, bf16[768,1024]{1,0:T(8,128)(2,1)S(1)} %get-tuple-element.105.image_ref, f32[768,1024]{1,0:T(8,128)S(1)} %get-tuple-element.103.acc_ref), custom_call_target="tpu_custom_call" | custom-call | bytes 6684672 | tf_op jit(solution)/shard_map/pallas_call | solution.py:46
  34.9 1.1 %collective-permute-start.9 = (bf16[192,1024]{1,0:T(8,128)(2,1)S(1)}, bf16[192,1024]{1,0:T(8,128)(2,1)S(1)}, u32[]{:S(2)}, u32[]{:S(2)}) collective-permute-start(bf16[192,1024]{1,0:T(8,128)(2,1)S(1)} %get-tuple-element.106), channel_id=1, source_target_pairs={{0,4},{4,0},{8,12},{12,8},{16,20},{20,16},{24,28},{28,24},{1,5},{5... | collective-permute-start | bytes 1179656 | tf_op jit(solution)/shard_map/ppermute | solution.py:436
  36.1 0.1 collective-permute-start.10
  36.1 0.9 %collective-permute-start.15 = (bf16[256,1024]{1,0:T(8,128)(2,1)S(1)}, bf16[256,1024]{1,0:T(8,128)(2,1)S(1)}, u32[]{:S(2)}, u32[]{:S(2)}) collective-permute-start(bf16[256,1024]{1,0:T(8,128)(2,1)S(1)} %get-tuple-element.119), channel_id=1, source_target_pairs={{0,8},{4,20},{8,0},{12,28},{16,24},{20,4},{24,16},{28,12},{1,9},{5... | collective-permute-start | bytes 1572872 | tf_op jit(solution)/shard_map/ppermute | solution.py:441
  37.0 1.2 %collective-permute-start.17 = (bf16[128,1024]{1,0:T(8,128)(2,1)S(1)}, bf16[128,1024]{1,0:T(8,128)(2,1)S(1)}, u32[]{:S(2)}, u32[]{:S(2)}) collective-permute-start(bf16[128,1024]{1,0:T(8,128)(2,1)S(1)} %get-tuple-element.122), channel_id=1, source_target_pairs={{0,8},{4,20},{8,0},{12,28},{16,24},{20,4},{24,16},{28,12},{1,9},{5... | collective-permute-start | bytes 786440 | tf_op jit(solution)/shard_map/ppermute | solution.py:441
  38.2 0.8 %shard_map.98.refs_5_ = f32[384,1024]{1,0:T(8,128)S(1)} custom-call(bf16[768,768]{1,0:T(8,128)(2,1)S(1)} %get-tuple-element.99.weight_ref, bf16[768,1024]{1,0:T(8,128)(2,1)S(1)} %get-tuple-element.105.image_ref, f32[768,1024]{1,0:T(8,128)S(1)} %get-tuple-element.103.acc_ref), custom_call_target="tpu_custom_call" | custom-call | bytes 7471104 | tf_op jit(solution)/shard_map/pallas_call | solution.py:46
  39.0 0.6 %shard_map.99 = (bf16[384,256]{1,0:T(8,128)(2,1)S(1)}, bf16[384,256]{1,0:T(8,128)(2,1)S(1)}, bf16[384,256]{1,0:T(8,128)(2,1)S(1)}, bf16[384,256]{1,0:T(8,128)(2,1)S(1)}) custom-call(f32[384,128]{1,0:T(8,128)S(1)} %get-tuple-element.95.refs_0_, bf16[384,256]{1,0:T(8,128)(2,1)S(1)} %get-tuple-element.77.refs_0_.refs_1_, ...), custom_call_target="tpu_custom_call" | custom-call | bytes 4128768 | tf_op jit(solution)/shard_map/pallas_call | solution.py:46
  39.6 2.6 %collective-permute-start.11 = (bf16[384,256]{1,0:T(8,128)(2,1)S(1)}, bf16[384,256]{1,0:T(8,128)(2,1)S(1)}, u32[]{:S(2)}, u32[]{:S(2)}) collective-permute-start(bf16[384,256]{1,0:T(8,128)(2,1)S(1)} %get-tuple-element.110), channel_id=1, source_target_pairs={{0,3},{1,2},{2,1},{3,0},{4,7},{5,6},{6,5},{7,4},{8,11},{9,10},{10,... | collective-permute-start | bytes 589832 | tf_op jit(solution)/shard_map/ppermute | solution.py:436
  42.2 1.9 %collective-permute-start.13 = (bf16[384,256]{1,0:T(8,128)(2,1)S(1)}, bf16[384,256]{1,0:T(8,128)(2,1)S(1)}, u32[]{:S(2)}, u32[]{:S(2)}) collective-permute-start(bf16[384,256]{1,0:T(8,128)(2,1)S(1)} %get-tuple-element.112), channel_id=1, source_target_pairs={{0,1},{1,0},{2,3},{3,2},{4,5},{5,4},{6,7},{7,6},{8,9},{9,8},{10,11... | collective-permute-start | bytes 589832 | tf_op jit(solution)/shard_map/ppermute | solution.py:436
  44.1 0.8 %shard_map.100 = (f32[384,1024]{1,0:T(8,128)S(1)}, bf16[384,1024]{1,0:T(8,128)(2,1)S(1)}) custom-call(bf16[768,768]{1,0:T(8,128)(2,1)S(1)} %get-tuple-element.115.weight_ref, bf16[768,1024]{1,0:T(8,128)(2,1)S(1)} %get-tuple-element.91.refs_6_.unit_ref, bf16[384,1024]{1,0:T(8,128)(2,1)S(1)} %collective-permute-done.14.add_ref), custom_call_target="tpu_custom_call" | custom-call | bytes 5898240 | tf_op jit(solution)/shard_map/pallas_call | solution.py:46
  44.9 0.8 %shard_map.101.refs_6_.sum_ref = f32[384,1024]{1,0:T(8,128)S(1)} custom-call(bf16[768,384]{1,0:T(8,128)(2,1)S(1)} %get-tuple-element.97.refs_8_.weight_ref, bf16[768,1024]{1,0:T(8,128)(2,1)S(1)} %get-tuple-element.91.refs_6_.unit_ref, bf16[384,1024]{1,0:T(8,128)(2,1)S(1)} %get-tuple-element.117.add_ref), custom_call_target="tpu_custom_call" | custom-call | tf_op jit(solution)/shard_map/pallas_call | solution.py:46
  45.7 1.0 %collective-permute-done.15.in_ref = bf16[256,1024]{1,0:T(8,128)(2,1)S(1)} collective-permute-done((bf16[256,1024]{1,0:T(8,128)(2,1)S(1)}, bf16[256,1024]{1,0:T(8,128)(2,1)S(1)}, u32[]{:S(2)}, u32[]{:S(2)}) %collective-permute-start.15) | collective-permute-done | bytes 524320 | tf_op jit(solution)/shard_map/ppermute | solution.py:441
  46.7 0.1 shard_map.102
  46.8 1.6 %collective-permute-start.16 = (bf16[256,1024]{1,0:T(8,128)(2,1)S(1)}, bf16[256,1024]{1,0:T(8,128)(2,1)S(1)}, u32[]{:S(2)}, u32[]{:S(2)}) collective-permute-start(bf16[256,1024]{1,0:T(8,128)(2,1)S(1)} %shard_map.102), channel_id=1, source_target_pairs={{0,16},{4,12},{8,24},{12,4},{16,0},{20,28},{24,8},{28,20},{1,17},{... | collective-permute-start | bytes 1572872 | tf_op jit(solution)/shard_map/ppermute | solution.py:441
  48.3 1.6 %collective-permute-done.17.in_ref = bf16[128,1024]{1,0:T(8,128)(2,1)S(1)} collective-permute-done((bf16[128,1024]{1,0:T(8,128)(2,1)S(1)}, bf16[128,1024]{1,0:T(8,128)(2,1)S(1)}, u32[]{:S(2)}, u32[]{:S(2)}) %collective-permute-start.17) | collective-permute-done | bytes 262176 | tf_op jit(solution)/shard_map/ppermute | solution.py:441
  50.0 0.1 shard_map.105
  50.0 1.6 %collective-permute-start.18 = (bf16[128,1024]{1,0:T(8,128)(2,1)S(1)}, bf16[128,1024]{1,0:T(8,128)(2,1)S(1)}, u32[]{:S(2)}, u32[]{:S(2)}) collective-permute-start(bf16[128,1024]{1,0:T(8,128)(2,1)S(1)} %shard_map.105), channel_id=1, source_target_pairs={{0,16},{4,12},{8,24},{12,4},{16,0},{20,28},{24,8},{28,20},{1,17},{... | collective-permute-start | bytes 786440 | tf_op jit(solution)/shard_map/ppermute | solution.py:441
  51.6 6.7 %collective-permute-done.12.refs_1_.refs_2_ = bf16[384,256]{1,0:T(8,128)(2,1)S(1)} collective-permute-done((bf16[384,256]{1,0:T(8,128)(2,1)S(1)}, bf16[384,256]{1,0:T(8,128)(2,1)S(1)}, u32[]{:S(2)}, u32[]{:S(2)}) %collective-permute-start.12) | collective-permute-done | bytes 196640 | tf_op jit(solution)/shard_map/ppermute | solution.py:436
  58.4 1.4 %shard_map.104 = (bf16[1536,256]{1,0:T(8,128)(2,1)}, bf16[384,1024]{1,0:T(8,128)(2,1)}) custom-call(bf16[384,256]{1,0:T(8,128)(2,1)S(1)} %get-tuple-element.109.refs_0_, bf16[384,256]{1,0:T(8,128)(2,1)S(1)} %collective-permute-done.11.refs_0_.refs_1_, bf16[384,256]{1,0:T(8,128)(2,1)S(1)} %collective-permute-done.12.refs_1_.refs_2_, ...), custom_call_target="tpu_custom_call" | custom-call | bytes 5443584 | tf_op jit(solution)/shard_map/pallas_call | solution.py:46
  59.8 1.0 %shard_map.106 = bf16[384,1024]{1,0:T(8,128)(2,1)} custom-call(bf16[384,1024]{1,0:T(8,128)(2,1)S(1)} %get-tuple-element.113.refs_4_.raw_ref, f32[384,128]{1,0:T(8,128)S(1)} %get-tuple-element.114.refs_5_.scale_ref, f32[384,1024]{1,0:T(8,128)S(1)} %shard_map.101.refs_6_.sum_ref, ...), custom_call_target="tpu_custom_call", output_to_operand_aliasing={{}: (4, {})} | custom-call | bytes 4390912 | tf_op jit(solution)/shard_map/pallas_call | solution.py:46
  (19 shorter events, 0.0 us)
Async XLA Ops:
  0.6 14.7 %collective-permute-start = (bf16[384,1024]{1,0:T(8,128)(2,1)}, bf16[384,1024]{1,0:T(8,128)(2,1)S(1)}, u32[]{:S(2)}, u32[]{:S(2)}) collective-permute-start(bf16[384,1024]{1,0:T(8,128)(2,1)} %raw_ref.1), channel_id=1, source_target_pairs={{0,16},{4,12},{8,24},{12,4},{16,0},{20,28},{24,8},{28,20},{1,17},{... | collective-permute-start | bytes 2359304 | tf_op jit(solution)/shard_map/ppermute | solution.py:441
  3.7 1.1 %copy-start = (bf16[1536,256]{1,0:T(8,128)(2,1)S(1)}, bf16[1536,256]{1,0:T(8,128)(2,1)}, u32[]{:S(2)}) copy-start(bf16[1536,256]{1,0:T(8,128)(2,1)} %text_ref.1) | copy-start | bytes 2359300
  4.8 8.8 %copy-start.1 = (s32[12288]{0:T(1024)S(1)}, s32[12288]{0:T(1024)}, u32[]{:S(2)}) copy-start(s32[12288]{0:T(1024)} %param.11) | copy-start | bytes 147460
  4.8 8.8 %copy-start.2 = (s32[12288]{0:T(1024)S(1)}, s32[12288]{0:T(1024)}, u32[]{:S(2)}) copy-start(s32[12288]{0:T(1024)} %param.12) | copy-start | bytes 147460
  4.8 8.8 %copy-start.3 = (s32[96,8,3]{0,1,2:T(8,128)S(1)}, s32[96,8,3]{0,1,2:T(8,128)}, u32[]{:S(2)}) copy-start(s32[96,8,3]{0,1,2:T(8,128)} %param.13) | copy-start | bytes 27652
  4.9 18.5 %collective-permute-start.1 = (bf16[384,256]{1,0:T(8,128)(2,1)S(1)}, bf16[384,256]{1,0:T(8,128)(2,1)S(1)}, u32[]{:S(2)}, u32[]{:S(2)}) collective-permute-start(bf16[384,256]{1,0:T(8,128)(2,1)S(1)} %get-tuple-element.78), channel_id=1, source_target_pairs={{0,3},{1,2},{2,1},{3,0},{4,7},{5,6},{6,5},{7,4},{8,11},{9,10},{10,... | collective-permute-start | bytes 589832 | tf_op jit(solution)/shard_map/ppermute | solution.py:436
  8.5 16.4 %collective-permute-start.2 = (bf16[384,256]{1,0:T(8,128)(2,1)S(1)}, bf16[384,256]{1,0:T(8,128)(2,1)S(1)}, u32[]{:S(2)}, u32[]{:S(2)}) collective-permute-start(bf16[384,256]{1,0:T(8,128)(2,1)S(1)} %get-tuple-element.79), channel_id=1, source_target_pairs={{0,2},{1,3},{2,0},{3,1},{4,6},{5,7},{6,4},{7,5},{8,10},{9,11},{10,... | collective-permute-start | bytes 589832 | tf_op jit(solution)/shard_map/ppermute | solution.py:436
  8.5 14.8 %collective-permute-start.3 = (bf16[384,256]{1,0:T(8,128)(2,1)S(1)}, bf16[384,256]{1,0:T(8,128)(2,1)S(1)}, u32[]{:S(2)}, u32[]{:S(2)}) collective-permute-start(bf16[384,256]{1,0:T(8,128)(2,1)S(1)} %get-tuple-element.80), channel_id=1, source_target_pairs={{0,1},{1,0},{2,3},{3,2},{4,5},{5,4},{6,7},{7,6},{8,9},{9,8},{10,11... | collective-permute-start | bytes 589832 | tf_op jit(solution)/shard_map/ppermute | solution.py:436
  10.7 12.3 %collective-permute-start.4 = (bf16[384,1024]{1,0:T(8,128)(2,1)}, bf16[384,1024]{1,0:T(8,128)(2,1)S(1)}, u32[]{:S(2)}, u32[]{:S(2)}) collective-permute-start(bf16[384,1024]{1,0:T(8,128)(2,1)} %raw_ref.1), channel_id=1, source_target_pairs={{0,8},{4,20},{8,0},{12,28},{16,24},{20,4},{24,16},{28,12},{1,9},{5... | collective-permute-start | bytes 2359304 | tf_op jit(solution)/shard_map/ppermute | solution.py:441
  15.3 16.6 %collective-permute-start.8 = (bf16[384,1024]{1,0:T(8,128)(2,1)S(1)}, bf16[384,1024]{1,0:T(8,128)(2,1)S(1)}, u32[]{:S(2)}, u32[]{:S(2)}) collective-permute-start(bf16[384,1024]{1,0:T(8,128)(2,1)S(1)} %collective-permute-done.raw_ref), channel_id=1, source_target_pairs={{0,8},{4,20},{8,0},{12,28},{16,24},{20,4},{24,16},{28,12},{1,9},{5... | collective-permute-start | bytes 2359304 | tf_op jit(solution)/shard_map/ppermute | solution.py:441
  25.3 2.2 %collective-permute-start.5 = (bf16[128,1024]{1,0:T(8,128)(2,1)S(1)}, bf16[128,1024]{1,0:T(8,128)(2,1)S(1)}, u32[]{:S(2)}, u32[]{:S(2)}) collective-permute-start(bf16[128,1024]{1,0:T(8,128)(2,1)S(1)} %get-tuple-element.88), channel_id=1, source_target_pairs={{0,4},{4,0},{8,12},{12,8},{16,20},{20,16},{24,28},{28,24},{1,5},{5... | collective-permute-start | bytes 786440 | tf_op jit(solution)/shard_map/ppermute | solution.py:436
  25.4 2.2 %collective-permute-start.6 = (bf16[128,1024]{1,0:T(8,128)(2,1)S(1)}, bf16[128,1024]{1,0:T(8,128)(2,1)S(1)}, u32[]{:S(2)}, u32[]{:S(2)}) collective-permute-start(bf16[128,1024]{1,0:T(8,128)(2,1)S(1)} %get-tuple-element.89), channel_id=1, source_target_pairs={{0,4},{4,0},{8,12},{12,8},{16,20},{20,16},{24,28},{28,24},{1,5},{5... | collective-permute-start | bytes 786440 | tf_op jit(solution)/shard_map/ppermute | solution.py:436
  25.9 1.8 %collective-permute-start.7 = (bf16[128,1024]{1,0:T(8,128)(2,1)S(1)}, bf16[128,1024]{1,0:T(8,128)(2,1)S(1)}, u32[]{:S(2)}, u32[]{:S(2)}) collective-permute-start(bf16[128,1024]{1,0:T(8,128)(2,1)S(1)} %get-tuple-element.90), channel_id=1, source_target_pairs={{0,4},{4,0},{8,12},{12,8},{16,20},{20,16},{24,28},{28,24},{1,5},{5... | collective-permute-start | bytes 786440 | tf_op jit(solution)/shard_map/ppermute | solution.py:436
  29.0 13.2 %collective-permute-start.14 = (bf16[384,1024]{1,0:T(8,128)(2,1)S(1)}, bf16[384,1024]{1,0:T(8,128)(2,1)S(1)}, u32[]{:S(2)}, u32[]{:S(2)}) collective-permute-start(bf16[384,1024]{1,0:T(8,128)(2,1)S(1)} %get-tuple-element.116), channel_id=1, source_target_pairs={{0,8},{4,20},{8,0},{12,28},{16,24},{20,4},{24,16},{28,12},{1,9},{5... | collective-permute-start | bytes 2359304 | tf_op jit(solution)/shard_map/ppermute | solution.py:441
  34.9 4.0 %collective-permute-start.9 = (bf16[192,1024]{1,0:T(8,128)(2,1)S(1)}, bf16[192,1024]{1,0:T(8,128)(2,1)S(1)}, u32[]{:S(2)}, u32[]{:S(2)}) collective-permute-start(bf16[192,1024]{1,0:T(8,128)(2,1)S(1)} %get-tuple-element.106), channel_id=1, source_target_pairs={{0,4},{4,0},{8,12},{12,8},{16,20},{20,16},{24,28},{28,24},{1,5},{5... | collective-permute-start | bytes 1179656 | tf_op jit(solution)/shard_map/ppermute | solution.py:436
  36.1 2.9 %collective-permute-start.10 = (bf16[192,1024]{1,0:T(8,128)(2,1)S(1)}, bf16[192,1024]{1,0:T(8,128)(2,1)S(1)}, u32[]{:S(2)}, u32[]{:S(2)}) collective-permute-start(bf16[192,1024]{1,0:T(8,128)(2,1)S(1)} %get-tuple-element.107), channel_id=1, source_target_pairs={{0,4},{4,0},{8,12},{12,8},{16,20},{20,16},{24,28},{28,24},{1,5},{5... | collective-permute-start | bytes 1179656 | tf_op jit(solution)/shard_map/ppermute | solution.py:436
  36.1 10.5 %collective-permute-start.15 = (bf16[256,1024]{1,0:T(8,128)(2,1)S(1)}, bf16[256,1024]{1,0:T(8,128)(2,1)S(1)}, u32[]{:S(2)}, u32[]{:S(2)}) collective-permute-start(bf16[256,1024]{1,0:T(8,128)(2,1)S(1)} %get-tuple-element.119), channel_id=1, source_target_pairs={{0,8},{4,20},{8,0},{12,28},{16,24},{20,4},{24,16},{28,12},{1,9},{5... | collective-permute-start | bytes 1572872 | tf_op jit(solution)/shard_map/ppermute | solution.py:441
  37.0 13.0 %collective-permute-start.17 = (bf16[128,1024]{1,0:T(8,128)(2,1)S(1)}, bf16[128,1024]{1,0:T(8,128)(2,1)S(1)}, u32[]{:S(2)}, u32[]{:S(2)}) collective-permute-start(bf16[128,1024]{1,0:T(8,128)(2,1)S(1)} %get-tuple-element.122), channel_id=1, source_target_pairs={{0,8},{4,20},{8,0},{12,28},{16,24},{20,4},{24,16},{28,12},{1,9},{5... | collective-permute-start | bytes 786440 | tf_op jit(solution)/shard_map/ppermute | solution.py:441
  39.6 12.0 %collective-permute-start.11 = (bf16[384,256]{1,0:T(8,128)(2,1)S(1)}, bf16[384,256]{1,0:T(8,128)(2,1)S(1)}, u32[]{:S(2)}, u32[]{:S(2)}) collective-permute-start(bf16[384,256]{1,0:T(8,128)(2,1)S(1)} %get-tuple-element.110), channel_id=1, source_target_pairs={{0,3},{1,2},{2,1},{3,0},{4,7},{5,6},{6,5},{7,4},{8,11},{9,10},{10,... | collective-permute-start | bytes 589832 | tf_op jit(solution)/shard_map/ppermute | solution.py:436
  42.1 16.2 %collective-permute-start.12 = (bf16[384,256]{1,0:T(8,128)(2,1)S(1)}, bf16[384,256]{1,0:T(8,128)(2,1)S(1)}, u32[]{:S(2)}, u32[]{:S(2)}) collective-permute-start(bf16[384,256]{1,0:T(8,128)(2,1)S(1)} %get-tuple-element.111), channel_id=1, source_target_pairs={{0,2},{1,3},{2,0},{3,1},{4,6},{5,7},{6,4},{7,5},{8,10},{9,11},{10,... | collective-permute-start | bytes 589832 | tf_op jit(solution)/shard_map/ppermute | solution.py:436
  42.2 16.2 %collective-permute-start.13 = (bf16[384,256]{1,0:T(8,128)(2,1)S(1)}, bf16[384,256]{1,0:T(8,128)(2,1)S(1)}, u32[]{:S(2)}, u32[]{:S(2)}) collective-permute-start(bf16[384,256]{1,0:T(8,128)(2,1)S(1)} %get-tuple-element.112), channel_id=1, source_target_pairs={{0,1},{1,0},{2,3},{3,2},{4,5},{5,4},{6,7},{7,6},{8,9},{9,8},{10,11... | collective-permute-start | bytes 589832 | tf_op jit(solution)/shard_map/ppermute | solution.py:436
  46.8 11.6 %collective-permute-start.16 = (bf16[256,1024]{1,0:T(8,128)(2,1)S(1)}, bf16[256,1024]{1,0:T(8,128)(2,1)S(1)}, u32[]{:S(2)}, u32[]{:S(2)}) collective-permute-start(bf16[256,1024]{1,0:T(8,128)(2,1)S(1)} %shard_map.102), channel_id=1, source_target_pairs={{0,16},{4,12},{8,24},{12,4},{16,0},{20,28},{24,8},{28,20},{1,17},{... | collective-permute-start | bytes 1572872 | tf_op jit(solution)/shard_map/ppermute | solution.py:441
  50.0 9.7 %collective-permute-start.18 = (bf16[128,1024]{1,0:T(8,128)(2,1)S(1)}, bf16[128,1024]{1,0:T(8,128)(2,1)S(1)}, u32[]{:S(2)}, u32[]{:S(2)}) collective-permute-start(bf16[128,1024]{1,0:T(8,128)(2,1)S(1)} %shard_map.105), channel_id=1, source_target_pairs={{0,16},{4,12},{8,24},{12,4},{16,0},{20,28},{24,8},{28,20},{1,17},{... | collective-permute-start | bytes 786440 | tf_op jit(solution)/shard_map/ppermute | solution.py:441

commit v14 on v13

--- a/solution.py
+++ b/solution.py
@@ -33,7 +33,6 @@
     scratch=(),
     flops=0,
     moved=None,
-    aliases=None,
     limit=24,
 ):
     if moved is None:
@@ -49,7 +48,6 @@
             in_specs=specs,
             out_specs=[ANY_SPEC if outs_anywhere else VMEM_SPEC] * len(outs),
             scratch_shapes=list(scratch),
-            input_output_aliases=aliases or {},
             compiler_params=pltpu.CompilerParams(vmem_limit_bytes=limit * MIB),
             cost_estimate=pl.CostEstimate(flops=flops, bytes_accessed=moved, transcendentals=0),
         )(*operands)
@@ -141,10 +139,11 @@
     raw_out_ref[...] = raw_ref[...]
 
 
-def near_images_body(first_ref, second_unit_ref, out_ref):
+def near_images_body(first_ref, second_unit_ref, own_unit_ref, out_ref):
     rows = first_ref.shape[0]
     unit_images(first_ref, out_ref)
-    out_ref[rows:, :] = second_unit_ref[...]
+    out_ref[rows : 2 * rows, :] = second_unit_ref[...]
+    out_ref[2 * rows :, :] = own_unit_ref[...]
 
 
 def neighbour_bits(shard):
@@ -225,14 +224,12 @@
 
 def near_own_body(tiles, *refs):
     pairs = Pairs(refs, tiles)
-    unit_ref, own_image_ref, near_image_ref, own_weight_ref, weight_ref = refs[Pairs.count :]
+    unit_ref, image_ref, own_weight_ref, weight_ref = refs[Pairs.count :]
     rows = unit_ref.shape[0]
-    first = dot_nt(unit_ref[...], near_image_ref[pl.ds(0, rows), :])
-    second = dot_nt(unit_ref[...], near_image_ref[pl.ds(rows, rows), :])
-    pairs.weigh(first, 0, 1, weight_ref, 0, 0)
-    own = dot_nt(unit_ref[...], own_image_ref[...])
-    pairs.weigh(second, 0, 2, weight_ref, 0, rows)
-    pairs.weigh(own, 0, 0, own_weight_ref, 0, 0, "diagonal")
+    products = dot_nt(unit_ref[...], image_ref[...])
+    pairs.weigh(products[:, :rows], 0, 1, weight_ref, 0, 0)
+    pairs.weigh(products[:, rows : 2 * rows], 0, 2, weight_ref, 0, rows)
+    pairs.weigh(products[:, 2 * rows :], 0, 0, own_weight_ref, 0, 0, "diagonal")
 
 
 def first_sum_body(tiles, *refs):
@@ -252,20 +249,19 @@
 
 def near_sum_body(tiles, *refs):
     pairs = Pairs(refs, tiles)
-    unit_ref, own_image_ref, near_image_ref, own_weight_in_ref, weight_in_ref, first_ref = refs[
-        Pairs.count : Pairs.count + 6
+    unit_ref, image_ref, own_weight_in_ref, weight_in_ref, first_ref = refs[
+        Pairs.count : Pairs.count + 5
     ]
-    own_weight_ref, acc_ref, weight_ref = refs[Pairs.count + 6 :]
-    rows = own_image_ref.shape[0]
-    second = dot_nt(unit_ref[rows:, :], near_image_ref[pl.ds(rows, rows), :])
-    own = dot_nt(unit_ref[rows:, :], own_image_ref[...])
+    own_weight_ref, acc_ref, weight_ref = refs[Pairs.count + 5 :]
+    rows = first_ref.shape[1]
+    products = dot_nt(unit_ref[rows:, :], image_ref[rows:, :])
     own_weight_ref[:rows, :] = own_weight_in_ref[...]
     weight_ref[:, :rows] = first_ref[...]
     weight_ref[:rows, rows:] = weight_in_ref[:, rows:]
-    pairs.weigh(second, 1, 2, weight_ref, rows, rows)
-    pairs.weigh(own, 1, 0, own_weight_ref, rows, 0)
+    pairs.weigh(products[:, :rows], 1, 2, weight_ref, rows, rows)
+    pairs.weigh(products[:, rows:], 1, 0, own_weight_ref, rows, 0)
     acc_ref[...] = jnp.dot(
-        weight_ref[...], near_image_ref[...], preferred_element_type=jnp.float32
+        weight_ref[...], image_ref[: 2 * rows, :], preferred_element_type=jnp.float32
     )
 
 
@@ -395,9 +391,9 @@
         copies[-1].start()
 
 
-def finish_body(chunks, count, *refs):
+def finish_body(chunks, adds, *refs):
     part_refs, (raw_ref, scale_ref, sum_ref) = refs[:chunks], refs[chunks : chunks + 3]
-    add_ref = refs[chunks + 3] if len(refs) == chunks + 9 else None
+    add_refs = refs[chunks + 3 : chunks + 3 + adds]
     text_ref, image_ref, grad_ref, sems = refs[-4:]
     place = lax.axis_index("tp")
     rows = part_refs[0].shape[0]
@@ -414,19 +410,13 @@
                 )
             )
             copies[-1].start()
-    finish_rows(
-        0, count, raw_ref, scale_ref, sum_ref, add_ref, grad_ref, image_ref, sems, copies
-    )
-    for copy in copies:
-        copy.wait()
-
-
-def finish_last_body(start, raw_ref, scale_ref, sum_ref, add_ref, _, image_ref, grad_ref, sems):
-    copies = []
-    count = add_ref.shape[0]
-    finish_rows(
-        start, count, raw_ref, scale_ref, sum_ref, add_ref, grad_ref, image_ref, sems, copies
-    )
+    start = 0
+    for add_ref in add_refs or [None]:
+        count = rows if add_ref is None else add_ref.shape[0]
+        finish_rows(
+            start, count, raw_ref, scale_ref, sum_ref, add_ref, grad_ref, image_ref, sems, copies
+        )
+        start += count
     for copy in copies:
         copy.wait()
 
@@ -510,7 +500,7 @@
             unit_images_body, [bf16(rows)], [from_second], flops=WAIT_FLOPS // 2, limit=8
         )[0]
         near_images = call_kernel(
-            near_images_body, [bf16(2 * rows)], [from_first, second_images], limit=8
+            near_images_body, [bf16(3 * rows)], [from_first, second_images, own_images], limit=8
         )[0]
         text_raw[-1], near_images = lax.optimization_barrier((text_raw[-1], near_images))
     text_own, text_scales, *pieces = call_kernel(
@@ -539,33 +529,19 @@
             flops=WAIT_FLOPS,
             limit=8,
         )
-        head = pieces[0].shape[0] if pieces else rows
-        text_grad, image_grad = call_kernel(
-            functools.partial(finish_body, groups, head),
-            [bf16(groups * rows, width), bf16(rows)],
-            text_parts + [image_raw, image_scales, total] + pieces[:1] + arrived,
-            outs_anywhere=True,
-            scratch=[
-                pltpu.VMEM((rows, embed), jnp.bfloat16),
-                pltpu.SemaphoreType.DMA(((groups + 2) * tiles,)),
-            ],
-            limit=8,
-        )
-        if pieces:
-            image_grad = call_kernel(
-                functools.partial(finish_last_body, head),
-                [bf16(rows)],
-                [image_raw, image_scales, total, pieces[1], image_grad],
-                anywhere=(4,),
+        return tuple(
+            call_kernel(
+                functools.partial(finish_body, groups, len(pieces)),
+                [bf16(groups * rows, width), bf16(rows)],
+                text_parts + [image_raw, image_scales, total] + pieces + arrived,
                 outs_anywhere=True,
-                aliases={4: 0},
                 scratch=[
                     pltpu.VMEM((rows, embed), jnp.bfloat16),
-                    pltpu.SemaphoreType.DMA((2 * tiles,)),
+                    pltpu.SemaphoreType.DMA(((groups + 2) * tiles,)),
                 ],
                 limit=8,
-            )[0]
-        return (text_grad, image_grad)
+            )
+        )
 
     if not square:
         columns = gathered.shape[0]
@@ -590,7 +566,7 @@
     own_weights, near_weights = call_kernel(
         functools.partial(near_own_body, tiles),
         [bf16(rows, rows), bf16(rows, 2 * rows)],
-        lists + [text_own, own_images, near_images],
+        lists + [text_own, near_images],
         limit=16,
     )
     units, first_weights, first_sum = call_kernel(
@@ -603,7 +579,7 @@
     own_weights, acc, near_weights = call_kernel(
         functools.partial(near_sum_body, tiles),
         [bf16(2 * rows, rows), f32(2 * rows), bf16(2 * rows, 2 * rows)],
-        lists + [units, own_images, near_images, own_weights, near_weights, first_weights],
+        lists + [units, near_images, own_weights, near_weights, first_weights],
         limit=24,
     )
     own_weights, from_far = lax.optimization_barrier((own_weights, from_far))

time: 61 us -> 60.6 us (level)
  Pallas kernels: 17.3 us -> 16.2 us
  waiting for transfers between devices: 15.8 us -> 16.6 us
    pallas_call x21 -> x20, Pallas kernels: 17.3 us -> 16.2 us  [call_kernel(): pl.pallas_call(body, out_shape=outs, in_specs=specs, out_specs=[ANY_SPEC...]
    ppermute x8, waiting for transfers between devices: 7.36 us -> 8.15 us  [swap_near(): lax.ppermute(value, 'blk', [(i, i ^ neighbour_bits(i)[which]) for i in ra...]
  transfers between devices with their start and end apart: 19 -> 19, of which waited for: 7 -> 8; matrix products, arithmetic and copies ran while one was open for 0% -> 0% of each run, Pallas kernels for 27% -> 24%
where the time goes in v14:
time: 60.6 us; the launch traced here: 60.4 us
  starting transfers between devices  24.3 us (40%)
  waiting for transfers between devices  16.6 us (27%)
  Pallas kernels  16.2 us (27%)
  between operations  2.14 us (4%)
  local copies, waits for them, and re-layouts  1.14 us (2%)
    pallas_call x20, Pallas kernels, call_kernel(): pl.pallas_call(body, out_shape=outs, in_specs=specs, out_specs=[ANY_SPEC...  16.2 us
    ppermute x8, starting transfers between devices, swap_near(): lax.ppermute(value, 'blk', [(i, i ^ neighbour_bits(i)[which]) for i in ra...  13.7 us
    ppermute x11, starting transfers between devices, swap(): return lax.ppermute(value, axis, [(i, i ^ bits) for i in range(count)])  10.6 us
    ppermute x11, waiting for transfers between devices, swap(): return lax.ppermute(value, axis, [(i, i ^ bits) for i in range(count)])  8.43 us
    ppermute x8, waiting for transfers between devices, swap_near(): lax.ppermute(value, 'blk', [(i, i ^ neighbour_bits(i)[which]) for i in ra...  8.15 us
  transfers between devices with their start and end apart: 19, of which 8 were waited for; matrix products, arithmetic and copies ran while one was open for 0% of the time, Pallas kernels for 24%

profile of v14, /device:TPU:0, one launch (start us, length us, event | category | flops | bytes accessed | tf_op | source)
XLA Modules:
  0.0 60.4 jit_solution(12613313797450997932)
XLA Ops:
  0.6 3.0 %collective-permute-start = (bf16[384,1024]{1,0:T(8,128)(2,1)}, bf16[384,1024]{1,0:T(8,128)(2,1)S(1)}, u32[]{:S(2)}, u32[]{:S(2)}) collective-permute-start(bf16[384,1024]{1,0:T(8,128)(2,1)} %raw_ref.1), channel_id=1, source_target_pairs={{0,16},{4,12},{8,24},{12,4},{16,0},{20,28},{24,8},{28,20},{1,17},{... | collective-permute-start | bytes 2359304 | tf_op jit(solution)/shard_map/ppermute | solution.py:431
  3.7 1.1 %copy-done = bf16[1536,256]{1,0:T(8,128)(2,1)S(1)} copy-done((bf16[1536,256]{1,0:T(8,128)(2,1)S(1)}, bf16[1536,256]{1,0:T(8,128)(2,1)}, u32[]{:S(2)}) %copy-start) | copy-done | bytes 786456
  4.8 0.1 shard_map.88
  4.9 3.7 %collective-permute-start.1 = (bf16[384,256]{1,0:T(8,128)(2,1)S(1)}, bf16[384,256]{1,0:T(8,128)(2,1)S(1)}, u32[]{:S(2)}, u32[]{:S(2)}) collective-permute-start(bf16[384,256]{1,0:T(8,128)(2,1)S(1)} %get-tuple-element.76), channel_id=1, source_target_pairs={{0,3},{1,2},{2,1},{3,0},{4,7},{5,6},{6,5},{7,4},{8,11},{9,10},{10,... | collective-permute-start | bytes 589832 | tf_op jit(solution)/shard_map/ppermute | solution.py:426
  8.5 0.8 %collective-permute-start.3 = (bf16[384,256]{1,0:T(8,128)(2,1)S(1)}, bf16[384,256]{1,0:T(8,128)(2,1)S(1)}, u32[]{:S(2)}, u32[]{:S(2)}) collective-permute-start(bf16[384,256]{1,0:T(8,128)(2,1)S(1)} %get-tuple-element.78), channel_id=1, source_target_pairs={{0,1},{1,0},{2,3},{3,2},{4,5},{5,4},{6,7},{7,6},{8,9},{9,8},{10,11... | collective-permute-start | bytes 589832 | tf_op jit(solution)/shard_map/ppermute | solution.py:426
  9.3 1.4 %shard_map.86 = (bf16[384,1024]{1,0:T(8,128)(2,1)S(1)}, bf16[384,1024]{1,0:T(8,128)(2,1)S(1)}, f32[384,128]{1,0:T(8,128)S(1)}) custom-call(bf16[384,1024]{1,0:T(8,128)(2,1)} %raw_ref.1), custom_call_target="tpu_custom_call" | custom-call | bytes 2555904 | tf_op jit(solution)/shard_map/pallas_call | solution.py:45
  10.7 1.6 %collective-permute-start.4 = (bf16[384,1024]{1,0:T(8,128)(2,1)}, bf16[384,1024]{1,0:T(8,128)(2,1)S(1)}, u32[]{:S(2)}, u32[]{:S(2)}) collective-permute-start(bf16[384,1024]{1,0:T(8,128)(2,1)} %raw_ref.1), channel_id=1, source_target_pairs={{0,8},{4,20},{8,0},{12,28},{16,24},{20,4},{24,16},{28,12},{1,9},{5... | collective-permute-start | bytes 2359304 | tf_op jit(solution)/shard_map/ppermute | solution.py:431
  13.6 1.1 %shard_map.87 = (f32[2,128]{1,0:T(2,128)S(1)}, f32[72,128]{1,0:T(8,128)S(1)}, s32[12,128]{1,0:T(8,128)S(1)}, s32[768,128]{1,0:T(8,128)S(1)}, f32[384,128]{1,0:T(8,128)S(1)}, /*index=5*/f32[4,128]{1,0:T(4,128)S(1)}) custom-call(f32[1]{0:T(128)S(6)} %copy.9.refs_0_, f32[1]{0:T(128)S(6)} %copy.10.refs_1_, s32[3,8,96]{2,1,0:T(8,128)S(1)} %bitcast.5, ...), custom_call_target="tpu_custom_call" | custom-call | bytes 743432 | tf_op jit(solution)/shard_map/pallas_call | solution.py:45
  14.7 0.6 %collective-permute-done.raw_ref = bf16[384,1024]{1,0:T(8,128)(2,1)S(1)} collective-permute-done((bf16[384,1024]{1,0:T(8,128)(2,1)}, bf16[384,1024]{1,0:T(8,128)(2,1)S(1)}, u32[]{:S(2)}, u32[]{:S(2)}) %collective-permute-start) | collective-permute-done | bytes 786464 | tf_op jit(solution)/shard_map/ppermute | solution.py:431
  15.3 3.3 %collective-permute-start.8 = (bf16[384,1024]{1,0:T(8,128)(2,1)S(1)}, bf16[384,1024]{1,0:T(8,128)(2,1)S(1)}, u32[]{:S(2)}, u32[]{:S(2)}) collective-permute-start(bf16[384,1024]{1,0:T(8,128)(2,1)S(1)} %collective-permute-done.raw_ref), channel_id=1, source_target_pairs={{0,8},{4,20},{8,0},{12,28},{16,24},{20,4},{24,16},{28,12},{1,9},{5... | collective-permute-start | bytes 2359304 | tf_op jit(solution)/shard_map/ppermute | solution.py:431
  18.6 0.2 shard_map.89.second_unit_ref
  18.9 4.1 %collective-permute-done.4.first_ref = bf16[384,1024]{1,0:T(8,128)(2,1)S(1)} collective-permute-done((bf16[384,1024]{1,0:T(8,128)(2,1)}, bf16[384,1024]{1,0:T(8,128)(2,1)S(1)}, u32[]{:S(2)}, u32[]{:S(2)}) %collective-permute-start.4) | collective-permute-done | bytes 786464 | tf_op jit(solution)/shard_map/ppermute | solution.py:431
  23.0 0.3 shard_map.90.refs_7_
  23.3 0.0 collective-permute-done.1.refs_1_.refs_2_
  23.4 1.6 %collective-permute-done.2.refs_2_.refs_3_ = bf16[384,256]{1,0:T(8,128)(2,1)S(1)} collective-permute-done((bf16[384,256]{1,0:T(8,128)(2,1)S(1)}, bf16[384,256]{1,0:T(8,128)(2,1)S(1)}, u32[]{:S(2)}, u32[]{:S(2)}) %collective-permute-start.2) | collective-permute-done | bytes 196640 | tf_op jit(solution)/shard_map/ppermute | solution.py:426
  24.9 0.4 shard_map.91
  25.3 0.1 collective-permute-start.5
  25.4 0.5 collective-permute-start.6
  25.9 0.1 collective-permute-start.7
  26.0 1.4 %shard_map.92 = (bf16[384,384]{1,0:T(8,128)(2,1)S(1)}, bf16[384,768]{1,0:T(8,128)(2,1)S(1)}) custom-call(f32[2,128]{1,0:T(2,128)S(1)} %get-tuple-element.69.refs_0_, f32[72,128]{1,0:T(8,128)S(1)} %get-tuple-element.70.refs_1_, s32[12,128]{1,0:T(8,128)S(1)} %get-tuple-element.71.refs_2_, s32[768,128]{1,0:T(8,128)S(1)} %get-tuple-element.72.refs_3_, ...), custom_call_target="tpu_custom_call" | custom-call | bytes 4666368 | tf_op jit(solution)/shard_map/pallas_call | solution.py:45
  27.4 0.0 collective-permute-done.5.refs_9_
  27.4 0.0 collective-permute-done.6.refs_10_
  27.4 0.2 collective-permute-done.7.refs_11_
  27.7 1.3 %shard_map.93 = (bf16[768,1024]{1,0:T(8,128)(2,1)S(1)}, bf16[768,384]{1,0:T(8,128)(2,1)S(1)}, bf16[384,1024]{1,0:T(8,128)(2,1)S(1)}) custom-call(f32[2,128]{1,0:T(2,128)S(1)} %get-tuple-element.69.refs_0_, f32[72,128]{1,0:T(8,128)S(1)} %get-tuple-element.70.refs_1_, s32[12,128]{1,0:T(8,128)S(1)} %get-tuple-element.71.refs_2_, ...), custom_call_target="tpu_custom_call" | custom-call | bytes 8107008 | tf_op jit(solution)/shard_map/pallas_call | solution.py:45
  29.0 0.6 collective-permute-start.14
  29.6 2.2 %shard_map.94 = (bf16[768,384]{1,0:T(8,128)(2,1)S(1)}, f32[768,1024]{1,0:T(8,128)S(1)}, bf16[768,768]{1,0:T(8,128)(2,1)S(1)}) custom-call(f32[2,128]{1,0:T(2,128)S(1)} %get-tuple-element.69.refs_0_, f32[72,128]{1,0:T(8,128)S(1)} %get-tuple-element.70.refs_1_, s32[12,128]{1,0:T(8,128)S(1)} %get-tuple-element.71.refs_2_, ...), custom_call_target="tpu_custom_call" | custom-call | bytes 10957824 | tf_op jit(solution)/shard_map/pallas_call | solution.py:45
  31.8 1.4 %shard_map.95 = (bf16[768,768]{1,0:T(8,128)(2,1)S(1)}, bf16[768,1024]{1,0:T(8,128)(2,1)S(1)}) custom-call(f32[2,128]{1,0:T(2,128)S(1)} %get-tuple-element.69.refs_0_, f32[72,128]{1,0:T(8,128)S(1)} %get-tuple-element.70.refs_1_, s32[12,128]{1,0:T(8,128)S(1)} %get-tuple-element.71.refs_2_, s32[768,128]{1,0:T(8,128)S(1)} %get-tuple-element.72.refs_3_, ...), custom_call_target="tpu_custom_call" | custom-call | bytes 7123968 | tf_op jit(solution)/shard_map/pallas_call | solution.py:45
  33.2 0.8 %shard_map.96 = (bf16[256,1024]{1,0:T(8,128)(2,1)S(1)}, bf16[128,1024]{1,0:T(8,128)(2,1)S(1)}) custom-call(bf16[768,768]{1,0:T(8,128)(2,1)S(1)} %get-tuple-element.97.weight_ref, bf16[768,1024]{1,0:T(8,128)(2,1)S(1)} %get-tuple-element.89.refs_6_.unit_ref), custom_call_target="tpu_custom_call" | custom-call | bytes 3538944 | tf_op jit(solution)/shard_map/pallas_call | solution.py:45
  34.1 0.8 %shard_map.97 = (bf16[192,1024]{1,0:T(8,128)(2,1)S(1)}, bf16[192,1024]{1,0:T(8,128)(2,1)S(1)}) custom-call(bf16[768,768]{1,0:T(8,128)(2,1)S(1)} %get-tuple-element.97.weight_ref, bf16[768,1024]{1,0:T(8,128)(2,1)S(1)} %get-tuple-element.103.image_ref, f32[768,1024]{1,0:T(8,128)S(1)} %get-tuple-element.101.acc_ref), custom_call_target="tpu_custom_call" | custom-call | bytes 6684672 | tf_op jit(solution)/shard_map/pallas_call | solution.py:45
  34.9 1.0 %collective-permute-start.9 = (bf16[192,1024]{1,0:T(8,128)(2,1)S(1)}, bf16[192,1024]{1,0:T(8,128)(2,1)S(1)}, u32[]{:S(2)}, u32[]{:S(2)}) collective-permute-start(bf16[192,1024]{1,0:T(8,128)(2,1)S(1)} %get-tuple-element.104), channel_id=1, source_target_pairs={{0,4},{4,0},{8,12},{12,8},{16,20},{20,16},{24,28},{28,24},{1,5},{5... | collective-permute-start | bytes 1179656 | tf_op jit(solution)/shard_map/ppermute | solution.py:426
  35.8 0.1 collective-permute-start.10
  35.9 1.0 %collective-permute-start.15 = (bf16[256,1024]{1,0:T(8,128)(2,1)S(1)}, bf16[256,1024]{1,0:T(8,128)(2,1)S(1)}, u32[]{:S(2)}, u32[]{:S(2)}) collective-permute-start(bf16[256,1024]{1,0:T(8,128)(2,1)S(1)} %get-tuple-element.117), channel_id=1, source_target_pairs={{0,8},{4,20},{8,0},{12,28},{16,24},{20,4},{24,16},{28,12},{1,9},{5... | collective-permute-start | bytes 1572872 | tf_op jit(solution)/shard_map/ppermute | solution.py:431
  36.9 1.0 %collective-permute-start.17 = (bf16[128,1024]{1,0:T(8,128)(2,1)S(1)}, bf16[128,1024]{1,0:T(8,128)(2,1)S(1)}, u32[]{:S(2)}, u32[]{:S(2)}) collective-permute-start(bf16[128,1024]{1,0:T(8,128)(2,1)S(1)} %get-tuple-element.119), channel_id=1, source_target_pairs={{0,8},{4,20},{8,0},{12,28},{16,24},{20,4},{24,16},{28,12},{1,9},{5... | collective-permute-start | bytes 786440 | tf_op jit(solution)/shard_map/ppermute | solution.py:431
  37.9 0.8 %shard_map.98.refs_5_ = f32[384,1024]{1,0:T(8,128)S(1)} custom-call(bf16[768,768]{1,0:T(8,128)(2,1)S(1)} %get-tuple-element.97.weight_ref, bf16[768,1024]{1,0:T(8,128)(2,1)S(1)} %get-tuple-element.103.image_ref, f32[768,1024]{1,0:T(8,128)S(1)} %get-tuple-element.101.acc_ref), custom_call_target="tpu_custom_call" | custom-call | bytes 7471104 | tf_op jit(solution)/shard_map/pallas_call | solution.py:45
  38.7 0.0 collective-permute-done.10.refs_7_
  38.8 0.6 %shard_map.99 = (bf16[384,256]{1,0:T(8,128)(2,1)S(1)}, bf16[384,256]{1,0:T(8,128)(2,1)S(1)}, bf16[384,256]{1,0:T(8,128)(2,1)S(1)}, bf16[384,256]{1,0:T(8,128)(2,1)S(1)}) custom-call(f32[384,128]{1,0:T(8,128)S(1)} %get-tuple-element.93.refs_0_, bf16[384,256]{1,0:T(8,128)(2,1)S(1)} %get-tuple-element.75.refs_0_.refs_1_, ...), custom_call_target="tpu_custom_call" | custom-call | bytes 4128768 | tf_op jit(solution)/shard_map/pallas_call | solution.py:45
  39.4 2.8 %collective-permute-start.11 = (bf16[384,256]{1,0:T(8,128)(2,1)S(1)}, bf16[384,256]{1,0:T(8,128)(2,1)S(1)}, u32[]{:S(2)}, u32[]{:S(2)}) collective-permute-start(bf16[384,256]{1,0:T(8,128)(2,1)S(1)} %get-tuple-element.108), channel_id=1, source_target_pairs={{0,3},{1,2},{2,1},{3,0},{4,7},{5,6},{6,5},{7,4},{8,11},{9,10},{10,... | collective-permute-start | bytes 589832 | tf_op jit(solution)/shard_map/ppermute | solution.py:426
  42.2 1.7 %collective-permute-start.13 = (bf16[384,256]{1,0:T(8,128)(2,1)S(1)}, bf16[384,256]{1,0:T(8,128)(2,1)S(1)}, u32[]{:S(2)}, u32[]{:S(2)}) collective-permute-start(bf16[384,256]{1,0:T(8,128)(2,1)S(1)} %get-tuple-element.110), channel_id=1, source_target_pairs={{0,1},{1,0},{2,3},{3,2},{4,5},{5,4},{6,7},{7,6},{8,9},{9,8},{10,11... | collective-permute-start | bytes 589832 | tf_op jit(solution)/shard_map/ppermute | solution.py:426
  43.8 0.8 %shard_map.100 = (f32[384,1024]{1,0:T(8,128)S(1)}, bf16[384,1024]{1,0:T(8,128)(2,1)S(1)}) custom-call(bf16[768,768]{1,0:T(8,128)(2,1)S(1)} %get-tuple-element.113.weight_ref, bf16[768,1024]{1,0:T(8,128)(2,1)S(1)} %get-tuple-element.89.refs_6_.unit_ref, bf16[384,1024]{1,0:T(8,128)(2,1)S(1)} %collective-permute-done.14.add_ref), custom_call_target="tpu_custom_call" | custom-call | bytes 5898240 | tf_op jit(solution)/shard_map/pallas_call | solution.py:45
  44.6 0.8 %shard_map.101.refs_6_ = f32[384,1024]{1,0:T(8,128)S(1)} custom-call(bf16[768,384]{1,0:T(8,128)(2,1)S(1)} %get-tuple-element.95.refs_8_.weight_ref, bf16[768,1024]{1,0:T(8,128)(2,1)S(1)} %get-tuple-element.89.refs_6_.unit_ref, bf16[384,1024]{1,0:T(8,128)(2,1)S(1)} %get-tuple-element.115.add_ref), custom_call_target="tpu_custom_call" | custom-call | tf_op jit(solution)/shard_map/pallas_call | solution.py:45
  45.5 1.2 %collective-permute-done.15.in_ref = bf16[256,1024]{1,0:T(8,128)(2,1)S(1)} collective-permute-done((bf16[256,1024]{1,0:T(8,128)(2,1)S(1)}, bf16[256,1024]{1,0:T(8,128)(2,1)S(1)}, u32[]{:S(2)}, u32[]{:S(2)}) %collective-permute-start.15) | collective-permute-done | bytes 524320 | tf_op jit(solution)/shard_map/ppermute | solution.py:431
  46.7 0.1 shard_map.102
  46.8 1.6 %collective-permute-start.16 = (bf16[256,1024]{1,0:T(8,128)(2,1)S(1)}, bf16[256,1024]{1,0:T(8,128)(2,1)S(1)}, u32[]{:S(2)}, u32[]{:S(2)}) collective-permute-start(bf16[256,1024]{1,0:T(8,128)(2,1)S(1)} %shard_map.102), channel_id=1, source_target_pairs={{0,16},{4,12},{8,24},{12,4},{16,0},{20,28},{24,8},{28,20},{1,17},{... | collective-permute-start | bytes 1572872 | tf_op jit(solution)/shard_map/ppermute | solution.py:431
  48.3 1.8 %collective-permute-done.17.in_ref = bf16[128,1024]{1,0:T(8,128)(2,1)S(1)} collective-permute-done((bf16[128,1024]{1,0:T(8,128)(2,1)S(1)}, bf16[128,1024]{1,0:T(8,128)(2,1)S(1)}, u32[]{:S(2)}, u32[]{:S(2)}) %collective-permute-start.17) | collective-permute-done | bytes 262176 | tf_op jit(solution)/shard_map/ppermute | solution.py:431
  50.2 1.6 %collective-permute-start.18 = (bf16[128,1024]{1,0:T(8,128)(2,1)S(1)}, bf16[128,1024]{1,0:T(8,128)(2,1)S(1)}, u32[]{:S(2)}, u32[]{:S(2)}) collective-permute-start(bf16[128,1024]{1,0:T(8,128)(2,1)S(1)} %shard_map.103), channel_id=1, source_target_pairs={{0,16},{4,12},{8,24},{12,4},{16,0},{20,28},{24,8},{28,20},{1,17},{... | collective-permute-start | bytes 786440 | tf_op jit(solution)/shard_map/ppermute | solution.py:431
  51.8 6.6 %collective-permute-done.12.refs_1_.refs_2_ = bf16[384,256]{1,0:T(8,128)(2,1)S(1)} collective-permute-done((bf16[384,256]{1,0:T(8,128)(2,1)S(1)}, bf16[384,256]{1,0:T(8,128)(2,1)S(1)}, u32[]{:S(2)}, u32[]{:S(2)}) %collective-permute-start.12) | collective-permute-done | bytes 196640 | tf_op jit(solution)/shard_map/ppermute | solution.py:426
  58.4 0.4 collective-permute-done.18.refs_8_
  58.8 1.6 %shard_map.105 = (bf16[1536,256]{1,0:T(8,128)(2,1)}, bf16[384,1024]{1,0:T(8,128)(2,1)}) custom-call(bf16[384,256]{1,0:T(8,128)(2,1)S(1)} %get-tuple-element.107.refs_0_, bf16[384,256]{1,0:T(8,128)(2,1)S(1)} %collective-permute-done.11.refs_0_.refs_1_, bf16[384,256]{1,0:T(8,128)(2,1)S(1)} %collective-permute-done.12.refs_1_.refs_2_, ...), custom_call_target="tpu_custom_call" | custom-call | bytes 5705728 | tf_op jit(solution)/shard_map/pallas_call | solution.py:45
  (18 shorter events, 0.1 us)
Async XLA Ops:
  0.6 14.7 %collective-permute-start = (bf16[384,1024]{1,0:T(8,128)(2,1)}, bf16[384,1024]{1,0:T(8,128)(2,1)S(1)}, u32[]{:S(2)}, u32[]{:S(2)}) collective-permute-start(bf16[384,1024]{1,0:T(8,128)(2,1)} %raw_ref.1), channel_id=1, source_target_pairs={{0,16},{4,12},{8,24},{12,4},{16,0},{20,28},{24,8},{28,20},{1,17},{... | collective-permute-start | bytes 2359304 | tf_op jit(solution)/shard_map/ppermute | solution.py:431
  3.7 1.1 %copy-start = (bf16[1536,256]{1,0:T(8,128)(2,1)S(1)}, bf16[1536,256]{1,0:T(8,128)(2,1)}, u32[]{:S(2)}) copy-start(bf16[1536,256]{1,0:T(8,128)(2,1)} %text_ref.1) | copy-start | bytes 2359300
  4.8 8.8 %copy-start.1 = (s32[12288]{0:T(1024)S(1)}, s32[12288]{0:T(1024)}, u32[]{:S(2)}) copy-start(s32[12288]{0:T(1024)} %param.11) | copy-start | bytes 147460
  4.8 8.8 %copy-start.2 = (s32[12288]{0:T(1024)S(1)}, s32[12288]{0:T(1024)}, u32[]{:S(2)}) copy-start(s32[12288]{0:T(1024)} %param.12) | copy-start | bytes 147460
  4.8 8.8 %copy-start.3 = (s32[96,8,3]{0,1,2:T(8,128)S(1)}, s32[96,8,3]{0,1,2:T(8,128)}, u32[]{:S(2)}) copy-start(s32[96,8,3]{0,1,2:T(8,128)} %param.13) | copy-start | bytes 27652
  4.9 18.5 %collective-permute-start.1 = (bf16[384,256]{1,0:T(8,128)(2,1)S(1)}, bf16[384,256]{1,0:T(8,128)(2,1)S(1)}, u32[]{:S(2)}, u32[]{:S(2)}) collective-permute-start(bf16[384,256]{1,0:T(8,128)(2,1)S(1)} %get-tuple-element.76), channel_id=1, source_target_pairs={{0,3},{1,2},{2,1},{3,0},{4,7},{5,6},{6,5},{7,4},{8,11},{9,10},{10,... | collective-permute-start | bytes 589832 | tf_op jit(solution)/shard_map/ppermute | solution.py:426
  8.5 16.4 %collective-permute-start.2 = (bf16[384,256]{1,0:T(8,128)(2,1)S(1)}, bf16[384,256]{1,0:T(8,128)(2,1)S(1)}, u32[]{:S(2)}, u32[]{:S(2)}) collective-permute-start(bf16[384,256]{1,0:T(8,128)(2,1)S(1)} %get-tuple-element.77), channel_id=1, source_target_pairs={{0,2},{1,3},{2,0},{3,1},{4,6},{5,7},{6,4},{7,5},{8,10},{9,11},{10,... | collective-permute-start | bytes 589832 | tf_op jit(solution)/shard_map/ppermute | solution.py:426
  8.5 14.8 %collective-permute-start.3 = (bf16[384,256]{1,0:T(8,128)(2,1)S(1)}, bf16[384,256]{1,0:T(8,128)(2,1)S(1)}, u32[]{:S(2)}, u32[]{:S(2)}) collective-permute-start(bf16[384,256]{1,0:T(8,128)(2,1)S(1)} %get-tuple-element.78), channel_id=1, source_target_pairs={{0,1},{1,0},{2,3},{3,2},{4,5},{5,4},{6,7},{7,6},{8,9},{9,8},{10,11... | collective-permute-start | bytes 589832 | tf_op jit(solution)/shard_map/ppermute | solution.py:426
  10.7 12.3 %collective-permute-start.4 = (bf16[384,1024]{1,0:T(8,128)(2,1)}, bf16[384,1024]{1,0:T(8,128)(2,1)S(1)}, u32[]{:S(2)}, u32[]{:S(2)}) collective-permute-start(bf16[384,1024]{1,0:T(8,128)(2,1)} %raw_ref.1), channel_id=1, source_target_pairs={{0,8},{4,20},{8,0},{12,28},{16,24},{20,4},{24,16},{28,12},{1,9},{5... | collective-permute-start | bytes 2359304 | tf_op jit(solution)/shard_map/ppermute | solution.py:431
  15.3 16.5 %collective-permute-start.8 = (bf16[384,1024]{1,0:T(8,128)(2,1)S(1)}, bf16[384,1024]{1,0:T(8,128)(2,1)S(1)}, u32[]{:S(2)}, u32[]{:S(2)}) collective-permute-start(bf16[384,1024]{1,0:T(8,128)(2,1)S(1)} %collective-permute-done.raw_ref), channel_id=1, source_target_pairs={{0,8},{4,20},{8,0},{12,28},{16,24},{20,4},{24,16},{28,12},{1,9},{5... | collective-permute-start | bytes 2359304 | tf_op jit(solution)/shard_map/ppermute | solution.py:431
  25.3 2.1 %collective-permute-start.5 = (bf16[128,1024]{1,0:T(8,128)(2,1)S(1)}, bf16[128,1024]{1,0:T(8,128)(2,1)S(1)}, u32[]{:S(2)}, u32[]{:S(2)}) collective-permute-start(bf16[128,1024]{1,0:T(8,128)(2,1)S(1)} %get-tuple-element.86), channel_id=1, source_target_pairs={{0,4},{4,0},{8,12},{12,8},{16,20},{20,16},{24,28},{28,24},{1,5},{5... | collective-permute-start | bytes 786440 | tf_op jit(solution)/shard_map/ppermute | solution.py:426
  25.4 2.0 %collective-permute-start.6 = (bf16[128,1024]{1,0:T(8,128)(2,1)S(1)}, bf16[128,1024]{1,0:T(8,128)(2,1)S(1)}, u32[]{:S(2)}, u32[]{:S(2)}) collective-permute-start(bf16[128,1024]{1,0:T(8,128)(2,1)S(1)} %get-tuple-element.87), channel_id=1, source_target_pairs={{0,4},{4,0},{8,12},{12,8},{16,20},{20,16},{24,28},{28,24},{1,5},{5... | collective-permute-start | bytes 786440 | tf_op jit(solution)/shard_map/ppermute | solution.py:426
  25.9 1.8 %collective-permute-start.7 = (bf16[128,1024]{1,0:T(8,128)(2,1)S(1)}, bf16[128,1024]{1,0:T(8,128)(2,1)S(1)}, u32[]{:S(2)}, u32[]{:S(2)}) collective-permute-start(bf16[128,1024]{1,0:T(8,128)(2,1)S(1)} %get-tuple-element.88), channel_id=1, source_target_pairs={{0,4},{4,0},{8,12},{12,8},{16,20},{20,16},{24,28},{28,24},{1,5},{5... | collective-permute-start | bytes 786440 | tf_op jit(solution)/shard_map/ppermute | solution.py:426
  29.0 13.2 %collective-permute-start.14 = (bf16[384,1024]{1,0:T(8,128)(2,1)S(1)}, bf16[384,1024]{1,0:T(8,128)(2,1)S(1)}, u32[]{:S(2)}, u32[]{:S(2)}) collective-permute-start(bf16[384,1024]{1,0:T(8,128)(2,1)S(1)} %get-tuple-element.114), channel_id=1, source_target_pairs={{0,8},{4,20},{8,0},{12,28},{16,24},{20,4},{24,16},{28,12},{1,9},{5... | collective-permute-start | bytes 2359304 | tf_op jit(solution)/shard_map/ppermute | solution.py:431
  34.9 3.9 %collective-permute-start.9 = (bf16[192,1024]{1,0:T(8,128)(2,1)S(1)}, bf16[192,1024]{1,0:T(8,128)(2,1)S(1)}, u32[]{:S(2)}, u32[]{:S(2)}) collective-permute-start(bf16[192,1024]{1,0:T(8,128)(2,1)S(1)} %get-tuple-element.104), channel_id=1, source_target_pairs={{0,4},{4,0},{8,12},{12,8},{16,20},{20,16},{24,28},{28,24},{1,5},{5... | collective-permute-start | bytes 1179656 | tf_op jit(solution)/shard_map/ppermute | solution.py:426
  35.8 2.9 %collective-permute-start.10 = (bf16[192,1024]{1,0:T(8,128)(2,1)S(1)}, bf16[192,1024]{1,0:T(8,128)(2,1)S(1)}, u32[]{:S(2)}, u32[]{:S(2)}) collective-permute-start(bf16[192,1024]{1,0:T(8,128)(2,1)S(1)} %get-tuple-element.105), channel_id=1, source_target_pairs={{0,4},{4,0},{8,12},{12,8},{16,20},{20,16},{24,28},{28,24},{1,5},{5... | collective-permute-start | bytes 1179656 | tf_op jit(solution)/shard_map/ppermute | solution.py:426
  35.9 10.8 %collective-permute-start.15 = (bf16[256,1024]{1,0:T(8,128)(2,1)S(1)}, bf16[256,1024]{1,0:T(8,128)(2,1)S(1)}, u32[]{:S(2)}, u32[]{:S(2)}) collective-permute-start(bf16[256,1024]{1,0:T(8,128)(2,1)S(1)} %get-tuple-element.117), channel_id=1, source_target_pairs={{0,8},{4,20},{8,0},{12,28},{16,24},{20,4},{24,16},{28,12},{1,9},{5... | collective-permute-start | bytes 1572872 | tf_op jit(solution)/shard_map/ppermute | solution.py:431
  36.9 13.2 %collective-permute-start.17 = (bf16[128,1024]{1,0:T(8,128)(2,1)S(1)}, bf16[128,1024]{1,0:T(8,128)(2,1)S(1)}, u32[]{:S(2)}, u32[]{:S(2)}) collective-permute-start(bf16[128,1024]{1,0:T(8,128)(2,1)S(1)} %get-tuple-element.119), channel_id=1, source_target_pairs={{0,8},{4,20},{8,0},{12,28},{16,24},{20,4},{24,16},{28,12},{1,9},{5... | collective-permute-start | bytes 786440 | tf_op jit(solution)/shard_map/ppermute | solution.py:431
  39.4 12.4 %collective-permute-start.11 = (bf16[384,256]{1,0:T(8,128)(2,1)S(1)}, bf16[384,256]{1,0:T(8,128)(2,1)S(1)}, u32[]{:S(2)}, u32[]{:S(2)}) collective-permute-start(bf16[384,256]{1,0:T(8,128)(2,1)S(1)} %get-tuple-element.108), channel_id=1, source_target_pairs={{0,3},{1,2},{2,1},{3,0},{4,7},{5,6},{6,5},{7,4},{8,11},{9,10},{10,... | collective-permute-start | bytes 589832 | tf_op jit(solution)/shard_map/ppermute | solution.py:426
  42.2 16.2 %collective-permute-start.12 = (bf16[384,256]{1,0:T(8,128)(2,1)S(1)}, bf16[384,256]{1,0:T(8,128)(2,1)S(1)}, u32[]{:S(2)}, u32[]{:S(2)}) collective-permute-start(bf16[384,256]{1,0:T(8,128)(2,1)S(1)} %get-tuple-element.109), channel_id=1, source_target_pairs={{0,2},{1,3},{2,0},{3,1},{4,6},{5,7},{6,4},{7,5},{8,10},{9,11},{10,... | collective-permute-start | bytes 589832 | tf_op jit(solution)/shard_map/ppermute | solution.py:426
  42.2 16.2 %collective-permute-start.13 = (bf16[384,256]{1,0:T(8,128)(2,1)S(1)}, bf16[384,256]{1,0:T(8,128)(2,1)S(1)}, u32[]{:S(2)}, u32[]{:S(2)}) collective-permute-start(bf16[384,256]{1,0:T(8,128)(2,1)S(1)} %get-tuple-element.110), channel_id=1, source_target_pairs={{0,1},{1,0},{2,3},{3,2},{4,5},{5,4},{6,7},{7,6},{8,9},{9,8},{10,11... | collective-permute-start | bytes 589832 | tf_op jit(solution)/shard_map/ppermute | solution.py:426
  46.8 12.1 %collective-permute-start.16 = (bf16[256,1024]{1,0:T(8,128)(2,1)S(1)}, bf16[256,1024]{1,0:T(8,128)(2,1)S(1)}, u32[]{:S(2)}, u32[]{:S(2)}) collective-permute-start(bf16[256,1024]{1,0:T(8,128)(2,1)S(1)} %shard_map.102), channel_id=1, source_target_pairs={{0,16},{4,12},{8,24},{12,4},{16,0},{20,28},{24,8},{28,20},{1,17},{... | collective-permute-start | bytes 1572872 | tf_op jit(solution)/shard_map/ppermute | solution.py:431
  50.2 8.7 %collective-permute-start.18 = (bf16[128,1024]{1,0:T(8,128)(2,1)S(1)}, bf16[128,1024]{1,0:T(8,128)(2,1)S(1)}, u32[]{:S(2)}, u32[]{:S(2)}) collective-permute-start(bf16[128,1024]{1,0:T(8,128)(2,1)S(1)} %shard_map.103), channel_id=1, source_target_pairs={{0,16},{4,12},{8,24},{12,4},{16,0},{20,28},{24,8},{28,20},{1,17},{... | collective-permute-start | bytes 786440 | tf_op jit(solution)/shard_map/ppermute | solution.py:431

commit v15 on v14

--- a/solution.py
+++ b/solution.py
@@ -13,6 +13,7 @@
 WAIT_FLOPS = 20_000_000_000
 TEXT_PIECES = 3
 ACC_PIECES = 2
+STEP = 32
 CORES = 2
 EPS = 1e-06
 LOG2E = math.log2(math.e)
@@ -99,11 +100,11 @@
     piece_refs = refs[chunks + 2 :]
     place = lax.axis_index("tp")
     rows, width = chunk_refs[0].shape
-    for first in range(0, rows, TILE):
-        part = pl.ds(first, TILE)
+    for first in range(0, rows, STEP):
+        part = pl.ds(first, STEP)
         parts = [ref[part, :].astype(jnp.float32) for ref in chunk_refs]
         scales = row_scales(sum(jnp.sum(x * x, axis=-1, keepdims=True) for x in parts))
-        scale_ref[part, :] = jnp.broadcast_to(scales, (TILE, TILE))
+        scale_ref[part, :] = jnp.broadcast_to(scales, (STEP, TILE))
         for k, x in enumerate(parts):
             unit_ref[part, feature_slice(place ^ far_first(k, chunks), width)] = (x * scales).astype(jnp.bfloat16)
     split_rows(unit_ref, piece_refs)
@@ -120,14 +121,13 @@
 
 
 def unit_images(ref, image_ref, scale_ref=None):
-    step = 64
-    for first in range(0, ref.shape[0], step):
-        part = pl.ds(first, step)
+    for first in range(0, ref.shape[0], STEP):
+        part = pl.ds(first, STEP)
         values = ref[part, :].astype(jnp.float32)
         scales = row_scales(jnp.sum(values * values, axis=-1, keepdims=True))
         image_ref[part, :] = (values * scales).astype(jnp.bfloat16)
         if scale_ref is not None:
-            scale_ref[part, :] = jnp.broadcast_to(scales, (step, TILE))
+            scale_ref[part, :] = jnp.broadcast_to(scales, (STEP, TILE))
 
 
 def unit_images_body(raw_ref, out_ref):
@@ -352,14 +352,14 @@
     place = lax.axis_index("tp")
     rows, width = raw_refs[0].shape
     size = add_refs[0].shape[0]
-    for first in range(0, rows, TILE // 2):
-        part = pl.ds(first, TILE // 2)
+    for first in range(0, rows, STEP):
+        part = pl.ds(first, STEP)
         scales = scale_ref[part, :1]
         raws = [ref[part, :].astype(jnp.float32) for ref in raw_refs]
         accs = []
         for k in range(chunks):
             features = feature_slice(place ^ far_first(k, chunks), width)
-            added = add_refs[first // size][pl.ds(first % size, TILE // 2), features]
+            added = add_refs[first // size][pl.ds(first % size, STEP), features]
             accs.append(acc_ref[part, features] + added.astype(jnp.float32))
         inner = sum(jnp.sum(x * a, axis=-1, keepdims=True) for x, a in zip(raws, accs))
         inner = inner * scales * scales
@@ -373,16 +373,17 @@
 
 
 def finish_rows(start, count, raw_ref, scale_ref, sum_ref, add_ref, grad_ref, out_ref, sems, copies):
-    step = TILE // 2
-    for first in range(0, count, step):
-        part = pl.ds(start + first, step)
-        raw = raw_ref[part, :].astype(jnp.float32)
-        scales = scale_ref[part, :1]
-        acc = sum_ref[part, :]
-        if add_ref is not None:
-            acc = acc + add_ref[pl.ds(first, step), :].astype(jnp.float32)
-        inner = jnp.sum(raw * acc, axis=-1, keepdims=True) * scales * scales
-        grad_ref[part, :] = (scales * (acc - raw * inner)).astype(jnp.bfloat16)
+    for block in range(0, count, TILE // 2):
+        for first in range(block, block + TILE // 2, STEP):
+            part = pl.ds(start + first, STEP)
+            raw = raw_ref[part, :].astype(jnp.float32)
+            scales = scale_ref[part, :1]
+            acc = sum_ref[part, :]
+            if add_ref is not None:
+                acc = acc + add_ref[pl.ds(first, STEP), :].astype(jnp.float32)
+            inner = jnp.sum(raw * acc, axis=-1, keepdims=True) * scales * scales
+            grad_ref[part, :] = (scales * (acc - raw * inner)).astype(jnp.bfloat16)
+        part = pl.ds(start + block, TILE // 2)
         copies.append(
             pltpu.make_async_copy(
                 grad_ref.at[part, :], out_ref.at[part, :], sems.at[len(copies)]

time: 60.6 us -> 60.6 us (level)
  no operation moved by 1% of the time
where the time goes in v15:
time: 60.6 us; the launch traced here: 60.3 us
  starting transfers between devices  24.3 us (40%)
  waiting for transfers between devices  16.6 us (27%)
  Pallas kernels  16.2 us (27%)
  between operations  2.13 us (4%)
  local copies, waits for them, and re-layouts  1.14 us (2%)
    pallas_call x20, Pallas kernels, call_kernel(): pl.pallas_call(body, out_shape=outs, in_specs=specs, out_specs=[ANY_SPEC...  16.2 us
    ppermute x8, starting transfers between devices, swap_near(): lax.ppermute(value, 'blk', [(i, i ^ neighbour_bits(i)[which]) for i in ra...  13.7 us
    ppermute x11, starting transfers between devices, swap(): return lax.ppermute(value, axis, [(i, i ^ bits) for i in range(count)])  10.6 us
    ppermute x11, waiting for transfers between devices, swap(): return lax.ppermute(value, axis, [(i, i ^ bits) for i in range(count)])  8.47 us
    ppermute x8, waiting for transfers between devices, swap_near(): lax.ppermute(value, 'blk', [(i, i ^ neighbour_bits(i)[which]) for i in ra...  8.11 us
  transfers between devices with their start and end apart: 19, of which 8 were waited for; matrix products, arithmetic and copies ran while one was open for 0% of the time, Pallas kernels for 24%

profile of v15, /device:TPU:0, one launch (start us, length us, event | category | flops | bytes accessed | tf_op | source)
XLA Modules:
  0.0 60.3 jit_solution(8074460580632960931)
XLA Ops:
  0.6 3.0 %collective-permute-start = (bf16[384,1024]{1,0:T(8,128)(2,1)}, bf16[384,1024]{1,0:T(8,128)(2,1)S(1)}, u32[]{:S(2)}, u32[]{:S(2)}) collective-permute-start(bf16[384,1024]{1,0:T(8,128)(2,1)} %raw_ref.1), channel_id=1, source_target_pairs={{0,16},{4,12},{8,24},{12,4},{16,0},{20,28},{24,8},{28,20},{1,17},{... | collective-permute-start | bytes 2359304 | tf_op jit(solution)/shard_map/ppermute | solution.py:432
  3.7 1.1 %copy-done = bf16[1536,256]{1,0:T(8,128)(2,1)S(1)} copy-done((bf16[1536,256]{1,0:T(8,128)(2,1)S(1)}, bf16[1536,256]{1,0:T(8,128)(2,1)}, u32[]{:S(2)}) %copy-start) | copy-done | bytes 786456
  4.8 0.1 shard_map.88
  4.9 3.7 %collective-permute-start.1 = (bf16[384,256]{1,0:T(8,128)(2,1)S(1)}, bf16[384,256]{1,0:T(8,128)(2,1)S(1)}, u32[]{:S(2)}, u32[]{:S(2)}) collective-permute-start(bf16[384,256]{1,0:T(8,128)(2,1)S(1)} %get-tuple-element.76), channel_id=1, source_target_pairs={{0,3},{1,2},{2,1},{3,0},{4,7},{5,6},{6,5},{7,4},{8,11},{9,10},{10,... | collective-permute-start | bytes 589832 | tf_op jit(solution)/shard_map/ppermute | solution.py:427
  8.5 0.8 %collective-permute-start.3 = (bf16[384,256]{1,0:T(8,128)(2,1)S(1)}, bf16[384,256]{1,0:T(8,128)(2,1)S(1)}, u32[]{:S(2)}, u32[]{:S(2)}) collective-permute-start(bf16[384,256]{1,0:T(8,128)(2,1)S(1)} %get-tuple-element.78), channel_id=1, source_target_pairs={{0,1},{1,0},{2,3},{3,2},{4,5},{5,4},{6,7},{7,6},{8,9},{9,8},{10,11... | collective-permute-start | bytes 589832 | tf_op jit(solution)/shard_map/ppermute | solution.py:427
  9.3 1.4 %shard_map.86 = (bf16[384,1024]{1,0:T(8,128)(2,1)S(1)}, bf16[384,1024]{1,0:T(8,128)(2,1)S(1)}, f32[384,128]{1,0:T(8,128)S(1)}) custom-call(bf16[384,1024]{1,0:T(8,128)(2,1)} %raw_ref.1), custom_call_target="tpu_custom_call" | custom-call | bytes 2555904 | tf_op jit(solution)/shard_map/pallas_call | solution.py:46
  10.7 1.6 %collective-permute-start.4 = (bf16[384,1024]{1,0:T(8,128)(2,1)}, bf16[384,1024]{1,0:T(8,128)(2,1)S(1)}, u32[]{:S(2)}, u32[]{:S(2)}) collective-permute-start(bf16[384,1024]{1,0:T(8,128)(2,1)} %raw_ref.1), channel_id=1, source_target_pairs={{0,8},{4,20},{8,0},{12,28},{16,24},{20,4},{24,16},{28,12},{1,9},{5... | collective-permute-start | bytes 2359304 | tf_op jit(solution)/shard_map/ppermute | solution.py:432
  13.6 1.1 %shard_map.87 = (f32[2,128]{1,0:T(2,128)S(1)}, f32[72,128]{1,0:T(8,128)S(1)}, s32[12,128]{1,0:T(8,128)S(1)}, s32[768,128]{1,0:T(8,128)S(1)}, f32[384,128]{1,0:T(8,128)S(1)}, /*index=5*/f32[4,128]{1,0:T(4,128)S(1)}) custom-call(f32[1]{0:T(128)S(6)} %copy.9.refs_0_, f32[1]{0:T(128)S(6)} %copy.10.refs_1_, s32[3,8,96]{2,1,0:T(8,128)S(1)} %bitcast.5, ...), custom_call_target="tpu_custom_call" | custom-call | bytes 743432 | tf_op jit(solution)/shard_map/pallas_call | solution.py:46
  14.7 0.6 %collective-permute-done.raw_ref = bf16[384,1024]{1,0:T(8,128)(2,1)S(1)} collective-permute-done((bf16[384,1024]{1,0:T(8,128)(2,1)}, bf16[384,1024]{1,0:T(8,128)(2,1)S(1)}, u32[]{:S(2)}, u32[]{:S(2)}) %collective-permute-start) | collective-permute-done | bytes 786464 | tf_op jit(solution)/shard_map/ppermute | solution.py:432
  15.3 3.3 %collective-permute-start.8 = (bf16[384,1024]{1,0:T(8,128)(2,1)S(1)}, bf16[384,1024]{1,0:T(8,128)(2,1)S(1)}, u32[]{:S(2)}, u32[]{:S(2)}) collective-permute-start(bf16[384,1024]{1,0:T(8,128)(2,1)S(1)} %collective-permute-done.raw_ref), channel_id=1, source_target_pairs={{0,8},{4,20},{8,0},{12,28},{16,24},{20,4},{24,16},{28,12},{1,9},{5... | collective-permute-start | bytes 2359304 | tf_op jit(solution)/shard_map/ppermute | solution.py:432
  18.6 0.2 shard_map.89.second_unit_ref
  18.9 4.1 %collective-permute-done.4.first_ref = bf16[384,1024]{1,0:T(8,128)(2,1)S(1)} collective-permute-done((bf16[384,1024]{1,0:T(8,128)(2,1)}, bf16[384,1024]{1,0:T(8,128)(2,1)S(1)}, u32[]{:S(2)}, u32[]{:S(2)}) %collective-permute-start.4) | collective-permute-done | bytes 786464 | tf_op jit(solution)/shard_map/ppermute | solution.py:432
  23.0 0.3 shard_map.90.refs_7_
  23.3 0.0 collective-permute-done.1.refs_1_.refs_2_
  23.4 1.6 %collective-permute-done.2.refs_2_.refs_3_ = bf16[384,256]{1,0:T(8,128)(2,1)S(1)} collective-permute-done((bf16[384,256]{1,0:T(8,128)(2,1)S(1)}, bf16[384,256]{1,0:T(8,128)(2,1)S(1)}, u32[]{:S(2)}, u32[]{:S(2)}) %collective-permute-start.2) | collective-permute-done | bytes 196640 | tf_op jit(solution)/shard_map/ppermute | solution.py:427
  24.9 0.4 shard_map.91
  25.3 0.1 collective-permute-start.5
  25.4 0.5 collective-permute-start.6
  25.8 0.1 collective-permute-start.7
  25.9 1.4 %shard_map.92 = (bf16[384,384]{1,0:T(8,128)(2,1)S(1)}, bf16[384,768]{1,0:T(8,128)(2,1)S(1)}) custom-call(f32[2,128]{1,0:T(2,128)S(1)} %get-tuple-element.69.refs_0_, f32[72,128]{1,0:T(8,128)S(1)} %get-tuple-element.70.refs_1_, s32[12,128]{1,0:T(8,128)S(1)} %get-tuple-element.71.refs_2_, s32[768,128]{1,0:T(8,128)S(1)} %get-tuple-element.72.refs_3_, ...), custom_call_target="tpu_custom_call" | custom-call | bytes 4666368 | tf_op jit(solution)/shard_map/pallas_call | solution.py:46
  27.4 0.0 collective-permute-done.6.refs_10_
  27.4 0.2 collective-permute-done.7.refs_11_
  27.6 1.3 %shard_map.93 = (bf16[768,1024]{1,0:T(8,128)(2,1)S(1)}, bf16[768,384]{1,0:T(8,128)(2,1)S(1)}, bf16[384,1024]{1,0:T(8,128)(2,1)S(1)}) custom-call(f32[2,128]{1,0:T(2,128)S(1)} %get-tuple-element.69.refs_0_, f32[72,128]{1,0:T(8,128)S(1)} %get-tuple-element.70.refs_1_, s32[12,128]{1,0:T(8,128)S(1)} %get-tuple-element.71.refs_2_, ...), custom_call_target="tpu_custom_call" | custom-call | bytes 8107008 | tf_op jit(solution)/shard_map/pallas_call | solution.py:46
  28.9 0.6 collective-permute-start.14
  29.6 2.2 %shard_map.94 = (bf16[768,384]{1,0:T(8,128)(2,1)S(1)}, f32[768,1024]{1,0:T(8,128)S(1)}, bf16[768,768]{1,0:T(8,128)(2,1)S(1)}) custom-call(f32[2,128]{1,0:T(2,128)S(1)} %get-tuple-element.69.refs_0_, f32[72,128]{1,0:T(8,128)S(1)} %get-tuple-element.70.refs_1_, s32[12,128]{1,0:T(8,128)S(1)} %get-tuple-element.71.refs_2_, ...), custom_call_target="tpu_custom_call" | custom-call | bytes 10957824 | tf_op jit(solution)/shard_map/pallas_call | solution.py:46
  31.8 1.4 %shard_map.95 = (bf16[768,768]{1,0:T(8,128)(2,1)S(1)}, bf16[768,1024]{1,0:T(8,128)(2,1)S(1)}) custom-call(f32[2,128]{1,0:T(2,128)S(1)} %get-tuple-element.69.refs_0_, f32[72,128]{1,0:T(8,128)S(1)} %get-tuple-element.70.refs_1_, s32[12,128]{1,0:T(8,128)S(1)} %get-tuple-element.71.refs_2_, s32[768,128]{1,0:T(8,128)S(1)} %get-tuple-element.72.refs_3_, ...), custom_call_target="tpu_custom_call" | custom-call | bytes 7123968 | tf_op jit(solution)/shard_map/pallas_call | solution.py:46
  33.2 0.8 %shard_map.96 = (bf16[256,1024]{1,0:T(8,128)(2,1)S(1)}, bf16[128,1024]{1,0:T(8,128)(2,1)S(1)}) custom-call(bf16[768,768]{1,0:T(8,128)(2,1)S(1)} %get-tuple-element.97.weight_ref, bf16[768,1024]{1,0:T(8,128)(2,1)S(1)} %get-tuple-element.89.refs_6_.unit_ref), custom_call_target="tpu_custom_call" | custom-call | bytes 3538944 | tf_op jit(solution)/shard_map/pallas_call | solution.py:46
  34.0 0.8 %shard_map.97 = (bf16[192,1024]{1,0:T(8,128)(2,1)S(1)}, bf16[192,1024]{1,0:T(8,128)(2,1)S(1)}) custom-call(bf16[768,768]{1,0:T(8,128)(2,1)S(1)} %get-tuple-element.97.weight_ref, bf16[768,1024]{1,0:T(8,128)(2,1)S(1)} %get-tuple-element.103.image_ref, f32[768,1024]{1,0:T(8,128)S(1)} %get-tuple-element.101.acc_ref), custom_call_target="tpu_custom_call" | custom-call | bytes 6684672 | tf_op jit(solution)/shard_map/pallas_call | solution.py:46
  34.8 1.0 %collective-permute-start.9 = (bf16[192,1024]{1,0:T(8,128)(2,1)S(1)}, bf16[192,1024]{1,0:T(8,128)(2,1)S(1)}, u32[]{:S(2)}, u32[]{:S(2)}) collective-permute-start(bf16[192,1024]{1,0:T(8,128)(2,1)S(1)} %get-tuple-element.104), channel_id=1, source_target_pairs={{0,4},{4,0},{8,12},{12,8},{16,20},{20,16},{24,28},{28,24},{1,5},{5... | collective-permute-start | bytes 1179656 | tf_op jit(solution)/shard_map/ppermute | solution.py:427
  35.8 0.1 collective-permute-start.10
  35.9 1.0 %collective-permute-start.15 = (bf16[256,1024]{1,0:T(8,128)(2,1)S(1)}, bf16[256,1024]{1,0:T(8,128)(2,1)S(1)}, u32[]{:S(2)}, u32[]{:S(2)}) collective-permute-start(bf16[256,1024]{1,0:T(8,128)(2,1)S(1)} %get-tuple-element.117), channel_id=1, source_target_pairs={{0,8},{4,20},{8,0},{12,28},{16,24},{20,4},{24,16},{28,12},{1,9},{5... | collective-permute-start | bytes 1572872 | tf_op jit(solution)/shard_map/ppermute | solution.py:432
  36.9 1.0 %collective-permute-start.17 = (bf16[128,1024]{1,0:T(8,128)(2,1)S(1)}, bf16[128,1024]{1,0:T(8,128)(2,1)S(1)}, u32[]{:S(2)}, u32[]{:S(2)}) collective-permute-start(bf16[128,1024]{1,0:T(8,128)(2,1)S(1)} %get-tuple-element.119), channel_id=1, source_target_pairs={{0,8},{4,20},{8,0},{12,28},{16,24},{20,4},{24,16},{28,12},{1,9},{5... | collective-permute-start | bytes 786440 | tf_op jit(solution)/shard_map/ppermute | solution.py:432
  37.9 0.8 %shard_map.98.refs_5_ = f32[384,1024]{1,0:T(8,128)S(1)} custom-call(bf16[768,768]{1,0:T(8,128)(2,1)S(1)} %get-tuple-element.97.weight_ref, bf16[768,1024]{1,0:T(8,128)(2,1)S(1)} %get-tuple-element.103.image_ref, f32[768,1024]{1,0:T(8,128)S(1)} %get-tuple-element.101.acc_ref), custom_call_target="tpu_custom_call" | custom-call | bytes 7471104 | tf_op jit(solution)/shard_map/pallas_call | solution.py:46
  38.7 0.0 collective-permute-done.9.refs_6_
  38.7 0.6 %shard_map.99 = (bf16[384,256]{1,0:T(8,128)(2,1)S(1)}, bf16[384,256]{1,0:T(8,128)(2,1)S(1)}, bf16[384,256]{1,0:T(8,128)(2,1)S(1)}, bf16[384,256]{1,0:T(8,128)(2,1)S(1)}) custom-call(f32[384,128]{1,0:T(8,128)S(1)} %get-tuple-element.93.refs_0_, bf16[384,256]{1,0:T(8,128)(2,1)S(1)} %get-tuple-element.75.refs_0_.refs_1_, ...), custom_call_target="tpu_custom_call" | custom-call | bytes 4128768 | tf_op jit(solution)/shard_map/pallas_call | solution.py:46
  39.3 2.8 %collective-permute-start.11 = (bf16[384,256]{1,0:T(8,128)(2,1)S(1)}, bf16[384,256]{1,0:T(8,128)(2,1)S(1)}, u32[]{:S(2)}, u32[]{:S(2)}) collective-permute-start(bf16[384,256]{1,0:T(8,128)(2,1)S(1)} %get-tuple-element.108), channel_id=1, source_target_pairs={{0,3},{1,2},{2,1},{3,0},{4,7},{5,6},{6,5},{7,4},{8,11},{9,10},{10,... | collective-permute-start | bytes 589832 | tf_op jit(solution)/shard_map/ppermute | solution.py:427
  42.2 0.0 collective-permute-start.12
  42.2 1.6 %collective-permute-start.13 = (bf16[384,256]{1,0:T(8,128)(2,1)S(1)}, bf16[384,256]{1,0:T(8,128)(2,1)S(1)}, u32[]{:S(2)}, u32[]{:S(2)}) collective-permute-start(bf16[384,256]{1,0:T(8,128)(2,1)S(1)} %get-tuple-element.110), channel_id=1, source_target_pairs={{0,1},{1,0},{2,3},{3,2},{4,5},{5,4},{6,7},{7,6},{8,9},{9,8},{10,11... | collective-permute-start | bytes 589832 | tf_op jit(solution)/shard_map/ppermute | solution.py:427
  43.8 0.8 %shard_map.100 = (f32[384,1024]{1,0:T(8,128)S(1)}, bf16[384,1024]{1,0:T(8,128)(2,1)S(1)}) custom-call(bf16[768,768]{1,0:T(8,128)(2,1)S(1)} %get-tuple-element.113.weight_ref, bf16[768,1024]{1,0:T(8,128)(2,1)S(1)} %get-tuple-element.89.refs_6_.unit_ref, bf16[384,1024]{1,0:T(8,128)(2,1)S(1)} %collective-permute-done.14.add_ref), custom_call_target="tpu_custom_call" | custom-call | bytes 5898240 | tf_op jit(solution)/shard_map/pallas_call | solution.py:46
  44.6 0.8 %shard_map.101.refs_6_ = f32[384,1024]{1,0:T(8,128)S(1)} custom-call(bf16[768,384]{1,0:T(8,128)(2,1)S(1)} %get-tuple-element.95.refs_8_.weight_ref, bf16[768,1024]{1,0:T(8,128)(2,1)S(1)} %get-tuple-element.89.refs_6_.unit_ref, bf16[384,1024]{1,0:T(8,128)(2,1)S(1)} %get-tuple-element.115.add_ref), custom_call_target="tpu_custom_call" | custom-call | tf_op jit(solution)/shard_map/pallas_call | solution.py:46
  45.4 1.2 %collective-permute-done.15.in_ref = bf16[256,1024]{1,0:T(8,128)(2,1)S(1)} collective-permute-done((bf16[256,1024]{1,0:T(8,128)(2,1)S(1)}, bf16[256,1024]{1,0:T(8,128)(2,1)S(1)}, u32[]{:S(2)}, u32[]{:S(2)}) %collective-permute-start.15) | collective-permute-done | bytes 524320 | tf_op jit(solution)/shard_map/ppermute | solution.py:432
  46.6 0.1 shard_map.102
  46.7 1.6 %collective-permute-start.16 = (bf16[256,1024]{1,0:T(8,128)(2,1)S(1)}, bf16[256,1024]{1,0:T(8,128)(2,1)S(1)}, u32[]{:S(2)}, u32[]{:S(2)}) collective-permute-start(bf16[256,1024]{1,0:T(8,128)(2,1)S(1)} %shard_map.102), channel_id=1, source_target_pairs={{0,16},{4,12},{8,24},{12,4},{16,0},{20,28},{24,8},{28,20},{1,17},{... | collective-permute-start | bytes 1572872 | tf_op jit(solution)/shard_map/ppermute | solution.py:432
  48.3 1.8 %collective-permute-done.17.in_ref = bf16[128,1024]{1,0:T(8,128)(2,1)S(1)} collective-permute-done((bf16[128,1024]{1,0:T(8,128)(2,1)S(1)}, bf16[128,1024]{1,0:T(8,128)(2,1)S(1)}, u32[]{:S(2)}, u32[]{:S(2)}) %collective-permute-start.17) | collective-permute-done | bytes 262176 | tf_op jit(solution)/shard_map/ppermute | solution.py:432
  50.1 1.6 %collective-permute-start.18 = (bf16[128,1024]{1,0:T(8,128)(2,1)S(1)}, bf16[128,1024]{1,0:T(8,128)(2,1)S(1)}, u32[]{:S(2)}, u32[]{:S(2)}) collective-permute-start(bf16[128,1024]{1,0:T(8,128)(2,1)S(1)} %shard_map.103), channel_id=1, source_target_pairs={{0,16},{4,12},{8,24},{12,4},{16,0},{20,28},{24,8},{28,20},{1,17},{... | collective-permute-start | bytes 786440 | tf_op jit(solution)/shard_map/ppermute | solution.py:432
  51.7 6.7 %collective-permute-done.12.refs_1_.refs_2_ = bf16[384,256]{1,0:T(8,128)(2,1)S(1)} collective-permute-done((bf16[384,256]{1,0:T(8,128)(2,1)S(1)}, bf16[384,256]{1,0:T(8,128)(2,1)S(1)}, u32[]{:S(2)}, u32[]{:S(2)}) %collective-permute-start.12) | collective-permute-done | bytes 196640 | tf_op jit(solution)/shard_map/ppermute | solution.py:427
  58.4 0.4 collective-permute-done.18.refs_8_
  58.8 1.6 %shard_map.105 = (bf16[1536,256]{1,0:T(8,128)(2,1)}, bf16[384,1024]{1,0:T(8,128)(2,1)}) custom-call(bf16[384,256]{1,0:T(8,128)(2,1)S(1)} %get-tuple-element.107.refs_0_, bf16[384,256]{1,0:T(8,128)(2,1)S(1)} %collective-permute-done.11.refs_0_.refs_1_, bf16[384,256]{1,0:T(8,128)(2,1)S(1)} %collective-permute-done.12.refs_1_.refs_2_, ...), custom_call_target="tpu_custom_call" | custom-call | bytes 5705728 | tf_op jit(solution)/shard_map/pallas_call | solution.py:46
  (18 shorter events, 0.1 us)
Async XLA Ops:
  0.6 14.7 %collective-permute-start = (bf16[384,1024]{1,0:T(8,128)(2,1)}, bf16[384,1024]{1,0:T(8,128)(2,1)S(1)}, u32[]{:S(2)}, u32[]{:S(2)}) collective-permute-start(bf16[384,1024]{1,0:T(8,128)(2,1)} %raw_ref.1), channel_id=1, source_target_pairs={{0,16},{4,12},{8,24},{12,4},{16,0},{20,28},{24,8},{28,20},{1,17},{... | collective-permute-start | bytes 2359304 | tf_op jit(solution)/shard_map/ppermute | solution.py:432
  3.7 1.1 %copy-start = (bf16[1536,256]{1,0:T(8,128)(2,1)S(1)}, bf16[1536,256]{1,0:T(8,128)(2,1)}, u32[]{:S(2)}) copy-start(bf16[1536,256]{1,0:T(8,128)(2,1)} %text_ref.1) | copy-start | bytes 2359300
  4.8 8.8 %copy-start.1 = (s32[12288]{0:T(1024)S(1)}, s32[12288]{0:T(1024)}, u32[]{:S(2)}) copy-start(s32[12288]{0:T(1024)} %param.11) | copy-start | bytes 147460
  4.8 8.8 %copy-start.2 = (s32[12288]{0:T(1024)S(1)}, s32[12288]{0:T(1024)}, u32[]{:S(2)}) copy-start(s32[12288]{0:T(1024)} %param.12) | copy-start | bytes 147460
  4.8 8.8 %copy-start.3 = (s32[96,8,3]{0,1,2:T(8,128)S(1)}, s32[96,8,3]{0,1,2:T(8,128)}, u32[]{:S(2)}) copy-start(s32[96,8,3]{0,1,2:T(8,128)} %param.13) | copy-start | bytes 27652
  4.9 18.5 %collective-permute-start.1 = (bf16[384,256]{1,0:T(8,128)(2,1)S(1)}, bf16[384,256]{1,0:T(8,128)(2,1)S(1)}, u32[]{:S(2)}, u32[]{:S(2)}) collective-permute-start(bf16[384,256]{1,0:T(8,128)(2,1)S(1)} %get-tuple-element.76), channel_id=1, source_target_pairs={{0,3},{1,2},{2,1},{3,0},{4,7},{5,6},{6,5},{7,4},{8,11},{9,10},{10,... | collective-permute-start | bytes 589832 | tf_op jit(solution)/shard_map/ppermute | solution.py:427
  8.5 16.4 %collective-permute-start.2 = (bf16[384,256]{1,0:T(8,128)(2,1)S(1)}, bf16[384,256]{1,0:T(8,128)(2,1)S(1)}, u32[]{:S(2)}, u32[]{:S(2)}) collective-permute-start(bf16[384,256]{1,0:T(8,128)(2,1)S(1)} %get-tuple-element.77), channel_id=1, source_target_pairs={{0,2},{1,3},{2,0},{3,1},{4,6},{5,7},{6,4},{7,5},{8,10},{9,11},{10,... | collective-permute-start | bytes 589832 | tf_op jit(solution)/shard_map/ppermute | solution.py:427
  8.5 14.8 %collective-permute-start.3 = (bf16[384,256]{1,0:T(8,128)(2,1)S(1)}, bf16[384,256]{1,0:T(8,128)(2,1)S(1)}, u32[]{:S(2)}, u32[]{:S(2)}) collective-permute-start(bf16[384,256]{1,0:T(8,128)(2,1)S(1)} %get-tuple-element.78), channel_id=1, source_target_pairs={{0,1},{1,0},{2,3},{3,2},{4,5},{5,4},{6,7},{7,6},{8,9},{9,8},{10,11... | collective-permute-start | bytes 589832 | tf_op jit(solution)/shard_map/ppermute | solution.py:427
  10.7 12.3 %collective-permute-start.4 = (bf16[384,1024]{1,0:T(8,128)(2,1)}, bf16[384,1024]{1,0:T(8,128)(2,1)S(1)}, u32[]{:S(2)}, u32[]{:S(2)}) collective-permute-start(bf16[384,1024]{1,0:T(8,128)(2,1)} %raw_ref.1), channel_id=1, source_target_pairs={{0,8},{4,20},{8,0},{12,28},{16,24},{20,4},{24,16},{28,12},{1,9},{5... | collective-permute-start | bytes 2359304 | tf_op jit(solution)/shard_map/ppermute | solution.py:432
  15.3 16.4 %collective-permute-start.8 = (bf16[384,1024]{1,0:T(8,128)(2,1)S(1)}, bf16[384,1024]{1,0:T(8,128)(2,1)S(1)}, u32[]{:S(2)}, u32[]{:S(2)}) collective-permute-start(bf16[384,1024]{1,0:T(8,128)(2,1)S(1)} %collective-permute-done.raw_ref), channel_id=1, source_target_pairs={{0,8},{4,20},{8,0},{12,28},{16,24},{20,4},{24,16},{28,12},{1,9},{5... | collective-permute-start | bytes 2359304 | tf_op jit(solution)/shard_map/ppermute | solution.py:432
  25.3 2.1 %collective-permute-start.5 = (bf16[128,1024]{1,0:T(8,128)(2,1)S(1)}, bf16[128,1024]{1,0:T(8,128)(2,1)S(1)}, u32[]{:S(2)}, u32[]{:S(2)}) collective-permute-start(bf16[128,1024]{1,0:T(8,128)(2,1)S(1)} %get-tuple-element.86), channel_id=1, source_target_pairs={{0,4},{4,0},{8,12},{12,8},{16,20},{20,16},{24,28},{28,24},{1,5},{5... | collective-permute-start | bytes 786440 | tf_op jit(solution)/shard_map/ppermute | solution.py:427
  25.4 2.0 %collective-permute-start.6 = (bf16[128,1024]{1,0:T(8,128)(2,1)S(1)}, bf16[128,1024]{1,0:T(8,128)(2,1)S(1)}, u32[]{:S(2)}, u32[]{:S(2)}) collective-permute-start(bf16[128,1024]{1,0:T(8,128)(2,1)S(1)} %get-tuple-element.87), channel_id=1, source_target_pairs={{0,4},{4,0},{8,12},{12,8},{16,20},{20,16},{24,28},{28,24},{1,5},{5... | collective-permute-start | bytes 786440 | tf_op jit(solution)/shard_map/ppermute | solution.py:427
  25.8 1.8 %collective-permute-start.7 = (bf16[128,1024]{1,0:T(8,128)(2,1)S(1)}, bf16[128,1024]{1,0:T(8,128)(2,1)S(1)}, u32[]{:S(2)}, u32[]{:S(2)}) collective-permute-start(bf16[128,1024]{1,0:T(8,128)(2,1)S(1)} %get-tuple-element.88), channel_id=1, source_target_pairs={{0,4},{4,0},{8,12},{12,8},{16,20},{20,16},{24,28},{28,24},{1,5},{5... | collective-permute-start | bytes 786440 | tf_op jit(solution)/shard_map/ppermute | solution.py:427
  28.9 13.2 %collective-permute-start.14 = (bf16[384,1024]{1,0:T(8,128)(2,1)S(1)}, bf16[384,1024]{1,0:T(8,128)(2,1)S(1)}, u32[]{:S(2)}, u32[]{:S(2)}) collective-permute-start(bf16[384,1024]{1,0:T(8,128)(2,1)S(1)} %get-tuple-element.114), channel_id=1, source_target_pairs={{0,8},{4,20},{8,0},{12,28},{16,24},{20,4},{24,16},{28,12},{1,9},{5... | collective-permute-start | bytes 2359304 | tf_op jit(solution)/shard_map/ppermute | solution.py:432
  34.8 3.9 %collective-permute-start.9 = (bf16[192,1024]{1,0:T(8,128)(2,1)S(1)}, bf16[192,1024]{1,0:T(8,128)(2,1)S(1)}, u32[]{:S(2)}, u32[]{:S(2)}) collective-permute-start(bf16[192,1024]{1,0:T(8,128)(2,1)S(1)} %get-tuple-element.104), channel_id=1, source_target_pairs={{0,4},{4,0},{8,12},{12,8},{16,20},{20,16},{24,28},{28,24},{1,5},{5... | collective-permute-start | bytes 1179656 | tf_op jit(solution)/shard_map/ppermute | solution.py:427
  35.8 2.9 %collective-permute-start.10 = (bf16[192,1024]{1,0:T(8,128)(2,1)S(1)}, bf16[192,1024]{1,0:T(8,128)(2,1)S(1)}, u32[]{:S(2)}, u32[]{:S(2)}) collective-permute-start(bf16[192,1024]{1,0:T(8,128)(2,1)S(1)} %get-tuple-element.105), channel_id=1, source_target_pairs={{0,4},{4,0},{8,12},{12,8},{16,20},{20,16},{24,28},{28,24},{1,5},{5... | collective-permute-start | bytes 1179656 | tf_op jit(solution)/shard_map/ppermute | solution.py:427
  35.9 10.8 %collective-permute-start.15 = (bf16[256,1024]{1,0:T(8,128)(2,1)S(1)}, bf16[256,1024]{1,0:T(8,128)(2,1)S(1)}, u32[]{:S(2)}, u32[]{:S(2)}) collective-permute-start(bf16[256,1024]{1,0:T(8,128)(2,1)S(1)} %get-tuple-element.117), channel_id=1, source_target_pairs={{0,8},{4,20},{8,0},{12,28},{16,24},{20,4},{24,16},{28,12},{1,9},{5... | collective-permute-start | bytes 1572872 | tf_op jit(solution)/shard_map/ppermute | solution.py:432
  36.9 13.2 %collective-permute-start.17 = (bf16[128,1024]{1,0:T(8,128)(2,1)S(1)}, bf16[128,1024]{1,0:T(8,128)(2,1)S(1)}, u32[]{:S(2)}, u32[]{:S(2)}) collective-permute-start(bf16[128,1024]{1,0:T(8,128)(2,1)S(1)} %get-tuple-element.119), channel_id=1, source_target_pairs={{0,8},{4,20},{8,0},{12,28},{16,24},{20,4},{24,16},{28,12},{1,9},{5... | collective-permute-start | bytes 786440 | tf_op jit(solution)/shard_map/ppermute | solution.py:432
  39.3 12.4 %collective-permute-start.11 = (bf16[384,256]{1,0:T(8,128)(2,1)S(1)}, bf16[384,256]{1,0:T(8,128)(2,1)S(1)}, u32[]{:S(2)}, u32[]{:S(2)}) collective-permute-start(bf16[384,256]{1,0:T(8,128)(2,1)S(1)} %get-tuple-element.108), channel_id=1, source_target_pairs={{0,3},{1,2},{2,1},{3,0},{4,7},{5,6},{6,5},{7,4},{8,11},{9,10},{10,... | collective-permute-start | bytes 589832 | tf_op jit(solution)/shard_map/ppermute | solution.py:427
  42.2 16.2 %collective-permute-start.12 = (bf16[384,256]{1,0:T(8,128)(2,1)S(1)}, bf16[384,256]{1,0:T(8,128)(2,1)S(1)}, u32[]{:S(2)}, u32[]{:S(2)}) collective-permute-start(bf16[384,256]{1,0:T(8,128)(2,1)S(1)} %get-tuple-element.109), channel_id=1, source_target_pairs={{0,2},{1,3},{2,0},{3,1},{4,6},{5,7},{6,4},{7,5},{8,10},{9,11},{10,... | collective-permute-start | bytes 589832 | tf_op jit(solution)/shard_map/ppermute | solution.py:427
  42.2 16.2 %collective-permute-start.13 = (bf16[384,256]{1,0:T(8,128)(2,1)S(1)}, bf16[384,256]{1,0:T(8,128)(2,1)S(1)}, u32[]{:S(2)}, u32[]{:S(2)}) collective-permute-start(bf16[384,256]{1,0:T(8,128)(2,1)S(1)} %get-tuple-element.110), channel_id=1, source_target_pairs={{0,1},{1,0},{2,3},{3,2},{4,5},{5,4},{6,7},{7,6},{8,9},{9,8},{10,11... | collective-permute-start | bytes 589832 | tf_op jit(solution)/shard_map/ppermute | solution.py:427
  46.7 12.1 %collective-permute-start.16 = (bf16[256,1024]{1,0:T(8,128)(2,1)S(1)}, bf16[256,1024]{1,0:T(8,128)(2,1)S(1)}, u32[]{:S(2)}, u32[]{:S(2)}) collective-permute-start(bf16[256,1024]{1,0:T(8,128)(2,1)S(1)} %shard_map.102), channel_id=1, source_target_pairs={{0,16},{4,12},{8,24},{12,4},{16,0},{20,28},{24,8},{28,20},{1,17},{... | collective-permute-start | bytes 1572872 | tf_op jit(solution)/shard_map/ppermute | solution.py:432
  50.1 8.7 %collective-permute-start.18 = (bf16[128,1024]{1,0:T(8,128)(2,1)S(1)}, bf16[128,1024]{1,0:T(8,128)(2,1)S(1)}, u32[]{:S(2)}, u32[]{:S(2)}) collective-permute-start(bf16[128,1024]{1,0:T(8,128)(2,1)S(1)} %shard_map.103), channel_id=1, source_target_pairs={{0,16},{4,12},{8,24},{12,4},{16,0},{20,28},{24,8},{28,20},{1,17},{... | collective-permute-start | bytes 786440 | tf_op jit(solution)/shard_map/ppermute | solution.py:432

commit v16 on v15

--- a/solution.py
+++ b/solution.py
@@ -372,24 +372,16 @@
     out_ref[...] = sum(ref[: out_ref.shape[0], : out_ref.shape[1]] for ref in refs[:-1])
 
 
-def finish_rows(start, count, raw_ref, scale_ref, sum_ref, add_ref, grad_ref, out_ref, sems, copies):
-    for block in range(0, count, TILE // 2):
-        for first in range(block, block + TILE // 2, STEP):
-            part = pl.ds(start + first, STEP)
-            raw = raw_ref[part, :].astype(jnp.float32)
-            scales = scale_ref[part, :1]
-            acc = sum_ref[part, :]
-            if add_ref is not None:
-                acc = acc + add_ref[pl.ds(first, STEP), :].astype(jnp.float32)
-            inner = jnp.sum(raw * acc, axis=-1, keepdims=True) * scales * scales
-            grad_ref[part, :] = (scales * (acc - raw * inner)).astype(jnp.bfloat16)
-        part = pl.ds(start + block, TILE // 2)
-        copies.append(
-            pltpu.make_async_copy(
-                grad_ref.at[part, :], out_ref.at[part, :], sems.at[len(copies)]
-            )
-        )
-        copies[-1].start()
+def finish_rows(start, count, raw_ref, scale_ref, sum_ref, add_ref, grad_ref):
+    for first in range(0, count, STEP):
+        part = pl.ds(start + first, STEP)
+        raw = raw_ref[part, :].astype(jnp.float32)
+        scales = scale_ref[part, :1]
+        acc = sum_ref[part, :]
+        if add_ref is not None:
+            acc = acc + add_ref[pl.ds(first, STEP), :].astype(jnp.float32)
+        inner = jnp.sum(raw * acc, axis=-1, keepdims=True) * scales * scales
+        grad_ref[part, :] = (scales * (acc - raw * inner)).astype(jnp.bfloat16)
 
 
 def finish_body(chunks, adds, *refs):
@@ -414,9 +406,14 @@
     start = 0
     for add_ref in add_refs or [None]:
         count = rows if add_ref is None else add_ref.shape[0]
-        finish_rows(
-            start, count, raw_ref, scale_ref, sum_ref, add_ref, grad_ref, image_ref, sems, copies
-        )
+        finish_rows(start, count, raw_ref, scale_ref, sum_ref, add_ref, grad_ref)
+        part = pl.ds(start, count)
+        copies.append(
+            pltpu.make_async_copy(
+                grad_ref.at[part, :], image_ref.at[part, :], sems.at[len(copies)]
+            )
+        )
+        copies[-1].start()
         start += count
     for copy in copies:
         copy.wait()

time: 60.6 us -> 60.7 us (level)
  no operation moved by 1% of the time
where the time goes in v16:
time: 60.7 us; the launch traced here: 60.5 us
  starting transfers between devices  24.3 us (40%)
  waiting for transfers between devices  16.6 us (27%)
  Pallas kernels  16.3 us (27%)
  between operations  2.13 us (4%)
  local copies, waits for them, and re-layouts  1.14 us (2%)
    pallas_call x20, Pallas kernels, call_kernel(): pl.pallas_call(body, out_shape=outs, in_specs=specs, out_specs=[ANY_SPEC...  16.3 us
    ppermute x8, starting transfers between devices, swap_near(): lax.ppermute(value, 'blk', [(i, i ^ neighbour_bits(i)[which]) for i in ra...  13.7 us
    ppermute x11, starting transfers between devices, swap(): return lax.ppermute(value, axis, [(i, i ^ bits) for i in range(count)])  10.6 us
    ppermute x11, waiting for transfers between devices, swap(): return lax.ppermute(value, axis, [(i, i ^ bits) for i in range(count)])  8.47 us
    ppermute x8, waiting for transfers between devices, swap_near(): lax.ppermute(value, 'blk', [(i, i ^ neighbour_bits(i)[which]) for i in ra...  8.11 us
  transfers between devices with their start and end apart: 19, of which 8 were waited for; matrix products, arithmetic and copies ran while one was open for 0% of the time, Pallas kernels for 24%

profile of v16, /device:TPU:0, one launch (start us, length us, event | category | flops | bytes accessed | tf_op | source)
XLA Modules:
  0.0 60.5 jit_solution(12695349608043627080)
XLA Ops:
  0.6 3.0 %collective-permute-start = (bf16[384,1024]{1,0:T(8,128)(2,1)}, bf16[384,1024]{1,0:T(8,128)(2,1)S(1)}, u32[]{:S(2)}, u32[]{:S(2)}) collective-permute-start(bf16[384,1024]{1,0:T(8,128)(2,1)} %raw_ref.1), channel_id=1, source_target_pairs={{0,16},{4,12},{8,24},{12,4},{16,0},{20,28},{24,8},{28,20},{1,17},{... | collective-permute-start | bytes 2359304 | tf_op jit(solution)/shard_map/ppermute | solution.py:429
  3.7 1.1 %copy-done = bf16[1536,256]{1,0:T(8,128)(2,1)S(1)} copy-done((bf16[1536,256]{1,0:T(8,128)(2,1)S(1)}, bf16[1536,256]{1,0:T(8,128)(2,1)}, u32[]{:S(2)}) %copy-start) | copy-done | bytes 786456
  4.8 0.1 shard_map.88
  4.9 3.7 %collective-permute-start.1 = (bf16[384,256]{1,0:T(8,128)(2,1)S(1)}, bf16[384,256]{1,0:T(8,128)(2,1)S(1)}, u32[]{:S(2)}, u32[]{:S(2)}) collective-permute-start(bf16[384,256]{1,0:T(8,128)(2,1)S(1)} %get-tuple-element.76), channel_id=1, source_target_pairs={{0,3},{1,2},{2,1},{3,0},{4,7},{5,6},{6,5},{7,4},{8,11},{9,10},{10,... | collective-permute-start | bytes 589832 | tf_op jit(solution)/shard_map/ppermute | solution.py:424
  8.5 0.8 %collective-permute-start.3 = (bf16[384,256]{1,0:T(8,128)(2,1)S(1)}, bf16[384,256]{1,0:T(8,128)(2,1)S(1)}, u32[]{:S(2)}, u32[]{:S(2)}) collective-permute-start(bf16[384,256]{1,0:T(8,128)(2,1)S(1)} %get-tuple-element.78), channel_id=1, source_target_pairs={{0,1},{1,0},{2,3},{3,2},{4,5},{5,4},{6,7},{7,6},{8,9},{9,8},{10,11... | collective-permute-start | bytes 589832 | tf_op jit(solution)/shard_map/ppermute | solution.py:424
  9.3 1.4 %shard_map.86 = (bf16[384,1024]{1,0:T(8,128)(2,1)S(1)}, bf16[384,1024]{1,0:T(8,128)(2,1)S(1)}, f32[384,128]{1,0:T(8,128)S(1)}) custom-call(bf16[384,1024]{1,0:T(8,128)(2,1)} %raw_ref.1), custom_call_target="tpu_custom_call" | custom-call | bytes 2555904 | tf_op jit(solution)/shard_map/pallas_call | solution.py:46
  10.7 1.6 %collective-permute-start.4 = (bf16[384,1024]{1,0:T(8,128)(2,1)}, bf16[384,1024]{1,0:T(8,128)(2,1)S(1)}, u32[]{:S(2)}, u32[]{:S(2)}) collective-permute-start(bf16[384,1024]{1,0:T(8,128)(2,1)} %raw_ref.1), channel_id=1, source_target_pairs={{0,8},{4,20},{8,0},{12,28},{16,24},{20,4},{24,16},{28,12},{1,9},{5... | collective-permute-start | bytes 2359304 | tf_op jit(solution)/shard_map/ppermute | solution.py:429
  13.6 1.1 %shard_map.87 = (f32[2,128]{1,0:T(2,128)S(1)}, f32[72,128]{1,0:T(8,128)S(1)}, s32[12,128]{1,0:T(8,128)S(1)}, s32[768,128]{1,0:T(8,128)S(1)}, f32[384,128]{1,0:T(8,128)S(1)}, /*index=5*/f32[4,128]{1,0:T(4,128)S(1)}) custom-call(f32[1]{0:T(128)S(6)} %copy.9.refs_0_, f32[1]{0:T(128)S(6)} %copy.10.refs_1_, s32[3,8,96]{2,1,0:T(8,128)S(1)} %bitcast.5, ...), custom_call_target="tpu_custom_call" | custom-call | bytes 743432 | tf_op jit(solution)/shard_map/pallas_call | solution.py:46
  14.7 0.6 %collective-permute-done.raw_ref = bf16[384,1024]{1,0:T(8,128)(2,1)S(1)} collective-permute-done((bf16[384,1024]{1,0:T(8,128)(2,1)}, bf16[384,1024]{1,0:T(8,128)(2,1)S(1)}, u32[]{:S(2)}, u32[]{:S(2)}) %collective-permute-start) | collective-permute-done | bytes 786464 | tf_op jit(solution)/shard_map/ppermute | solution.py:429
  15.3 3.3 %collective-permute-start.8 = (bf16[384,1024]{1,0:T(8,128)(2,1)S(1)}, bf16[384,1024]{1,0:T(8,128)(2,1)S(1)}, u32[]{:S(2)}, u32[]{:S(2)}) collective-permute-start(bf16[384,1024]{1,0:T(8,128)(2,1)S(1)} %collective-permute-done.raw_ref), channel_id=1, source_target_pairs={{0,8},{4,20},{8,0},{12,28},{16,24},{20,4},{24,16},{28,12},{1,9},{5... | collective-permute-start | bytes 2359304 | tf_op jit(solution)/shard_map/ppermute | solution.py:429
  18.6 0.2 shard_map.89.second_unit_ref
  18.9 4.1 %collective-permute-done.4.first_ref = bf16[384,1024]{1,0:T(8,128)(2,1)S(1)} collective-permute-done((bf16[384,1024]{1,0:T(8,128)(2,1)}, bf16[384,1024]{1,0:T(8,128)(2,1)S(1)}, u32[]{:S(2)}, u32[]{:S(2)}) %collective-permute-start.4) | collective-permute-done | bytes 786464 | tf_op jit(solution)/shard_map/ppermute | solution.py:429
  23.0 0.3 shard_map.90.refs_7_
  23.3 0.0 collective-permute-done.1.refs_1_.refs_2_
  23.4 1.6 %collective-permute-done.2.refs_2_.refs_3_ = bf16[384,256]{1,0:T(8,128)(2,1)S(1)} collective-permute-done((bf16[384,256]{1,0:T(8,128)(2,1)S(1)}, bf16[384,256]{1,0:T(8,128)(2,1)S(1)}, u32[]{:S(2)}, u32[]{:S(2)}) %collective-permute-start.2) | collective-permute-done | bytes 196640 | tf_op jit(solution)/shard_map/ppermute | solution.py:424
  24.9 0.4 shard_map.91
  25.3 0.1 collective-permute-start.5
  25.4 0.5 collective-permute-start.6
  25.8 0.1 collective-permute-start.7
  25.9 1.4 %shard_map.92 = (bf16[384,384]{1,0:T(8,128)(2,1)S(1)}, bf16[384,768]{1,0:T(8,128)(2,1)S(1)}) custom-call(f32[2,128]{1,0:T(2,128)S(1)} %get-tuple-element.69.refs_0_, f32[72,128]{1,0:T(8,128)S(1)} %get-tuple-element.70.refs_1_, s32[12,128]{1,0:T(8,128)S(1)} %get-tuple-element.71.refs_2_, s32[768,128]{1,0:T(8,128)S(1)} %get-tuple-element.72.refs_3_, ...), custom_call_target="tpu_custom_call" | custom-call | bytes 4666368 | tf_op jit(solution)/shard_map/pallas_call | solution.py:46
  27.4 0.0 collective-permute-done.6.refs_10_
  27.4 0.2 collective-permute-done.7.refs_11_
  27.6 1.3 %shard_map.93 = (bf16[768,1024]{1,0:T(8,128)(2,1)S(1)}, bf16[768,384]{1,0:T(8,128)(2,1)S(1)}, bf16[384,1024]{1,0:T(8,128)(2,1)S(1)}) custom-call(f32[2,128]{1,0:T(2,128)S(1)} %get-tuple-element.69.refs_0_, f32[72,128]{1,0:T(8,128)S(1)} %get-tuple-element.70.refs_1_, s32[12,128]{1,0:T(8,128)S(1)} %get-tuple-element.71.refs_2_, ...), custom_call_target="tpu_custom_call" | custom-call | bytes 8107008 | tf_op jit(solution)/shard_map/pallas_call | solution.py:46
  28.9 0.6 collective-permute-start.14
  29.6 2.2 %shard_map.94 = (bf16[768,384]{1,0:T(8,128)(2,1)S(1)}, f32[768,1024]{1,0:T(8,128)S(1)}, bf16[768,768]{1,0:T(8,128)(2,1)S(1)}) custom-call(f32[2,128]{1,0:T(2,128)S(1)} %get-tuple-element.69.refs_0_, f32[72,128]{1,0:T(8,128)S(1)} %get-tuple-element.70.refs_1_, s32[12,128]{1,0:T(8,128)S(1)} %get-tuple-element.71.refs_2_, ...), custom_call_target="tpu_custom_call" | custom-call | bytes 10957824 | tf_op jit(solution)/shard_map/pallas_call | solution.py:46
  31.8 1.4 %shard_map.95 = (bf16[768,768]{1,0:T(8,128)(2,1)S(1)}, bf16[768,1024]{1,0:T(8,128)(2,1)S(1)}) custom-call(f32[2,128]{1,0:T(2,128)S(1)} %get-tuple-element.69.refs_0_, f32[72,128]{1,0:T(8,128)S(1)} %get-tuple-element.70.refs_1_, s32[12,128]{1,0:T(8,128)S(1)} %get-tuple-element.71.refs_2_, s32[768,128]{1,0:T(8,128)S(1)} %get-tuple-element.72.refs_3_, ...), custom_call_target="tpu_custom_call" | custom-call | bytes 7123968 | tf_op jit(solution)/shard_map/pallas_call | solution.py:46
  33.2 0.8 %shard_map.96 = (bf16[256,1024]{1,0:T(8,128)(2,1)S(1)}, bf16[128,1024]{1,0:T(8,128)(2,1)S(1)}) custom-call(bf16[768,768]{1,0:T(8,128)(2,1)S(1)} %get-tuple-element.97.weight_ref, bf16[768,1024]{1,0:T(8,128)(2,1)S(1)} %get-tuple-element.89.refs_6_.unit_ref), custom_call_target="tpu_custom_call" | custom-call | bytes 3538944 | tf_op jit(solution)/shard_map/pallas_call | solution.py:46
  34.0 0.8 %shard_map.97 = (bf16[192,1024]{1,0:T(8,128)(2,1)S(1)}, bf16[192,1024]{1,0:T(8,128)(2,1)S(1)}) custom-call(bf16[768,768]{1,0:T(8,128)(2,1)S(1)} %get-tuple-element.97.weight_ref, bf16[768,1024]{1,0:T(8,128)(2,1)S(1)} %get-tuple-element.103.image_ref, f32[768,1024]{1,0:T(8,128)S(1)} %get-tuple-element.101.acc_ref), custom_call_target="tpu_custom_call" | custom-call | bytes 6684672 | tf_op jit(solution)/shard_map/pallas_call | solution.py:46
  34.8 1.0 %collective-permute-start.9 = (bf16[192,1024]{1,0:T(8,128)(2,1)S(1)}, bf16[192,1024]{1,0:T(8,128)(2,1)S(1)}, u32[]{:S(2)}, u32[]{:S(2)}) collective-permute-start(bf16[192,1024]{1,0:T(8,128)(2,1)S(1)} %get-tuple-element.104), channel_id=1, source_target_pairs={{0,4},{4,0},{8,12},{12,8},{16,20},{20,16},{24,28},{28,24},{1,5},{5... | collective-permute-start | bytes 1179656 | tf_op jit(solution)/shard_map/ppermute | solution.py:424
  35.8 0.1 collective-permute-start.10
  35.9 1.0 %collective-permute-start.15 = (bf16[256,1024]{1,0:T(8,128)(2,1)S(1)}, bf16[256,1024]{1,0:T(8,128)(2,1)S(1)}, u32[]{:S(2)}, u32[]{:S(2)}) collective-permute-start(bf16[256,1024]{1,0:T(8,128)(2,1)S(1)} %get-tuple-element.117), channel_id=1, source_target_pairs={{0,8},{4,20},{8,0},{12,28},{16,24},{20,4},{24,16},{28,12},{1,9},{5... | collective-permute-start | bytes 1572872 | tf_op jit(solution)/shard_map/ppermute | solution.py:429
  36.9 1.0 %collective-permute-start.17 = (bf16[128,1024]{1,0:T(8,128)(2,1)S(1)}, bf16[128,1024]{1,0:T(8,128)(2,1)S(1)}, u32[]{:S(2)}, u32[]{:S(2)}) collective-permute-start(bf16[128,1024]{1,0:T(8,128)(2,1)S(1)} %get-tuple-element.119), channel_id=1, source_target_pairs={{0,8},{4,20},{8,0},{12,28},{16,24},{20,4},{24,16},{28,12},{1,9},{5... | collective-permute-start | bytes 786440 | tf_op jit(solution)/shard_map/ppermute | solution.py:429
  37.9 0.8 %shard_map.98.refs_5_ = f32[384,1024]{1,0:T(8,128)S(1)} custom-call(bf16[768,768]{1,0:T(8,128)(2,1)S(1)} %get-tuple-element.97.weight_ref, bf16[768,1024]{1,0:T(8,128)(2,1)S(1)} %get-tuple-element.103.image_ref, f32[768,1024]{1,0:T(8,128)S(1)} %get-tuple-element.101.acc_ref), custom_call_target="tpu_custom_call" | custom-call | bytes 7471104 | tf_op jit(solution)/shard_map/pallas_call | solution.py:46
  38.7 0.0 collective-permute-done.9.refs_6_
  38.7 0.6 %shard_map.99 = (bf16[384,256]{1,0:T(8,128)(2,1)S(1)}, bf16[384,256]{1,0:T(8,128)(2,1)S(1)}, bf16[384,256]{1,0:T(8,128)(2,1)S(1)}, bf16[384,256]{1,0:T(8,128)(2,1)S(1)}) custom-call(f32[384,128]{1,0:T(8,128)S(1)} %get-tuple-element.93.refs_0_, bf16[384,256]{1,0:T(8,128)(2,1)S(1)} %get-tuple-element.75.refs_0_.refs_1_, ...), custom_call_target="tpu_custom_call" | custom-call | bytes 4128768 | tf_op jit(solution)/shard_map/pallas_call | solution.py:46
  39.3 2.8 %collective-permute-start.11 = (bf16[384,256]{1,0:T(8,128)(2,1)S(1)}, bf16[384,256]{1,0:T(8,128)(2,1)S(1)}, u32[]{:S(2)}, u32[]{:S(2)}) collective-permute-start(bf16[384,256]{1,0:T(8,128)(2,1)S(1)} %get-tuple-element.108), channel_id=1, source_target_pairs={{0,3},{1,2},{2,1},{3,0},{4,7},{5,6},{6,5},{7,4},{8,11},{9,10},{10,... | collective-permute-start | bytes 589832 | tf_op jit(solution)/shard_map/ppermute | solution.py:424
  42.2 0.0 collective-permute-start.12
  42.2 1.6 %collective-permute-start.13 = (bf16[384,256]{1,0:T(8,128)(2,1)S(1)}, bf16[384,256]{1,0:T(8,128)(2,1)S(1)}, u32[]{:S(2)}, u32[]{:S(2)}) collective-permute-start(bf16[384,256]{1,0:T(8,128)(2,1)S(1)} %get-tuple-element.110), channel_id=1, source_target_pairs={{0,1},{1,0},{2,3},{3,2},{4,5},{5,4},{6,7},{7,6},{8,9},{9,8},{10,11... | collective-permute-start | bytes 589832 | tf_op jit(solution)/shard_map/ppermute | solution.py:424
  43.8 0.8 %shard_map.100 = (f32[384,1024]{1,0:T(8,128)S(1)}, bf16[384,1024]{1,0:T(8,128)(2,1)S(1)}) custom-call(bf16[768,768]{1,0:T(8,128)(2,1)S(1)} %get-tuple-element.113.weight_ref, bf16[768,1024]{1,0:T(8,128)(2,1)S(1)} %get-tuple-element.89.refs_6_.unit_ref, bf16[384,1024]{1,0:T(8,128)(2,1)S(1)} %collective-permute-done.14.add_ref), custom_call_target="tpu_custom_call" | custom-call | bytes 5898240 | tf_op jit(solution)/shard_map/pallas_call | solution.py:46
  44.6 0.8 %shard_map.101.refs_6_ = f32[384,1024]{1,0:T(8,128)S(1)} custom-call(bf16[768,384]{1,0:T(8,128)(2,1)S(1)} %get-tuple-element.95.refs_8_.weight_ref, bf16[768,1024]{1,0:T(8,128)(2,1)S(1)} %get-tuple-element.89.refs_6_.unit_ref, bf16[384,1024]{1,0:T(8,128)(2,1)S(1)} %get-tuple-element.115.add_ref), custom_call_target="tpu_custom_call" | custom-call | tf_op jit(solution)/shard_map/pallas_call | solution.py:46
  45.4 1.2 %collective-permute-done.15.in_ref = bf16[256,1024]{1,0:T(8,128)(2,1)S(1)} collective-permute-done((bf16[256,1024]{1,0:T(8,128)(2,1)S(1)}, bf16[256,1024]{1,0:T(8,128)(2,1)S(1)}, u32[]{:S(2)}, u32[]{:S(2)}) %collective-permute-start.15) | collective-permute-done | bytes 524320 | tf_op jit(solution)/shard_map/ppermute | solution.py:429
  46.6 0.1 shard_map.102
  46.7 1.6 %collective-permute-start.16 = (bf16[256,1024]{1,0:T(8,128)(2,1)S(1)}, bf16[256,1024]{1,0:T(8,128)(2,1)S(1)}, u32[]{:S(2)}, u32[]{:S(2)}) collective-permute-start(bf16[256,1024]{1,0:T(8,128)(2,1)S(1)} %shard_map.102), channel_id=1, source_target_pairs={{0,16},{4,12},{8,24},{12,4},{16,0},{20,28},{24,8},{28,20},{1,17},{... | collective-permute-start | bytes 1572872 | tf_op jit(solution)/shard_map/ppermute | solution.py:429
  48.3 1.8 %collective-permute-done.17.in_ref = bf16[128,1024]{1,0:T(8,128)(2,1)S(1)} collective-permute-done((bf16[128,1024]{1,0:T(8,128)(2,1)S(1)}, bf16[128,1024]{1,0:T(8,128)(2,1)S(1)}, u32[]{:S(2)}, u32[]{:S(2)}) %collective-permute-start.17) | collective-permute-done | bytes 262176 | tf_op jit(solution)/shard_map/ppermute | solution.py:429
  50.1 1.6 %collective-permute-start.18 = (bf16[128,1024]{1,0:T(8,128)(2,1)S(1)}, bf16[128,1024]{1,0:T(8,128)(2,1)S(1)}, u32[]{:S(2)}, u32[]{:S(2)}) collective-permute-start(bf16[128,1024]{1,0:T(8,128)(2,1)S(1)} %shard_map.103), channel_id=1, source_target_pairs={{0,16},{4,12},{8,24},{12,4},{16,0},{20,28},{24,8},{28,20},{1,17},{... | collective-permute-start | bytes 786440 | tf_op jit(solution)/shard_map/ppermute | solution.py:429
  51.7 6.7 %collective-permute-done.12.refs_1_.refs_2_ = bf16[384,256]{1,0:T(8,128)(2,1)S(1)} collective-permute-done((bf16[384,256]{1,0:T(8,128)(2,1)S(1)}, bf16[384,256]{1,0:T(8,128)(2,1)S(1)}, u32[]{:S(2)}, u32[]{:S(2)}) %collective-permute-start.12) | collective-permute-done | bytes 196640 | tf_op jit(solution)/shard_map/ppermute | solution.py:424
  58.4 0.4 collective-permute-done.18.refs_8_
  58.8 1.7 %shard_map.105 = (bf16[1536,256]{1,0:T(8,128)(2,1)}, bf16[384,1024]{1,0:T(8,128)(2,1)}) custom-call(bf16[384,256]{1,0:T(8,128)(2,1)S(1)} %get-tuple-element.107.refs_0_, bf16[384,256]{1,0:T(8,128)(2,1)S(1)} %collective-permute-done.11.refs_0_.refs_1_, bf16[384,256]{1,0:T(8,128)(2,1)S(1)} %collective-permute-done.12.refs_1_.refs_2_, ...), custom_call_target="tpu_custom_call" | custom-call | bytes 5705728 | tf_op jit(solution)/shard_map/pallas_call | solution.py:46
  (18 shorter events, 0.1 us)
Async XLA Ops:
  0.6 14.7 %collective-permute-start = (bf16[384,1024]{1,0:T(8,128)(2,1)}, bf16[384,1024]{1,0:T(8,128)(2,1)S(1)}, u32[]{:S(2)}, u32[]{:S(2)}) collective-permute-start(bf16[384,1024]{1,0:T(8,128)(2,1)} %raw_ref.1), channel_id=1, source_target_pairs={{0,16},{4,12},{8,24},{12,4},{16,0},{20,28},{24,8},{28,20},{1,17},{... | collective-permute-start | bytes 2359304 | tf_op jit(solution)/shard_map/ppermute | solution.py:429
  3.7 1.1 %copy-start = (bf16[1536,256]{1,0:T(8,128)(2,1)S(1)}, bf16[1536,256]{1,0:T(8,128)(2,1)}, u32[]{:S(2)}) copy-start(bf16[1536,256]{1,0:T(8,128)(2,1)} %text_ref.1) | copy-start | bytes 2359300
  4.8 8.8 %copy-start.1 = (s32[12288]{0:T(1024)S(1)}, s32[12288]{0:T(1024)}, u32[]{:S(2)}) copy-start(s32[12288]{0:T(1024)} %param.11) | copy-start | bytes 147460
  4.8 8.8 %copy-start.2 = (s32[12288]{0:T(1024)S(1)}, s32[12288]{0:T(1024)}, u32[]{:S(2)}) copy-start(s32[12288]{0:T(1024)} %param.12) | copy-start | bytes 147460
  4.8 8.8 %copy-start.3 = (s32[96,8,3]{0,1,2:T(8,128)S(1)}, s32[96,8,3]{0,1,2:T(8,128)}, u32[]{:S(2)}) copy-start(s32[96,8,3]{0,1,2:T(8,128)} %param.13) | copy-start | bytes 27652
  4.9 18.5 %collective-permute-start.1 = (bf16[384,256]{1,0:T(8,128)(2,1)S(1)}, bf16[384,256]{1,0:T(8,128)(2,1)S(1)}, u32[]{:S(2)}, u32[]{:S(2)}) collective-permute-start(bf16[384,256]{1,0:T(8,128)(2,1)S(1)} %get-tuple-element.76), channel_id=1, source_target_pairs={{0,3},{1,2},{2,1},{3,0},{4,7},{5,6},{6,5},{7,4},{8,11},{9,10},{10,... | collective-permute-start | bytes 589832 | tf_op jit(solution)/shard_map/ppermute | solution.py:424
  8.5 16.4 %collective-permute-start.2 = (bf16[384,256]{1,0:T(8,128)(2,1)S(1)}, bf16[384,256]{1,0:T(8,128)(2,1)S(1)}, u32[]{:S(2)}, u32[]{:S(2)}) collective-permute-start(bf16[384,256]{1,0:T(8,128)(2,1)S(1)} %get-tuple-element.77), channel_id=1, source_target_pairs={{0,2},{1,3},{2,0},{3,1},{4,6},{5,7},{6,4},{7,5},{8,10},{9,11},{10,... | collective-permute-start | bytes 589832 | tf_op jit(solution)/shard_map/ppermute | solution.py:424
  8.5 14.8 %collective-permute-start.3 = (bf16[384,256]{1,0:T(8,128)(2,1)S(1)}, bf16[384,256]{1,0:T(8,128)(2,1)S(1)}, u32[]{:S(2)}, u32[]{:S(2)}) collective-permute-start(bf16[384,256]{1,0:T(8,128)(2,1)S(1)} %get-tuple-element.78), channel_id=1, source_target_pairs={{0,1},{1,0},{2,3},{3,2},{4,5},{5,4},{6,7},{7,6},{8,9},{9,8},{10,11... | collective-permute-start | bytes 589832 | tf_op jit(solution)/shard_map/ppermute | solution.py:424
  10.7 12.3 %collective-permute-start.4 = (bf16[384,1024]{1,0:T(8,128)(2,1)}, bf16[384,1024]{1,0:T(8,128)(2,1)S(1)}, u32[]{:S(2)}, u32[]{:S(2)}) collective-permute-start(bf16[384,1024]{1,0:T(8,128)(2,1)} %raw_ref.1), channel_id=1, source_target_pairs={{0,8},{4,20},{8,0},{12,28},{16,24},{20,4},{24,16},{28,12},{1,9},{5... | collective-permute-start | bytes 2359304 | tf_op jit(solution)/shard_map/ppermute | solution.py:429
  15.3 16.4 %collective-permute-start.8 = (bf16[384,1024]{1,0:T(8,128)(2,1)S(1)}, bf16[384,1024]{1,0:T(8,128)(2,1)S(1)}, u32[]{:S(2)}, u32[]{:S(2)}) collective-permute-start(bf16[384,1024]{1,0:T(8,128)(2,1)S(1)} %collective-permute-done.raw_ref), channel_id=1, source_target_pairs={{0,8},{4,20},{8,0},{12,28},{16,24},{20,4},{24,16},{28,12},{1,9},{5... | collective-permute-start | bytes 2359304 | tf_op jit(solution)/shard_map/ppermute | solution.py:429
  25.3 2.1 %collective-permute-start.5 = (bf16[128,1024]{1,0:T(8,128)(2,1)S(1)}, bf16[128,1024]{1,0:T(8,128)(2,1)S(1)}, u32[]{:S(2)}, u32[]{:S(2)}) collective-permute-start(bf16[128,1024]{1,0:T(8,128)(2,1)S(1)} %get-tuple-element.86), channel_id=1, source_target_pairs={{0,4},{4,0},{8,12},{12,8},{16,20},{20,16},{24,28},{28,24},{1,5},{5... | collective-permute-start | bytes 786440 | tf_op jit(solution)/shard_map/ppermute | solution.py:424
  25.4 2.0 %collective-permute-start.6 = (bf16[128,1024]{1,0:T(8,128)(2,1)S(1)}, bf16[128,1024]{1,0:T(8,128)(2,1)S(1)}, u32[]{:S(2)}, u32[]{:S(2)}) collective-permute-start(bf16[128,1024]{1,0:T(8,128)(2,1)S(1)} %get-tuple-element.87), channel_id=1, source_target_pairs={{0,4},{4,0},{8,12},{12,8},{16,20},{20,16},{24,28},{28,24},{1,5},{5... | collective-permute-start | bytes 786440 | tf_op jit(solution)/shard_map/ppermute | solution.py:424
  25.8 1.8 %collective-permute-start.7 = (bf16[128,1024]{1,0:T(8,128)(2,1)S(1)}, bf16[128,1024]{1,0:T(8,128)(2,1)S(1)}, u32[]{:S(2)}, u32[]{:S(2)}) collective-permute-start(bf16[128,1024]{1,0:T(8,128)(2,1)S(1)} %get-tuple-element.88), channel_id=1, source_target_pairs={{0,4},{4,0},{8,12},{12,8},{16,20},{20,16},{24,28},{28,24},{1,5},{5... | collective-permute-start | bytes 786440 | tf_op jit(solution)/shard_map/ppermute | solution.py:424
  28.9 13.2 %collective-permute-start.14 = (bf16[384,1024]{1,0:T(8,128)(2,1)S(1)}, bf16[384,1024]{1,0:T(8,128)(2,1)S(1)}, u32[]{:S(2)}, u32[]{:S(2)}) collective-permute-start(bf16[384,1024]{1,0:T(8,128)(2,1)S(1)} %get-tuple-element.114), channel_id=1, source_target_pairs={{0,8},{4,20},{8,0},{12,28},{16,24},{20,4},{24,16},{28,12},{1,9},{5... | collective-permute-start | bytes 2359304 | tf_op jit(solution)/shard_map/ppermute | solution.py:429
  34.8 3.9 %collective-permute-start.9 = (bf16[192,1024]{1,0:T(8,128)(2,1)S(1)}, bf16[192,1024]{1,0:T(8,128)(2,1)S(1)}, u32[]{:S(2)}, u32[]{:S(2)}) collective-permute-start(bf16[192,1024]{1,0:T(8,128)(2,1)S(1)} %get-tuple-element.104), channel_id=1, source_target_pairs={{0,4},{4,0},{8,12},{12,8},{16,20},{20,16},{24,28},{28,24},{1,5},{5... | collective-permute-start | bytes 1179656 | tf_op jit(solution)/shard_map/ppermute | solution.py:424
  35.8 2.9 %collective-permute-start.10 = (bf16[192,1024]{1,0:T(8,128)(2,1)S(1)}, bf16[192,1024]{1,0:T(8,128)(2,1)S(1)}, u32[]{:S(2)}, u32[]{:S(2)}) collective-permute-start(bf16[192,1024]{1,0:T(8,128)(2,1)S(1)} %get-tuple-element.105), channel_id=1, source_target_pairs={{0,4},{4,0},{8,12},{12,8},{16,20},{20,16},{24,28},{28,24},{1,5},{5... | collective-permute-start | bytes 1179656 | tf_op jit(solution)/shard_map/ppermute | solution.py:424
  35.9 10.8 %collective-permute-start.15 = (bf16[256,1024]{1,0:T(8,128)(2,1)S(1)}, bf16[256,1024]{1,0:T(8,128)(2,1)S(1)}, u32[]{:S(2)}, u32[]{:S(2)}) collective-permute-start(bf16[256,1024]{1,0:T(8,128)(2,1)S(1)} %get-tuple-element.117), channel_id=1, source_target_pairs={{0,8},{4,20},{8,0},{12,28},{16,24},{20,4},{24,16},{28,12},{1,9},{5... | collective-permute-start | bytes 1572872 | tf_op jit(solution)/shard_map/ppermute | solution.py:429
  36.9 13.2 %collective-permute-start.17 = (bf16[128,1024]{1,0:T(8,128)(2,1)S(1)}, bf16[128,1024]{1,0:T(8,128)(2,1)S(1)}, u32[]{:S(2)}, u32[]{:S(2)}) collective-permute-start(bf16[128,1024]{1,0:T(8,128)(2,1)S(1)} %get-tuple-element.119), channel_id=1, source_target_pairs={{0,8},{4,20},{8,0},{12,28},{16,24},{20,4},{24,16},{28,12},{1,9},{5... | collective-permute-start | bytes 786440 | tf_op jit(solution)/shard_map/ppermute | solution.py:429
  39.3 12.4 %collective-permute-start.11 = (bf16[384,256]{1,0:T(8,128)(2,1)S(1)}, bf16[384,256]{1,0:T(8,128)(2,1)S(1)}, u32[]{:S(2)}, u32[]{:S(2)}) collective-permute-start(bf16[384,256]{1,0:T(8,128)(2,1)S(1)} %get-tuple-element.108), channel_id=1, source_target_pairs={{0,3},{1,2},{2,1},{3,0},{4,7},{5,6},{6,5},{7,4},{8,11},{9,10},{10,... | collective-permute-start | bytes 589832 | tf_op jit(solution)/shard_map/ppermute | solution.py:424
  42.2 16.2 %collective-permute-start.12 = (bf16[384,256]{1,0:T(8,128)(2,1)S(1)}, bf16[384,256]{1,0:T(8,128)(2,1)S(1)}, u32[]{:S(2)}, u32[]{:S(2)}) collective-permute-start(bf16[384,256]{1,0:T(8,128)(2,1)S(1)} %get-tuple-element.109), channel_id=1, source_target_pairs={{0,2},{1,3},{2,0},{3,1},{4,6},{5,7},{6,4},{7,5},{8,10},{9,11},{10,... | collective-permute-start | bytes 589832 | tf_op jit(solution)/shard_map/ppermute | solution.py:424
  42.2 16.2 %collective-permute-start.13 = (bf16[384,256]{1,0:T(8,128)(2,1)S(1)}, bf16[384,256]{1,0:T(8,128)(2,1)S(1)}, u32[]{:S(2)}, u32[]{:S(2)}) collective-permute-start(bf16[384,256]{1,0:T(8,128)(2,1)S(1)} %get-tuple-element.110), channel_id=1, source_target_pairs={{0,1},{1,0},{2,3},{3,2},{4,5},{5,4},{6,7},{7,6},{8,9},{9,8},{10,11... | collective-permute-start | bytes 589832 | tf_op jit(solution)/shard_map/ppermute | solution.py:424
  46.7 12.1 %collective-permute-start.16 = (bf16[256,1024]{1,0:T(8,128)(2,1)S(1)}, bf16[256,1024]{1,0:T(8,128)(2,1)S(1)}, u32[]{:S(2)}, u32[]{:S(2)}) collective-permute-start(bf16[256,1024]{1,0:T(8,128)(2,1)S(1)} %shard_map.102), channel_id=1, source_target_pairs={{0,16},{4,12},{8,24},{12,4},{16,0},{20,28},{24,8},{28,20},{1,17},{... | collective-permute-start | bytes 1572872 | tf_op jit(solution)/shard_map/ppermute | solution.py:429
  50.1 8.7 %collective-permute-start.18 = (bf16[128,1024]{1,0:T(8,128)(2,1)S(1)}, bf16[128,1024]{1,0:T(8,128)(2,1)S(1)}, u32[]{:S(2)}, u32[]{:S(2)}) collective-permute-start(bf16[128,1024]{1,0:T(8,128)(2,1)S(1)} %shard_map.103), channel_id=1, source_target_pairs={{0,16},{4,12},{8,24},{12,4},{16,0},{20,28},{24,8},{28,20},{1,17},{... | collective-permute-start | bytes 786440 | tf_op jit(solution)/shard_map/ppermute | solution.py:429

commit v17 on v15

--- a/solution.py
+++ b/solution.py
@@ -80,6 +80,8 @@
 
 
 def far_first(k, chunks):
+    if chunks > 2 and k in (1, 2):
+        return chunks - 3 + k
     return (chunks - k) % chunks
 
 

time: 60.6 us -> 59.2 us (0.977)
  starting transfers between devices: 24.3 us -> 23.1 us
    ppermute x11, starting transfers between devices: 10.6 us -> 9.73 us  [swap(): return lax.ppermute(value, axis, [(i, i ^ bits) for i in range(count)])]
    ppermute x11, waiting for transfers between devices: 8.47 us -> 7.79 us  [swap(): return lax.ppermute(value, axis, [(i, i ^ bits) for i in range(count)])]
  transfers between devices with their start and end apart: 19 -> 19, of which waited for: 8 -> 9; matrix products, arithmetic and copies ran while one was open for 0% -> 0% of each run, Pallas kernels for 24% -> 25%
where the time goes in v17:
time: 59.2 us; the launch traced here: 59 us
  starting transfers between devices  23.1 us (39%)
  waiting for transfers between devices  16.4 us (28%)
  Pallas kernels  16.2 us (27%)
  between operations  2.14 us (4%)
  local copies, waits for them, and re-layouts  1.14 us (2%)
    pallas_call x20, Pallas kernels, call_kernel(): pl.pallas_call(body, out_shape=outs, in_specs=specs, out_specs=[ANY_SPEC...  16.2 us
    ppermute x8, starting transfers between devices, swap_near(): lax.ppermute(value, 'blk', [(i, i ^ neighbour_bits(i)[which]) for i in ra...  13.4 us
    ppermute x11, starting transfers between devices, swap(): return lax.ppermute(value, axis, [(i, i ^ bits) for i in range(count)])  9.73 us
    ppermute x8, waiting for transfers between devices, swap_near(): lax.ppermute(value, 'blk', [(i, i ^ neighbour_bits(i)[which]) for i in ra...  8.61 us
    ppermute x11, waiting for transfers between devices, swap(): return lax.ppermute(value, axis, [(i, i ^ bits) for i in range(count)])  7.79 us
  transfers between devices with their start and end apart: 19, of which 9 were waited for; matrix products, arithmetic and copies ran while one was open for 0% of the time, Pallas kernels for 25%

profile of v17, /device:TPU:0, one launch (start us, length us, event | category | flops | bytes accessed | tf_op | source)
XLA Modules:
  0.0 59.0 jit_solution(12090347792953127007)
XLA Ops:
  0.6 3.0 %collective-permute-start = (bf16[384,1024]{1,0:T(8,128)(2,1)}, bf16[384,1024]{1,0:T(8,128)(2,1)S(1)}, u32[]{:S(2)}, u32[]{:S(2)}) collective-permute-start(bf16[384,1024]{1,0:T(8,128)(2,1)} %raw_ref.1), channel_id=1, source_target_pairs={{0,16},{4,12},{8,24},{12,4},{16,0},{20,28},{24,8},{28,20},{1,17},{... | collective-permute-start | bytes 2359304 | tf_op jit(solution)/shard_map/ppermute | solution.py:434
  3.7 1.1 %copy-done = bf16[1536,256]{1,0:T(8,128)(2,1)S(1)} copy-done((bf16[1536,256]{1,0:T(8,128)(2,1)S(1)}, bf16[1536,256]{1,0:T(8,128)(2,1)}, u32[]{:S(2)}) %copy-start) | copy-done | bytes 786456
  4.8 0.1 shard_map.88
  4.9 2.7 %collective-permute-start.1 = (bf16[384,256]{1,0:T(8,128)(2,1)S(1)}, bf16[384,256]{1,0:T(8,128)(2,1)S(1)}, u32[]{:S(2)}, u32[]{:S(2)}) collective-permute-start(bf16[384,256]{1,0:T(8,128)(2,1)S(1)} %get-tuple-element.76), channel_id=1, source_target_pairs={{0,2},{1,3},{2,0},{3,1},{4,6},{5,7},{6,4},{7,5},{8,10},{9,11},{10,... | collective-permute-start | bytes 589832 | tf_op jit(solution)/shard_map/ppermute | solution.py:429
  7.5 1.3 %collective-permute-start.2 = (bf16[384,256]{1,0:T(8,128)(2,1)S(1)}, bf16[384,256]{1,0:T(8,128)(2,1)S(1)}, u32[]{:S(2)}, u32[]{:S(2)}) collective-permute-start(bf16[384,256]{1,0:T(8,128)(2,1)S(1)} %get-tuple-element.77), channel_id=1, source_target_pairs={{0,3},{1,2},{2,1},{3,0},{4,7},{5,6},{6,5},{7,4},{8,11},{9,10},{10,... | collective-permute-start | bytes 589832 | tf_op jit(solution)/shard_map/ppermute | solution.py:429
  8.9 0.2 collective-permute-start.3
  9.1 1.4 %shard_map.86 = (bf16[384,1024]{1,0:T(8,128)(2,1)S(1)}, bf16[384,1024]{1,0:T(8,128)(2,1)S(1)}, f32[384,128]{1,0:T(8,128)S(1)}) custom-call(bf16[384,1024]{1,0:T(8,128)(2,1)} %raw_ref.1), custom_call_target="tpu_custom_call" | custom-call | bytes 2555904 | tf_op jit(solution)/shard_map/pallas_call | solution.py:46
  10.5 1.6 %collective-permute-start.4 = (bf16[384,1024]{1,0:T(8,128)(2,1)}, bf16[384,1024]{1,0:T(8,128)(2,1)S(1)}, u32[]{:S(2)}, u32[]{:S(2)}) collective-permute-start(bf16[384,1024]{1,0:T(8,128)(2,1)} %raw_ref.1), channel_id=1, source_target_pairs={{0,8},{4,20},{8,0},{12,28},{16,24},{20,4},{24,16},{28,12},{1,9},{5... | collective-permute-start | bytes 2359304 | tf_op jit(solution)/shard_map/ppermute | solution.py:434
  13.4 1.1 %shard_map.87 = (f32[2,128]{1,0:T(2,128)S(1)}, f32[72,128]{1,0:T(8,128)S(1)}, s32[12,128]{1,0:T(8,128)S(1)}, s32[768,128]{1,0:T(8,128)S(1)}, f32[384,128]{1,0:T(8,128)S(1)}, /*index=5*/f32[4,128]{1,0:T(4,128)S(1)}) custom-call(f32[1]{0:T(128)S(6)} %copy.9.refs_0_, f32[1]{0:T(128)S(6)} %copy.10.refs_1_, s32[3,8,96]{2,1,0:T(8,128)S(1)} %bitcast.5, ...), custom_call_target="tpu_custom_call" | custom-call | bytes 743432 | tf_op jit(solution)/shard_map/pallas_call | solution.py:46
  14.5 0.9 %collective-permute-done.raw_ref = bf16[384,1024]{1,0:T(8,128)(2,1)S(1)} collective-permute-done((bf16[384,1024]{1,0:T(8,128)(2,1)}, bf16[384,1024]{1,0:T(8,128)(2,1)S(1)}, u32[]{:S(2)}, u32[]{:S(2)}) %collective-permute-start) | collective-permute-done | bytes 786464 | tf_op jit(solution)/shard_map/ppermute | solution.py:434
  15.4 3.3 %collective-permute-start.8 = (bf16[384,1024]{1,0:T(8,128)(2,1)S(1)}, bf16[384,1024]{1,0:T(8,128)(2,1)S(1)}, u32[]{:S(2)}, u32[]{:S(2)}) collective-permute-start(bf16[384,1024]{1,0:T(8,128)(2,1)S(1)} %collective-permute-done.raw_ref), channel_id=1, source_target_pairs={{0,8},{4,20},{8,0},{12,28},{16,24},{20,4},{24,16},{28,12},{1,9},{5... | collective-permute-start | bytes 2359304 | tf_op jit(solution)/shard_map/ppermute | solution.py:434
  18.7 0.2 shard_map.89.second_unit_ref
  19.0 3.8 %collective-permute-done.4.first_ref = bf16[384,1024]{1,0:T(8,128)(2,1)S(1)} collective-permute-done((bf16[384,1024]{1,0:T(8,128)(2,1)}, bf16[384,1024]{1,0:T(8,128)(2,1)S(1)}, u32[]{:S(2)}, u32[]{:S(2)}) %collective-permute-start.4) | collective-permute-done | bytes 786464 | tf_op jit(solution)/shard_map/ppermute | solution.py:434
  22.8 0.3 shard_map.90.refs_7_
  23.1 0.0 collective-permute-done.1.refs_1_.refs_2_
  23.1 0.4 shard_map.91
  23.5 0.1 collective-permute-start.5
  23.6 0.5 collective-permute-start.6
  24.1 0.1 collective-permute-start.7
  24.2 1.4 %shard_map.92 = (bf16[384,384]{1,0:T(8,128)(2,1)S(1)}, bf16[384,768]{1,0:T(8,128)(2,1)S(1)}) custom-call(f32[2,128]{1,0:T(2,128)S(1)} %get-tuple-element.69.refs_0_, f32[72,128]{1,0:T(8,128)S(1)} %get-tuple-element.70.refs_1_, s32[12,128]{1,0:T(8,128)S(1)} %get-tuple-element.71.refs_2_, s32[768,128]{1,0:T(8,128)S(1)} %get-tuple-element.72.refs_3_, ...), custom_call_target="tpu_custom_call" | custom-call | bytes 4666368 | tf_op jit(solution)/shard_map/pallas_call | solution.py:46
  25.6 0.2 collective-permute-done.7.refs_11_
  25.9 1.3 %shard_map.93 = (bf16[768,1024]{1,0:T(8,128)(2,1)S(1)}, bf16[768,384]{1,0:T(8,128)(2,1)S(1)}, bf16[384,1024]{1,0:T(8,128)(2,1)S(1)}) custom-call(f32[2,128]{1,0:T(2,128)S(1)} %get-tuple-element.69.refs_0_, f32[72,128]{1,0:T(8,128)S(1)} %get-tuple-element.70.refs_1_, s32[12,128]{1,0:T(8,128)S(1)} %get-tuple-element.71.refs_2_, ...), custom_call_target="tpu_custom_call" | custom-call | bytes 8107008 | tf_op jit(solution)/shard_map/pallas_call | solution.py:46
  27.2 1.6 %collective-permute-start.14 = (bf16[384,1024]{1,0:T(8,128)(2,1)S(1)}, bf16[384,1024]{1,0:T(8,128)(2,1)S(1)}, u32[]{:S(2)}, u32[]{:S(2)}) collective-permute-start(bf16[384,1024]{1,0:T(8,128)(2,1)S(1)} %get-tuple-element.114), channel_id=1, source_target_pairs={{0,8},{4,20},{8,0},{12,28},{16,24},{20,4},{24,16},{28,12},{1,9},{5... | collective-permute-start | bytes 2359304 | tf_op jit(solution)/shard_map/ppermute | solution.py:434
  28.8 2.2 %shard_map.94 = (bf16[768,384]{1,0:T(8,128)(2,1)S(1)}, f32[768,1024]{1,0:T(8,128)S(1)}, bf16[768,768]{1,0:T(8,128)(2,1)S(1)}) custom-call(f32[2,128]{1,0:T(2,128)S(1)} %get-tuple-element.69.refs_0_, f32[72,128]{1,0:T(8,128)S(1)} %get-tuple-element.70.refs_1_, s32[12,128]{1,0:T(8,128)S(1)} %get-tuple-element.71.refs_2_, ...), custom_call_target="tpu_custom_call" | custom-call | bytes 10957824 | tf_op jit(solution)/shard_map/pallas_call | solution.py:46
  31.0 0.2 collective-permute-done.8.refs_9_
  31.2 1.4 %shard_map.95 = (bf16[768,768]{1,0:T(8,128)(2,1)S(1)}, bf16[768,1024]{1,0:T(8,128)(2,1)S(1)}) custom-call(f32[2,128]{1,0:T(2,128)S(1)} %get-tuple-element.69.refs_0_, f32[72,128]{1,0:T(8,128)S(1)} %get-tuple-element.70.refs_1_, s32[12,128]{1,0:T(8,128)S(1)} %get-tuple-element.71.refs_2_, s32[768,128]{1,0:T(8,128)S(1)} %get-tuple-element.72.refs_3_, ...), custom_call_target="tpu_custom_call" | custom-call | bytes 7123968 | tf_op jit(solution)/shard_map/pallas_call | solution.py:46
  32.6 0.8 %shard_map.96 = (bf16[256,1024]{1,0:T(8,128)(2,1)S(1)}, bf16[128,1024]{1,0:T(8,128)(2,1)S(1)}) custom-call(bf16[768,768]{1,0:T(8,128)(2,1)S(1)} %get-tuple-element.97.weight_ref, bf16[768,1024]{1,0:T(8,128)(2,1)S(1)} %get-tuple-element.89.refs_6_.unit_ref), custom_call_target="tpu_custom_call" | custom-call | bytes 3538944 | tf_op jit(solution)/shard_map/pallas_call | solution.py:46
  33.4 0.8 %shard_map.97 = (bf16[192,1024]{1,0:T(8,128)(2,1)S(1)}, bf16[192,1024]{1,0:T(8,128)(2,1)S(1)}) custom-call(bf16[768,768]{1,0:T(8,128)(2,1)S(1)} %get-tuple-element.97.weight_ref, bf16[768,1024]{1,0:T(8,128)(2,1)S(1)} %get-tuple-element.103.image_ref, f32[768,1024]{1,0:T(8,128)S(1)} %get-tuple-element.101.acc_ref), custom_call_target="tpu_custom_call" | custom-call | bytes 6684672 | tf_op jit(solution)/shard_map/pallas_call | solution.py:46
  34.2 0.1 collective-permute-start.9
  34.3 0.5 collective-permute-start.10
  34.8 1.5 %collective-permute-start.15 = (bf16[256,1024]{1,0:T(8,128)(2,1)S(1)}, bf16[256,1024]{1,0:T(8,128)(2,1)S(1)}, u32[]{:S(2)}, u32[]{:S(2)}) collective-permute-start(bf16[256,1024]{1,0:T(8,128)(2,1)S(1)} %get-tuple-element.117), channel_id=1, source_target_pairs={{0,8},{4,20},{8,0},{12,28},{16,24},{20,4},{24,16},{28,12},{1,9},{5... | collective-permute-start | bytes 1572872 | tf_op jit(solution)/shard_map/ppermute | solution.py:434
  36.3 0.5 collective-permute-start.17
  36.8 0.8 %shard_map.98.refs_5_ = f32[384,1024]{1,0:T(8,128)S(1)} custom-call(bf16[768,768]{1,0:T(8,128)(2,1)S(1)} %get-tuple-element.97.weight_ref, bf16[768,1024]{1,0:T(8,128)(2,1)S(1)} %get-tuple-element.103.image_ref, f32[768,1024]{1,0:T(8,128)S(1)} %get-tuple-element.101.acc_ref), custom_call_target="tpu_custom_call" | custom-call | bytes 7471104 | tf_op jit(solution)/shard_map/pallas_call | solution.py:46
  37.7 0.6 %shard_map.99 = (bf16[384,256]{1,0:T(8,128)(2,1)S(1)}, bf16[384,256]{1,0:T(8,128)(2,1)S(1)}, bf16[384,256]{1,0:T(8,128)(2,1)S(1)}, bf16[384,256]{1,0:T(8,128)(2,1)S(1)}) custom-call(f32[384,128]{1,0:T(8,128)S(1)} %get-tuple-element.93.refs_0_, bf16[384,256]{1,0:T(8,128)(2,1)S(1)} %get-tuple-element.75.refs_0_.refs_1_, ...), custom_call_target="tpu_custom_call" | custom-call | bytes 4128768 | tf_op jit(solution)/shard_map/pallas_call | solution.py:46
  38.3 3.6 %collective-permute-start.11 = (bf16[384,256]{1,0:T(8,128)(2,1)S(1)}, bf16[384,256]{1,0:T(8,128)(2,1)S(1)}, u32[]{:S(2)}, u32[]{:S(2)}) collective-permute-start(bf16[384,256]{1,0:T(8,128)(2,1)S(1)} %get-tuple-element.108), channel_id=1, source_target_pairs={{0,2},{1,3},{2,0},{3,1},{4,6},{5,7},{6,4},{7,5},{8,10},{9,11},{10,... | collective-permute-start | bytes 589832 | tf_op jit(solution)/shard_map/ppermute | solution.py:429
  41.9 0.6 %collective-permute-start.12 = (bf16[384,256]{1,0:T(8,128)(2,1)S(1)}, bf16[384,256]{1,0:T(8,128)(2,1)S(1)}, u32[]{:S(2)}, u32[]{:S(2)}) collective-permute-start(bf16[384,256]{1,0:T(8,128)(2,1)S(1)} %get-tuple-element.109), channel_id=1, source_target_pairs={{0,3},{1,2},{2,1},{3,0},{4,7},{5,6},{6,5},{7,4},{8,11},{9,10},{10,... | collective-permute-start | bytes 589832 | tf_op jit(solution)/shard_map/ppermute | solution.py:429
  42.5 0.0 collective-permute-start.13
  42.6 0.8 %shard_map.100 = (f32[384,1024]{1,0:T(8,128)S(1)}, bf16[384,1024]{1,0:T(8,128)(2,1)S(1)}) custom-call(bf16[768,768]{1,0:T(8,128)(2,1)S(1)} %get-tuple-element.113.weight_ref, bf16[768,1024]{1,0:T(8,128)(2,1)S(1)} %get-tuple-element.89.refs_6_.unit_ref, bf16[384,1024]{1,0:T(8,128)(2,1)S(1)} %collective-permute-done.14.add_ref), custom_call_target="tpu_custom_call" | custom-call | bytes 5898240 | tf_op jit(solution)/shard_map/pallas_call | solution.py:46
  43.4 0.8 %shard_map.101.refs_6_ = f32[384,1024]{1,0:T(8,128)S(1)} custom-call(bf16[768,384]{1,0:T(8,128)(2,1)S(1)} %get-tuple-element.95.refs_8_.weight_ref, bf16[768,1024]{1,0:T(8,128)(2,1)S(1)} %get-tuple-element.89.refs_6_.unit_ref, bf16[384,1024]{1,0:T(8,128)(2,1)S(1)} %get-tuple-element.115.add_ref), custom_call_target="tpu_custom_call" | custom-call | tf_op jit(solution)/shard_map/pallas_call | solution.py:46
  44.2 1.1 %collective-permute-done.15.in_ref = bf16[256,1024]{1,0:T(8,128)(2,1)S(1)} collective-permute-done((bf16[256,1024]{1,0:T(8,128)(2,1)S(1)}, bf16[256,1024]{1,0:T(8,128)(2,1)S(1)}, u32[]{:S(2)}, u32[]{:S(2)}) %collective-permute-start.15) | collective-permute-done | bytes 524320 | tf_op jit(solution)/shard_map/ppermute | solution.py:434
  45.2 0.1 shard_map.102
  45.3 1.0 %collective-permute-start.16 = (bf16[256,1024]{1,0:T(8,128)(2,1)S(1)}, bf16[256,1024]{1,0:T(8,128)(2,1)S(1)}, u32[]{:S(2)}, u32[]{:S(2)}) collective-permute-start(bf16[256,1024]{1,0:T(8,128)(2,1)S(1)} %shard_map.102), channel_id=1, source_target_pairs={{0,16},{4,12},{8,24},{12,4},{16,0},{20,28},{24,8},{28,20},{1,17},{... | collective-permute-start | bytes 1572872 | tf_op jit(solution)/shard_map/ppermute | solution.py:434
  46.3 1.8 %collective-permute-done.17.in_ref = bf16[128,1024]{1,0:T(8,128)(2,1)S(1)} collective-permute-done((bf16[128,1024]{1,0:T(8,128)(2,1)S(1)}, bf16[128,1024]{1,0:T(8,128)(2,1)S(1)}, u32[]{:S(2)}, u32[]{:S(2)}) %collective-permute-start.17) | collective-permute-done | bytes 262176 | tf_op jit(solution)/shard_map/ppermute | solution.py:434
  48.2 0.9 %collective-permute-start.18 = (bf16[128,1024]{1,0:T(8,128)(2,1)S(1)}, bf16[128,1024]{1,0:T(8,128)(2,1)S(1)}, u32[]{:S(2)}, u32[]{:S(2)}) collective-permute-start(bf16[128,1024]{1,0:T(8,128)(2,1)S(1)} %shard_map.103), channel_id=1, source_target_pairs={{0,16},{4,12},{8,24},{12,4},{16,0},{20,28},{24,8},{28,20},{1,17},{... | collective-permute-start | bytes 786440 | tf_op jit(solution)/shard_map/ppermute | solution.py:434
  49.1 6.5 %collective-permute-done.11.refs_0_.refs_1_ = bf16[384,256]{1,0:T(8,128)(2,1)S(1)} collective-permute-done((bf16[384,256]{1,0:T(8,128)(2,1)S(1)}, bf16[384,256]{1,0:T(8,128)(2,1)S(1)}, u32[]{:S(2)}, u32[]{:S(2)}) %collective-permute-start.11) | collective-permute-done | bytes 196640 | tf_op jit(solution)/shard_map/ppermute | solution.py:429
  55.6 1.0 %collective-permute-done.13.refs_2_.refs_3_ = bf16[384,256]{1,0:T(8,128)(2,1)S(1)} collective-permute-done((bf16[384,256]{1,0:T(8,128)(2,1)S(1)}, bf16[384,256]{1,0:T(8,128)(2,1)S(1)}, u32[]{:S(2)}, u32[]{:S(2)}) %collective-permute-start.13) | collective-permute-done | bytes 196640 | tf_op jit(solution)/shard_map/ppermute | solution.py:429
  56.7 0.7 %collective-permute-done.18.refs_8_ = bf16[128,1024]{1,0:T(8,128)(2,1)S(1)} collective-permute-done((bf16[128,1024]{1,0:T(8,128)(2,1)S(1)}, bf16[128,1024]{1,0:T(8,128)(2,1)S(1)}, u32[]{:S(2)}, u32[]{:S(2)}) %collective-permute-start.18) | collective-permute-done | bytes 262176 | tf_op jit(solution)/shard_map/ppermute | solution.py:434
  57.4 1.6 %shard_map.105 = (bf16[1536,256]{1,0:T(8,128)(2,1)}, bf16[384,1024]{1,0:T(8,128)(2,1)}) custom-call(bf16[384,256]{1,0:T(8,128)(2,1)S(1)} %get-tuple-element.107.refs_0_, bf16[384,256]{1,0:T(8,128)(2,1)S(1)} %collective-permute-done.11.refs_0_.refs_1_, bf16[384,256]{1,0:T(8,128)(2,1)S(1)} %collective-permute-done.12.refs_1_.refs_2_, ...), custom_call_target="tpu_custom_call" | custom-call | bytes 5705728 | tf_op jit(solution)/shard_map/pallas_call | solution.py:46
  (18 shorter events, 0.1 us)
Async XLA Ops:
  0.6 14.8 %collective-permute-start = (bf16[384,1024]{1,0:T(8,128)(2,1)}, bf16[384,1024]{1,0:T(8,128)(2,1)S(1)}, u32[]{:S(2)}, u32[]{:S(2)}) collective-permute-start(bf16[384,1024]{1,0:T(8,128)(2,1)} %raw_ref.1), channel_id=1, source_target_pairs={{0,16},{4,12},{8,24},{12,4},{16,0},{20,28},{24,8},{28,20},{1,17},{... | collective-permute-start | bytes 2359304 | tf_op jit(solution)/shard_map/ppermute | solution.py:434
  3.7 1.1 %copy-start = (bf16[1536,256]{1,0:T(8,128)(2,1)S(1)}, bf16[1536,256]{1,0:T(8,128)(2,1)}, u32[]{:S(2)}) copy-start(bf16[1536,256]{1,0:T(8,128)(2,1)} %text_ref.1) | copy-start | bytes 2359300
  4.8 8.6 %copy-start.1 = (s32[12288]{0:T(1024)S(1)}, s32[12288]{0:T(1024)}, u32[]{:S(2)}) copy-start(s32[12288]{0:T(1024)} %param.11) | copy-start | bytes 147460
  4.8 8.6 %copy-start.2 = (s32[12288]{0:T(1024)S(1)}, s32[12288]{0:T(1024)}, u32[]{:S(2)}) copy-start(s32[12288]{0:T(1024)} %param.12) | copy-start | bytes 147460
  4.8 8.6 %copy-start.3 = (s32[96,8,3]{0,1,2:T(8,128)S(1)}, s32[96,8,3]{0,1,2:T(8,128)}, u32[]{:S(2)}) copy-start(s32[96,8,3]{0,1,2:T(8,128)} %param.13) | copy-start | bytes 27652
  4.9 18.3 %collective-permute-start.1 = (bf16[384,256]{1,0:T(8,128)(2,1)S(1)}, bf16[384,256]{1,0:T(8,128)(2,1)S(1)}, u32[]{:S(2)}, u32[]{:S(2)}) collective-permute-start(bf16[384,256]{1,0:T(8,128)(2,1)S(1)} %get-tuple-element.76), channel_id=1, source_target_pairs={{0,2},{1,3},{2,0},{3,1},{4,6},{5,7},{6,4},{7,5},{8,10},{9,11},{10,... | collective-permute-start | bytes 589832 | tf_op jit(solution)/shard_map/ppermute | solution.py:429
  7.5 15.6 %collective-permute-start.2 = (bf16[384,256]{1,0:T(8,128)(2,1)S(1)}, bf16[384,256]{1,0:T(8,128)(2,1)S(1)}, u32[]{:S(2)}, u32[]{:S(2)}) collective-permute-start(bf16[384,256]{1,0:T(8,128)(2,1)S(1)} %get-tuple-element.77), channel_id=1, source_target_pairs={{0,3},{1,2},{2,1},{3,0},{4,7},{5,6},{6,5},{7,4},{8,11},{9,10},{10,... | collective-permute-start | bytes 589832 | tf_op jit(solution)/shard_map/ppermute | solution.py:429
  8.9 14.3 %collective-permute-start.3 = (bf16[384,256]{1,0:T(8,128)(2,1)S(1)}, bf16[384,256]{1,0:T(8,128)(2,1)S(1)}, u32[]{:S(2)}, u32[]{:S(2)}) collective-permute-start(bf16[384,256]{1,0:T(8,128)(2,1)S(1)} %get-tuple-element.78), channel_id=1, source_target_pairs={{0,1},{1,0},{2,3},{3,2},{4,5},{5,4},{6,7},{7,6},{8,9},{9,8},{10,11... | collective-permute-start | bytes 589832 | tf_op jit(solution)/shard_map/ppermute | solution.py:429
  10.5 12.3 %collective-permute-start.4 = (bf16[384,1024]{1,0:T(8,128)(2,1)}, bf16[384,1024]{1,0:T(8,128)(2,1)S(1)}, u32[]{:S(2)}, u32[]{:S(2)}) collective-permute-start(bf16[384,1024]{1,0:T(8,128)(2,1)} %raw_ref.1), channel_id=1, source_target_pairs={{0,8},{4,20},{8,0},{12,28},{16,24},{20,4},{24,16},{28,12},{1,9},{5... | collective-permute-start | bytes 2359304 | tf_op jit(solution)/shard_map/ppermute | solution.py:434
  15.4 15.8 %collective-permute-start.8 = (bf16[384,1024]{1,0:T(8,128)(2,1)S(1)}, bf16[384,1024]{1,0:T(8,128)(2,1)S(1)}, u32[]{:S(2)}, u32[]{:S(2)}) collective-permute-start(bf16[384,1024]{1,0:T(8,128)(2,1)S(1)} %collective-permute-done.raw_ref), channel_id=1, source_target_pairs={{0,8},{4,20},{8,0},{12,28},{16,24},{20,4},{24,16},{28,12},{1,9},{5... | collective-permute-start | bytes 2359304 | tf_op jit(solution)/shard_map/ppermute | solution.py:434
  23.5 2.1 %collective-permute-start.5 = (bf16[128,1024]{1,0:T(8,128)(2,1)S(1)}, bf16[128,1024]{1,0:T(8,128)(2,1)S(1)}, u32[]{:S(2)}, u32[]{:S(2)}) collective-permute-start(bf16[128,1024]{1,0:T(8,128)(2,1)S(1)} %get-tuple-element.86), channel_id=1, source_target_pairs={{0,4},{4,0},{8,12},{12,8},{16,20},{20,16},{24,28},{28,24},{1,5},{5... | collective-permute-start | bytes 786440 | tf_op jit(solution)/shard_map/ppermute | solution.py:429
  23.6 2.0 %collective-permute-start.6 = (bf16[128,1024]{1,0:T(8,128)(2,1)S(1)}, bf16[128,1024]{1,0:T(8,128)(2,1)S(1)}, u32[]{:S(2)}, u32[]{:S(2)}) collective-permute-start(bf16[128,1024]{1,0:T(8,128)(2,1)S(1)} %get-tuple-element.87), channel_id=1, source_target_pairs={{0,4},{4,0},{8,12},{12,8},{16,20},{20,16},{24,28},{28,24},{1,5},{5... | collective-permute-start | bytes 786440 | tf_op jit(solution)/shard_map/ppermute | solution.py:429
  24.1 1.8 %collective-permute-start.7 = (bf16[128,1024]{1,0:T(8,128)(2,1)S(1)}, bf16[128,1024]{1,0:T(8,128)(2,1)S(1)}, u32[]{:S(2)}, u32[]{:S(2)}) collective-permute-start(bf16[128,1024]{1,0:T(8,128)(2,1)S(1)} %get-tuple-element.88), channel_id=1, source_target_pairs={{0,4},{4,0},{8,12},{12,8},{16,20},{20,16},{24,28},{28,24},{1,5},{5... | collective-permute-start | bytes 786440 | tf_op jit(solution)/shard_map/ppermute | solution.py:429
  27.2 15.3 %collective-permute-start.14 = (bf16[384,1024]{1,0:T(8,128)(2,1)S(1)}, bf16[384,1024]{1,0:T(8,128)(2,1)S(1)}, u32[]{:S(2)}, u32[]{:S(2)}) collective-permute-start(bf16[384,1024]{1,0:T(8,128)(2,1)S(1)} %get-tuple-element.114), channel_id=1, source_target_pairs={{0,8},{4,20},{8,0},{12,28},{16,24},{20,4},{24,16},{28,12},{1,9},{5... | collective-permute-start | bytes 2359304 | tf_op jit(solution)/shard_map/ppermute | solution.py:434
  34.2 3.4 %collective-permute-start.9 = (bf16[192,1024]{1,0:T(8,128)(2,1)S(1)}, bf16[192,1024]{1,0:T(8,128)(2,1)S(1)}, u32[]{:S(2)}, u32[]{:S(2)}) collective-permute-start(bf16[192,1024]{1,0:T(8,128)(2,1)S(1)} %get-tuple-element.104), channel_id=1, source_target_pairs={{0,4},{4,0},{8,12},{12,8},{16,20},{20,16},{24,28},{28,24},{1,5},{5... | collective-permute-start | bytes 1179656 | tf_op jit(solution)/shard_map/ppermute | solution.py:429
  34.3 3.3 %collective-permute-start.10 = (bf16[192,1024]{1,0:T(8,128)(2,1)S(1)}, bf16[192,1024]{1,0:T(8,128)(2,1)S(1)}, u32[]{:S(2)}, u32[]{:S(2)}) collective-permute-start(bf16[192,1024]{1,0:T(8,128)(2,1)S(1)} %get-tuple-element.105), channel_id=1, source_target_pairs={{0,4},{4,0},{8,12},{12,8},{16,20},{20,16},{24,28},{28,24},{1,5},{5... | collective-permute-start | bytes 1179656 | tf_op jit(solution)/shard_map/ppermute | solution.py:429
  34.8 10.4 %collective-permute-start.15 = (bf16[256,1024]{1,0:T(8,128)(2,1)S(1)}, bf16[256,1024]{1,0:T(8,128)(2,1)S(1)}, u32[]{:S(2)}, u32[]{:S(2)}) collective-permute-start(bf16[256,1024]{1,0:T(8,128)(2,1)S(1)} %get-tuple-element.117), channel_id=1, source_target_pairs={{0,8},{4,20},{8,0},{12,28},{16,24},{20,4},{24,16},{28,12},{1,9},{5... | collective-permute-start | bytes 1572872 | tf_op jit(solution)/shard_map/ppermute | solution.py:434
  36.3 11.9 %collective-permute-start.17 = (bf16[128,1024]{1,0:T(8,128)(2,1)S(1)}, bf16[128,1024]{1,0:T(8,128)(2,1)S(1)}, u32[]{:S(2)}, u32[]{:S(2)}) collective-permute-start(bf16[128,1024]{1,0:T(8,128)(2,1)S(1)} %get-tuple-element.119), channel_id=1, source_target_pairs={{0,8},{4,20},{8,0},{12,28},{16,24},{20,4},{24,16},{28,12},{1,9},{5... | collective-permute-start | bytes 786440 | tf_op jit(solution)/shard_map/ppermute | solution.py:434
  38.3 17.4 %collective-permute-start.11 = (bf16[384,256]{1,0:T(8,128)(2,1)S(1)}, bf16[384,256]{1,0:T(8,128)(2,1)S(1)}, u32[]{:S(2)}, u32[]{:S(2)}) collective-permute-start(bf16[384,256]{1,0:T(8,128)(2,1)S(1)} %get-tuple-element.108), channel_id=1, source_target_pairs={{0,2},{1,3},{2,0},{3,1},{4,6},{5,7},{6,4},{7,5},{8,10},{9,11},{10,... | collective-permute-start | bytes 589832 | tf_op jit(solution)/shard_map/ppermute | solution.py:429
  41.9 13.7 %collective-permute-start.12 = (bf16[384,256]{1,0:T(8,128)(2,1)S(1)}, bf16[384,256]{1,0:T(8,128)(2,1)S(1)}, u32[]{:S(2)}, u32[]{:S(2)}) collective-permute-start(bf16[384,256]{1,0:T(8,128)(2,1)S(1)} %get-tuple-element.109), channel_id=1, source_target_pairs={{0,3},{1,2},{2,1},{3,0},{4,7},{5,6},{6,5},{7,4},{8,11},{9,10},{10,... | collective-permute-start | bytes 589832 | tf_op jit(solution)/shard_map/ppermute | solution.py:429
  42.5 14.1 %collective-permute-start.13 = (bf16[384,256]{1,0:T(8,128)(2,1)S(1)}, bf16[384,256]{1,0:T(8,128)(2,1)S(1)}, u32[]{:S(2)}, u32[]{:S(2)}) collective-permute-start(bf16[384,256]{1,0:T(8,128)(2,1)S(1)} %get-tuple-element.110), channel_id=1, source_target_pairs={{0,1},{1,0},{2,3},{3,2},{4,5},{5,4},{6,7},{7,6},{8,9},{9,8},{10,11... | collective-permute-start | bytes 589832 | tf_op jit(solution)/shard_map/ppermute | solution.py:429
  45.3 12.1 %collective-permute-start.16 = (bf16[256,1024]{1,0:T(8,128)(2,1)S(1)}, bf16[256,1024]{1,0:T(8,128)(2,1)S(1)}, u32[]{:S(2)}, u32[]{:S(2)}) collective-permute-start(bf16[256,1024]{1,0:T(8,128)(2,1)S(1)} %shard_map.102), channel_id=1, source_target_pairs={{0,16},{4,12},{8,24},{12,4},{16,0},{20,28},{24,8},{28,20},{1,17},{... | collective-permute-start | bytes 1572872 | tf_op jit(solution)/shard_map/ppermute | solution.py:434
  48.2 9.2 %collective-permute-start.18 = (bf16[128,1024]{1,0:T(8,128)(2,1)S(1)}, bf16[128,1024]{1,0:T(8,128)(2,1)S(1)}, u32[]{:S(2)}, u32[]{:S(2)}) collective-permute-start(bf16[128,1024]{1,0:T(8,128)(2,1)S(1)} %shard_map.103), channel_id=1, source_target_pairs={{0,16},{4,12},{8,24},{12,4},{16,0},{20,28},{24,8},{28,20},{1,17},{... | collective-permute-start | bytes 786440 | tf_op jit(solution)/shard_map/ppermute | solution.py:434

commit v18 on v17

--- a/solution.py
+++ b/solution.py
@@ -85,6 +85,10 @@
     return (chunks - k) % chunks
 
 
+def way_out(k, chunks):
+    return (chunks - k) % chunks
+
+
 def feature_slice(peer, width):
     return pl.ds(pl.multiple_of(peer * width, width), width)
 
@@ -366,7 +370,8 @@
         inner = sum(jnp.sum(x * a, axis=-1, keepdims=True) for x, a in zip(raws, accs))
         inner = inner * scales * scales
         for k in range(chunks):
-            out_refs[k][part, :] = (scales * (accs[k] - raws[k] * inner)).astype(jnp.bfloat16)
+            out_ref = out_refs[way_out(far_first(k, chunks), chunks)]
+            out_ref[part, :] = (scales * (accs[k] - raws[k] * inner)).astype(jnp.bfloat16)
 
 
 def arrived_body(*refs):
@@ -402,7 +407,7 @@
     rows = part_refs[0].shape[0]
     copies = []
     for k in range(chunks):
-        peer = place ^ far_first(k, chunks)
+        peer = place ^ way_out(k, chunks)
         for first in range(0, rows, TILE):
             block = pl.ds(pl.multiple_of(peer * rows + first, TILE), TILE)
             copies.append(
@@ -434,9 +439,9 @@
     return lax.ppermute(value, "blk", [(i, i ^ neighbour_bits(i)[which]) for i in range(count)])
 
 
-def swap_chunks(chunks):
+def swap_chunks(chunks, order):
     count = len(chunks)
-    return chunks[:1] + [swap(chunks[k], "tp", far_first(k, count)) for k in range(1, count)]
+    return chunks[:1] + [swap(chunks[k], "tp", order(k, count)) for k in range(1, count)]
 
 
 def per_device(text_emb, image_emb, logit_scale, logit_bias, bucket, positive, blocks):
@@ -458,7 +463,7 @@
         return struct((count, columns), jnp.int32)
 
     picked = call_kernel(pick_body, [bf16(rows, width)] * groups, [text_emb], limit=8)
-    text_raw = swap_chunks(picked)
+    text_raw = swap_chunks(picked, far_first)
     if square:
         from_second = swap_near(image_emb, 1)
     else:
@@ -522,7 +527,7 @@
             [text_scales] + text_raw + [acc_own] + [swap(piece, "blk", 1) for piece in acc_other],
             limit=16,
         )
-        return swap_chunks(parts)
+        return swap_chunks(parts, way_out)
 
     def finish(text_parts, total, pieces):
         arrived = call_kernel(

time: 59.2 us -> 61 us (1.030)
  waiting for transfers between devices: 16.4 us -> 18.1 us
    ppermute x11, waiting for transfers between devices: 7.79 us -> 10.3 us  [swap(): return lax.ppermute(value, axis, [(i, i ^ bits) for i in range(count)])]
    ppermute x8, waiting for transfers between devices: 8.61 us -> 7.71 us  [swap_near(): lax.ppermute(value, 'blk', [(i, i ^ neighbour_bits(i)[which]) for i in ra...]
  transfers between devices with their start and end apart: 19 -> 19, of which waited for: 9 -> 7; matrix products, arithmetic and copies ran while one was open for 0% -> 0% of each run, Pallas kernels for 25% -> 24%
where the time goes in v18:
time: 61 us; the launch traced here: 60.8 us
  starting transfers between devices  23.3 us (38%)
  waiting for transfers between devices  18.1 us (30%)
  Pallas kernels  16.2 us (27%)
  between operations  2.16 us (4%)
  local copies, waits for them, and re-layouts  1.14 us (2%)
    pallas_call x20, Pallas kernels, call_kernel(): pl.pallas_call(body, out_shape=outs, in_specs=specs, out_specs=[ANY_SPEC...  16.2 us
    ppermute x8, starting transfers between devices, swap_near(): lax.ppermute(value, 'blk', [(i, i ^ neighbour_bits(i)[which]) for i in ra...  13.4 us
    ppermute x11, waiting for transfers between devices, swap(): return lax.ppermute(value, axis, [(i, i ^ bits) for i in range(count)])  10.3 us
    ppermute x11, starting transfers between devices, swap(): return lax.ppermute(value, axis, [(i, i ^ bits) for i in range(count)])  9.9 us
    ppermute x8, waiting for transfers between devices, swap_near(): lax.ppermute(value, 'blk', [(i, i ^ neighbour_bits(i)[which]) for i in ra...  7.71 us
  transfers between devices with their start and end apart: 19, of which 7 were waited for; matrix products, arithmetic and copies ran while one was open for 0% of the time, Pallas kernels for 24%

profile of v18, /device:TPU:0, one launch (start us, length us, event | category | flops | bytes accessed | tf_op | source)
XLA Modules:
  0.0 60.8 jit_solution(1439404592182235200)
XLA Ops:
  0.6 3.0 %collective-permute-start = (bf16[384,1024]{1,0:T(8,128)(2,1)}, bf16[384,1024]{1,0:T(8,128)(2,1)S(1)}, u32[]{:S(2)}, u32[]{:S(2)}) collective-permute-start(bf16[384,1024]{1,0:T(8,128)(2,1)} %raw_ref.1), channel_id=1, source_target_pairs={{0,16},{4,12},{8,24},{12,4},{16,0},{20,28},{24,8},{28,20},{1,17},{... | collective-permute-start | bytes 2359304 | tf_op jit(solution)/shard_map/ppermute | solution.py:439
  3.7 1.1 %copy-done = bf16[1536,256]{1,0:T(8,128)(2,1)S(1)} copy-done((bf16[1536,256]{1,0:T(8,128)(2,1)S(1)}, bf16[1536,256]{1,0:T(8,128)(2,1)}, u32[]{:S(2)}) %copy-start) | copy-done | bytes 786456
  4.8 0.1 shard_map.88
  4.9 2.7 %collective-permute-start.1 = (bf16[384,256]{1,0:T(8,128)(2,1)S(1)}, bf16[384,256]{1,0:T(8,128)(2,1)S(1)}, u32[]{:S(2)}, u32[]{:S(2)}) collective-permute-start(bf16[384,256]{1,0:T(8,128)(2,1)S(1)} %get-tuple-element.76), channel_id=1, source_target_pairs={{0,2},{1,3},{2,0},{3,1},{4,6},{5,7},{6,4},{7,5},{8,10},{9,11},{10,... | collective-permute-start | bytes 589832 | tf_op jit(solution)/shard_map/ppermute | solution.py:434
  7.5 1.3 %collective-permute-start.2 = (bf16[384,256]{1,0:T(8,128)(2,1)S(1)}, bf16[384,256]{1,0:T(8,128)(2,1)S(1)}, u32[]{:S(2)}, u32[]{:S(2)}) collective-permute-start(bf16[384,256]{1,0:T(8,128)(2,1)S(1)} %get-tuple-element.77), channel_id=1, source_target_pairs={{0,3},{1,2},{2,1},{3,0},{4,7},{5,6},{6,5},{7,4},{8,11},{9,10},{10,... | collective-permute-start | bytes 589832 | tf_op jit(solution)/shard_map/ppermute | solution.py:434
  8.9 0.2 collective-permute-start.3
  9.1 1.4 %shard_map.86 = (bf16[384,1024]{1,0:T(8,128)(2,1)S(1)}, bf16[384,1024]{1,0:T(8,128)(2,1)S(1)}, f32[384,128]{1,0:T(8,128)S(1)}) custom-call(bf16[384,1024]{1,0:T(8,128)(2,1)} %raw_ref.1), custom_call_target="tpu_custom_call" | custom-call | bytes 2555904 | tf_op jit(solution)/shard_map/pallas_call | solution.py:46
  10.5 1.6 %collective-permute-start.4 = (bf16[384,1024]{1,0:T(8,128)(2,1)}, bf16[384,1024]{1,0:T(8,128)(2,1)S(1)}, u32[]{:S(2)}, u32[]{:S(2)}) collective-permute-start(bf16[384,1024]{1,0:T(8,128)(2,1)} %raw_ref.1), channel_id=1, source_target_pairs={{0,8},{4,20},{8,0},{12,28},{16,24},{20,4},{24,16},{28,12},{1,9},{5... | collective-permute-start | bytes 2359304 | tf_op jit(solution)/shard_map/ppermute | solution.py:439
  13.4 1.1 %shard_map.87 = (f32[2,128]{1,0:T(2,128)S(1)}, f32[72,128]{1,0:T(8,128)S(1)}, s32[12,128]{1,0:T(8,128)S(1)}, s32[768,128]{1,0:T(8,128)S(1)}, f32[384,128]{1,0:T(8,128)S(1)}, /*index=5*/f32[4,128]{1,0:T(4,128)S(1)}) custom-call(f32[1]{0:T(128)S(6)} %copy.9.refs_0_, f32[1]{0:T(128)S(6)} %copy.10.refs_1_, s32[3,8,96]{2,1,0:T(8,128)S(1)} %bitcast.5, ...), custom_call_target="tpu_custom_call" | custom-call | bytes 743432 | tf_op jit(solution)/shard_map/pallas_call | solution.py:46
  14.5 0.9 %collective-permute-done.raw_ref = bf16[384,1024]{1,0:T(8,128)(2,1)S(1)} collective-permute-done((bf16[384,1024]{1,0:T(8,128)(2,1)}, bf16[384,1024]{1,0:T(8,128)(2,1)S(1)}, u32[]{:S(2)}, u32[]{:S(2)}) %collective-permute-start) | collective-permute-done | bytes 786464 | tf_op jit(solution)/shard_map/ppermute | solution.py:439
  15.4 3.3 %collective-permute-start.8 = (bf16[384,1024]{1,0:T(8,128)(2,1)S(1)}, bf16[384,1024]{1,0:T(8,128)(2,1)S(1)}, u32[]{:S(2)}, u32[]{:S(2)}) collective-permute-start(bf16[384,1024]{1,0:T(8,128)(2,1)S(1)} %collective-permute-done.raw_ref), channel_id=1, source_target_pairs={{0,8},{4,20},{8,0},{12,28},{16,24},{20,4},{24,16},{28,12},{1,9},{5... | collective-permute-start | bytes 2359304 | tf_op jit(solution)/shard_map/ppermute | solution.py:439
  18.7 0.2 shard_map.89.second_unit_ref
  19.0 3.8 %collective-permute-done.4.first_ref = bf16[384,1024]{1,0:T(8,128)(2,1)S(1)} collective-permute-done((bf16[384,1024]{1,0:T(8,128)(2,1)}, bf16[384,1024]{1,0:T(8,128)(2,1)S(1)}, u32[]{:S(2)}, u32[]{:S(2)}) %collective-permute-start.4) | collective-permute-done | bytes 786464 | tf_op jit(solution)/shard_map/ppermute | solution.py:439
  22.8 0.3 shard_map.90.refs_7_
  23.1 0.0 collective-permute-done.3.refs_3_.refs_4_
  23.1 0.0 collective-permute-done.1.refs_1_.refs_2_
  23.1 0.4 shard_map.91
  23.5 0.1 collective-permute-start.5
  23.6 0.5 collective-permute-start.6
  24.1 0.1 collective-permute-start.7
  24.2 1.4 %shard_map.92 = (bf16[384,384]{1,0:T(8,128)(2,1)S(1)}, bf16[384,768]{1,0:T(8,128)(2,1)S(1)}) custom-call(f32[2,128]{1,0:T(2,128)S(1)} %get-tuple-element.69.refs_0_, f32[72,128]{1,0:T(8,128)S(1)} %get-tuple-element.70.refs_1_, s32[12,128]{1,0:T(8,128)S(1)} %get-tuple-element.71.refs_2_, s32[768,128]{1,0:T(8,128)S(1)} %get-tuple-element.72.refs_3_, ...), custom_call_target="tpu_custom_call" | custom-call | bytes 4666368 | tf_op jit(solution)/shard_map/pallas_call | solution.py:46
  25.6 0.0 collective-permute-done.6.refs_10_
  25.6 0.2 collective-permute-done.7.refs_11_
  25.9 1.3 %shard_map.93 = (bf16[768,1024]{1,0:T(8,128)(2,1)S(1)}, bf16[768,384]{1,0:T(8,128)(2,1)S(1)}, bf16[384,1024]{1,0:T(8,128)(2,1)S(1)}) custom-call(f32[2,128]{1,0:T(2,128)S(1)} %get-tuple-element.69.refs_0_, f32[72,128]{1,0:T(8,128)S(1)} %get-tuple-element.70.refs_1_, s32[12,128]{1,0:T(8,128)S(1)} %get-tuple-element.71.refs_2_, ...), custom_call_target="tpu_custom_call" | custom-call | bytes 8107008 | tf_op jit(solution)/shard_map/pallas_call | solution.py:46
  27.2 1.6 %collective-permute-start.14 = (bf16[384,1024]{1,0:T(8,128)(2,1)S(1)}, bf16[384,1024]{1,0:T(8,128)(2,1)S(1)}, u32[]{:S(2)}, u32[]{:S(2)}) collective-permute-start(bf16[384,1024]{1,0:T(8,128)(2,1)S(1)} %get-tuple-element.114), channel_id=1, source_target_pairs={{0,8},{4,20},{8,0},{12,28},{16,24},{20,4},{24,16},{28,12},{1,9},{5... | collective-permute-start | bytes 2359304 | tf_op jit(solution)/shard_map/ppermute | solution.py:439
  28.8 2.2 %shard_map.94 = (bf16[768,384]{1,0:T(8,128)(2,1)S(1)}, f32[768,1024]{1,0:T(8,128)S(1)}, bf16[768,768]{1,0:T(8,128)(2,1)S(1)}) custom-call(f32[2,128]{1,0:T(2,128)S(1)} %get-tuple-element.69.refs_0_, f32[72,128]{1,0:T(8,128)S(1)} %get-tuple-element.70.refs_1_, s32[12,128]{1,0:T(8,128)S(1)} %get-tuple-element.71.refs_2_, ...), custom_call_target="tpu_custom_call" | custom-call | bytes 10957824 | tf_op jit(solution)/shard_map/pallas_call | solution.py:46
  31.0 0.2 collective-permute-done.8.refs_9_
  31.2 1.4 %shard_map.95 = (bf16[768,768]{1,0:T(8,128)(2,1)S(1)}, bf16[768,1024]{1,0:T(8,128)(2,1)S(1)}) custom-call(f32[2,128]{1,0:T(2,128)S(1)} %get-tuple-element.69.refs_0_, f32[72,128]{1,0:T(8,128)S(1)} %get-tuple-element.70.refs_1_, s32[12,128]{1,0:T(8,128)S(1)} %get-tuple-element.71.refs_2_, s32[768,128]{1,0:T(8,128)S(1)} %get-tuple-element.72.refs_3_, ...), custom_call_target="tpu_custom_call" | custom-call | bytes 7123968 | tf_op jit(solution)/shard_map/pallas_call | solution.py:46
  32.6 0.8 %shard_map.96 = (bf16[256,1024]{1,0:T(8,128)(2,1)S(1)}, bf16[128,1024]{1,0:T(8,128)(2,1)S(1)}) custom-call(bf16[768,768]{1,0:T(8,128)(2,1)S(1)} %get-tuple-element.97.weight_ref, bf16[768,1024]{1,0:T(8,128)(2,1)S(1)} %get-tuple-element.89.refs_6_.unit_ref), custom_call_target="tpu_custom_call" | custom-call | bytes 3538944 | tf_op jit(solution)/shard_map/pallas_call | solution.py:46
  33.4 0.8 %shard_map.97 = (bf16[192,1024]{1,0:T(8,128)(2,1)S(1)}, bf16[192,1024]{1,0:T(8,128)(2,1)S(1)}) custom-call(bf16[768,768]{1,0:T(8,128)(2,1)S(1)} %get-tuple-element.97.weight_ref, bf16[768,1024]{1,0:T(8,128)(2,1)S(1)} %get-tuple-element.103.image_ref, f32[768,1024]{1,0:T(8,128)S(1)} %get-tuple-element.101.acc_ref), custom_call_target="tpu_custom_call" | custom-call | bytes 6684672 | tf_op jit(solution)/shard_map/pallas_call | solution.py:46
  34.2 0.1 collective-permute-start.9
  34.3 0.5 collective-permute-start.10
  34.8 1.5 %collective-permute-start.15 = (bf16[256,1024]{1,0:T(8,128)(2,1)S(1)}, bf16[256,1024]{1,0:T(8,128)(2,1)S(1)}, u32[]{:S(2)}, u32[]{:S(2)}) collective-permute-start(bf16[256,1024]{1,0:T(8,128)(2,1)S(1)} %get-tuple-element.117), channel_id=1, source_target_pairs={{0,8},{4,20},{8,0},{12,28},{16,24},{20,4},{24,16},{28,12},{1,9},{5... | collective-permute-start | bytes 1572872 | tf_op jit(solution)/shard_map/ppermute | solution.py:439
  36.3 0.5 collective-permute-start.17
  36.8 0.8 %shard_map.98.refs_5_ = f32[384,1024]{1,0:T(8,128)S(1)} custom-call(bf16[768,768]{1,0:T(8,128)(2,1)S(1)} %get-tuple-element.97.weight_ref, bf16[768,1024]{1,0:T(8,128)(2,1)S(1)} %get-tuple-element.103.image_ref, f32[768,1024]{1,0:T(8,128)S(1)} %get-tuple-element.101.acc_ref), custom_call_target="tpu_custom_call" | custom-call | bytes 7471104 | tf_op jit(solution)/shard_map/pallas_call | solution.py:46
  37.7 0.6 %shard_map.99 = (bf16[384,256]{1,0:T(8,128)(2,1)S(1)}, bf16[384,256]{1,0:T(8,128)(2,1)S(1)}, bf16[384,256]{1,0:T(8,128)(2,1)S(1)}, bf16[384,256]{1,0:T(8,128)(2,1)S(1)}) custom-call(f32[384,128]{1,0:T(8,128)S(1)} %get-tuple-element.93.refs_0_, bf16[384,256]{1,0:T(8,128)(2,1)S(1)} %get-tuple-element.75.refs_0_.refs_1_, ...), custom_call_target="tpu_custom_call" | custom-call | bytes 4128768 | tf_op jit(solution)/shard_map/pallas_call | solution.py:46
  38.3 3.3 %collective-permute-start.11 = (bf16[384,256]{1,0:T(8,128)(2,1)S(1)}, bf16[384,256]{1,0:T(8,128)(2,1)S(1)}, u32[]{:S(2)}, u32[]{:S(2)}) collective-permute-start(bf16[384,256]{1,0:T(8,128)(2,1)S(1)} %get-tuple-element.108), channel_id=1, source_target_pairs={{0,3},{1,2},{2,1},{3,0},{4,7},{5,6},{6,5},{7,4},{8,11},{9,10},{10,... | collective-permute-start | bytes 589832 | tf_op jit(solution)/shard_map/ppermute | solution.py:434
  41.6 0.4 collective-permute-start.12
  42.0 0.7 %collective-permute-start.13 = (bf16[384,256]{1,0:T(8,128)(2,1)S(1)}, bf16[384,256]{1,0:T(8,128)(2,1)S(1)}, u32[]{:S(2)}, u32[]{:S(2)}) collective-permute-start(bf16[384,256]{1,0:T(8,128)(2,1)S(1)} %get-tuple-element.110), channel_id=1, source_target_pairs={{0,1},{1,0},{2,3},{3,2},{4,5},{5,4},{6,7},{7,6},{8,9},{9,8},{10,11... | collective-permute-start | bytes 589832 | tf_op jit(solution)/shard_map/ppermute | solution.py:434
  42.7 0.8 %shard_map.100 = (f32[384,1024]{1,0:T(8,128)S(1)}, bf16[384,1024]{1,0:T(8,128)(2,1)S(1)}) custom-call(bf16[768,768]{1,0:T(8,128)(2,1)S(1)} %get-tuple-element.113.weight_ref, bf16[768,1024]{1,0:T(8,128)(2,1)S(1)} %get-tuple-element.89.refs_6_.unit_ref, bf16[384,1024]{1,0:T(8,128)(2,1)S(1)} %collective-permute-done.14.add_ref), custom_call_target="tpu_custom_call" | custom-call | bytes 5898240 | tf_op jit(solution)/shard_map/pallas_call | solution.py:46
  43.5 0.8 %shard_map.101.refs_6_ = f32[384,1024]{1,0:T(8,128)S(1)} custom-call(bf16[768,384]{1,0:T(8,128)(2,1)S(1)} %get-tuple-element.95.refs_8_.weight_ref, bf16[768,1024]{1,0:T(8,128)(2,1)S(1)} %get-tuple-element.89.refs_6_.unit_ref, bf16[384,1024]{1,0:T(8,128)(2,1)S(1)} %get-tuple-element.115.add_ref), custom_call_target="tpu_custom_call" | custom-call | tf_op jit(solution)/shard_map/pallas_call | solution.py:46
  44.4 0.9 %collective-permute-done.15.in_ref = bf16[256,1024]{1,0:T(8,128)(2,1)S(1)} collective-permute-done((bf16[256,1024]{1,0:T(8,128)(2,1)S(1)}, bf16[256,1024]{1,0:T(8,128)(2,1)S(1)}, u32[]{:S(2)}, u32[]{:S(2)}) %collective-permute-start.15) | collective-permute-done | bytes 524320 | tf_op jit(solution)/shard_map/ppermute | solution.py:439
  45.2 0.1 shard_map.102
  45.3 1.0 %collective-permute-start.16 = (bf16[256,1024]{1,0:T(8,128)(2,1)S(1)}, bf16[256,1024]{1,0:T(8,128)(2,1)S(1)}, u32[]{:S(2)}, u32[]{:S(2)}) collective-permute-start(bf16[256,1024]{1,0:T(8,128)(2,1)S(1)} %shard_map.102), channel_id=1, source_target_pairs={{0,16},{4,12},{8,24},{12,4},{16,0},{20,28},{24,8},{28,20},{1,17},{... | collective-permute-start | bytes 1572872 | tf_op jit(solution)/shard_map/ppermute | solution.py:439
  46.3 1.8 %collective-permute-done.17.in_ref = bf16[128,1024]{1,0:T(8,128)(2,1)S(1)} collective-permute-done((bf16[128,1024]{1,0:T(8,128)(2,1)S(1)}, bf16[128,1024]{1,0:T(8,128)(2,1)S(1)}, u32[]{:S(2)}, u32[]{:S(2)}) %collective-permute-start.17) | collective-permute-done | bytes 262176 | tf_op jit(solution)/shard_map/ppermute | solution.py:439
  48.2 0.9 %collective-permute-start.18 = (bf16[128,1024]{1,0:T(8,128)(2,1)S(1)}, bf16[128,1024]{1,0:T(8,128)(2,1)S(1)}, u32[]{:S(2)}, u32[]{:S(2)}) collective-permute-start(bf16[128,1024]{1,0:T(8,128)(2,1)S(1)} %shard_map.103), channel_id=1, source_target_pairs={{0,16},{4,12},{8,24},{12,4},{16,0},{20,28},{24,8},{28,20},{1,17},{... | collective-permute-start | bytes 786440 | tf_op jit(solution)/shard_map/ppermute | solution.py:439
  49.1 10.1 %collective-permute-done.12.refs_1_.refs_2_ = bf16[384,256]{1,0:T(8,128)(2,1)S(1)} collective-permute-done((bf16[384,256]{1,0:T(8,128)(2,1)S(1)}, bf16[384,256]{1,0:T(8,128)(2,1)S(1)}, u32[]{:S(2)}, u32[]{:S(2)}) %collective-permute-start.12) | collective-permute-done | bytes 196640 | tf_op jit(solution)/shard_map/ppermute | solution.py:434
  59.2 1.6 %shard_map.105 = (bf16[1536,256]{1,0:T(8,128)(2,1)}, bf16[384,1024]{1,0:T(8,128)(2,1)}) custom-call(bf16[384,256]{1,0:T(8,128)(2,1)S(1)} %get-tuple-element.107.refs_0_, bf16[384,256]{1,0:T(8,128)(2,1)S(1)} %collective-permute-done.11.refs_0_.refs_1_, bf16[384,256]{1,0:T(8,128)(2,1)S(1)} %collective-permute-done.12.refs_1_.refs_2_, ...), custom_call_target="tpu_custom_call" | custom-call | bytes 5705728 | tf_op jit(solution)/shard_map/pallas_call | solution.py:46
  (18 shorter events, 0.1 us)
Async XLA Ops:
  0.6 14.8 %collective-permute-start = (bf16[384,1024]{1,0:T(8,128)(2,1)}, bf16[384,1024]{1,0:T(8,128)(2,1)S(1)}, u32[]{:S(2)}, u32[]{:S(2)}) collective-permute-start(bf16[384,1024]{1,0:T(8,128)(2,1)} %raw_ref.1), channel_id=1, source_target_pairs={{0,16},{4,12},{8,24},{12,4},{16,0},{20,28},{24,8},{28,20},{1,17},{... | collective-permute-start | bytes 2359304 | tf_op jit(solution)/shard_map/ppermute | solution.py:439
  3.7 1.1 %copy-start = (bf16[1536,256]{1,0:T(8,128)(2,1)S(1)}, bf16[1536,256]{1,0:T(8,128)(2,1)}, u32[]{:S(2)}) copy-start(bf16[1536,256]{1,0:T(8,128)(2,1)} %text_ref.1) | copy-start | bytes 2359300
  4.8 8.6 %copy-start.1 = (s32[12288]{0:T(1024)S(1)}, s32[12288]{0:T(1024)}, u32[]{:S(2)}) copy-start(s32[12288]{0:T(1024)} %param.11) | copy-start | bytes 147460
  4.8 8.6 %copy-start.2 = (s32[12288]{0:T(1024)S(1)}, s32[12288]{0:T(1024)}, u32[]{:S(2)}) copy-start(s32[12288]{0:T(1024)} %param.12) | copy-start | bytes 147460
  4.8 8.6 %copy-start.3 = (s32[96,8,3]{0,1,2:T(8,128)S(1)}, s32[96,8,3]{0,1,2:T(8,128)}, u32[]{:S(2)}) copy-start(s32[96,8,3]{0,1,2:T(8,128)} %param.13) | copy-start | bytes 27652
  4.9 18.3 %collective-permute-start.1 = (bf16[384,256]{1,0:T(8,128)(2,1)S(1)}, bf16[384,256]{1,0:T(8,128)(2,1)S(1)}, u32[]{:S(2)}, u32[]{:S(2)}) collective-permute-start(bf16[384,256]{1,0:T(8,128)(2,1)S(1)} %get-tuple-element.76), channel_id=1, source_target_pairs={{0,2},{1,3},{2,0},{3,1},{4,6},{5,7},{6,4},{7,5},{8,10},{9,11},{10,... | collective-permute-start | bytes 589832 | tf_op jit(solution)/shard_map/ppermute | solution.py:434
  7.5 15.6 %collective-permute-start.2 = (bf16[384,256]{1,0:T(8,128)(2,1)S(1)}, bf16[384,256]{1,0:T(8,128)(2,1)S(1)}, u32[]{:S(2)}, u32[]{:S(2)}) collective-permute-start(bf16[384,256]{1,0:T(8,128)(2,1)S(1)} %get-tuple-element.77), channel_id=1, source_target_pairs={{0,3},{1,2},{2,1},{3,0},{4,7},{5,6},{6,5},{7,4},{8,11},{9,10},{10,... | collective-permute-start | bytes 589832 | tf_op jit(solution)/shard_map/ppermute | solution.py:434
  8.9 14.3 %collective-permute-start.3 = (bf16[384,256]{1,0:T(8,128)(2,1)S(1)}, bf16[384,256]{1,0:T(8,128)(2,1)S(1)}, u32[]{:S(2)}, u32[]{:S(2)}) collective-permute-start(bf16[384,256]{1,0:T(8,128)(2,1)S(1)} %get-tuple-element.78), channel_id=1, source_target_pairs={{0,1},{1,0},{2,3},{3,2},{4,5},{5,4},{6,7},{7,6},{8,9},{9,8},{10,11... | collective-permute-start | bytes 589832 | tf_op jit(solution)/shard_map/ppermute | solution.py:434
  10.5 12.3 %collective-permute-start.4 = (bf16[384,1024]{1,0:T(8,128)(2,1)}, bf16[384,1024]{1,0:T(8,128)(2,1)S(1)}, u32[]{:S(2)}, u32[]{:S(2)}) collective-permute-start(bf16[384,1024]{1,0:T(8,128)(2,1)} %raw_ref.1), channel_id=1, source_target_pairs={{0,8},{4,20},{8,0},{12,28},{16,24},{20,4},{24,16},{28,12},{1,9},{5... | collective-permute-start | bytes 2359304 | tf_op jit(solution)/shard_map/ppermute | solution.py:439
  15.4 15.8 %collective-permute-start.8 = (bf16[384,1024]{1,0:T(8,128)(2,1)S(1)}, bf16[384,1024]{1,0:T(8,128)(2,1)S(1)}, u32[]{:S(2)}, u32[]{:S(2)}) collective-permute-start(bf16[384,1024]{1,0:T(8,128)(2,1)S(1)} %collective-permute-done.raw_ref), channel_id=1, source_target_pairs={{0,8},{4,20},{8,0},{12,28},{16,24},{20,4},{24,16},{28,12},{1,9},{5... | collective-permute-start | bytes 2359304 | tf_op jit(solution)/shard_map/ppermute | solution.py:439
  23.5 2.1 %collective-permute-start.5 = (bf16[128,1024]{1,0:T(8,128)(2,1)S(1)}, bf16[128,1024]{1,0:T(8,128)(2,1)S(1)}, u32[]{:S(2)}, u32[]{:S(2)}) collective-permute-start(bf16[128,1024]{1,0:T(8,128)(2,1)S(1)} %get-tuple-element.86), channel_id=1, source_target_pairs={{0,4},{4,0},{8,12},{12,8},{16,20},{20,16},{24,28},{28,24},{1,5},{5... | collective-permute-start | bytes 786440 | tf_op jit(solution)/shard_map/ppermute | solution.py:434
  23.6 2.0 %collective-permute-start.6 = (bf16[128,1024]{1,0:T(8,128)(2,1)S(1)}, bf16[128,1024]{1,0:T(8,128)(2,1)S(1)}, u32[]{:S(2)}, u32[]{:S(2)}) collective-permute-start(bf16[128,1024]{1,0:T(8,128)(2,1)S(1)} %get-tuple-element.87), channel_id=1, source_target_pairs={{0,4},{4,0},{8,12},{12,8},{16,20},{20,16},{24,28},{28,24},{1,5},{5... | collective-permute-start | bytes 786440 | tf_op jit(solution)/shard_map/ppermute | solution.py:434
  24.1 1.8 %collective-permute-start.7 = (bf16[128,1024]{1,0:T(8,128)(2,1)S(1)}, bf16[128,1024]{1,0:T(8,128)(2,1)S(1)}, u32[]{:S(2)}, u32[]{:S(2)}) collective-permute-start(bf16[128,1024]{1,0:T(8,128)(2,1)S(1)} %get-tuple-element.88), channel_id=1, source_target_pairs={{0,4},{4,0},{8,12},{12,8},{16,20},{20,16},{24,28},{28,24},{1,5},{5... | collective-permute-start | bytes 786440 | tf_op jit(solution)/shard_map/ppermute | solution.py:434
  27.2 14.8 %collective-permute-start.14 = (bf16[384,1024]{1,0:T(8,128)(2,1)S(1)}, bf16[384,1024]{1,0:T(8,128)(2,1)S(1)}, u32[]{:S(2)}, u32[]{:S(2)}) collective-permute-start(bf16[384,1024]{1,0:T(8,128)(2,1)S(1)} %get-tuple-element.114), channel_id=1, source_target_pairs={{0,8},{4,20},{8,0},{12,28},{16,24},{20,4},{24,16},{28,12},{1,9},{5... | collective-permute-start | bytes 2359304 | tf_op jit(solution)/shard_map/ppermute | solution.py:439
  34.2 3.4 %collective-permute-start.9 = (bf16[192,1024]{1,0:T(8,128)(2,1)S(1)}, bf16[192,1024]{1,0:T(8,128)(2,1)S(1)}, u32[]{:S(2)}, u32[]{:S(2)}) collective-permute-start(bf16[192,1024]{1,0:T(8,128)(2,1)S(1)} %get-tuple-element.104), channel_id=1, source_target_pairs={{0,4},{4,0},{8,12},{12,8},{16,20},{20,16},{24,28},{28,24},{1,5},{5... | collective-permute-start | bytes 1179656 | tf_op jit(solution)/shard_map/ppermute | solution.py:434
  34.3 3.3 %collective-permute-start.10 = (bf16[192,1024]{1,0:T(8,128)(2,1)S(1)}, bf16[192,1024]{1,0:T(8,128)(2,1)S(1)}, u32[]{:S(2)}, u32[]{:S(2)}) collective-permute-start(bf16[192,1024]{1,0:T(8,128)(2,1)S(1)} %get-tuple-element.105), channel_id=1, source_target_pairs={{0,4},{4,0},{8,12},{12,8},{16,20},{20,16},{24,28},{28,24},{1,5},{5... | collective-permute-start | bytes 1179656 | tf_op jit(solution)/shard_map/ppermute | solution.py:434
  34.8 10.4 %collective-permute-start.15 = (bf16[256,1024]{1,0:T(8,128)(2,1)S(1)}, bf16[256,1024]{1,0:T(8,128)(2,1)S(1)}, u32[]{:S(2)}, u32[]{:S(2)}) collective-permute-start(bf16[256,1024]{1,0:T(8,128)(2,1)S(1)} %get-tuple-element.117), channel_id=1, source_target_pairs={{0,8},{4,20},{8,0},{12,28},{16,24},{20,4},{24,16},{28,12},{1,9},{5... | collective-permute-start | bytes 1572872 | tf_op jit(solution)/shard_map/ppermute | solution.py:439
  36.3 11.9 %collective-permute-start.17 = (bf16[128,1024]{1,0:T(8,128)(2,1)S(1)}, bf16[128,1024]{1,0:T(8,128)(2,1)S(1)}, u32[]{:S(2)}, u32[]{:S(2)}) collective-permute-start(bf16[128,1024]{1,0:T(8,128)(2,1)S(1)} %get-tuple-element.119), channel_id=1, source_target_pairs={{0,8},{4,20},{8,0},{12,28},{16,24},{20,4},{24,16},{28,12},{1,9},{5... | collective-permute-start | bytes 786440 | tf_op jit(solution)/shard_map/ppermute | solution.py:439
  38.3 10.8 %collective-permute-start.11 = (bf16[384,256]{1,0:T(8,128)(2,1)S(1)}, bf16[384,256]{1,0:T(8,128)(2,1)S(1)}, u32[]{:S(2)}, u32[]{:S(2)}) collective-permute-start(bf16[384,256]{1,0:T(8,128)(2,1)S(1)} %get-tuple-element.108), channel_id=1, source_target_pairs={{0,3},{1,2},{2,1},{3,0},{4,7},{5,6},{6,5},{7,4},{8,11},{9,10},{10,... | collective-permute-start | bytes 589832 | tf_op jit(solution)/shard_map/ppermute | solution.py:434
  41.6 17.6 %collective-permute-start.12 = (bf16[384,256]{1,0:T(8,128)(2,1)S(1)}, bf16[384,256]{1,0:T(8,128)(2,1)S(1)}, u32[]{:S(2)}, u32[]{:S(2)}) collective-permute-start(bf16[384,256]{1,0:T(8,128)(2,1)S(1)} %get-tuple-element.109), channel_id=1, source_target_pairs={{0,2},{1,3},{2,0},{3,1},{4,6},{5,7},{6,4},{7,5},{8,10},{9,11},{10,... | collective-permute-start | bytes 589832 | tf_op jit(solution)/shard_map/ppermute | solution.py:434
  42.0 17.2 %collective-permute-start.13 = (bf16[384,256]{1,0:T(8,128)(2,1)S(1)}, bf16[384,256]{1,0:T(8,128)(2,1)S(1)}, u32[]{:S(2)}, u32[]{:S(2)}) collective-permute-start(bf16[384,256]{1,0:T(8,128)(2,1)S(1)} %get-tuple-element.110), channel_id=1, source_target_pairs={{0,1},{1,0},{2,3},{3,2},{4,5},{5,4},{6,7},{7,6},{8,9},{9,8},{10,11... | collective-permute-start | bytes 589832 | tf_op jit(solution)/shard_map/ppermute | solution.py:434
  45.3 13.9 %collective-permute-start.16 = (bf16[256,1024]{1,0:T(8,128)(2,1)S(1)}, bf16[256,1024]{1,0:T(8,128)(2,1)S(1)}, u32[]{:S(2)}, u32[]{:S(2)}) collective-permute-start(bf16[256,1024]{1,0:T(8,128)(2,1)S(1)} %shard_map.102), channel_id=1, source_target_pairs={{0,16},{4,12},{8,24},{12,4},{16,0},{20,28},{24,8},{28,20},{1,17},{... | collective-permute-start | bytes 1572872 | tf_op jit(solution)/shard_map/ppermute | solution.py:439
  48.2 11.0 %collective-permute-start.18 = (bf16[128,1024]{1,0:T(8,128)(2,1)S(1)}, bf16[128,1024]{1,0:T(8,128)(2,1)S(1)}, u32[]{:S(2)}, u32[]{:S(2)}) collective-permute-start(bf16[128,1024]{1,0:T(8,128)(2,1)S(1)} %shard_map.103), channel_id=1, source_target_pairs={{0,16},{4,12},{8,24},{12,4},{16,0},{20,28},{24,8},{28,20},{1,17},{... | collective-permute-start | bytes 786440 | tf_op jit(solution)/shard_map/ppermute | solution.py:439

commit v19 on v17

--- a/solution.py
+++ b/solution.py
@@ -592,7 +592,7 @@
         lists + [units, own_images, own_weights, from_far],
         limit=16,
     )
-    sizes = [rows - TILE, TILE]
+    sizes = [rows // 2] * 2
     far_sum = call_kernel(
         far_sum_body, [bf16(size) for size in sizes], [far_weights, units], limit=16
     )

time: 59.2 us -> 59.7 us (level)
  waiting for transfers between devices: 16.4 us -> 17.2 us
  starting transfers between devices: 23.1 us -> 22.4 us
    ppermute x8, waiting for transfers between devices: 8.61 us -> 11 us  [swap_near(): lax.ppermute(value, 'blk', [(i, i ^ neighbour_bits(i)[which]) for i in ra...]
    ppermute x11, waiting for transfers between devices: 7.79 us -> 6.23 us  [swap(): return lax.ppermute(value, axis, [(i, i ^ bits) for i in range(count)])]
    ppermute x8, starting transfers between devices: 13.4 us -> 12.7 us  [swap_near(): lax.ppermute(value, 'blk', [(i, i ^ neighbour_bits(i)[which]) for i in ra...]
where the time goes in v19:
time: 59.7 us; the launch traced here: 59.1 us
  starting transfers between devices  22.4 us (38%)
  waiting for transfers between devices  17.2 us (29%)
  Pallas kernels  16.2 us (27%)
  between operations  2.14 us (4%)
  local copies, waits for them, and re-layouts  1.14 us (2%)
    pallas_call x20, Pallas kernels, call_kernel(): pl.pallas_call(body, out_shape=outs, in_specs=specs, out_specs=[ANY_SPEC...  16.2 us
    ppermute x8, starting transfers between devices, swap_near(): lax.ppermute(value, 'blk', [(i, i ^ neighbour_bits(i)[which]) for i in ra...  12.7 us
    ppermute x8, waiting for transfers between devices, swap_near(): lax.ppermute(value, 'blk', [(i, i ^ neighbour_bits(i)[which]) for i in ra...  11 us
    ppermute x11, starting transfers between devices, swap(): return lax.ppermute(value, axis, [(i, i ^ bits) for i in range(count)])  9.73 us
    ppermute x11, waiting for transfers between devices, swap(): return lax.ppermute(value, axis, [(i, i ^ bits) for i in range(count)])  6.23 us
  transfers between devices with their start and end apart: 19, of which 9 were waited for; matrix products, arithmetic and copies ran while one was open for 0% of the time, Pallas kernels for 25%

profile of v19, /device:TPU:0, one launch (start us, length us, event | category | flops | bytes accessed | tf_op | source)
XLA Modules:
  0.0 59.1 jit_solution(12373250395886743804)
XLA Ops:
  0.6 3.0 %collective-permute-start = (bf16[384,1024]{1,0:T(8,128)(2,1)}, bf16[384,1024]{1,0:T(8,128)(2,1)S(1)}, u32[]{:S(2)}, u32[]{:S(2)}) collective-permute-start(bf16[384,1024]{1,0:T(8,128)(2,1)} %raw_ref.1), channel_id=1, source_target_pairs={{0,16},{4,12},{8,24},{12,4},{16,0},{20,28},{24,8},{28,20},{1,17},{... | collective-permute-start | bytes 2359304 | tf_op jit(solution)/shard_map/ppermute | solution.py:434
  3.7 1.1 %copy-done = bf16[1536,256]{1,0:T(8,128)(2,1)S(1)} copy-done((bf16[1536,256]{1,0:T(8,128)(2,1)S(1)}, bf16[1536,256]{1,0:T(8,128)(2,1)}, u32[]{:S(2)}) %copy-start) | copy-done | bytes 786456
  4.8 0.1 shard_map.88
  4.9 2.7 %collective-permute-start.1 = (bf16[384,256]{1,0:T(8,128)(2,1)S(1)}, bf16[384,256]{1,0:T(8,128)(2,1)S(1)}, u32[]{:S(2)}, u32[]{:S(2)}) collective-permute-start(bf16[384,256]{1,0:T(8,128)(2,1)S(1)} %get-tuple-element.76), channel_id=1, source_target_pairs={{0,2},{1,3},{2,0},{3,1},{4,6},{5,7},{6,4},{7,5},{8,10},{9,11},{10,... | collective-permute-start | bytes 589832 | tf_op jit(solution)/shard_map/ppermute | solution.py:429
  7.5 1.3 %collective-permute-start.2 = (bf16[384,256]{1,0:T(8,128)(2,1)S(1)}, bf16[384,256]{1,0:T(8,128)(2,1)S(1)}, u32[]{:S(2)}, u32[]{:S(2)}) collective-permute-start(bf16[384,256]{1,0:T(8,128)(2,1)S(1)} %get-tuple-element.77), channel_id=1, source_target_pairs={{0,3},{1,2},{2,1},{3,0},{4,7},{5,6},{6,5},{7,4},{8,11},{9,10},{10,... | collective-permute-start | bytes 589832 | tf_op jit(solution)/shard_map/ppermute | solution.py:429
  8.9 0.2 collective-permute-start.3
  9.1 1.4 %shard_map.86 = (bf16[384,1024]{1,0:T(8,128)(2,1)S(1)}, bf16[384,1024]{1,0:T(8,128)(2,1)S(1)}, f32[384,128]{1,0:T(8,128)S(1)}) custom-call(bf16[384,1024]{1,0:T(8,128)(2,1)} %raw_ref.1), custom_call_target="tpu_custom_call" | custom-call | bytes 2555904 | tf_op jit(solution)/shard_map/pallas_call | solution.py:46
  10.5 1.6 %collective-permute-start.4 = (bf16[384,1024]{1,0:T(8,128)(2,1)}, bf16[384,1024]{1,0:T(8,128)(2,1)S(1)}, u32[]{:S(2)}, u32[]{:S(2)}) collective-permute-start(bf16[384,1024]{1,0:T(8,128)(2,1)} %raw_ref.1), channel_id=1, source_target_pairs={{0,8},{4,20},{8,0},{12,28},{16,24},{20,4},{24,16},{28,12},{1,9},{5... | collective-permute-start | bytes 2359304 | tf_op jit(solution)/shard_map/ppermute | solution.py:434
  13.4 1.1 %shard_map.87 = (f32[2,128]{1,0:T(2,128)S(1)}, f32[72,128]{1,0:T(8,128)S(1)}, s32[12,128]{1,0:T(8,128)S(1)}, s32[768,128]{1,0:T(8,128)S(1)}, f32[384,128]{1,0:T(8,128)S(1)}, /*index=5*/f32[4,128]{1,0:T(4,128)S(1)}) custom-call(f32[1]{0:T(128)S(6)} %copy.9.refs_0_, f32[1]{0:T(128)S(6)} %copy.10.refs_1_, s32[3,8,96]{2,1,0:T(8,128)S(1)} %bitcast.5, ...), custom_call_target="tpu_custom_call" | custom-call | bytes 743432 | tf_op jit(solution)/shard_map/pallas_call | solution.py:46
  14.5 0.9 %collective-permute-done.raw_ref = bf16[384,1024]{1,0:T(8,128)(2,1)S(1)} collective-permute-done((bf16[384,1024]{1,0:T(8,128)(2,1)}, bf16[384,1024]{1,0:T(8,128)(2,1)S(1)}, u32[]{:S(2)}, u32[]{:S(2)}) %collective-permute-start) | collective-permute-done | bytes 786464 | tf_op jit(solution)/shard_map/ppermute | solution.py:434
  15.4 3.3 %collective-permute-start.8 = (bf16[384,1024]{1,0:T(8,128)(2,1)S(1)}, bf16[384,1024]{1,0:T(8,128)(2,1)S(1)}, u32[]{:S(2)}, u32[]{:S(2)}) collective-permute-start(bf16[384,1024]{1,0:T(8,128)(2,1)S(1)} %collective-permute-done.raw_ref), channel_id=1, source_target_pairs={{0,8},{4,20},{8,0},{12,28},{16,24},{20,4},{24,16},{28,12},{1,9},{5... | collective-permute-start | bytes 2359304 | tf_op jit(solution)/shard_map/ppermute | solution.py:434
  18.7 0.2 shard_map.89.second_unit_ref
  19.0 3.8 %collective-permute-done.4.first_ref = bf16[384,1024]{1,0:T(8,128)(2,1)S(1)} collective-permute-done((bf16[384,1024]{1,0:T(8,128)(2,1)}, bf16[384,1024]{1,0:T(8,128)(2,1)S(1)}, u32[]{:S(2)}, u32[]{:S(2)}) %collective-permute-start.4) | collective-permute-done | bytes 786464 | tf_op jit(solution)/shard_map/ppermute | solution.py:434
  22.8 0.3 shard_map.90.refs_7_
  23.1 0.4 shard_map.91
  23.5 0.1 collective-permute-start.5
  23.6 0.5 collective-permute-start.6
  24.1 0.1 collective-permute-start.7
  24.2 1.4 %shard_map.92 = (bf16[384,384]{1,0:T(8,128)(2,1)S(1)}, bf16[384,768]{1,0:T(8,128)(2,1)S(1)}) custom-call(f32[2,128]{1,0:T(2,128)S(1)} %get-tuple-element.69.refs_0_, f32[72,128]{1,0:T(8,128)S(1)} %get-tuple-element.70.refs_1_, s32[12,128]{1,0:T(8,128)S(1)} %get-tuple-element.71.refs_2_, s32[768,128]{1,0:T(8,128)S(1)} %get-tuple-element.72.refs_3_, ...), custom_call_target="tpu_custom_call" | custom-call | bytes 4666368 | tf_op jit(solution)/shard_map/pallas_call | solution.py:46
  25.6 0.2 collective-permute-done.7.refs_11_
  25.9 1.3 %shard_map.93 = (bf16[768,1024]{1,0:T(8,128)(2,1)S(1)}, bf16[768,384]{1,0:T(8,128)(2,1)S(1)}, bf16[384,1024]{1,0:T(8,128)(2,1)S(1)}) custom-call(f32[2,128]{1,0:T(2,128)S(1)} %get-tuple-element.69.refs_0_, f32[72,128]{1,0:T(8,128)S(1)} %get-tuple-element.70.refs_1_, s32[12,128]{1,0:T(8,128)S(1)} %get-tuple-element.71.refs_2_, ...), custom_call_target="tpu_custom_call" | custom-call | bytes 8107008 | tf_op jit(solution)/shard_map/pallas_call | solution.py:46
  27.2 1.6 %collective-permute-start.14 = (bf16[384,1024]{1,0:T(8,128)(2,1)S(1)}, bf16[384,1024]{1,0:T(8,128)(2,1)S(1)}, u32[]{:S(2)}, u32[]{:S(2)}) collective-permute-start(bf16[384,1024]{1,0:T(8,128)(2,1)S(1)} %get-tuple-element.114), channel_id=1, source_target_pairs={{0,8},{4,20},{8,0},{12,28},{16,24},{20,4},{24,16},{28,12},{1,9},{5... | collective-permute-start | bytes 2359304 | tf_op jit(solution)/shard_map/ppermute | solution.py:434
  28.8 2.2 %shard_map.94 = (bf16[768,384]{1,0:T(8,128)(2,1)S(1)}, f32[768,1024]{1,0:T(8,128)S(1)}, bf16[768,768]{1,0:T(8,128)(2,1)S(1)}) custom-call(f32[2,128]{1,0:T(2,128)S(1)} %get-tuple-element.69.refs_0_, f32[72,128]{1,0:T(8,128)S(1)} %get-tuple-element.70.refs_1_, s32[12,128]{1,0:T(8,128)S(1)} %get-tuple-element.71.refs_2_, ...), custom_call_target="tpu_custom_call" | custom-call | bytes 10957824 | tf_op jit(solution)/shard_map/pallas_call | solution.py:46
  31.0 0.2 collective-permute-done.8.refs_9_
  31.2 1.4 %shard_map.95 = (bf16[768,768]{1,0:T(8,128)(2,1)S(1)}, bf16[768,1024]{1,0:T(8,128)(2,1)S(1)}) custom-call(f32[2,128]{1,0:T(2,128)S(1)} %get-tuple-element.69.refs_0_, f32[72,128]{1,0:T(8,128)S(1)} %get-tuple-element.70.refs_1_, s32[12,128]{1,0:T(8,128)S(1)} %get-tuple-element.71.refs_2_, s32[768,128]{1,0:T(8,128)S(1)} %get-tuple-element.72.refs_3_, ...), custom_call_target="tpu_custom_call" | custom-call | bytes 7123968 | tf_op jit(solution)/shard_map/pallas_call | solution.py:46
  32.6 0.8 %shard_map.96 = (bf16[192,1024]{1,0:T(8,128)(2,1)S(1)}, bf16[192,1024]{1,0:T(8,128)(2,1)S(1)}) custom-call(bf16[768,768]{1,0:T(8,128)(2,1)S(1)} %get-tuple-element.97.weight_ref, bf16[768,1024]{1,0:T(8,128)(2,1)S(1)} %get-tuple-element.89.refs_6_.unit_ref), custom_call_target="tpu_custom_call" | custom-call | bytes 3538944 | tf_op jit(solution)/shard_map/pallas_call | solution.py:46
  33.4 0.8 %shard_map.97 = (bf16[192,1024]{1,0:T(8,128)(2,1)S(1)}, bf16[192,1024]{1,0:T(8,128)(2,1)S(1)}) custom-call(bf16[768,768]{1,0:T(8,128)(2,1)S(1)} %get-tuple-element.97.weight_ref, bf16[768,1024]{1,0:T(8,128)(2,1)S(1)} %get-tuple-element.103.image_ref, f32[768,1024]{1,0:T(8,128)S(1)} %get-tuple-element.101.acc_ref), custom_call_target="tpu_custom_call" | custom-call | bytes 6684672 | tf_op jit(solution)/shard_map/pallas_call | solution.py:46
  34.2 0.1 collective-permute-start.9
  34.3 0.5 collective-permute-start.10
  34.8 1.5 %collective-permute-start.15 = (bf16[192,1024]{1,0:T(8,128)(2,1)S(1)}, bf16[192,1024]{1,0:T(8,128)(2,1)S(1)}, u32[]{:S(2)}, u32[]{:S(2)}) collective-permute-start(bf16[192,1024]{1,0:T(8,128)(2,1)S(1)} %get-tuple-element.117), channel_id=1, source_target_pairs={{0,8},{4,20},{8,0},{12,28},{16,24},{20,4},{24,16},{28,12},{1,9},{5... | collective-permute-start | bytes 1179656 | tf_op jit(solution)/shard_map/ppermute | solution.py:434
  36.3 0.5 collective-permute-start.17
  36.8 0.8 %shard_map.98.refs_5_ = f32[384,1024]{1,0:T(8,128)S(1)} custom-call(bf16[768,768]{1,0:T(8,128)(2,1)S(1)} %get-tuple-element.97.weight_ref, bf16[768,1024]{1,0:T(8,128)(2,1)S(1)} %get-tuple-element.103.image_ref, f32[768,1024]{1,0:T(8,128)S(1)} %get-tuple-element.101.acc_ref), custom_call_target="tpu_custom_call" | custom-call | bytes 7471104 | tf_op jit(solution)/shard_map/pallas_call | solution.py:46
  37.7 0.6 %shard_map.99 = (bf16[384,256]{1,0:T(8,128)(2,1)S(1)}, bf16[384,256]{1,0:T(8,128)(2,1)S(1)}, bf16[384,256]{1,0:T(8,128)(2,1)S(1)}, bf16[384,256]{1,0:T(8,128)(2,1)S(1)}) custom-call(f32[384,128]{1,0:T(8,128)S(1)} %get-tuple-element.93.refs_0_, bf16[384,256]{1,0:T(8,128)(2,1)S(1)} %get-tuple-element.75.refs_0_.refs_1_, ...), custom_call_target="tpu_custom_call" | custom-call | bytes 4128768 | tf_op jit(solution)/shard_map/pallas_call | solution.py:46
  38.3 3.6 %collective-permute-start.11 = (bf16[384,256]{1,0:T(8,128)(2,1)S(1)}, bf16[384,256]{1,0:T(8,128)(2,1)S(1)}, u32[]{:S(2)}, u32[]{:S(2)}) collective-permute-start(bf16[384,256]{1,0:T(8,128)(2,1)S(1)} %get-tuple-element.108), channel_id=1, source_target_pairs={{0,2},{1,3},{2,0},{3,1},{4,6},{5,7},{6,4},{7,5},{8,10},{9,11},{10,... | collective-permute-start | bytes 589832 | tf_op jit(solution)/shard_map/ppermute | solution.py:429
  41.9 0.6 %collective-permute-start.12 = (bf16[384,256]{1,0:T(8,128)(2,1)S(1)}, bf16[384,256]{1,0:T(8,128)(2,1)S(1)}, u32[]{:S(2)}, u32[]{:S(2)}) collective-permute-start(bf16[384,256]{1,0:T(8,128)(2,1)S(1)} %get-tuple-element.109), channel_id=1, source_target_pairs={{0,3},{1,2},{2,1},{3,0},{4,7},{5,6},{6,5},{7,4},{8,11},{9,10},{10,... | collective-permute-start | bytes 589832 | tf_op jit(solution)/shard_map/ppermute | solution.py:429
  42.5 0.0 collective-permute-start.13
  42.6 0.8 %shard_map.100 = (f32[384,1024]{1,0:T(8,128)S(1)}, bf16[384,1024]{1,0:T(8,128)(2,1)S(1)}) custom-call(bf16[768,768]{1,0:T(8,128)(2,1)S(1)} %get-tuple-element.113.weight_ref, bf16[768,1024]{1,0:T(8,128)(2,1)S(1)} %get-tuple-element.89.refs_6_.unit_ref, bf16[384,1024]{1,0:T(8,128)(2,1)S(1)} %collective-permute-done.14.add_ref), custom_call_target="tpu_custom_call" | custom-call | bytes 5898240 | tf_op jit(solution)/shard_map/pallas_call | solution.py:46
  43.4 0.5 collective-permute-done.15.in_ref
  43.8 0.1 shard_map.102
  43.9 1.0 %collective-permute-start.16 = (bf16[192,1024]{1,0:T(8,128)(2,1)S(1)}, bf16[192,1024]{1,0:T(8,128)(2,1)S(1)}, u32[]{:S(2)}, u32[]{:S(2)}) collective-permute-start(bf16[192,1024]{1,0:T(8,128)(2,1)S(1)} %shard_map.102), channel_id=1, source_target_pairs={{0,16},{4,12},{8,24},{12,4},{16,0},{20,28},{24,8},{28,20},{1,17},{... | collective-permute-start | bytes 1179656 | tf_op jit(solution)/shard_map/ppermute | solution.py:434
  44.9 4.7 %collective-permute-done.17.in_ref = bf16[192,1024]{1,0:T(8,128)(2,1)S(1)} collective-permute-done((bf16[192,1024]{1,0:T(8,128)(2,1)S(1)}, bf16[192,1024]{1,0:T(8,128)(2,1)S(1)}, u32[]{:S(2)}, u32[]{:S(2)}) %collective-permute-start.17) | collective-permute-done | bytes 393248 | tf_op jit(solution)/shard_map/ppermute | solution.py:434
  49.6 0.1 shard_map.103
  49.7 0.2 collective-permute-start.18
  49.9 0.8 %shard_map.101.refs_6_ = f32[384,1024]{1,0:T(8,128)S(1)} custom-call(bf16[768,384]{1,0:T(8,128)(2,1)S(1)} %get-tuple-element.95.refs_8_.weight_ref, bf16[768,1024]{1,0:T(8,128)(2,1)S(1)} %get-tuple-element.89.refs_6_.unit_ref, bf16[384,1024]{1,0:T(8,128)(2,1)S(1)} %get-tuple-element.115.add_ref), custom_call_target="tpu_custom_call" | custom-call | tf_op jit(solution)/shard_map/pallas_call | solution.py:46
  50.7 5.0 %collective-permute-done.11.refs_0_.refs_1_ = bf16[384,256]{1,0:T(8,128)(2,1)S(1)} collective-permute-done((bf16[384,256]{1,0:T(8,128)(2,1)S(1)}, bf16[384,256]{1,0:T(8,128)(2,1)S(1)}, u32[]{:S(2)}, u32[]{:S(2)}) %collective-permute-start.11) | collective-permute-done | bytes 196640 | tf_op jit(solution)/shard_map/ppermute | solution.py:429
  55.6 1.0 %collective-permute-done.13.refs_2_.refs_3_ = bf16[384,256]{1,0:T(8,128)(2,1)S(1)} collective-permute-done((bf16[384,256]{1,0:T(8,128)(2,1)S(1)}, bf16[384,256]{1,0:T(8,128)(2,1)S(1)}, u32[]{:S(2)}, u32[]{:S(2)}) %collective-permute-start.13) | collective-permute-done | bytes 196640 | tf_op jit(solution)/shard_map/ppermute | solution.py:429
  56.7 0.9 %collective-permute-done.18.refs_8_ = bf16[192,1024]{1,0:T(8,128)(2,1)S(1)} collective-permute-done((bf16[192,1024]{1,0:T(8,128)(2,1)S(1)}, bf16[192,1024]{1,0:T(8,128)(2,1)S(1)}, u32[]{:S(2)}, u32[]{:S(2)}) %collective-permute-start.18) | collective-permute-done | bytes 393248 | tf_op jit(solution)/shard_map/ppermute | solution.py:434
  57.5 1.6 %shard_map.105 = (bf16[1536,256]{1,0:T(8,128)(2,1)}, bf16[384,1024]{1,0:T(8,128)(2,1)}) custom-call(bf16[384,256]{1,0:T(8,128)(2,1)S(1)} %get-tuple-element.107.refs_0_, bf16[384,256]{1,0:T(8,128)(2,1)S(1)} %collective-permute-done.11.refs_0_.refs_1_, bf16[384,256]{1,0:T(8,128)(2,1)S(1)} %collective-permute-done.12.refs_1_.refs_2_, ...), custom_call_target="tpu_custom_call" | custom-call | bytes 5705728 | tf_op jit(solution)/shard_map/pallas_call | solution.py:46
  (18 shorter events, 0.0 us)
Async XLA Ops:
  0.6 14.8 %collective-permute-start = (bf16[384,1024]{1,0:T(8,128)(2,1)}, bf16[384,1024]{1,0:T(8,128)(2,1)S(1)}, u32[]{:S(2)}, u32[]{:S(2)}) collective-permute-start(bf16[384,1024]{1,0:T(8,128)(2,1)} %raw_ref.1), channel_id=1, source_target_pairs={{0,16},{4,12},{8,24},{12,4},{16,0},{20,28},{24,8},{28,20},{1,17},{... | collective-permute-start | bytes 2359304 | tf_op jit(solution)/shard_map/ppermute | solution.py:434
  3.7 1.1 %copy-start = (bf16[1536,256]{1,0:T(8,128)(2,1)S(1)}, bf16[1536,256]{1,0:T(8,128)(2,1)}, u32[]{:S(2)}) copy-start(bf16[1536,256]{1,0:T(8,128)(2,1)} %text_ref.1) | copy-start | bytes 2359300
  4.8 8.6 %copy-start.1 = (s32[12288]{0:T(1024)S(1)}, s32[12288]{0:T(1024)}, u32[]{:S(2)}) copy-start(s32[12288]{0:T(1024)} %param.11) | copy-start | bytes 147460
  4.8 8.6 %copy-start.2 = (s32[12288]{0:T(1024)S(1)}, s32[12288]{0:T(1024)}, u32[]{:S(2)}) copy-start(s32[12288]{0:T(1024)} %param.12) | copy-start | bytes 147460
  4.8 8.6 %copy-start.3 = (s32[96,8,3]{0,1,2:T(8,128)S(1)}, s32[96,8,3]{0,1,2:T(8,128)}, u32[]{:S(2)}) copy-start(s32[96,8,3]{0,1,2:T(8,128)} %param.13) | copy-start | bytes 27652
  4.9 18.3 %collective-permute-start.1 = (bf16[384,256]{1,0:T(8,128)(2,1)S(1)}, bf16[384,256]{1,0:T(8,128)(2,1)S(1)}, u32[]{:S(2)}, u32[]{:S(2)}) collective-permute-start(bf16[384,256]{1,0:T(8,128)(2,1)S(1)} %get-tuple-element.76), channel_id=1, source_target_pairs={{0,2},{1,3},{2,0},{3,1},{4,6},{5,7},{6,4},{7,5},{8,10},{9,11},{10,... | collective-permute-start | bytes 589832 | tf_op jit(solution)/shard_map/ppermute | solution.py:429
  7.5 15.6 %collective-permute-start.2 = (bf16[384,256]{1,0:T(8,128)(2,1)S(1)}, bf16[384,256]{1,0:T(8,128)(2,1)S(1)}, u32[]{:S(2)}, u32[]{:S(2)}) collective-permute-start(bf16[384,256]{1,0:T(8,128)(2,1)S(1)} %get-tuple-element.77), channel_id=1, source_target_pairs={{0,3},{1,2},{2,1},{3,0},{4,7},{5,6},{6,5},{7,4},{8,11},{9,10},{10,... | collective-permute-start | bytes 589832 | tf_op jit(solution)/shard_map/ppermute | solution.py:429
  8.9 14.3 %collective-permute-start.3 = (bf16[384,256]{1,0:T(8,128)(2,1)S(1)}, bf16[384,256]{1,0:T(8,128)(2,1)S(1)}, u32[]{:S(2)}, u32[]{:S(2)}) collective-permute-start(bf16[384,256]{1,0:T(8,128)(2,1)S(1)} %get-tuple-element.78), channel_id=1, source_target_pairs={{0,1},{1,0},{2,3},{3,2},{4,5},{5,4},{6,7},{7,6},{8,9},{9,8},{10,11... | collective-permute-start | bytes 589832 | tf_op jit(solution)/shard_map/ppermute | solution.py:429
  10.5 12.3 %collective-permute-start.4 = (bf16[384,1024]{1,0:T(8,128)(2,1)}, bf16[384,1024]{1,0:T(8,128)(2,1)S(1)}, u32[]{:S(2)}, u32[]{:S(2)}) collective-permute-start(bf16[384,1024]{1,0:T(8,128)(2,1)} %raw_ref.1), channel_id=1, source_target_pairs={{0,8},{4,20},{8,0},{12,28},{16,24},{20,4},{24,16},{28,12},{1,9},{5... | collective-permute-start | bytes 2359304 | tf_op jit(solution)/shard_map/ppermute | solution.py:434
  15.4 15.8 %collective-permute-start.8 = (bf16[384,1024]{1,0:T(8,128)(2,1)S(1)}, bf16[384,1024]{1,0:T(8,128)(2,1)S(1)}, u32[]{:S(2)}, u32[]{:S(2)}) collective-permute-start(bf16[384,1024]{1,0:T(8,128)(2,1)S(1)} %collective-permute-done.raw_ref), channel_id=1, source_target_pairs={{0,8},{4,20},{8,0},{12,28},{16,24},{20,4},{24,16},{28,12},{1,9},{5... | collective-permute-start | bytes 2359304 | tf_op jit(solution)/shard_map/ppermute | solution.py:434
  23.5 2.1 %collective-permute-start.5 = (bf16[128,1024]{1,0:T(8,128)(2,1)S(1)}, bf16[128,1024]{1,0:T(8,128)(2,1)S(1)}, u32[]{:S(2)}, u32[]{:S(2)}) collective-permute-start(bf16[128,1024]{1,0:T(8,128)(2,1)S(1)} %get-tuple-element.86), channel_id=1, source_target_pairs={{0,4},{4,0},{8,12},{12,8},{16,20},{20,16},{24,28},{28,24},{1,5},{5... | collective-permute-start | bytes 786440 | tf_op jit(solution)/shard_map/ppermute | solution.py:429
  23.6 2.0 %collective-permute-start.6 = (bf16[128,1024]{1,0:T(8,128)(2,1)S(1)}, bf16[128,1024]{1,0:T(8,128)(2,1)S(1)}, u32[]{:S(2)}, u32[]{:S(2)}) collective-permute-start(bf16[128,1024]{1,0:T(8,128)(2,1)S(1)} %get-tuple-element.87), channel_id=1, source_target_pairs={{0,4},{4,0},{8,12},{12,8},{16,20},{20,16},{24,28},{28,24},{1,5},{5... | collective-permute-start | bytes 786440 | tf_op jit(solution)/shard_map/ppermute | solution.py:429
  24.1 1.8 %collective-permute-start.7 = (bf16[128,1024]{1,0:T(8,128)(2,1)S(1)}, bf16[128,1024]{1,0:T(8,128)(2,1)S(1)}, u32[]{:S(2)}, u32[]{:S(2)}) collective-permute-start(bf16[128,1024]{1,0:T(8,128)(2,1)S(1)} %get-tuple-element.88), channel_id=1, source_target_pairs={{0,4},{4,0},{8,12},{12,8},{16,20},{20,16},{24,28},{28,24},{1,5},{5... | collective-permute-start | bytes 786440 | tf_op jit(solution)/shard_map/ppermute | solution.py:429
  27.2 15.3 %collective-permute-start.14 = (bf16[384,1024]{1,0:T(8,128)(2,1)S(1)}, bf16[384,1024]{1,0:T(8,128)(2,1)S(1)}, u32[]{:S(2)}, u32[]{:S(2)}) collective-permute-start(bf16[384,1024]{1,0:T(8,128)(2,1)S(1)} %get-tuple-element.114), channel_id=1, source_target_pairs={{0,8},{4,20},{8,0},{12,28},{16,24},{20,4},{24,16},{28,12},{1,9},{5... | collective-permute-start | bytes 2359304 | tf_op jit(solution)/shard_map/ppermute | solution.py:434
  34.2 3.4 %collective-permute-start.9 = (bf16[192,1024]{1,0:T(8,128)(2,1)S(1)}, bf16[192,1024]{1,0:T(8,128)(2,1)S(1)}, u32[]{:S(2)}, u32[]{:S(2)}) collective-permute-start(bf16[192,1024]{1,0:T(8,128)(2,1)S(1)} %get-tuple-element.104), channel_id=1, source_target_pairs={{0,4},{4,0},{8,12},{12,8},{16,20},{20,16},{24,28},{28,24},{1,5},{5... | collective-permute-start | bytes 1179656 | tf_op jit(solution)/shard_map/ppermute | solution.py:429
  34.3 3.3 %collective-permute-start.10 = (bf16[192,1024]{1,0:T(8,128)(2,1)S(1)}, bf16[192,1024]{1,0:T(8,128)(2,1)S(1)}, u32[]{:S(2)}, u32[]{:S(2)}) collective-permute-start(bf16[192,1024]{1,0:T(8,128)(2,1)S(1)} %get-tuple-element.105), channel_id=1, source_target_pairs={{0,4},{4,0},{8,12},{12,8},{16,20},{20,16},{24,28},{28,24},{1,5},{5... | collective-permute-start | bytes 1179656 | tf_op jit(solution)/shard_map/ppermute | solution.py:429
  34.8 9.0 %collective-permute-start.15 = (bf16[192,1024]{1,0:T(8,128)(2,1)S(1)}, bf16[192,1024]{1,0:T(8,128)(2,1)S(1)}, u32[]{:S(2)}, u32[]{:S(2)}) collective-permute-start(bf16[192,1024]{1,0:T(8,128)(2,1)S(1)} %get-tuple-element.117), channel_id=1, source_target_pairs={{0,8},{4,20},{8,0},{12,28},{16,24},{20,4},{24,16},{28,12},{1,9},{5... | collective-permute-start | bytes 1179656 | tf_op jit(solution)/shard_map/ppermute | solution.py:434
  36.3 13.3 %collective-permute-start.17 = (bf16[192,1024]{1,0:T(8,128)(2,1)S(1)}, bf16[192,1024]{1,0:T(8,128)(2,1)S(1)}, u32[]{:S(2)}, u32[]{:S(2)}) collective-permute-start(bf16[192,1024]{1,0:T(8,128)(2,1)S(1)} %get-tuple-element.119), channel_id=1, source_target_pairs={{0,8},{4,20},{8,0},{12,28},{16,24},{20,4},{24,16},{28,12},{1,9},{5... | collective-permute-start | bytes 1179656 | tf_op jit(solution)/shard_map/ppermute | solution.py:434
  38.3 17.4 %collective-permute-start.11 = (bf16[384,256]{1,0:T(8,128)(2,1)S(1)}, bf16[384,256]{1,0:T(8,128)(2,1)S(1)}, u32[]{:S(2)}, u32[]{:S(2)}) collective-permute-start(bf16[384,256]{1,0:T(8,128)(2,1)S(1)} %get-tuple-element.108), channel_id=1, source_target_pairs={{0,2},{1,3},{2,0},{3,1},{4,6},{5,7},{6,4},{7,5},{8,10},{9,11},{10,... | collective-permute-start | bytes 589832 | tf_op jit(solution)/shard_map/ppermute | solution.py:429
  41.9 13.7 %collective-permute-start.12 = (bf16[384,256]{1,0:T(8,128)(2,1)S(1)}, bf16[384,256]{1,0:T(8,128)(2,1)S(1)}, u32[]{:S(2)}, u32[]{:S(2)}) collective-permute-start(bf16[384,256]{1,0:T(8,128)(2,1)S(1)} %get-tuple-element.109), channel_id=1, source_target_pairs={{0,3},{1,2},{2,1},{3,0},{4,7},{5,6},{6,5},{7,4},{8,11},{9,10},{10,... | collective-permute-start | bytes 589832 | tf_op jit(solution)/shard_map/ppermute | solution.py:429
  42.5 14.1 %collective-permute-start.13 = (bf16[384,256]{1,0:T(8,128)(2,1)S(1)}, bf16[384,256]{1,0:T(8,128)(2,1)S(1)}, u32[]{:S(2)}, u32[]{:S(2)}) collective-permute-start(bf16[384,256]{1,0:T(8,128)(2,1)S(1)} %get-tuple-element.110), channel_id=1, source_target_pairs={{0,1},{1,0},{2,3},{3,2},{4,5},{5,4},{6,7},{7,6},{8,9},{9,8},{10,11... | collective-permute-start | bytes 589832 | tf_op jit(solution)/shard_map/ppermute | solution.py:429
  43.9 13.6 %collective-permute-start.16 = (bf16[192,1024]{1,0:T(8,128)(2,1)S(1)}, bf16[192,1024]{1,0:T(8,128)(2,1)S(1)}, u32[]{:S(2)}, u32[]{:S(2)}) collective-permute-start(bf16[192,1024]{1,0:T(8,128)(2,1)S(1)} %shard_map.102), channel_id=1, source_target_pairs={{0,16},{4,12},{8,24},{12,4},{16,0},{20,28},{24,8},{28,20},{1,17},{... | collective-permute-start | bytes 1179656 | tf_op jit(solution)/shard_map/ppermute | solution.py:434
  49.7 7.8 %collective-permute-start.18 = (bf16[192,1024]{1,0:T(8,128)(2,1)S(1)}, bf16[192,1024]{1,0:T(8,128)(2,1)S(1)}, u32[]{:S(2)}, u32[]{:S(2)}) collective-permute-start(bf16[192,1024]{1,0:T(8,128)(2,1)S(1)} %shard_map.103), channel_id=1, source_target_pairs={{0,16},{4,12},{8,24},{12,4},{16,0},{20,28},{24,8},{28,20},{1,17},{... | collective-permute-start | bytes 1179656 | tf_op jit(solution)/shard_map/ppermute | solution.py:434

commit v20 on v19

--- a/solution.py
+++ b/solution.py
@@ -267,25 +267,22 @@
     )
 
 
-def far_weights_body(tiles, *refs):
+def far_body(tiles, pieces, *refs):
     pairs = Pairs(refs, tiles)
-    unit_ref, own_image_ref, own_weight_ref, raw_ref = refs[Pairs.count : Pairs.count + 4]
-    weight_ref, image_ref = refs[Pairs.count + 4 :]
+    unit_ref, own_image_ref, own_weight_ref, raw_ref, acc_ref = refs[Pairs.count : Pairs.count + 5]
+    weight_ref, image_ref = refs[Pairs.count + 5 : Pairs.count + 7]
+    sum_refs, text_refs = refs[Pairs.count + 7 : Pairs.count + 7 + pieces], refs[Pairs.count + 7 + pieces :]
     rows = raw_ref.shape[0]
     unit_images(raw_ref, image_ref.at[pl.ds(rows, rows), :])
     products = dot_nt(unit_ref[...], image_ref[rows:, :])
-    for half in range(CORES):
-        part = products[half * rows : (half + 1) * rows, :]
-        pairs.weigh(part, half, 3, weight_ref, half * rows, rows)
     image_ref[:rows, :] = own_image_ref[...]
     weight_ref[:, :rows] = own_weight_ref[...]
-
-
-def far_sum_body(weight_ref, unit_ref, *out_refs):
-    rows = weight_ref.shape[1] // 2
+    pairs.weigh(products[rows:, :], 1, 3, weight_ref, rows, rows)
+    text_sum_body(1, weight_ref, image_ref, acc_ref, *text_refs)
+    pairs.weigh(products[:rows, :], 0, 3, weight_ref, 0, rows)
     total = dot_tn(weight_ref[:, rows:], unit_ref[...]).astype(jnp.bfloat16)
     start = 0
-    for ref in out_refs:
+    for ref in sum_refs:
         ref[...] = total[start : start + ref.shape[0], :]
         start += ref.shape[0]
 
@@ -586,24 +583,16 @@
         limit=24,
     )
     own_weights, from_far = lax.optimization_barrier((own_weights, from_far))
-    far_weights, far_images = call_kernel(
-        functools.partial(far_weights_body, tiles),
-        [bf16(2 * rows, 2 * rows), bf16(2 * rows)],
-        lists + [units, own_images, own_weights, from_far],
-        limit=16,
-    )
-    sizes = [rows // 2] * 2
-    far_sum = call_kernel(
-        far_sum_body, [bf16(size) for size in sizes], [far_weights, units], limit=16
-    )
-    far_images, far_sum[0] = lax.optimization_barrier((far_images, far_sum[0]))
-    acc_other = call_kernel(
-        functools.partial(text_sum_body, 1),
-        [bf16(rows // ACC_PIECES)] * ACC_PIECES,
-        [far_weights, far_images, acc],
-        limit=16,
-    )
-    far_images, acc_other[0] = lax.optimization_barrier((far_images, acc_other[0]))
+    sizes = [rows - TILE, TILE]
+    far_weights, far_images, *rest = call_kernel(
+        functools.partial(far_body, tiles, len(sizes)),
+        [bf16(2 * rows, 2 * rows), bf16(2 * rows)]
+        + [bf16(size) for size in sizes]
+        + [bf16(rows // ACC_PIECES)] * ACC_PIECES,
+        lists + [units, own_images, own_weights, from_far, acc],
+        limit=24,
+    )
+    far_sum, acc_other = rest[: len(sizes)], rest[len(sizes) :]
     acc_own = call_kernel(
         functools.partial(text_sum_body, 0),
         [f32(rows)],

time: 59.7 us -> 59.2 us (level)
  starting transfers between devices: 22.4 us -> 23.2 us
    ppermute x8, waiting for transfers between devices: 11 us -> 9.37 us  [swap_near(): lax.ppermute(value, 'blk', [(i, i ^ neighbour_bits(i)[which]) for i in ra...]
    ppermute x11, waiting for transfers between devices: 6.23 us -> 7.34 us  [swap(): return lax.ppermute(value, axis, [(i, i ^ bits) for i in range(count)])]
    ppermute x8, starting transfers between devices: 12.7 us -> 13.5 us  [swap_near(): lax.ppermute(value, 'blk', [(i, i ^ neighbour_bits(i)[which]) for i in ra...]
    pallas_call x20 -> x18, Pallas kernels: 16.2 us -> 15.8 us  [call_kernel(): pl.pallas_call(body, out_shape=outs, in_specs=specs, out_specs=[ANY_SPEC...]
  transfers between devices with their start and end apart: 19 -> 19, of which waited for: 9 -> 9; matrix products, arithmetic and copies ran while one was open for 0% -> 0% of each run, Pallas kernels for 25% -> 24%
where the time goes in v20:
time: 59.2 us; the launch traced here: 59 us
  starting transfers between devices  23.2 us (39%)
  waiting for transfers between devices  16.7 us (28%)
  Pallas kernels  15.8 us (27%)
  between operations  2.12 us (4%)
  local copies, waits for them, and re-layouts  1.14 us (2%)
    pallas_call x18, Pallas kernels, call_kernel(): pl.pallas_call(body, out_shape=outs, in_specs=specs, out_specs=[ANY_SPEC...  15.8 us
    ppermute x8, starting transfers between devices, swap_near(): lax.ppermute(value, 'blk', [(i, i ^ neighbour_bits(i)[which]) for i in ra...  13.5 us
    ppermute x11, starting transfers between devices, swap(): return lax.ppermute(value, axis, [(i, i ^ bits) for i in range(count)])  9.73 us
    ppermute x8, waiting for transfers between devices, swap_near(): lax.ppermute(value, 'blk', [(i, i ^ neighbour_bits(i)[which]) for i in ra...  9.37 us
    ppermute x11, waiting for transfers between devices, swap(): return lax.ppermute(value, axis, [(i, i ^ bits) for i in range(count)])  7.34 us
  transfers between devices with their start and end apart: 19, of which 9 were waited for; matrix products, arithmetic and copies ran while one was open for 0% of the time, Pallas kernels for 24%

profile of v20, /device:TPU:0, one launch (start us, length us, event | category | flops | bytes accessed | tf_op | source)
XLA Modules:
  0.0 59.0 jit_solution(1237711932149089767)
XLA Ops:
  0.6 3.0 %collective-permute-start = (bf16[384,1024]{1,0:T(8,128)(2,1)}, bf16[384,1024]{1,0:T(8,128)(2,1)S(1)}, u32[]{:S(2)}, u32[]{:S(2)}) collective-permute-start(bf16[384,1024]{1,0:T(8,128)(2,1)} %raw_ref.1), channel_id=1, source_target_pairs={{0,16},{4,12},{8,24},{12,4},{16,0},{20,28},{24,8},{28,20},{1,17},{... | collective-permute-start | bytes 2359304 | tf_op jit(solution)/shard_map/ppermute | solution.py:431
  3.7 1.1 %copy-done = bf16[1536,256]{1,0:T(8,128)(2,1)S(1)} copy-done((bf16[1536,256]{1,0:T(8,128)(2,1)S(1)}, bf16[1536,256]{1,0:T(8,128)(2,1)}, u32[]{:S(2)}) %copy-start) | copy-done | bytes 786456
  4.8 0.1 shard_map.88
  4.9 2.7 %collective-permute-start.1 = (bf16[384,256]{1,0:T(8,128)(2,1)S(1)}, bf16[384,256]{1,0:T(8,128)(2,1)S(1)}, u32[]{:S(2)}, u32[]{:S(2)}) collective-permute-start(bf16[384,256]{1,0:T(8,128)(2,1)S(1)} %get-tuple-element.72), channel_id=1, source_target_pairs={{0,2},{1,3},{2,0},{3,1},{4,6},{5,7},{6,4},{7,5},{8,10},{9,11},{10,... | collective-permute-start | bytes 589832 | tf_op jit(solution)/shard_map/ppermute | solution.py:426
  7.5 1.3 %collective-permute-start.2 = (bf16[384,256]{1,0:T(8,128)(2,1)S(1)}, bf16[384,256]{1,0:T(8,128)(2,1)S(1)}, u32[]{:S(2)}, u32[]{:S(2)}) collective-permute-start(bf16[384,256]{1,0:T(8,128)(2,1)S(1)} %get-tuple-element.73), channel_id=1, source_target_pairs={{0,3},{1,2},{2,1},{3,0},{4,7},{5,6},{6,5},{7,4},{8,11},{9,10},{10,... | collective-permute-start | bytes 589832 | tf_op jit(solution)/shard_map/ppermute | solution.py:426
  8.9 0.2 collective-permute-start.3
  9.1 1.4 %shard_map.86 = (bf16[384,1024]{1,0:T(8,128)(2,1)S(1)}, bf16[384,1024]{1,0:T(8,128)(2,1)S(1)}, f32[384,128]{1,0:T(8,128)S(1)}) custom-call(bf16[384,1024]{1,0:T(8,128)(2,1)} %raw_ref.1), custom_call_target="tpu_custom_call" | custom-call | bytes 2555904 | tf_op jit(solution)/shard_map/pallas_call | solution.py:46
  10.5 1.6 %collective-permute-start.4 = (bf16[384,1024]{1,0:T(8,128)(2,1)}, bf16[384,1024]{1,0:T(8,128)(2,1)S(1)}, u32[]{:S(2)}, u32[]{:S(2)}) collective-permute-start(bf16[384,1024]{1,0:T(8,128)(2,1)} %raw_ref.1), channel_id=1, source_target_pairs={{0,8},{4,20},{8,0},{12,28},{16,24},{20,4},{24,16},{28,12},{1,9},{5... | collective-permute-start | bytes 2359304 | tf_op jit(solution)/shard_map/ppermute | solution.py:431
  13.4 1.1 %shard_map.87 = (f32[2,128]{1,0:T(2,128)S(1)}, f32[72,128]{1,0:T(8,128)S(1)}, s32[12,128]{1,0:T(8,128)S(1)}, s32[768,128]{1,0:T(8,128)S(1)}, f32[384,128]{1,0:T(8,128)S(1)}, /*index=5*/f32[4,128]{1,0:T(4,128)S(1)}) custom-call(f32[1]{0:T(128)S(6)} %copy.9.refs_0_, f32[1]{0:T(128)S(6)} %copy.10.refs_1_, s32[3,8,96]{2,1,0:T(8,128)S(1)} %bitcast.5, ...), custom_call_target="tpu_custom_call" | custom-call | bytes 743432 | tf_op jit(solution)/shard_map/pallas_call | solution.py:46
  14.5 0.9 %collective-permute-done.raw_ref = bf16[384,1024]{1,0:T(8,128)(2,1)S(1)} collective-permute-done((bf16[384,1024]{1,0:T(8,128)(2,1)}, bf16[384,1024]{1,0:T(8,128)(2,1)S(1)}, u32[]{:S(2)}, u32[]{:S(2)}) %collective-permute-start) | collective-permute-done | bytes 786464 | tf_op jit(solution)/shard_map/ppermute | solution.py:431
  15.4 3.3 %collective-permute-start.8 = (bf16[384,1024]{1,0:T(8,128)(2,1)S(1)}, bf16[384,1024]{1,0:T(8,128)(2,1)S(1)}, u32[]{:S(2)}, u32[]{:S(2)}) collective-permute-start(bf16[384,1024]{1,0:T(8,128)(2,1)S(1)} %collective-permute-done.raw_ref), channel_id=1, source_target_pairs={{0,8},{4,20},{8,0},{12,28},{16,24},{20,4},{24,16},{28,12},{1,9},{5... | collective-permute-start | bytes 2359304 | tf_op jit(solution)/shard_map/ppermute | solution.py:431
  18.7 0.2 shard_map.89.second_unit_ref
  19.0 3.8 %collective-permute-done.4.first_ref = bf16[384,1024]{1,0:T(8,128)(2,1)S(1)} collective-permute-done((bf16[384,1024]{1,0:T(8,128)(2,1)}, bf16[384,1024]{1,0:T(8,128)(2,1)S(1)}, u32[]{:S(2)}, u32[]{:S(2)}) %collective-permute-start.4) | collective-permute-done | bytes 786464 | tf_op jit(solution)/shard_map/ppermute | solution.py:431
  22.8 0.3 shard_map.90.refs_7_
  23.2 0.0 collective-permute-done.2.refs_2_.refs_3_
  23.2 0.4 shard_map.91
  23.5 0.1 collective-permute-start.5
  23.6 0.5 collective-permute-start.6
  24.1 0.1 collective-permute-start.7
  24.2 1.4 %shard_map.92 = (bf16[384,384]{1,0:T(8,128)(2,1)S(1)}, bf16[384,768]{1,0:T(8,128)(2,1)S(1)}) custom-call(f32[2,128]{1,0:T(2,128)S(1)} %get-tuple-element.65.refs_0_, f32[72,128]{1,0:T(8,128)S(1)} %get-tuple-element.66.refs_1_, s32[12,128]{1,0:T(8,128)S(1)} %get-tuple-element.67.refs_2_, s32[768,128]{1,0:T(8,128)S(1)} %get-tuple-element.68.refs_3_, ...), custom_call_target="tpu_custom_call" | custom-call | bytes 4666368 | tf_op jit(solution)/shard_map/pallas_call | solution.py:46
  25.6 0.0 collective-permute-done.5.refs_9_
  25.6 0.2 collective-permute-done.7.refs_11_
  25.9 1.3 %shard_map.93 = (bf16[768,1024]{1,0:T(8,128)(2,1)S(1)}, bf16[768,384]{1,0:T(8,128)(2,1)S(1)}, bf16[384,1024]{1,0:T(8,128)(2,1)S(1)}) custom-call(f32[2,128]{1,0:T(2,128)S(1)} %get-tuple-element.65.refs_0_, f32[72,128]{1,0:T(8,128)S(1)} %get-tuple-element.66.refs_1_, s32[12,128]{1,0:T(8,128)S(1)} %get-tuple-element.67.refs_2_, ...), custom_call_target="tpu_custom_call" | custom-call | bytes 8107008 | tf_op jit(solution)/shard_map/pallas_call | solution.py:46
  27.2 1.6 %collective-permute-start.14 = (bf16[384,1024]{1,0:T(8,128)(2,1)S(1)}, bf16[384,1024]{1,0:T(8,128)(2,1)S(1)}, u32[]{:S(2)}, u32[]{:S(2)}) collective-permute-start(bf16[384,1024]{1,0:T(8,128)(2,1)S(1)} %get-tuple-element.106), channel_id=1, source_target_pairs={{0,8},{4,20},{8,0},{12,28},{16,24},{20,4},{24,16},{28,12},{1,9},{5... | collective-permute-start | bytes 2359304 | tf_op jit(solution)/shard_map/ppermute | solution.py:431
  28.8 2.2 %shard_map.94 = (bf16[768,384]{1,0:T(8,128)(2,1)S(1)}, f32[768,1024]{1,0:T(8,128)S(1)}, bf16[768,768]{1,0:T(8,128)(2,1)S(1)}) custom-call(f32[2,128]{1,0:T(2,128)S(1)} %get-tuple-element.65.refs_0_, f32[72,128]{1,0:T(8,128)S(1)} %get-tuple-element.66.refs_1_, s32[12,128]{1,0:T(8,128)S(1)} %get-tuple-element.67.refs_2_, ...), custom_call_target="tpu_custom_call" | custom-call | bytes 10957824 | tf_op jit(solution)/shard_map/pallas_call | solution.py:46
  31.0 0.2 collective-permute-done.8.refs_9_
  31.2 2.6 %shard_map.95 = (bf16[768,768]{1,0:T(8,128)(2,1)S(1)}, bf16[768,1024]{1,0:T(8,128)(2,1)S(1)}, bf16[256,1024]{1,0:T(8,128)(2,1)S(1)}, bf16[128,1024]{1,0:T(8,128)...) custom-call(f32[2,128]{1,0:T(2,128)S(1)} %get-tuple-element.65.refs_0_, ...), custom_call_target="tpu_custom_call" | custom-call | bytes 11842560 | tf_op jit(solution)/shard_map/pallas_call | solution.py:46
  33.8 0.1 collective-permute-start.9
  33.9 0.5 collective-permute-start.10
  34.4 1.5 %collective-permute-start.15 = (bf16[256,1024]{1,0:T(8,128)(2,1)S(1)}, bf16[256,1024]{1,0:T(8,128)(2,1)S(1)}, u32[]{:S(2)}, u32[]{:S(2)}) collective-permute-start(bf16[256,1024]{1,0:T(8,128)(2,1)S(1)} %get-tuple-element.109), channel_id=1, source_target_pairs={{0,8},{4,20},{8,0},{12,28},{16,24},{20,4},{24,16},{28,12},{1,9},{5... | collective-permute-start | bytes 1572872 | tf_op jit(solution)/shard_map/ppermute | solution.py:431
  35.9 0.5 collective-permute-start.17
  36.4 0.8 %shard_map.96.refs_5_ = f32[384,1024]{1,0:T(8,128)S(1)} custom-call(bf16[768,768]{1,0:T(8,128)(2,1)S(1)} %get-tuple-element.94.weight_ref, bf16[768,1024]{1,0:T(8,128)(2,1)S(1)} %get-tuple-element.95.image_ref, f32[768,1024]{1,0:T(8,128)S(1)} %get-tuple-element.93.refs_10_.acc_ref), custom_call_target="tpu_custom_call" | custom-call | bytes 7471104 | tf_op jit(solution)/shard_map/pallas_call | solution.py:46
  37.2 0.6 %shard_map.97 = (bf16[384,256]{1,0:T(8,128)(2,1)S(1)}, bf16[384,256]{1,0:T(8,128)(2,1)S(1)}, bf16[384,256]{1,0:T(8,128)(2,1)S(1)}, bf16[384,256]{1,0:T(8,128)(2,1)S(1)}) custom-call(f32[384,128]{1,0:T(8,128)S(1)} %get-tuple-element.89.refs_0_, bf16[384,256]{1,0:T(8,128)(2,1)S(1)} %get-tuple-element.71.refs_0_.refs_1_, ...), custom_call_target="tpu_custom_call" | custom-call | bytes 4128768 | tf_op jit(solution)/shard_map/pallas_call | solution.py:46
  37.9 3.6 %collective-permute-start.11 = (bf16[384,256]{1,0:T(8,128)(2,1)S(1)}, bf16[384,256]{1,0:T(8,128)(2,1)S(1)}, u32[]{:S(2)}, u32[]{:S(2)}) collective-permute-start(bf16[384,256]{1,0:T(8,128)(2,1)S(1)} %get-tuple-element.100), channel_id=1, source_target_pairs={{0,2},{1,3},{2,0},{3,1},{4,6},{5,7},{6,4},{7,5},{8,10},{9,11},{10,... | collective-permute-start | bytes 589832 | tf_op jit(solution)/shard_map/ppermute | solution.py:426
  41.5 0.6 collective-permute-start.12
  42.1 0.0 collective-permute-done.14.add_ref
  42.1 0.1 collective-permute-start.13
  42.1 0.8 %shard_map.98 = (f32[384,1024]{1,0:T(8,128)S(1)}, bf16[384,1024]{1,0:T(8,128)(2,1)S(1)}) custom-call(bf16[768,768]{1,0:T(8,128)(2,1)S(1)} %get-tuple-element.105.weight_ref, bf16[768,1024]{1,0:T(8,128)(2,1)S(1)} %get-tuple-element.85.refs_6_.unit_ref, bf16[384,1024]{1,0:T(8,128)(2,1)S(1)} %collective-permute-done.14.add_ref), custom_call_target="tpu_custom_call" | custom-call | bytes 5898240 | tf_op jit(solution)/shard_map/pallas_call | solution.py:46
  43.0 0.8 %shard_map.99.refs_6_ = f32[384,1024]{1,0:T(8,128)S(1)} custom-call(bf16[768,384]{1,0:T(8,128)(2,1)S(1)} %get-tuple-element.91.refs_8_.weight_ref, bf16[768,1024]{1,0:T(8,128)(2,1)S(1)} %get-tuple-element.85.refs_6_.unit_ref, bf16[384,1024]{1,0:T(8,128)(2,1)S(1)} %get-tuple-element.107.add_ref), custom_call_target="tpu_custom_call" | custom-call | tf_op jit(solution)/shard_map/pallas_call | solution.py:46
  43.8 1.5 %collective-permute-done.15.in_ref = bf16[256,1024]{1,0:T(8,128)(2,1)S(1)} collective-permute-done((bf16[256,1024]{1,0:T(8,128)(2,1)S(1)}, bf16[256,1024]{1,0:T(8,128)(2,1)S(1)}, u32[]{:S(2)}, u32[]{:S(2)}) %collective-permute-start.15) | collective-permute-done | bytes 524320 | tf_op jit(solution)/shard_map/ppermute | solution.py:431
  45.2 0.1 shard_map.100
  45.4 1.0 %collective-permute-start.16 = (bf16[256,1024]{1,0:T(8,128)(2,1)S(1)}, bf16[256,1024]{1,0:T(8,128)(2,1)S(1)}, u32[]{:S(2)}, u32[]{:S(2)}) collective-permute-start(bf16[256,1024]{1,0:T(8,128)(2,1)S(1)} %shard_map.100), channel_id=1, source_target_pairs={{0,16},{4,12},{8,24},{12,4},{16,0},{20,28},{24,8},{28,20},{1,17},{... | collective-permute-start | bytes 1572872 | tf_op jit(solution)/shard_map/ppermute | solution.py:431
  46.4 1.7 %collective-permute-done.17.in_ref = bf16[128,1024]{1,0:T(8,128)(2,1)S(1)} collective-permute-done((bf16[128,1024]{1,0:T(8,128)(2,1)S(1)}, bf16[128,1024]{1,0:T(8,128)(2,1)S(1)}, u32[]{:S(2)}, u32[]{:S(2)}) %collective-permute-start.17) | collective-permute-done | bytes 262176 | tf_op jit(solution)/shard_map/ppermute | solution.py:431
  48.2 1.0 %collective-permute-start.18 = (bf16[128,1024]{1,0:T(8,128)(2,1)S(1)}, bf16[128,1024]{1,0:T(8,128)(2,1)S(1)}, u32[]{:S(2)}, u32[]{:S(2)}) collective-permute-start(bf16[128,1024]{1,0:T(8,128)(2,1)S(1)} %shard_map.101), channel_id=1, source_target_pairs={{0,16},{4,12},{8,24},{12,4},{16,0},{20,28},{24,8},{28,20},{1,17},{... | collective-permute-start | bytes 786440 | tf_op jit(solution)/shard_map/ppermute | solution.py:431
  49.1 6.1 %collective-permute-done.11.refs_0_.refs_1_ = bf16[384,256]{1,0:T(8,128)(2,1)S(1)} collective-permute-done((bf16[384,256]{1,0:T(8,128)(2,1)S(1)}, bf16[384,256]{1,0:T(8,128)(2,1)S(1)}, u32[]{:S(2)}, u32[]{:S(2)}) %collective-permute-start.11) | collective-permute-done | bytes 196640 | tf_op jit(solution)/shard_map/ppermute | solution.py:426
  55.2 1.0 %collective-permute-done.13.refs_2_.refs_3_ = bf16[384,256]{1,0:T(8,128)(2,1)S(1)} collective-permute-done((bf16[384,256]{1,0:T(8,128)(2,1)S(1)}, bf16[384,256]{1,0:T(8,128)(2,1)S(1)}, u32[]{:S(2)}, u32[]{:S(2)}) %collective-permute-start.13) | collective-permute-done | bytes 196640 | tf_op jit(solution)/shard_map/ppermute | solution.py:426
  56.2 1.2 %collective-permute-done.18.refs_8_ = bf16[128,1024]{1,0:T(8,128)(2,1)S(1)} collective-permute-done((bf16[128,1024]{1,0:T(8,128)(2,1)S(1)}, bf16[128,1024]{1,0:T(8,128)(2,1)S(1)}, u32[]{:S(2)}, u32[]{:S(2)}) %collective-permute-start.18) | collective-permute-done | bytes 262176 | tf_op jit(solution)/shard_map/ppermute | solution.py:431
  57.5 1.6 %shard_map.103 = (bf16[1536,256]{1,0:T(8,128)(2,1)}, bf16[384,1024]{1,0:T(8,128)(2,1)}) custom-call(bf16[384,256]{1,0:T(8,128)(2,1)S(1)} %get-tuple-element.99.refs_0_, bf16[384,256]{1,0:T(8,128)(2,1)S(1)} %collective-permute-done.11.refs_0_.refs_1_, bf16[384,256]{1,0:T(8,128)(2,1)S(1)} %collective-permute-done.12.refs_1_.refs_2_, ...), custom_call_target="tpu_custom_call" | custom-call | bytes 5705728 | tf_op jit(solution)/shard_map/pallas_call | solution.py:46
  (16 shorter events, 0.1 us)
Async XLA Ops:
  0.6 14.8 %collective-permute-start = (bf16[384,1024]{1,0:T(8,128)(2,1)}, bf16[384,1024]{1,0:T(8,128)(2,1)S(1)}, u32[]{:S(2)}, u32[]{:S(2)}) collective-permute-start(bf16[384,1024]{1,0:T(8,128)(2,1)} %raw_ref.1), channel_id=1, source_target_pairs={{0,16},{4,12},{8,24},{12,4},{16,0},{20,28},{24,8},{28,20},{1,17},{... | collective-permute-start | bytes 2359304 | tf_op jit(solution)/shard_map/ppermute | solution.py:431
  3.7 1.1 %copy-start = (bf16[1536,256]{1,0:T(8,128)(2,1)S(1)}, bf16[1536,256]{1,0:T(8,128)(2,1)}, u32[]{:S(2)}) copy-start(bf16[1536,256]{1,0:T(8,128)(2,1)} %text_ref.1) | copy-start | bytes 2359300
  4.8 8.6 %copy-start.1 = (s32[12288]{0:T(1024)S(1)}, s32[12288]{0:T(1024)}, u32[]{:S(2)}) copy-start(s32[12288]{0:T(1024)} %param.11) | copy-start | bytes 147460
  4.8 8.6 %copy-start.2 = (s32[12288]{0:T(1024)S(1)}, s32[12288]{0:T(1024)}, u32[]{:S(2)}) copy-start(s32[12288]{0:T(1024)} %param.12) | copy-start | bytes 147460
  4.8 8.6 %copy-start.3 = (s32[96,8,3]{0,1,2:T(8,128)S(1)}, s32[96,8,3]{0,1,2:T(8,128)}, u32[]{:S(2)}) copy-start(s32[96,8,3]{0,1,2:T(8,128)} %param.13) | copy-start | bytes 27652
  4.9 18.3 %collective-permute-start.1 = (bf16[384,256]{1,0:T(8,128)(2,1)S(1)}, bf16[384,256]{1,0:T(8,128)(2,1)S(1)}, u32[]{:S(2)}, u32[]{:S(2)}) collective-permute-start(bf16[384,256]{1,0:T(8,128)(2,1)S(1)} %get-tuple-element.72), channel_id=1, source_target_pairs={{0,2},{1,3},{2,0},{3,1},{4,6},{5,7},{6,4},{7,5},{8,10},{9,11},{10,... | collective-permute-start | bytes 589832 | tf_op jit(solution)/shard_map/ppermute | solution.py:426
  7.5 15.6 %collective-permute-start.2 = (bf16[384,256]{1,0:T(8,128)(2,1)S(1)}, bf16[384,256]{1,0:T(8,128)(2,1)S(1)}, u32[]{:S(2)}, u32[]{:S(2)}) collective-permute-start(bf16[384,256]{1,0:T(8,128)(2,1)S(1)} %get-tuple-element.73), channel_id=1, source_target_pairs={{0,3},{1,2},{2,1},{3,0},{4,7},{5,6},{6,5},{7,4},{8,11},{9,10},{10,... | collective-permute-start | bytes 589832 | tf_op jit(solution)/shard_map/ppermute | solution.py:426
  8.9 14.3 %collective-permute-start.3 = (bf16[384,256]{1,0:T(8,128)(2,1)S(1)}, bf16[384,256]{1,0:T(8,128)(2,1)S(1)}, u32[]{:S(2)}, u32[]{:S(2)}) collective-permute-start(bf16[384,256]{1,0:T(8,128)(2,1)S(1)} %get-tuple-element.74), channel_id=1, source_target_pairs={{0,1},{1,0},{2,3},{3,2},{4,5},{5,4},{6,7},{7,6},{8,9},{9,8},{10,11... | collective-permute-start | bytes 589832 | tf_op jit(solution)/shard_map/ppermute | solution.py:426
  10.5 12.3 %collective-permute-start.4 = (bf16[384,1024]{1,0:T(8,128)(2,1)}, bf16[384,1024]{1,0:T(8,128)(2,1)S(1)}, u32[]{:S(2)}, u32[]{:S(2)}) collective-permute-start(bf16[384,1024]{1,0:T(8,128)(2,1)} %raw_ref.1), channel_id=1, source_target_pairs={{0,8},{4,20},{8,0},{12,28},{16,24},{20,4},{24,16},{28,12},{1,9},{5... | collective-permute-start | bytes 2359304 | tf_op jit(solution)/shard_map/ppermute | solution.py:431
  15.4 15.8 %collective-permute-start.8 = (bf16[384,1024]{1,0:T(8,128)(2,1)S(1)}, bf16[384,1024]{1,0:T(8,128)(2,1)S(1)}, u32[]{:S(2)}, u32[]{:S(2)}) collective-permute-start(bf16[384,1024]{1,0:T(8,128)(2,1)S(1)} %collective-permute-done.raw_ref), channel_id=1, source_target_pairs={{0,8},{4,20},{8,0},{12,28},{16,24},{20,4},{24,16},{28,12},{1,9},{5... | collective-permute-start | bytes 2359304 | tf_op jit(solution)/shard_map/ppermute | solution.py:431
  23.5 2.1 %collective-permute-start.5 = (bf16[128,1024]{1,0:T(8,128)(2,1)S(1)}, bf16[128,1024]{1,0:T(8,128)(2,1)S(1)}, u32[]{:S(2)}, u32[]{:S(2)}) collective-permute-start(bf16[128,1024]{1,0:T(8,128)(2,1)S(1)} %get-tuple-element.82), channel_id=1, source_target_pairs={{0,4},{4,0},{8,12},{12,8},{16,20},{20,16},{24,28},{28,24},{1,5},{5... | collective-permute-start | bytes 786440 | tf_op jit(solution)/shard_map/ppermute | solution.py:426
  23.6 2.0 %collective-permute-start.6 = (bf16[128,1024]{1,0:T(8,128)(2,1)S(1)}, bf16[128,1024]{1,0:T(8,128)(2,1)S(1)}, u32[]{:S(2)}, u32[]{:S(2)}) collective-permute-start(bf16[128,1024]{1,0:T(8,128)(2,1)S(1)} %get-tuple-element.83), channel_id=1, source_target_pairs={{0,4},{4,0},{8,12},{12,8},{16,20},{20,16},{24,28},{28,24},{1,5},{5... | collective-permute-start | bytes 786440 | tf_op jit(solution)/shard_map/ppermute | solution.py:426
  24.1 1.8 %collective-permute-start.7 = (bf16[128,1024]{1,0:T(8,128)(2,1)S(1)}, bf16[128,1024]{1,0:T(8,128)(2,1)S(1)}, u32[]{:S(2)}, u32[]{:S(2)}) collective-permute-start(bf16[128,1024]{1,0:T(8,128)(2,1)S(1)} %get-tuple-element.84), channel_id=1, source_target_pairs={{0,4},{4,0},{8,12},{12,8},{16,20},{20,16},{24,28},{28,24},{1,5},{5... | collective-permute-start | bytes 786440 | tf_op jit(solution)/shard_map/ppermute | solution.py:426
  27.2 14.9 %collective-permute-start.14 = (bf16[384,1024]{1,0:T(8,128)(2,1)S(1)}, bf16[384,1024]{1,0:T(8,128)(2,1)S(1)}, u32[]{:S(2)}, u32[]{:S(2)}) collective-permute-start(bf16[384,1024]{1,0:T(8,128)(2,1)S(1)} %get-tuple-element.106), channel_id=1, source_target_pairs={{0,8},{4,20},{8,0},{12,28},{16,24},{20,4},{24,16},{28,12},{1,9},{5... | collective-permute-start | bytes 2359304 | tf_op jit(solution)/shard_map/ppermute | solution.py:431
  33.8 3.4 %collective-permute-start.9 = (bf16[192,1024]{1,0:T(8,128)(2,1)S(1)}, bf16[192,1024]{1,0:T(8,128)(2,1)S(1)}, u32[]{:S(2)}, u32[]{:S(2)}) collective-permute-start(bf16[192,1024]{1,0:T(8,128)(2,1)S(1)} %get-tuple-element.96), channel_id=1, source_target_pairs={{0,4},{4,0},{8,12},{12,8},{16,20},{20,16},{24,28},{28,24},{1,5},{5... | collective-permute-start | bytes 1179656 | tf_op jit(solution)/shard_map/ppermute | solution.py:426
  33.9 3.3 %collective-permute-start.10 = (bf16[192,1024]{1,0:T(8,128)(2,1)S(1)}, bf16[192,1024]{1,0:T(8,128)(2,1)S(1)}, u32[]{:S(2)}, u32[]{:S(2)}) collective-permute-start(bf16[192,1024]{1,0:T(8,128)(2,1)S(1)} %get-tuple-element.97), channel_id=1, source_target_pairs={{0,4},{4,0},{8,12},{12,8},{16,20},{20,16},{24,28},{28,24},{1,5},{5... | collective-permute-start | bytes 1179656 | tf_op jit(solution)/shard_map/ppermute | solution.py:426
  34.4 10.8 %collective-permute-start.15 = (bf16[256,1024]{1,0:T(8,128)(2,1)S(1)}, bf16[256,1024]{1,0:T(8,128)(2,1)S(1)}, u32[]{:S(2)}, u32[]{:S(2)}) collective-permute-start(bf16[256,1024]{1,0:T(8,128)(2,1)S(1)} %get-tuple-element.109), channel_id=1, source_target_pairs={{0,8},{4,20},{8,0},{12,28},{16,24},{20,4},{24,16},{28,12},{1,9},{5... | collective-permute-start | bytes 1572872 | tf_op jit(solution)/shard_map/ppermute | solution.py:431
  35.9 12.2 %collective-permute-start.17 = (bf16[128,1024]{1,0:T(8,128)(2,1)S(1)}, bf16[128,1024]{1,0:T(8,128)(2,1)S(1)}, u32[]{:S(2)}, u32[]{:S(2)}) collective-permute-start(bf16[128,1024]{1,0:T(8,128)(2,1)S(1)} %get-tuple-element.111), channel_id=1, source_target_pairs={{0,8},{4,20},{8,0},{12,28},{16,24},{20,4},{24,16},{28,12},{1,9},{5... | collective-permute-start | bytes 786440 | tf_op jit(solution)/shard_map/ppermute | solution.py:431
  37.9 17.3 %collective-permute-start.11 = (bf16[384,256]{1,0:T(8,128)(2,1)S(1)}, bf16[384,256]{1,0:T(8,128)(2,1)S(1)}, u32[]{:S(2)}, u32[]{:S(2)}) collective-permute-start(bf16[384,256]{1,0:T(8,128)(2,1)S(1)} %get-tuple-element.100), channel_id=1, source_target_pairs={{0,2},{1,3},{2,0},{3,1},{4,6},{5,7},{6,4},{7,5},{8,10},{9,11},{10,... | collective-permute-start | bytes 589832 | tf_op jit(solution)/shard_map/ppermute | solution.py:426
  41.5 13.7 %collective-permute-start.12 = (bf16[384,256]{1,0:T(8,128)(2,1)S(1)}, bf16[384,256]{1,0:T(8,128)(2,1)S(1)}, u32[]{:S(2)}, u32[]{:S(2)}) collective-permute-start(bf16[384,256]{1,0:T(8,128)(2,1)S(1)} %get-tuple-element.101), channel_id=1, source_target_pairs={{0,3},{1,2},{2,1},{3,0},{4,7},{5,6},{6,5},{7,4},{8,11},{9,10},{10,... | collective-permute-start | bytes 589832 | tf_op jit(solution)/shard_map/ppermute | solution.py:426
  42.1 14.1 %collective-permute-start.13 = (bf16[384,256]{1,0:T(8,128)(2,1)S(1)}, bf16[384,256]{1,0:T(8,128)(2,1)S(1)}, u32[]{:S(2)}, u32[]{:S(2)}) collective-permute-start(bf16[384,256]{1,0:T(8,128)(2,1)S(1)} %get-tuple-element.102), channel_id=1, source_target_pairs={{0,1},{1,0},{2,3},{3,2},{4,5},{5,4},{6,7},{7,6},{8,9},{9,8},{10,11... | collective-permute-start | bytes 589832 | tf_op jit(solution)/shard_map/ppermute | solution.py:426
  45.4 12.1 %collective-permute-start.16 = (bf16[256,1024]{1,0:T(8,128)(2,1)S(1)}, bf16[256,1024]{1,0:T(8,128)(2,1)S(1)}, u32[]{:S(2)}, u32[]{:S(2)}) collective-permute-start(bf16[256,1024]{1,0:T(8,128)(2,1)S(1)} %shard_map.100), channel_id=1, source_target_pairs={{0,16},{4,12},{8,24},{12,4},{16,0},{20,28},{24,8},{28,20},{1,17},{... | collective-permute-start | bytes 1572872 | tf_op jit(solution)/shard_map/ppermute | solution.py:431
  48.2 9.3 %collective-permute-start.18 = (bf16[128,1024]{1,0:T(8,128)(2,1)S(1)}, bf16[128,1024]{1,0:T(8,128)(2,1)S(1)}, u32[]{:S(2)}, u32[]{:S(2)}) collective-permute-start(bf16[128,1024]{1,0:T(8,128)(2,1)S(1)} %shard_map.101), channel_id=1, source_target_pairs={{0,16},{4,12},{8,24},{12,4},{16,0},{20,28},{24,8},{28,20},{1,17},{... | collective-permute-start | bytes 786440 | tf_op jit(solution)/shard_map/ppermute | solution.py:431

commit v21 on v20

--- a/solution.py
+++ b/solution.py
@@ -34,6 +34,7 @@
     scratch=(),
     flops=0,
     moved=None,
+    aliases=None,
     limit=24,
 ):
     if moved is None:
@@ -49,6 +50,7 @@
             in_specs=specs,
             out_specs=[ANY_SPEC if outs_anywhere else VMEM_SPEC] * len(outs),
             scratch_shapes=list(scratch),
+            input_output_aliases=aliases or {},
             compiler_params=pltpu.CompilerParams(vmem_limit_bytes=limit * MIB),
             cost_estimate=pl.CostEstimate(flops=flops, bytes_accessed=moved, transcendentals=0),
         )(*operands)
@@ -391,6 +393,14 @@
         copies[-1].start()
 
 
+def own_block_body(part_ref, out_ref, sem):
+    rows = part_ref.shape[0]
+    block = pl.ds(pl.multiple_of(lax.axis_index("tp") * rows, rows), rows)
+    copy = pltpu.make_async_copy(part_ref, out_ref.at[block, :], sem)
+    copy.start()
+    copy.wait()
+
+
 def finish_body(chunks, adds, *refs):
     part_refs, (raw_ref, scale_ref, sum_ref) = refs[:chunks], refs[chunks : chunks + 3]
     add_refs = refs[chunks + 3 : chunks + 3 + adds]
@@ -398,7 +408,7 @@
     place = lax.axis_index("tp")
     rows = part_refs[0].shape[0]
     copies = []
-    for k in range(chunks):
+    for k in range(1, chunks):
         peer = place ^ far_first(k, chunks)
         for first in range(0, rows, TILE):
             block = pl.ds(pl.multiple_of(peer * rows + first, TILE), TILE)
@@ -522,6 +532,15 @@
         return swap_chunks(parts)
 
     def finish(text_parts, total, pieces):
+        text_own_block = call_kernel(
+            own_block_body,
+            [bf16(groups * rows, width)],
+            text_parts[:1],
+            outs_anywhere=True,
+            scratch=[pltpu.SemaphoreType.DMA],
+            moved=0,
+            limit=8,
+        )[0]
         arrived = call_kernel(
             arrived_body,
             [struct((16, TILE), jnp.bfloat16)],
@@ -533,7 +552,13 @@
             call_kernel(
                 functools.partial(finish_body, groups, len(pieces)),
                 [bf16(groups * rows, width), bf16(rows)],
-                text_parts + [image_raw, image_scales, total] + pieces + arrived,
+                text_parts
+                + [image_raw, image_scales, total]
+                + pieces
+                + arrived
+                + [text_own_block],
+                anywhere=(groups + 4 + len(pieces),),
+                aliases={groups + 4 + len(pieces): 0},
                 outs_anywhere=True,
                 scratch=[
                     pltpu.VMEM((rows, embed), jnp.bfloat16),
@@ -619,6 +644,7 @@
     base = call_kernel(
         own_sum_body, [f32(rows)], [own_weights, units, image_add], moved=0, limit=16
     )[0]
+    text_parts[0], base = lax.optimization_barrier((text_parts[0], base))
     return finish(text_parts, base, image_last)
 
 

time: 59.2 us -> 59.2 us (level)
  Pallas kernels: 15.8 us -> 16.5 us
  waiting for transfers between devices: 16.7 us -> 16 us
    ppermute x8, waiting for transfers between devices: 9.37 us -> 8.68 us  [swap_near(): lax.ppermute(value, 'blk', [(i, i ^ neighbour_bits(i)[which]) for i in ra...]
    pallas_call x18 -> x19, Pallas kernels: 15.8 us -> 16.5 us  [call_kernel(): pl.pallas_call(body, out_shape=outs, in_specs=specs, out_specs=[ANY_SPEC...]
  transfers between devices with their start and end apart: 19 -> 19, of which waited for: 9 -> 9; matrix products, arithmetic and copies ran while one was open for 0% -> 0% of each run, Pallas kernels for 24% -> 25%
where the time goes in v21:
time: 59.2 us; the launch traced here: 58.9 us
  starting transfers between devices  23.2 us (39%)
  Pallas kernels  16.5 us (28%)
  waiting for transfers between devices  16 us (27%)
  between operations  2.13 us (4%)
  local copies, waits for them, and re-layouts  1.14 us (2%)
    pallas_call x19, Pallas kernels, call_kernel(): pl.pallas_call(body, out_shape=outs, in_specs=specs, out_specs=[ANY_SPEC...  16.5 us
    ppermute x8, starting transfers between devices, swap_near(): lax.ppermute(value, 'blk', [(i, i ^ neighbour_bits(i)[which]) for i in ra...  13.5 us
    ppermute x11, starting transfers between devices, swap(): return lax.ppermute(value, axis, [(i, i ^ bits) for i in range(count)])  9.73 us
    ppermute x8, waiting for transfers between devices, swap_near(): lax.ppermute(value, 'blk', [(i, i ^ neighbour_bits(i)[which]) for i in ra...  8.68 us
    ppermute x11, waiting for transfers between devices, swap(): return lax.ppermute(value, axis, [(i, i ^ bits) for i in range(count)])  7.32 us
  transfers between devices with their start and end apart: 19, of which 9 were waited for; matrix products, arithmetic and copies ran while one was open for 0% of the time, Pallas kernels for 25%

profile of v21, /device:TPU:0, one launch (start us, length us, event | category | flops | bytes accessed | tf_op | source)
XLA Modules:
  0.0 58.9 jit_solution(2607120717753517901)
XLA Ops:
  0.6 3.0 %collective-permute-start = (bf16[384,1024]{1,0:T(8,128)(2,1)}, bf16[384,1024]{1,0:T(8,128)(2,1)S(1)}, u32[]{:S(2)}, u32[]{:S(2)}) collective-permute-start(bf16[384,1024]{1,0:T(8,128)(2,1)} %raw_ref.1), channel_id=1, source_target_pairs={{0,16},{4,12},{8,24},{12,4},{16,0},{20,28},{24,8},{28,20},{1,17},{... | collective-permute-start | bytes 2359304 | tf_op jit(solution)/shard_map/ppermute | solution.py:441
  3.7 1.1 %copy-done = bf16[1536,256]{1,0:T(8,128)(2,1)S(1)} copy-done((bf16[1536,256]{1,0:T(8,128)(2,1)S(1)}, bf16[1536,256]{1,0:T(8,128)(2,1)}, u32[]{:S(2)}) %copy-start) | copy-done | bytes 786456
  4.8 0.1 shard_map.88
  4.9 2.7 %collective-permute-start.1 = (bf16[384,256]{1,0:T(8,128)(2,1)S(1)}, bf16[384,256]{1,0:T(8,128)(2,1)S(1)}, u32[]{:S(2)}, u32[]{:S(2)}) collective-permute-start(bf16[384,256]{1,0:T(8,128)(2,1)S(1)} %get-tuple-element.74), channel_id=1, source_target_pairs={{0,2},{1,3},{2,0},{3,1},{4,6},{5,7},{6,4},{7,5},{8,10},{9,11},{10,... | collective-permute-start | bytes 589832 | tf_op jit(solution)/shard_map/ppermute | solution.py:436
  7.5 1.3 %collective-permute-start.2 = (bf16[384,256]{1,0:T(8,128)(2,1)S(1)}, bf16[384,256]{1,0:T(8,128)(2,1)S(1)}, u32[]{:S(2)}, u32[]{:S(2)}) collective-permute-start(bf16[384,256]{1,0:T(8,128)(2,1)S(1)} %get-tuple-element.75), channel_id=1, source_target_pairs={{0,3},{1,2},{2,1},{3,0},{4,7},{5,6},{6,5},{7,4},{8,11},{9,10},{10,... | collective-permute-start | bytes 589832 | tf_op jit(solution)/shard_map/ppermute | solution.py:436
  8.9 0.2 collective-permute-start.3
  9.1 1.4 %shard_map.86 = (bf16[384,1024]{1,0:T(8,128)(2,1)S(1)}, bf16[384,1024]{1,0:T(8,128)(2,1)S(1)}, f32[384,128]{1,0:T(8,128)S(1)}) custom-call(bf16[384,1024]{1,0:T(8,128)(2,1)} %raw_ref.1), custom_call_target="tpu_custom_call" | custom-call | bytes 2555904 | tf_op jit(solution)/shard_map/pallas_call | solution.py:47
  10.5 1.6 %collective-permute-start.4 = (bf16[384,1024]{1,0:T(8,128)(2,1)}, bf16[384,1024]{1,0:T(8,128)(2,1)S(1)}, u32[]{:S(2)}, u32[]{:S(2)}) collective-permute-start(bf16[384,1024]{1,0:T(8,128)(2,1)} %raw_ref.1), channel_id=1, source_target_pairs={{0,8},{4,20},{8,0},{12,28},{16,24},{20,4},{24,16},{28,12},{1,9},{5... | collective-permute-start | bytes 2359304 | tf_op jit(solution)/shard_map/ppermute | solution.py:441
  13.4 1.1 %shard_map.87 = (f32[2,128]{1,0:T(2,128)S(1)}, f32[72,128]{1,0:T(8,128)S(1)}, s32[12,128]{1,0:T(8,128)S(1)}, s32[768,128]{1,0:T(8,128)S(1)}, f32[384,128]{1,0:T(8,128)S(1)}, /*index=5*/f32[4,128]{1,0:T(4,128)S(1)}) custom-call(f32[1]{0:T(128)S(6)} %copy.11.refs_0_, f32[1]{0:T(128)S(6)} %copy.12.refs_1_, s32[3,8,96]{2,1,0:T(8,128)S(1)} %bitcast.5, ...), custom_call_target="tpu_custom_call" | custom-call | bytes 743432 | tf_op jit(solution)/shard_map/pallas_call | solution.py:47
  14.5 0.9 %collective-permute-done.raw_ref = bf16[384,1024]{1,0:T(8,128)(2,1)S(1)} collective-permute-done((bf16[384,1024]{1,0:T(8,128)(2,1)}, bf16[384,1024]{1,0:T(8,128)(2,1)S(1)}, u32[]{:S(2)}, u32[]{:S(2)}) %collective-permute-start) | collective-permute-done | bytes 786464 | tf_op jit(solution)/shard_map/ppermute | solution.py:441
  15.4 3.3 %collective-permute-start.8 = (bf16[384,1024]{1,0:T(8,128)(2,1)S(1)}, bf16[384,1024]{1,0:T(8,128)(2,1)S(1)}, u32[]{:S(2)}, u32[]{:S(2)}) collective-permute-start(bf16[384,1024]{1,0:T(8,128)(2,1)S(1)} %collective-permute-done.raw_ref), channel_id=1, source_target_pairs={{0,8},{4,20},{8,0},{12,28},{16,24},{20,4},{24,16},{28,12},{1,9},{5... | collective-permute-start | bytes 2359304 | tf_op jit(solution)/shard_map/ppermute | solution.py:441
  18.7 0.2 shard_map.89.second_unit_ref
  19.0 3.8 %collective-permute-done.4.first_ref = bf16[384,1024]{1,0:T(8,128)(2,1)S(1)} collective-permute-done((bf16[384,1024]{1,0:T(8,128)(2,1)}, bf16[384,1024]{1,0:T(8,128)(2,1)S(1)}, u32[]{:S(2)}, u32[]{:S(2)}) %collective-permute-start.4) | collective-permute-done | bytes 786464 | tf_op jit(solution)/shard_map/ppermute | solution.py:441
  22.8 0.3 shard_map.90.refs_7_
  23.2 0.0 collective-permute-done.2.refs_2_.refs_3_
  23.2 0.4 shard_map.91
  23.5 0.1 collective-permute-start.5
  23.6 0.5 collective-permute-start.6
  24.1 0.1 collective-permute-start.7
  24.2 1.4 %shard_map.92 = (bf16[384,384]{1,0:T(8,128)(2,1)S(1)}, bf16[384,768]{1,0:T(8,128)(2,1)S(1)}) custom-call(f32[2,128]{1,0:T(2,128)S(1)} %get-tuple-element.67.refs_0_, f32[72,128]{1,0:T(8,128)S(1)} %get-tuple-element.68.refs_1_, s32[12,128]{1,0:T(8,128)S(1)} %get-tuple-element.69.refs_2_, s32[768,128]{1,0:T(8,128)S(1)} %get-tuple-element.70.refs_3_, ...), custom_call_target="tpu_custom_call" | custom-call | bytes 4666368 | tf_op jit(solution)/shard_map/pallas_call | solution.py:47
  25.6 0.2 collective-permute-done.7.refs_11_
  25.9 1.3 %shard_map.93 = (bf16[768,1024]{1,0:T(8,128)(2,1)S(1)}, bf16[768,384]{1,0:T(8,128)(2,1)S(1)}, bf16[384,1024]{1,0:T(8,128)(2,1)S(1)}) custom-call(f32[2,128]{1,0:T(2,128)S(1)} %get-tuple-element.67.refs_0_, f32[72,128]{1,0:T(8,128)S(1)} %get-tuple-element.68.refs_1_, s32[12,128]{1,0:T(8,128)S(1)} %get-tuple-element.69.refs_2_, ...), custom_call_target="tpu_custom_call" | custom-call | bytes 8107008 | tf_op jit(solution)/shard_map/pallas_call | solution.py:47
  27.2 1.6 %collective-permute-start.11 = (bf16[384,1024]{1,0:T(8,128)(2,1)S(1)}, bf16[384,1024]{1,0:T(8,128)(2,1)S(1)}, u32[]{:S(2)}, u32[]{:S(2)}) collective-permute-start(bf16[384,1024]{1,0:T(8,128)(2,1)S(1)} %get-tuple-element.103), channel_id=1, source_target_pairs={{0,8},{4,20},{8,0},{12,28},{16,24},{20,4},{24,16},{28,12},{1,9},{5... | collective-permute-start | bytes 2359304 | tf_op jit(solution)/shard_map/ppermute | solution.py:441
  28.8 2.2 %shard_map.94 = (bf16[768,384]{1,0:T(8,128)(2,1)S(1)}, f32[768,1024]{1,0:T(8,128)S(1)}, bf16[768,768]{1,0:T(8,128)(2,1)S(1)}) custom-call(f32[2,128]{1,0:T(2,128)S(1)} %get-tuple-element.67.refs_0_, f32[72,128]{1,0:T(8,128)S(1)} %get-tuple-element.68.refs_1_, s32[12,128]{1,0:T(8,128)S(1)} %get-tuple-element.69.refs_2_, ...), custom_call_target="tpu_custom_call" | custom-call | bytes 10957824 | tf_op jit(solution)/shard_map/pallas_call | solution.py:47
  31.0 0.2 collective-permute-done.8.refs_9_
  31.2 2.6 %shard_map.95 = (bf16[768,768]{1,0:T(8,128)(2,1)S(1)}, bf16[768,1024]{1,0:T(8,128)(2,1)S(1)}, bf16[256,1024]{1,0:T(8,128)(2,1)S(1)}, bf16[128,1024]{1,0:T(8,128)...) custom-call(f32[2,128]{1,0:T(2,128)S(1)} %get-tuple-element.67.refs_0_, ...), custom_call_target="tpu_custom_call" | custom-call | bytes 11842560 | tf_op jit(solution)/shard_map/pallas_call | solution.py:47
  33.8 0.1 collective-permute-start.9
  33.9 0.5 collective-permute-start.10
  34.4 1.5 %collective-permute-start.15 = (bf16[256,1024]{1,0:T(8,128)(2,1)S(1)}, bf16[256,1024]{1,0:T(8,128)(2,1)S(1)}, u32[]{:S(2)}, u32[]{:S(2)}) collective-permute-start(bf16[256,1024]{1,0:T(8,128)(2,1)S(1)} %get-tuple-element.113), channel_id=1, source_target_pairs={{0,8},{4,20},{8,0},{12,28},{16,24},{20,4},{24,16},{28,12},{1,9},{5... | collective-permute-start | bytes 1572872 | tf_op jit(solution)/shard_map/ppermute | solution.py:441
  35.9 0.5 collective-permute-start.17
  36.4 0.8 %shard_map.96.refs_5_ = f32[384,1024]{1,0:T(8,128)S(1)} custom-call(bf16[768,768]{1,0:T(8,128)(2,1)S(1)} %get-tuple-element.96.weight_ref, bf16[768,1024]{1,0:T(8,128)(2,1)S(1)} %get-tuple-element.97.image_ref, f32[768,1024]{1,0:T(8,128)S(1)} %get-tuple-element.95.refs_10_.acc_ref), custom_call_target="tpu_custom_call" | custom-call | bytes 7471104 | tf_op jit(solution)/shard_map/pallas_call | solution.py:47
  37.2 0.6 %shard_map.97 = (bf16[384,256]{1,0:T(8,128)(2,1)S(1)}, bf16[384,256]{1,0:T(8,128)(2,1)S(1)}, bf16[384,256]{1,0:T(8,128)(2,1)S(1)}, bf16[384,256]{1,0:T(8,128)(2,1)S(1)}) custom-call(f32[384,128]{1,0:T(8,128)S(1)} %get-tuple-element.91.refs_0_, bf16[384,256]{1,0:T(8,128)(2,1)S(1)} %get-tuple-element.73.refs_0_.refs_1_, ...), custom_call_target="tpu_custom_call" | custom-call | bytes 4128768 | tf_op jit(solution)/shard_map/pallas_call | solution.py:47
  37.9 3.6 %collective-permute-start.12 = (bf16[384,256]{1,0:T(8,128)(2,1)S(1)}, bf16[384,256]{1,0:T(8,128)(2,1)S(1)}, u32[]{:S(2)}, u32[]{:S(2)}) collective-permute-start(bf16[384,256]{1,0:T(8,128)(2,1)S(1)} %get-tuple-element.106), channel_id=1, source_target_pairs={{0,2},{1,3},{2,0},{3,1},{4,6},{5,7},{6,4},{7,5},{8,10},{9,11},{10,... | collective-permute-start | bytes 589832 | tf_op jit(solution)/shard_map/ppermute | solution.py:436
  41.5 0.6 %collective-permute-start.13 = (bf16[384,256]{1,0:T(8,128)(2,1)S(1)}, bf16[384,256]{1,0:T(8,128)(2,1)S(1)}, u32[]{:S(2)}, u32[]{:S(2)}) collective-permute-start(bf16[384,256]{1,0:T(8,128)(2,1)S(1)} %get-tuple-element.107), channel_id=1, source_target_pairs={{0,3},{1,2},{2,1},{3,0},{4,7},{5,6},{6,5},{7,4},{8,11},{9,10},{10,... | collective-permute-start | bytes 589832 | tf_op jit(solution)/shard_map/ppermute | solution.py:436
  42.1 0.0 collective-permute-start.14
  42.1 0.8 %shard_map.98 = (f32[384,1024]{1,0:T(8,128)S(1)}, bf16[384,1024]{1,0:T(8,128)(2,1)S(1)}) custom-call(bf16[768,768]{1,0:T(8,128)(2,1)S(1)} %get-tuple-element.102.weight_ref, bf16[768,1024]{1,0:T(8,128)(2,1)S(1)} %get-tuple-element.87.refs_6_.unit_ref, bf16[384,1024]{1,0:T(8,128)(2,1)S(1)} %collective-permute-done.11.add_ref), custom_call_target="tpu_custom_call" | custom-call | bytes 5898240 | tf_op jit(solution)/shard_map/pallas_call | solution.py:47
  43.0 0.8 %shard_map.99.refs_6_ = f32[384,1024]{1,0:T(8,128)S(1)} custom-call(bf16[768,384]{1,0:T(8,128)(2,1)S(1)} %get-tuple-element.93.refs_8_.weight_ref, bf16[768,1024]{1,0:T(8,128)(2,1)S(1)} %get-tuple-element.87.refs_6_.unit_ref, bf16[384,1024]{1,0:T(8,128)(2,1)S(1)} %get-tuple-element.104.add_ref), custom_call_target="tpu_custom_call" | custom-call | tf_op jit(solution)/shard_map/pallas_call | solution.py:47
  43.8 0.7 %shard_map.103.refs_10_ = bf16[1536,256]{1,0:T(8,128)(2,1)} custom-call(bf16[384,256]{1,0:T(8,128)(2,1)S(1)} %get-tuple-element.105.part_ref.refs_0_), custom_call_target="tpu_custom_call" | custom-call | tf_op jit(solution)/shard_map/pallas_call | solution.py:47
  44.5 0.8 %collective-permute-done.15.in_ref = bf16[256,1024]{1,0:T(8,128)(2,1)S(1)} collective-permute-done((bf16[256,1024]{1,0:T(8,128)(2,1)S(1)}, bf16[256,1024]{1,0:T(8,128)(2,1)S(1)}, u32[]{:S(2)}, u32[]{:S(2)}) %collective-permute-start.15) | collective-permute-done | bytes 524320 | tf_op jit(solution)/shard_map/ppermute | solution.py:441
  45.2 0.1 shard_map.100
  45.4 1.0 %collective-permute-start.16 = (bf16[256,1024]{1,0:T(8,128)(2,1)S(1)}, bf16[256,1024]{1,0:T(8,128)(2,1)S(1)}, u32[]{:S(2)}, u32[]{:S(2)}) collective-permute-start(bf16[256,1024]{1,0:T(8,128)(2,1)S(1)} %shard_map.100), channel_id=1, source_target_pairs={{0,16},{4,12},{8,24},{12,4},{16,0},{20,28},{24,8},{28,20},{1,17},{... | collective-permute-start | bytes 1572872 | tf_op jit(solution)/shard_map/ppermute | solution.py:441
  46.4 1.7 %collective-permute-done.17.in_ref = bf16[128,1024]{1,0:T(8,128)(2,1)S(1)} collective-permute-done((bf16[128,1024]{1,0:T(8,128)(2,1)S(1)}, bf16[128,1024]{1,0:T(8,128)(2,1)S(1)}, u32[]{:S(2)}, u32[]{:S(2)}) %collective-permute-start.17) | collective-permute-done | bytes 262176 | tf_op jit(solution)/shard_map/ppermute | solution.py:441
  48.1 0.1 shard_map.101
  48.2 1.0 %collective-permute-start.18 = (bf16[128,1024]{1,0:T(8,128)(2,1)S(1)}, bf16[128,1024]{1,0:T(8,128)(2,1)S(1)}, u32[]{:S(2)}, u32[]{:S(2)}) collective-permute-start(bf16[128,1024]{1,0:T(8,128)(2,1)S(1)} %shard_map.101), channel_id=1, source_target_pairs={{0,16},{4,12},{8,24},{12,4},{16,0},{20,28},{24,8},{28,20},{1,17},{... | collective-permute-start | bytes 786440 | tf_op jit(solution)/shard_map/ppermute | solution.py:441
  49.2 6.0 %collective-permute-done.12.refs_0_.refs_1_ = bf16[384,256]{1,0:T(8,128)(2,1)S(1)} collective-permute-done((bf16[384,256]{1,0:T(8,128)(2,1)S(1)}, bf16[384,256]{1,0:T(8,128)(2,1)S(1)}, u32[]{:S(2)}, u32[]{:S(2)}) %collective-permute-start.12) | collective-permute-done | bytes 196640 | tf_op jit(solution)/shard_map/ppermute | solution.py:436
  55.2 1.0 %collective-permute-done.14.refs_2_.refs_3_ = bf16[384,256]{1,0:T(8,128)(2,1)S(1)} collective-permute-done((bf16[384,256]{1,0:T(8,128)(2,1)S(1)}, bf16[384,256]{1,0:T(8,128)(2,1)S(1)}, u32[]{:S(2)}, u32[]{:S(2)}) %collective-permute-start.14) | collective-permute-done | bytes 196640 | tf_op jit(solution)/shard_map/ppermute | solution.py:436
  56.2 1.2 %collective-permute-done.18.refs_8_ = bf16[128,1024]{1,0:T(8,128)(2,1)S(1)} collective-permute-done((bf16[128,1024]{1,0:T(8,128)(2,1)S(1)}, bf16[128,1024]{1,0:T(8,128)(2,1)S(1)}, u32[]{:S(2)}, u32[]{:S(2)}) %collective-permute-start.18) | collective-permute-done | bytes 262176 | tf_op jit(solution)/shard_map/ppermute | solution.py:441
  57.5 1.5 %shard_map.104 = (bf16[1536,256]{1,0:T(8,128)(2,1)}, bf16[384,1024]{1,0:T(8,128)(2,1)}) custom-call(bf16[384,256]{1,0:T(8,128)(2,1)S(1)} %get-tuple-element.105.part_ref.refs_0_, bf16[384,256]{1,0:T(8,128)(2,1)S(1)} %collective-permute-done.12.refs_0_.refs_1_, ...), custom_call_target="tpu_custom_call", output_to_operand_aliasing={{0}: (10, {})} | custom-call | bytes 6492160 | tf_op jit(solution)/shard_map/pallas_call | solution.py:47
  (17 shorter events, 0.0 us)
Async XLA Ops:
  0.6 14.8 %collective-permute-start = (bf16[384,1024]{1,0:T(8,128)(2,1)}, bf16[384,1024]{1,0:T(8,128)(2,1)S(1)}, u32[]{:S(2)}, u32[]{:S(2)}) collective-permute-start(bf16[384,1024]{1,0:T(8,128)(2,1)} %raw_ref.1), channel_id=1, source_target_pairs={{0,16},{4,12},{8,24},{12,4},{16,0},{20,28},{24,8},{28,20},{1,17},{... | collective-permute-start | bytes 2359304 | tf_op jit(solution)/shard_map/ppermute | solution.py:441
  3.7 1.1 %copy-start = (bf16[1536,256]{1,0:T(8,128)(2,1)S(1)}, bf16[1536,256]{1,0:T(8,128)(2,1)}, u32[]{:S(2)}) copy-start(bf16[1536,256]{1,0:T(8,128)(2,1)} %text_ref.1) | copy-start | bytes 2359300
  4.8 8.6 %copy-start.1 = (s32[12288]{0:T(1024)S(1)}, s32[12288]{0:T(1024)}, u32[]{:S(2)}) copy-start(s32[12288]{0:T(1024)} %param.11) | copy-start | bytes 147460
  4.8 8.6 %copy-start.2 = (s32[12288]{0:T(1024)S(1)}, s32[12288]{0:T(1024)}, u32[]{:S(2)}) copy-start(s32[12288]{0:T(1024)} %param.12) | copy-start | bytes 147460
  4.8 8.6 %copy-start.3 = (s32[96,8,3]{0,1,2:T(8,128)S(1)}, s32[96,8,3]{0,1,2:T(8,128)}, u32[]{:S(2)}) copy-start(s32[96,8,3]{0,1,2:T(8,128)} %param.13) | copy-start | bytes 27652
  4.9 18.3 %collective-permute-start.1 = (bf16[384,256]{1,0:T(8,128)(2,1)S(1)}, bf16[384,256]{1,0:T(8,128)(2,1)S(1)}, u32[]{:S(2)}, u32[]{:S(2)}) collective-permute-start(bf16[384,256]{1,0:T(8,128)(2,1)S(1)} %get-tuple-element.74), channel_id=1, source_target_pairs={{0,2},{1,3},{2,0},{3,1},{4,6},{5,7},{6,4},{7,5},{8,10},{9,11},{10,... | collective-permute-start | bytes 589832 | tf_op jit(solution)/shard_map/ppermute | solution.py:436
  7.5 15.6 %collective-permute-start.2 = (bf16[384,256]{1,0:T(8,128)(2,1)S(1)}, bf16[384,256]{1,0:T(8,128)(2,1)S(1)}, u32[]{:S(2)}, u32[]{:S(2)}) collective-permute-start(bf16[384,256]{1,0:T(8,128)(2,1)S(1)} %get-tuple-element.75), channel_id=1, source_target_pairs={{0,3},{1,2},{2,1},{3,0},{4,7},{5,6},{6,5},{7,4},{8,11},{9,10},{10,... | collective-permute-start | bytes 589832 | tf_op jit(solution)/shard_map/ppermute | solution.py:436
  8.9 14.3 %collective-permute-start.3 = (bf16[384,256]{1,0:T(8,128)(2,1)S(1)}, bf16[384,256]{1,0:T(8,128)(2,1)S(1)}, u32[]{:S(2)}, u32[]{:S(2)}) collective-permute-start(bf16[384,256]{1,0:T(8,128)(2,1)S(1)} %get-tuple-element.76), channel_id=1, source_target_pairs={{0,1},{1,0},{2,3},{3,2},{4,5},{5,4},{6,7},{7,6},{8,9},{9,8},{10,11... | collective-permute-start | bytes 589832 | tf_op jit(solution)/shard_map/ppermute | solution.py:436
  10.5 12.3 %collective-permute-start.4 = (bf16[384,1024]{1,0:T(8,128)(2,1)}, bf16[384,1024]{1,0:T(8,128)(2,1)S(1)}, u32[]{:S(2)}, u32[]{:S(2)}) collective-permute-start(bf16[384,1024]{1,0:T(8,128)(2,1)} %raw_ref.1), channel_id=1, source_target_pairs={{0,8},{4,20},{8,0},{12,28},{16,24},{20,4},{24,16},{28,12},{1,9},{5... | collective-permute-start | bytes 2359304 | tf_op jit(solution)/shard_map/ppermute | solution.py:441
  15.4 15.8 %collective-permute-start.8 = (bf16[384,1024]{1,0:T(8,128)(2,1)S(1)}, bf16[384,1024]{1,0:T(8,128)(2,1)S(1)}, u32[]{:S(2)}, u32[]{:S(2)}) collective-permute-start(bf16[384,1024]{1,0:T(8,128)(2,1)S(1)} %collective-permute-done.raw_ref), channel_id=1, source_target_pairs={{0,8},{4,20},{8,0},{12,28},{16,24},{20,4},{24,16},{28,12},{1,9},{5... | collective-permute-start | bytes 2359304 | tf_op jit(solution)/shard_map/ppermute | solution.py:441
  23.5 2.1 %collective-permute-start.5 = (bf16[128,1024]{1,0:T(8,128)(2,1)S(1)}, bf16[128,1024]{1,0:T(8,128)(2,1)S(1)}, u32[]{:S(2)}, u32[]{:S(2)}) collective-permute-start(bf16[128,1024]{1,0:T(8,128)(2,1)S(1)} %get-tuple-element.84), channel_id=1, source_target_pairs={{0,4},{4,0},{8,12},{12,8},{16,20},{20,16},{24,28},{28,24},{1,5},{5... | collective-permute-start | bytes 786440 | tf_op jit(solution)/shard_map/ppermute | solution.py:436
  23.6 2.0 %collective-permute-start.6 = (bf16[128,1024]{1,0:T(8,128)(2,1)S(1)}, bf16[128,1024]{1,0:T(8,128)(2,1)S(1)}, u32[]{:S(2)}, u32[]{:S(2)}) collective-permute-start(bf16[128,1024]{1,0:T(8,128)(2,1)S(1)} %get-tuple-element.85), channel_id=1, source_target_pairs={{0,4},{4,0},{8,12},{12,8},{16,20},{20,16},{24,28},{28,24},{1,5},{5... | collective-permute-start | bytes 786440 | tf_op jit(solution)/shard_map/ppermute | solution.py:436
  24.1 1.8 %collective-permute-start.7 = (bf16[128,1024]{1,0:T(8,128)(2,1)S(1)}, bf16[128,1024]{1,0:T(8,128)(2,1)S(1)}, u32[]{:S(2)}, u32[]{:S(2)}) collective-permute-start(bf16[128,1024]{1,0:T(8,128)(2,1)S(1)} %get-tuple-element.86), channel_id=1, source_target_pairs={{0,4},{4,0},{8,12},{12,8},{16,20},{20,16},{24,28},{28,24},{1,5},{5... | collective-permute-start | bytes 786440 | tf_op jit(solution)/shard_map/ppermute | solution.py:436
  27.2 14.9 %collective-permute-start.11 = (bf16[384,1024]{1,0:T(8,128)(2,1)S(1)}, bf16[384,1024]{1,0:T(8,128)(2,1)S(1)}, u32[]{:S(2)}, u32[]{:S(2)}) collective-permute-start(bf16[384,1024]{1,0:T(8,128)(2,1)S(1)} %get-tuple-element.103), channel_id=1, source_target_pairs={{0,8},{4,20},{8,0},{12,28},{16,24},{20,4},{24,16},{28,12},{1,9},{5... | collective-permute-start | bytes 2359304 | tf_op jit(solution)/shard_map/ppermute | solution.py:441
  33.8 3.4 %collective-permute-start.9 = (bf16[192,1024]{1,0:T(8,128)(2,1)S(1)}, bf16[192,1024]{1,0:T(8,128)(2,1)S(1)}, u32[]{:S(2)}, u32[]{:S(2)}) collective-permute-start(bf16[192,1024]{1,0:T(8,128)(2,1)S(1)} %get-tuple-element.98), channel_id=1, source_target_pairs={{0,4},{4,0},{8,12},{12,8},{16,20},{20,16},{24,28},{28,24},{1,5},{5... | collective-permute-start | bytes 1179656 | tf_op jit(solution)/shard_map/ppermute | solution.py:436
  33.9 3.3 %collective-permute-start.10 = (bf16[192,1024]{1,0:T(8,128)(2,1)S(1)}, bf16[192,1024]{1,0:T(8,128)(2,1)S(1)}, u32[]{:S(2)}, u32[]{:S(2)}) collective-permute-start(bf16[192,1024]{1,0:T(8,128)(2,1)S(1)} %get-tuple-element.99), channel_id=1, source_target_pairs={{0,4},{4,0},{8,12},{12,8},{16,20},{20,16},{24,28},{28,24},{1,5},{5... | collective-permute-start | bytes 1179656 | tf_op jit(solution)/shard_map/ppermute | solution.py:436
  34.4 10.8 %collective-permute-start.15 = (bf16[256,1024]{1,0:T(8,128)(2,1)S(1)}, bf16[256,1024]{1,0:T(8,128)(2,1)S(1)}, u32[]{:S(2)}, u32[]{:S(2)}) collective-permute-start(bf16[256,1024]{1,0:T(8,128)(2,1)S(1)} %get-tuple-element.113), channel_id=1, source_target_pairs={{0,8},{4,20},{8,0},{12,28},{16,24},{20,4},{24,16},{28,12},{1,9},{5... | collective-permute-start | bytes 1572872 | tf_op jit(solution)/shard_map/ppermute | solution.py:441
  35.9 12.2 %collective-permute-start.17 = (bf16[128,1024]{1,0:T(8,128)(2,1)S(1)}, bf16[128,1024]{1,0:T(8,128)(2,1)S(1)}, u32[]{:S(2)}, u32[]{:S(2)}) collective-permute-start(bf16[128,1024]{1,0:T(8,128)(2,1)S(1)} %get-tuple-element.115), channel_id=1, source_target_pairs={{0,8},{4,20},{8,0},{12,28},{16,24},{20,4},{24,16},{28,12},{1,9},{5... | collective-permute-start | bytes 786440 | tf_op jit(solution)/shard_map/ppermute | solution.py:441
  37.9 17.3 %collective-permute-start.12 = (bf16[384,256]{1,0:T(8,128)(2,1)S(1)}, bf16[384,256]{1,0:T(8,128)(2,1)S(1)}, u32[]{:S(2)}, u32[]{:S(2)}) collective-permute-start(bf16[384,256]{1,0:T(8,128)(2,1)S(1)} %get-tuple-element.106), channel_id=1, source_target_pairs={{0,2},{1,3},{2,0},{3,1},{4,6},{5,7},{6,4},{7,5},{8,10},{9,11},{10,... | collective-permute-start | bytes 589832 | tf_op jit(solution)/shard_map/ppermute | solution.py:436
  41.5 13.7 %collective-permute-start.13 = (bf16[384,256]{1,0:T(8,128)(2,1)S(1)}, bf16[384,256]{1,0:T(8,128)(2,1)S(1)}, u32[]{:S(2)}, u32[]{:S(2)}) collective-permute-start(bf16[384,256]{1,0:T(8,128)(2,1)S(1)} %get-tuple-element.107), channel_id=1, source_target_pairs={{0,3},{1,2},{2,1},{3,0},{4,7},{5,6},{6,5},{7,4},{8,11},{9,10},{10,... | collective-permute-start | bytes 589832 | tf_op jit(solution)/shard_map/ppermute | solution.py:436
  42.1 14.1 %collective-permute-start.14 = (bf16[384,256]{1,0:T(8,128)(2,1)S(1)}, bf16[384,256]{1,0:T(8,128)(2,1)S(1)}, u32[]{:S(2)}, u32[]{:S(2)}) collective-permute-start(bf16[384,256]{1,0:T(8,128)(2,1)S(1)} %get-tuple-element.108), channel_id=1, source_target_pairs={{0,1},{1,0},{2,3},{3,2},{4,5},{5,4},{6,7},{7,6},{8,9},{9,8},{10,11... | collective-permute-start | bytes 589832 | tf_op jit(solution)/shard_map/ppermute | solution.py:436
  45.4 12.1 %collective-permute-start.16 = (bf16[256,1024]{1,0:T(8,128)(2,1)S(1)}, bf16[256,1024]{1,0:T(8,128)(2,1)S(1)}, u32[]{:S(2)}, u32[]{:S(2)}) collective-permute-start(bf16[256,1024]{1,0:T(8,128)(2,1)S(1)} %shard_map.100), channel_id=1, source_target_pairs={{0,16},{4,12},{8,24},{12,4},{16,0},{20,28},{24,8},{28,20},{1,17},{... | collective-permute-start | bytes 1572872 | tf_op jit(solution)/shard_map/ppermute | solution.py:441
  48.2 9.2 %collective-permute-start.18 = (bf16[128,1024]{1,0:T(8,128)(2,1)S(1)}, bf16[128,1024]{1,0:T(8,128)(2,1)S(1)}, u32[]{:S(2)}, u32[]{:S(2)}) collective-permute-start(bf16[128,1024]{1,0:T(8,128)(2,1)S(1)} %shard_map.101), channel_id=1, source_target_pairs={{0,16},{4,12},{8,24},{12,4},{16,0},{20,28},{24,8},{28,20},{1,17},{... | collective-permute-start | bytes 786440 | tf_op jit(solution)/shard_map/ppermute | solution.py:441

commit v22 on v21

--- a/solution.py
+++ b/solution.py
@@ -608,7 +608,7 @@
         limit=24,
     )
     own_weights, from_far = lax.optimization_barrier((own_weights, from_far))
-    sizes = [rows - TILE, TILE]
+    sizes = [rows // 2] * 2
     far_weights, far_images, *rest = call_kernel(
         functools.partial(far_body, tiles, len(sizes)),
         [bf16(2 * rows, 2 * rows), bf16(2 * rows)]

time: 59.2 us -> 59.6 us (level)
  waiting for transfers between devices: 16 us -> 16.9 us
  starting transfers between devices: 23.2 us -> 22.5 us
    ppermute x8, waiting for transfers between devices: 8.68 us -> 11 us  [swap_near(): lax.ppermute(value, 'blk', [(i, i ^ neighbour_bits(i)[which]) for i in ra...]
    ppermute x11, waiting for transfers between devices: 7.32 us -> 5.84 us  [swap(): return lax.ppermute(value, axis, [(i, i ^ bits) for i in range(count)])]
    ppermute x8, starting transfers between devices: 13.5 us -> 12.7 us  [swap_near(): lax.ppermute(value, 'blk', [(i, i ^ neighbour_bits(i)[which]) for i in ra...]
where the time goes in v22:
time: 59.6 us; the launch traced here: 59.1 us
  starting transfers between devices  22.5 us (38%)
  waiting for transfers between devices  16.9 us (28%)
  Pallas kernels  16.4 us (28%)
  between operations  2.13 us (4%)
  local copies, waits for them, and re-layouts  1.14 us (2%)
    pallas_call x19, Pallas kernels, call_kernel(): pl.pallas_call(body, out_shape=outs, in_specs=specs, out_specs=[ANY_SPEC...  16.4 us
    ppermute x8, starting transfers between devices, swap_near(): lax.ppermute(value, 'blk', [(i, i ^ neighbour_bits(i)[which]) for i in ra...  12.7 us
    ppermute x8, waiting for transfers between devices, swap_near(): lax.ppermute(value, 'blk', [(i, i ^ neighbour_bits(i)[which]) for i in ra...  11 us
    ppermute x11, starting transfers between devices, swap(): return lax.ppermute(value, axis, [(i, i ^ bits) for i in range(count)])  9.73 us
    ppermute x11, waiting for transfers between devices, swap(): return lax.ppermute(value, axis, [(i, i ^ bits) for i in range(count)])  5.84 us
  transfers between devices with their start and end apart: 19, of which 9 were waited for; matrix products, arithmetic and copies ran while one was open for 0% of the time, Pallas kernels for 25%

profile of v22, /device:TPU:0, one launch (start us, length us, event | category | flops | bytes accessed | tf_op | source)
XLA Modules:
  0.0 59.1 jit_solution(1185424037643462991)
XLA Ops:
  0.6 3.0 %collective-permute-start = (bf16[384,1024]{1,0:T(8,128)(2,1)}, bf16[384,1024]{1,0:T(8,128)(2,1)S(1)}, u32[]{:S(2)}, u32[]{:S(2)}) collective-permute-start(bf16[384,1024]{1,0:T(8,128)(2,1)} %raw_ref.1), channel_id=1, source_target_pairs={{0,16},{4,12},{8,24},{12,4},{16,0},{20,28},{24,8},{28,20},{1,17},{... | collective-permute-start | bytes 2359304 | tf_op jit(solution)/shard_map/ppermute | solution.py:441
  3.7 1.1 %copy-done = bf16[1536,256]{1,0:T(8,128)(2,1)S(1)} copy-done((bf16[1536,256]{1,0:T(8,128)(2,1)S(1)}, bf16[1536,256]{1,0:T(8,128)(2,1)}, u32[]{:S(2)}) %copy-start) | copy-done | bytes 786456
  4.8 0.1 shard_map.88
  4.9 2.7 %collective-permute-start.1 = (bf16[384,256]{1,0:T(8,128)(2,1)S(1)}, bf16[384,256]{1,0:T(8,128)(2,1)S(1)}, u32[]{:S(2)}, u32[]{:S(2)}) collective-permute-start(bf16[384,256]{1,0:T(8,128)(2,1)S(1)} %get-tuple-element.74), channel_id=1, source_target_pairs={{0,2},{1,3},{2,0},{3,1},{4,6},{5,7},{6,4},{7,5},{8,10},{9,11},{10,... | collective-permute-start | bytes 589832 | tf_op jit(solution)/shard_map/ppermute | solution.py:436
  7.5 1.3 %collective-permute-start.2 = (bf16[384,256]{1,0:T(8,128)(2,1)S(1)}, bf16[384,256]{1,0:T(8,128)(2,1)S(1)}, u32[]{:S(2)}, u32[]{:S(2)}) collective-permute-start(bf16[384,256]{1,0:T(8,128)(2,1)S(1)} %get-tuple-element.75), channel_id=1, source_target_pairs={{0,3},{1,2},{2,1},{3,0},{4,7},{5,6},{6,5},{7,4},{8,11},{9,10},{10,... | collective-permute-start | bytes 589832 | tf_op jit(solution)/shard_map/ppermute | solution.py:436
  8.9 0.2 collective-permute-start.3
  9.1 1.4 %shard_map.86 = (bf16[384,1024]{1,0:T(8,128)(2,1)S(1)}, bf16[384,1024]{1,0:T(8,128)(2,1)S(1)}, f32[384,128]{1,0:T(8,128)S(1)}) custom-call(bf16[384,1024]{1,0:T(8,128)(2,1)} %raw_ref.1), custom_call_target="tpu_custom_call" | custom-call | bytes 2555904 | tf_op jit(solution)/shard_map/pallas_call | solution.py:47
  10.5 1.6 %collective-permute-start.4 = (bf16[384,1024]{1,0:T(8,128)(2,1)}, bf16[384,1024]{1,0:T(8,128)(2,1)S(1)}, u32[]{:S(2)}, u32[]{:S(2)}) collective-permute-start(bf16[384,1024]{1,0:T(8,128)(2,1)} %raw_ref.1), channel_id=1, source_target_pairs={{0,8},{4,20},{8,0},{12,28},{16,24},{20,4},{24,16},{28,12},{1,9},{5... | collective-permute-start | bytes 2359304 | tf_op jit(solution)/shard_map/ppermute | solution.py:441
  13.4 1.1 %shard_map.87 = (f32[2,128]{1,0:T(2,128)S(1)}, f32[72,128]{1,0:T(8,128)S(1)}, s32[12,128]{1,0:T(8,128)S(1)}, s32[768,128]{1,0:T(8,128)S(1)}, f32[384,128]{1,0:T(8,128)S(1)}, /*index=5*/f32[4,128]{1,0:T(4,128)S(1)}) custom-call(f32[1]{0:T(128)S(6)} %copy.11.refs_0_, f32[1]{0:T(128)S(6)} %copy.12.refs_1_, s32[3,8,96]{2,1,0:T(8,128)S(1)} %bitcast.5, ...), custom_call_target="tpu_custom_call" | custom-call | bytes 743432 | tf_op jit(solution)/shard_map/pallas_call | solution.py:47
  14.5 0.9 %collective-permute-done.raw_ref = bf16[384,1024]{1,0:T(8,128)(2,1)S(1)} collective-permute-done((bf16[384,1024]{1,0:T(8,128)(2,1)}, bf16[384,1024]{1,0:T(8,128)(2,1)S(1)}, u32[]{:S(2)}, u32[]{:S(2)}) %collective-permute-start) | collective-permute-done | bytes 786464 | tf_op jit(solution)/shard_map/ppermute | solution.py:441
  15.4 3.3 %collective-permute-start.8 = (bf16[384,1024]{1,0:T(8,128)(2,1)S(1)}, bf16[384,1024]{1,0:T(8,128)(2,1)S(1)}, u32[]{:S(2)}, u32[]{:S(2)}) collective-permute-start(bf16[384,1024]{1,0:T(8,128)(2,1)S(1)} %collective-permute-done.raw_ref), channel_id=1, source_target_pairs={{0,8},{4,20},{8,0},{12,28},{16,24},{20,4},{24,16},{28,12},{1,9},{5... | collective-permute-start | bytes 2359304 | tf_op jit(solution)/shard_map/ppermute | solution.py:441
  18.7 0.2 shard_map.89.second_unit_ref
  19.0 3.8 %collective-permute-done.4.first_ref = bf16[384,1024]{1,0:T(8,128)(2,1)S(1)} collective-permute-done((bf16[384,1024]{1,0:T(8,128)(2,1)}, bf16[384,1024]{1,0:T(8,128)(2,1)S(1)}, u32[]{:S(2)}, u32[]{:S(2)}) %collective-permute-start.4) | collective-permute-done | bytes 786464 | tf_op jit(solution)/shard_map/ppermute | solution.py:441
  22.8 0.3 shard_map.90.refs_7_
  23.1 0.0 collective-permute-done.1.refs_1_.refs_2_
  23.2 0.4 shard_map.91
  23.5 0.1 collective-permute-start.5
  23.6 0.5 collective-permute-start.6
  24.1 0.1 collective-permute-start.7
  24.2 1.4 %shard_map.92 = (bf16[384,384]{1,0:T(8,128)(2,1)S(1)}, bf16[384,768]{1,0:T(8,128)(2,1)S(1)}) custom-call(f32[2,128]{1,0:T(2,128)S(1)} %get-tuple-element.67.refs_0_, f32[72,128]{1,0:T(8,128)S(1)} %get-tuple-element.68.refs_1_, s32[12,128]{1,0:T(8,128)S(1)} %get-tuple-element.69.refs_2_, s32[768,128]{1,0:T(8,128)S(1)} %get-tuple-element.70.refs_3_, ...), custom_call_target="tpu_custom_call" | custom-call | bytes 4666368 | tf_op jit(solution)/shard_map/pallas_call | solution.py:47
  25.6 0.2 collective-permute-done.7.refs_11_
  25.9 1.3 %shard_map.93 = (bf16[768,1024]{1,0:T(8,128)(2,1)S(1)}, bf16[768,384]{1,0:T(8,128)(2,1)S(1)}, bf16[384,1024]{1,0:T(8,128)(2,1)S(1)}) custom-call(f32[2,128]{1,0:T(2,128)S(1)} %get-tuple-element.67.refs_0_, f32[72,128]{1,0:T(8,128)S(1)} %get-tuple-element.68.refs_1_, s32[12,128]{1,0:T(8,128)S(1)} %get-tuple-element.69.refs_2_, ...), custom_call_target="tpu_custom_call" | custom-call | bytes 8107008 | tf_op jit(solution)/shard_map/pallas_call | solution.py:47
  27.2 1.6 %collective-permute-start.11 = (bf16[384,1024]{1,0:T(8,128)(2,1)S(1)}, bf16[384,1024]{1,0:T(8,128)(2,1)S(1)}, u32[]{:S(2)}, u32[]{:S(2)}) collective-permute-start(bf16[384,1024]{1,0:T(8,128)(2,1)S(1)} %get-tuple-element.103), channel_id=1, source_target_pairs={{0,8},{4,20},{8,0},{12,28},{16,24},{20,4},{24,16},{28,12},{1,9},{5... | collective-permute-start | bytes 2359304 | tf_op jit(solution)/shard_map/ppermute | solution.py:441
  28.8 2.2 %shard_map.94 = (bf16[768,384]{1,0:T(8,128)(2,1)S(1)}, f32[768,1024]{1,0:T(8,128)S(1)}, bf16[768,768]{1,0:T(8,128)(2,1)S(1)}) custom-call(f32[2,128]{1,0:T(2,128)S(1)} %get-tuple-element.67.refs_0_, f32[72,128]{1,0:T(8,128)S(1)} %get-tuple-element.68.refs_1_, s32[12,128]{1,0:T(8,128)S(1)} %get-tuple-element.69.refs_2_, ...), custom_call_target="tpu_custom_call" | custom-call | bytes 10957824 | tf_op jit(solution)/shard_map/pallas_call | solution.py:47
  31.0 0.2 collective-permute-done.8.refs_9_
  31.2 2.6 %shard_map.95 = (bf16[768,768]{1,0:T(8,128)(2,1)S(1)}, bf16[768,1024]{1,0:T(8,128)(2,1)S(1)}, bf16[192,1024]{1,0:T(8,128)(2,1)S(1)}, bf16[192,1024]{1,0:T(8,128)...) custom-call(f32[2,128]{1,0:T(2,128)S(1)} %get-tuple-element.67.refs_0_, ...), custom_call_target="tpu_custom_call" | custom-call | bytes 11842560 | tf_op jit(solution)/shard_map/pallas_call | solution.py:47
  33.8 0.1 collective-permute-start.9
  33.9 0.5 collective-permute-start.10
  34.4 1.5 %collective-permute-start.15 = (bf16[192,1024]{1,0:T(8,128)(2,1)S(1)}, bf16[192,1024]{1,0:T(8,128)(2,1)S(1)}, u32[]{:S(2)}, u32[]{:S(2)}) collective-permute-start(bf16[192,1024]{1,0:T(8,128)(2,1)S(1)} %get-tuple-element.113), channel_id=1, source_target_pairs={{0,8},{4,20},{8,0},{12,28},{16,24},{20,4},{24,16},{28,12},{1,9},{5... | collective-permute-start | bytes 1179656 | tf_op jit(solution)/shard_map/ppermute | solution.py:441
  35.9 0.5 collective-permute-start.17
  36.4 0.8 %shard_map.96.refs_5_ = f32[384,1024]{1,0:T(8,128)S(1)} custom-call(bf16[768,768]{1,0:T(8,128)(2,1)S(1)} %get-tuple-element.96.weight_ref, bf16[768,1024]{1,0:T(8,128)(2,1)S(1)} %get-tuple-element.97.image_ref, f32[768,1024]{1,0:T(8,128)S(1)} %get-tuple-element.95.refs_10_.acc_ref), custom_call_target="tpu_custom_call" | custom-call | bytes 7471104 | tf_op jit(solution)/shard_map/pallas_call | solution.py:47
  37.2 0.6 %shard_map.97 = (bf16[384,256]{1,0:T(8,128)(2,1)S(1)}, bf16[384,256]{1,0:T(8,128)(2,1)S(1)}, bf16[384,256]{1,0:T(8,128)(2,1)S(1)}, bf16[384,256]{1,0:T(8,128)(2,1)S(1)}) custom-call(f32[384,128]{1,0:T(8,128)S(1)} %get-tuple-element.91.refs_0_, bf16[384,256]{1,0:T(8,128)(2,1)S(1)} %get-tuple-element.73.refs_0_.refs_1_, ...), custom_call_target="tpu_custom_call" | custom-call | bytes 4128768 | tf_op jit(solution)/shard_map/pallas_call | solution.py:47
  37.9 3.6 %collective-permute-start.12 = (bf16[384,256]{1,0:T(8,128)(2,1)S(1)}, bf16[384,256]{1,0:T(8,128)(2,1)S(1)}, u32[]{:S(2)}, u32[]{:S(2)}) collective-permute-start(bf16[384,256]{1,0:T(8,128)(2,1)S(1)} %get-tuple-element.106), channel_id=1, source_target_pairs={{0,2},{1,3},{2,0},{3,1},{4,6},{5,7},{6,4},{7,5},{8,10},{9,11},{10,... | collective-permute-start | bytes 589832 | tf_op jit(solution)/shard_map/ppermute | solution.py:436
  41.5 0.6 collective-permute-start.13
  42.1 0.1 collective-permute-start.14
  42.1 0.8 %shard_map.98 = (f32[384,1024]{1,0:T(8,128)S(1)}, bf16[384,1024]{1,0:T(8,128)(2,1)S(1)}) custom-call(bf16[768,768]{1,0:T(8,128)(2,1)S(1)} %get-tuple-element.102.weight_ref, bf16[768,1024]{1,0:T(8,128)(2,1)S(1)} %get-tuple-element.87.refs_6_.unit_ref, bf16[384,1024]{1,0:T(8,128)(2,1)S(1)} %collective-permute-done.11.add_ref), custom_call_target="tpu_custom_call" | custom-call | bytes 5898240 | tf_op jit(solution)/shard_map/pallas_call | solution.py:47
  43.0 0.9 %collective-permute-done.15.in_ref = bf16[192,1024]{1,0:T(8,128)(2,1)S(1)} collective-permute-done((bf16[192,1024]{1,0:T(8,128)(2,1)S(1)}, bf16[192,1024]{1,0:T(8,128)(2,1)S(1)}, u32[]{:S(2)}, u32[]{:S(2)}) %collective-permute-start.15) | collective-permute-done | bytes 393248 | tf_op jit(solution)/shard_map/ppermute | solution.py:441
  43.8 0.1 shard_map.100
  43.9 1.0 %collective-permute-start.16 = (bf16[192,1024]{1,0:T(8,128)(2,1)S(1)}, bf16[192,1024]{1,0:T(8,128)(2,1)S(1)}, u32[]{:S(2)}, u32[]{:S(2)}) collective-permute-start(bf16[192,1024]{1,0:T(8,128)(2,1)S(1)} %shard_map.100), channel_id=1, source_target_pairs={{0,16},{4,12},{8,24},{12,4},{16,0},{20,28},{24,8},{28,20},{1,17},{... | collective-permute-start | bytes 1179656 | tf_op jit(solution)/shard_map/ppermute | solution.py:441
  44.9 0.8 %shard_map.99.refs_6_ = f32[384,1024]{1,0:T(8,128)S(1)} custom-call(bf16[768,384]{1,0:T(8,128)(2,1)S(1)} %get-tuple-element.93.refs_8_.weight_ref, bf16[768,1024]{1,0:T(8,128)(2,1)S(1)} %get-tuple-element.87.refs_6_.unit_ref, bf16[384,1024]{1,0:T(8,128)(2,1)S(1)} %get-tuple-element.104.add_ref), custom_call_target="tpu_custom_call" | custom-call | tf_op jit(solution)/shard_map/pallas_call | solution.py:47
  45.8 3.9 %collective-permute-done.17.in_ref = bf16[192,1024]{1,0:T(8,128)(2,1)S(1)} collective-permute-done((bf16[192,1024]{1,0:T(8,128)(2,1)S(1)}, bf16[192,1024]{1,0:T(8,128)(2,1)S(1)}, u32[]{:S(2)}, u32[]{:S(2)}) %collective-permute-start.17) | collective-permute-done | bytes 393248 | tf_op jit(solution)/shard_map/ppermute | solution.py:441
  49.6 0.1 shard_map.101
  49.7 0.2 collective-permute-start.18
  49.9 0.7 %shard_map.103.refs_10_ = bf16[1536,256]{1,0:T(8,128)(2,1)} custom-call(bf16[384,256]{1,0:T(8,128)(2,1)S(1)} %get-tuple-element.105.part_ref.refs_0_), custom_call_target="tpu_custom_call" | custom-call | tf_op jit(solution)/shard_map/pallas_call | solution.py:47
  50.6 4.6 %collective-permute-done.12.refs_0_.refs_1_ = bf16[384,256]{1,0:T(8,128)(2,1)S(1)} collective-permute-done((bf16[384,256]{1,0:T(8,128)(2,1)S(1)}, bf16[384,256]{1,0:T(8,128)(2,1)S(1)}, u32[]{:S(2)}, u32[]{:S(2)}) %collective-permute-start.12) | collective-permute-done | bytes 196640 | tf_op jit(solution)/shard_map/ppermute | solution.py:436
  55.2 1.0 %collective-permute-done.14.refs_2_.refs_3_ = bf16[384,256]{1,0:T(8,128)(2,1)S(1)} collective-permute-done((bf16[384,256]{1,0:T(8,128)(2,1)S(1)}, bf16[384,256]{1,0:T(8,128)(2,1)S(1)}, u32[]{:S(2)}, u32[]{:S(2)}) %collective-permute-start.14) | collective-permute-done | bytes 196640 | tf_op jit(solution)/shard_map/ppermute | solution.py:436
  56.2 1.3 %collective-permute-done.18.refs_8_ = bf16[192,1024]{1,0:T(8,128)(2,1)S(1)} collective-permute-done((bf16[192,1024]{1,0:T(8,128)(2,1)S(1)}, bf16[192,1024]{1,0:T(8,128)(2,1)S(1)}, u32[]{:S(2)}, u32[]{:S(2)}) %collective-permute-start.18) | collective-permute-done | bytes 393248 | tf_op jit(solution)/shard_map/ppermute | solution.py:441
  57.6 1.5 %shard_map.104 = (bf16[1536,256]{1,0:T(8,128)(2,1)}, bf16[384,1024]{1,0:T(8,128)(2,1)}) custom-call(bf16[384,256]{1,0:T(8,128)(2,1)S(1)} %get-tuple-element.105.part_ref.refs_0_, bf16[384,256]{1,0:T(8,128)(2,1)S(1)} %collective-permute-done.12.refs_0_.refs_1_, ...), custom_call_target="tpu_custom_call", output_to_operand_aliasing={{0}: (10, {})} | custom-call | bytes 6492160 | tf_op jit(solution)/shard_map/pallas_call | solution.py:47
  (17 shorter events, 0.0 us)
Async XLA Ops:
  0.6 14.8 %collective-permute-start = (bf16[384,1024]{1,0:T(8,128)(2,1)}, bf16[384,1024]{1,0:T(8,128)(2,1)S(1)}, u32[]{:S(2)}, u32[]{:S(2)}) collective-permute-start(bf16[384,1024]{1,0:T(8,128)(2,1)} %raw_ref.1), channel_id=1, source_target_pairs={{0,16},{4,12},{8,24},{12,4},{16,0},{20,28},{24,8},{28,20},{1,17},{... | collective-permute-start | bytes 2359304 | tf_op jit(solution)/shard_map/ppermute | solution.py:441
  3.7 1.1 %copy-start = (bf16[1536,256]{1,0:T(8,128)(2,1)S(1)}, bf16[1536,256]{1,0:T(8,128)(2,1)}, u32[]{:S(2)}) copy-start(bf16[1536,256]{1,0:T(8,128)(2,1)} %text_ref.1) | copy-start | bytes 2359300
  4.8 8.6 %copy-start.1 = (s32[12288]{0:T(1024)S(1)}, s32[12288]{0:T(1024)}, u32[]{:S(2)}) copy-start(s32[12288]{0:T(1024)} %param.11) | copy-start | bytes 147460
  4.8 8.6 %copy-start.2 = (s32[12288]{0:T(1024)S(1)}, s32[12288]{0:T(1024)}, u32[]{:S(2)}) copy-start(s32[12288]{0:T(1024)} %param.12) | copy-start | bytes 147460
  4.8 8.6 %copy-start.3 = (s32[96,8,3]{0,1,2:T(8,128)S(1)}, s32[96,8,3]{0,1,2:T(8,128)}, u32[]{:S(2)}) copy-start(s32[96,8,3]{0,1,2:T(8,128)} %param.13) | copy-start | bytes 27652
  4.9 18.3 %collective-permute-start.1 = (bf16[384,256]{1,0:T(8,128)(2,1)S(1)}, bf16[384,256]{1,0:T(8,128)(2,1)S(1)}, u32[]{:S(2)}, u32[]{:S(2)}) collective-permute-start(bf16[384,256]{1,0:T(8,128)(2,1)S(1)} %get-tuple-element.74), channel_id=1, source_target_pairs={{0,2},{1,3},{2,0},{3,1},{4,6},{5,7},{6,4},{7,5},{8,10},{9,11},{10,... | collective-permute-start | bytes 589832 | tf_op jit(solution)/shard_map/ppermute | solution.py:436
  7.5 15.6 %collective-permute-start.2 = (bf16[384,256]{1,0:T(8,128)(2,1)S(1)}, bf16[384,256]{1,0:T(8,128)(2,1)S(1)}, u32[]{:S(2)}, u32[]{:S(2)}) collective-permute-start(bf16[384,256]{1,0:T(8,128)(2,1)S(1)} %get-tuple-element.75), channel_id=1, source_target_pairs={{0,3},{1,2},{2,1},{3,0},{4,7},{5,6},{6,5},{7,4},{8,11},{9,10},{10,... | collective-permute-start | bytes 589832 | tf_op jit(solution)/shard_map/ppermute | solution.py:436
  8.9 14.3 %collective-permute-start.3 = (bf16[384,256]{1,0:T(8,128)(2,1)S(1)}, bf16[384,256]{1,0:T(8,128)(2,1)S(1)}, u32[]{:S(2)}, u32[]{:S(2)}) collective-permute-start(bf16[384,256]{1,0:T(8,128)(2,1)S(1)} %get-tuple-element.76), channel_id=1, source_target_pairs={{0,1},{1,0},{2,3},{3,2},{4,5},{5,4},{6,7},{7,6},{8,9},{9,8},{10,11... | collective-permute-start | bytes 589832 | tf_op jit(solution)/shard_map/ppermute | solution.py:436
  10.5 12.3 %collective-permute-start.4 = (bf16[384,1024]{1,0:T(8,128)(2,1)}, bf16[384,1024]{1,0:T(8,128)(2,1)S(1)}, u32[]{:S(2)}, u32[]{:S(2)}) collective-permute-start(bf16[384,1024]{1,0:T(8,128)(2,1)} %raw_ref.1), channel_id=1, source_target_pairs={{0,8},{4,20},{8,0},{12,28},{16,24},{20,4},{24,16},{28,12},{1,9},{5... | collective-permute-start | bytes 2359304 | tf_op jit(solution)/shard_map/ppermute | solution.py:441
  15.4 15.8 %collective-permute-start.8 = (bf16[384,1024]{1,0:T(8,128)(2,1)S(1)}, bf16[384,1024]{1,0:T(8,128)(2,1)S(1)}, u32[]{:S(2)}, u32[]{:S(2)}) collective-permute-start(bf16[384,1024]{1,0:T(8,128)(2,1)S(1)} %collective-permute-done.raw_ref), channel_id=1, source_target_pairs={{0,8},{4,20},{8,0},{12,28},{16,24},{20,4},{24,16},{28,12},{1,9},{5... | collective-permute-start | bytes 2359304 | tf_op jit(solution)/shard_map/ppermute | solution.py:441
  23.5 2.1 %collective-permute-start.5 = (bf16[128,1024]{1,0:T(8,128)(2,1)S(1)}, bf16[128,1024]{1,0:T(8,128)(2,1)S(1)}, u32[]{:S(2)}, u32[]{:S(2)}) collective-permute-start(bf16[128,1024]{1,0:T(8,128)(2,1)S(1)} %get-tuple-element.84), channel_id=1, source_target_pairs={{0,4},{4,0},{8,12},{12,8},{16,20},{20,16},{24,28},{28,24},{1,5},{5... | collective-permute-start | bytes 786440 | tf_op jit(solution)/shard_map/ppermute | solution.py:436
  23.6 2.0 %collective-permute-start.6 = (bf16[128,1024]{1,0:T(8,128)(2,1)S(1)}, bf16[128,1024]{1,0:T(8,128)(2,1)S(1)}, u32[]{:S(2)}, u32[]{:S(2)}) collective-permute-start(bf16[128,1024]{1,0:T(8,128)(2,1)S(1)} %get-tuple-element.85), channel_id=1, source_target_pairs={{0,4},{4,0},{8,12},{12,8},{16,20},{20,16},{24,28},{28,24},{1,5},{5... | collective-permute-start | bytes 786440 | tf_op jit(solution)/shard_map/ppermute | solution.py:436
  24.1 1.8 %collective-permute-start.7 = (bf16[128,1024]{1,0:T(8,128)(2,1)S(1)}, bf16[128,1024]{1,0:T(8,128)(2,1)S(1)}, u32[]{:S(2)}, u32[]{:S(2)}) collective-permute-start(bf16[128,1024]{1,0:T(8,128)(2,1)S(1)} %get-tuple-element.86), channel_id=1, source_target_pairs={{0,4},{4,0},{8,12},{12,8},{16,20},{20,16},{24,28},{28,24},{1,5},{5... | collective-permute-start | bytes 786440 | tf_op jit(solution)/shard_map/ppermute | solution.py:436
  27.2 14.9 %collective-permute-start.11 = (bf16[384,1024]{1,0:T(8,128)(2,1)S(1)}, bf16[384,1024]{1,0:T(8,128)(2,1)S(1)}, u32[]{:S(2)}, u32[]{:S(2)}) collective-permute-start(bf16[384,1024]{1,0:T(8,128)(2,1)S(1)} %get-tuple-element.103), channel_id=1, source_target_pairs={{0,8},{4,20},{8,0},{12,28},{16,24},{20,4},{24,16},{28,12},{1,9},{5... | collective-permute-start | bytes 2359304 | tf_op jit(solution)/shard_map/ppermute | solution.py:441
  33.8 3.4 %collective-permute-start.9 = (bf16[192,1024]{1,0:T(8,128)(2,1)S(1)}, bf16[192,1024]{1,0:T(8,128)(2,1)S(1)}, u32[]{:S(2)}, u32[]{:S(2)}) collective-permute-start(bf16[192,1024]{1,0:T(8,128)(2,1)S(1)} %get-tuple-element.98), channel_id=1, source_target_pairs={{0,4},{4,0},{8,12},{12,8},{16,20},{20,16},{24,28},{28,24},{1,5},{5... | collective-permute-start | bytes 1179656 | tf_op jit(solution)/shard_map/ppermute | solution.py:436
  33.9 3.3 %collective-permute-start.10 = (bf16[192,1024]{1,0:T(8,128)(2,1)S(1)}, bf16[192,1024]{1,0:T(8,128)(2,1)S(1)}, u32[]{:S(2)}, u32[]{:S(2)}) collective-permute-start(bf16[192,1024]{1,0:T(8,128)(2,1)S(1)} %get-tuple-element.99), channel_id=1, source_target_pairs={{0,4},{4,0},{8,12},{12,8},{16,20},{20,16},{24,28},{28,24},{1,5},{5... | collective-permute-start | bytes 1179656 | tf_op jit(solution)/shard_map/ppermute | solution.py:436
  34.4 9.4 %collective-permute-start.15 = (bf16[192,1024]{1,0:T(8,128)(2,1)S(1)}, bf16[192,1024]{1,0:T(8,128)(2,1)S(1)}, u32[]{:S(2)}, u32[]{:S(2)}) collective-permute-start(bf16[192,1024]{1,0:T(8,128)(2,1)S(1)} %get-tuple-element.113), channel_id=1, source_target_pairs={{0,8},{4,20},{8,0},{12,28},{16,24},{20,4},{24,16},{28,12},{1,9},{5... | collective-permute-start | bytes 1179656 | tf_op jit(solution)/shard_map/ppermute | solution.py:441
  35.9 13.7 %collective-permute-start.17 = (bf16[192,1024]{1,0:T(8,128)(2,1)S(1)}, bf16[192,1024]{1,0:T(8,128)(2,1)S(1)}, u32[]{:S(2)}, u32[]{:S(2)}) collective-permute-start(bf16[192,1024]{1,0:T(8,128)(2,1)S(1)} %get-tuple-element.115), channel_id=1, source_target_pairs={{0,8},{4,20},{8,0},{12,28},{16,24},{20,4},{24,16},{28,12},{1,9},{5... | collective-permute-start | bytes 1179656 | tf_op jit(solution)/shard_map/ppermute | solution.py:441
  37.9 17.3 %collective-permute-start.12 = (bf16[384,256]{1,0:T(8,128)(2,1)S(1)}, bf16[384,256]{1,0:T(8,128)(2,1)S(1)}, u32[]{:S(2)}, u32[]{:S(2)}) collective-permute-start(bf16[384,256]{1,0:T(8,128)(2,1)S(1)} %get-tuple-element.106), channel_id=1, source_target_pairs={{0,2},{1,3},{2,0},{3,1},{4,6},{5,7},{6,4},{7,5},{8,10},{9,11},{10,... | collective-permute-start | bytes 589832 | tf_op jit(solution)/shard_map/ppermute | solution.py:436
  41.5 13.7 %collective-permute-start.13 = (bf16[384,256]{1,0:T(8,128)(2,1)S(1)}, bf16[384,256]{1,0:T(8,128)(2,1)S(1)}, u32[]{:S(2)}, u32[]{:S(2)}) collective-permute-start(bf16[384,256]{1,0:T(8,128)(2,1)S(1)} %get-tuple-element.107), channel_id=1, source_target_pairs={{0,3},{1,2},{2,1},{3,0},{4,7},{5,6},{6,5},{7,4},{8,11},{9,10},{10,... | collective-permute-start | bytes 589832 | tf_op jit(solution)/shard_map/ppermute | solution.py:436
  42.1 14.1 %collective-permute-start.14 = (bf16[384,256]{1,0:T(8,128)(2,1)S(1)}, bf16[384,256]{1,0:T(8,128)(2,1)S(1)}, u32[]{:S(2)}, u32[]{:S(2)}) collective-permute-start(bf16[384,256]{1,0:T(8,128)(2,1)S(1)} %get-tuple-element.108), channel_id=1, source_target_pairs={{0,1},{1,0},{2,3},{3,2},{4,5},{5,4},{6,7},{7,6},{8,9},{9,8},{10,11... | collective-permute-start | bytes 589832 | tf_op jit(solution)/shard_map/ppermute | solution.py:436
  43.9 13.7 %collective-permute-start.16 = (bf16[192,1024]{1,0:T(8,128)(2,1)S(1)}, bf16[192,1024]{1,0:T(8,128)(2,1)S(1)}, u32[]{:S(2)}, u32[]{:S(2)}) collective-permute-start(bf16[192,1024]{1,0:T(8,128)(2,1)S(1)} %shard_map.100), channel_id=1, source_target_pairs={{0,16},{4,12},{8,24},{12,4},{16,0},{20,28},{24,8},{28,20},{1,17},{... | collective-permute-start | bytes 1179656 | tf_op jit(solution)/shard_map/ppermute | solution.py:441
  49.7 7.8 %collective-permute-start.18 = (bf16[192,1024]{1,0:T(8,128)(2,1)S(1)}, bf16[192,1024]{1,0:T(8,128)(2,1)S(1)}, u32[]{:S(2)}, u32[]{:S(2)}) collective-permute-start(bf16[192,1024]{1,0:T(8,128)(2,1)S(1)} %shard_map.101), channel_id=1, source_target_pairs={{0,16},{4,12},{8,24},{12,4},{16,0},{20,28},{24,8},{28,20},{1,17},{... | collective-permute-start | bytes 1179656 | tf_op jit(solution)/shard_map/ppermute | solution.py:441

commit v23 on v21

--- a/solution.py
+++ b/solution.py
@@ -13,7 +13,7 @@
 WAIT_FLOPS = 20_000_000_000
 TEXT_PIECES = 3
 ACC_PIECES = 2
-STEP = 32
+STEP = 16
 CORES = 2
 EPS = 1e-06
 LOG2E = math.log2(math.e)

time: 59.2 us -> 59.2 us (level)
  no operation moved by 1% of the time
where the time goes in v23:
time: 59.2 us; the launch traced here: 58.9 us
  starting transfers between devices  23.2 us (39%)
  Pallas kernels  16.5 us (28%)
  waiting for transfers between devices  16 us (27%)
  between operations  2.13 us (4%)
  local copies, waits for them, and re-layouts  1.14 us (2%)
    pallas_call x19, Pallas kernels, call_kernel(): pl.pallas_call(body, out_shape=outs, in_specs=specs, out_specs=[ANY_SPEC...  16.5 us
    ppermute x8, starting transfers between devices, swap_near(): lax.ppermute(value, 'blk', [(i, i ^ neighbour_bits(i)[which]) for i in ra...  13.5 us
    ppermute x11, starting transfers between devices, swap(): return lax.ppermute(value, axis, [(i, i ^ bits) for i in range(count)])  9.72 us
    ppermute x8, waiting for transfers between devices, swap_near(): lax.ppermute(value, 'blk', [(i, i ^ neighbour_bits(i)[which]) for i in ra...  8.69 us
    ppermute x11, waiting for transfers between devices, swap(): return lax.ppermute(value, axis, [(i, i ^ bits) for i in range(count)])  7.33 us
  transfers between devices with their start and end apart: 19, of which 9 were waited for; matrix products, arithmetic and copies ran while one was open for 0% of the time, Pallas kernels for 25%

profile of v23, /device:TPU:0, one launch (start us, length us, event | category | flops | bytes accessed | tf_op | source)
XLA Modules:
  0.0 58.9 jit_solution(208512030570264150)
XLA Ops:
  0.6 3.0 %collective-permute-start = (bf16[384,1024]{1,0:T(8,128)(2,1)}, bf16[384,1024]{1,0:T(8,128)(2,1)S(1)}, u32[]{:S(2)}, u32[]{:S(2)}) collective-permute-start(bf16[384,1024]{1,0:T(8,128)(2,1)} %raw_ref.1), channel_id=1, source_target_pairs={{0,16},{4,12},{8,24},{12,4},{16,0},{20,28},{24,8},{28,20},{1,17},{... | collective-permute-start | bytes 2359304 | tf_op jit(solution)/shard_map/ppermute | solution.py:441
  3.7 1.1 %copy-done = bf16[1536,256]{1,0:T(8,128)(2,1)S(1)} copy-done((bf16[1536,256]{1,0:T(8,128)(2,1)S(1)}, bf16[1536,256]{1,0:T(8,128)(2,1)}, u32[]{:S(2)}) %copy-start) | copy-done | bytes 786456
  4.8 0.1 shard_map.88
  4.9 2.7 %collective-permute-start.1 = (bf16[384,256]{1,0:T(8,128)(2,1)S(1)}, bf16[384,256]{1,0:T(8,128)(2,1)S(1)}, u32[]{:S(2)}, u32[]{:S(2)}) collective-permute-start(bf16[384,256]{1,0:T(8,128)(2,1)S(1)} %get-tuple-element.74), channel_id=1, source_target_pairs={{0,2},{1,3},{2,0},{3,1},{4,6},{5,7},{6,4},{7,5},{8,10},{9,11},{10,... | collective-permute-start | bytes 589832 | tf_op jit(solution)/shard_map/ppermute | solution.py:436
  7.5 1.3 %collective-permute-start.2 = (bf16[384,256]{1,0:T(8,128)(2,1)S(1)}, bf16[384,256]{1,0:T(8,128)(2,1)S(1)}, u32[]{:S(2)}, u32[]{:S(2)}) collective-permute-start(bf16[384,256]{1,0:T(8,128)(2,1)S(1)} %get-tuple-element.75), channel_id=1, source_target_pairs={{0,3},{1,2},{2,1},{3,0},{4,7},{5,6},{6,5},{7,4},{8,11},{9,10},{10,... | collective-permute-start | bytes 589832 | tf_op jit(solution)/shard_map/ppermute | solution.py:436
  8.9 0.2 collective-permute-start.3
  9.1 1.4 %shard_map.86 = (bf16[384,1024]{1,0:T(8,128)(2,1)S(1)}, bf16[384,1024]{1,0:T(8,128)(2,1)S(1)}, f32[384,128]{1,0:T(8,128)S(1)}) custom-call(bf16[384,1024]{1,0:T(8,128)(2,1)} %raw_ref.1), custom_call_target="tpu_custom_call" | custom-call | bytes 2555904 | tf_op jit(solution)/shard_map/pallas_call | solution.py:47
  10.5 1.6 %collective-permute-start.4 = (bf16[384,1024]{1,0:T(8,128)(2,1)}, bf16[384,1024]{1,0:T(8,128)(2,1)S(1)}, u32[]{:S(2)}, u32[]{:S(2)}) collective-permute-start(bf16[384,1024]{1,0:T(8,128)(2,1)} %raw_ref.1), channel_id=1, source_target_pairs={{0,8},{4,20},{8,0},{12,28},{16,24},{20,4},{24,16},{28,12},{1,9},{5... | collective-permute-start | bytes 2359304 | tf_op jit(solution)/shard_map/ppermute | solution.py:441
  13.4 1.1 %shard_map.87 = (f32[2,128]{1,0:T(2,128)S(1)}, f32[72,128]{1,0:T(8,128)S(1)}, s32[12,128]{1,0:T(8,128)S(1)}, s32[768,128]{1,0:T(8,128)S(1)}, f32[384,128]{1,0:T(8,128)S(1)}, /*index=5*/f32[4,128]{1,0:T(4,128)S(1)}) custom-call(f32[1]{0:T(128)S(6)} %copy.11.refs_0_, f32[1]{0:T(128)S(6)} %copy.12.refs_1_, s32[3,8,96]{2,1,0:T(8,128)S(1)} %bitcast.5, ...), custom_call_target="tpu_custom_call" | custom-call | bytes 743432 | tf_op jit(solution)/shard_map/pallas_call | solution.py:47
  14.5 0.9 %collective-permute-done.raw_ref = bf16[384,1024]{1,0:T(8,128)(2,1)S(1)} collective-permute-done((bf16[384,1024]{1,0:T(8,128)(2,1)}, bf16[384,1024]{1,0:T(8,128)(2,1)S(1)}, u32[]{:S(2)}, u32[]{:S(2)}) %collective-permute-start) | collective-permute-done | bytes 786464 | tf_op jit(solution)/shard_map/ppermute | solution.py:441
  15.4 3.3 %collective-permute-start.8 = (bf16[384,1024]{1,0:T(8,128)(2,1)S(1)}, bf16[384,1024]{1,0:T(8,128)(2,1)S(1)}, u32[]{:S(2)}, u32[]{:S(2)}) collective-permute-start(bf16[384,1024]{1,0:T(8,128)(2,1)S(1)} %collective-permute-done.raw_ref), channel_id=1, source_target_pairs={{0,8},{4,20},{8,0},{12,28},{16,24},{20,4},{24,16},{28,12},{1,9},{5... | collective-permute-start | bytes 2359304 | tf_op jit(solution)/shard_map/ppermute | solution.py:441
  18.7 0.2 shard_map.89.second_unit_ref
  19.0 3.8 %collective-permute-done.4.first_ref = bf16[384,1024]{1,0:T(8,128)(2,1)S(1)} collective-permute-done((bf16[384,1024]{1,0:T(8,128)(2,1)}, bf16[384,1024]{1,0:T(8,128)(2,1)S(1)}, u32[]{:S(2)}, u32[]{:S(2)}) %collective-permute-start.4) | collective-permute-done | bytes 786464 | tf_op jit(solution)/shard_map/ppermute | solution.py:441
  22.8 0.3 shard_map.90.refs_7_
  23.1 0.0 collective-permute-done.1.refs_1_.refs_2_
  23.2 0.4 shard_map.91
  23.5 0.1 collective-permute-start.5
  23.6 0.5 collective-permute-start.6
  24.1 0.1 collective-permute-start.7
  24.2 1.4 %shard_map.92 = (bf16[384,384]{1,0:T(8,128)(2,1)S(1)}, bf16[384,768]{1,0:T(8,128)(2,1)S(1)}) custom-call(f32[2,128]{1,0:T(2,128)S(1)} %get-tuple-element.67.refs_0_, f32[72,128]{1,0:T(8,128)S(1)} %get-tuple-element.68.refs_1_, s32[12,128]{1,0:T(8,128)S(1)} %get-tuple-element.69.refs_2_, s32[768,128]{1,0:T(8,128)S(1)} %get-tuple-element.70.refs_3_, ...), custom_call_target="tpu_custom_call" | custom-call | bytes 4666368 | tf_op jit(solution)/shard_map/pallas_call | solution.py:47
  25.6 0.2 collective-permute-done.7.refs_11_
  25.9 1.3 %shard_map.93 = (bf16[768,1024]{1,0:T(8,128)(2,1)S(1)}, bf16[768,384]{1,0:T(8,128)(2,1)S(1)}, bf16[384,1024]{1,0:T(8,128)(2,1)S(1)}) custom-call(f32[2,128]{1,0:T(2,128)S(1)} %get-tuple-element.67.refs_0_, f32[72,128]{1,0:T(8,128)S(1)} %get-tuple-element.68.refs_1_, s32[12,128]{1,0:T(8,128)S(1)} %get-tuple-element.69.refs_2_, ...), custom_call_target="tpu_custom_call" | custom-call | bytes 8107008 | tf_op jit(solution)/shard_map/pallas_call | solution.py:47
  27.2 1.6 %collective-permute-start.11 = (bf16[384,1024]{1,0:T(8,128)(2,1)S(1)}, bf16[384,1024]{1,0:T(8,128)(2,1)S(1)}, u32[]{:S(2)}, u32[]{:S(2)}) collective-permute-start(bf16[384,1024]{1,0:T(8,128)(2,1)S(1)} %get-tuple-element.103), channel_id=1, source_target_pairs={{0,8},{4,20},{8,0},{12,28},{16,24},{20,4},{24,16},{28,12},{1,9},{5... | collective-permute-start | bytes 2359304 | tf_op jit(solution)/shard_map/ppermute | solution.py:441
  28.8 2.2 %shard_map.94 = (bf16[768,384]{1,0:T(8,128)(2,1)S(1)}, f32[768,1024]{1,0:T(8,128)S(1)}, bf16[768,768]{1,0:T(8,128)(2,1)S(1)}) custom-call(f32[2,128]{1,0:T(2,128)S(1)} %get-tuple-element.67.refs_0_, f32[72,128]{1,0:T(8,128)S(1)} %get-tuple-element.68.refs_1_, s32[12,128]{1,0:T(8,128)S(1)} %get-tuple-element.69.refs_2_, ...), custom_call_target="tpu_custom_call" | custom-call | bytes 10957824 | tf_op jit(solution)/shard_map/pallas_call | solution.py:47
  31.0 0.3 collective-permute-done.8.refs_9_
  31.2 2.6 %shard_map.95 = (bf16[768,768]{1,0:T(8,128)(2,1)S(1)}, bf16[768,1024]{1,0:T(8,128)(2,1)S(1)}, bf16[256,1024]{1,0:T(8,128)(2,1)S(1)}, bf16[128,1024]{1,0:T(8,128)...) custom-call(f32[2,128]{1,0:T(2,128)S(1)} %get-tuple-element.67.refs_0_, ...), custom_call_target="tpu_custom_call" | custom-call | bytes 11842560 | tf_op jit(solution)/shard_map/pallas_call | solution.py:47
  33.8 0.1 collective-permute-start.9
  33.9 0.5 collective-permute-start.10
  34.4 1.5 %collective-permute-start.15 = (bf16[256,1024]{1,0:T(8,128)(2,1)S(1)}, bf16[256,1024]{1,0:T(8,128)(2,1)S(1)}, u32[]{:S(2)}, u32[]{:S(2)}) collective-permute-start(bf16[256,1024]{1,0:T(8,128)(2,1)S(1)} %get-tuple-element.113), channel_id=1, source_target_pairs={{0,8},{4,20},{8,0},{12,28},{16,24},{20,4},{24,16},{28,12},{1,9},{5... | collective-permute-start | bytes 1572872 | tf_op jit(solution)/shard_map/ppermute | solution.py:441
  35.9 0.5 collective-permute-start.17
  36.4 0.8 %shard_map.96.refs_5_ = f32[384,1024]{1,0:T(8,128)S(1)} custom-call(bf16[768,768]{1,0:T(8,128)(2,1)S(1)} %get-tuple-element.96.weight_ref, bf16[768,1024]{1,0:T(8,128)(2,1)S(1)} %get-tuple-element.97.image_ref, f32[768,1024]{1,0:T(8,128)S(1)} %get-tuple-element.95.refs_10_.acc_ref), custom_call_target="tpu_custom_call" | custom-call | bytes 7471104 | tf_op jit(solution)/shard_map/pallas_call | solution.py:47
  37.2 0.6 %shard_map.97 = (bf16[384,256]{1,0:T(8,128)(2,1)S(1)}, bf16[384,256]{1,0:T(8,128)(2,1)S(1)}, bf16[384,256]{1,0:T(8,128)(2,1)S(1)}, bf16[384,256]{1,0:T(8,128)(2,1)S(1)}) custom-call(f32[384,128]{1,0:T(8,128)S(1)} %get-tuple-element.91.refs_0_, bf16[384,256]{1,0:T(8,128)(2,1)S(1)} %get-tuple-element.73.refs_0_.refs_1_, ...), custom_call_target="tpu_custom_call" | custom-call | bytes 4128768 | tf_op jit(solution)/shard_map/pallas_call | solution.py:47
  37.9 3.6 %collective-permute-start.12 = (bf16[384,256]{1,0:T(8,128)(2,1)S(1)}, bf16[384,256]{1,0:T(8,128)(2,1)S(1)}, u32[]{:S(2)}, u32[]{:S(2)}) collective-permute-start(bf16[384,256]{1,0:T(8,128)(2,1)S(1)} %get-tuple-element.106), channel_id=1, source_target_pairs={{0,2},{1,3},{2,0},{3,1},{4,6},{5,7},{6,4},{7,5},{8,10},{9,11},{10,... | collective-permute-start | bytes 589832 | tf_op jit(solution)/shard_map/ppermute | solution.py:436
  41.5 0.6 collective-permute-start.13
  42.1 0.1 collective-permute-start.14
  42.1 0.8 %shard_map.98 = (f32[384,1024]{1,0:T(8,128)S(1)}, bf16[384,1024]{1,0:T(8,128)(2,1)S(1)}) custom-call(bf16[768,768]{1,0:T(8,128)(2,1)S(1)} %get-tuple-element.102.weight_ref, bf16[768,1024]{1,0:T(8,128)(2,1)S(1)} %get-tuple-element.87.refs_6_.unit_ref, bf16[384,1024]{1,0:T(8,128)(2,1)S(1)} %collective-permute-done.11.add_ref), custom_call_target="tpu_custom_call" | custom-call | bytes 5898240 | tf_op jit(solution)/shard_map/pallas_call | solution.py:47
  43.0 0.8 %shard_map.99.refs_6_ = f32[384,1024]{1,0:T(8,128)S(1)} custom-call(bf16[768,384]{1,0:T(8,128)(2,1)S(1)} %get-tuple-element.93.refs_8_.weight_ref, bf16[768,1024]{1,0:T(8,128)(2,1)S(1)} %get-tuple-element.87.refs_6_.unit_ref, bf16[384,1024]{1,0:T(8,128)(2,1)S(1)} %get-tuple-element.104.add_ref), custom_call_target="tpu_custom_call" | custom-call | tf_op jit(solution)/shard_map/pallas_call | solution.py:47
  43.8 0.7 %shard_map.103.refs_10_ = bf16[1536,256]{1,0:T(8,128)(2,1)} custom-call(bf16[384,256]{1,0:T(8,128)(2,1)S(1)} %get-tuple-element.105.part_ref.refs_0_), custom_call_target="tpu_custom_call" | custom-call | tf_op jit(solution)/shard_map/pallas_call | solution.py:47
  44.5 0.8 %collective-permute-done.15.in_ref = bf16[256,1024]{1,0:T(8,128)(2,1)S(1)} collective-permute-done((bf16[256,1024]{1,0:T(8,128)(2,1)S(1)}, bf16[256,1024]{1,0:T(8,128)(2,1)S(1)}, u32[]{:S(2)}, u32[]{:S(2)}) %collective-permute-start.15) | collective-permute-done | bytes 524320 | tf_op jit(solution)/shard_map/ppermute | solution.py:441
  45.2 0.1 shard_map.100
  45.4 1.0 %collective-permute-start.16 = (bf16[256,1024]{1,0:T(8,128)(2,1)S(1)}, bf16[256,1024]{1,0:T(8,128)(2,1)S(1)}, u32[]{:S(2)}, u32[]{:S(2)}) collective-permute-start(bf16[256,1024]{1,0:T(8,128)(2,1)S(1)} %shard_map.100), channel_id=1, source_target_pairs={{0,16},{4,12},{8,24},{12,4},{16,0},{20,28},{24,8},{28,20},{1,17},{... | collective-permute-start | bytes 1572872 | tf_op jit(solution)/shard_map/ppermute | solution.py:441
  46.4 1.7 %collective-permute-done.17.in_ref = bf16[128,1024]{1,0:T(8,128)(2,1)S(1)} collective-permute-done((bf16[128,1024]{1,0:T(8,128)(2,1)S(1)}, bf16[128,1024]{1,0:T(8,128)(2,1)S(1)}, u32[]{:S(2)}, u32[]{:S(2)}) %collective-permute-start.17) | collective-permute-done | bytes 262176 | tf_op jit(solution)/shard_map/ppermute | solution.py:441
  48.1 0.1 shard_map.101
  48.2 0.9 %collective-permute-start.18 = (bf16[128,1024]{1,0:T(8,128)(2,1)S(1)}, bf16[128,1024]{1,0:T(8,128)(2,1)S(1)}, u32[]{:S(2)}, u32[]{:S(2)}) collective-permute-start(bf16[128,1024]{1,0:T(8,128)(2,1)S(1)} %shard_map.101), channel_id=1, source_target_pairs={{0,16},{4,12},{8,24},{12,4},{16,0},{20,28},{24,8},{28,20},{1,17},{... | collective-permute-start | bytes 786440 | tf_op jit(solution)/shard_map/ppermute | solution.py:441
  49.2 6.0 %collective-permute-done.12.refs_0_.refs_1_ = bf16[384,256]{1,0:T(8,128)(2,1)S(1)} collective-permute-done((bf16[384,256]{1,0:T(8,128)(2,1)S(1)}, bf16[384,256]{1,0:T(8,128)(2,1)S(1)}, u32[]{:S(2)}, u32[]{:S(2)}) %collective-permute-start.12) | collective-permute-done | bytes 196640 | tf_op jit(solution)/shard_map/ppermute | solution.py:436
  55.2 1.0 %collective-permute-done.14.refs_2_.refs_3_ = bf16[384,256]{1,0:T(8,128)(2,1)S(1)} collective-permute-done((bf16[384,256]{1,0:T(8,128)(2,1)S(1)}, bf16[384,256]{1,0:T(8,128)(2,1)S(1)}, u32[]{:S(2)}, u32[]{:S(2)}) %collective-permute-start.14) | collective-permute-done | bytes 196640 | tf_op jit(solution)/shard_map/ppermute | solution.py:436
  56.2 1.2 %collective-permute-done.18.refs_8_ = bf16[128,1024]{1,0:T(8,128)(2,1)S(1)} collective-permute-done((bf16[128,1024]{1,0:T(8,128)(2,1)S(1)}, bf16[128,1024]{1,0:T(8,128)(2,1)S(1)}, u32[]{:S(2)}, u32[]{:S(2)}) %collective-permute-start.18) | collective-permute-done | bytes 262176 | tf_op jit(solution)/shard_map/ppermute | solution.py:441
  57.5 1.5 %shard_map.104 = (bf16[1536,256]{1,0:T(8,128)(2,1)}, bf16[384,1024]{1,0:T(8,128)(2,1)}) custom-call(bf16[384,256]{1,0:T(8,128)(2,1)S(1)} %get-tuple-element.105.part_ref.refs_0_, bf16[384,256]{1,0:T(8,128)(2,1)S(1)} %collective-permute-done.12.refs_0_.refs_1_, ...), custom_call_target="tpu_custom_call", output_to_operand_aliasing={{0}: (10, {})} | custom-call | bytes 6492160 | tf_op jit(solution)/shard_map/pallas_call | solution.py:47
  (17 shorter events, 0.0 us)
Async XLA Ops:
  0.6 14.8 %collective-permute-start = (bf16[384,1024]{1,0:T(8,128)(2,1)}, bf16[384,1024]{1,0:T(8,128)(2,1)S(1)}, u32[]{:S(2)}, u32[]{:S(2)}) collective-permute-start(bf16[384,1024]{1,0:T(8,128)(2,1)} %raw_ref.1), channel_id=1, source_target_pairs={{0,16},{4,12},{8,24},{12,4},{16,0},{20,28},{24,8},{28,20},{1,17},{... | collective-permute-start | bytes 2359304 | tf_op jit(solution)/shard_map/ppermute | solution.py:441
  3.7 1.1 %copy-start = (bf16[1536,256]{1,0:T(8,128)(2,1)S(1)}, bf16[1536,256]{1,0:T(8,128)(2,1)}, u32[]{:S(2)}) copy-start(bf16[1536,256]{1,0:T(8,128)(2,1)} %text_ref.1) | copy-start | bytes 2359300
  4.8 8.6 %copy-start.1 = (s32[12288]{0:T(1024)S(1)}, s32[12288]{0:T(1024)}, u32[]{:S(2)}) copy-start(s32[12288]{0:T(1024)} %param.11) | copy-start | bytes 147460
  4.8 8.6 %copy-start.2 = (s32[12288]{0:T(1024)S(1)}, s32[12288]{0:T(1024)}, u32[]{:S(2)}) copy-start(s32[12288]{0:T(1024)} %param.12) | copy-start | bytes 147460
  4.8 8.6 %copy-start.3 = (s32[96,8,3]{0,1,2:T(8,128)S(1)}, s32[96,8,3]{0,1,2:T(8,128)}, u32[]{:S(2)}) copy-start(s32[96,8,3]{0,1,2:T(8,128)} %param.13) | copy-start | bytes 27652
  4.9 18.3 %collective-permute-start.1 = (bf16[384,256]{1,0:T(8,128)(2,1)S(1)}, bf16[384,256]{1,0:T(8,128)(2,1)S(1)}, u32[]{:S(2)}, u32[]{:S(2)}) collective-permute-start(bf16[384,256]{1,0:T(8,128)(2,1)S(1)} %get-tuple-element.74), channel_id=1, source_target_pairs={{0,2},{1,3},{2,0},{3,1},{4,6},{5,7},{6,4},{7,5},{8,10},{9,11},{10,... | collective-permute-start | bytes 589832 | tf_op jit(solution)/shard_map/ppermute | solution.py:436
  7.5 15.6 %collective-permute-start.2 = (bf16[384,256]{1,0:T(8,128)(2,1)S(1)}, bf16[384,256]{1,0:T(8,128)(2,1)S(1)}, u32[]{:S(2)}, u32[]{:S(2)}) collective-permute-start(bf16[384,256]{1,0:T(8,128)(2,1)S(1)} %get-tuple-element.75), channel_id=1, source_target_pairs={{0,3},{1,2},{2,1},{3,0},{4,7},{5,6},{6,5},{7,4},{8,11},{9,10},{10,... | collective-permute-start | bytes 589832 | tf_op jit(solution)/shard_map/ppermute | solution.py:436
  8.9 14.3 %collective-permute-start.3 = (bf16[384,256]{1,0:T(8,128)(2,1)S(1)}, bf16[384,256]{1,0:T(8,128)(2,1)S(1)}, u32[]{:S(2)}, u32[]{:S(2)}) collective-permute-start(bf16[384,256]{1,0:T(8,128)(2,1)S(1)} %get-tuple-element.76), channel_id=1, source_target_pairs={{0,1},{1,0},{2,3},{3,2},{4,5},{5,4},{6,7},{7,6},{8,9},{9,8},{10,11... | collective-permute-start | bytes 589832 | tf_op jit(solution)/shard_map/ppermute | solution.py:436
  10.5 12.3 %collective-permute-start.4 = (bf16[384,1024]{1,0:T(8,128)(2,1)}, bf16[384,1024]{1,0:T(8,128)(2,1)S(1)}, u32[]{:S(2)}, u32[]{:S(2)}) collective-permute-start(bf16[384,1024]{1,0:T(8,128)(2,1)} %raw_ref.1), channel_id=1, source_target_pairs={{0,8},{4,20},{8,0},{12,28},{16,24},{20,4},{24,16},{28,12},{1,9},{5... | collective-permute-start | bytes 2359304 | tf_op jit(solution)/shard_map/ppermute | solution.py:441
  15.4 15.8 %collective-permute-start.8 = (bf16[384,1024]{1,0:T(8,128)(2,1)S(1)}, bf16[384,1024]{1,0:T(8,128)(2,1)S(1)}, u32[]{:S(2)}, u32[]{:S(2)}) collective-permute-start(bf16[384,1024]{1,0:T(8,128)(2,1)S(1)} %collective-permute-done.raw_ref), channel_id=1, source_target_pairs={{0,8},{4,20},{8,0},{12,28},{16,24},{20,4},{24,16},{28,12},{1,9},{5... | collective-permute-start | bytes 2359304 | tf_op jit(solution)/shard_map/ppermute | solution.py:441
  23.5 2.1 %collective-permute-start.5 = (bf16[128,1024]{1,0:T(8,128)(2,1)S(1)}, bf16[128,1024]{1,0:T(8,128)(2,1)S(1)}, u32[]{:S(2)}, u32[]{:S(2)}) collective-permute-start(bf16[128,1024]{1,0:T(8,128)(2,1)S(1)} %get-tuple-element.84), channel_id=1, source_target_pairs={{0,4},{4,0},{8,12},{12,8},{16,20},{20,16},{24,28},{28,24},{1,5},{5... | collective-permute-start | bytes 786440 | tf_op jit(solution)/shard_map/ppermute | solution.py:436
  23.6 2.0 %collective-permute-start.6 = (bf16[128,1024]{1,0:T(8,128)(2,1)S(1)}, bf16[128,1024]{1,0:T(8,128)(2,1)S(1)}, u32[]{:S(2)}, u32[]{:S(2)}) collective-permute-start(bf16[128,1024]{1,0:T(8,128)(2,1)S(1)} %get-tuple-element.85), channel_id=1, source_target_pairs={{0,4},{4,0},{8,12},{12,8},{16,20},{20,16},{24,28},{28,24},{1,5},{5... | collective-permute-start | bytes 786440 | tf_op jit(solution)/shard_map/ppermute | solution.py:436
  24.1 1.8 %collective-permute-start.7 = (bf16[128,1024]{1,0:T(8,128)(2,1)S(1)}, bf16[128,1024]{1,0:T(8,128)(2,1)S(1)}, u32[]{:S(2)}, u32[]{:S(2)}) collective-permute-start(bf16[128,1024]{1,0:T(8,128)(2,1)S(1)} %get-tuple-element.86), channel_id=1, source_target_pairs={{0,4},{4,0},{8,12},{12,8},{16,20},{20,16},{24,28},{28,24},{1,5},{5... | collective-permute-start | bytes 786440 | tf_op jit(solution)/shard_map/ppermute | solution.py:436
  27.2 14.9 %collective-permute-start.11 = (bf16[384,1024]{1,0:T(8,128)(2,1)S(1)}, bf16[384,1024]{1,0:T(8,128)(2,1)S(1)}, u32[]{:S(2)}, u32[]{:S(2)}) collective-permute-start(bf16[384,1024]{1,0:T(8,128)(2,1)S(1)} %get-tuple-element.103), channel_id=1, source_target_pairs={{0,8},{4,20},{8,0},{12,28},{16,24},{20,4},{24,16},{28,12},{1,9},{5... | collective-permute-start | bytes 2359304 | tf_op jit(solution)/shard_map/ppermute | solution.py:441
  33.8 3.4 %collective-permute-start.9 = (bf16[192,1024]{1,0:T(8,128)(2,1)S(1)}, bf16[192,1024]{1,0:T(8,128)(2,1)S(1)}, u32[]{:S(2)}, u32[]{:S(2)}) collective-permute-start(bf16[192,1024]{1,0:T(8,128)(2,1)S(1)} %get-tuple-element.98), channel_id=1, source_target_pairs={{0,4},{4,0},{8,12},{12,8},{16,20},{20,16},{24,28},{28,24},{1,5},{5... | collective-permute-start | bytes 1179656 | tf_op jit(solution)/shard_map/ppermute | solution.py:436
  33.9 3.3 %collective-permute-start.10 = (bf16[192,1024]{1,0:T(8,128)(2,1)S(1)}, bf16[192,1024]{1,0:T(8,128)(2,1)S(1)}, u32[]{:S(2)}, u32[]{:S(2)}) collective-permute-start(bf16[192,1024]{1,0:T(8,128)(2,1)S(1)} %get-tuple-element.99), channel_id=1, source_target_pairs={{0,4},{4,0},{8,12},{12,8},{16,20},{20,16},{24,28},{28,24},{1,5},{5... | collective-permute-start | bytes 1179656 | tf_op jit(solution)/shard_map/ppermute | solution.py:436
  34.4 10.8 %collective-permute-start.15 = (bf16[256,1024]{1,0:T(8,128)(2,1)S(1)}, bf16[256,1024]{1,0:T(8,128)(2,1)S(1)}, u32[]{:S(2)}, u32[]{:S(2)}) collective-permute-start(bf16[256,1024]{1,0:T(8,128)(2,1)S(1)} %get-tuple-element.113), channel_id=1, source_target_pairs={{0,8},{4,20},{8,0},{12,28},{16,24},{20,4},{24,16},{28,12},{1,9},{5... | collective-permute-start | bytes 1572872 | tf_op jit(solution)/shard_map/ppermute | solution.py:441
  35.9 12.2 %collective-permute-start.17 = (bf16[128,1024]{1,0:T(8,128)(2,1)S(1)}, bf16[128,1024]{1,0:T(8,128)(2,1)S(1)}, u32[]{:S(2)}, u32[]{:S(2)}) collective-permute-start(bf16[128,1024]{1,0:T(8,128)(2,1)S(1)} %get-tuple-element.115), channel_id=1, source_target_pairs={{0,8},{4,20},{8,0},{12,28},{16,24},{20,4},{24,16},{28,12},{1,9},{5... | collective-permute-start | bytes 786440 | tf_op jit(solution)/shard_map/ppermute | solution.py:441
  37.9 17.3 %collective-permute-start.12 = (bf16[384,256]{1,0:T(8,128)(2,1)S(1)}, bf16[384,256]{1,0:T(8,128)(2,1)S(1)}, u32[]{:S(2)}, u32[]{:S(2)}) collective-permute-start(bf16[384,256]{1,0:T(8,128)(2,1)S(1)} %get-tuple-element.106), channel_id=1, source_target_pairs={{0,2},{1,3},{2,0},{3,1},{4,6},{5,7},{6,4},{7,5},{8,10},{9,11},{10,... | collective-permute-start | bytes 589832 | tf_op jit(solution)/shard_map/ppermute | solution.py:436
  41.5 13.7 %collective-permute-start.13 = (bf16[384,256]{1,0:T(8,128)(2,1)S(1)}, bf16[384,256]{1,0:T(8,128)(2,1)S(1)}, u32[]{:S(2)}, u32[]{:S(2)}) collective-permute-start(bf16[384,256]{1,0:T(8,128)(2,1)S(1)} %get-tuple-element.107), channel_id=1, source_target_pairs={{0,3},{1,2},{2,1},{3,0},{4,7},{5,6},{6,5},{7,4},{8,11},{9,10},{10,... | collective-permute-start | bytes 589832 | tf_op jit(solution)/shard_map/ppermute | solution.py:436
  42.1 14.1 %collective-permute-start.14 = (bf16[384,256]{1,0:T(8,128)(2,1)S(1)}, bf16[384,256]{1,0:T(8,128)(2,1)S(1)}, u32[]{:S(2)}, u32[]{:S(2)}) collective-permute-start(bf16[384,256]{1,0:T(8,128)(2,1)S(1)} %get-tuple-element.108), channel_id=1, source_target_pairs={{0,1},{1,0},{2,3},{3,2},{4,5},{5,4},{6,7},{7,6},{8,9},{9,8},{10,11... | collective-permute-start | bytes 589832 | tf_op jit(solution)/shard_map/ppermute | solution.py:436
  45.4 12.1 %collective-permute-start.16 = (bf16[256,1024]{1,0:T(8,128)(2,1)S(1)}, bf16[256,1024]{1,0:T(8,128)(2,1)S(1)}, u32[]{:S(2)}, u32[]{:S(2)}) collective-permute-start(bf16[256,1024]{1,0:T(8,128)(2,1)S(1)} %shard_map.100), channel_id=1, source_target_pairs={{0,16},{4,12},{8,24},{12,4},{16,0},{20,28},{24,8},{28,20},{1,17},{... | collective-permute-start | bytes 1572872 | tf_op jit(solution)/shard_map/ppermute | solution.py:441
  48.2 9.2 %collective-permute-start.18 = (bf16[128,1024]{1,0:T(8,128)(2,1)S(1)}, bf16[128,1024]{1,0:T(8,128)(2,1)S(1)}, u32[]{:S(2)}, u32[]{:S(2)}) collective-permute-start(bf16[128,1024]{1,0:T(8,128)(2,1)S(1)} %shard_map.101), channel_id=1, source_target_pairs={{0,16},{4,12},{8,24},{12,4},{16,0},{20,28},{24,8},{28,20},{1,17},{... | collective-permute-start | bytes 786440 | tf_op jit(solution)/shard_map/ppermute | solution.py:441
